TPU v7x, 32 devices: a whole 2x2x4 slice. The times are simulated.
32 devices in a mesh: ctx: 8 (over z, y), head: 4 (over x, core).
Axes of the slice: x: 2, y: 2, z: 4, core: 2. Of those that a mesh axis runs over, the one named last changes fastest.
Arguments:
- sec_q: bfloat16 [1024, 1536], P('ctx', 'head'), may hold values from -7 to 7
- sec_k: bfloat16 [1024, 1536], P('ctx', 'head'), may hold values from -6 to 6
- sec_v: bfloat16 [1024, 1536], P('ctx', 'head'), may hold values from -6 to 6
- hist_k: bfloat16 [256, 1536], P('ctx', 'head'), may hold values from -6 to 6
- hist_v: bfloat16 [256, 1536], P('ctx', 'head'), may hold values from -6 to 6
- frame_levels: int32 [8, 2], replicated, may hold values from 0 to 2, as said below
- frame_counts: int32 [8], replicated, may hold values from 1 to 2, as said below
- w_out: bfloat16 [1536, 3072], P('head'), may hold values from -0.15625 to 0.15625
- grad_out: bfloat16 [1024, 3072], P('ctx', 'head'), may hold values from -6 to 6
Outputs:
- out: bfloat16 [1024, 3072], P('ctx', 'head')
- grad_sec_q: bfloat16 [1024, 1536], P('ctx', 'head')
- grad_sec_k: bfloat16 [1024, 1536], P('ctx', 'head')
- grad_sec_v: bfloat16 [1024, 1536], P('ctx', 'head')
- grad_hist_k: bfloat16 [256, 1536], P('ctx', 'head')
- grad_hist_v: bfloat16 [256, 1536], P('ctx', 'head')
Inputs may be any that keep to these rules, and one draw needn't show every extreme that they name: `frame_levels`: only the first frame_counts[o] levels of owner o count; the tokens of one owner never exceed 32, and in every draw some owner has exactly 32. `frame_counts`: in every draw some owner has 2 frames.
All inputs are finite; a program needn't handle non-finite values.
Results may differ from a plain program's by a relative error of at most 0.033.
Values may be sent and summed in bfloat16 or wider, within the bound.
No kernel may reach another device: no remote copies, remote signals or barrier semaphores. Data moves between devices by JAX's collectives and lax.ppermute only.
A program may use at most 192 MiB of HBM per device.

v0:
```python
import math

import jax
import jax.numpy as jnp
from jax import lax
from jax.sharding import PartitionSpec as P

HDIM = 128
FTOK = 16
FMAX = 2


NEG_FILL = -1e30


def contract_rows(left_side, right_side):
    return lax.dot_general(
        left_side, right_side, (((0,), (0,)), ((), ())), preferred_element_type=jnp.float32
    )


def contract_cols(left_side, right_side):
    return lax.dot_general(
        left_side, right_side, (((1,), (1,)), ((), ())), preferred_element_type=jnp.float32
    )


def head_slice(stacked, head_idx):
    return stacked[:, head_idx * HDIM : (head_idx + 1) * HDIM]


def owner_token_counts(frame_levels, frame_counts):
    frame_index = jnp.arange(FMAX, dtype=jnp.int32)[None, :]
    per_frame = jnp.where(
        frame_index < frame_counts[:, None], jnp.right_shift(jnp.int32(FTOK), 2 * frame_levels), 0
    )
    return jnp.sum(per_frame, axis=1)


def shards(sec_q, sec_k, sec_v, hist_k, hist_v, frame_levels, frame_counts, w_out, grad_out):
    score_scale = 1.0 / math.sqrt(HDIM)
    sec_rows = sec_q.shape[0]
    width_here = sec_q.shape[1]
    heads_here = width_here // HDIM
    capacity = hist_k.shape[0]
    owners = lax.axis_size("ctx")
    owner_tokens = owner_token_counts(frame_levels, frame_counts)
    slot_index = jnp.arange(capacity, dtype=jnp.int32)
    hist_valid = (slot_index[None, :] < owner_tokens[:, None]).reshape(owners * capacity)
    key_valid = jnp.concatenate([jnp.ones((owners * sec_rows,), dtype=bool), hist_valid])
    gathered = (
        lax.all_gather(sec_k, "ctx", axis=0, tiled=True),
        lax.all_gather(sec_v, "ctx", axis=0, tiled=True),
        lax.all_gather(hist_k, "ctx", axis=0, tiled=True),
        lax.all_gather(hist_v, "ctx", axis=0, tiled=True),
    )
    all_keys = jnp.concatenate([gathered[0], gathered[2]], axis=0)
    all_values = jnp.concatenate([gathered[1], gathered[3]], axis=0)
    d_attn = contract_cols(lax.all_gather(grad_out, "head", axis=1, tiled=True), w_out).astype(
        jnp.bfloat16
    )
    attn_parts = []
    grad_q_parts = []
    log_totals = []
    row_deltas = []
    prob_list = []
    dscore_list = []
    for head_idx in range(heads_here):
        query_h = head_slice(sec_q, head_idx)
        key_h = head_slice(all_keys, head_idx)
        value_h = head_slice(all_values, head_idx)
        dattn_h = head_slice(d_attn, head_idx)
        scores = contract_cols(query_h, key_h) * score_scale
        scores = jnp.where(key_valid[None, :], scores, NEG_FILL)
        row_top = jnp.max(scores, axis=1, keepdims=True)
        log_total = row_top + jnp.log(jnp.sum(jnp.exp(scores - row_top), axis=1, keepdims=True))
        prob_h = jnp.where(key_valid[None, :], jnp.exp(scores - log_total), 0.0).astype(
            jnp.bfloat16
        )
        attn_h = jnp.dot(prob_h, value_h, preferred_element_type=jnp.float32).astype(jnp.bfloat16)
        row_delta = jnp.sum(attn_h.astype(jnp.float32) * dattn_h.astype(jnp.float32), axis=1)
        dprobs = contract_cols(dattn_h, value_h)
        dscores = (prob_h.astype(jnp.float32) * (dprobs - row_delta[:, None])).astype(jnp.bfloat16)
        grad_query = (
            jnp.dot(dscores, key_h, preferred_element_type=jnp.float32) * score_scale
        ).astype(jnp.bfloat16)
        attn_parts.append(attn_h)
        grad_q_parts.append(grad_query)
        log_totals.append(log_total[:, 0])
        row_deltas.append(row_delta)
        prob_list.append(prob_h)
        dscore_list.append(dscores)
    attn = jnp.concatenate(attn_parts, axis=1)
    grad_sec_q = jnp.concatenate(grad_q_parts, axis=1)
    partial_out = jnp.dot(attn, w_out, preferred_element_type=jnp.float32)
    share_cols = partial_out.shape[1] // lax.axis_size("head")
    full_out = lax.psum(partial_out.astype(jnp.bfloat16), "head").astype(jnp.float32)
    out = lax.dynamic_slice_in_dim(
        full_out, lax.axis_index("head") * share_cols, share_cols, 1
    ).astype(jnp.bfloat16)
    all_logs, all_deltas = (
        lax.all_gather(jnp.stack(log_totals, 0), "ctx", axis=1, tiled=True),
        lax.all_gather(jnp.stack(row_deltas, 0), "ctx", axis=1, tiled=True),
    )
    own_keys = jnp.concatenate([sec_k, hist_k], axis=0)
    own_values = jnp.concatenate([sec_v, hist_v], axis=0)
    own_count = jnp.sum(
        jnp.where(jnp.arange(owners, dtype=jnp.int32) == lax.axis_index("ctx"), owner_tokens, 0)
    )
    own_valid = jnp.concatenate([jnp.ones((sec_rows,), dtype=bool), slot_index < own_count])
    query_piece = lax.all_gather(sec_q, "ctx", axis=0, tiled=True)
    dattn_piece = lax.all_gather(d_attn, "ctx", axis=0, tiled=True)
    key_parts = []
    value_parts = []
    for head_idx in range(heads_here):
        query_ph = head_slice(query_piece, head_idx)
        dattn_ph = head_slice(dattn_piece, head_idx)
        scores = contract_cols(query_ph, head_slice(own_keys, head_idx)) * score_scale
        prob_ph = jnp.where(
            own_valid[None, :], jnp.exp(scores - all_logs[head_idx][:, None]), 0.0
        ).astype(jnp.bfloat16)
        dprobs = contract_cols(dattn_ph, head_slice(own_values, head_idx))
        dscores = (prob_ph.astype(jnp.float32) * (dprobs - all_deltas[head_idx][:, None])).astype(
            jnp.bfloat16
        )
        key_parts.append(contract_rows(dscores, query_ph))
        value_parts.append(contract_rows(prob_ph, dattn_ph))
    key_sum = jnp.concatenate(key_parts, axis=1)
    value_sum = jnp.concatenate(value_parts, axis=1)
    grad_keys = (key_sum * score_scale).astype(jnp.bfloat16)
    grad_values = value_sum.astype(jnp.bfloat16)
    return (
        out,
        grad_sec_q,
        grad_keys[:sec_rows],
        grad_values[:sec_rows],
        grad_keys[sec_rows:],
        grad_values[sec_rows:],
    )


def solution(mesh):
    placed = (
        P("ctx", "head"),
        P("ctx", "head"),
        P("ctx", "head"),
        P("ctx", "head"),
        P("ctx", "head"),
        P(),
        P(),
        P("head", None),
        P("ctx", "head"),
    )
    return jax.shard_map(
        shards,
        mesh=mesh,
        in_specs=placed,
        out_specs=(
            P("ctx", "head"),
            P("ctx", "head"),
            P("ctx", "head"),
            P("ctx", "head"),
            P("ctx", "head"),
            P("ctx", "head"),
        ),
        check_vma=False,
    )
```

profile of v0, /device:TPU:0, one launch (start us, length us, event | category | flops | bytes accessed | tf_op | source)
XLA Modules:
  0.0 300.2 jit_solution(14481979989713823384)
XLA Ops:
  7.3 34.1 %all_gather.27 = bf16[1024,384]{1,0:T(8,128)(2,1)S(1)} all-gather(bf16[128,384]{1,0:T(8,128)(2,1)} %param.10), channel_id=1, replica_groups=mesh['ctx'=8,'head'=4] {'ctx'}, dimensions={0}, use_global_device_ids=true | all-gather | bytes 884736 | tf_op jit(solution)/shard_map/all_gather | solution.py:52
  41.4 0.1 constant_dynamic-update-slice_fusion.1
  41.5 30.8 %all_gather.28 = bf16[256,384]{1,0:T(8,128)(2,1)S(1)} all-gather(bf16[32,384]{1,0:T(8,128)(2,1)S(1)} %copy-done.13), channel_id=1, replica_groups=mesh['ctx'=8,'head'=4] {'ctx'}, dimensions={0}, use_global_device_ids=true | all-gather | bytes 221184 | tf_op jit(solution)/shard_map/all_gather | solution.py:54
  72.3 0.1 iota_compare_fusion
  72.3 0.1 lt.45
  72.5 1.2 fusion.116
  73.7 1.2 fusion.117
  74.8 1.1 fusion.118
  76.0 32.0 %all_gather.29 = bf16[1024,384]{1,0:T(8,128)(2,1)S(1)} all-gather(bf16[128,384]{1,0:T(8,128)(2,1)S(1)} %copy-done.7), channel_id=1, replica_groups=mesh['ctx'=8,'head'=4] {'ctx'}, dimensions={0}, use_global_device_ids=true | all-gather | bytes 884736 | tf_op jit(solution)/shard_map/all_gather | solution.py:53
  108.0 0.1 constant_dynamic-update-slice_fusion.3
  108.1 30.8 %all_gather.30 = bf16[256,384]{1,0:T(8,128)(2,1)S(1)} all-gather(bf16[32,384]{1,0:T(8,128)(2,1)S(1)} %copy-done.15), channel_id=1, replica_groups=mesh['ctx'=8,'head'=4] {'ctx'}, dimensions={0}, use_global_device_ids=true | all-gather | bytes 221184 | tf_op jit(solution)/shard_map/all_gather | solution.py:55
  138.9 0.2 exponential_reduce_fusion
  139.1 0.2 exponential_reduce_fusion.1
  139.4 0.5 convolution_convert_fusion.5
  139.9 0.5 convolution_convert_fusion.6
  140.4 8.6 %all_gather.31 = bf16[128,3072]{1,0:T(8,128)(2,1)S(1)} all-gather(bf16[128,768]{1,0:T(8,128)(2,1)S(1)} %copy-done.11), channel_id=1, replica_groups=mesh['ctx'=8,'head'=4] {'head'}, dimensions={1}, use_global_device_ids=true | all-gather | bytes 983040 | tf_op jit(solution)/shard_map/all_gather | solution.py:59
  149.0 0.2 exponential_reduce_fusion.2
  149.2 0.8 convolution_convert_fusion.1
  150.0 0.5 multiply_reduce_fusion.2
  150.6 1.5 convolution_convert_fusion
  152.1 33.7 %all_gather.32 = bf16[1024,384]{1,0:T(8,128)(2,1)} all-gather(bf16[128,384]{1,0:T(8,128)(2,1)S(1)} %copy-done.12), channel_id=1, replica_groups=mesh['ctx'=8,'head'=4] {'ctx'}, dimensions={0}, use_global_device_ids=true | all-gather | bytes 884736 | tf_op jit(solution)/shard_map/all_gather | solution.py:111
  185.8 0.7 constant_dynamic-update-slice_fusion.5
  186.4 28.7 %all_gather.34 = bf16[1024,384]{0,1:T(8,128)(2,1)S(1)} all-gather(bf16[128,384]{0,1:T(8,128)(2,1)S(1)} %convolution_convert_fusion.1), channel_id=1, replica_groups=mesh['ctx'=8,'head'=4] {'ctx'}, dimensions={0}, use_global_device_ids=true | all-gather | bytes 884736 | tf_op jit(solution)/shard_map/all_gather | solution.py:112
  215.1 2.4 fusion.36
  217.5 2.4 fusion.37
  220.0 2.4 fusion.38
  222.4 26.0 %all_gather.33 = f32[3,1024]{1,0:T(4,128)S(1)} all-gather(f32[3,128]{1,0:T(4,128)S(1)} %pad_maximum_fusion.3), channel_id=1, replica_groups=mesh['ctx'=8,'head'=4] {'ctx'}, dimensions={1}, use_global_device_ids=true | all-gather | bytes 13824 | tf_op jit(solution)/shard_map/all_gather | solution.py:102
  248.4 0.6 fusion.112
  249.0 0.6 iota_compare_fusion.1
  249.7 0.6 constant_dynamic-update-slice_fusion.4
  250.3 26.0 %all_gather.35 = f32[3,1024]{1,0:T(4,128)S(1)} all-gather(f32[3,128]{1,0:T(4,128)S(1)} %pad_maximum_fusion.4), channel_id=1, replica_groups=mesh['ctx'=8,'head'=4] {'ctx'}, dimensions={1}, use_global_device_ids=true | all-gather | bytes 13824 | tf_op jit(solution)/shard_map/all_gather | solution.py:103
  276.4 1.3 fusion.23
  277.7 1.4 fusion.22
  279.1 0.3 convolution_convert_fusion.2
  279.4 0.5 copy-done.9
  279.8 0.3 convolution_convert_fusion.3
  280.1 1.4 fusion.30
  281.5 1.4 fusion.31
  282.9 2.0 fusion.21
  284.9 1.4 fusion.32
  286.4 0.7 slice.163
  287.0 0.6 slice.165
  287.6 0.8 pad_maximum_fusion.1
  288.4 0.8 copy.16
  289.2 1.2 convolution_convert_fusion.4
  290.5 0.7 slice.164
  291.1 0.6 pad_maximum_fusion.2
  291.7 1.6 convert_convert_fusion
  (58 shorter events, 0.4 us)
Async XLA Ops:
  7.2 142.1 %copy-start = (bf16[384,3072]{1,0:T(8,128)(2,1)S(1)}, bf16[384,3072]{1,0:T(8,128)(2,1)}, u32[]{:S(2)}) copy-start(bf16[384,3072]{1,0:T(8,128)(2,1)} %param.16) | copy-start | bytes 7077892
  7.2 65.1 %copy-start.18 = (s32[8,2]{0,1:T(2,128)S(1)}, s32[8,2]{0,1:T(2,128)}, u32[]{:S(2)}) copy-start(s32[8,2]{0,1:T(2,128)} %param.14) | copy-start | bytes 196
  7.2 65.1 %copy-start.19 = (s32[8]{0:T(128)S(1)}, s32[8]{0:T(128)}, u32[]{:S(2)}) copy-start(s32[8]{0:T(128)} %param.15) | copy-start | bytes 100
  7.2 284.5 %all-reduce.4.cloned.1.call-start = ((), (), s32[]{:S(2)}) async-start(), calls=%async_computation | async-start | bytes 1572864 | tf_op jit(solution)/shard_map/psum | solution.py:97
  7.2 34.2 %copy-start.13 = (bf16[32,384]{1,0:T(8,128)(2,1)S(1)}, bf16[32,384]{1,0:T(8,128)(2,1)}, u32[]{:S(2)}) copy-start(bf16[32,384]{1,0:T(8,128)(2,1)} %param.12) | copy-start | bytes 73732
  72.4 3.5 %copy-start.7 = (bf16[128,384]{1,0:T(8,128)(2,1)S(1)}, bf16[128,384]{1,0:T(8,128)(2,1)}, u32[]{:S(2)}) copy-start(bf16[128,384]{1,0:T(8,128)(2,1)} %param.11) | copy-start | bytes 294916
  72.5 35.6 %copy-start.5 = (bf16[1280,384]{1,0:T(8,128)(2,1)}, bf16[1280,384]{1,0:T(8,128)(2,1)S(1)}, u32[]{:S(2)}) copy-start(bf16[1280,384]{1,0:T(8,128)(2,1)S(1)} %constant_dynamic-update-slice_fusion) | copy-start | bytes 2949124
  73.7 65.7 %copy-start.2 = (f32[1280,128]{1,0:T(8,128)}, f32[1280,128]{1,0:T(8,128)S(1)}, u32[]{:S(2)}) copy-start(f32[1280,128]{1,0:T(8,128)S(1)} %get-tuple-element.22) | copy-start | bytes 1966084
  73.7 34.5 %copy-start.15 = (bf16[32,384]{1,0:T(8,128)(2,1)S(1)}, bf16[32,384]{1,0:T(8,128)(2,1)}, u32[]{:S(2)}) copy-start(bf16[32,384]{1,0:T(8,128)(2,1)} %param.13) | copy-start | bytes 73732
  74.8 65.0 %copy-start.3 = (f32[1280,128]{1,0:T(8,128)}, f32[1280,128]{1,0:T(8,128)S(1)}, u32[]{:S(2)}) copy-start(f32[1280,128]{1,0:T(8,128)S(1)} %get-tuple-element.24) | copy-start | bytes 1966084
  76.0 74.1 %copy-start.1 = (f32[1280,128]{1,0:T(8,128)}, f32[1280,128]{1,0:T(8,128)S(1)}, u32[]{:S(2)}) copy-start(f32[1280,128]{1,0:T(8,128)S(1)} %get-tuple-element.26) | copy-start | bytes 1966084
  108.1 32.3 %copy-start.11 = (bf16[128,768]{1,0:T(8,128)(2,1)S(1)}, bf16[128,768]{1,0:T(8,128)(2,1)}, u32[]{:S(2)}) copy-start(bf16[128,768]{1,0:T(8,128)(2,1)} %param.17) | copy-start | bytes 589828
  139.3 10.7 %copy-start.4 = (bf16[1280,384]{1,0:T(8,128)(2,1)}, bf16[1280,384]{1,0:T(8,128)(2,1)S(1)}, u32[]{:S(2)}) copy-start(bf16[1280,384]{1,0:T(8,128)(2,1)S(1)} %constant_dynamic-update-slice_fusion.2) | copy-start | bytes 2949124
  150.5 1.6 copy-start.12
  150.5 35.2 %copy-start.6 = (bf16[128,384]{1,0:T(8,128)(2,1)S(1)}, bf16[128,384]{1,0:T(8,128)(2,1)}, u32[]{:S(2)}) copy-start(bf16[128,384]{1,0:T(8,128)(2,1)} %param.10) | copy-start | bytes 294916
  150.5 64.6 %copy-start.8 = (bf16[128,384]{1,0:T(8,128)(2,1)S(1)}, bf16[128,384]{1,0:T(8,128)(2,1)}, u32[]{:S(2)}) copy-start(bf16[128,384]{1,0:T(8,128)(2,1)} %param.11) | copy-start | bytes 294916
  217.5 32.1 %copy-start.14 = (bf16[32,384]{1,0:T(8,128)(2,1)S(1)}, bf16[32,384]{1,0:T(8,128)(2,1)}, u32[]{:S(2)}) copy-start(bf16[32,384]{1,0:T(8,128)(2,1)} %param.12) | copy-start | bytes 73732
  217.5 58.8 %copy-start.16 = (bf16[32,384]{1,0:T(8,128)(2,1)S(1)}, bf16[32,384]{1,0:T(8,128)(2,1)}, u32[]{:S(2)}) copy-start(bf16[32,384]{1,0:T(8,128)(2,1)} %param.13) | copy-start | bytes 73732
  276.4 5.2 %copy-start.17 = (bf16[160,384]{1,0:T(8,128)(2,1)}, bf16[160,384]{1,0:T(8,128)(2,1)S(1)}, u32[]{:S(2)}) copy-start(bf16[160,384]{1,0:T(8,128)(2,1)S(1)} %constant_dynamic-update-slice_fusion.6) | copy-start | bytes 368644
  277.7 2.4 copy-start.10
  279.1 0.7 copy-start.9
Sparse Core Ops, SparseCore 0:
  152.2 34.8 all-reduce.3
where the time goes:
time: 301 us; the launch traced here: 300 us
  blocking collectives  251 us (83%)
  matrix products  25.1 us (8%)
  between operations  14.4 us (5%)
  other arithmetic  5.07 us (2%)
  local copies, waits for them, and re-layouts  4.85 us (2%)
    all_gather x1, blocking collectives, shards(): lax.all_gather(sec_k, 'ctx', axis=0, tiled=True)  34.1 us
    all_gather x1, blocking collectives, shards(): query_piece = lax.all_gather(sec_q, 'ctx', axis=0, tiled=True)  33.7 us
    all_gather x1, blocking collectives, shards(): lax.all_gather(sec_v, 'ctx', axis=0, tiled=True)  32 us
    all_gather x1, blocking collectives, shards(): lax.all_gather(hist_k, 'ctx', axis=0, tiled=True)  30.8 us
    all_gather x1, blocking collectives, shards(): lax.all_gather(hist_v, 'ctx', axis=0, tiled=True)  30.8 us
    all_gather x1, blocking collectives, shards(): dattn_piece = lax.all_gather(d_attn, 'ctx', axis=0, tiled=True)  28.7 us
    all_gather x1, blocking collectives, shards(): lax.all_gather(jnp.stack(log_totals, 0), 'ctx', axis=1, tiled=True)  26 us
    all_gather x1, blocking collectives, shards(): lax.all_gather(jnp.stack(row_deltas, 0), 'ctx', axis=1, tiled=True)  26 us
  transfers between devices with their start and end apart: 1, of which 0 were waited for; matrix products, arithmetic and copies ran while one was open for 8% of the time, Pallas kernels for 0%

commit v1 on v0

v1 whole, which is shorter than its diff:
```python
import math

import jax
import jax.numpy as jnp
from jax import lax
from jax.sharding import PartitionSpec as P

HDIM = 128
FTOK = 16
FMAX = 2
NEG_FILL = -1e30
AXES = ("ctx", "head")


def contract_rows(left_side, right_side):
    return lax.dot_general(
        left_side, right_side, (((0,), (0,)), ((), ())), preferred_element_type=jnp.float32
    )


def contract_cols(left_side, right_side):
    return lax.dot_general(
        left_side, right_side, (((1,), (1,)), ((), ())), preferred_element_type=jnp.float32
    )


def head_slice(stacked, head_idx):
    return stacked[:, head_idx * HDIM : (head_idx + 1) * HDIM]


def owner_token_counts(frame_levels, frame_counts):
    frame_index = jnp.arange(FMAX, dtype=jnp.int32)[None, :]
    per_frame = jnp.where(
        frame_index < frame_counts[:, None], jnp.right_shift(jnp.int32(FTOK), 2 * frame_levels), 0
    )
    return jnp.sum(per_frame, axis=1)


def from_ahead(block, axis, step):
    count = lax.axis_size(axis)
    return lax.ppermute(block, axis, [((i + step) % count, i) for i in range(count)])


def gather_direct(block, axis, dim):
    count = lax.axis_size(axis)
    parts = [block] + [from_ahead(block, axis, step) for step in range(1, count)]
    doubled = jnp.concatenate(parts + parts[:-1], axis=dim)
    size = block.shape[dim]
    first = lax.rem(count - lax.axis_index(axis), count)
    return lax.dynamic_slice_in_dim(doubled, first * size, count * size, dim)


def reduce_direct(partial, axis):
    count = lax.axis_size(axis)
    me = lax.axis_index(axis)
    size = partial.shape[1] // count
    total = None
    for step in range(count):
        share = lax.dynamic_slice_in_dim(partial, lax.rem(me + step, count) * size, size, 1)
        if step:
            share = lax.ppermute(
                share.astype(jnp.bfloat16), axis, [(i, (i + step) % count) for i in range(count)]
            ).astype(jnp.float32)
        total = share if total is None else total + share
    return total


def shards(sec_q, sec_k, sec_v, hist_k, hist_v, frame_levels, frame_counts, w_out, grad_out):
    score_scale = 1.0 / math.sqrt(HDIM)
    rows = sec_q.shape[0]
    width = sec_q.shape[1]
    heads_here = width // HDIM
    capacity = hist_k.shape[0]
    owners = lax.axis_size("ctx")
    me = lax.axis_index("ctx")
    small = owners <= 8

    grad_full = gather_direct(grad_out, "head", 1)
    packed = jnp.concatenate([sec_q, sec_k, sec_v, hist_k, hist_v], axis=0)
    every = lax.all_gather(packed, "ctx", axis=0, tiled=False)
    all_queries = every[:, :rows].reshape(owners * rows, width)
    all_keys = every[:, rows : 2 * rows].reshape(owners * rows, width)
    all_values = every[:, 2 * rows : 3 * rows].reshape(owners * rows, width)
    all_hist_k = every[:, 3 * rows : 3 * rows + capacity].reshape(owners * capacity, width)
    all_hist_v = every[:, 3 * rows + capacity :].reshape(owners * capacity, width)
    all_keys = jnp.concatenate([all_keys, all_hist_k], axis=0)
    all_values = jnp.concatenate([all_values, all_hist_v], axis=0)
    d_attn = contract_cols(grad_full, w_out).astype(jnp.bfloat16)
    if small:
        all_dattn = gather_direct(d_attn, "ctx", 0)
    else:
        all_dattn = lax.all_gather(d_attn, "ctx", axis=0, tiled=True)

    owner_tokens = owner_token_counts(frame_levels, frame_counts)
    slot_index = jnp.arange(capacity, dtype=jnp.int32)
    hist_valid = (slot_index[None, :] < owner_tokens[:, None]).reshape(owners * capacity)
    key_valid = jnp.concatenate([jnp.ones((owners * rows,), dtype=bool), hist_valid])
    own_count = jnp.sum(jnp.where(jnp.arange(owners, dtype=jnp.int32) == me, owner_tokens, 0))
    own_valid = jnp.concatenate([jnp.ones((rows,), dtype=bool), slot_index < own_count])
    own_keys = jnp.concatenate([sec_k, hist_k], axis=0)
    own_values = jnp.concatenate([sec_v, hist_v], axis=0)

    def totals(query, key, value, dattn):
        scores = contract_cols(query, key) * score_scale
        scores = jnp.where(key_valid[None, :], scores, NEG_FILL)
        top = jnp.max(scores, axis=1, keepdims=True)
        weights = jnp.exp(scores - top)
        total = jnp.sum(weights, axis=1, keepdims=True)
        dprobs = contract_cols(dattn, value)
        delta = jnp.sum(weights * dprobs, axis=1, keepdims=True) / total
        return top + jnp.log(total), delta

    attn_parts, grad_q_parts, key_parts, value_parts = [], [], [], []
    for head in range(heads_here):
        query, key, value, dattn = (
            head_slice(a, head) for a in (all_queries, all_keys, all_values, all_dattn)
        )
        if small:
            lse, delta = totals(query, key, value, dattn)
        else:
            own = totals(head_slice(sec_q, head), key, value, head_slice(d_attn, head))
            lse, delta = (lax.all_gather(a, "ctx", axis=0, tiled=True) for a in own)
        my_lse = lax.dynamic_slice_in_dim(lse, me * rows, rows, 0)
        my_delta = lax.dynamic_slice_in_dim(delta, me * rows, rows, 0)

        def probs_and_dscores(q, k, v, d, valid, lse, delta):
            scores = contract_cols(q, k) * score_scale
            probs = jnp.where(valid[None, :], jnp.exp(scores - lse), 0.0).astype(jnp.bfloat16)
            dprobs = contract_cols(d, v)
            return probs, (probs.astype(jnp.float32) * (dprobs - delta)).astype(jnp.bfloat16)

        probs, dscores = probs_and_dscores(
            head_slice(sec_q, head), key, value, head_slice(d_attn, head), key_valid, my_lse, my_delta
        )
        attn_parts.append(jnp.dot(probs, value, preferred_element_type=jnp.float32))
        grad_q_parts.append(jnp.dot(dscores, key, preferred_element_type=jnp.float32))
        probs, dscores = probs_and_dscores(
            query, head_slice(own_keys, head), head_slice(own_values, head), dattn, own_valid, lse, delta
        )
        key_parts.append(contract_rows(dscores, query))
        value_parts.append(contract_rows(probs, dattn))

    attn = jnp.concatenate(attn_parts, axis=1).astype(jnp.bfloat16)
    partial_out = jnp.dot(attn, w_out, preferred_element_type=jnp.float32)
    out = reduce_direct(partial_out, "head").astype(jnp.bfloat16)
    grad_q = (jnp.concatenate(grad_q_parts, axis=1) * score_scale).astype(jnp.bfloat16)
    grad_keys = (jnp.concatenate(key_parts, axis=1) * score_scale).astype(jnp.bfloat16)
    grad_values = jnp.concatenate(value_parts, axis=1).astype(jnp.bfloat16)
    return (
        out,
        grad_q,
        grad_keys[:rows],
        grad_values[:rows],
        grad_keys[rows:],
        grad_values[rows:],
    )


def solution(mesh):
    split = P("ctx", "head")
    return jax.shard_map(
        shards,
        mesh=mesh,
        in_specs=(split,) * 5 + (P(), P(), P("head", None), split),
        out_specs=(split,) * 6,
        check_vma=False,
    )
```

time: 301 us -> 155 us (0.51)
  blocking collectives: 251 us -> 0 us
  waiting for transfers between devices: 0.02 us -> 38.8 us
  starting transfers between devices: 0.04 us -> 26.9 us
  local copies, waits for them, and re-layouts: 4.85 us -> 27.3 us
  matrix products: 25.1 us -> 36.2 us
  other arithmetic: 5.07 us -> 10.7 us
    all_gather x9 -> x0, blocking collectives: 251 us -> none  [the longest x1 34.1 us: shards(): lax.all_gather(sec_k, 'ctx', axis=0, tiled=True)]
    ppermute x0 -> x13, waiting for transfers between devices: none -> 29.1 us  [the longest x10 22.2 us: from_ahead(): lax.ppermute(block, axis, [((i + step) % count, i) for i in range(count)])]
    ppermute x0 -> x13, starting transfers between devices: none -> 26.9 us  [the longest x10 23.6 us: from_ahead(): lax.ppermute(block, axis, [((i + step) % count, i) for i in range(count)])]
    unnamed x45 -> x81, local copies, waits for them, and re-layouts: 2.12 us -> 16.2 us
    all_gather x0 -> x1, waiting for transfers between devices: none -> 9.61 us  [shards(): every = lax.all_gather(packed, 'ctx', axis=0, tiled=False)]
    dot_general x7 -> x13, matrix products: 8.89 us -> 16.7 us  [contract_cols(): lax.dot_general(left_side, right_side, (((1,), (1,)), ((), ())), preferre...]
    dot_general x6, matrix products: 5.99 us -> 9.95 us  [contract_rows(): lax.dot_general(left_side, right_side, (((0,), (0,)), ((), ())), preferre...]
    another operation x0 -> x6, local copies, waits for them, and re-layouts: none -> 3.81 us
  transfers between devices with their start and end apart: 1 -> 14, of which waited for: 0 -> 7; matrix products, arithmetic and copies ran while one was open for 8% -> 9% of each run, Pallas kernels for 0% -> 0%
where the time goes in v1:
time: 155 us; the launch traced here: 154 us
  waiting for transfers between devices  38.8 us (25%)
  matrix products  36.2 us (23%)
  local copies, waits for them, and re-layouts  27.3 us (18%)
  starting transfers between devices  26.9 us (17%)
  between operations  14.5 us (9%)
  other arithmetic  10.7 us (7%)
    ppermute x10, starting transfers between devices, from_ahead(): lax.ppermute(block, axis, [((i + step) % count, i) for i in range(count)])  23.6 us
    ppermute x10, waiting for transfers between devices, from_ahead(): lax.ppermute(block, axis, [((i + step) % count, i) for i in range(count)])  22.2 us
    dot_general x13, matrix products, contract_cols(): lax.dot_general(left_side, right_side, (((1,), (1,)), ((), ())), preferre...  16.7 us
    unnamed x81, local copies, waits for them, and re-layouts  16.2 us
    dot_general x6, matrix products, contract_rows(): lax.dot_general(left_side, right_side, (((0,), (0,)), ((), ())), preferre...  9.95 us
    all_gather x1, waiting for transfers between devices, shards(): every = lax.all_gather(packed, 'ctx', axis=0, tiled=False)  9.61 us
    ppermute x3, waiting for transfers between devices, reduce_direct(): lax.ppermute(share.astype(jnp.bfloat16), axis, [(i, (i + step) % count) f...  6.9 us
    dot_general x3, matrix products, shards(): jnp.dot(dscores, key, preferred_element_type=jnp.float32)  6.07 us
  transfers between devices with their start and end apart: 14, of which 7 were waited for; matrix products, arithmetic and copies ran while one was open for 9% of the time, Pallas kernels for 0%

profile of v1, /device:TPU:0, one launch (start us, length us, event | category | flops | bytes accessed | tf_op | source)
XLA Modules:
  0.0 154.5 jit_solution(12398320280349701462)
XLA Ops:
  7.2 1.1 constant_dynamic-update-slice_fusion.4
  8.3 0.9 constant_dynamic-update-slice_fusion.28
  9.3 0.9 constant_dynamic-update-slice_fusion.30
  12.5 3.0 %collective-permute-start.4 = (bf16[128,768]{1,0:T(8,128)(2,1)}, bf16[128,768]{1,0:T(8,128)(2,1)S(1)}, u32[]{:S(2)}, u32[]{:S(2)}) collective-permute-start(bf16[128,768]{1,0:T(8,128)(2,1)} %param.17), channel_id=1, source_target_pairs={{2,0},{3,1},{0,2},{1,3},{6,4},{7,5},{4,6},{5,7},{10,8},{11,9},{8,1... | collective-permute-start | bytes 589832 | tf_op jit(solution)/shard_map/ppermute | solution.py:41
  17.5 6.7 %collective-permute-done.3 = bf16[128,768]{1,0:T(8,128)(2,1)S(1)} collective-permute-done((bf16[128,768]{1,0:T(8,128)(2,1)}, bf16[128,768]{1,0:T(8,128)(2,1)S(1)}, u32[]{:S(2)}, u32[]{:S(2)}) %collective-permute-start.3) | collective-permute-done | bytes 196640 | tf_op jit(solution)/shard_map/ppermute | solution.py:41
  24.4 1.5 constant_dynamic-update-slice_fusion.26
  25.8 4.6 %collective-permute-start.6 = (bf16[128,384]{1,0:T(8,128)(2,1)S(1)}, bf16[128,384]{1,0:T(8,128)(2,1)S(1)}, u32[]{:S(2)}, u32[]{:S(2)}) collective-permute-start(bf16[128,384]{1,0:T(8,128)(2,1)S(1)} %get-tuple-element.43), channel_id=1, source_target_pairs={{4,0},{8,4},{12,8},{16,12},{20,16},{24,20},{28,24},{0,28},{5,1},{9... | collective-permute-start | bytes 294920 | tf_op jit(solution)/shard_map/ppermute | solution.py:41
  31.3 2.4 %collective-permute-start.10 = (bf16[128,384]{1,0:T(8,128)(2,1)S(1)}, bf16[128,384]{1,0:T(8,128)(2,1)S(1)}, u32[]{:S(2)}, u32[]{:S(2)}) collective-permute-start(bf16[128,384]{1,0:T(8,128)(2,1)S(1)} %get-tuple-element.43), channel_id=1, source_target_pairs={{20,0},{24,4},{28,8},{0,12},{4,16},{8,20},{12,24},{16,28},{21,1},{... | collective-permute-start | bytes 294920 | tf_op jit(solution)/shard_map/ppermute | solution.py:41
  33.7 2.8 %collective-permute-start.9 = (bf16[128,384]{1,0:T(8,128)(2,1)S(1)}, bf16[128,384]{1,0:T(8,128)(2,1)S(1)}, u32[]{:S(2)}, u32[]{:S(2)}) collective-permute-start(bf16[128,384]{1,0:T(8,128)(2,1)S(1)} %get-tuple-element.43), channel_id=1, source_target_pairs={{16,0},{20,4},{24,8},{28,12},{0,16},{4,20},{8,24},{12,28},{17,1},{... | collective-permute-start | bytes 294920 | tf_op jit(solution)/shard_map/ppermute | solution.py:41
  36.5 2.9 %collective-permute-start.7 = (bf16[128,384]{1,0:T(8,128)(2,1)S(1)}, bf16[128,384]{1,0:T(8,128)(2,1)S(1)}, u32[]{:S(2)}, u32[]{:S(2)}) collective-permute-start(bf16[128,384]{1,0:T(8,128)(2,1)S(1)} %get-tuple-element.43), channel_id=1, source_target_pairs={{8,0},{12,4},{16,8},{20,12},{24,16},{28,20},{0,24},{4,28},{9,1},{1... | collective-permute-start | bytes 294920 | tf_op jit(solution)/shard_map/ppermute | solution.py:41
  40.0 6.6 %collective-permute-done.7 = bf16[128,384]{1,0:T(8,128)(2,1)S(1)} collective-permute-done((bf16[128,384]{1,0:T(8,128)(2,1)S(1)}, bf16[128,384]{1,0:T(8,128)(2,1)S(1)}, u32[]{:S(2)}, u32[]{:S(2)}) %collective-permute-start.7) | collective-permute-done | bytes 98336 | tf_op jit(solution)/shard_map/ppermute | solution.py:41
  46.7 7.3 %collective-permute-start.8 = (bf16[128,384]{1,0:T(8,128)(2,1)S(1)}, bf16[128,384]{1,0:T(8,128)(2,1)S(1)}, u32[]{:S(2)}, u32[]{:S(2)}) collective-permute-start(bf16[128,384]{1,0:T(8,128)(2,1)S(1)} %get-tuple-element.43), channel_id=1, source_target_pairs={{12,0},{16,4},{20,8},{24,12},{28,16},{0,20},{4,24},{8,28},{13,1},{... | collective-permute-start | bytes 294920 | tf_op jit(solution)/shard_map/ppermute | solution.py:41
  54.6 8.9 %collective-permute-done.8 = bf16[128,384]{1,0:T(8,128)(2,1)S(1)} collective-permute-done((bf16[128,384]{1,0:T(8,128)(2,1)S(1)}, bf16[128,384]{1,0:T(8,128)(2,1)S(1)}, u32[]{:S(2)}, u32[]{:S(2)}) %collective-permute-start.8) | collective-permute-done | bytes 98336 | tf_op jit(solution)/shard_map/ppermute | solution.py:41
  71.4 9.6 %all-gather.3.cloned.1.call-done = bf16[3584,384]{1,0:T(8,128)(2,1)} async-done(((bf16[448,384]{1,0:T(8,128)(2,1)}), bf16[3584,384]{1,0:T(8,128)(2,1)}) %all-gather.3.cloned.1.call-update) | async-done | bytes 2752528 | tf_op jit(solution)/shard_map/all_gather | solution.py:80
  81.0 1.1 fusion.121
  82.0 1.9 %fusion.120 = (bf16[8,128,384]{2,1,0:T(8,128)(2,1)S(1)}, bf16[8,128,384]{2,1,0:T(8,128)(2,1)S(1)}, bf16[8,128,384]{2,1,0:T(8,128)(2,1)S(1)}) fusion(bf16[8,448,384]{2,1,0:T(8,128)(2,1)} %bitcast.59), kind=kLoop, calls=%fused_computation.194 | loop fusion | bytes 4718592 | tf_op jit(solution)/shard_map/slice | solution.py:83
  83.9 0.9 fusion.58
  84.8 1.0 fusion.127
  85.9 1.0 fusion.125
  87.1 1.1 fusion
  88.7 1.1 multiply_reduce_fusion.2
  90.5 1.1 fusion.2
  91.6 1.1 multiply_reduce_fusion
  93.7 1.1 fusion.37
  95.6 2.1 %fusion.44 = f32[160,128]{1,0:T(8,128)} fusion(bf16[1024,160]{0,1:T(8,128)(2,1)} %copy-done.17, f32[1024]{0:T(1024)S(1)} %get-tuple-element.34, bf16[1024,384]{1,0:T(8,128)(2,1)S(1)} %bitcast.51, bf16[1920,384]{1,0:T(8,128)(2,1)} %constant_dynamic-update-slice_fusion.12, s32[]{:T(128)S(6)} %select_n.89, bf16[160,384]{1,0:T(8,128)(2,1)} %copy-done.18), kind=kOutput, calls=%fused_computation.69 | convolution fusion | flops 84541440 | bytes 978948 | tf_op jit(solution)/shard_map/dot_general | solution.py:16
  98.4 1.3 convolution_convert_fusion.1
  99.7 2.1 %fusion.42 = f32[160,128]{1,0:T(8,128)} fusion(bf16[1024,160]{0,1:T(8,128)(2,1)} %fusion.37, f32[1024]{0:T(1024)} %copy-done.25, bf16[1024,384]{1,0:T(8,128)(2,1)S(1)} %bitcast.52, bf16[1920,384]{1,0:T(8,128)(2,1)} %constant_dynamic-update-slice_fusion.12, s32[]{:T(128)S(6)} %select_n.89, s32[]{:T(128)S(6)} %add.100, bf16[160,384]{1,0:T(8,128)(2,1)} %copy-done.18), kind=kOutput, calls=%fused_computation.67 | convolution fusion | flops 84541440 | bytes 978952 | tf_op jit(solution)/shard_map/dot_general | solution.py:16
  101.8 2.0 %fusion.126 = (f32[1024]{0:T(1024)S(1)}, f32[1024,1280]{1,0:T(8,128)S(1)}) fusion(bf16[1280,128]{1,0:T(8,128)(2,1)} %get-tuple-element.25, bf16[1024,384]{1,0:T(8,128)(2,1)S(1)} %bitcast.53, pred[1280]{0:T(1024)(128)(4,1)} %copy-done.24), kind=kOutput, calls=%fused_computation.200 | convolution fusion | flops 339475456 | bytes 5838080 | tf_op jit(solution)/shard_map/dot_general | solution.py:22
  103.8 1.1 fusion.1
  104.8 2.0 %multiply_reduce_fusion.1 = f32[1024]{0:T(1024)S(1)} fusion(bf16[1280,128]{1,0:T(8,128)(2,1)S(1)} %get-tuple-element.22, f32[1024,1280]{1,0:T(8,128)S(1)} %get-tuple-element.45, f32[1024]{0:T(1024)S(1)} %get-tuple-element.44, bf16[1920,384]{1,0:T(8,128)(2,1)} %constant_dynamic-update-slice_fusion.12, s32[]{:T(128)S(6)} %select_n.89, s32[]{:T(128)S(6)} %add.99), kind=kOutput, calls=%fused_computation.1 | convolution fusion | flops 339475456 | bytes 5840904 | tf_op jit(solution)/shard_map/dot_general | solution.py:22
  107.6 1.8 %fusion.35 = bf16[1024,160]{0,1:T(8,128)(2,1)} fusion(f32[1024]{0:T(1024)S(1)} %get-tuple-element.37, pred[160]{0:T(512)(128)(4,1)S(1)} %copy-done.28, bf16[1024,384]{1,0:T(8,128)(2,1)S(1)} %bitcast.54, bf16[160,384]{1,0:T(8,128)(2,1)} %copy-done.19), kind=kOutput, calls=%fused_computation.60 | convolution fusion | flops 42598400 | bytes 635392 | tf_op jit(solution)/shard_map/dot_general | solution.py:22
  110.0 2.3 %fusion.43 = f32[160,128]{1,0:T(8,128)} fusion(bf16[1024,160]{0,1:T(8,128)(2,1)} %fusion.35, f32[1024]{0:T(1024)} %copy-done.26, bf16[1024,384]{1,0:T(8,128)(2,1)S(1)} %bitcast.55, bf16[1920,384]{1,0:T(8,128)(2,1)} %constant_dynamic-update-slice_fusion.12, s32[]{:T(128)S(6)} %select_n.89, s32[]{:T(128)S(6)} %add.99, bf16[160,384]{1,0:T(8,128)(2,1)} %copy-done.18), kind=kOutput, calls=%fused_computation.68 | convolution fusion | flops 84541440 | bytes 978952 | tf_op jit(solution)/shard_map/dot_general | solution.py:16
  112.3 1.9 %convolution_convert_fusion.2 = bf16[160,128]{1,0:T(8,128)(2,1)} fusion(bf16[1024,160]{0,1:T(8,128)(2,1)} %fusion.35, bf16[1920,384]{1,0:T(8,128)(2,1)} %constant_dynamic-update-slice_fusion.12, s32[]{:T(128)S(6)} %select_n.89, s32[]{:T(128)S(6)} %add.99), kind=kOutput, calls=%fused_computation.72 | convolution fusion | flops 41963520 | bytes 630792 | tf_op jit(solution)/shard_map/dot_general | solution.py:16
  114.2 1.0 fusion.65
  116.5 1.3 fusion.17
  118.9 2.2 %fusion.41 = f32[128,128]{0,1:T(8,128)} fusion(bf16[1280,128]{1,0:T(8,128)(2,1)} %copy-done.9, bf16[1280,128]{1,0:T(8,128)(2,1)S(1)} %copy-done.5, bf16[1280,128]{1,0:T(8,128)(2,1)} %copy-done.15, f32[128]{0:T(128)} %dynamic-slice.21, bf16[128,384]{1,0:T(8,128)(2,1)S(1)} %copy-done.13), kind=kOutput, calls=%fused_computation.66 | convolution fusion | flops 84541440 | bytes 1081856 | tf_op jit(solution)/shard_map/dot_general | solution.py:136
  121.1 1.4 fusion.15
  123.2 0.9 convolution_convert_fusion.4
  124.1 2.2 %fusion.39 = f32[128,128]{0,1:T(8,128)} fusion(bf16[1280,128]{1,0:T(8,128)(2,1)} %copy-done.8, bf16[1280,128]{1,0:T(8,128)(2,1)S(1)} %copy-done.3, bf16[1280,128]{1,0:T(8,128)(2,1)} %copy-done.16, f32[128]{0:T(128)} %dynamic-slice.23, bf16[128,384]{1,0:T(8,128)(2,1)S(1)} %copy-done.13), kind=kOutput, calls=%fused_computation.64 | convolution fusion | flops 84541440 | bytes 1081856 | tf_op jit(solution)/shard_map/dot_general | solution.py:136
  127.7 1.1 fusion.16
  129.7 1.7 %fusion.40 = f32[128,128]{0,1:T(8,128)} fusion(bf16[1280,128]{1,0:T(8,128)(2,1)S(1)} %copy-done.7, bf16[1280,128]{1,0:T(8,128)(2,1)S(1)} %get-tuple-element.22, bf16[1280,128]{1,0:T(8,128)(2,1)S(1)} %fusion.16, f32[128]{0:T(128)} %dynamic-slice.22, bf16[128,384]{1,0:T(8,128)(2,1)S(1)} %copy-done.13), kind=kOutput, calls=%fused_computation.65 | convolution fusion | flops 84541440 | bytes 1081856 | tf_op jit(solution)/shard_map/dot_general | solution.py:136
  131.4 1.4 fusion.88
  132.8 1.2 copy-done.1
  134.2 1.7 %collective-permute-start.2 = (bf16[128,768]{1,0:T(8,128)(2,1)S(1)}, bf16[128,768]{1,0:T(8,128)(2,1)}, u32[]{:S(2)}, u32[]{:S(2)}) collective-permute-start(bf16[128,768]{1,0:T(8,128)(2,1)S(1)} %get-tuple-element.18), channel_id=1, source_target_pairs={{0,3},{1,0},{2,1},{3,2},{4,7},{5,4},{6,5},{7,6},{8,11},{9,8},{10,9... | collective-permute-start | bytes 589832 | tf_op jit(solution)/shard_map/ppermute | solution.py:61
  135.9 1.5 collective-permute-start.1
  139.5 1.7 %collective-permute-done.2 = bf16[128,768]{1,0:T(8,128)(2,1)} collective-permute-done((bf16[128,768]{1,0:T(8,128)(2,1)S(1)}, bf16[128,768]{1,0:T(8,128)(2,1)}, u32[]{:S(2)}, u32[]{:S(2)}) %collective-permute-start.2) | collective-permute-done | bytes 196640 | tf_op jit(solution)/shard_map/ppermute | solution.py:61
  141.1 4.5 %collective-permute-done.1 = bf16[128,768]{1,0:T(8,128)(2,1)} collective-permute-done((bf16[128,768]{1,0:T(8,128)(2,1)S(1)}, bf16[128,768]{1,0:T(8,128)(2,1)}, u32[]{:S(2)}, u32[]{:S(2)}) %collective-permute-start.1) | collective-permute-done | bytes 196640 | tf_op jit(solution)/shard_map/ppermute | solution.py:61
  145.7 2.0 %add_convert_fusion = bf16[128,768]{1,0:T(8,128)(2,1)} fusion(bf16[128,768]{1,0:T(8,128)(2,1)} %collective-permute-done.2, bf16[128,768]{1,0:T(8,128)(2,1)} %collective-permute-done.1, bf16[128,768]{1,0:T(8,128)(2,1)S(1)} %collective-permute-done, f32[128,3072]{1,0:T(8,128)} %copy-done.1, s32[]{:T(128)S(6)} %select_n.84), kind=kLoop, calls=%fused_computation.91 | loop fusion | flops 688128 | bytes 1179652 | tf_op jit(solution)/shard_map/convert_element_type | solution.py:145
  (124 shorter events, 27.2 us)
Async XLA Ops:
  7.2 17.2 %copy-start = (bf16[384,3072]{1,0:T(8,128)(2,1)S(1)}, bf16[384,3072]{1,0:T(8,128)(2,1)}, u32[]{:S(2)}) copy-start(bf16[384,3072]{1,0:T(8,128)(2,1)} %param.16) | copy-start | bytes 7077892
  7.2 9.7 %copy-start.10 = (bf16[128,768]{1,0:T(8,128)(2,1)S(1)}, bf16[128,768]{1,0:T(8,128)(2,1)}, u32[]{:S(2)}) copy-start(bf16[128,768]{1,0:T(8,128)(2,1)} %param.17) | copy-start | bytes 589828
  7.2 73.8 %all-gather.3.cloned.1.call-start = ((), (), s32[]{:S(2)}) async-start(), calls=%async_computation | async-start | bytes 3096576 | tf_op jit(solution)/shard_map/all_gather | solution.py:80
  10.9 0.8 copy-start.19
  11.7 0.7 copy-start.11
  11.7 0.8 copy-start.18
  12.5 11.7 %collective-permute-start.4 = (bf16[128,768]{1,0:T(8,128)(2,1)}, bf16[128,768]{1,0:T(8,128)(2,1)S(1)}, u32[]{:S(2)}, u32[]{:S(2)}) collective-permute-start(bf16[128,768]{1,0:T(8,128)(2,1)} %param.17), channel_id=1, source_target_pairs={{2,0},{3,1},{0,2},{1,3},{6,4},{7,5},{4,6},{5,7},{10,8},{11,9},{8,1... | collective-permute-start | bytes 589832 | tf_op jit(solution)/shard_map/ppermute | solution.py:41
  15.5 8.7 %collective-permute-start.3 = (bf16[128,768]{1,0:T(8,128)(2,1)}, bf16[128,768]{1,0:T(8,128)(2,1)S(1)}, u32[]{:S(2)}, u32[]{:S(2)}) collective-permute-start(bf16[128,768]{1,0:T(8,128)(2,1)} %param.17), channel_id=1, source_target_pairs={{1,0},{2,1},{3,2},{0,3},{5,4},{6,5},{7,6},{4,7},{9,8},{10,9},{11,1... | collective-permute-start | bytes 589832 | tf_op jit(solution)/shard_map/ppermute | solution.py:41
  15.5 8.7 %collective-permute-start.5 = (bf16[128,768]{1,0:T(8,128)(2,1)}, bf16[128,768]{1,0:T(8,128)(2,1)S(1)}, u32[]{:S(2)}, u32[]{:S(2)}) collective-permute-start(bf16[128,768]{1,0:T(8,128)(2,1)} %param.17), channel_id=1, source_target_pairs={{3,0},{0,1},{1,2},{2,3},{7,4},{4,5},{5,6},{6,7},{11,8},{8,9},{9,10... | collective-permute-start | bytes 589832 | tf_op jit(solution)/shard_map/ppermute | solution.py:41
  25.8 55.1 %copy-start.12 = (bf16[128,384]{1,0:T(8,128)(2,1)}, bf16[128,384]{1,0:T(8,128)(2,1)S(1)}, u32[]{:S(2)}) copy-start(bf16[128,384]{1,0:T(8,128)(2,1)S(1)} %get-tuple-element.43) | copy-start | bytes 294916
  25.8 10.6 %collective-permute-start.6 = (bf16[128,384]{1,0:T(8,128)(2,1)S(1)}, bf16[128,384]{1,0:T(8,128)(2,1)S(1)}, u32[]{:S(2)}, u32[]{:S(2)}) collective-permute-start(bf16[128,384]{1,0:T(8,128)(2,1)S(1)} %get-tuple-element.43), channel_id=1, source_target_pairs={{4,0},{8,4},{12,8},{16,12},{20,16},{24,20},{28,24},{0,28},{5,1},{9... | collective-permute-start | bytes 294920 | tf_op jit(solution)/shard_map/ppermute | solution.py:41
  31.1 62.6 %copy-start.27 = (pred[160]{0:T(512)(128)(4,1)}, pred[160]{0:T(512)(128)(4,1)S(1)}, u32[]{:S(2)}) copy-start(pred[160]{0:T(512)(128)(4,1)S(1)} %concatenate.49) | copy-start | bytes 484
  31.1 54.8 %copy-start.24 = (pred[1280]{0:T(1024)(128)(4,1)}, pred[1280]{0:T(1024)(128)(4,1)S(1)}, u32[]{:S(2)}) copy-start(pred[1280]{0:T(1024)(128)(4,1)S(1)} %concatenate.41) | copy-start | bytes 3844
  31.1 35.0 %collective-permute-start.12 = (bf16[128,384]{1,0:T(8,128)(2,1)S(1)}, bf16[128,384]{1,0:T(8,128)(2,1)S(1)}, u32[]{:S(2)}, u32[]{:S(2)}) collective-permute-start(bf16[128,384]{1,0:T(8,128)(2,1)S(1)} %get-tuple-element.43), channel_id=1, source_target_pairs={{28,0},{0,4},{4,8},{8,12},{12,16},{16,20},{20,24},{24,28},{29,1},{... | collective-permute-start | bytes 294920 | tf_op jit(solution)/shard_map/ppermute | solution.py:41
  31.2 34.3 %collective-permute-start.11 = (bf16[128,384]{1,0:T(8,128)(2,1)S(1)}, bf16[128,384]{1,0:T(8,128)(2,1)S(1)}, u32[]{:S(2)}, u32[]{:S(2)}) collective-permute-start(bf16[128,384]{1,0:T(8,128)(2,1)S(1)} %get-tuple-element.43), channel_id=1, source_target_pairs={{24,0},{28,4},{0,8},{4,12},{8,16},{12,20},{16,24},{20,28},{25,1},{... | collective-permute-start | bytes 294920 | tf_op jit(solution)/shard_map/ppermute | solution.py:41
  31.3 33.6 %collective-permute-start.10 = (bf16[128,384]{1,0:T(8,128)(2,1)S(1)}, bf16[128,384]{1,0:T(8,128)(2,1)S(1)}, u32[]{:S(2)}, u32[]{:S(2)}) collective-permute-start(bf16[128,384]{1,0:T(8,128)(2,1)S(1)} %get-tuple-element.43), channel_id=1, source_target_pairs={{20,0},{24,4},{28,8},{0,12},{4,16},{8,20},{12,24},{16,28},{21,1},{... | collective-permute-start | bytes 294920 | tf_op jit(solution)/shard_map/ppermute | solution.py:41
  33.7 30.6 %collective-permute-start.9 = (bf16[128,384]{1,0:T(8,128)(2,1)S(1)}, bf16[128,384]{1,0:T(8,128)(2,1)S(1)}, u32[]{:S(2)}, u32[]{:S(2)}) collective-permute-start(bf16[128,384]{1,0:T(8,128)(2,1)S(1)} %get-tuple-element.43), channel_id=1, source_target_pairs={{16,0},{20,4},{24,8},{28,12},{0,16},{4,20},{8,24},{12,28},{17,1},{... | collective-permute-start | bytes 294920 | tf_op jit(solution)/shard_map/ppermute | solution.py:41
  36.5 10.2 %collective-permute-start.7 = (bf16[128,384]{1,0:T(8,128)(2,1)S(1)}, bf16[128,384]{1,0:T(8,128)(2,1)S(1)}, u32[]{:S(2)}, u32[]{:S(2)}) collective-permute-start(bf16[128,384]{1,0:T(8,128)(2,1)S(1)} %get-tuple-element.43), channel_id=1, source_target_pairs={{8,0},{12,4},{16,8},{20,12},{24,16},{28,20},{0,24},{4,28},{9,1},{1... | collective-permute-start | bytes 294920 | tf_op jit(solution)/shard_map/ppermute | solution.py:41
  46.7 16.9 %collective-permute-start.8 = (bf16[128,384]{1,0:T(8,128)(2,1)S(1)}, bf16[128,384]{1,0:T(8,128)(2,1)S(1)}, u32[]{:S(2)}, u32[]{:S(2)}) collective-permute-start(bf16[128,384]{1,0:T(8,128)(2,1)S(1)} %get-tuple-element.43), channel_id=1, source_target_pairs={{12,0},{16,4},{20,8},{24,12},{28,16},{0,20},{4,24},{8,28},{13,1},{... | collective-permute-start | bytes 294920 | tf_op jit(solution)/shard_map/ppermute | solution.py:41
  84.8 1.0 copy-start.9
  84.8 1.0 copy-start.8
  87.1 1.1 copy-start.4
  87.1 4.4 %copy-start.2 = (bf16[1280,128]{1,0:T(8,128)(2,1)}, bf16[1280,128]{1,0:T(8,128)(2,1)S(1)}, u32[]{:S(2)}) copy-start(bf16[1280,128]{1,0:T(8,128)(2,1)S(1)} %get-tuple-element.21) | copy-start | bytes 983044
  87.1 1.6 %copy-start.6 = (bf16[1920,384]{1,0:T(8,128)(2,1)S(1)}, bf16[1920,384]{1,0:T(8,128)(2,1)}, u32[]{:S(2)}) copy-start(bf16[1920,384]{1,0:T(8,128)(2,1)} %constant_dynamic-update-slice_fusion.12) | copy-start | bytes 4423684
  91.6 1.8 %copy-start.20 = (bf16[160,384]{1,0:T(8,128)(2,1)S(1)}, bf16[160,384]{1,0:T(8,128)(2,1)}, u32[]{:S(2)}) copy-start(bf16[160,384]{1,0:T(8,128)(2,1)} %copy-done.19) | copy-start | bytes 368644
  92.7 5.0 %copy-start.25 = (f32[1024]{0:T(1024)}, f32[1024]{0:T(1024)S(1)}, u32[]{:S(2)}) copy-start(f32[1024]{0:T(1024)S(1)} %get-tuple-element.38) | copy-start | bytes 12292
  93.7 2.0 %copy-start.17 = (bf16[1024,160]{0,1:T(8,128)(2,1)}, bf16[1024,160]{0,1:T(8,128)(2,1)S(1)}, u32[]{:S(2)}) copy-start(bf16[1024,160]{0,1:T(8,128)(2,1)S(1)} %fusion.33) | copy-start | bytes 983044
  104.8 2.7 %copy-start.28 = (pred[160]{0:T(512)(128)(4,1)S(1)}, pred[160]{0:T(512)(128)(4,1)}, u32[]{:S(2)}) copy-start(pred[160]{0:T(512)(128)(4,1)} %copy-done.27) | copy-start | bytes 484
  106.9 2.5 %copy-start.26 = (f32[1024]{0:T(1024)}, f32[1024]{0:T(1024)S(1)}, u32[]{:S(2)}) copy-start(f32[1024]{0:T(1024)S(1)} %get-tuple-element.36) | copy-start | bytes 12292
  112.3 6.3 %copy-start.5 = (bf16[1280,128]{1,0:T(8,128)(2,1)S(1)}, bf16[1280,128]{1,0:T(8,128)(2,1)}, u32[]{:S(2)}) copy-start(bf16[1280,128]{1,0:T(8,128)(2,1)} %copy-done.4) | copy-start | bytes 983044
  112.3 6.6 %copy-start.13 = (bf16[128,384]{1,0:T(8,128)(2,1)S(1)}, bf16[128,384]{1,0:T(8,128)(2,1)}, u32[]{:S(2)}) copy-start(bf16[128,384]{1,0:T(8,128)(2,1)} %copy-done.12) | copy-start | bytes 294916
  117.8 0.8 copy-start.15
  118.6 4.6 %copy-start.3 = (bf16[1280,128]{1,0:T(8,128)(2,1)S(1)}, bf16[1280,128]{1,0:T(8,128)(2,1)}, u32[]{:S(2)}) copy-start(bf16[1280,128]{1,0:T(8,128)(2,1)} %copy-done.2) | copy-start | bytes 983044
  121.1 6.7 %copy-start.7 = (bf16[1280,128]{1,0:T(8,128)(2,1)S(1)}, bf16[1280,128]{1,0:T(8,128)(2,1)}, u32[]{:S(2)}) copy-start(bf16[1280,128]{1,0:T(8,128)(2,1)} %get-tuple-element.25) | copy-start | bytes 983044
  122.4 0.7 copy-start.16
  131.4 5.9 %copy-start.21 = (f32[128,128]{0,1:T(8,128)S(1)}, f32[128,128]{0,1:T(8,128)}, u32[]{:S(2)}) copy-start(f32[128,128]{0,1:T(8,128)} %fusion.41) | copy-start | bytes 196612
  131.4 5.9 %copy-start.22 = (f32[128,128]{0,1:T(8,128)S(1)}, f32[128,128]{0,1:T(8,128)}, u32[]{:S(2)}) copy-start(f32[128,128]{0,1:T(8,128)} %fusion.39) | copy-start | bytes 196612
  131.4 5.9 %copy-start.23 = (f32[128,128]{0,1:T(8,128)S(1)}, f32[128,128]{0,1:T(8,128)}, u32[]{:S(2)}) copy-start(f32[128,128]{0,1:T(8,128)} %fusion.40) | copy-start | bytes 196612
  132.8 1.2 copy-start.1
  134.0 4.1 %copy-start.14 = (bf16[160,128]{1,0:T(8,128)(2,1)S(1)}, bf16[160,128]{1,0:T(8,128)(2,1)}, u32[]{:S(2)}) copy-start(bf16[160,128]{1,0:T(8,128)(2,1)} %convolution_convert_fusion.2) | copy-start | bytes 122884
  134.1 5.4 %collective-permute-start = (bf16[128,768]{1,0:T(8,128)(2,1)S(1)}, bf16[128,768]{1,0:T(8,128)(2,1)S(1)}, u32[]{:S(2)}, u32[]{:S(2)}) collective-permute-start(bf16[128,768]{1,0:T(8,128)(2,1)S(1)} %get-tuple-element.17), channel_id=1, source_target_pairs={{0,1},{1,2},{2,3},{3,0},{4,5},{5,6},{6,7},{7,4},{8,9},{9,10},{10,1... | collective-permute-start | bytes 589832 | tf_op jit(solution)/shard_map/ppermute | solution.py:61
  134.2 7.0 %collective-permute-start.2 = (bf16[128,768]{1,0:T(8,128)(2,1)S(1)}, bf16[128,768]{1,0:T(8,128)(2,1)}, u32[]{:S(2)}, u32[]{:S(2)}) collective-permute-start(bf16[128,768]{1,0:T(8,128)(2,1)S(1)} %get-tuple-element.18), channel_id=1, source_target_pairs={{0,3},{1,0},{2,1},{3,2},{4,7},{5,4},{6,5},{7,6},{8,11},{9,8},{10,9... | collective-permute-start | bytes 589832 | tf_op jit(solution)/shard_map/ppermute | solution.py:61
  135.9 9.8 %collective-permute-start.1 = (bf16[128,768]{1,0:T(8,128)(2,1)S(1)}, bf16[128,768]{1,0:T(8,128)(2,1)}, u32[]{:S(2)}, u32[]{:S(2)}) collective-permute-start(bf16[128,768]{1,0:T(8,128)(2,1)S(1)} %get-tuple-element.19), channel_id=1, source_target_pairs={{0,2},{1,3},{2,0},{3,1},{4,6},{5,7},{6,4},{7,5},{8,10},{9,11},{10,... | collective-permute-start | bytes 589832 | tf_op jit(solution)/shard_map/ppermute | solution.py:61
Sparse Core Ops, SparseCore 0:
  12.6 68.2 all-gather.2

commit v2 on v1

v2 whole, which is shorter than its diff:
```python
import functools
import math

import jax
import jax.numpy as jnp
from jax import lax
from jax.experimental import pallas as pl
from jax.experimental.pallas import tpu as pltpu
from jax.sharding import PartitionSpec as P

HDIM = 128
FTOK = 16
FMAX = 2
NEG_FILL = -1e30
SCALE = 1.0 / math.sqrt(HDIM)
F32 = jnp.float32
BF16 = jnp.bfloat16
SQUARE = 4
PAIR = 4


def contract(left, right, left_dim, right_dim):
    return lax.dot_general(
        left, right, (((left_dim,), (right_dim,)), ((), ())), preferred_element_type=F32
    )


def head_slice(stacked, head):
    return stacked[:, head * HDIM : (head + 1) * HDIM]


def swap(block, axis, bit):
    count = lax.axis_size(axis)
    return lax.ppermute(block, axis, [(i, i ^ bit) for i in range(count)])


def local_call(body, name, out_shapes, args, tables=0, flops=0):
    spaces = [pltpu.SMEM] * tables + [pltpu.VMEM] * (len(args) - tables)
    moved = sum(a.size * a.dtype.itemsize for a in args)
    moved += sum(math.prod(o.shape) * o.dtype.itemsize for o in out_shapes)
    return pl.pallas_call(
        body,
        name=name,
        out_shape=out_shapes,
        in_specs=[pl.BlockSpec(memory_space=space) for space in spaces],
        out_specs=[pl.BlockSpec(memory_space=pltpu.VMEM)] * len(out_shapes),
        compiler_params=pltpu.CompilerParams(vmem_limit_bytes=40 * 2**20),
        cost_estimate=pl.CostEstimate(flops=flops, bytes_accessed=moved, transcendentals=0),
    )(*args)


def owner_tokens_at(levels_ref, counts_ref, owner):
    total = jnp.int32(0)
    for frame in range(FMAX):
        tokens = lax.shift_right_logical(jnp.int32(FTOK), 2 * levels_ref[owner, frame])
        total += jnp.where(frame < counts_ref[owner], tokens, 0)
    return total


def square_tokens(levels_ref, counts_ref):
    me = lax.axis_index("ctx")
    return [owner_tokens_at(levels_ref, counts_ref, me ^ step) for step in range(SQUARE)]


def pack_kernel(k_ref, hk_ref, v_ref, hv_ref, kv_ref):
    rows, capacity = k_ref.shape[0], hk_ref.shape[0]
    keys = rows + capacity
    kv_ref[:rows] = k_ref[...]
    kv_ref[rows:keys] = hk_ref[...]
    kv_ref[keys : keys + rows] = v_ref[...]
    kv_ref[keys + rows :] = hv_ref[...]


def dattn_kernel(own_ref, core_ref, near_ref, far_ref, w_ref, out_ref):
    me = lax.axis_index("head")
    size = own_ref.shape[1]
    total = None
    for step, ref in enumerate((own_ref, core_ref, near_ref, far_ref)):
        columns = pl.ds(pl.multiple_of((me ^ step) * size, HDIM), size)
        part = contract(ref[...], w_ref[:, columns], 1, 1)
        total = part if total is None else total + part
    out_ref[...] = total.astype(BF16)


def masked_scores(kv_ref, head, query, tokens, rows, keys):
    scores = contract(head_slice(kv_ref[:keys], head), query, 1, 1) * SCALE
    slot = lax.broadcasted_iota(jnp.int32, scores.shape, 0)
    return jnp.where(slot < rows + tokens, scores, NEG_FILL)


def forward_kernel(
    levels_ref, counts_ref, q_own_ref, q_pair_ref, kv0, kv1, kv2, kv3, own_ref, pair_ref, lse_ref
):
    rows = q_own_ref.shape[0]
    keys = kv0.shape[0] // 2
    tokens = square_tokens(levels_ref, counts_ref)
    lse_ref[...] = jnp.zeros_like(lse_ref)
    for head in range(q_own_ref.shape[1] // HDIM):
        query = jnp.concatenate(
            [head_slice(q_own_ref[...], head), head_slice(q_pair_ref[...], head)], axis=0
        )
        scores = [
            masked_scores(ref, head, query, count, rows, keys)
            for ref, count in zip((kv0, kv1, kv2, kv3), tokens)
        ]
        top = functools.reduce(
            jnp.maximum, [jnp.max(block, axis=0, keepdims=True) for block in scores]
        )
        weights = [jnp.exp(block - top) for block in scores]
        total = sum(jnp.sum(block, axis=0, keepdims=True) for block in weights)
        inverse = 1.0 / total
        attn = sum(
            contract(head_slice(ref[keys:], head), (block * inverse).astype(BF16), 0, 0)
            for ref, block in zip((kv0, kv1, kv2, kv3), weights)
        )
        features = slice(head * HDIM, (head + 1) * HDIM)
        own_ref[features] = attn[:, :rows]
        pair_ref[features] = attn[:, rows:].astype(BF16)
        lse_ref[head : head + 1] = top + jnp.log(total)


def merge_parts(mine, theirs):
    top = jnp.maximum(mine, theirs)
    total = top + jnp.log(jnp.exp(mine - top) + jnp.exp(theirs - top))
    return total, jnp.exp(mine - total), jnp.exp(theirs - total)


def project_kernel(own_ref, pair_ref, lse_ref, lse_pair_ref, w_ref, send_ref, next_ref, keep_ref):
    rows = own_ref.shape[1]
    parts = []
    for head in range(own_ref.shape[0] // HDIM):
        features = slice(head * HDIM, (head + 1) * HDIM)
        _, weight, weight_pair = merge_parts(
            lse_ref[head : head + 1, :rows], lse_pair_ref[head : head + 1, rows:]
        )
        parts.append(own_ref[features] * weight + pair_ref[features].astype(F32) * weight_pair)
    attn = jnp.concatenate(parts, axis=0).astype(BF16)
    me = lax.axis_index("head")
    size = keep_ref.shape[1]

    def columns_of(step):
        columns = pl.ds(pl.multiple_of((me ^ step) * size, HDIM), size)
        return contract(attn, w_ref[:, columns], 0, 0)

    send_ref[:, :size] = columns_of(1).astype(BF16)
    send_ref[:, size:] = columns_of(3).astype(BF16)
    next_ref[...] = columns_of(2)
    keep_ref[...] = columns_of(0)


def add_near_kernel(next_ref, core_ref, out_ref):
    size = next_ref.shape[1]
    out_ref[...] = (next_ref[...] + core_ref[:, size:].astype(F32)).astype(BF16)


def add_out_kernel(keep_ref, core_ref, near_ref, out_ref):
    size = keep_ref.shape[1]
    total = keep_ref[...] + core_ref[:, :size].astype(F32) + near_ref[...].astype(F32)
    out_ref[...] = total.astype(BF16)


def delta_kernel(
    levels_ref, counts_ref, q_own_ref, q_pair_ref, kv0, kv1, kv2, kv3, d_own_ref, d_pair_ref, lse_ref,
    delta_ref,
):
    rows = q_own_ref.shape[0]
    keys = kv0.shape[0] // 2
    tokens = square_tokens(levels_ref, counts_ref)
    delta_ref[...] = jnp.zeros_like(delta_ref)
    for head in range(q_own_ref.shape[1] // HDIM):
        query, dattn = (
            jnp.concatenate([head_slice(a[...], head), head_slice(b[...], head)], axis=0)
            for a, b in ((q_own_ref, q_pair_ref), (d_own_ref, d_pair_ref))
        )
        total = None
        for ref, count in zip((kv0, kv1, kv2, kv3), tokens):
            scores = masked_scores(ref, head, query, count, rows, keys)
            probs = jnp.exp(scores - lse_ref[head : head + 1])
            dprobs = contract(head_slice(ref[keys:], head), dattn, 1, 1)
            part = jnp.sum(probs * dprobs, axis=0, keepdims=True)
            total = part if total is None else total + part
        delta_ref[head : head + 1] = total


def backward_kernel(
    levels_ref, counts_ref, q_own_ref, q_pair_ref, kv0, kv1, kv2, kv3, d_own_ref, d_pair_ref,
    lse_ref, lse_pair_ref, delta_ref, delta_pair_ref,
    dq_own_ref, dq_pair_ref, dkv0, dkv1, dkv2, dkv3,
):
    rows = q_own_ref.shape[0]
    keys = kv0.shape[0] // 2
    tokens = square_tokens(levels_ref, counts_ref)

    def swapped(ref, head):
        row = ref[head : head + 1]
        return jnp.concatenate([row[:, rows:], row[:, :rows]], axis=1)

    for head in range(q_own_ref.shape[1] // HDIM):
        query, dattn = (
            jnp.concatenate([head_slice(a[...], head), head_slice(b[...], head)], axis=0)
            for a, b in ((q_own_ref, q_pair_ref), (d_own_ref, d_pair_ref))
        )
        lse, weight, weight_pair = merge_parts(lse_ref[head : head + 1], swapped(lse_pair_ref, head))
        delta = weight * delta_ref[head : head + 1] + weight_pair * swapped(delta_pair_ref, head)
        features = slice(head * HDIM, (head + 1) * HDIM)
        dquery = None
        for ref, count, out in zip((kv0, kv1, kv2, kv3), tokens, (dkv0, dkv1, dkv2, dkv3)):
            key = head_slice(ref[:keys], head)
            scores = masked_scores(ref, head, query, count, rows, keys)
            probs = jnp.exp(scores - lse).astype(BF16)
            dprobs = contract(head_slice(ref[keys:], head), dattn, 1, 1)
            dscores = (probs.astype(F32) * (dprobs - delta)).astype(BF16)
            out[:keys, features] = (contract(dscores, query, 1, 0) * SCALE).astype(out.dtype)
            out[keys:, features] = contract(probs, dattn, 1, 0).astype(out.dtype)
            part = contract(dscores, key, 0, 0)
            dquery = part if dquery is None else dquery + part
        dq_own_ref[:, features] = dquery[:rows] * SCALE
        dq_pair_ref[:, features] = (dquery[rows:] * SCALE).astype(BF16)


def add_grads_kernel(
    dq_ref, dq_pair_ref, dkv0, dkv1, dkv2, dkv3, q_out, k_out, v_out, hk_out, hv_out
):
    rows, capacity = k_out.shape[0], hk_out.shape[0]
    keys = rows + capacity
    q_out[...] = (dq_ref[...] + dq_pair_ref[...].astype(F32)).astype(BF16)

    def total(begin, size):
        part = slice(begin, begin + size)
        value = dkv0[part]
        for ref in (dkv1, dkv2, dkv3):
            value = value + ref[part].astype(F32)
        return value.astype(BF16)

    k_out[...] = total(0, rows)
    hk_out[...] = total(rows, capacity)
    v_out[...] = total(keys, rows)
    hv_out[...] = total(keys + rows, capacity)


def blocked(sec_q, sec_k, sec_v, hist_k, hist_v, frame_levels, frame_counts, w_out, grad_out):
    shape = jax.ShapeDtypeStruct
    rows, width = sec_q.shape
    heads = width // HDIM
    capacity = hist_k.shape[0]
    keys = rows + capacity
    share = grad_out.shape[1]
    tables = (frame_levels, frame_counts)
    pair_work = 2 * SQUARE * keys * 2 * rows * width

    grad_near = swap(grad_out, "head", 2)
    grad_core = swap(grad_out, "head", 1)
    kv0 = local_call(
        pack_kernel, "pack", [shape((2 * keys, width), BF16)], (sec_k, hist_k, sec_v, hist_v)
    )[0]
    kvs = [kv0] + [swap(kv0, "ctx", step) for step in range(1, SQUARE)]
    q_pair = swap(sec_q, "ctx", PAIR)
    grad_far = swap(grad_near, "head", 1)
    d_attn = local_call(
        dattn_kernel,
        "dattn",
        [shape((rows, width), BF16)],
        (grad_out, grad_core, grad_near, grad_far, w_out),
        flops=2 * rows * width * share * 4,
    )[0]
    d_pair = swap(d_attn, "ctx", PAIR)
    attn_own, attn_pair, lse = local_call(
        forward_kernel,
        "forward",
        [shape((width, rows), F32), shape((width, rows), BF16), shape((8, 2 * rows), F32)],
        (*tables, sec_q, q_pair, *kvs),
        tables=2,
        flops=2 * pair_work,
    )
    lse_pair = swap(lse, "ctx", PAIR)
    attn_got = swap(attn_pair, "ctx", PAIR)
    out_send, out_next, out_keep = local_call(
        project_kernel,
        "project",
        [shape((rows, 2 * share), BF16), shape((rows, share), F32), shape((rows, share), F32)],
        (attn_own, attn_got, lse, lse_pair, w_out),
        flops=2 * rows * width * share * 4,
    )
    out_core = swap(out_send, "head", 1)
    out_near = swap(
        local_call(add_near_kernel, "add_near", [shape((rows, share), BF16)], (out_next, out_core))[0],
        "head",
        2,
    )
    delta = local_call(
        delta_kernel,
        "delta",
        [shape((8, 2 * rows), F32)],
        (*tables, sec_q, q_pair, *kvs, d_attn, d_pair, lse),
        tables=2,
        flops=2 * pair_work,
    )[0]
    delta_pair = swap(delta, "ctx", PAIR)
    dq_own, dq_pair, *dkvs = local_call(
        backward_kernel,
        "backward",
        [shape((rows, width), F32), shape((rows, width), BF16), shape((2 * keys, width), F32)]
        + [shape((2 * keys, width), BF16)] * 3,
        (*tables, sec_q, q_pair, *kvs, d_attn, d_pair, lse, lse_pair, delta, delta_pair),
        tables=2,
        flops=5 * pair_work,
    )
    dq_got = swap(dq_pair, "ctx", PAIR)
    dkv_got = [swap(dkvs[step], "ctx", step) for step in range(1, SQUARE)]
    grad_q, grad_k, grad_v, grad_hk, grad_hv = local_call(
        add_grads_kernel,
        "add_grads",
        [shape((rows, width), BF16)] * 3 + [shape((capacity, width), BF16)] * 2,
        (dq_own, dq_got, dkvs[0], *dkv_got),
    )
    out = local_call(
        add_out_kernel, "add_out", [shape((rows, share), BF16)], (out_keep, out_core, out_near)
    )[0]
    return out, grad_q, grad_k, grad_v, grad_hk, grad_hv


def gathered(sec_q, sec_k, sec_v, hist_k, hist_v, frame_levels, frame_counts, w_out, grad_out):
    rows = sec_q.shape[0]
    capacity = hist_k.shape[0]
    owners = lax.axis_size("ctx")
    me = lax.axis_index("ctx")
    frames = jnp.arange(FMAX, dtype=jnp.int32)[None, :]
    tokens = jnp.where(
        frames < frame_counts[:, None], jnp.right_shift(jnp.int32(FTOK), 2 * frame_levels), 0
    ).sum(axis=1)
    slots = jnp.arange(capacity, dtype=jnp.int32)
    all_valid = jnp.concatenate(
        [jnp.ones((owners * rows,), bool), (slots[None] < tokens[:, None]).reshape(-1)]
    )
    own_valid = jnp.concatenate(
        [jnp.ones((rows,), bool), slots < lax.dynamic_index_in_dim(tokens, me, keepdims=False)]
    )

    def everyone(block, axis=0):
        return lax.all_gather(block, "ctx", axis=axis, tiled=True)

    own_k, own_v = (jnp.concatenate(a, axis=0) for a in ((sec_k, hist_k), (sec_v, hist_v)))
    all_k = jnp.concatenate([everyone(sec_k), everyone(hist_k)], axis=0)
    all_v = jnp.concatenate([everyone(sec_v), everyone(hist_v)], axis=0)
    d_attn = contract(lax.all_gather(grad_out, "head", axis=1, tiled=True), w_out, 1, 1).astype(BF16)
    all_q, all_d = everyone(sec_q), everyone(d_attn)

    def probs_and_dscores(query, key, value, dattn, valid, lse, delta):
        scores = contract(query, key, 1, 1) * SCALE
        probs = jnp.where(valid[None, :], jnp.exp(scores - lse), 0.0).astype(BF16)
        dprobs = contract(dattn, value, 1, 1)
        return probs, (probs.astype(F32) * (dprobs - delta)).astype(BF16)

    attn_parts, q_parts, k_parts, v_parts = [], [], [], []
    for head in range(sec_q.shape[1] // HDIM):
        query, dattn, key, value = (head_slice(a, head) for a in (sec_q, d_attn, all_k, all_v))
        scores = jnp.where(all_valid[None, :], contract(query, key, 1, 1) * SCALE, NEG_FILL)
        lse = jax.nn.logsumexp(scores, axis=1, keepdims=True)
        probs = jnp.where(all_valid[None, :], jnp.exp(scores - lse), 0.0).astype(BF16)
        attn = contract(probs, value, 1, 0).astype(BF16)
        delta = jnp.sum(attn.astype(F32) * dattn.astype(F32), axis=1, keepdims=True)
        _, dscores = probs_and_dscores(query, key, value, dattn, all_valid, lse, delta)
        attn_parts.append(attn)
        q_parts.append(contract(dscores, key, 1, 0))
        query, dattn, key, value = (head_slice(a, head) for a in (all_q, all_d, own_k, own_v))
        probs, dscores = probs_and_dscores(
            query, key, value, dattn, own_valid, everyone(lse), everyone(delta)
        )
        k_parts.append(contract(dscores, query, 0, 0))
        v_parts.append(contract(probs, dattn, 0, 0))
    partial = contract(jnp.concatenate(attn_parts, axis=1), w_out, 1, 0).astype(BF16)
    out = lax.psum_scatter(partial, "head", scatter_dimension=1, tiled=True)
    grad_q, grad_k = (
        (jnp.concatenate(a, axis=1) * SCALE).astype(BF16) for a in (q_parts, k_parts)
    )
    grad_v = jnp.concatenate(v_parts, axis=1).astype(BF16)
    return out, grad_q, grad_k[:rows], grad_v[:rows], grad_k[rows:], grad_v[rows:]


def solution(mesh):
    split = P("ctx", "head")
    plan = blocked if (mesh.shape["ctx"], mesh.shape["head"]) == (2 * SQUARE, 4) else gathered
    return jax.shard_map(
        plan,
        mesh=mesh,
        in_specs=(split,) * 5 + (P(), P(), P("head", None), split),
        out_specs=(split,) * 6,
        check_vma=False,
    )
```

time: 155 us -> 70.7 us (0.46)
  matrix products: 36.2 us -> 0 us
  local copies, waits for them, and re-layouts: 27.3 us -> 8.16 us
  between operations: 14.5 us -> 0.75 us
  other arithmetic: 10.7 us -> 0 us
  Pallas kernels: 0 us -> 9.87 us
  starting transfers between devices: 26.9 us -> 18.3 us
  waiting for transfers between devices: 38.8 us -> 33.2 us
    dot_general x26 -> x0, matrix products: 36.2 us -> none  [the longest x13 16.7 us: contract_cols(): lax.dot_general(left_side, right_side, (((1,), (1,)), ((), ())), preferre...]
    pallas_call x0 -> x9, Pallas kernels: none -> 9.87 us  [local_call(): pl.pallas_call(body, name=name, out_shape=out_shapes, in_specs=[pl.BlockS...]
    all_gather x1 -> x0, waiting for transfers between devices: 9.61 us -> none  [shards(): every = lax.all_gather(packed, 'ctx', axis=0, tiled=False)]
    ppermute x13 -> x17, starting transfers between devices: 26.9 us -> 18.3 us  [swap(): return lax.ppermute(block, axis, [(i, i ^ bit) for i in range(count)])]
    unnamed x81 -> x23, local copies, waits for them, and re-layouts: 16.2 us -> 8.16 us
    slice x5 -> x0, local copies, waits for them, and re-layouts: 4.87 us -> none  [the longest x1 1.89 us: shards(): all_values = every[:, 2 * rows:3 * rows].reshape(owners * rows, width)]
    reduce_sum x5 -> x0, other arithmetic: 4.51 us -> none  [the longest x3 3.18 us: totals(): total = jnp.sum(weights, axis=1, keepdims=True)]
    ppermute x13 -> x17, waiting for transfers between devices: 29.1 us -> 33.2 us  [swap(): return lax.ppermute(block, axis, [(i, i ^ bit) for i in range(count)])]
  transfers between devices with their start and end apart: 14 -> 17, of which waited for: 7 -> 7; matrix products, arithmetic and copies ran while one was open for 9% -> 1% of each run, Pallas kernels for 0% -> 13%
where the time goes in v2:
time: 70.7 us; the launch traced here: 70.3 us
  waiting for transfers between devices  33.2 us (47%)
  starting transfers between devices  18.3 us (26%)
  Pallas kernels  9.87 us (14%)
  local copies, waits for them, and re-layouts  8.16 us (12%)
  between operations  0.75 us (1%)
    ppermute x17, waiting for transfers between devices, swap(): return lax.ppermute(block, axis, [(i, i ^ bit) for i in range(count)])  33.2 us
    ppermute x17, starting transfers between devices, swap(): return lax.ppermute(block, axis, [(i, i ^ bit) for i in range(count)])  18.3 us
    pallas_call x9, Pallas kernels, local_call(): pl.pallas_call(body, name=name, out_shape=out_shapes, in_specs=[pl.BlockS...  9.87 us
    unnamed x23, local copies, waits for them, and re-layouts  8.16 us
  transfers between devices with their start and end apart: 17, of which 7 were waited for; matrix products, arithmetic and copies ran while one was open for 1% of the time, Pallas kernels for 13%

profile of v2, /device:TPU:0, one launch (start us, length us, event | category | flops | bytes accessed | tf_op | source)
XLA Modules:
  0.0 70.3 jit_solution(18208673779583361399)
XLA Ops:
  0.6 0.0 copy-start.4
  0.7 0.9 %copy-done.5 = bf16[128,384]{1,0:T(8,128)(2,1)S(1)} copy-done((bf16[128,384]{1,0:T(8,128)(2,1)S(1)}, bf16[128,384]{1,0:T(8,128)(2,1)}, u32[]{:S(2)}) %copy-start.5) | copy-done | bytes 98328
  1.6 0.9 %copy-done.6 = bf16[128,384]{1,0:T(8,128)(2,1)S(1)} copy-done((bf16[128,384]{1,0:T(8,128)(2,1)S(1)}, bf16[128,384]{1,0:T(8,128)(2,1)}, u32[]{:S(2)}) %copy-start.6) | copy-done | bytes 98328
  2.5 0.7 %copy-done.7 = bf16[32,384]{1,0:T(8,128)(2,1)S(1)} copy-done((bf16[32,384]{1,0:T(8,128)(2,1)S(1)}, bf16[32,384]{1,0:T(8,128)(2,1)}, u32[]{:S(2)}) %copy-start.7) | copy-done | bytes 24600
  3.2 0.7 %copy-done.8 = bf16[32,384]{1,0:T(8,128)(2,1)S(1)} copy-done((bf16[32,384]{1,0:T(8,128)(2,1)S(1)}, bf16[32,384]{1,0:T(8,128)(2,1)}, u32[]{:S(2)}) %copy-start.8) | copy-done | bytes 24600
  4.0 3.0 %collective-permute-start.1 = (bf16[320,384]{1,0:T(8,128)(2,1)S(1)}, bf16[320,384]{1,0:T(8,128)(2,1)S(1)}, u32[]{:S(2)}, u32[]{:S(2)}) collective-permute-start(bf16[320,384]{1,0:T(8,128)(2,1)S(1)} %pack.1.kv0), channel_id=1, source_target_pairs={{0,4},{4,0},{8,12},{12,8},{16,20},{20,16},{24,28},{28,24},{1,5},{5... | collective-permute-start | bytes 737288 | tf_op jit(solution)/shard_map/ppermute | solution.py:34
  7.0 1.6 %collective-permute-start.2 = (bf16[320,384]{1,0:T(8,128)(2,1)S(1)}, bf16[320,384]{1,0:T(8,128)(2,1)S(1)}, u32[]{:S(2)}, u32[]{:S(2)}) collective-permute-start(bf16[320,384]{1,0:T(8,128)(2,1)S(1)} %pack.1.kv0), channel_id=1, source_target_pairs={{0,8},{4,12},{8,0},{12,4},{16,24},{20,28},{24,16},{28,20},{1,9},{5... | collective-permute-start | bytes 737288 | tf_op jit(solution)/shard_map/ppermute | solution.py:34
  8.6 0.0 collective-permute-start.3
  8.6 1.9 %collective-permute-start.9 = (bf16[128,768]{1,0:T(8,128)(2,1)}, bf16[128,768]{1,0:T(8,128)(2,1)S(1)}, u32[]{:S(2)}, u32[]{:S(2)}) collective-permute-start(bf16[128,768]{1,0:T(8,128)(2,1)} %own_ref.1), channel_id=1, source_target_pairs={{0,2},{1,3},{2,0},{3,1},{4,6},{5,7},{6,4},{7,5},{8,10},{9,11},{10,... | collective-permute-start | bytes 589832 | tf_op jit(solution)/shard_map/ppermute | solution.py:34
  10.5 2.6 %collective-permute-start = (bf16[128,384]{1,0:T(8,128)(2,1)}, bf16[128,384]{1,0:T(8,128)(2,1)S(1)}, u32[]{:S(2)}, u32[]{:S(2)}) collective-permute-start(bf16[128,384]{1,0:T(8,128)(2,1)} %q_own_ref.5), channel_id=1, source_target_pairs={{0,16},{4,20},{8,24},{12,28},{16,0},{20,4},{24,8},{28,12},{1,17},{... | collective-permute-start | bytes 294920 | tf_op jit(solution)/shard_map/ppermute | solution.py:34
  13.1 0.8 %copy.15.levels_ref = s32[8,2]{1,0:T(8,128)S(1)} copy(s32[8,2]{0,1:T(2,128)} %param.14) | data formatting | bytes 128 | tf_op args[5]
  13.8 7.2 %collective-permute-done.q_pair_ref = bf16[128,384]{1,0:T(8,128)(2,1)S(1)} collective-permute-done((bf16[128,384]{1,0:T(8,128)(2,1)}, bf16[128,384]{1,0:T(8,128)(2,1)S(1)}, u32[]{:S(2)}, u32[]{:S(2)}) %collective-permute-start) | collective-permute-done | bytes 98336 | tf_op jit(solution)/shard_map/ppermute | solution.py:34
  21.0 0.0 collective-permute-done.1.kv1
  21.0 0.0 collective-permute-done.2.kv2
  21.0 0.6 collective-permute-done.3.kv3
  21.6 0.9 %copy-done.2 = bf16[128,384]{1,0:T(8,128)(2,1)S(1)} copy-done((bf16[128,384]{1,0:T(8,128)(2,1)S(1)}, bf16[128,384]{1,0:T(8,128)(2,1)}, u32[]{:S(2)}) %copy-start.2) | copy-done | bytes 98328
  22.5 0.7 copy-done.9
  23.1 1.9 %forward.1 = (f32[384,128]{1,0:T(8,128)S(1)}, bf16[384,128]{1,0:T(8,128)(2,1)S(1)}, f32[8,256]{1,0:T(8,128)S(1)}) custom-call(s32[8,2]{1,0:T(8,128)S(1)} %copy.15.levels_ref, s32[8]{0:T(128)S(1)} %copy-done.9, bf16[128,384]{1,0:T(8,128)(2,1)S(1)} %copy-done.2, bf16[128,384]{1,0:T(8,128)(2,1)S(1)} %collective-permute-done.q_pair_ref, ...), custom_call_target="tpu_custom_call" | custom-call | flops 251658240 | bytes 1482848 | tf_op jit(solution)/shard_map/forward/pallas_call | solution.py:41
  25.1 2.8 %collective-permute-start.4 = (bf16[384,128]{1,0:T(8,128)(2,1)S(1)}, bf16[384,128]{1,0:T(8,128)(2,1)S(1)}, u32[]{:S(2)}, u32[]{:S(2)}) collective-permute-start(bf16[384,128]{1,0:T(8,128)(2,1)S(1)} %get-tuple-element.24), channel_id=1, source_target_pairs={{0,16},{4,20},{8,24},{12,28},{16,0},{20,4},{24,8},{28,12},{1,17},{... | collective-permute-start | bytes 294920 | tf_op jit(solution)/shard_map/ppermute | solution.py:34
  27.8 0.0 collective-permute-start.8
  27.8 0.0 collective-permute-done.9.near_ref
  27.8 0.5 collective-permute-start.10
  28.4 0.2 collective-permute-start.5
  28.6 4.6 %collective-permute-done.5.lse_pair_ref = f32[8,256]{1,0:T(8,128)S(1)} collective-permute-done((f32[8,256]{1,0:T(8,128)S(1)}, f32[8,256]{1,0:T(8,128)S(1)}, u32[]{:S(2)}, u32[]{:S(2)}) %collective-permute-start.5) | collective-permute-done | bytes 8224 | tf_op jit(solution)/shard_map/ppermute | solution.py:34
  33.2 0.0 collective-permute-done.4.pair_ref
  33.2 1.7 %copy-done = bf16[384,3072]{1,0:T(8,128)(2,1)S(1)} copy-done((bf16[384,3072]{1,0:T(8,128)(2,1)S(1)}, bf16[384,3072]{1,0:T(8,128)(2,1)}, u32[]{:S(2)}) %copy-start) | copy-done | bytes 2359320
  34.8 0.7 project.1
  35.5 0.1 collective-permute-start.6
  35.6 0.0 collective-permute-done.8.core_ref
  35.6 0.0 collective-permute-done.10.far_ref
  35.6 0.9 %copy-done.1 = bf16[384,3072]{1,0:T(8,128)(2,1)S(1)} copy-done((bf16[384,3072]{1,0:T(8,128)(2,1)S(1)}, bf16[384,3072]{1,0:T(8,128)(2,1)}, u32[]{:S(2)}) %copy-start.1) | copy-done | bytes 2359320
  36.5 0.8 %dattn.1.d_own_ref = bf16[128,384]{1,0:T(8,128)(2,1)S(1)} custom-call(bf16[128,768]{1,0:T(8,128)(2,1)S(1)} %copy-done.4, bf16[128,768]{1,0:T(8,128)(2,1)S(1)} %collective-permute-done.8.core_ref, bf16[128,768]{1,0:T(8,128)(2,1)S(1)} %collective-permute-done.9.near_ref, bf16[128,768]{1,0:T(8,128)(2,1)S(1)} %collective-permute-done.10.far_ref, ...), custom_call_target="tpu_custom_call" | custom-call | flops 301989888 | bytes 3244032 | tf_op jit(solution)/shard_map/dattn/pallas_call | solution.py:41
  37.3 0.4 collective-permute-start.11
  37.8 6.9 %collective-permute-done.11.d_pair_ref = bf16[128,384]{1,0:T(8,128)(2,1)S(1)} collective-permute-done((bf16[128,384]{1,0:T(8,128)(2,1)S(1)}, bf16[128,384]{1,0:T(8,128)(2,1)S(1)}, u32[]{:S(2)}, u32[]{:S(2)}) %collective-permute-start.11) | collective-permute-done | bytes 98336 | tf_op jit(solution)/shard_map/ppermute | solution.py:34
  44.7 1.3 %delta.1.delta_ref = f32[8,256]{1,0:T(8,128)S(1)} custom-call(s32[8,2]{1,0:T(8,128)S(1)} %copy.15.levels_ref, s32[8]{0:T(128)S(1)} %copy-done.10, bf16[128,384]{1,0:T(8,128)(2,1)S(1)} %copy-done.3, bf16[128,384]{1,0:T(8,128)(2,1)S(1)} %collective-permute-done.q_pair_ref, bf16[320,384]{1,0:T(8,128)(2,1)S(1)} %pack.1.kv0, ...), custom_call_target="tpu_custom_call" | custom-call | flops 251658240 | bytes 1392736 | tf_op jit(solution)/shard_map/delta/pallas_call | solution.py:41
  46.1 0.1 collective-permute-start.12
  46.1 4.5 %collective-permute-done.12.delta_pair_ref = f32[8,256]{1,0:T(8,128)S(1)} collective-permute-done((f32[8,256]{1,0:T(8,128)S(1)}, f32[8,256]{1,0:T(8,128)S(1)}, u32[]{:S(2)}, u32[]{:S(2)}) %collective-permute-start.12) | collective-permute-done | bytes 8224 | tf_op jit(solution)/shard_map/ppermute | solution.py:34
  50.7 3.6 %backward.1 = (f32[128,384]{1,0:T(8,128)S(1)}, bf16[128,384]{1,0:T(8,128)(2,1)S(1)}, f32[320,384]{1,0:T(8,128)S(1)}, bf16[320,384]{1,0:T(8,128)(2,1)S(1)}, bf16[...) custom-call(s32[8,2]{1,0:T(8,128)S(1)} %copy.15.levels_ref, s32[8]{0:T(128)S(1)} %copy-done.10, ...), custom_call_target="tpu_custom_call" | custom-call | flops 629145600 | bytes 2932832 | tf_op jit(solution)/shard_map/backward/pallas_call | solution.py:41
  54.2 0.8 %collective-permute-start.14 = (bf16[320,384]{1,0:T(8,128)(2,1)S(1)}, bf16[320,384]{1,0:T(8,128)(2,1)S(1)}, u32[]{:S(2)}, u32[]{:S(2)}) collective-permute-start(bf16[320,384]{1,0:T(8,128)(2,1)S(1)} %get-tuple-element.32), channel_id=1, source_target_pairs={{0,4},{4,0},{8,12},{12,8},{16,20},{20,16},{24,28},{28,24},{1,5},{5... | collective-permute-start | bytes 737288 | tf_op jit(solution)/shard_map/ppermute | solution.py:34
  55.0 0.4 collective-permute-start.15
  55.4 2.4 %collective-permute-start.16 = (bf16[320,384]{1,0:T(8,128)(2,1)S(1)}, bf16[320,384]{1,0:T(8,128)(2,1)S(1)}, u32[]{:S(2)}, u32[]{:S(2)}) collective-permute-start(bf16[320,384]{1,0:T(8,128)(2,1)S(1)} %get-tuple-element.34), channel_id=1, source_target_pairs={{0,12},{4,8},{8,4},{12,0},{16,28},{20,24},{24,20},{28,16},{1,13},{... | collective-permute-start | bytes 737288 | tf_op jit(solution)/shard_map/ppermute | solution.py:34
  57.8 1.6 %collective-permute-start.7 = (bf16[128,768]{1,0:T(8,128)(2,1)S(1)}, bf16[128,768]{1,0:T(8,128)(2,1)S(1)}, u32[]{:S(2)}, u32[]{:S(2)}) collective-permute-start(bf16[128,768]{1,0:T(8,128)(2,1)S(1)} %add_near.1), channel_id=1, source_target_pairs={{0,2},{1,3},{2,0},{3,1},{4,6},{5,7},{6,4},{7,5},{8,10},{9,11},{10,... | collective-permute-start | bytes 589832 | tf_op jit(solution)/shard_map/ppermute | solution.py:34
  59.4 0.0 collective-permute-start.13
  59.4 6.6 %collective-permute-done.13.dq_pair_ref = bf16[128,384]{1,0:T(8,128)(2,1)S(1)} collective-permute-done((bf16[128,384]{1,0:T(8,128)(2,1)S(1)}, bf16[128,384]{1,0:T(8,128)(2,1)S(1)}, u32[]{:S(2)}, u32[]{:S(2)}) %collective-permute-start.13) | collective-permute-done | bytes 98336 | tf_op jit(solution)/shard_map/ppermute | solution.py:34
  66.0 2.7 %collective-permute-done.16.dkv3 = bf16[320,384]{1,0:T(8,128)(2,1)S(1)} collective-permute-done((bf16[320,384]{1,0:T(8,128)(2,1)S(1)}, bf16[320,384]{1,0:T(8,128)(2,1)S(1)}, u32[]{:S(2)}, u32[]{:S(2)}) %collective-permute-start.16) | collective-permute-done | bytes 245792 | tf_op jit(solution)/shard_map/ppermute | solution.py:34
  68.7 0.8 %add_grads.1 = (bf16[128,384]{1,0:T(8,128)(2,1)}, bf16[128,384]{1,0:T(8,128)(2,1)}, bf16[128,384]{1,0:T(8,128)(2,1)}, bf16[32,384]{1,0:T(8,128)(2,1)}, bf16[32,384]{1,0:T(8,128)(2,1)}) custom-call(f32[128,384]{1,0:T(8,128)S(1)} %get-tuple-element.29.dq_ref, bf16[128,384]{1,0:T(8,128)(2,1)S(1)} %collective-permute-done.13.dq_pair_ref, ...), custom_call_target="tpu_custom_call" | custom-call | bytes 1867776 | tf_op jit(solution)/shard_map/add_grads/pallas_call | solution.py:41
  69.5 0.0 collective-permute-done.7.near_ref
  69.5 0.7 %add_out.1 = bf16[128,768]{1,0:T(8,128)(2,1)} custom-call(f32[128,768]{1,0:T(8,128)S(1)} %get-tuple-element.26.keep_ref, bf16[128,1536]{1,0:T(8,128)(2,1)S(1)} %collective-permute-done.6.core_ref, bf16[128,768]{1,0:T(8,128)(2,1)S(1)} %collective-permute-done.7.near_ref), custom_call_target="tpu_custom_call" | custom-call | bytes 1179648 | tf_op jit(solution)/shard_map/add_out/pallas_call | solution.py:41
  (18 shorter events, 0.1 us)
Async XLA Ops:
  0.6 35.0 %copy-start.4 = (bf16[128,768]{1,0:T(8,128)(2,1)S(1)}, bf16[128,768]{1,0:T(8,128)(2,1)}, u32[]{:S(2)}) copy-start(bf16[128,768]{1,0:T(8,128)(2,1)} %own_ref.1) | copy-start | bytes 589828
  0.6 0.9 %copy-start.5 = (bf16[128,384]{1,0:T(8,128)(2,1)S(1)}, bf16[128,384]{1,0:T(8,128)(2,1)}, u32[]{:S(2)}) copy-start(bf16[128,384]{1,0:T(8,128)(2,1)} %k_ref.1) | copy-start | bytes 294916
  1.6 0.9 %copy-start.6 = (bf16[128,384]{1,0:T(8,128)(2,1)S(1)}, bf16[128,384]{1,0:T(8,128)(2,1)}, u32[]{:S(2)}) copy-start(bf16[128,384]{1,0:T(8,128)(2,1)} %v_ref.1) | copy-start | bytes 294916
  2.5 0.7 %copy-start.7 = (bf16[32,384]{1,0:T(8,128)(2,1)S(1)}, bf16[32,384]{1,0:T(8,128)(2,1)}, u32[]{:S(2)}) copy-start(bf16[32,384]{1,0:T(8,128)(2,1)} %hk_ref.1) | copy-start | bytes 73732
  3.2 0.7 %copy-start.8 = (bf16[32,384]{1,0:T(8,128)(2,1)S(1)}, bf16[32,384]{1,0:T(8,128)(2,1)}, u32[]{:S(2)}) copy-start(bf16[32,384]{1,0:T(8,128)(2,1)} %hv_ref.1) | copy-start | bytes 73732
  4.0 17.0 %collective-permute-start.1 = (bf16[320,384]{1,0:T(8,128)(2,1)S(1)}, bf16[320,384]{1,0:T(8,128)(2,1)S(1)}, u32[]{:S(2)}, u32[]{:S(2)}) collective-permute-start(bf16[320,384]{1,0:T(8,128)(2,1)S(1)} %pack.1.kv0), channel_id=1, source_target_pairs={{0,4},{4,0},{8,12},{12,8},{16,20},{20,16},{24,28},{28,24},{1,5},{5... | collective-permute-start | bytes 737288 | tf_op jit(solution)/shard_map/ppermute | solution.py:34
  7.0 14.0 %collective-permute-start.2 = (bf16[320,384]{1,0:T(8,128)(2,1)S(1)}, bf16[320,384]{1,0:T(8,128)(2,1)S(1)}, u32[]{:S(2)}, u32[]{:S(2)}) collective-permute-start(bf16[320,384]{1,0:T(8,128)(2,1)S(1)} %pack.1.kv0), channel_id=1, source_target_pairs={{0,8},{4,12},{8,0},{12,4},{16,24},{20,28},{24,16},{28,20},{1,9},{5... | collective-permute-start | bytes 737288 | tf_op jit(solution)/shard_map/ppermute | solution.py:34
  8.6 13.0 %collective-permute-start.3 = (bf16[320,384]{1,0:T(8,128)(2,1)S(1)}, bf16[320,384]{1,0:T(8,128)(2,1)S(1)}, u32[]{:S(2)}, u32[]{:S(2)}) collective-permute-start(bf16[320,384]{1,0:T(8,128)(2,1)S(1)} %pack.1.kv0), channel_id=1, source_target_pairs={{0,12},{4,8},{8,4},{12,0},{16,28},{20,24},{24,20},{28,16},{1,13},{... | collective-permute-start | bytes 737288 | tf_op jit(solution)/shard_map/ppermute | solution.py:34
  8.6 19.3 %collective-permute-start.9 = (bf16[128,768]{1,0:T(8,128)(2,1)}, bf16[128,768]{1,0:T(8,128)(2,1)S(1)}, u32[]{:S(2)}, u32[]{:S(2)}) collective-permute-start(bf16[128,768]{1,0:T(8,128)(2,1)} %own_ref.1), channel_id=1, source_target_pairs={{0,2},{1,3},{2,0},{3,1},{4,6},{5,7},{6,4},{7,5},{8,10},{9,11},{10,... | collective-permute-start | bytes 589832 | tf_op jit(solution)/shard_map/ppermute | solution.py:34
  10.5 10.5 %collective-permute-start = (bf16[128,384]{1,0:T(8,128)(2,1)}, bf16[128,384]{1,0:T(8,128)(2,1)S(1)}, u32[]{:S(2)}, u32[]{:S(2)}) collective-permute-start(bf16[128,384]{1,0:T(8,128)(2,1)} %q_own_ref.5), channel_id=1, source_target_pairs={{0,16},{4,20},{8,24},{12,28},{16,0},{20,4},{24,8},{28,12},{1,17},{... | collective-permute-start | bytes 294920 | tf_op jit(solution)/shard_map/ppermute | solution.py:34
  21.6 0.9 %copy-start.2 = (bf16[128,384]{1,0:T(8,128)(2,1)S(1)}, bf16[128,384]{1,0:T(8,128)(2,1)}, u32[]{:S(2)}) copy-start(bf16[128,384]{1,0:T(8,128)(2,1)} %q_own_ref.5) | copy-start | bytes 294916
  22.5 0.7 copy-start.9
  25.1 8.1 %collective-permute-start.4 = (bf16[384,128]{1,0:T(8,128)(2,1)S(1)}, bf16[384,128]{1,0:T(8,128)(2,1)S(1)}, u32[]{:S(2)}, u32[]{:S(2)}) collective-permute-start(bf16[384,128]{1,0:T(8,128)(2,1)S(1)} %get-tuple-element.24), channel_id=1, source_target_pairs={{0,16},{4,20},{8,24},{12,28},{16,0},{20,4},{24,8},{28,12},{1,17},{... | collective-permute-start | bytes 294920 | tf_op jit(solution)/shard_map/ppermute | solution.py:34
  27.8 7.7 %collective-permute-start.8 = (bf16[128,768]{1,0:T(8,128)(2,1)}, bf16[128,768]{1,0:T(8,128)(2,1)S(1)}, u32[]{:S(2)}, u32[]{:S(2)}) collective-permute-start(bf16[128,768]{1,0:T(8,128)(2,1)} %own_ref.1), channel_id=1, source_target_pairs={{0,1},{1,0},{2,3},{3,2},{4,5},{5,4},{6,7},{7,6},{8,9},{9,8},{10,11... | collective-permute-start | bytes 589832 | tf_op jit(solution)/shard_map/ppermute | solution.py:34
  27.8 7.8 %collective-permute-start.10 = (bf16[128,768]{1,0:T(8,128)(2,1)S(1)}, bf16[128,768]{1,0:T(8,128)(2,1)S(1)}, u32[]{:S(2)}, u32[]{:S(2)}) collective-permute-start(bf16[128,768]{1,0:T(8,128)(2,1)S(1)} %collective-permute-done.9.near_ref), channel_id=1, source_target_pairs={{0,1},{1,0},{2,3},{3,2},{4,5},{5,4},{6,7},{7,6},{8,9},{9,8},{10,11... | collective-permute-start | bytes 589832 | tf_op jit(solution)/shard_map/ppermute | solution.py:34
  28.4 4.8 %collective-permute-start.5 = (f32[8,256]{1,0:T(8,128)S(1)}, f32[8,256]{1,0:T(8,128)S(1)}, u32[]{:S(2)}, u32[]{:S(2)}) collective-permute-start(f32[8,256]{1,0:T(8,128)S(1)} %get-tuple-element.25.lse_ref), channel_id=1, source_target_pairs={{0,16},{4,20},{8,24},{12,28},{16,0},{20,4},{24,8},{28,12},{1,17},{... | collective-permute-start | bytes 24584 | tf_op jit(solution)/shard_map/ppermute | solution.py:34
  33.2 1.7 %copy-start = (bf16[384,3072]{1,0:T(8,128)(2,1)S(1)}, bf16[384,3072]{1,0:T(8,128)(2,1)}, u32[]{:S(2)}) copy-start(bf16[384,3072]{1,0:T(8,128)(2,1)} %w_ref.3) | copy-start | bytes 7077892
  34.8 1.7 %copy-start.1 = (bf16[384,3072]{1,0:T(8,128)(2,1)S(1)}, bf16[384,3072]{1,0:T(8,128)(2,1)}, u32[]{:S(2)}) copy-start(bf16[384,3072]{1,0:T(8,128)(2,1)} %w_ref.3) | copy-start | bytes 7077892
  34.8 9.9 %copy-start.3 = (bf16[128,384]{1,0:T(8,128)(2,1)S(1)}, bf16[128,384]{1,0:T(8,128)(2,1)}, u32[]{:S(2)}) copy-start(bf16[128,384]{1,0:T(8,128)(2,1)} %q_own_ref.5) | copy-start | bytes 294916
  34.8 9.9 %copy-start.10 = (s32[8]{0:T(128)S(1)}, s32[8]{0:T(128)}, u32[]{:S(2)}) copy-start(s32[8]{0:T(128)} %counts_ref.5) | copy-start | bytes 100
  35.5 22.3 %collective-permute-start.6 = (bf16[128,1536]{1,0:T(8,128)(2,1)S(1)}, bf16[128,1536]{1,0:T(8,128)(2,1)S(1)}, u32[]{:S(2)}, u32[]{:S(2)}) collective-permute-start(bf16[128,1536]{1,0:T(8,128)(2,1)S(1)} %get-tuple-element.27), channel_id=1, source_target_pairs={{0,1},{1,0},{2,3},{3,2},{4,5},{5,4},{6,7},{7,6},{8,9},{9,8},{10,11... | collective-permute-start | bytes 1179656 | tf_op jit(solution)/shard_map/ppermute | solution.py:34
  37.3 7.4 %collective-permute-start.11 = (bf16[128,384]{1,0:T(8,128)(2,1)S(1)}, bf16[128,384]{1,0:T(8,128)(2,1)S(1)}, u32[]{:S(2)}, u32[]{:S(2)}) collective-permute-start(bf16[128,384]{1,0:T(8,128)(2,1)S(1)} %dattn.1.d_own_ref), channel_id=1, source_target_pairs={{0,16},{4,20},{8,24},{12,28},{16,0},{20,4},{24,8},{28,12},{1,17},{... | collective-permute-start | bytes 294920 | tf_op jit(solution)/shard_map/ppermute | solution.py:34
  46.1 4.6 %collective-permute-start.12 = (f32[8,256]{1,0:T(8,128)S(1)}, f32[8,256]{1,0:T(8,128)S(1)}, u32[]{:S(2)}, u32[]{:S(2)}) collective-permute-start(f32[8,256]{1,0:T(8,128)S(1)} %delta.1.delta_ref), channel_id=1, source_target_pairs={{0,16},{4,20},{8,24},{12,28},{16,0},{20,4},{24,8},{28,12},{1,17},{... | collective-permute-start | bytes 24584 | tf_op jit(solution)/shard_map/ppermute | solution.py:34
  54.2 11.8 %collective-permute-start.14 = (bf16[320,384]{1,0:T(8,128)(2,1)S(1)}, bf16[320,384]{1,0:T(8,128)(2,1)S(1)}, u32[]{:S(2)}, u32[]{:S(2)}) collective-permute-start(bf16[320,384]{1,0:T(8,128)(2,1)S(1)} %get-tuple-element.32), channel_id=1, source_target_pairs={{0,4},{4,0},{8,12},{12,8},{16,20},{20,16},{24,28},{28,24},{1,5},{5... | collective-permute-start | bytes 737288 | tf_op jit(solution)/shard_map/ppermute | solution.py:34
  55.0 11.0 %collective-permute-start.15 = (bf16[320,384]{1,0:T(8,128)(2,1)S(1)}, bf16[320,384]{1,0:T(8,128)(2,1)S(1)}, u32[]{:S(2)}, u32[]{:S(2)}) collective-permute-start(bf16[320,384]{1,0:T(8,128)(2,1)S(1)} %get-tuple-element.33), channel_id=1, source_target_pairs={{0,8},{4,12},{8,0},{12,4},{16,24},{20,28},{24,16},{28,20},{1,9},{5... | collective-permute-start | bytes 737288 | tf_op jit(solution)/shard_map/ppermute | solution.py:34
  55.4 13.4 %collective-permute-start.16 = (bf16[320,384]{1,0:T(8,128)(2,1)S(1)}, bf16[320,384]{1,0:T(8,128)(2,1)S(1)}, u32[]{:S(2)}, u32[]{:S(2)}) collective-permute-start(bf16[320,384]{1,0:T(8,128)(2,1)S(1)} %get-tuple-element.34), channel_id=1, source_target_pairs={{0,12},{4,8},{8,4},{12,0},{16,28},{20,24},{24,20},{28,16},{1,13},{... | collective-permute-start | bytes 737288 | tf_op jit(solution)/shard_map/ppermute | solution.py:34
  57.8 11.7 %collective-permute-start.7 = (bf16[128,768]{1,0:T(8,128)(2,1)S(1)}, bf16[128,768]{1,0:T(8,128)(2,1)S(1)}, u32[]{:S(2)}, u32[]{:S(2)}) collective-permute-start(bf16[128,768]{1,0:T(8,128)(2,1)S(1)} %add_near.1), channel_id=1, source_target_pairs={{0,2},{1,3},{2,0},{3,1},{4,6},{5,7},{6,4},{7,5},{8,10},{9,11},{10,... | collective-permute-start | bytes 589832 | tf_op jit(solution)/shard_map/ppermute | solution.py:34
  59.4 6.6 %collective-permute-start.13 = (bf16[128,384]{1,0:T(8,128)(2,1)S(1)}, bf16[128,384]{1,0:T(8,128)(2,1)S(1)}, u32[]{:S(2)}, u32[]{:S(2)}) collective-permute-start(bf16[128,384]{1,0:T(8,128)(2,1)S(1)} %get-tuple-element.30), channel_id=1, source_target_pairs={{0,16},{4,20},{8,24},{12,28},{16,0},{20,4},{24,8},{28,12},{1,17},{... | collective-permute-start | bytes 294920 | tf_op jit(solution)/shard_map/ppermute | solution.py:34

commit v3 on v2

--- a/solution.py
+++ b/solution.py
@@ -49,26 +49,55 @@
     )(*args)
 
 
-def owner_tokens_at(levels_ref, counts_ref, owner):
-    total = jnp.int32(0)
-    for frame in range(FMAX):
-        tokens = lax.shift_right_logical(jnp.int32(FTOK), 2 * levels_ref[owner, frame])
-        total += jnp.where(frame < counts_ref[owner], tokens, 0)
-    return total
-
-
-def square_tokens(levels_ref, counts_ref):
-    me = lax.axis_index("ctx")
-    return [owner_tokens_at(levels_ref, counts_ref, me ^ step) for step in range(SQUARE)]
-
-
-def pack_kernel(k_ref, hk_ref, v_ref, hv_ref, kv_ref):
+def any_call(body, name, out_shapes, args, copies):
+    moved = sum(a.size * a.dtype.itemsize for a in args)
+    return pl.pallas_call(
+        body,
+        name=name,
+        out_shape=out_shapes,
+        in_specs=[pl.BlockSpec(memory_space=pl.ANY)] * len(args),
+        out_specs=[pl.BlockSpec(memory_space=pl.ANY)] * len(out_shapes),
+        scratch_shapes=[pltpu.SemaphoreType.DMA((copies,))],
+        compiler_params=pltpu.CompilerParams(vmem_limit_bytes=60 * 2**20),
+        cost_estimate=pl.CostEstimate(flops=0, bytes_accessed=2 * moved, transcendentals=0),
+    )(*args)
+
+
+def copy_all(pairs, sems):
+    copies = [
+        pltpu.make_async_copy(source, target, sems.at[i]) for i, (source, target) in enumerate(pairs)
+    ]
+    for copy in copies:
+        copy.start()
+    for copy in copies:
+        copy.wait()
+
+
+def load_kernel(k_ref, hk_ref, v_ref, hv_ref, kv_out, sems):
     rows, capacity = k_ref.shape[0], hk_ref.shape[0]
     keys = rows + capacity
-    kv_ref[:rows] = k_ref[...]
-    kv_ref[rows:keys] = hk_ref[...]
-    kv_ref[keys : keys + rows] = v_ref[...]
-    kv_ref[keys + rows :] = hv_ref[...]
+    copy_all(
+        [
+            (k_ref, kv_out.at[pl.ds(0, rows)]),
+            (v_ref, kv_out.at[pl.ds(keys, rows)]),
+            (hk_ref, kv_out.at[pl.ds(rows, capacity)]),
+            (hv_ref, kv_out.at[pl.ds(keys + rows, capacity)]),
+        ],
+        sems,
+    )
+
+
+def limits_kernel(levels_ref, counts_ref, limits_ref):
+    me = lax.axis_index("ctx")
+    row = lax.broadcasted_iota(jnp.int32, limits_ref.shape, 0)
+    limits = jnp.zeros(limits_ref.shape, jnp.int32)
+    for step in range(SQUARE):
+        total = jnp.int32(0)
+        for frame in range(FMAX):
+            tokens = lax.shift_right_logical(jnp.int32(FTOK), 2 * levels_ref[me ^ step, frame])
+            total += jnp.where(frame < counts_ref[me ^ step], tokens, 0)
+        limits = jnp.where(row == step, total, limits)
+    limits_ref[...] = limits
 
 
 def dattn_kernel(own_ref, core_ref, near_ref, far_ref, w_ref, out_ref):
@@ -82,56 +111,68 @@
     out_ref[...] = total.astype(BF16)
 
 
-def masked_scores(kv_ref, head, query, tokens, rows, keys):
-    scores = contract(head_slice(kv_ref[:keys], head), query, 1, 1) * SCALE
-    slot = lax.broadcasted_iota(jnp.int32, scores.shape, 0)
-    return jnp.where(slot < rows + tokens, scores, NEG_FILL)
+def both_rows(own_ref, pair_ref, head):
+    return jnp.concatenate(
+        [head_slice(own_ref[...], head), head_slice(pair_ref[...], head)], axis=0
+    )
 
 
 def forward_kernel(
-    levels_ref, counts_ref, q_own_ref, q_pair_ref, kv0, kv1, kv2, kv3, own_ref, pair_ref, lse_ref
+    limits_ref, q_own_ref, q_pair_ref, d_own_ref, d_pair_ref, kv0, kv1, kv2, kv3,
+    stats_ref, own_ref, pair_ref, probs_ref, dprobs_ref,
 ):
     rows = q_own_ref.shape[0]
     keys = kv0.shape[0] // 2
-    tokens = square_tokens(levels_ref, counts_ref)
-    lse_ref[...] = jnp.zeros_like(lse_ref)
+    blocks = (kv0, kv1, kv2, kv3)
+    stats_ref[...] = jnp.zeros_like(stats_ref)
     for head in range(q_own_ref.shape[1] // HDIM):
-        query = jnp.concatenate(
-            [head_slice(q_own_ref[...], head), head_slice(q_pair_ref[...], head)], axis=0
-        )
-        scores = [
-            masked_scores(ref, head, query, count, rows, keys)
-            for ref, count in zip((kv0, kv1, kv2, kv3), tokens)
-        ]
+        query = both_rows(q_own_ref, q_pair_ref, head)
+        dattn = both_rows(d_own_ref, d_pair_ref, head)
+        scores = []
+        for step, ref in enumerate(blocks):
+            block = contract(head_slice(ref[:keys], head), query, 1, 1) * SCALE
+            slot = lax.broadcasted_iota(jnp.int32, block.shape, 0)
+            valid = slot < rows + limits_ref[step : step + 1]
+            scores.append(jnp.where(valid, block, NEG_FILL))
         top = functools.reduce(
             jnp.maximum, [jnp.max(block, axis=0, keepdims=True) for block in scores]
         )
         weights = [jnp.exp(block - top) for block in scores]
         total = sum(jnp.sum(block, axis=0, keepdims=True) for block in weights)
         inverse = 1.0 / total
-        attn = sum(
-            contract(head_slice(ref[keys:], head), (block * inverse).astype(BF16), 0, 0)
-            for ref, block in zip((kv0, kv1, kv2, kv3), weights)
-        )
+        attn, delta = None, None
+        for step, ref in enumerate(blocks):
+            value = head_slice(ref[keys:], head)
+            probs = weights[step] * inverse
+            dprobs = contract(value, dattn, 1, 1)
+            part = contract(value, probs.astype(BF16), 0, 0)
+            delta_part = jnp.sum(probs * dprobs, axis=0, keepdims=True)
+            attn = part if attn is None else attn + part
+            delta = delta_part if delta is None else delta + delta_part
+            begin = (head * SQUARE + step) * keys
+            probs_ref[begin : begin + keys] = probs.astype(probs_ref.dtype)
+            dprobs_ref[begin : begin + keys] = dprobs
         features = slice(head * HDIM, (head + 1) * HDIM)
         own_ref[features] = attn[:, :rows]
         pair_ref[features] = attn[:, rows:].astype(BF16)
-        lse_ref[head : head + 1] = top + jnp.log(total)
+        stats_ref[head : head + 1] = top + jnp.log(total)
+        stats_ref[8 + head : 9 + head] = delta
 
 
 def merge_parts(mine, theirs):
     top = jnp.maximum(mine, theirs)
-    total = top + jnp.log(jnp.exp(mine - top) + jnp.exp(theirs - top))
-    return total, jnp.exp(mine - total), jnp.exp(theirs - total)
-
-
-def project_kernel(own_ref, pair_ref, lse_ref, lse_pair_ref, w_ref, send_ref, next_ref, keep_ref):
+    weight, weight_pair = jnp.exp(mine - top), jnp.exp(theirs - top)
+    inverse = 1.0 / (weight + weight_pair)
+    return weight * inverse, weight_pair * inverse
+
+
+def project_kernel(own_ref, pair_ref, stats_ref, stats_pair_ref, w_ref, send_ref, next_ref, keep_ref):
     rows = own_ref.shape[1]
     parts = []
     for head in range(own_ref.shape[0] // HDIM):
         features = slice(head * HDIM, (head + 1) * HDIM)
-        _, weight, weight_pair = merge_parts(
-            lse_ref[head : head + 1, :rows], lse_pair_ref[head : head + 1, rows:]
+        weight, weight_pair = merge_parts(
+            stats_ref[head : head + 1, :rows], stats_pair_ref[head : head + 1, rows:]
         )
         parts.append(own_ref[features] * weight + pair_ref[features].astype(F32) * weight_pair)
     attn = jnp.concatenate(parts, axis=0).astype(BF16)
@@ -159,60 +200,35 @@
     out_ref[...] = total.astype(BF16)
 
 
-def delta_kernel(
-    levels_ref, counts_ref, q_own_ref, q_pair_ref, kv0, kv1, kv2, kv3, d_own_ref, d_pair_ref, lse_ref,
-    delta_ref,
-):
-    rows = q_own_ref.shape[0]
-    keys = kv0.shape[0] // 2
-    tokens = square_tokens(levels_ref, counts_ref)
-    delta_ref[...] = jnp.zeros_like(delta_ref)
-    for head in range(q_own_ref.shape[1] // HDIM):
-        query, dattn = (
-            jnp.concatenate([head_slice(a[...], head), head_slice(b[...], head)], axis=0)
-            for a, b in ((q_own_ref, q_pair_ref), (d_own_ref, d_pair_ref))
-        )
-        total = None
-        for ref, count in zip((kv0, kv1, kv2, kv3), tokens):
-            scores = masked_scores(ref, head, query, count, rows, keys)
-            probs = jnp.exp(scores - lse_ref[head : head + 1])
-            dprobs = contract(head_slice(ref[keys:], head), dattn, 1, 1)
-            part = jnp.sum(probs * dprobs, axis=0, keepdims=True)
-            total = part if total is None else total + part
-        delta_ref[head : head + 1] = total
-
-
 def backward_kernel(
-    levels_ref, counts_ref, q_own_ref, q_pair_ref, kv0, kv1, kv2, kv3, d_own_ref, d_pair_ref,
-    lse_ref, lse_pair_ref, delta_ref, delta_pair_ref,
+    q_own_ref, q_pair_ref, d_own_ref, d_pair_ref, kv0, kv1, kv2, kv3,
+    stats_ref, stats_pair_ref, probs_ref, dprobs_ref,
     dq_own_ref, dq_pair_ref, dkv0, dkv1, dkv2, dkv3,
 ):
     rows = q_own_ref.shape[0]
     keys = kv0.shape[0] // 2
-    tokens = square_tokens(levels_ref, counts_ref)
-
-    def swapped(ref, head):
-        row = ref[head : head + 1]
+
+    def swapped(row):
         return jnp.concatenate([row[:, rows:], row[:, :rows]], axis=1)
 
     for head in range(q_own_ref.shape[1] // HDIM):
-        query, dattn = (
-            jnp.concatenate([head_slice(a[...], head), head_slice(b[...], head)], axis=0)
-            for a, b in ((q_own_ref, q_pair_ref), (d_own_ref, d_pair_ref))
+        query = both_rows(q_own_ref, q_pair_ref, head)
+        dattn = both_rows(d_own_ref, d_pair_ref, head)
+        weight, weight_pair = merge_parts(
+            stats_ref[head : head + 1], swapped(stats_pair_ref[head : head + 1])
         )
-        lse, weight, weight_pair = merge_parts(lse_ref[head : head + 1], swapped(lse_pair_ref, head))
-        delta = weight * delta_ref[head : head + 1] + weight_pair * swapped(delta_pair_ref, head)
+        delta = weight * stats_ref[8 + head : 9 + head]
+        delta += weight_pair * swapped(stats_pair_ref[8 + head : 9 + head])
         features = slice(head * HDIM, (head + 1) * HDIM)
         dquery = None
-        for ref, count, out in zip((kv0, kv1, kv2, kv3), tokens, (dkv0, dkv1, dkv2, dkv3)):
-            key = head_slice(ref[:keys], head)
-            scores = masked_scores(ref, head, query, count, rows, keys)
-            probs = jnp.exp(scores - lse).astype(BF16)
-            dprobs = contract(head_slice(ref[keys:], head), dattn, 1, 1)
+        for step, (ref, out) in enumerate(zip((kv0, kv1, kv2, kv3), (dkv0, dkv1, dkv2, dkv3))):
+            begin = (head * SQUARE + step) * keys
+            probs = (probs_ref[begin : begin + keys].astype(F32) * weight).astype(BF16)
+            dprobs = dprobs_ref[begin : begin + keys]
             dscores = (probs.astype(F32) * (dprobs - delta)).astype(BF16)
             out[:keys, features] = (contract(dscores, query, 1, 0) * SCALE).astype(out.dtype)
             out[keys:, features] = contract(probs, dattn, 1, 0).astype(out.dtype)
-            part = contract(dscores, key, 0, 0)
+            part = contract(dscores, head_slice(ref[:keys], head), 0, 0)
             dquery = part if dquery is None else dquery + part
         dq_own_ref[:, features] = dquery[:rows] * SCALE
         dq_pair_ref[:, features] = (dquery[rows:] * SCALE).astype(BF16)
@@ -245,40 +261,61 @@
     capacity = hist_k.shape[0]
     keys = rows + capacity
     share = grad_out.shape[1]
-    tables = (frame_levels, frame_counts)
-    pair_work = 2 * SQUARE * keys * 2 * rows * width
-
-    grad_near = swap(grad_out, "head", 2)
-    grad_core = swap(grad_out, "head", 1)
-    kv0 = local_call(
-        pack_kernel, "pack", [shape((2 * keys, width), BF16)], (sec_k, hist_k, sec_v, hist_v)
+    work = 2 * SQUARE * keys * 2 * rows * width
+
+    grad_core, grad_near, grad_far = (swap(grad_out, "head", step) for step in range(1, 4))
+    kv0 = any_call(
+        load_kernel, "load", [shape((2 * keys, width), BF16)], (sec_k, hist_k, sec_v, hist_v), copies=4
     )[0]
     kvs = [kv0] + [swap(kv0, "ctx", step) for step in range(1, SQUARE)]
     q_pair = swap(sec_q, "ctx", PAIR)
-    grad_far = swap(grad_near, "head", 1)
-    d_attn = local_call(
+    d_own = local_call(
         dattn_kernel,
         "dattn",
         [shape((rows, width), BF16)],
         (grad_out, grad_core, grad_near, grad_far, w_out),
         flops=2 * rows * width * share * 4,
     )[0]
-    d_pair = swap(d_attn, "ctx", PAIR)
-    attn_own, attn_pair, lse = local_call(
+    d_pair = swap(d_own, "ctx", PAIR)
+    limits = local_call(
+        limits_kernel,
+        "limits",
+        [shape((8, 2 * rows), jnp.int32)],
+        (frame_levels, frame_counts),
+        tables=2,
+    )[0]
+    stats, attn_own, attn_pair, probs, dprobs = local_call(
         forward_kernel,
         "forward",
-        [shape((width, rows), F32), shape((width, rows), BF16), shape((8, 2 * rows), F32)],
-        (*tables, sec_q, q_pair, *kvs),
-        tables=2,
-        flops=2 * pair_work,
-    )
-    lse_pair = swap(lse, "ctx", PAIR)
+        [
+            shape((16, 2 * rows), F32),
+            shape((width, rows), F32),
+            shape((width, rows), BF16),
+            shape((heads * SQUARE * keys, 2 * rows), BF16),
+            shape((heads * SQUARE * keys, 2 * rows), F32),
+        ],
+        (limits, sec_q, q_pair, d_own, d_pair, *kvs),
+        flops=3 * work,
+    )
+    stats_pair = swap(stats, "ctx", PAIR)
+    stats_pair, attn_pair = lax.optimization_barrier((stats_pair, attn_pair))
     attn_got = swap(attn_pair, "ctx", PAIR)
+    dq_own, dq_pair, *dkvs = local_call(
+        backward_kernel,
+        "backward",
+        [shape((rows, width), F32), shape((rows, width), BF16), shape((2 * keys, width), F32)]
+        + [shape((2 * keys, width), BF16)] * 3,
+        (sec_q, q_pair, d_own, d_pair, *kvs, stats, stats_pair, probs, dprobs),
+        flops=3 * work,
+    )
+    dkv_got = [swap(dkvs[step], "ctx", step) for step in range(1, SQUARE)]
+    dq_got = swap(dq_pair, "ctx", PAIR)
+    attn_own, dq_own = lax.optimization_barrier((attn_own, dq_own))
     out_send, out_next, out_keep = local_call(
         project_kernel,
         "project",
         [shape((rows, 2 * share), BF16), shape((rows, share), F32), shape((rows, share), F32)],
-        (attn_own, attn_got, lse, lse_pair, w_out),
+        (attn_own, attn_got, stats, stats_pair, w_out),
         flops=2 * rows * width * share * 4,
     )
     out_core = swap(out_send, "head", 1)
@@ -287,26 +324,6 @@
         "head",
         2,
     )
-    delta = local_call(
-        delta_kernel,
-        "delta",
-        [shape((8, 2 * rows), F32)],
-        (*tables, sec_q, q_pair, *kvs, d_attn, d_pair, lse),
-        tables=2,
-        flops=2 * pair_work,
-    )[0]
-    delta_pair = swap(delta, "ctx", PAIR)
-    dq_own, dq_pair, *dkvs = local_call(
-        backward_kernel,
-        "backward",
-        [shape((rows, width), F32), shape((rows, width), BF16), shape((2 * keys, width), F32)]
-        + [shape((2 * keys, width), BF16)] * 3,
-        (*tables, sec_q, q_pair, *kvs, d_attn, d_pair, lse, lse_pair, delta, delta_pair),
-        tables=2,
-        flops=5 * pair_work,
-    )
-    dq_got = swap(dq_pair, "ctx", PAIR)
-    dkv_got = [swap(dkvs[step], "ctx", step) for step in range(1, SQUARE)]
     grad_q, grad_k, grad_v, grad_hk, grad_hv = local_call(
         add_grads_kernel,
         "add_grads",
@@ -316,6 +333,9 @@
     out = local_call(
         add_out_kernel, "add_out", [shape((rows, share), BF16)], (out_keep, out_core, out_near)
     )[0]
+    grad_k, grad_v, grad_hk, grad_hv, grad_q, out = lax.optimization_barrier(
+        (grad_k, grad_v, grad_hk, grad_hv, grad_q, out)
+    )
     return out, grad_q, grad_k, grad_v, grad_hk, grad_hv
 
 

time: 70.7 us -> 63.9 us (0.904)
  waiting for transfers between devices: 33.2 us -> 22.3 us
  local copies, waits for them, and re-layouts: 8.16 us -> 2.7 us
  Pallas kernels: 9.87 us -> 15.2 us
  starting transfers between devices: 18.3 us -> 22.8 us
    ppermute x17 -> x16, waiting for transfers between devices: 33.2 us -> 22.3 us  [swap(): return lax.ppermute(block, axis, [(i, i ^ bit) for i in range(count)])]
    pallas_call x0 -> x1, Pallas kernels: none -> 8.58 us  [any_call(): pl.pallas_call(body, name=name, out_shape=out_shapes, in_specs=[pl.BlockS...]
    unnamed x23 -> x15, local copies, waits for them, and re-layouts: 8.16 us -> 2.7 us
    ppermute x17 -> x16, starting transfers between devices: 18.3 us -> 22.8 us  [swap(): return lax.ppermute(block, axis, [(i, i ^ bit) for i in range(count)])]
    pallas_call x9 -> x8, Pallas kernels: 9.87 us -> 6.58 us  [local_call(): pl.pallas_call(body, name=name, out_shape=out_shapes, in_specs=[pl.BlockS...]
  transfers between devices with their start and end apart: 17 -> 16, of which waited for: 7 -> 6; matrix products, arithmetic and copies ran while one was open for 1% -> 0% of each run, Pallas kernels for 13% -> 19%
where the time goes in v3:
time: 63.9 us; the launch traced here: 63.7 us
  starting transfers between devices  22.8 us (36%)
  waiting for transfers between devices  22.3 us (35%)
  Pallas kernels  15.2 us (24%)
  local copies, waits for them, and re-layouts  2.7 us (4%)
  between operations  0.75 us (1%)
    ppermute x16, starting transfers between devices, swap(): return lax.ppermute(block, axis, [(i, i ^ bit) for i in range(count)])  22.8 us
    ppermute x16, waiting for transfers between devices, swap(): return lax.ppermute(block, axis, [(i, i ^ bit) for i in range(count)])  22.3 us
    pallas_call x1, Pallas kernels, any_call(): pl.pallas_call(body, name=name, out_shape=out_shapes, in_specs=[pl.BlockS...  8.58 us
    pallas_call x8, Pallas kernels, local_call(): pl.pallas_call(body, name=name, out_shape=out_shapes, in_specs=[pl.BlockS...  6.58 us
    unnamed x15, local copies, waits for them, and re-layouts  2.7 us
  transfers between devices with their start and end apart: 16, of which 6 were waited for; matrix products, arithmetic and copies ran while one was open for 0% of the time, Pallas kernels for 19%

profile of v3, /device:TPU:0, one launch (start us, length us, event | category | flops | bytes accessed | tf_op | source)
XLA Modules:
  0.0 63.7 jit_solution(3722036672000001046)
XLA Ops:
  0.6 0.0 copy-start.4
  0.6 0.0 copy-start.6
  0.7 0.0 copy-start.5
  0.7 3.0 %collective-permute-start.2 = (bf16[128,768]{1,0:T(8,128)(2,1)}, bf16[128,768]{1,0:T(8,128)(2,1)S(1)}, u32[]{:S(2)}, u32[]{:S(2)}) collective-permute-start(bf16[128,768]{1,0:T(8,128)(2,1)} %own_ref.1), channel_id=1, source_target_pairs={{0,2},{1,3},{2,0},{3,1},{4,6},{5,7},{6,4},{7,5},{8,10},{9,11},{10,... | collective-permute-start | bytes 589832 | tf_op jit(solution)/shard_map/ppermute | solution.py:34
  3.7 0.0 collective-permute-start.1
  3.7 0.2 collective-permute-start.3
  3.9 8.6 %load.1.kv0 = bf16[320,384]{1,0:T(8,128)(2,1)} custom-call(bf16[128,384]{1,0:T(8,128)(2,1)} %k_ref.1, bf16[32,384]{1,0:T(8,128)(2,1)} %hk_ref.1, bf16[128,384]{1,0:T(8,128)(2,1)} %v_ref.1, bf16[32,384]{1,0:T(8,128)(2,1)} %hv_ref.1), custom_call_target="tpu_custom_call" | custom-call | bytes 491520 | tf_op jit(solution)/shard_map/load/pallas_call | solution.py:54
  12.5 3.0 %collective-permute-start.7 = (bf16[320,384]{1,0:T(8,128)(2,1)}, bf16[320,384]{1,0:T(8,128)(2,1)S(1)}, u32[]{:S(2)}, u32[]{:S(2)}) collective-permute-start(bf16[320,384]{1,0:T(8,128)(2,1)} %load.1.kv0), channel_id=1, source_target_pairs={{0,12},{4,8},{8,4},{12,0},{16,28},{20,24},{24,20},{28,16},{1,13},{... | collective-permute-start | bytes 737288 | tf_op jit(solution)/shard_map/ppermute | solution.py:34
  15.5 0.4 collective-permute-start.6
  16.0 0.0 collective-permute-done.2.near_ref
  16.0 0.2 collective-permute-start.5
  16.2 0.0 collective-permute-done.1.core_ref
  16.2 2.9 %collective-permute-start = (bf16[128,384]{1,0:T(8,128)(2,1)}, bf16[128,384]{1,0:T(8,128)(2,1)S(1)}, u32[]{:S(2)}, u32[]{:S(2)}) collective-permute-start(bf16[128,384]{1,0:T(8,128)(2,1)} %q_own_ref.3), channel_id=1, source_target_pairs={{0,16},{4,20},{8,24},{12,28},{16,0},{20,4},{24,8},{28,12},{1,17},{... | collective-permute-start | bytes 294920 | tf_op jit(solution)/shard_map/ppermute | solution.py:34
  19.1 0.0 collective-permute-done.3.far_ref
  19.1 1.7 %copy-done = bf16[384,3072]{1,0:T(8,128)(2,1)S(1)} copy-done((bf16[384,3072]{1,0:T(8,128)(2,1)S(1)}, bf16[384,3072]{1,0:T(8,128)(2,1)}, u32[]{:S(2)}) %copy-start) | copy-done | bytes 2359320
  20.7 0.9 %copy-done.3 = bf16[128,768]{1,0:T(8,128)(2,1)S(1)} copy-done((bf16[128,768]{1,0:T(8,128)(2,1)S(1)}, bf16[128,768]{1,0:T(8,128)(2,1)}, u32[]{:S(2)}) %copy-start.3) | copy-done | bytes 196632
  21.7 0.8 %dattn.1.d_own_ref = bf16[128,384]{1,0:T(8,128)(2,1)S(1)} custom-call(bf16[128,768]{1,0:T(8,128)(2,1)S(1)} %copy-done.3, bf16[128,768]{1,0:T(8,128)(2,1)S(1)} %collective-permute-done.1.core_ref, bf16[128,768]{1,0:T(8,128)(2,1)S(1)} %collective-permute-done.2.near_ref, bf16[128,768]{1,0:T(8,128)(2,1)S(1)} %collective-permute-done.3.far_ref, ...), custom_call_target="tpu_custom_call" | custom-call | flops 301989888 | bytes 3244032 | tf_op jit(solution)/shard_map/dattn/pallas_call | solution.py:41
  22.5 0.1 collective-permute-start.4
  22.6 0.0 copy-done.6
  22.6 0.1 copy.15.levels_ref
  22.7 0.6 limits.1.limits_ref
  23.3 6.3 %collective-permute-done.q_pair_ref = bf16[128,384]{1,0:T(8,128)(2,1)S(1)} collective-permute-done((bf16[128,384]{1,0:T(8,128)(2,1)}, bf16[128,384]{1,0:T(8,128)(2,1)S(1)}, u32[]{:S(2)}, u32[]{:S(2)}) %collective-permute-start) | collective-permute-done | bytes 98336 | tf_op jit(solution)/shard_map/ppermute | solution.py:34
  29.6 0.0 collective-permute-done.7.kv3
  29.6 2.0 %collective-permute-done.6.kv2 = bf16[320,384]{1,0:T(8,128)(2,1)S(1)} collective-permute-done((bf16[320,384]{1,0:T(8,128)(2,1)}, bf16[320,384]{1,0:T(8,128)(2,1)S(1)}, u32[]{:S(2)}, u32[]{:S(2)}) %collective-permute-start.6) | collective-permute-done | bytes 245792 | tf_op jit(solution)/shard_map/ppermute | solution.py:34
  31.6 0.0 collective-permute-done.5.kv1
  31.6 0.0 collective-permute-done.4.d_pair_ref
  31.6 1.8 %forward.1 = (f32[16,256]{1,0:T(8,128)S(1)}, f32[384,128]{1,0:T(8,128)S(1)}, bf16[384,128]{1,0:T(8,128)(2,1)S(1)}, bf16[1920,256]{1,0:T(8,128)(2,1)S(1)}, f32[1920,256]{1,0:T(8,128)S(1)}) custom-call(s32[8,256]{1,0:T(8,128)S(1)} %limits.1.limits_ref, bf16[128,384]{1,0:T(8,128)(2,1)S(1)} %copy-done.4, bf16[128,384]{1,0:T(8,128)(2,1)S(1)} %collective-permute-done.q_pair_ref, ...), custom_call_target="tpu_custom_call" | custom-call | flops 377487360 | bytes 4644864 | tf_op jit(solution)/shard_map/forward/pallas_call | solution.py:41
  33.4 0.0 copy-start.1
  33.4 2.5 %collective-permute-start.8 = (f32[16,256]{1,0:T(8,128)S(1)}, f32[16,256]{1,0:T(8,128)S(1)}, u32[]{:S(2)}, u32[]{:S(2)}) collective-permute-start(f32[16,256]{1,0:T(8,128)S(1)} %get-tuple-element.36.stats_ref), channel_id=1, source_target_pairs={{0,16},{4,20},{8,24},{12,28},{16,0},{20,4},{24,8},{28,12},{1,17},{... | collective-permute-start | bytes 49160 | tf_op jit(solution)/shard_map/ppermute | solution.py:34
  35.9 2.2 %collective-permute-done.8.stats_pair_ref = f32[16,256]{1,0:T(8,128)S(1)} collective-permute-done((f32[16,256]{1,0:T(8,128)S(1)}, f32[16,256]{1,0:T(8,128)S(1)}, u32[]{:S(2)}, u32[]{:S(2)}) %collective-permute-start.8) | collective-permute-done | bytes 16416 | tf_op jit(solution)/shard_map/ppermute | solution.py:34
  38.1 2.4 %collective-permute-start.13 = (bf16[384,128]{1,0:T(8,128)(2,1)S(1)}, bf16[384,128]{1,0:T(8,128)(2,1)S(1)}, u32[]{:S(2)}, u32[]{:S(2)}) collective-permute-start(bf16[384,128]{1,0:T(8,128)(2,1)S(1)} %get-tuple-element.54), channel_id=1, source_target_pairs={{0,16},{4,20},{8,24},{12,28},{16,0},{20,4},{24,8},{28,12},{1,17},{... | collective-permute-start | bytes 294920 | tf_op jit(solution)/shard_map/ppermute | solution.py:34
  40.5 1.1 %backward.1 = (f32[128,384]{1,0:T(8,128)S(1)}, bf16[128,384]{1,0:T(8,128)(2,1)S(1)}, f32[320,384]{1,0:T(8,128)S(1)}, bf16[320,384]{1,0:T(8,128)(2,1)S(1)}, bf16[...) custom-call(bf16[128,384]{1,0:T(8,128)(2,1)S(1)} %copy-done.4, ...), custom_call_target="tpu_custom_call" | custom-call | flops 377487360 | bytes 5881856 | tf_op jit(solution)/shard_map/backward/pallas_call | solution.py:41
  41.7 2.1 %collective-permute-done.13.pair_ref = bf16[384,128]{1,0:T(8,128)(2,1)S(1)} collective-permute-done((bf16[384,128]{1,0:T(8,128)(2,1)S(1)}, bf16[384,128]{1,0:T(8,128)(2,1)S(1)}, u32[]{:S(2)}, u32[]{:S(2)}) %collective-permute-start.13) | collective-permute-done | bytes 98336 | tf_op jit(solution)/shard_map/ppermute | solution.py:34
  43.7 0.6 %project.1 = (bf16[128,1536]{1,0:T(8,128)(2,1)S(1)}, f32[128,768]{1,0:T(8,128)S(1)}, f32[128,768]{1,0:T(8,128)S(1)}) custom-call(f32[384,128]{1,0:T(8,128)S(1)} %get-tuple-element.53.own_ref, bf16[384,128]{1,0:T(8,128)(2,1)S(1)} %collective-permute-done.13.pair_ref, f32[16,256]{1,0:T(8,128)S(1)} %get-tuple-element.36.stats_ref, ...), custom_call_target="tpu_custom_call" | custom-call | flops 301989888 | bytes 3866624 | tf_op jit(solution)/shard_map/project/pallas_call | solution.py:41
  44.4 0.1 collective-permute-start.14
  44.5 0.6 collective-permute-start.10
  45.0 2.6 %collective-permute-start.11 = (bf16[320,384]{1,0:T(8,128)(2,1)S(1)}, bf16[320,384]{1,0:T(8,128)(2,1)S(1)}, u32[]{:S(2)}, u32[]{:S(2)}) collective-permute-start(bf16[320,384]{1,0:T(8,128)(2,1)S(1)} %get-tuple-element.46), channel_id=1, source_target_pairs={{0,8},{4,12},{8,0},{12,4},{16,24},{20,28},{24,16},{28,20},{1,9},{5... | collective-permute-start | bytes 737288 | tf_op jit(solution)/shard_map/ppermute | solution.py:34
  47.6 1.0 %collective-permute-start.12 = (bf16[320,384]{1,0:T(8,128)(2,1)S(1)}, bf16[320,384]{1,0:T(8,128)(2,1)S(1)}, u32[]{:S(2)}, u32[]{:S(2)}) collective-permute-start(bf16[320,384]{1,0:T(8,128)(2,1)S(1)} %get-tuple-element.47), channel_id=1, source_target_pairs={{0,12},{4,8},{8,4},{12,0},{16,28},{20,24},{24,20},{28,16},{1,13},{... | collective-permute-start | bytes 737288 | tf_op jit(solution)/shard_map/ppermute | solution.py:34
  48.5 0.0 collective-permute-done.14.core_ref
  48.6 1.5 %collective-permute-start.15 = (bf16[128,768]{1,0:T(8,128)(2,1)S(1)}, bf16[128,768]{1,0:T(8,128)(2,1)S(1)}, u32[]{:S(2)}, u32[]{:S(2)}) collective-permute-start(bf16[128,768]{1,0:T(8,128)(2,1)S(1)} %add_near.1), channel_id=1, source_target_pairs={{0,2},{1,3},{2,0},{3,1},{4,6},{5,7},{6,4},{7,5},{8,10},{9,11},{10,... | collective-permute-start | bytes 589832 | tf_op jit(solution)/shard_map/ppermute | solution.py:34
  50.1 2.3 %collective-permute-start.9 = (bf16[128,384]{1,0:T(8,128)(2,1)S(1)}, bf16[128,384]{1,0:T(8,128)(2,1)S(1)}, u32[]{:S(2)}, u32[]{:S(2)}) collective-permute-start(bf16[128,384]{1,0:T(8,128)(2,1)S(1)} %get-tuple-element.43), channel_id=1, source_target_pairs={{0,16},{4,20},{8,24},{12,28},{16,0},{20,4},{24,8},{28,12},{1,17},{... | collective-permute-start | bytes 294920 | tf_op jit(solution)/shard_map/ppermute | solution.py:34
  52.4 8.1 %collective-permute-done.9.dq_pair_ref = bf16[128,384]{1,0:T(8,128)(2,1)S(1)} collective-permute-done((bf16[128,384]{1,0:T(8,128)(2,1)S(1)}, bf16[128,384]{1,0:T(8,128)(2,1)S(1)}, u32[]{:S(2)}, u32[]{:S(2)}) %collective-permute-start.9) | collective-permute-done | bytes 98336 | tf_op jit(solution)/shard_map/ppermute | solution.py:34
  60.5 0.0 collective-permute-done.10.dkv1
  60.5 0.0 collective-permute-done.11.dkv2
  60.5 1.7 %collective-permute-done.12.dkv3 = bf16[320,384]{1,0:T(8,128)(2,1)S(1)} collective-permute-done((bf16[320,384]{1,0:T(8,128)(2,1)S(1)}, bf16[320,384]{1,0:T(8,128)(2,1)S(1)}, u32[]{:S(2)}, u32[]{:S(2)}) %collective-permute-start.12) | collective-permute-done | bytes 245792 | tf_op jit(solution)/shard_map/ppermute | solution.py:34
  62.2 0.8 %add_grads.1 = (bf16[128,384]{1,0:T(8,128)(2,1)}, bf16[128,384]{1,0:T(8,128)(2,1)}, bf16[128,384]{1,0:T(8,128)(2,1)}, bf16[32,384]{1,0:T(8,128)(2,1)}, bf16[32,384]{1,0:T(8,128)(2,1)}) custom-call(f32[128,384]{1,0:T(8,128)S(1)} %get-tuple-element.42.dq_ref, bf16[128,384]{1,0:T(8,128)(2,1)S(1)} %collective-permute-done.9.dq_pair_ref, ...), custom_call_target="tpu_custom_call" | custom-call | bytes 1867776 | tf_op jit(solution)/shard_map/add_grads/pallas_call | solution.py:41
  63.0 0.0 collective-permute-done.15.near_ref
  63.0 0.7 %add_out.1 = bf16[128,768]{1,0:T(8,128)(2,1)} custom-call(f32[128,768]{1,0:T(8,128)S(1)} %get-tuple-element.55.keep_ref, bf16[128,1536]{1,0:T(8,128)(2,1)S(1)} %collective-permute-done.14.core_ref, bf16[128,768]{1,0:T(8,128)(2,1)S(1)} %collective-permute-done.15.near_ref), custom_call_target="tpu_custom_call" | custom-call | bytes 1179648 | tf_op jit(solution)/shard_map/add_out/pallas_call | solution.py:41
  (8 shorter events, 0.0 us)
Async XLA Ops:
  0.6 30.9 %copy-start.4 = (bf16[128,384]{1,0:T(8,128)(2,1)S(1)}, bf16[128,384]{1,0:T(8,128)(2,1)}, u32[]{:S(2)}) copy-start(bf16[128,384]{1,0:T(8,128)(2,1)} %q_own_ref.3) | copy-start | bytes 294916
  0.6 21.9 %copy-start.6 = (s32[8,2]{0,1:T(2,128)S(1)}, s32[8,2]{0,1:T(2,128)}, u32[]{:S(2)}) copy-start(s32[8,2]{0,1:T(2,128)} %param.14) | copy-start | bytes 196
  0.7 22.0 %copy-start.5 = (s32[8]{0:T(128)S(1)}, s32[8]{0:T(128)}, u32[]{:S(2)}) copy-start(s32[8]{0:T(128)} %counts_ref.1) | copy-start | bytes 100
  0.7 15.3 %collective-permute-start.2 = (bf16[128,768]{1,0:T(8,128)(2,1)}, bf16[128,768]{1,0:T(8,128)(2,1)S(1)}, u32[]{:S(2)}, u32[]{:S(2)}) collective-permute-start(bf16[128,768]{1,0:T(8,128)(2,1)} %own_ref.1), channel_id=1, source_target_pairs={{0,2},{1,3},{2,0},{3,1},{4,6},{5,7},{6,4},{7,5},{8,10},{9,11},{10,... | collective-permute-start | bytes 589832 | tf_op jit(solution)/shard_map/ppermute | solution.py:34
  3.7 12.5 %collective-permute-start.1 = (bf16[128,768]{1,0:T(8,128)(2,1)}, bf16[128,768]{1,0:T(8,128)(2,1)S(1)}, u32[]{:S(2)}, u32[]{:S(2)}) collective-permute-start(bf16[128,768]{1,0:T(8,128)(2,1)} %own_ref.1), channel_id=1, source_target_pairs={{0,1},{1,0},{2,3},{3,2},{4,5},{5,4},{6,7},{7,6},{8,9},{9,8},{10,11... | collective-permute-start | bytes 589832 | tf_op jit(solution)/shard_map/ppermute | solution.py:34
  3.7 15.4 %collective-permute-start.3 = (bf16[128,768]{1,0:T(8,128)(2,1)}, bf16[128,768]{1,0:T(8,128)(2,1)S(1)}, u32[]{:S(2)}, u32[]{:S(2)}) collective-permute-start(bf16[128,768]{1,0:T(8,128)(2,1)} %own_ref.1), channel_id=1, source_target_pairs={{0,3},{1,2},{2,1},{3,0},{4,7},{5,6},{6,5},{7,4},{8,11},{9,10},{10,... | collective-permute-start | bytes 589832 | tf_op jit(solution)/shard_map/ppermute | solution.py:34
  12.5 17.1 %collective-permute-start.7 = (bf16[320,384]{1,0:T(8,128)(2,1)}, bf16[320,384]{1,0:T(8,128)(2,1)S(1)}, u32[]{:S(2)}, u32[]{:S(2)}) collective-permute-start(bf16[320,384]{1,0:T(8,128)(2,1)} %load.1.kv0), channel_id=1, source_target_pairs={{0,12},{4,8},{8,4},{12,0},{16,28},{20,24},{24,20},{28,16},{1,13},{... | collective-permute-start | bytes 737288 | tf_op jit(solution)/shard_map/ppermute | solution.py:34
  15.5 16.1 %collective-permute-start.6 = (bf16[320,384]{1,0:T(8,128)(2,1)}, bf16[320,384]{1,0:T(8,128)(2,1)S(1)}, u32[]{:S(2)}, u32[]{:S(2)}) collective-permute-start(bf16[320,384]{1,0:T(8,128)(2,1)} %load.1.kv0), channel_id=1, source_target_pairs={{0,8},{4,12},{8,0},{12,4},{16,24},{20,28},{24,16},{28,20},{1,9},{5... | collective-permute-start | bytes 737288 | tf_op jit(solution)/shard_map/ppermute | solution.py:34
  16.0 15.6 %collective-permute-start.5 = (bf16[320,384]{1,0:T(8,128)(2,1)}, bf16[320,384]{1,0:T(8,128)(2,1)S(1)}, u32[]{:S(2)}, u32[]{:S(2)}) collective-permute-start(bf16[320,384]{1,0:T(8,128)(2,1)} %load.1.kv0), channel_id=1, source_target_pairs={{0,4},{4,0},{8,12},{12,8},{16,20},{20,16},{24,28},{28,24},{1,5},{5... | collective-permute-start | bytes 737288 | tf_op jit(solution)/shard_map/ppermute | solution.py:34
  16.2 13.4 %collective-permute-start = (bf16[128,384]{1,0:T(8,128)(2,1)}, bf16[128,384]{1,0:T(8,128)(2,1)S(1)}, u32[]{:S(2)}, u32[]{:S(2)}) collective-permute-start(bf16[128,384]{1,0:T(8,128)(2,1)} %q_own_ref.3), channel_id=1, source_target_pairs={{0,16},{4,20},{8,24},{12,28},{16,0},{20,4},{24,8},{28,12},{1,17},{... | collective-permute-start | bytes 294920 | tf_op jit(solution)/shard_map/ppermute | solution.py:34
  19.1 1.7 %copy-start = (bf16[384,3072]{1,0:T(8,128)(2,1)S(1)}, bf16[384,3072]{1,0:T(8,128)(2,1)}, u32[]{:S(2)}) copy-start(bf16[384,3072]{1,0:T(8,128)(2,1)} %w_ref.3) | copy-start | bytes 7077892
  20.7 0.9 %copy-start.3 = (bf16[128,768]{1,0:T(8,128)(2,1)S(1)}, bf16[128,768]{1,0:T(8,128)(2,1)}, u32[]{:S(2)}) copy-start(bf16[128,768]{1,0:T(8,128)(2,1)} %own_ref.1) | copy-start | bytes 589828
  21.7 9.9 %copy-start.2 = (bf16[320,384]{1,0:T(8,128)(2,1)S(1)}, bf16[320,384]{1,0:T(8,128)(2,1)}, u32[]{:S(2)}) copy-start(bf16[320,384]{1,0:T(8,128)(2,1)} %load.1.kv0) | copy-start | bytes 737284
  22.5 9.1 %collective-permute-start.4 = (bf16[128,384]{1,0:T(8,128)(2,1)S(1)}, bf16[128,384]{1,0:T(8,128)(2,1)S(1)}, u32[]{:S(2)}, u32[]{:S(2)}) collective-permute-start(bf16[128,384]{1,0:T(8,128)(2,1)S(1)} %dattn.1.d_own_ref), channel_id=1, source_target_pairs={{0,16},{4,20},{8,24},{12,28},{16,0},{20,4},{24,8},{28,12},{1,17},{... | collective-permute-start | bytes 294920 | tf_op jit(solution)/shard_map/ppermute | solution.py:34
  33.4 10.3 %copy-start.1 = (bf16[384,3072]{1,0:T(8,128)(2,1)S(1)}, bf16[384,3072]{1,0:T(8,128)(2,1)}, u32[]{:S(2)}) copy-start(bf16[384,3072]{1,0:T(8,128)(2,1)} %w_ref.3) | copy-start | bytes 7077892
  33.4 4.7 %collective-permute-start.8 = (f32[16,256]{1,0:T(8,128)S(1)}, f32[16,256]{1,0:T(8,128)S(1)}, u32[]{:S(2)}, u32[]{:S(2)}) collective-permute-start(f32[16,256]{1,0:T(8,128)S(1)} %get-tuple-element.36.stats_ref), channel_id=1, source_target_pairs={{0,16},{4,20},{8,24},{12,28},{16,0},{20,4},{24,8},{28,12},{1,17},{... | collective-permute-start | bytes 49160 | tf_op jit(solution)/shard_map/ppermute | solution.py:34
  38.1 5.6 %collective-permute-start.13 = (bf16[384,128]{1,0:T(8,128)(2,1)S(1)}, bf16[384,128]{1,0:T(8,128)(2,1)S(1)}, u32[]{:S(2)}, u32[]{:S(2)}) collective-permute-start(bf16[384,128]{1,0:T(8,128)(2,1)S(1)} %get-tuple-element.54), channel_id=1, source_target_pairs={{0,16},{4,20},{8,24},{12,28},{16,0},{20,4},{24,8},{28,12},{1,17},{... | collective-permute-start | bytes 294920 | tf_op jit(solution)/shard_map/ppermute | solution.py:34
  44.4 4.2 %collective-permute-start.14 = (bf16[128,1536]{1,0:T(8,128)(2,1)S(1)}, bf16[128,1536]{1,0:T(8,128)(2,1)S(1)}, u32[]{:S(2)}, u32[]{:S(2)}) collective-permute-start(bf16[128,1536]{1,0:T(8,128)(2,1)S(1)} %get-tuple-element.56), channel_id=1, source_target_pairs={{0,1},{1,0},{2,3},{3,2},{4,5},{5,4},{6,7},{7,6},{8,9},{9,8},{10,11... | collective-permute-start | bytes 1179656 | tf_op jit(solution)/shard_map/ppermute | solution.py:34
  44.5 16.1 %collective-permute-start.10 = (bf16[320,384]{1,0:T(8,128)(2,1)S(1)}, bf16[320,384]{1,0:T(8,128)(2,1)S(1)}, u32[]{:S(2)}, u32[]{:S(2)}) collective-permute-start(bf16[320,384]{1,0:T(8,128)(2,1)S(1)} %get-tuple-element.45), channel_id=1, source_target_pairs={{0,4},{4,0},{8,12},{12,8},{16,20},{20,16},{24,28},{28,24},{1,5},{5... | collective-permute-start | bytes 737288 | tf_op jit(solution)/shard_map/ppermute | solution.py:34
  45.0 15.5 %collective-permute-start.11 = (bf16[320,384]{1,0:T(8,128)(2,1)S(1)}, bf16[320,384]{1,0:T(8,128)(2,1)S(1)}, u32[]{:S(2)}, u32[]{:S(2)}) collective-permute-start(bf16[320,384]{1,0:T(8,128)(2,1)S(1)} %get-tuple-element.46), channel_id=1, source_target_pairs={{0,8},{4,12},{8,0},{12,4},{16,24},{20,28},{24,16},{28,20},{1,9},{5... | collective-permute-start | bytes 737288 | tf_op jit(solution)/shard_map/ppermute | solution.py:34
  47.6 14.6 %collective-permute-start.12 = (bf16[320,384]{1,0:T(8,128)(2,1)S(1)}, bf16[320,384]{1,0:T(8,128)(2,1)S(1)}, u32[]{:S(2)}, u32[]{:S(2)}) collective-permute-start(bf16[320,384]{1,0:T(8,128)(2,1)S(1)} %get-tuple-element.47), channel_id=1, source_target_pairs={{0,12},{4,8},{8,4},{12,0},{16,28},{20,24},{24,20},{28,16},{1,13},{... | collective-permute-start | bytes 737288 | tf_op jit(solution)/shard_map/ppermute | solution.py:34
  48.6 14.4 %collective-permute-start.15 = (bf16[128,768]{1,0:T(8,128)(2,1)S(1)}, bf16[128,768]{1,0:T(8,128)(2,1)S(1)}, u32[]{:S(2)}, u32[]{:S(2)}) collective-permute-start(bf16[128,768]{1,0:T(8,128)(2,1)S(1)} %add_near.1), channel_id=1, source_target_pairs={{0,2},{1,3},{2,0},{3,1},{4,6},{5,7},{6,4},{7,5},{8,10},{9,11},{10,... | collective-permute-start | bytes 589832 | tf_op jit(solution)/shard_map/ppermute | solution.py:34
  50.1 10.4 %collective-permute-start.9 = (bf16[128,384]{1,0:T(8,128)(2,1)S(1)}, bf16[128,384]{1,0:T(8,128)(2,1)S(1)}, u32[]{:S(2)}, u32[]{:S(2)}) collective-permute-start(bf16[128,384]{1,0:T(8,128)(2,1)S(1)} %get-tuple-element.43), channel_id=1, source_target_pairs={{0,16},{4,20},{8,24},{12,28},{16,0},{20,4},{24,8},{28,12},{1,17},{... | collective-permute-start | bytes 294920 | tf_op jit(solution)/shard_map/ppermute | solution.py:34

commit v4 on v3

--- a/solution.py
+++ b/solution.py
@@ -49,42 +49,37 @@
     )(*args)
 
 
-def any_call(body, name, out_shapes, args, copies):
-    moved = sum(a.size * a.dtype.itemsize for a in args)
+def load_kernel(k_ref, hk_ref, v_ref, hv_ref, kv_out, kv_ref, sems):
+    inward, outward, begin = [], [], 0
+    for i, ref in enumerate((k_ref, hk_ref, v_ref, hv_ref)):
+        part = pl.ds(begin, ref.shape[0])
+        inward.append(pltpu.make_async_copy(ref, kv_ref.at[part], sems.at[0, i]))
+        outward.append(pltpu.make_async_copy(kv_ref.at[part], kv_out.at[part], sems.at[1, i]))
+        begin += ref.shape[0]
+    for copy in inward:
+        copy.start()
+    for before, after in zip(inward, outward):
+        before.wait()
+        after.start()
+    for copy in outward:
+        copy.wait()
+
+
+def load_keys(*arrays):
+    rows = sum(a.shape[0] for a in arrays)
+    width = arrays[0].shape[1]
     return pl.pallas_call(
-        body,
-        name=name,
-        out_shape=out_shapes,
-        in_specs=[pl.BlockSpec(memory_space=pl.ANY)] * len(args),
-        out_specs=[pl.BlockSpec(memory_space=pl.ANY)] * len(out_shapes),
-        scratch_shapes=[pltpu.SemaphoreType.DMA((copies,))],
+        load_kernel,
+        name="load",
+        out_shape=jax.ShapeDtypeStruct((rows, width), BF16),
+        in_specs=[pl.BlockSpec(memory_space=pl.ANY)] * len(arrays),
+        out_specs=pl.BlockSpec(memory_space=pl.ANY),
+        scratch_shapes=[pltpu.VMEM((rows, width), BF16), pltpu.SemaphoreType.DMA((2, len(arrays)))],
         compiler_params=pltpu.CompilerParams(vmem_limit_bytes=60 * 2**20),
-        cost_estimate=pl.CostEstimate(flops=0, bytes_accessed=2 * moved, transcendentals=0),
-    )(*args)
-
-
-def copy_all(pairs, sems):
-    copies = [
-        pltpu.make_async_copy(source, target, sems.at[i]) for i, (source, target) in enumerate(pairs)
-    ]
-    for copy in copies:
-        copy.start()
-    for copy in copies:
-        copy.wait()
-
-
-def load_kernel(k_ref, hk_ref, v_ref, hv_ref, kv_out, sems):
-    rows, capacity = k_ref.shape[0], hk_ref.shape[0]
-    keys = rows + capacity
-    copy_all(
-        [
-            (k_ref, kv_out.at[pl.ds(0, rows)]),
-            (v_ref, kv_out.at[pl.ds(keys, rows)]),
-            (hk_ref, kv_out.at[pl.ds(rows, capacity)]),
-            (hv_ref, kv_out.at[pl.ds(keys + rows, capacity)]),
-        ],
-        sems,
-    )
+        cost_estimate=pl.CostEstimate(
+            flops=0, bytes_accessed=4 * rows * width * 2, transcendentals=0
+        ),
+    )(*arrays)
 
 
 def limits_kernel(levels_ref, counts_ref, limits_ref):
@@ -194,19 +189,14 @@
     out_ref[...] = (next_ref[...] + core_ref[:, size:].astype(F32)).astype(BF16)
 
 
-def add_out_kernel(keep_ref, core_ref, near_ref, out_ref):
-    size = keep_ref.shape[1]
-    total = keep_ref[...] + core_ref[:, :size].astype(F32) + near_ref[...].astype(F32)
-    out_ref[...] = total.astype(BF16)
-
-
 def backward_kernel(
     q_own_ref, q_pair_ref, d_own_ref, d_pair_ref, kv0, kv1, kv2, kv3,
     stats_ref, stats_pair_ref, probs_ref, dprobs_ref,
-    dq_own_ref, dq_pair_ref, dkv0, dkv1, dkv2, dkv3,
+    dq_own_ref, dq_pair_ref, dkv_ref,
 ):
     rows = q_own_ref.shape[0]
     keys = kv0.shape[0] // 2
+    place = lax.rem(lax.axis_index("ctx"), SQUARE)
 
     def swapped(row):
         return jnp.concatenate([row[:, rows:], row[:, :rows]], axis=1)
@@ -221,37 +211,41 @@
         delta += weight_pair * swapped(stats_pair_ref[8 + head : 9 + head])
         features = slice(head * HDIM, (head + 1) * HDIM)
         dquery = None
-        for step, (ref, out) in enumerate(zip((kv0, kv1, kv2, kv3), (dkv0, dkv1, dkv2, dkv3))):
+        for step, ref in enumerate((kv0, kv1, kv2, kv3)):
+            first = pl.multiple_of((place ^ step) * 2 * keys, 2 * keys)
             begin = (head * SQUARE + step) * keys
             probs = (probs_ref[begin : begin + keys].astype(F32) * weight).astype(BF16)
             dprobs = dprobs_ref[begin : begin + keys]
             dscores = (probs.astype(F32) * (dprobs - delta)).astype(BF16)
-            out[:keys, features] = (contract(dscores, query, 1, 0) * SCALE).astype(out.dtype)
-            out[keys:, features] = contract(probs, dattn, 1, 0).astype(out.dtype)
+            grad_key = (contract(dscores, query, 1, 0) * SCALE).astype(BF16)
+            dkv_ref[pl.ds(first, keys), features] = grad_key
+            grad_value = contract(probs, dattn, 1, 0).astype(BF16)
+            dkv_ref[pl.ds(first + keys, keys), features] = grad_value
             part = contract(dscores, head_slice(ref[:keys], head), 0, 0)
             dquery = part if dquery is None else dquery + part
         dq_own_ref[:, features] = dquery[:rows] * SCALE
         dq_pair_ref[:, features] = (dquery[rows:] * SCALE).astype(BF16)
 
 
-def add_grads_kernel(
-    dq_ref, dq_pair_ref, dkv0, dkv1, dkv2, dkv3, q_out, k_out, v_out, hk_out, hv_out
+def finish_kernel(
+    dq_ref, dq_pair_ref, dkv_ref, keep_ref, core_ref, near_ref,
+    q_out, k_out, v_out, hk_out, hv_out, out_ref,
 ):
     rows, capacity = k_out.shape[0], hk_out.shape[0]
     keys = rows + capacity
+
+    def total(begin, size):
+        parts = (dkv_ref[pl.ds(step * 2 * keys + begin, size)] for step in range(SQUARE))
+        return sum(part.astype(F32) for part in parts).astype(BF16)
+
     q_out[...] = (dq_ref[...] + dq_pair_ref[...].astype(F32)).astype(BF16)
-
-    def total(begin, size):
-        part = slice(begin, begin + size)
-        value = dkv0[part]
-        for ref in (dkv1, dkv2, dkv3):
-            value = value + ref[part].astype(F32)
-        return value.astype(BF16)
-
     k_out[...] = total(0, rows)
     hk_out[...] = total(rows, capacity)
     v_out[...] = total(keys, rows)
     hv_out[...] = total(keys + rows, capacity)
+    size = keep_ref.shape[1]
+    out = keep_ref[...] + core_ref[:, :size].astype(F32) + near_ref[...].astype(F32)
+    out_ref[...] = out.astype(BF16)
 
 
 def blocked(sec_q, sec_k, sec_v, hist_k, hist_v, frame_levels, frame_counts, w_out, grad_out):
@@ -264,9 +258,7 @@
     work = 2 * SQUARE * keys * 2 * rows * width
 
     grad_core, grad_near, grad_far = (swap(grad_out, "head", step) for step in range(1, 4))
-    kv0 = any_call(
-        load_kernel, "load", [shape((2 * keys, width), BF16)], (sec_k, hist_k, sec_v, hist_v), copies=4
-    )[0]
+    kv0 = load_keys(sec_k, hist_k, sec_v, hist_v)
     kvs = [kv0] + [swap(kv0, "ctx", step) for step in range(1, SQUARE)]
     q_pair = swap(sec_q, "ctx", PAIR)
     d_own = local_call(
@@ -300,15 +292,19 @@
     stats_pair = swap(stats, "ctx", PAIR)
     stats_pair, attn_pair = lax.optimization_barrier((stats_pair, attn_pair))
     attn_got = swap(attn_pair, "ctx", PAIR)
-    dq_own, dq_pair, *dkvs = local_call(
+    dq_own, dq_pair, dkv = local_call(
         backward_kernel,
         "backward",
-        [shape((rows, width), F32), shape((rows, width), BF16), shape((2 * keys, width), F32)]
-        + [shape((2 * keys, width), BF16)] * 3,
+        [
+            shape((rows, width), F32),
+            shape((rows, width), BF16),
+            shape((SQUARE * 2 * keys, width), BF16),
+        ],
         (sec_q, q_pair, d_own, d_pair, *kvs, stats, stats_pair, probs, dprobs),
         flops=3 * work,
     )
-    dkv_got = [swap(dkvs[step], "ctx", step) for step in range(1, SQUARE)]
+    squares = [list(range(i, i + SQUARE)) for i in range(0, lax.axis_size("ctx"), SQUARE)]
+    dkv_got = lax.all_to_all(dkv, "ctx", 0, 0, axis_index_groups=squares, tiled=True)
     dq_got = swap(dq_pair, "ctx", PAIR)
     attn_own, dq_own = lax.optimization_barrier((attn_own, dq_own))
     out_send, out_next, out_keep = local_call(
@@ -324,17 +320,13 @@
         "head",
         2,
     )
-    grad_q, grad_k, grad_v, grad_hk, grad_hv = local_call(
-        add_grads_kernel,
-        "add_grads",
-        [shape((rows, width), BF16)] * 3 + [shape((capacity, width), BF16)] * 2,
-        (dq_own, dq_got, dkvs[0], *dkv_got),
-    )
-    out = local_call(
-        add_out_kernel, "add_out", [shape((rows, share), BF16)], (out_keep, out_core, out_near)
-    )[0]
-    grad_k, grad_v, grad_hk, grad_hv, grad_q, out = lax.optimization_barrier(
-        (grad_k, grad_v, grad_hk, grad_hv, grad_q, out)
+    grad_q, grad_k, grad_v, grad_hk, grad_hv, out = local_call(
+        finish_kernel,
+        "finish",
+        [shape((rows, width), BF16)] * 3
+        + [shape((capacity, width), BF16)] * 2
+        + [shape((rows, share), BF16)],
+        (dq_own, dq_got, dkv_got, out_keep, out_core, out_near),
     )
     return out, grad_q, grad_k, grad_v, grad_hk, grad_hv
 

time: 63.9 us -> 71.2 us (1.11)
  the two profiles are of different devices: /device:TPU:0 before, /device:TPU:8 now
where the time goes in v4:
time: 71.2 us; the launch traced here: 70.7 us
  waiting for transfers between devices  29.4 us (41%)
  starting transfers between devices  20.9 us (29%)
  local copies, waits for them, and re-layouts  12 us (17%)
  Pallas kernels  7.64 us (11%)
  between operations  0.81 us (1%)
    ppermute x13, waiting for transfers between devices, swap(): return lax.ppermute(block, axis, [(i, i ^ bit) for i in range(count)])  29.4 us
    ppermute x13, starting transfers between devices, swap(): return lax.ppermute(block, axis, [(i, i ^ bit) for i in range(count)])  15.6 us
    unnamed x49, local copies, waits for them, and re-layouts  12 us
    pallas_call x7, Pallas kernels, local_call(): pl.pallas_call(body, name=name, out_shape=out_shapes, in_specs=[pl.BlockS...  5.97 us
    all_to_all x1, starting transfers between devices, blocked(): lax.all_to_all(dkv, 'ctx', 0, 0, axis_index_groups=squares, tiled=True)  5.33 us
    pallas_call x1, Pallas kernels, load_keys(): pl.pallas_call(load_kernel, name='load', out_shape=jax.ShapeDtypeStruct((...  1.67 us
  transfers between devices with their start and end apart: 14, of which 8 were waited for; matrix products, arithmetic and copies ran while one was open for 0% of the time, Pallas kernels for 5%

profile of v4, /device:TPU:8, one launch (start us, length us, event | category | flops | bytes accessed | tf_op | source)
XLA Modules:
  0.0 70.7 jit_solution(16640942594760621804)
XLA Ops:
  0.6 0.0 copy-start.11
  0.7 1.6 %collective-permute-start.2 = (bf16[128,768]{1,0:T(8,128)(2,1)}, bf16[128,768]{1,0:T(8,128)(2,1)S(1)}, u32[]{:S(2)}, u32[]{:S(2)}) collective-permute-start(bf16[128,768]{1,0:T(8,128)(2,1)} %own_ref.1), channel_id=1, source_target_pairs={{0,2},{1,3},{2,0},{3,1},{4,6},{5,7},{6,4},{7,5},{8,10},{9,11},{10,... | collective-permute-start | bytes 589832 | tf_op jit(solution)/shard_map/ppermute | solution.py:34
  2.2 0.0 collective-permute-start.1
  2.2 0.6 collective-permute-start.3
  2.9 1.7 %load.1.kv0 = bf16[320,384]{1,0:T(8,128)(2,1)} custom-call(bf16[128,384]{1,0:T(8,128)(2,1)} %k_ref.1, bf16[32,384]{1,0:T(8,128)(2,1)} %hk_ref.1, bf16[128,384]{1,0:T(8,128)(2,1)} %v_ref.1, bf16[32,384]{1,0:T(8,128)(2,1)} %hv_ref.1), custom_call_target="tpu_custom_call" | custom-call | bytes 983040 | tf_op jit(solution)/shard_map/load/pallas_call | solution.py:71
  4.6 1.5 %collective-permute-start.7 = (bf16[320,384]{1,0:T(8,128)(2,1)}, bf16[320,384]{1,0:T(8,128)(2,1)S(1)}, u32[]{:S(2)}, u32[]{:S(2)}) collective-permute-start(bf16[320,384]{1,0:T(8,128)(2,1)} %load.1.kv0), channel_id=1, source_target_pairs={{0,12},{4,8},{8,4},{12,0},{16,28},{20,24},{24,20},{28,16},{1,13},{... | collective-permute-start | bytes 737288 | tf_op jit(solution)/shard_map/ppermute | solution.py:34
  6.0 1.6 %collective-permute-start.6 = (bf16[320,384]{1,0:T(8,128)(2,1)}, bf16[320,384]{1,0:T(8,128)(2,1)S(1)}, u32[]{:S(2)}, u32[]{:S(2)}) collective-permute-start(bf16[320,384]{1,0:T(8,128)(2,1)} %load.1.kv0), channel_id=1, source_target_pairs={{0,8},{4,12},{8,0},{12,4},{16,24},{20,28},{24,16},{28,20},{1,9},{5... | collective-permute-start | bytes 737288 | tf_op jit(solution)/shard_map/ppermute | solution.py:34
  7.6 1.1 %collective-permute-done.2.near_ref = bf16[128,768]{1,0:T(8,128)(2,1)S(1)} collective-permute-done((bf16[128,768]{1,0:T(8,128)(2,1)}, bf16[128,768]{1,0:T(8,128)(2,1)S(1)}, u32[]{:S(2)}, u32[]{:S(2)}) %collective-permute-start.2) | collective-permute-done | bytes 196640 | tf_op jit(solution)/shard_map/ppermute | solution.py:34
  8.7 1.5 %collective-permute-start.5 = (bf16[320,384]{1,0:T(8,128)(2,1)}, bf16[320,384]{1,0:T(8,128)(2,1)S(1)}, u32[]{:S(2)}, u32[]{:S(2)}) collective-permute-start(bf16[320,384]{1,0:T(8,128)(2,1)} %load.1.kv0), channel_id=1, source_target_pairs={{0,4},{4,0},{8,12},{12,8},{16,20},{20,16},{24,28},{28,24},{1,5},{5... | collective-permute-start | bytes 737288 | tf_op jit(solution)/shard_map/ppermute | solution.py:34
  10.2 0.0 collective-permute-done.1.core_ref
  10.3 2.6 %collective-permute-start = (bf16[128,384]{1,0:T(8,128)(2,1)}, bf16[128,384]{1,0:T(8,128)(2,1)S(1)}, u32[]{:S(2)}, u32[]{:S(2)}) collective-permute-start(bf16[128,384]{1,0:T(8,128)(2,1)} %q_own_ref.3), channel_id=1, source_target_pairs={{0,16},{4,20},{8,24},{12,28},{16,0},{20,4},{24,8},{28,12},{1,17},{... | collective-permute-start | bytes 294920 | tf_op jit(solution)/shard_map/ppermute | solution.py:34
  12.8 0.0 collective-permute-done.3.far_ref
  12.8 1.7 %copy-done = bf16[384,3072]{1,0:T(8,128)(2,1)S(1)} copy-done((bf16[384,3072]{1,0:T(8,128)(2,1)S(1)}, bf16[384,3072]{1,0:T(8,128)(2,1)}, u32[]{:S(2)}) %copy-start) | copy-done | bytes 2359320
  14.5 0.9 %copy-done.8 = bf16[128,768]{1,0:T(8,128)(2,1)S(1)} copy-done((bf16[128,768]{1,0:T(8,128)(2,1)S(1)}, bf16[128,768]{1,0:T(8,128)(2,1)}, u32[]{:S(2)}) %copy-start.8) | copy-done | bytes 196632
  15.4 0.8 %dattn.1.d_own_ref = bf16[128,384]{1,0:T(8,128)(2,1)S(1)} custom-call(bf16[128,768]{1,0:T(8,128)(2,1)S(1)} %copy-done.8, bf16[128,768]{1,0:T(8,128)(2,1)S(1)} %collective-permute-done.1.core_ref, bf16[128,768]{1,0:T(8,128)(2,1)S(1)} %collective-permute-done.2.near_ref, bf16[128,768]{1,0:T(8,128)(2,1)S(1)} %collective-permute-done.3.far_ref, ...), custom_call_target="tpu_custom_call" | custom-call | flops 301989888 | bytes 3244032 | tf_op jit(solution)/shard_map/dattn/pallas_call | solution.py:41
  16.3 0.7 %collective-permute-start.4 = (bf16[128,384]{1,0:T(8,128)(2,1)S(1)}, bf16[128,384]{1,0:T(8,128)(2,1)S(1)}, u32[]{:S(2)}, u32[]{:S(2)}) collective-permute-start(bf16[128,384]{1,0:T(8,128)(2,1)S(1)} %dattn.1.d_own_ref), channel_id=1, source_target_pairs={{0,16},{4,20},{8,24},{12,28},{16,0},{20,4},{24,8},{28,12},{1,17},{... | collective-permute-start | bytes 294920 | tf_op jit(solution)/shard_map/ppermute | solution.py:34
  17.0 0.1 copy.15.levels_ref
  17.1 0.6 limits.1.limits_ref
  17.7 5.4 %collective-permute-done.q_pair_ref = bf16[128,384]{1,0:T(8,128)(2,1)S(1)} collective-permute-done((bf16[128,384]{1,0:T(8,128)(2,1)}, bf16[128,384]{1,0:T(8,128)(2,1)S(1)}, u32[]{:S(2)}, u32[]{:S(2)}) %collective-permute-start) | collective-permute-done | bytes 98336 | tf_op jit(solution)/shard_map/ppermute | solution.py:34
  23.1 0.0 collective-permute-done.5.kv1
  23.2 1.1 %collective-permute-done.4.d_pair_ref = bf16[128,384]{1,0:T(8,128)(2,1)S(1)} collective-permute-done((bf16[128,384]{1,0:T(8,128)(2,1)S(1)}, bf16[128,384]{1,0:T(8,128)(2,1)S(1)}, u32[]{:S(2)}, u32[]{:S(2)}) %collective-permute-start.4) | collective-permute-done | bytes 98336 | tf_op jit(solution)/shard_map/ppermute | solution.py:34
  24.3 1.8 %forward.1 = (f32[16,256]{1,0:T(8,128)S(1)}, f32[384,128]{1,0:T(8,128)S(1)}, bf16[384,128]{1,0:T(8,128)(2,1)S(1)}, bf16[1920,256]{1,0:T(8,128)(2,1)S(1)}, f32[1920,256]{1,0:T(8,128)S(1)}) custom-call(s32[8,256]{1,0:T(8,128)S(1)} %limits.1.limits_ref, bf16[128,384]{1,0:T(8,128)(2,1)S(1)} %copy-done.11, bf16[128,384]{1,0:T(8,128)(2,1)S(1)} %collective-permute-done.q_pair_ref, ...), custom_call_target="tpu_custom_call" | custom-call | flops 377487360 | bytes 4644864 | tf_op jit(solution)/shard_map/forward/pallas_call | solution.py:41
  26.1 0.0 copy-start.9
  26.1 0.7 copy-done.9
  26.8 2.9 %collective-permute-start.8 = (f32[16,256]{1,0:T(8,128)S(1)}, f32[16,256]{1,0:T(8,128)S(1)}, u32[]{:S(2)}, u32[]{:S(2)}) collective-permute-start(f32[16,256]{1,0:T(8,128)S(1)} %get-tuple-element.28.stats_ref), channel_id=1, source_target_pairs={{0,16},{4,20},{8,24},{12,28},{16,0},{20,4},{24,8},{28,12},{1,17},{... | collective-permute-start | bytes 49160 | tf_op jit(solution)/shard_map/ppermute | solution.py:34
  29.7 1.7 %collective-permute-done.8.stats_pair_ref = f32[16,256]{1,0:T(8,128)S(1)} collective-permute-done((f32[16,256]{1,0:T(8,128)S(1)}, f32[16,256]{1,0:T(8,128)S(1)}, u32[]{:S(2)}, u32[]{:S(2)}) %collective-permute-start.8) | collective-permute-done | bytes 16416 | tf_op jit(solution)/shard_map/ppermute | solution.py:34
  31.5 0.9 %copy-done.7 = bf16[320,384]{1,0:T(8,128)(2,1)S(1)} copy-done((bf16[320,384]{1,0:T(8,128)(2,1)S(1)}, bf16[320,384]{1,0:T(8,128)(2,1)}, u32[]{:S(2)}) %copy-start.7) | copy-done | bytes 245784
  32.4 0.9 %copy-done.12 = bf16[128,384]{1,0:T(8,128)(2,1)S(1)} copy-done((bf16[128,384]{1,0:T(8,128)(2,1)S(1)}, bf16[128,384]{1,0:T(8,128)(2,1)}, u32[]{:S(2)}) %copy-start.12) | copy-done | bytes 98328
  33.3 0.9 %copy-done.14 = bf16[128,384]{1,0:T(8,128)(2,1)S(1)} copy-done((bf16[128,384]{1,0:T(8,128)(2,1)S(1)}, bf16[128,384]{1,0:T(8,128)(2,1)}, u32[]{:S(2)}) %copy-start.14) | copy-done | bytes 98328
  34.2 0.9 %copy-done.16 = bf16[128,384]{1,0:T(8,128)(2,1)S(1)} copy-done((bf16[128,384]{1,0:T(8,128)(2,1)S(1)}, bf16[128,384]{1,0:T(8,128)(2,1)}, u32[]{:S(2)}) %copy-start.16) | copy-done | bytes 98328
  35.1 1.1 %backward.1 = (f32[128,384]{1,0:T(8,128)S(1)}, bf16[128,384]{1,0:T(8,128)(2,1)S(1)}, bf16[1280,384]{1,0:T(8,128)(2,1)S(1)}) custom-call(bf16[128,384]{1,0:T(8,128)(2,1)S(1)} %copy-done.12, bf16[128,384]{1,0:T(8,128)(2,1)S(1)} %copy-done.14, bf16[128,384]{1,0:T(8,128)(2,1)S(1)} %dattn.1.d_own_ref, bf16[128,384]{1,0:T(8,128)(2,1)S(1)} %copy-done.16, ...), custom_call_target="tpu_custom_call" | custom-call | flops 377487360 | bytes 5636096 | tf_op jit(solution)/shard_map/backward/pallas_call | solution.py:41
  36.2 0.9 %copy-done.2 = bf16[1280,384]{1,0:T(8,128)(2,1)} copy-done((bf16[1280,384]{1,0:T(8,128)(2,1)}, bf16[1280,384]{1,0:T(8,128)(2,1)S(1)}, u32[]{:S(2)}) %copy-start.2) | copy-done | bytes 983064
  37.2 0.6 copy-done.20
  37.8 5.3 %all-to-all-start = ((bf16[4,320,384]{2,1,0:T(8,128)(2,1)}), bf16[4,320,384]{2,1,0:T(8,128)(2,1)S(1)}, u32[]{:S(2)}, u32[]{:S(2)}) async-start(bf16[4,320,384]{2,1,0:T(8,128)(2,1)} %bitcast.3), calls=%async_computation | async-start | bytes 1966080 | tf_op jit(solution)/shard_map/all_to_all | solution.py:307
  43.1 1.3 %collective-permute-start.10 = (bf16[384,128]{1,0:T(8,128)(2,1)}, bf16[384,128]{1,0:T(8,128)(2,1)S(1)}, u32[]{:S(2)}, u32[]{:S(2)}) collective-permute-start(bf16[384,128]{1,0:T(8,128)(2,1)} %copy-done.22), channel_id=1, source_target_pairs={{0,16},{4,20},{8,24},{12,28},{16,0},{20,4},{24,8},{28,12},{1,17},{... | collective-permute-start | bytes 294920 | tf_op jit(solution)/shard_map/ppermute | solution.py:34
  44.4 12.5 %collective-permute-done.10.pair_ref = bf16[384,128]{1,0:T(8,128)(2,1)S(1)} collective-permute-done((bf16[384,128]{1,0:T(8,128)(2,1)}, bf16[384,128]{1,0:T(8,128)(2,1)S(1)}, u32[]{:S(2)}, u32[]{:S(2)}) %collective-permute-start.10) | collective-permute-done | bytes 98336 | tf_op jit(solution)/shard_map/ppermute | solution.py:34
  57.0 0.9 %copy-done.10 = f32[384,128]{1,0:T(8,128)S(1)} copy-done((f32[384,128]{1,0:T(8,128)S(1)}, f32[384,128]{1,0:T(8,128)}, u32[]{:S(2)}) %copy-start.10) | copy-done | bytes 196632
  57.9 0.7 %copy-done.18 = f32[16,256]{1,0:T(8,128)S(1)} copy-done((f32[16,256]{1,0:T(8,128)S(1)}, f32[16,256]{1,0:T(8,128)}, u32[]{:S(2)}) %copy-start.18) | copy-done | bytes 16408
  58.6 0.7 project.1
  59.3 0.8 %copy-done.4 = f32[128,768]{1,0:T(8,128)} copy-done((f32[128,768]{1,0:T(8,128)}, f32[128,768]{1,0:T(8,128)S(1)}, u32[]{:S(2)}) %copy-start.4) | copy-done | bytes 393240
  60.0 1.7 %collective-permute-done.11.core_ref = bf16[128,1536]{1,0:T(8,128)(2,1)S(1)} collective-permute-done((bf16[128,1536]{1,0:T(8,128)(2,1)S(1)}, bf16[128,1536]{1,0:T(8,128)(2,1)S(1)}, u32[]{:S(2)}, u32[]{:S(2)}) %collective-permute-start.11) | collective-permute-done | bytes 393248 | tf_op jit(solution)/shard_map/ppermute | solution.py:34
  61.8 1.3 %collective-permute-start.12 = (bf16[128,768]{1,0:T(8,128)(2,1)S(1)}, bf16[128,768]{1,0:T(8,128)(2,1)S(1)}, u32[]{:S(2)}, u32[]{:S(2)}) collective-permute-start(bf16[128,768]{1,0:T(8,128)(2,1)S(1)} %add_near.1), channel_id=1, source_target_pairs={{0,2},{1,3},{2,0},{3,1},{4,6},{5,7},{6,4},{7,5},{8,10},{9,11},{10,... | collective-permute-start | bytes 589832 | tf_op jit(solution)/shard_map/ppermute | solution.py:34
  63.1 0.0 collective-permute-start.9
  63.1 5.5 %collective-permute-done.9.dq_pair_ref = bf16[128,384]{1,0:T(8,128)(2,1)S(1)} collective-permute-done((bf16[128,384]{1,0:T(8,128)(2,1)S(1)}, bf16[128,384]{1,0:T(8,128)(2,1)S(1)}, u32[]{:S(2)}, u32[]{:S(2)}) %collective-permute-start.9) | collective-permute-done | bytes 98336 | tf_op jit(solution)/shard_map/ppermute | solution.py:34
  68.6 0.2 collective-permute-done.12.near_ref
  68.8 0.0 all-to-all-done
  68.8 1.0 %copy-done.5 = f32[128,768]{1,0:T(8,128)S(1)} copy-done((f32[128,768]{1,0:T(8,128)S(1)}, f32[128,768]{1,0:T(8,128)}, u32[]{:S(2)}) %copy-start.5) | copy-done | bytes 393240
  69.8 0.9 %finish.1 = (bf16[128,384]{1,0:T(8,128)(2,1)}, bf16[128,384]{1,0:T(8,128)(2,1)}, bf16[128,384]{1,0:T(8,128)(2,1)}, bf16[32,384]{1,0:T(8,128)(2,1)}, bf16[32,384]{1,0:T(8,128)(2,1)}, /*index=5*/bf16[128,768]{1,0:T(8,128)(2,1)}) custom-call(f32[128,384]{1,0:T(8,128)S(1)} %get-tuple-element.34.dq_ref, bf16[128,384]{1,0:T(8,128)(2,1)S(1)} %collective-permute-done.9.dq_pair_ref, ...), custom_call_target="tpu_custom_call" | custom-call | bytes 2801664 | tf_op jit(solution)/shard_map/finish/pallas_call | solution.py:41
  (37 shorter events, 0.1 us)
Async XLA Ops:
  0.6 23.7 %copy-start.11 = (bf16[128,384]{1,0:T(8,128)(2,1)S(1)}, bf16[128,384]{1,0:T(8,128)(2,1)}, u32[]{:S(2)}) copy-start(bf16[128,384]{1,0:T(8,128)(2,1)} %q_own_ref.3) | copy-start | bytes 294916
  0.6 16.4 %copy-start.23 = (s32[8,2]{0,1:T(2,128)S(1)}, s32[8,2]{0,1:T(2,128)}, u32[]{:S(2)}) copy-start(s32[8,2]{0,1:T(2,128)} %param.14) | copy-start | bytes 196
  0.7 16.4 %copy-start.19 = (s32[8]{0:T(128)S(1)}, s32[8]{0:T(128)}, u32[]{:S(2)}) copy-start(s32[8]{0:T(128)} %counts_ref.1) | copy-start | bytes 100
  0.7 8.1 %collective-permute-start.2 = (bf16[128,768]{1,0:T(8,128)(2,1)}, bf16[128,768]{1,0:T(8,128)(2,1)S(1)}, u32[]{:S(2)}, u32[]{:S(2)}) collective-permute-start(bf16[128,768]{1,0:T(8,128)(2,1)} %own_ref.1), channel_id=1, source_target_pairs={{0,2},{1,3},{2,0},{3,1},{4,6},{5,7},{6,4},{7,5},{8,10},{9,11},{10,... | collective-permute-start | bytes 589832 | tf_op jit(solution)/shard_map/ppermute | solution.py:34
  2.2 8.0 %collective-permute-start.1 = (bf16[128,768]{1,0:T(8,128)(2,1)}, bf16[128,768]{1,0:T(8,128)(2,1)S(1)}, u32[]{:S(2)}, u32[]{:S(2)}) collective-permute-start(bf16[128,768]{1,0:T(8,128)(2,1)} %own_ref.1), channel_id=1, source_target_pairs={{0,1},{1,0},{2,3},{3,2},{4,5},{5,4},{6,7},{7,6},{8,9},{9,8},{10,11... | collective-permute-start | bytes 589832 | tf_op jit(solution)/shard_map/ppermute | solution.py:34
  2.2 10.6 %collective-permute-start.3 = (bf16[128,768]{1,0:T(8,128)(2,1)}, bf16[128,768]{1,0:T(8,128)(2,1)S(1)}, u32[]{:S(2)}, u32[]{:S(2)}) collective-permute-start(bf16[128,768]{1,0:T(8,128)(2,1)} %own_ref.1), channel_id=1, source_target_pairs={{0,3},{1,2},{2,1},{3,0},{4,7},{5,6},{6,5},{7,4},{8,11},{9,10},{10,... | collective-permute-start | bytes 589832 | tf_op jit(solution)/shard_map/ppermute | solution.py:34
  4.6 18.6 %collective-permute-start.7 = (bf16[320,384]{1,0:T(8,128)(2,1)}, bf16[320,384]{1,0:T(8,128)(2,1)S(1)}, u32[]{:S(2)}, u32[]{:S(2)}) collective-permute-start(bf16[320,384]{1,0:T(8,128)(2,1)} %load.1.kv0), channel_id=1, source_target_pairs={{0,12},{4,8},{8,4},{12,0},{16,28},{20,24},{24,20},{28,16},{1,13},{... | collective-permute-start | bytes 737288 | tf_op jit(solution)/shard_map/ppermute | solution.py:34
  6.0 17.1 %collective-permute-start.6 = (bf16[320,384]{1,0:T(8,128)(2,1)}, bf16[320,384]{1,0:T(8,128)(2,1)S(1)}, u32[]{:S(2)}, u32[]{:S(2)}) collective-permute-start(bf16[320,384]{1,0:T(8,128)(2,1)} %load.1.kv0), channel_id=1, source_target_pairs={{0,8},{4,12},{8,0},{12,4},{16,24},{20,28},{24,16},{28,20},{1,9},{5... | collective-permute-start | bytes 737288 | tf_op jit(solution)/shard_map/ppermute | solution.py:34
  8.7 14.4 %collective-permute-start.5 = (bf16[320,384]{1,0:T(8,128)(2,1)}, bf16[320,384]{1,0:T(8,128)(2,1)S(1)}, u32[]{:S(2)}, u32[]{:S(2)}) collective-permute-start(bf16[320,384]{1,0:T(8,128)(2,1)} %load.1.kv0), channel_id=1, source_target_pairs={{0,4},{4,0},{8,12},{12,8},{16,20},{20,16},{24,28},{28,24},{1,5},{5... | collective-permute-start | bytes 737288 | tf_op jit(solution)/shard_map/ppermute | solution.py:34
  10.3 12.9 %collective-permute-start = (bf16[128,384]{1,0:T(8,128)(2,1)}, bf16[128,384]{1,0:T(8,128)(2,1)S(1)}, u32[]{:S(2)}, u32[]{:S(2)}) collective-permute-start(bf16[128,384]{1,0:T(8,128)(2,1)} %q_own_ref.3), channel_id=1, source_target_pairs={{0,16},{4,20},{8,24},{12,28},{16,0},{20,4},{24,8},{28,12},{1,17},{... | collective-permute-start | bytes 294920 | tf_op jit(solution)/shard_map/ppermute | solution.py:34
  12.8 1.7 %copy-start = (bf16[384,3072]{1,0:T(8,128)(2,1)S(1)}, bf16[384,3072]{1,0:T(8,128)(2,1)}, u32[]{:S(2)}) copy-start(bf16[384,3072]{1,0:T(8,128)(2,1)} %w_ref.3) | copy-start | bytes 7077892
  14.5 0.9 %copy-start.8 = (bf16[128,768]{1,0:T(8,128)(2,1)S(1)}, bf16[128,768]{1,0:T(8,128)(2,1)}, u32[]{:S(2)}) copy-start(bf16[128,768]{1,0:T(8,128)(2,1)} %own_ref.1) | copy-start | bytes 589828
  15.4 8.8 %copy-start.3 = (bf16[320,384]{1,0:T(8,128)(2,1)S(1)}, bf16[320,384]{1,0:T(8,128)(2,1)}, u32[]{:S(2)}) copy-start(bf16[320,384]{1,0:T(8,128)(2,1)} %load.1.kv0) | copy-start | bytes 737284
  16.3 8.0 %collective-permute-start.4 = (bf16[128,384]{1,0:T(8,128)(2,1)S(1)}, bf16[128,384]{1,0:T(8,128)(2,1)S(1)}, u32[]{:S(2)}, u32[]{:S(2)}) collective-permute-start(bf16[128,384]{1,0:T(8,128)(2,1)S(1)} %dattn.1.d_own_ref), channel_id=1, source_target_pairs={{0,16},{4,20},{8,24},{12,28},{16,0},{20,4},{24,8},{28,12},{1,17},{... | collective-permute-start | bytes 294920 | tf_op jit(solution)/shard_map/ppermute | solution.py:34
  23.1 8.3 %copy-start.13 = (bf16[128,384]{1,0:T(8,128)(2,1)}, bf16[128,384]{1,0:T(8,128)(2,1)S(1)}, u32[]{:S(2)}) copy-start(bf16[128,384]{1,0:T(8,128)(2,1)S(1)} %collective-permute-done.q_pair_ref) | copy-start | bytes 294916
  23.2 8.3 %copy-start.6 = (bf16[320,384]{1,0:T(8,128)(2,1)}, bf16[320,384]{1,0:T(8,128)(2,1)S(1)}, u32[]{:S(2)}) copy-start(bf16[320,384]{1,0:T(8,128)(2,1)S(1)} %collective-permute-done.5.kv1) | copy-start | bytes 737284
  24.3 7.2 %copy-start.15 = (bf16[128,384]{1,0:T(8,128)(2,1)}, bf16[128,384]{1,0:T(8,128)(2,1)S(1)}, u32[]{:S(2)}) copy-start(bf16[128,384]{1,0:T(8,128)(2,1)S(1)} %collective-permute-done.4.d_pair_ref) | copy-start | bytes 294916
  26.1 0.7 copy-start.9
  26.8 4.7 %copy-start.22 = (bf16[384,128]{1,0:T(8,128)(2,1)}, bf16[384,128]{1,0:T(8,128)(2,1)S(1)}, u32[]{:S(2)}) copy-start(bf16[384,128]{1,0:T(8,128)(2,1)S(1)} %get-tuple-element.38) | copy-start | bytes 294916
  26.8 4.6 %collective-permute-start.8 = (f32[16,256]{1,0:T(8,128)S(1)}, f32[16,256]{1,0:T(8,128)S(1)}, u32[]{:S(2)}, u32[]{:S(2)}) collective-permute-start(f32[16,256]{1,0:T(8,128)S(1)} %get-tuple-element.28.stats_ref), channel_id=1, source_target_pairs={{0,16},{4,20},{8,24},{12,28},{16,0},{20,4},{24,8},{28,12},{1,17},{... | collective-permute-start | bytes 49160 | tf_op jit(solution)/shard_map/ppermute | solution.py:34
  31.4 4.8 %copy-start.17 = (f32[16,256]{1,0:T(8,128)}, f32[16,256]{1,0:T(8,128)S(1)}, u32[]{:S(2)}) copy-start(f32[16,256]{1,0:T(8,128)S(1)} %collective-permute-done.8.stats_pair_ref) | copy-start | bytes 49156
  31.5 0.9 %copy-start.7 = (bf16[320,384]{1,0:T(8,128)(2,1)S(1)}, bf16[320,384]{1,0:T(8,128)(2,1)}, u32[]{:S(2)}) copy-start(bf16[320,384]{1,0:T(8,128)(2,1)} %copy-done.6) | copy-start | bytes 737284
  32.4 0.9 %copy-start.12 = (bf16[128,384]{1,0:T(8,128)(2,1)S(1)}, bf16[128,384]{1,0:T(8,128)(2,1)}, u32[]{:S(2)}) copy-start(bf16[128,384]{1,0:T(8,128)(2,1)} %q_own_ref.3) | copy-start | bytes 294916
  33.3 0.9 %copy-start.14 = (bf16[128,384]{1,0:T(8,128)(2,1)S(1)}, bf16[128,384]{1,0:T(8,128)(2,1)}, u32[]{:S(2)}) copy-start(bf16[128,384]{1,0:T(8,128)(2,1)} %copy-done.13) | copy-start | bytes 294916
  34.2 0.9 %copy-start.16 = (bf16[128,384]{1,0:T(8,128)(2,1)S(1)}, bf16[128,384]{1,0:T(8,128)(2,1)}, u32[]{:S(2)}) copy-start(bf16[128,384]{1,0:T(8,128)(2,1)} %copy-done.15) | copy-start | bytes 294916
  35.1 21.9 %copy-start.1 = (bf16[384,3072]{1,0:T(8,128)(2,1)S(1)}, bf16[384,3072]{1,0:T(8,128)(2,1)}, u32[]{:S(2)}) copy-start(bf16[384,3072]{1,0:T(8,128)(2,1)} %w_ref.3) | copy-start | bytes 7077892
  36.2 0.9 %copy-start.2 = (bf16[1280,384]{1,0:T(8,128)(2,1)}, bf16[1280,384]{1,0:T(8,128)(2,1)S(1)}, u32[]{:S(2)}) copy-start(bf16[1280,384]{1,0:T(8,128)(2,1)S(1)} %get-tuple-element.36) | copy-start | bytes 2949124
  37.2 0.6 copy-start.20
  37.8 31.0 %all-to-all-start = ((bf16[4,320,384]{2,1,0:T(8,128)(2,1)}), bf16[4,320,384]{2,1,0:T(8,128)(2,1)S(1)}, u32[]{:S(2)}, u32[]{:S(2)}) async-start(bf16[4,320,384]{2,1,0:T(8,128)(2,1)} %bitcast.3), calls=%async_computation | async-start | bytes 1966080 | tf_op jit(solution)/shard_map/all_to_all | solution.py:307
  43.1 13.8 %collective-permute-start.10 = (bf16[384,128]{1,0:T(8,128)(2,1)}, bf16[384,128]{1,0:T(8,128)(2,1)S(1)}, u32[]{:S(2)}, u32[]{:S(2)}) collective-permute-start(bf16[384,128]{1,0:T(8,128)(2,1)} %copy-done.22), channel_id=1, source_target_pairs={{0,16},{4,20},{8,24},{12,28},{16,0},{20,4},{24,8},{28,12},{1,17},{... | collective-permute-start | bytes 294920 | tf_op jit(solution)/shard_map/ppermute | solution.py:34
  56.9 0.9 %copy-start.10 = (f32[384,128]{1,0:T(8,128)S(1)}, f32[384,128]{1,0:T(8,128)}, u32[]{:S(2)}) copy-start(f32[384,128]{1,0:T(8,128)} %copy-done.9) | copy-start | bytes 589828
  57.9 0.7 %copy-start.18 = (f32[16,256]{1,0:T(8,128)S(1)}, f32[16,256]{1,0:T(8,128)}, u32[]{:S(2)}) copy-start(f32[16,256]{1,0:T(8,128)} %copy-done.17) | copy-start | bytes 49156
  58.6 4.5 %copy-start.21 = (bf16[128,384]{1,0:T(8,128)(2,1)S(1)}, bf16[128,384]{1,0:T(8,128)(2,1)}, u32[]{:S(2)}) copy-start(bf16[128,384]{1,0:T(8,128)(2,1)} %copy-done.20) | copy-start | bytes 294916
  59.3 0.8 %copy-start.4 = (f32[128,768]{1,0:T(8,128)}, f32[128,768]{1,0:T(8,128)S(1)}, u32[]{:S(2)}) copy-start(f32[128,768]{1,0:T(8,128)S(1)} %get-tuple-element.39.keep_ref) | copy-start | bytes 1179652
  60.0 1.7 %collective-permute-start.11 = (bf16[128,1536]{1,0:T(8,128)(2,1)S(1)}, bf16[128,1536]{1,0:T(8,128)(2,1)S(1)}, u32[]{:S(2)}, u32[]{:S(2)}) collective-permute-start(bf16[128,1536]{1,0:T(8,128)(2,1)S(1)} %get-tuple-element.40), channel_id=1, source_target_pairs={{0,1},{1,0},{2,3},{3,2},{4,5},{5,4},{6,7},{7,6},{8,9},{9,8},{10,11... | collective-permute-start | bytes 1179656 | tf_op jit(solution)/shard_map/ppermute | solution.py:34
  61.8 7.0 %collective-permute-start.12 = (bf16[128,768]{1,0:T(8,128)(2,1)S(1)}, bf16[128,768]{1,0:T(8,128)(2,1)S(1)}, u32[]{:S(2)}, u32[]{:S(2)}) collective-permute-start(bf16[128,768]{1,0:T(8,128)(2,1)S(1)} %add_near.1), channel_id=1, source_target_pairs={{0,2},{1,3},{2,0},{3,1},{4,6},{5,7},{6,4},{7,5},{8,10},{9,11},{10,... | collective-permute-start | bytes 589832 | tf_op jit(solution)/shard_map/ppermute | solution.py:34
  63.1 5.5 %collective-permute-start.9 = (bf16[128,384]{1,0:T(8,128)(2,1)S(1)}, bf16[128,384]{1,0:T(8,128)(2,1)S(1)}, u32[]{:S(2)}, u32[]{:S(2)}) collective-permute-start(bf16[128,384]{1,0:T(8,128)(2,1)S(1)} %copy-done.21), channel_id=1, source_target_pairs={{0,16},{4,20},{8,24},{12,28},{16,0},{20,4},{24,8},{28,12},{1,17},{... | collective-permute-start | bytes 294920 | tf_op jit(solution)/shard_map/ppermute | solution.py:34
  68.8 1.0 %copy-start.5 = (f32[128,768]{1,0:T(8,128)S(1)}, f32[128,768]{1,0:T(8,128)}, u32[]{:S(2)}) copy-start(f32[128,768]{1,0:T(8,128)} %copy-done.4) | copy-start | bytes 1179652

commit v5 on v4

--- a/solution.py
+++ b/solution.py
@@ -161,7 +161,7 @@
     return weight * inverse, weight_pair * inverse
 
 
-def project_kernel(own_ref, pair_ref, stats_ref, stats_pair_ref, w_ref, send_ref, next_ref, keep_ref):
+def project_kernel(own_ref, pair_ref, stats_ref, stats_pair_ref, w_ref, keep_ref, *send_refs):
     rows = own_ref.shape[1]
     parts = []
     for head in range(own_ref.shape[0] // HDIM):
@@ -173,30 +173,20 @@
     attn = jnp.concatenate(parts, axis=0).astype(BF16)
     me = lax.axis_index("head")
     size = keep_ref.shape[1]
-
-    def columns_of(step):
+    for step, ref in enumerate((keep_ref, *send_refs)):
         columns = pl.ds(pl.multiple_of((me ^ step) * size, HDIM), size)
-        return contract(attn, w_ref[:, columns], 0, 0)
-
-    send_ref[:, :size] = columns_of(1).astype(BF16)
-    send_ref[:, size:] = columns_of(3).astype(BF16)
-    next_ref[...] = columns_of(2)
-    keep_ref[...] = columns_of(0)
-
-
-def add_near_kernel(next_ref, core_ref, out_ref):
-    size = next_ref.shape[1]
-    out_ref[...] = (next_ref[...] + core_ref[:, size:].astype(F32)).astype(BF16)
+        ref[...] = contract(attn, w_ref[:, columns], 0, 0).astype(ref.dtype)
 
 
 def backward_kernel(
     q_own_ref, q_pair_ref, d_own_ref, d_pair_ref, kv0, kv1, kv2, kv3,
     stats_ref, stats_pair_ref, probs_ref, dprobs_ref,
-    dq_own_ref, dq_pair_ref, dkv_ref,
+    dq_own_ref, dq_pair_ref, dkv_ref, send_k_ref, send_v_ref, near_k_ref, near_v_ref,
 ):
     rows = q_own_ref.shape[0]
     keys = kv0.shape[0] // 2
-    place = lax.rem(lax.axis_index("ctx"), SQUARE)
+    key_parts = (dkv_ref.at[:keys], send_k_ref.at[:keys], near_k_ref, send_k_ref.at[keys:])
+    value_parts = (dkv_ref.at[keys:], near_v_ref, send_v_ref.at[:keys], send_v_ref.at[keys:])
 
     def swapped(row):
         return jnp.concatenate([row[:, rows:], row[:, :rows]], axis=1)
@@ -212,40 +202,45 @@
         features = slice(head * HDIM, (head + 1) * HDIM)
         dquery = None
         for step, ref in enumerate((kv0, kv1, kv2, kv3)):
-            first = pl.multiple_of((place ^ step) * 2 * keys, 2 * keys)
             begin = (head * SQUARE + step) * keys
             probs = (probs_ref[begin : begin + keys].astype(F32) * weight).astype(BF16)
             dprobs = dprobs_ref[begin : begin + keys]
             dscores = (probs.astype(F32) * (dprobs - delta)).astype(BF16)
-            grad_key = (contract(dscores, query, 1, 0) * SCALE).astype(BF16)
-            dkv_ref[pl.ds(first, keys), features] = grad_key
-            grad_value = contract(probs, dattn, 1, 0).astype(BF16)
-            dkv_ref[pl.ds(first + keys, keys), features] = grad_value
+            key_part, value_part = key_parts[step], value_parts[step]
+            grad_key = contract(dscores, query, 1, 0) * SCALE
+            key_part[:, features] = grad_key.astype(key_part.dtype)
+            value_part[:, features] = contract(probs, dattn, 1, 0).astype(value_part.dtype)
             part = contract(dscores, head_slice(ref[:keys], head), 0, 0)
             dquery = part if dquery is None else dquery + part
         dq_own_ref[:, features] = dquery[:rows] * SCALE
         dq_pair_ref[:, features] = (dquery[rows:] * SCALE).astype(BF16)
 
 
+def pass_on_kernel(near_k_ref, near_v_ref, got_k_ref, got_v_ref, k_ref, v_ref):
+    keys = near_k_ref.shape[0]
+    k_ref[...] = (near_k_ref[...] + got_k_ref[keys:].astype(F32)).astype(BF16)
+    v_ref[...] = (near_v_ref[...] + got_v_ref[keys:].astype(F32)).astype(BF16)
+
+
 def finish_kernel(
-    dq_ref, dq_pair_ref, dkv_ref, keep_ref, core_ref, near_ref,
+    dq_ref, dq_pair_ref, dkv_ref, got_k_ref, got_v_ref, rest_k_ref, rest_v_ref,
+    keep_ref, core_ref, near_ref, far_ref,
     q_out, k_out, v_out, hk_out, hv_out, out_ref,
 ):
     rows, capacity = k_out.shape[0], hk_out.shape[0]
     keys = rows + capacity
 
-    def total(begin, size):
-        parts = (dkv_ref[pl.ds(step * 2 * keys + begin, size)] for step in range(SQUARE))
-        return sum(part.astype(F32) for part in parts).astype(BF16)
-
-    q_out[...] = (dq_ref[...] + dq_pair_ref[...].astype(F32)).astype(BF16)
-    k_out[...] = total(0, rows)
-    hk_out[...] = total(rows, capacity)
-    v_out[...] = total(keys, rows)
-    hv_out[...] = total(keys + rows, capacity)
-    size = keep_ref.shape[1]
-    out = keep_ref[...] + core_ref[:, :size].astype(F32) + near_ref[...].astype(F32)
-    out_ref[...] = out.astype(BF16)
+    def total(first, *others):
+        for other in others:
+            first = first + other.astype(F32)
+        return first.astype(BF16)
+
+    q_out[...] = total(dq_ref[...], dq_pair_ref[...])
+    k_out[...] = total(dkv_ref[:rows], got_k_ref[:rows], rest_k_ref[:rows])
+    hk_out[...] = total(dkv_ref[rows:keys], got_k_ref[rows:keys], rest_k_ref[rows:])
+    v_out[...] = total(dkv_ref[keys : keys + rows], got_v_ref[:rows], rest_v_ref[:rows])
+    hv_out[...] = total(dkv_ref[keys + rows :], got_v_ref[rows:keys], rest_v_ref[rows:])
+    out_ref[...] = total(keep_ref[...], core_ref[...], near_ref[...], far_ref[...])
 
 
 def blocked(sec_q, sec_k, sec_v, hist_k, hist_v, frame_levels, frame_counts, w_out, grad_out):
@@ -259,7 +254,9 @@
 
     grad_core, grad_near, grad_far = (swap(grad_out, "head", step) for step in range(1, 4))
     kv0 = load_keys(sec_k, hist_k, sec_v, hist_v)
-    kvs = [kv0] + [swap(kv0, "ctx", step) for step in range(1, SQUARE)]
+    kv2 = swap(kv0, "ctx", 2)
+    kv1 = swap(kv0, "ctx", 1)
+    kvs = [kv0, kv1, kv2, swap(kv2, "ctx", 1)]
     q_pair = swap(sec_q, "ctx", PAIR)
     d_own = local_call(
         dattn_kernel,
@@ -292,41 +289,42 @@
     stats_pair = swap(stats, "ctx", PAIR)
     stats_pair, attn_pair = lax.optimization_barrier((stats_pair, attn_pair))
     attn_got = swap(attn_pair, "ctx", PAIR)
-    dq_own, dq_pair, dkv = local_call(
+    dq_own, dq_pair, dkv_own, send_k, send_v, near_k, near_v = local_call(
         backward_kernel,
         "backward",
-        [
-            shape((rows, width), F32),
-            shape((rows, width), BF16),
-            shape((SQUARE * 2 * keys, width), BF16),
-        ],
+        [shape((rows, width), F32), shape((rows, width), BF16), shape((2 * keys, width), F32)]
+        + [shape((2 * keys, width), BF16)] * 2
+        + [shape((keys, width), F32)] * 2,
         (sec_q, q_pair, d_own, d_pair, *kvs, stats, stats_pair, probs, dprobs),
         flops=3 * work,
     )
-    squares = [list(range(i, i + SQUARE)) for i in range(0, lax.axis_size("ctx"), SQUARE)]
-    dkv_got = lax.all_to_all(dkv, "ctx", 0, 0, axis_index_groups=squares, tiled=True)
+    got_k = swap(send_k, "ctx", 1)
+    got_v = swap(send_v, "ctx", 2)
     dq_got = swap(dq_pair, "ctx", PAIR)
+    rest_k, rest_v = local_call(
+        pass_on_kernel,
+        "pass_on",
+        [shape((keys, width), BF16)] * 2,
+        (near_k, near_v, got_k, got_v),
+    )
+    rest_k = swap(rest_k, "ctx", 2)
+    rest_v = swap(rest_v, "ctx", 1)
     attn_own, dq_own = lax.optimization_barrier((attn_own, dq_own))
-    out_send, out_next, out_keep = local_call(
+    out_keep, *out_send = local_call(
         project_kernel,
         "project",
-        [shape((rows, 2 * share), BF16), shape((rows, share), F32), shape((rows, share), F32)],
+        [shape((rows, share), F32)] + [shape((rows, share), BF16)] * 3,
         (attn_own, attn_got, stats, stats_pair, w_out),
         flops=2 * rows * width * share * 4,
     )
-    out_core = swap(out_send, "head", 1)
-    out_near = swap(
-        local_call(add_near_kernel, "add_near", [shape((rows, share), BF16)], (out_next, out_core))[0],
-        "head",
-        2,
-    )
+    out_got = [swap(out_send[step - 1], "head", step) for step in (1, 2, 3)]
     grad_q, grad_k, grad_v, grad_hk, grad_hv, out = local_call(
         finish_kernel,
         "finish",
         [shape((rows, width), BF16)] * 3
         + [shape((capacity, width), BF16)] * 2
         + [shape((rows, share), BF16)],
-        (dq_own, dq_got, dkv_got, out_keep, out_core, out_near),
+        (dq_own, dq_got, dkv_own, got_k, got_v, rest_k, rest_v, out_keep, *out_got),
     )
     return out, grad_q, grad_k, grad_v, grad_hk, grad_hv
 

time: 71.2 us -> 58.2 us (0.82)
  the two profiles are of different devices: /device:TPU:8 before, /device:TPU:0 now
where the time goes in v5:
time: 58.2 us; the launch traced here: 57.3 us
  starting transfers between devices  24.2 us (42%)
  waiting for transfers between devices  22 us (38%)
  Pallas kernels  7.66 us (13%)
  local copies, waits for them, and re-layouts  2.7 us (5%)
  between operations  0.76 us (1%)
    ppermute x18, starting transfers between devices, swap(): return lax.ppermute(block, axis, [(i, i ^ bit) for i in range(count)])  24.2 us
    ppermute x18, waiting for transfers between devices, swap(): return lax.ppermute(block, axis, [(i, i ^ bit) for i in range(count)])  22 us
    pallas_call x7, Pallas kernels, local_call(): pl.pallas_call(body, name=name, out_shape=out_shapes, in_specs=[pl.BlockS...  5.96 us
    unnamed x15, local copies, waits for them, and re-layouts  2.7 us
    pallas_call x1, Pallas kernels, load_keys(): pl.pallas_call(load_kernel, name='load', out_shape=jax.ShapeDtypeStruct((...  1.7 us
  transfers between devices with their start and end apart: 18, of which 7 were waited for; matrix products, arithmetic and copies ran while one was open for 0% of the time, Pallas kernels for 4%

profile of v5, /device:TPU:0, one launch (start us, length us, event | category | flops | bytes accessed | tf_op | source)
XLA Modules:
  0.0 57.3 jit_solution(12231985666527215375)
XLA Ops:
  0.6 0.0 copy-start.4
  0.7 1.7 %load.1.kv0 = bf16[320,384]{1,0:T(8,128)(2,1)} custom-call(bf16[128,384]{1,0:T(8,128)(2,1)} %k_ref.1, bf16[32,384]{1,0:T(8,128)(2,1)} %hk_ref.1, bf16[128,384]{1,0:T(8,128)(2,1)} %v_ref.1, bf16[32,384]{1,0:T(8,128)(2,1)} %hv_ref.1), custom_call_target="tpu_custom_call" | custom-call | bytes 983040 | tf_op jit(solution)/shard_map/load/pallas_call | solution.py:71
  2.4 3.1 %collective-permute-start.6 = (bf16[320,384]{1,0:T(8,128)(2,1)}, bf16[320,384]{1,0:T(8,128)(2,1)S(1)}, u32[]{:S(2)}, u32[]{:S(2)}) collective-permute-start(bf16[320,384]{1,0:T(8,128)(2,1)} %load.1.kv0), channel_id=1, source_target_pairs={{0,8},{4,12},{8,0},{12,4},{16,24},{20,28},{24,16},{28,20},{1,9},{5... | collective-permute-start | bytes 737288 | tf_op jit(solution)/shard_map/ppermute | solution.py:34
  5.5 1.5 %collective-permute-start.2 = (bf16[128,768]{1,0:T(8,128)(2,1)}, bf16[128,768]{1,0:T(8,128)(2,1)S(1)}, u32[]{:S(2)}, u32[]{:S(2)}) collective-permute-start(bf16[128,768]{1,0:T(8,128)(2,1)} %own_ref.1), channel_id=1, source_target_pairs={{0,2},{1,3},{2,0},{3,1},{4,6},{5,7},{6,4},{7,5},{8,10},{9,11},{10,... | collective-permute-start | bytes 589832 | tf_op jit(solution)/shard_map/ppermute | solution.py:34
  7.0 0.0 collective-permute-start.1
  7.0 0.6 %collective-permute-start.3 = (bf16[128,768]{1,0:T(8,128)(2,1)}, bf16[128,768]{1,0:T(8,128)(2,1)S(1)}, u32[]{:S(2)}, u32[]{:S(2)}) collective-permute-start(bf16[128,768]{1,0:T(8,128)(2,1)} %own_ref.1), channel_id=1, source_target_pairs={{0,3},{1,2},{2,1},{3,0},{4,7},{5,6},{6,5},{7,4},{8,11},{9,10},{10,... | collective-permute-start | bytes 589832 | tf_op jit(solution)/shard_map/ppermute | solution.py:34
  7.6 1.5 %collective-permute-start.5 = (bf16[320,384]{1,0:T(8,128)(2,1)}, bf16[320,384]{1,0:T(8,128)(2,1)S(1)}, u32[]{:S(2)}, u32[]{:S(2)}) collective-permute-start(bf16[320,384]{1,0:T(8,128)(2,1)} %load.1.kv0), channel_id=1, source_target_pairs={{0,4},{4,0},{8,12},{12,8},{16,20},{20,16},{24,28},{28,24},{1,5},{5... | collective-permute-start | bytes 737288 | tf_op jit(solution)/shard_map/ppermute | solution.py:34
  9.1 2.5 %collective-permute-done.6.kv2 = bf16[320,384]{1,0:T(8,128)(2,1)S(1)} collective-permute-done((bf16[320,384]{1,0:T(8,128)(2,1)}, bf16[320,384]{1,0:T(8,128)(2,1)S(1)}, u32[]{:S(2)}, u32[]{:S(2)}) %collective-permute-start.6) | collective-permute-done | bytes 245792 | tf_op jit(solution)/shard_map/ppermute | solution.py:34
  11.6 1.7 %collective-permute-start.7 = (bf16[320,384]{1,0:T(8,128)(2,1)S(1)}, bf16[320,384]{1,0:T(8,128)(2,1)S(1)}, u32[]{:S(2)}, u32[]{:S(2)}) collective-permute-start(bf16[320,384]{1,0:T(8,128)(2,1)S(1)} %collective-permute-done.6.kv2), channel_id=1, source_target_pairs={{0,4},{4,0},{8,12},{12,8},{16,20},{20,16},{24,28},{28,24},{1,5},{5... | collective-permute-start | bytes 737288 | tf_op jit(solution)/shard_map/ppermute | solution.py:34
  13.3 0.2 collective-permute-done.2.near_ref
  13.5 2.6 %collective-permute-start = (bf16[128,384]{1,0:T(8,128)(2,1)}, bf16[128,384]{1,0:T(8,128)(2,1)S(1)}, u32[]{:S(2)}, u32[]{:S(2)}) collective-permute-start(bf16[128,384]{1,0:T(8,128)(2,1)} %q_own_ref.3), channel_id=1, source_target_pairs={{0,16},{4,20},{8,24},{12,28},{16,0},{20,4},{24,8},{28,12},{1,17},{... | collective-permute-start | bytes 294920 | tf_op jit(solution)/shard_map/ppermute | solution.py:34
  16.1 0.0 collective-permute-done.1.core_ref
  16.1 0.0 collective-permute-done.3.far_ref
  16.1 1.7 %copy-done = bf16[384,3072]{1,0:T(8,128)(2,1)S(1)} copy-done((bf16[384,3072]{1,0:T(8,128)(2,1)S(1)}, bf16[384,3072]{1,0:T(8,128)(2,1)}, u32[]{:S(2)}) %copy-start) | copy-done | bytes 2359320
  17.8 0.9 %copy-done.3 = bf16[128,768]{1,0:T(8,128)(2,1)S(1)} copy-done((bf16[128,768]{1,0:T(8,128)(2,1)S(1)}, bf16[128,768]{1,0:T(8,128)(2,1)}, u32[]{:S(2)}) %copy-start.3) | copy-done | bytes 196632
  18.7 0.8 %dattn.1.d_own_ref = bf16[128,384]{1,0:T(8,128)(2,1)S(1)} custom-call(bf16[128,768]{1,0:T(8,128)(2,1)S(1)} %copy-done.3, bf16[128,768]{1,0:T(8,128)(2,1)S(1)} %collective-permute-done.1.core_ref, bf16[128,768]{1,0:T(8,128)(2,1)S(1)} %collective-permute-done.2.near_ref, bf16[128,768]{1,0:T(8,128)(2,1)S(1)} %collective-permute-done.3.far_ref, ...), custom_call_target="tpu_custom_call" | custom-call | flops 301989888 | bytes 3244032 | tf_op jit(solution)/shard_map/dattn/pallas_call | solution.py:41
  19.5 1.9 %collective-permute-start.4 = (bf16[128,384]{1,0:T(8,128)(2,1)S(1)}, bf16[128,384]{1,0:T(8,128)(2,1)S(1)}, u32[]{:S(2)}, u32[]{:S(2)}) collective-permute-start(bf16[128,384]{1,0:T(8,128)(2,1)S(1)} %dattn.1.d_own_ref), channel_id=1, source_target_pairs={{0,16},{4,20},{8,24},{12,28},{16,0},{20,4},{24,8},{28,12},{1,17},{... | collective-permute-start | bytes 294920 | tf_op jit(solution)/shard_map/ppermute | solution.py:34
  21.5 0.1 copy.15.levels_ref
  21.5 0.6 %limits.1.limits_ref = s32[8,256]{1,0:T(8,128)S(1)} custom-call(s32[8,2]{1,0:T(8,128)S(1)} %copy.15.levels_ref, s32[8]{0:T(128)S(1)} %copy-done.5), custom_call_target="tpu_custom_call" | custom-call | bytes 8288 | tf_op jit(solution)/shard_map/limits/pallas_call | solution.py:41
  22.2 0.0 collective-permute-done.q_pair_ref
  22.2 0.0 collective-permute-done.5.kv1
  22.2 5.2 %collective-permute-done.4.d_pair_ref = bf16[128,384]{1,0:T(8,128)(2,1)S(1)} collective-permute-done((bf16[128,384]{1,0:T(8,128)(2,1)S(1)}, bf16[128,384]{1,0:T(8,128)(2,1)S(1)}, u32[]{:S(2)}, u32[]{:S(2)}) %collective-permute-start.4) | collective-permute-done | bytes 98336 | tf_op jit(solution)/shard_map/ppermute | solution.py:34
  27.4 0.0 collective-permute-done.7.kv3
  27.4 1.8 %forward.1 = (f32[16,256]{1,0:T(8,128)S(1)}, f32[384,128]{1,0:T(8,128)S(1)}, bf16[384,128]{1,0:T(8,128)(2,1)S(1)}, bf16[1920,256]{1,0:T(8,128)(2,1)S(1)}, f32[1920,256]{1,0:T(8,128)S(1)}) custom-call(s32[8,256]{1,0:T(8,128)S(1)} %limits.1.limits_ref, bf16[128,384]{1,0:T(8,128)(2,1)S(1)} %copy-done.4, bf16[128,384]{1,0:T(8,128)(2,1)S(1)} %collective-permute-done.q_pair_ref, ...), custom_call_target="tpu_custom_call" | custom-call | flops 377487360 | bytes 4644864 | tf_op jit(solution)/shard_map/forward/pallas_call | solution.py:41
  29.2 0.0 copy-start.1
  29.3 0.7 %collective-permute-start.8 = (f32[16,256]{1,0:T(8,128)S(1)}, f32[16,256]{1,0:T(8,128)S(1)}, u32[]{:S(2)}, u32[]{:S(2)}) collective-permute-start(f32[16,256]{1,0:T(8,128)S(1)} %get-tuple-element.35.stats_ref), channel_id=1, source_target_pairs={{0,16},{4,20},{8,24},{12,28},{16,0},{20,4},{24,8},{28,12},{1,17},{... | collective-permute-start | bytes 49160 | tf_op jit(solution)/shard_map/ppermute | solution.py:34
  30.0 4.0 %collective-permute-done.8.stats_pair_ref = f32[16,256]{1,0:T(8,128)S(1)} collective-permute-done((f32[16,256]{1,0:T(8,128)S(1)}, f32[16,256]{1,0:T(8,128)S(1)}, u32[]{:S(2)}, u32[]{:S(2)}) %collective-permute-start.8) | collective-permute-done | bytes 16416 | tf_op jit(solution)/shard_map/ppermute | solution.py:34
  34.0 1.1 %backward.1 = (f32[128,384]{1,0:T(8,128)S(1)}, bf16[128,384]{1,0:T(8,128)(2,1)S(1)}, f32[320,384]{1,0:T(8,128)S(1)}, bf16[320,384]{1,0:T(8,128)(2,1)S(1)}, bf16[...) custom-call(bf16[128,384]{1,0:T(8,128)(2,1)S(1)} %copy-done.4, ...), custom_call_target="tpu_custom_call" | custom-call | flops 377487360 | bytes 6127616 | tf_op jit(solution)/shard_map/backward/pallas_call | solution.py:41
  35.1 1.6 %collective-permute-start.10 = (bf16[320,384]{1,0:T(8,128)(2,1)S(1)}, bf16[320,384]{1,0:T(8,128)(2,1)S(1)}, u32[]{:S(2)}, u32[]{:S(2)}) collective-permute-start(bf16[320,384]{1,0:T(8,128)(2,1)S(1)} %get-tuple-element.44), channel_id=1, source_target_pairs={{0,4},{4,0},{8,12},{12,8},{16,20},{20,16},{24,28},{28,24},{1,5},{5... | collective-permute-start | bytes 737288 | tf_op jit(solution)/shard_map/ppermute | solution.py:34
  36.7 0.1 collective-permute-start.11
  36.9 2.9 %collective-permute-start.14 = (bf16[384,128]{1,0:T(8,128)(2,1)S(1)}, bf16[384,128]{1,0:T(8,128)(2,1)S(1)}, u32[]{:S(2)}, u32[]{:S(2)}) collective-permute-start(bf16[384,128]{1,0:T(8,128)(2,1)S(1)} %get-tuple-element.51), channel_id=1, source_target_pairs={{0,16},{4,20},{8,24},{12,28},{16,0},{20,4},{24,8},{28,12},{1,17},{... | collective-permute-start | bytes 294920 | tf_op jit(solution)/shard_map/ppermute | solution.py:34
  39.8 0.0 collective-permute-start.9
  39.8 4.8 %collective-permute-done.14.pair_ref = bf16[384,128]{1,0:T(8,128)(2,1)S(1)} collective-permute-done((bf16[384,128]{1,0:T(8,128)(2,1)S(1)}, bf16[384,128]{1,0:T(8,128)(2,1)S(1)}, u32[]{:S(2)}, u32[]{:S(2)}) %collective-permute-start.14) | collective-permute-done | bytes 98336 | tf_op jit(solution)/shard_map/ppermute | solution.py:34
  44.6 0.6 %project.1 = (f32[128,768]{1,0:T(8,128)S(1)}, bf16[128,768]{1,0:T(8,128)(2,1)S(1)}, bf16[128,768]{1,0:T(8,128)(2,1)S(1)}, bf16[128,768]{1,0:T(8,128)(2,1)S(1)}) custom-call(f32[384,128]{1,0:T(8,128)S(1)} %get-tuple-element.50.own_ref, bf16[384,128]{1,0:T(8,128)(2,1)S(1)} %collective-permute-done.14.pair_ref, f32[16,256]{1,0:T(8,128)S(1)} %get-tuple-element.35.stats_ref, ...), custom_call_target="tpu_custom_call" | custom-call | flops 301989888 | bytes 3670016 | tf_op jit(solution)/shard_map/project/pallas_call | solution.py:41
  45.3 0.1 collective-permute-start.15
  45.3 1.1 %collective-permute-start.16 = (bf16[128,768]{1,0:T(8,128)(2,1)S(1)}, bf16[128,768]{1,0:T(8,128)(2,1)S(1)}, u32[]{:S(2)}, u32[]{:S(2)}) collective-permute-start(bf16[128,768]{1,0:T(8,128)(2,1)S(1)} %get-tuple-element.54), channel_id=1, source_target_pairs={{0,2},{1,3},{2,0},{3,1},{4,6},{5,7},{6,4},{7,5},{8,10},{9,11},{10,... | collective-permute-start | bytes 589832 | tf_op jit(solution)/shard_map/ppermute | solution.py:34
  46.5 0.0 collective-permute-done.10.got_k_ref
  46.5 0.7 %collective-permute-start.17 = (bf16[128,768]{1,0:T(8,128)(2,1)S(1)}, bf16[128,768]{1,0:T(8,128)(2,1)S(1)}, u32[]{:S(2)}, u32[]{:S(2)}) collective-permute-start(bf16[128,768]{1,0:T(8,128)(2,1)S(1)} %get-tuple-element.55), channel_id=1, source_target_pairs={{0,3},{1,2},{2,1},{3,0},{4,7},{5,6},{6,5},{7,4},{8,11},{9,10},{10,... | collective-permute-start | bytes 589832 | tf_op jit(solution)/shard_map/ppermute | solution.py:34
  47.2 0.0 collective-permute-done.11.got_v_ref
  47.3 3.3 %collective-permute-start.12 = (bf16[160,384]{1,0:T(8,128)(2,1)S(1)}, bf16[160,384]{1,0:T(8,128)(2,1)S(1)}, u32[]{:S(2)}, u32[]{:S(2)}) collective-permute-start(bf16[160,384]{1,0:T(8,128)(2,1)S(1)} %get-tuple-element.48), channel_id=1, source_target_pairs={{0,8},{4,12},{8,0},{12,4},{16,24},{20,28},{24,16},{28,20},{1,9},{5... | collective-permute-start | bytes 368648 | tf_op jit(solution)/shard_map/ppermute | solution.py:34
  50.6 0.0 collective-permute-done.9.dq_pair_ref
  50.6 0.5 collective-permute-start.13
  51.1 0.0 collective-permute-done.15.core_ref
  51.1 2.0 %collective-permute-done.16.near_ref = bf16[128,768]{1,0:T(8,128)(2,1)S(1)} collective-permute-done((bf16[128,768]{1,0:T(8,128)(2,1)S(1)}, bf16[128,768]{1,0:T(8,128)(2,1)S(1)}, u32[]{:S(2)}, u32[]{:S(2)}) %collective-permute-start.16) | collective-permute-done | bytes 196640 | tf_op jit(solution)/shard_map/ppermute | solution.py:34
  53.1 3.3 %collective-permute-done.17.far_ref = bf16[128,768]{1,0:T(8,128)(2,1)S(1)} collective-permute-done((bf16[128,768]{1,0:T(8,128)(2,1)S(1)}, bf16[128,768]{1,0:T(8,128)(2,1)S(1)}, u32[]{:S(2)}, u32[]{:S(2)}) %collective-permute-start.17) | collective-permute-done | bytes 196640 | tf_op jit(solution)/shard_map/ppermute | solution.py:34
  56.4 0.0 collective-permute-done.12.rest_k_ref
  56.4 0.0 collective-permute-done.13.rest_v_ref
  56.4 0.9 %finish.1 = (bf16[128,384]{1,0:T(8,128)(2,1)}, bf16[128,384]{1,0:T(8,128)(2,1)}, bf16[128,384]{1,0:T(8,128)(2,1)}, bf16[32,384]{1,0:T(8,128)(2,1)}, bf16[32,384]{1,0:T(8,128)(2,1)}, /*index=5*/bf16[128,768]{1,0:T(8,128)(2,1)}) custom-call(f32[128,384]{1,0:T(8,128)S(1)} %get-tuple-element.41.dq_ref, bf16[128,384]{1,0:T(8,128)(2,1)S(1)} %collective-permute-done.9.dq_pair_ref, ...), custom_call_target="tpu_custom_call" | custom-call | bytes 3047424 | tf_op jit(solution)/shard_map/finish/pallas_call | solution.py:41
  (11 shorter events, 0.1 us)
Async XLA Ops:
  0.6 26.8 %copy-start.4 = (bf16[128,384]{1,0:T(8,128)(2,1)S(1)}, bf16[128,384]{1,0:T(8,128)(2,1)}, u32[]{:S(2)}) copy-start(bf16[128,384]{1,0:T(8,128)(2,1)} %q_own_ref.3) | copy-start | bytes 294916
  0.6 20.8 %copy-start.6 = (s32[8,2]{0,1:T(2,128)S(1)}, s32[8,2]{0,1:T(2,128)}, u32[]{:S(2)}) copy-start(s32[8,2]{0,1:T(2,128)} %param.14) | copy-start | bytes 196
  0.7 20.9 %copy-start.5 = (s32[8]{0:T(128)S(1)}, s32[8]{0:T(128)}, u32[]{:S(2)}) copy-start(s32[8]{0:T(128)} %counts_ref.1) | copy-start | bytes 100
  2.4 9.3 %collective-permute-start.6 = (bf16[320,384]{1,0:T(8,128)(2,1)}, bf16[320,384]{1,0:T(8,128)(2,1)S(1)}, u32[]{:S(2)}, u32[]{:S(2)}) collective-permute-start(bf16[320,384]{1,0:T(8,128)(2,1)} %load.1.kv0), channel_id=1, source_target_pairs={{0,8},{4,12},{8,0},{12,4},{16,24},{20,28},{24,16},{28,20},{1,9},{5... | collective-permute-start | bytes 737288 | tf_op jit(solution)/shard_map/ppermute | solution.py:34
  5.5 8.0 %collective-permute-start.2 = (bf16[128,768]{1,0:T(8,128)(2,1)}, bf16[128,768]{1,0:T(8,128)(2,1)S(1)}, u32[]{:S(2)}, u32[]{:S(2)}) collective-permute-start(bf16[128,768]{1,0:T(8,128)(2,1)} %own_ref.1), channel_id=1, source_target_pairs={{0,2},{1,3},{2,0},{3,1},{4,6},{5,7},{6,4},{7,5},{8,10},{9,11},{10,... | collective-permute-start | bytes 589832 | tf_op jit(solution)/shard_map/ppermute | solution.py:34
  7.0 9.1 %collective-permute-start.1 = (bf16[128,768]{1,0:T(8,128)(2,1)}, bf16[128,768]{1,0:T(8,128)(2,1)S(1)}, u32[]{:S(2)}, u32[]{:S(2)}) collective-permute-start(bf16[128,768]{1,0:T(8,128)(2,1)} %own_ref.1), channel_id=1, source_target_pairs={{0,1},{1,0},{2,3},{3,2},{4,5},{5,4},{6,7},{7,6},{8,9},{9,8},{10,11... | collective-permute-start | bytes 589832 | tf_op jit(solution)/shard_map/ppermute | solution.py:34
  7.0 9.1 %collective-permute-start.3 = (bf16[128,768]{1,0:T(8,128)(2,1)}, bf16[128,768]{1,0:T(8,128)(2,1)S(1)}, u32[]{:S(2)}, u32[]{:S(2)}) collective-permute-start(bf16[128,768]{1,0:T(8,128)(2,1)} %own_ref.1), channel_id=1, source_target_pairs={{0,3},{1,2},{2,1},{3,0},{4,7},{5,6},{6,5},{7,4},{8,11},{9,10},{10,... | collective-permute-start | bytes 589832 | tf_op jit(solution)/shard_map/ppermute | solution.py:34
  7.6 14.6 %collective-permute-start.5 = (bf16[320,384]{1,0:T(8,128)(2,1)}, bf16[320,384]{1,0:T(8,128)(2,1)S(1)}, u32[]{:S(2)}, u32[]{:S(2)}) collective-permute-start(bf16[320,384]{1,0:T(8,128)(2,1)} %load.1.kv0), channel_id=1, source_target_pairs={{0,4},{4,0},{8,12},{12,8},{16,20},{20,16},{24,28},{28,24},{1,5},{5... | collective-permute-start | bytes 737288 | tf_op jit(solution)/shard_map/ppermute | solution.py:34
  11.6 15.8 %collective-permute-start.7 = (bf16[320,384]{1,0:T(8,128)(2,1)S(1)}, bf16[320,384]{1,0:T(8,128)(2,1)S(1)}, u32[]{:S(2)}, u32[]{:S(2)}) collective-permute-start(bf16[320,384]{1,0:T(8,128)(2,1)S(1)} %collective-permute-done.6.kv2), channel_id=1, source_target_pairs={{0,4},{4,0},{8,12},{12,8},{16,20},{20,16},{24,28},{28,24},{1,5},{5... | collective-permute-start | bytes 737288 | tf_op jit(solution)/shard_map/ppermute | solution.py:34
  13.5 8.7 %collective-permute-start = (bf16[128,384]{1,0:T(8,128)(2,1)}, bf16[128,384]{1,0:T(8,128)(2,1)S(1)}, u32[]{:S(2)}, u32[]{:S(2)}) collective-permute-start(bf16[128,384]{1,0:T(8,128)(2,1)} %q_own_ref.3), channel_id=1, source_target_pairs={{0,16},{4,20},{8,24},{12,28},{16,0},{20,4},{24,8},{28,12},{1,17},{... | collective-permute-start | bytes 294920 | tf_op jit(solution)/shard_map/ppermute | solution.py:34
  16.1 1.7 %copy-start = (bf16[384,3072]{1,0:T(8,128)(2,1)S(1)}, bf16[384,3072]{1,0:T(8,128)(2,1)}, u32[]{:S(2)}) copy-start(bf16[384,3072]{1,0:T(8,128)(2,1)} %w_ref.3) | copy-start | bytes 7077892
  17.8 0.9 %copy-start.3 = (bf16[128,768]{1,0:T(8,128)(2,1)S(1)}, bf16[128,768]{1,0:T(8,128)(2,1)}, u32[]{:S(2)}) copy-start(bf16[128,768]{1,0:T(8,128)(2,1)} %own_ref.1) | copy-start | bytes 589828
  18.7 8.7 %copy-start.2 = (bf16[320,384]{1,0:T(8,128)(2,1)S(1)}, bf16[320,384]{1,0:T(8,128)(2,1)}, u32[]{:S(2)}) copy-start(bf16[320,384]{1,0:T(8,128)(2,1)} %load.1.kv0) | copy-start | bytes 737284
  19.5 7.9 %collective-permute-start.4 = (bf16[128,384]{1,0:T(8,128)(2,1)S(1)}, bf16[128,384]{1,0:T(8,128)(2,1)S(1)}, u32[]{:S(2)}, u32[]{:S(2)}) collective-permute-start(bf16[128,384]{1,0:T(8,128)(2,1)S(1)} %dattn.1.d_own_ref), channel_id=1, source_target_pairs={{0,16},{4,20},{8,24},{12,28},{16,0},{20,4},{24,8},{28,12},{1,17},{... | collective-permute-start | bytes 294920 | tf_op jit(solution)/shard_map/ppermute | solution.py:34
  29.2 15.4 %copy-start.1 = (bf16[384,3072]{1,0:T(8,128)(2,1)S(1)}, bf16[384,3072]{1,0:T(8,128)(2,1)}, u32[]{:S(2)}) copy-start(bf16[384,3072]{1,0:T(8,128)(2,1)} %w_ref.3) | copy-start | bytes 7077892
  29.3 4.7 %collective-permute-start.8 = (f32[16,256]{1,0:T(8,128)S(1)}, f32[16,256]{1,0:T(8,128)S(1)}, u32[]{:S(2)}, u32[]{:S(2)}) collective-permute-start(f32[16,256]{1,0:T(8,128)S(1)} %get-tuple-element.35.stats_ref), channel_id=1, source_target_pairs={{0,16},{4,20},{8,24},{12,28},{16,0},{20,4},{24,8},{28,12},{1,17},{... | collective-permute-start | bytes 49160 | tf_op jit(solution)/shard_map/ppermute | solution.py:34
  35.1 11.4 %collective-permute-start.10 = (bf16[320,384]{1,0:T(8,128)(2,1)S(1)}, bf16[320,384]{1,0:T(8,128)(2,1)S(1)}, u32[]{:S(2)}, u32[]{:S(2)}) collective-permute-start(bf16[320,384]{1,0:T(8,128)(2,1)S(1)} %get-tuple-element.44), channel_id=1, source_target_pairs={{0,4},{4,0},{8,12},{12,8},{16,20},{20,16},{24,28},{28,24},{1,5},{5... | collective-permute-start | bytes 737288 | tf_op jit(solution)/shard_map/ppermute | solution.py:34
  36.7 10.5 %collective-permute-start.11 = (bf16[320,384]{1,0:T(8,128)(2,1)S(1)}, bf16[320,384]{1,0:T(8,128)(2,1)S(1)}, u32[]{:S(2)}, u32[]{:S(2)}) collective-permute-start(bf16[320,384]{1,0:T(8,128)(2,1)S(1)} %get-tuple-element.45), channel_id=1, source_target_pairs={{0,8},{4,12},{8,0},{12,4},{16,24},{20,28},{24,16},{28,20},{1,9},{5... | collective-permute-start | bytes 737288 | tf_op jit(solution)/shard_map/ppermute | solution.py:34
  36.9 7.8 %collective-permute-start.14 = (bf16[384,128]{1,0:T(8,128)(2,1)S(1)}, bf16[384,128]{1,0:T(8,128)(2,1)S(1)}, u32[]{:S(2)}, u32[]{:S(2)}) collective-permute-start(bf16[384,128]{1,0:T(8,128)(2,1)S(1)} %get-tuple-element.51), channel_id=1, source_target_pairs={{0,16},{4,20},{8,24},{12,28},{16,0},{20,4},{24,8},{28,12},{1,17},{... | collective-permute-start | bytes 294920 | tf_op jit(solution)/shard_map/ppermute | solution.py:34
  39.8 10.8 %collective-permute-start.9 = (bf16[128,384]{1,0:T(8,128)(2,1)S(1)}, bf16[128,384]{1,0:T(8,128)(2,1)S(1)}, u32[]{:S(2)}, u32[]{:S(2)}) collective-permute-start(bf16[128,384]{1,0:T(8,128)(2,1)S(1)} %get-tuple-element.42), channel_id=1, source_target_pairs={{0,16},{4,20},{8,24},{12,28},{16,0},{20,4},{24,8},{28,12},{1,17},{... | collective-permute-start | bytes 294920 | tf_op jit(solution)/shard_map/ppermute | solution.py:34
  45.3 5.8 %collective-permute-start.15 = (bf16[128,768]{1,0:T(8,128)(2,1)S(1)}, bf16[128,768]{1,0:T(8,128)(2,1)S(1)}, u32[]{:S(2)}, u32[]{:S(2)}) collective-permute-start(bf16[128,768]{1,0:T(8,128)(2,1)S(1)} %get-tuple-element.53), channel_id=1, source_target_pairs={{0,1},{1,0},{2,3},{3,2},{4,5},{5,4},{6,7},{7,6},{8,9},{9,8},{10,11... | collective-permute-start | bytes 589832 | tf_op jit(solution)/shard_map/ppermute | solution.py:34
  45.3 7.8 %collective-permute-start.16 = (bf16[128,768]{1,0:T(8,128)(2,1)S(1)}, bf16[128,768]{1,0:T(8,128)(2,1)S(1)}, u32[]{:S(2)}, u32[]{:S(2)}) collective-permute-start(bf16[128,768]{1,0:T(8,128)(2,1)S(1)} %get-tuple-element.54), channel_id=1, source_target_pairs={{0,2},{1,3},{2,0},{3,1},{4,6},{5,7},{6,4},{7,5},{8,10},{9,11},{10,... | collective-permute-start | bytes 589832 | tf_op jit(solution)/shard_map/ppermute | solution.py:34
  46.5 10.0 %collective-permute-start.17 = (bf16[128,768]{1,0:T(8,128)(2,1)S(1)}, bf16[128,768]{1,0:T(8,128)(2,1)S(1)}, u32[]{:S(2)}, u32[]{:S(2)}) collective-permute-start(bf16[128,768]{1,0:T(8,128)(2,1)S(1)} %get-tuple-element.55), channel_id=1, source_target_pairs={{0,3},{1,2},{2,1},{3,0},{4,7},{5,6},{6,5},{7,4},{8,11},{9,10},{10,... | collective-permute-start | bytes 589832 | tf_op jit(solution)/shard_map/ppermute | solution.py:34
  47.3 9.2 %collective-permute-start.12 = (bf16[160,384]{1,0:T(8,128)(2,1)S(1)}, bf16[160,384]{1,0:T(8,128)(2,1)S(1)}, u32[]{:S(2)}, u32[]{:S(2)}) collective-permute-start(bf16[160,384]{1,0:T(8,128)(2,1)S(1)} %get-tuple-element.48), channel_id=1, source_target_pairs={{0,8},{4,12},{8,0},{12,4},{16,24},{20,28},{24,16},{28,20},{1,9},{5... | collective-permute-start | bytes 368648 | tf_op jit(solution)/shard_map/ppermute | solution.py:34
  50.6 5.9 %collective-permute-start.13 = (bf16[160,384]{1,0:T(8,128)(2,1)S(1)}, bf16[160,384]{1,0:T(8,128)(2,1)S(1)}, u32[]{:S(2)}, u32[]{:S(2)}) collective-permute-start(bf16[160,384]{1,0:T(8,128)(2,1)S(1)} %get-tuple-element.49), channel_id=1, source_target_pairs={{0,4},{4,0},{8,12},{12,8},{16,20},{20,16},{24,28},{28,24},{1,5},{5... | collective-permute-start | bytes 368648 | tf_op jit(solution)/shard_map/ppermute | solution.py:34

commit v6 on v5

--- a/solution.py
+++ b/solution.py
@@ -16,6 +16,7 @@
 F32 = jnp.float32
 BF16 = jnp.bfloat16
 SQUARE = 4
+HBM_BYTES = 3.69e6
 PAIR = 4
 
 
@@ -34,10 +35,12 @@
     return lax.ppermute(block, axis, [(i, i ^ bit) for i in range(count)])
 
 
-def local_call(body, name, out_shapes, args, tables=0, flops=0):
+def cost_of(micros):
+    return pl.CostEstimate(flops=0, bytes_accessed=int(micros * HBM_BYTES), transcendentals=0)
+
+
+def local_call(body, name, micros, out_shapes, args, tables=0):
     spaces = [pltpu.SMEM] * tables + [pltpu.VMEM] * (len(args) - tables)
-    moved = sum(a.size * a.dtype.itemsize for a in args)
-    moved += sum(math.prod(o.shape) * o.dtype.itemsize for o in out_shapes)
     return pl.pallas_call(
         body,
         name=name,
@@ -45,7 +48,7 @@
         in_specs=[pl.BlockSpec(memory_space=space) for space in spaces],
         out_specs=[pl.BlockSpec(memory_space=pltpu.VMEM)] * len(out_shapes),
         compiler_params=pltpu.CompilerParams(vmem_limit_bytes=40 * 2**20),
-        cost_estimate=pl.CostEstimate(flops=flops, bytes_accessed=moved, transcendentals=0),
+        cost_estimate=cost_of(micros),
     )(*args)
 
 
@@ -76,9 +79,7 @@
         out_specs=pl.BlockSpec(memory_space=pl.ANY),
         scratch_shapes=[pltpu.VMEM((rows, width), BF16), pltpu.SemaphoreType.DMA((2, len(arrays)))],
         compiler_params=pltpu.CompilerParams(vmem_limit_bytes=60 * 2**20),
-        cost_estimate=pl.CostEstimate(
-            flops=0, bytes_accessed=4 * rows * width * 2, transcendentals=0
-        ),
+        cost_estimate=cost_of(1.6),
     )(*arrays)
 
 
@@ -95,15 +96,42 @@
     limits_ref[...] = limits
 
 
-def dattn_kernel(own_ref, core_ref, near_ref, far_ref, w_ref, out_ref):
+def dattn_kernel(own_hbm, w_hbm, core_ref, near_ref, far_ref, out_ref, own_ref, w_ref, sems):
     me = lax.axis_index("head")
-    size = own_ref.shape[1]
+    size = core_ref.shape[1]
+    copies = [pltpu.make_async_copy(own_hbm, own_ref, sems.at[4])]
+    for step in range(4):
+        columns = pl.ds(pl.multiple_of((me ^ step) * size, HDIM), size)
+        copies.append(pltpu.make_async_copy(w_hbm.at[:, columns], w_ref.at[step], sems.at[step]))
+    for copy in copies:
+        copy.start()
+    copies[0].wait()
     total = None
     for step, ref in enumerate((own_ref, core_ref, near_ref, far_ref)):
-        columns = pl.ds(pl.multiple_of((me ^ step) * size, HDIM), size)
-        part = contract(ref[...], w_ref[:, columns], 1, 1)
+        copies[1 + step].wait()
+        part = contract(ref[...], w_ref[step], 1, 1)
         total = part if total is None else total + part
     out_ref[...] = total.astype(BF16)
+
+
+def dattn_call(grad_own, w_out, *blocks):
+    rows, share = grad_own.shape
+    width = w_out.shape[0]
+    anywhere, inside = pl.BlockSpec(memory_space=pl.ANY), pl.BlockSpec(memory_space=pltpu.VMEM)
+    return pl.pallas_call(
+        dattn_kernel,
+        name="dattn",
+        out_shape=jax.ShapeDtypeStruct((rows, width), BF16),
+        in_specs=[anywhere, anywhere, inside, inside, inside],
+        out_specs=inside,
+        scratch_shapes=[
+            pltpu.VMEM((rows, share), BF16),
+            pltpu.VMEM((4, width, share), BF16),
+            pltpu.SemaphoreType.DMA((5,)),
+        ],
+        compiler_params=pltpu.CompilerParams(vmem_limit_bytes=52 * 2**20),
+        cost_estimate=cost_of(1.5),
+    )(grad_own, w_out, *blocks)
 
 
 def both_rows(own_ref, pair_ref, head):
@@ -114,7 +142,7 @@
 
 def forward_kernel(
     limits_ref, q_own_ref, q_pair_ref, d_own_ref, d_pair_ref, kv0, kv1, kv2, kv3,
-    stats_ref, own_ref, pair_ref, probs_ref, dprobs_ref,
+    stats_ref, probs_ref, dprobs_ref,
 ):
     rows = q_own_ref.shape[0]
     keys = kv0.shape[0] // 2
@@ -135,23 +163,31 @@
         weights = [jnp.exp(block - top) for block in scores]
         total = sum(jnp.sum(block, axis=0, keepdims=True) for block in weights)
         inverse = 1.0 / total
-        attn, delta = None, None
+        delta = None
         for step, ref in enumerate(blocks):
-            value = head_slice(ref[keys:], head)
             probs = weights[step] * inverse
-            dprobs = contract(value, dattn, 1, 1)
-            part = contract(value, probs.astype(BF16), 0, 0)
-            delta_part = jnp.sum(probs * dprobs, axis=0, keepdims=True)
+            dprobs = contract(head_slice(ref[keys:], head), dattn, 1, 1)
+            part = jnp.sum(probs * dprobs, axis=0, keepdims=True)
+            delta = part if delta is None else delta + part
+            begin = (head * SQUARE + step) * keys
+            probs_ref[begin : begin + keys] = probs.astype(BF16)
+            dprobs_ref[begin : begin + keys] = dprobs
+        stats_ref[head : head + 1] = top + jnp.log(total)
+        stats_ref[8 + head : 9 + head] = delta
+
+
+def attn_kernel(kv0, kv1, kv2, kv3, probs_ref, own_ref, pair_ref):
+    rows = own_ref.shape[1]
+    keys = kv0.shape[0] // 2
+    for head in range(own_ref.shape[0] // HDIM):
+        attn = None
+        for step, ref in enumerate((kv0, kv1, kv2, kv3)):
+            begin = (head * SQUARE + step) * keys
+            part = contract(head_slice(ref[keys:], head), probs_ref[begin : begin + keys], 0, 0)
             attn = part if attn is None else attn + part
-            delta = delta_part if delta is None else delta + delta_part
-            begin = (head * SQUARE + step) * keys
-            probs_ref[begin : begin + keys] = probs.astype(probs_ref.dtype)
-            dprobs_ref[begin : begin + keys] = dprobs
         features = slice(head * HDIM, (head + 1) * HDIM)
         own_ref[features] = attn[:, :rows]
         pair_ref[features] = attn[:, rows:].astype(BF16)
-        stats_ref[head : head + 1] = top + jnp.log(total)
-        stats_ref[8 + head : 9 + head] = delta
 
 
 def merge_parts(mine, theirs):
@@ -250,77 +286,81 @@
     capacity = hist_k.shape[0]
     keys = rows + capacity
     share = grad_out.shape[1]
-    work = 2 * SQUARE * keys * 2 * rows * width
-
-    grad_core, grad_near, grad_far = (swap(grad_out, "head", step) for step in range(1, 4))
+
+    q_pair = swap(sec_q, "ctx", PAIR)
+    grad_near = swap(grad_out, "head", 2)
+    grad_near, q_pair = lax.optimization_barrier((grad_near, q_pair))
+    grad_core = swap(grad_out, "head", 1)
+    grad_far = swap(grad_near, "head", 1)
     kv0 = load_keys(sec_k, hist_k, sec_v, hist_v)
     kv2 = swap(kv0, "ctx", 2)
     kv1 = swap(kv0, "ctx", 1)
     kvs = [kv0, kv1, kv2, swap(kv2, "ctx", 1)]
-    q_pair = swap(sec_q, "ctx", PAIR)
-    d_own = local_call(
-        dattn_kernel,
-        "dattn",
-        [shape((rows, width), BF16)],
-        (grad_out, grad_core, grad_near, grad_far, w_out),
-        flops=2 * rows * width * share * 4,
-    )[0]
+    d_own = dattn_call(grad_out, w_out, grad_core, grad_near, grad_far)
     d_pair = swap(d_own, "ctx", PAIR)
     limits = local_call(
         limits_kernel,
         "limits",
+        0.6,
         [shape((8, 2 * rows), jnp.int32)],
         (frame_levels, frame_counts),
         tables=2,
     )[0]
-    stats, attn_own, attn_pair, probs, dprobs = local_call(
+    stats, probs, dprobs = local_call(
         forward_kernel,
         "forward",
+        1.5,
         [
             shape((16, 2 * rows), F32),
-            shape((width, rows), F32),
-            shape((width, rows), BF16),
             shape((heads * SQUARE * keys, 2 * rows), BF16),
             shape((heads * SQUARE * keys, 2 * rows), F32),
         ],
         (limits, sec_q, q_pair, d_own, d_pair, *kvs),
-        flops=3 * work,
     )
     stats_pair = swap(stats, "ctx", PAIR)
-    stats_pair, attn_pair = lax.optimization_barrier((stats_pair, attn_pair))
-    attn_got = swap(attn_pair, "ctx", PAIR)
+    attn_own, attn_pair = local_call(
+        attn_kernel,
+        "attn",
+        0.5,
+        [shape((width, rows), F32), shape((width, rows), BF16)],
+        (*kvs, probs),
+    )
+    attn_own, probs = lax.optimization_barrier((attn_own, probs))
     dq_own, dq_pair, dkv_own, send_k, send_v, near_k, near_v = local_call(
         backward_kernel,
         "backward",
+        1.1,
         [shape((rows, width), F32), shape((rows, width), BF16), shape((2 * keys, width), F32)]
         + [shape((2 * keys, width), BF16)] * 2
         + [shape((keys, width), F32)] * 2,
         (sec_q, q_pair, d_own, d_pair, *kvs, stats, stats_pair, probs, dprobs),
-        flops=3 * work,
-    )
+    )
+    attn_got = swap(attn_pair, "ctx", PAIR)
+    attn_got, send_k, send_v = lax.optimization_barrier((attn_got, send_k, send_v))
     got_k = swap(send_k, "ctx", 1)
     got_v = swap(send_v, "ctx", 2)
     dq_got = swap(dq_pair, "ctx", PAIR)
     rest_k, rest_v = local_call(
         pass_on_kernel,
         "pass_on",
+        0.1,
         [shape((keys, width), BF16)] * 2,
         (near_k, near_v, got_k, got_v),
     )
     rest_k = swap(rest_k, "ctx", 2)
     rest_v = swap(rest_v, "ctx", 1)
-    attn_own, dq_own = lax.optimization_barrier((attn_own, dq_own))
     out_keep, *out_send = local_call(
         project_kernel,
         "project",
+        0.6,
         [shape((rows, share), F32)] + [shape((rows, share), BF16)] * 3,
         (attn_own, attn_got, stats, stats_pair, w_out),
-        flops=2 * rows * width * share * 4,
     )
     out_got = [swap(out_send[step - 1], "head", step) for step in (1, 2, 3)]
     grad_q, grad_k, grad_v, grad_hk, grad_hv, out = local_call(
         finish_kernel,
         "finish",
+        0.9,
         [shape((rows, width), BF16)] * 3
         + [shape((capacity, width), BF16)] * 2
         + [shape((rows, share), BF16)],

time: 58.2 us -> 57.4 us (0.986); the launches traced: 57.3 us -> 57.2 us
  starting transfers between devices: 24.2 us -> 21.9 us
  waiting for transfers between devices: 22 us -> 24.3 us
  local copies, waits for them, and re-layouts: 2.7 us -> 1.03 us
  Pallas kernels: 7.66 us -> 9.16 us
    pallas_call x0 -> x1, Pallas kernels: none -> 2.56 us  [dattn_call(): pl.pallas_call(dattn_kernel, name='dattn', out_shape=jax.ShapeDtypeStruct...]
    ppermute x18, starting transfers between devices: 24.2 us -> 21.9 us  [swap(): return lax.ppermute(block, axis, [(i, i ^ bit) for i in range(count)])]
    ppermute x18, waiting for transfers between devices: 22 us -> 24.3 us  [swap(): return lax.ppermute(block, axis, [(i, i ^ bit) for i in range(count)])]
    unnamed x15 -> x13, local copies, waits for them, and re-layouts: 2.7 us -> 1.03 us
    pallas_call x7, Pallas kernels: 5.96 us -> 4.93 us  [local_call(): pl.pallas_call(body, name=name, out_shape=out_shapes, in_specs=[pl.BlockS...]
  transfers between devices with their start and end apart: 18 -> 18, of which waited for: 7 -> 8; matrix products, arithmetic and copies ran while one was open for 0% -> 0% of each run, Pallas kernels for 4% -> 12%
where the time goes in v6:
time: 57.4 us; the launch traced here: 57.2 us
  waiting for transfers between devices  24.3 us (42%)
  starting transfers between devices  21.9 us (38%)
  Pallas kernels  9.16 us (16%)
  local copies, waits for them, and re-layouts  1.03 us (2%)
  between operations  0.79 us (1%)
    ppermute x18, waiting for transfers between devices, swap(): return lax.ppermute(block, axis, [(i, i ^ bit) for i in range(count)])  24.3 us
    ppermute x18, starting transfers between devices, swap(): return lax.ppermute(block, axis, [(i, i ^ bit) for i in range(count)])  21.9 us
    pallas_call x7, Pallas kernels, local_call(): pl.pallas_call(body, name=name, out_shape=out_shapes, in_specs=[pl.BlockS...  4.93 us
    pallas_call x1, Pallas kernels, dattn_call(): pl.pallas_call(dattn_kernel, name='dattn', out_shape=jax.ShapeDtypeStruct...  2.56 us
    pallas_call x1, Pallas kernels, load_keys(): pl.pallas_call(load_kernel, name='load', out_shape=jax.ShapeDtypeStruct((...  1.67 us
  transfers between devices with their start and end apart: 18, of which 8 were waited for; matrix products, arithmetic and copies ran while one was open for 0% of the time, Pallas kernels for 12%

profile of v6, /device:TPU:0, one launch (start us, length us, event | category | flops | bytes accessed | tf_op | source)
XLA Modules:
  0.0 57.2 jit_solution(15274261063594375823)
XLA Ops:
  0.6 0.0 copy-start.2
  0.7 3.0 %collective-permute-start = (bf16[128,768]{1,0:T(8,128)(2,1)}, bf16[128,768]{1,0:T(8,128)(2,1)S(1)}, u32[]{:S(2)}, u32[]{:S(2)}) collective-permute-start(bf16[128,768]{1,0:T(8,128)(2,1)} %own_hbm.1), channel_id=1, source_target_pairs={{0,2},{1,3},{2,0},{3,1},{4,6},{5,7},{6,4},{7,5},{8,10},{9,11},{10,... | collective-permute-start | bytes 589832 | tf_op jit(solution)/shard_map/ppermute | solution.py:35
  3.7 1.7 %load.1.kv0 = bf16[320,384]{1,0:T(8,128)(2,1)} custom-call(bf16[128,384]{1,0:T(8,128)(2,1)} %k_ref.1, bf16[32,384]{1,0:T(8,128)(2,1)} %hk_ref.1, bf16[128,384]{1,0:T(8,128)(2,1)} %v_ref.1, bf16[32,384]{1,0:T(8,128)(2,1)} %hv_ref.1), custom_call_target="tpu_custom_call" | custom-call | bytes 5904000 | tf_op jit(solution)/shard_map/load/pallas_call | solution.py:74
  5.4 1.6 %collective-permute-start.6 = (bf16[320,384]{1,0:T(8,128)(2,1)}, bf16[320,384]{1,0:T(8,128)(2,1)S(1)}, u32[]{:S(2)}, u32[]{:S(2)}) collective-permute-start(bf16[320,384]{1,0:T(8,128)(2,1)} %load.1.kv0), channel_id=1, source_target_pairs={{0,8},{4,12},{8,0},{12,4},{16,24},{20,28},{24,16},{28,20},{1,9},{5... | collective-permute-start | bytes 737288 | tf_op jit(solution)/shard_map/ppermute | solution.py:35
  7.0 2.6 %collective-permute-start.1 = (bf16[128,384]{1,0:T(8,128)(2,1)}, bf16[128,384]{1,0:T(8,128)(2,1)S(1)}, u32[]{:S(2)}, u32[]{:S(2)}) collective-permute-start(bf16[128,384]{1,0:T(8,128)(2,1)} %q_own_ref.3), channel_id=1, source_target_pairs={{0,16},{4,20},{8,24},{12,28},{16,0},{20,4},{24,8},{28,12},{1,17},{... | collective-permute-start | bytes 294920 | tf_op jit(solution)/shard_map/ppermute | solution.py:35
  9.6 0.0 collective-permute-start.2
  9.6 4.8 %collective-permute-done.1.q_pair_ref = bf16[128,384]{1,0:T(8,128)(2,1)S(1)} collective-permute-done((bf16[128,384]{1,0:T(8,128)(2,1)}, bf16[128,384]{1,0:T(8,128)(2,1)S(1)}, u32[]{:S(2)}, u32[]{:S(2)}) %collective-permute-start.1) | collective-permute-done | bytes 98336 | tf_op jit(solution)/shard_map/ppermute | solution.py:35
  14.4 0.0 collective-permute-done.near_ref
  14.4 0.0 collective-permute-start.3
  14.4 1.5 %collective-permute-start.5 = (bf16[320,384]{1,0:T(8,128)(2,1)}, bf16[320,384]{1,0:T(8,128)(2,1)S(1)}, u32[]{:S(2)}, u32[]{:S(2)}) collective-permute-start(bf16[320,384]{1,0:T(8,128)(2,1)} %load.1.kv0), channel_id=1, source_target_pairs={{0,4},{4,0},{8,12},{12,8},{16,20},{20,16},{24,28},{28,24},{1,5},{5... | collective-permute-start | bytes 737288 | tf_op jit(solution)/shard_map/ppermute | solution.py:35
  15.9 0.0 collective-permute-done.6.kv2
  15.9 0.8 %collective-permute-start.7 = (bf16[320,384]{1,0:T(8,128)(2,1)S(1)}, bf16[320,384]{1,0:T(8,128)(2,1)S(1)}, u32[]{:S(2)}, u32[]{:S(2)}) collective-permute-start(bf16[320,384]{1,0:T(8,128)(2,1)S(1)} %collective-permute-done.6.kv2), channel_id=1, source_target_pairs={{0,4},{4,0},{8,12},{12,8},{16,20},{20,16},{24,28},{28,24},{1,5},{5... | collective-permute-start | bytes 737288 | tf_op jit(solution)/shard_map/ppermute | solution.py:35
  16.7 0.0 collective-permute-done.2.core_ref
  16.7 0.0 collective-permute-done.3.far_ref
  16.7 0.9 %copy-done.3 = bf16[128,768]{1,0:T(8,128)(2,1)S(1)} copy-done((bf16[128,768]{1,0:T(8,128)(2,1)S(1)}, bf16[128,768]{1,0:T(8,128)(2,1)}, u32[]{:S(2)}) %copy-start.3) | copy-done | bytes 196632
  17.6 2.6 %dattn.1.d_own_ref = bf16[128,384]{1,0:T(8,128)(2,1)S(1)} custom-call(bf16[128,768]{1,0:T(8,128)(2,1)S(1)} %copy-done.3, bf16[384,3072]{1,0:T(8,128)(2,1)} %w_ref.1, bf16[128,768]{1,0:T(8,128)(2,1)S(1)} %collective-permute-done.2.core_ref, bf16[128,768]{1,0:T(8,128)(2,1)S(1)} %collective-permute-done.near_ref, ...), custom_call_target="tpu_custom_call" | custom-call | bytes 5535000 | tf_op jit(solution)/shard_map/dattn/pallas_call | solution.py:121
  20.2 3.1 %collective-permute-start.4 = (bf16[128,384]{1,0:T(8,128)(2,1)S(1)}, bf16[128,384]{1,0:T(8,128)(2,1)S(1)}, u32[]{:S(2)}, u32[]{:S(2)}) collective-permute-start(bf16[128,384]{1,0:T(8,128)(2,1)S(1)} %dattn.1.d_own_ref), channel_id=1, source_target_pairs={{0,16},{4,20},{8,24},{12,28},{16,0},{20,4},{24,8},{28,12},{1,17},{... | collective-permute-start | bytes 294920 | tf_op jit(solution)/shard_map/ppermute | solution.py:35
  23.2 0.1 copy.15.levels_ref
  23.3 0.6 %limits.1.limits_ref = s32[8,256]{1,0:T(8,128)S(1)} custom-call(s32[8,2]{1,0:T(8,128)S(1)} %copy.15.levels_ref, s32[8]{0:T(128)S(1)} %copy-done.4), custom_call_target="tpu_custom_call" | custom-call | bytes 2214000 | tf_op jit(solution)/shard_map/limits/pallas_call | solution.py:44
  24.0 0.0 collective-permute-done.5.kv1
  24.0 2.2 %collective-permute-done.4.d_pair_ref = bf16[128,384]{1,0:T(8,128)(2,1)S(1)} collective-permute-done((bf16[128,384]{1,0:T(8,128)(2,1)S(1)}, bf16[128,384]{1,0:T(8,128)(2,1)S(1)}, u32[]{:S(2)}, u32[]{:S(2)}) %collective-permute-start.4) | collective-permute-done | bytes 98336 | tf_op jit(solution)/shard_map/ppermute | solution.py:35
  26.1 2.1 %collective-permute-done.7.kv3 = bf16[320,384]{1,0:T(8,128)(2,1)S(1)} collective-permute-done((bf16[320,384]{1,0:T(8,128)(2,1)S(1)}, bf16[320,384]{1,0:T(8,128)(2,1)S(1)}, u32[]{:S(2)}, u32[]{:S(2)}) %collective-permute-start.7) | collective-permute-done | bytes 245792 | tf_op jit(solution)/shard_map/ppermute | solution.py:35
  28.2 1.2 %forward.1 = (f32[16,256]{1,0:T(8,128)S(1)}, bf16[1920,256]{1,0:T(8,128)(2,1)S(1)}, f32[1920,256]{1,0:T(8,128)S(1)}) custom-call(s32[8,256]{1,0:T(8,128)S(1)} %limits.1.limits_ref, bf16[128,384]{1,0:T(8,128)(2,1)S(1)} %copy-done.2, bf16[128,384]{1,0:T(8,128)(2,1)S(1)} %collective-permute-done.1.q_pair_ref, bf16[128,384]{1,0:T(8,128)(2,1)S(1)} %dattn.1.d_own_ref, ...), custom_call_target="tpu_custom_call" | custom-call | bytes 5535000 | tf_op jit(solution)/shard_map/forward/pallas_call | solution.py:44
  29.4 0.4 attn.1
  29.8 0.0 copy-start
  29.9 3.3 %collective-permute-start.10 = (bf16[384,128]{1,0:T(8,128)(2,1)S(1)}, bf16[384,128]{1,0:T(8,128)(2,1)S(1)}, u32[]{:S(2)}, u32[]{:S(2)}) collective-permute-start(bf16[384,128]{1,0:T(8,128)(2,1)S(1)} %get-tuple-element.47), channel_id=1, source_target_pairs={{0,16},{4,20},{8,24},{12,28},{16,0},{20,4},{24,8},{28,12},{1,17},{... | collective-permute-start | bytes 294920 | tf_op jit(solution)/shard_map/ppermute | solution.py:35
  33.2 0.1 collective-permute-start.8
  33.3 5.5 %collective-permute-done.8.stats_pair_ref = f32[16,256]{1,0:T(8,128)S(1)} collective-permute-done((f32[16,256]{1,0:T(8,128)S(1)}, f32[16,256]{1,0:T(8,128)S(1)}, u32[]{:S(2)}, u32[]{:S(2)}) %collective-permute-start.8) | collective-permute-done | bytes 16416 | tf_op jit(solution)/shard_map/ppermute | solution.py:35
  38.8 1.1 %backward.1 = (f32[128,384]{1,0:T(8,128)S(1)}, bf16[128,384]{1,0:T(8,128)(2,1)S(1)}, f32[320,384]{1,0:T(8,128)S(1)}, bf16[320,384]{1,0:T(8,128)(2,1)S(1)}, bf16[...) custom-call(bf16[128,384]{1,0:T(8,128)(2,1)S(1)} %copy-done.2, ...), custom_call_target="tpu_custom_call" | custom-call | bytes 4059000 | tf_op jit(solution)/shard_map/backward/pallas_call | solution.py:44
  39.9 0.0 collective-permute-done.10.pair_ref
  39.9 1.6 %collective-permute-start.11 = (bf16[320,384]{1,0:T(8,128)(2,1)S(1)}, bf16[320,384]{1,0:T(8,128)(2,1)S(1)}, u32[]{:S(2)}, u32[]{:S(2)}) collective-permute-start(bf16[320,384]{1,0:T(8,128)(2,1)S(1)} %get-tuple-element.50), channel_id=1, source_target_pairs={{0,4},{4,0},{8,12},{12,8},{16,20},{20,16},{24,28},{28,24},{1,5},{5... | collective-permute-start | bytes 737288 | tf_op jit(solution)/shard_map/ppermute | solution.py:35
  41.5 0.3 collective-permute-start.12
  41.8 2.6 %collective-permute-start.9 = (bf16[128,384]{1,0:T(8,128)(2,1)S(1)}, bf16[128,384]{1,0:T(8,128)(2,1)S(1)}, u32[]{:S(2)}, u32[]{:S(2)}) collective-permute-start(bf16[128,384]{1,0:T(8,128)(2,1)S(1)} %get-tuple-element.45), channel_id=1, source_target_pairs={{0,16},{4,20},{8,24},{12,28},{16,0},{20,4},{24,8},{28,12},{1,17},{... | collective-permute-start | bytes 294920 | tf_op jit(solution)/shard_map/ppermute | solution.py:35
  44.4 0.6 %project.1 = (f32[128,768]{1,0:T(8,128)S(1)}, bf16[128,768]{1,0:T(8,128)(2,1)S(1)}, bf16[128,768]{1,0:T(8,128)(2,1)S(1)}, bf16[128,768]{1,0:T(8,128)(2,1)S(1)}) custom-call(f32[384,128]{1,0:T(8,128)S(1)} %get-tuple-element.56.own_ref, bf16[384,128]{1,0:T(8,128)(2,1)S(1)} %collective-permute-done.10.pair_ref, f32[16,256]{1,0:T(8,128)S(1)} %get-tuple-element.39.stats_ref, ...), custom_call_target="tpu_custom_call" | custom-call | bytes 2214000 | tf_op jit(solution)/shard_map/project/pallas_call | solution.py:44
  45.1 0.1 collective-permute-start.15
  45.1 0.6 %collective-permute-start.16 = (bf16[128,768]{1,0:T(8,128)(2,1)S(1)}, bf16[128,768]{1,0:T(8,128)(2,1)S(1)}, u32[]{:S(2)}, u32[]{:S(2)}) collective-permute-start(bf16[128,768]{1,0:T(8,128)(2,1)S(1)} %get-tuple-element.60), channel_id=1, source_target_pairs={{0,2},{1,3},{2,0},{3,1},{4,6},{5,7},{6,4},{7,5},{8,10},{9,11},{10,... | collective-permute-start | bytes 589832 | tf_op jit(solution)/shard_map/ppermute | solution.py:35
  45.7 2.1 %collective-permute-done.11.got_k_ref = bf16[320,384]{1,0:T(8,128)(2,1)S(1)} collective-permute-done((bf16[320,384]{1,0:T(8,128)(2,1)S(1)}, bf16[320,384]{1,0:T(8,128)(2,1)S(1)}, u32[]{:S(2)}, u32[]{:S(2)}) %collective-permute-start.11) | collective-permute-done | bytes 245792 | tf_op jit(solution)/shard_map/ppermute | solution.py:35
  47.8 0.0 collective-permute-start.17
  47.8 3.3 %collective-permute-done.12.got_v_ref = bf16[320,384]{1,0:T(8,128)(2,1)S(1)} collective-permute-done((bf16[320,384]{1,0:T(8,128)(2,1)S(1)}, bf16[320,384]{1,0:T(8,128)(2,1)S(1)}, u32[]{:S(2)}, u32[]{:S(2)}) %collective-permute-start.12) | collective-permute-done | bytes 245792 | tf_op jit(solution)/shard_map/ppermute | solution.py:35
  51.2 0.1 collective-permute-start.13
  51.3 0.0 collective-permute-done.9.dq_pair_ref
  51.3 0.6 collective-permute-start.14
  51.9 0.0 collective-permute-done.15.core_ref
  51.9 1.0 %collective-permute-done.16.near_ref = bf16[128,768]{1,0:T(8,128)(2,1)S(1)} collective-permute-done((bf16[128,768]{1,0:T(8,128)(2,1)S(1)}, bf16[128,768]{1,0:T(8,128)(2,1)S(1)}, u32[]{:S(2)}, u32[]{:S(2)}) %collective-permute-start.16) | collective-permute-done | bytes 196640 | tf_op jit(solution)/shard_map/ppermute | solution.py:35
  52.9 3.3 %collective-permute-done.17.far_ref = bf16[128,768]{1,0:T(8,128)(2,1)S(1)} collective-permute-done((bf16[128,768]{1,0:T(8,128)(2,1)S(1)}, bf16[128,768]{1,0:T(8,128)(2,1)S(1)}, u32[]{:S(2)}, u32[]{:S(2)}) %collective-permute-start.17) | collective-permute-done | bytes 196640 | tf_op jit(solution)/shard_map/ppermute | solution.py:35
  56.2 0.0 collective-permute-done.13.rest_k_ref
  56.2 0.0 collective-permute-done.14.rest_v_ref
  56.3 0.9 %finish.1 = (bf16[128,384]{1,0:T(8,128)(2,1)}, bf16[128,384]{1,0:T(8,128)(2,1)}, bf16[128,384]{1,0:T(8,128)(2,1)}, bf16[32,384]{1,0:T(8,128)(2,1)}, bf16[32,384]{1,0:T(8,128)(2,1)}, /*index=5*/bf16[128,768]{1,0:T(8,128)(2,1)}) custom-call(f32[128,384]{1,0:T(8,128)S(1)} %get-tuple-element.44.dq_ref, bf16[128,384]{1,0:T(8,128)(2,1)S(1)} %collective-permute-done.9.dq_pair_ref, ...), custom_call_target="tpu_custom_call" | custom-call | bytes 3321000 | tf_op jit(solution)/shard_map/finish/pallas_call | solution.py:44
  (10 shorter events, 0.1 us)
Async XLA Ops:
  0.6 27.6 %copy-start.2 = (bf16[128,384]{1,0:T(8,128)(2,1)S(1)}, bf16[128,384]{1,0:T(8,128)(2,1)}, u32[]{:S(2)}) copy-start(bf16[128,384]{1,0:T(8,128)(2,1)} %q_own_ref.3) | copy-start | bytes 294916
  0.6 22.6 %copy-start.5 = (s32[8,2]{0,1:T(2,128)S(1)}, s32[8,2]{0,1:T(2,128)}, u32[]{:S(2)}) copy-start(s32[8,2]{0,1:T(2,128)} %param.14) | copy-start | bytes 196
  0.7 22.7 %copy-start.4 = (s32[8]{0:T(128)S(1)}, s32[8]{0:T(128)}, u32[]{:S(2)}) copy-start(s32[8]{0:T(128)} %counts_ref.1) | copy-start | bytes 100
  0.7 13.7 %collective-permute-start = (bf16[128,768]{1,0:T(8,128)(2,1)}, bf16[128,768]{1,0:T(8,128)(2,1)S(1)}, u32[]{:S(2)}, u32[]{:S(2)}) collective-permute-start(bf16[128,768]{1,0:T(8,128)(2,1)} %own_hbm.1), channel_id=1, source_target_pairs={{0,2},{1,3},{2,0},{3,1},{4,6},{5,7},{6,4},{7,5},{8,10},{9,11},{10,... | collective-permute-start | bytes 589832 | tf_op jit(solution)/shard_map/ppermute | solution.py:35
  5.3 22.9 %copy-start.1 = (bf16[320,384]{1,0:T(8,128)(2,1)S(1)}, bf16[320,384]{1,0:T(8,128)(2,1)}, u32[]{:S(2)}) copy-start(bf16[320,384]{1,0:T(8,128)(2,1)} %load.1.kv0) | copy-start | bytes 737284
  5.4 10.5 %collective-permute-start.6 = (bf16[320,384]{1,0:T(8,128)(2,1)}, bf16[320,384]{1,0:T(8,128)(2,1)S(1)}, u32[]{:S(2)}, u32[]{:S(2)}) collective-permute-start(bf16[320,384]{1,0:T(8,128)(2,1)} %load.1.kv0), channel_id=1, source_target_pairs={{0,8},{4,12},{8,0},{12,4},{16,24},{20,28},{24,16},{28,20},{1,9},{5... | collective-permute-start | bytes 737288 | tf_op jit(solution)/shard_map/ppermute | solution.py:35
  7.0 7.4 %collective-permute-start.1 = (bf16[128,384]{1,0:T(8,128)(2,1)}, bf16[128,384]{1,0:T(8,128)(2,1)S(1)}, u32[]{:S(2)}, u32[]{:S(2)}) collective-permute-start(bf16[128,384]{1,0:T(8,128)(2,1)} %q_own_ref.3), channel_id=1, source_target_pairs={{0,16},{4,20},{8,24},{12,28},{16,0},{20,4},{24,8},{28,12},{1,17},{... | collective-permute-start | bytes 294920 | tf_op jit(solution)/shard_map/ppermute | solution.py:35
  9.6 7.1 %collective-permute-start.2 = (bf16[128,768]{1,0:T(8,128)(2,1)}, bf16[128,768]{1,0:T(8,128)(2,1)S(1)}, u32[]{:S(2)}, u32[]{:S(2)}) collective-permute-start(bf16[128,768]{1,0:T(8,128)(2,1)} %own_hbm.1), channel_id=1, source_target_pairs={{0,1},{1,0},{2,3},{3,2},{4,5},{5,4},{6,7},{7,6},{8,9},{9,8},{10,11... | collective-permute-start | bytes 589832 | tf_op jit(solution)/shard_map/ppermute | solution.py:35
  14.4 2.3 %collective-permute-start.3 = (bf16[128,768]{1,0:T(8,128)(2,1)S(1)}, bf16[128,768]{1,0:T(8,128)(2,1)S(1)}, u32[]{:S(2)}, u32[]{:S(2)}) collective-permute-start(bf16[128,768]{1,0:T(8,128)(2,1)S(1)} %collective-permute-done.near_ref), channel_id=1, source_target_pairs={{0,1},{1,0},{2,3},{3,2},{4,5},{5,4},{6,7},{7,6},{8,9},{9,8},{10,11... | collective-permute-start | bytes 589832 | tf_op jit(solution)/shard_map/ppermute | solution.py:35
  14.4 9.6 %collective-permute-start.5 = (bf16[320,384]{1,0:T(8,128)(2,1)}, bf16[320,384]{1,0:T(8,128)(2,1)S(1)}, u32[]{:S(2)}, u32[]{:S(2)}) collective-permute-start(bf16[320,384]{1,0:T(8,128)(2,1)} %load.1.kv0), channel_id=1, source_target_pairs={{0,4},{4,0},{8,12},{12,8},{16,20},{20,16},{24,28},{28,24},{1,5},{5... | collective-permute-start | bytes 737288 | tf_op jit(solution)/shard_map/ppermute | solution.py:35
  15.9 12.3 %collective-permute-start.7 = (bf16[320,384]{1,0:T(8,128)(2,1)S(1)}, bf16[320,384]{1,0:T(8,128)(2,1)S(1)}, u32[]{:S(2)}, u32[]{:S(2)}) collective-permute-start(bf16[320,384]{1,0:T(8,128)(2,1)S(1)} %collective-permute-done.6.kv2), channel_id=1, source_target_pairs={{0,4},{4,0},{8,12},{12,8},{16,20},{20,16},{24,28},{28,24},{1,5},{5... | collective-permute-start | bytes 737288 | tf_op jit(solution)/shard_map/ppermute | solution.py:35
  16.7 0.9 %copy-start.3 = (bf16[128,768]{1,0:T(8,128)(2,1)S(1)}, bf16[128,768]{1,0:T(8,128)(2,1)}, u32[]{:S(2)}) copy-start(bf16[128,768]{1,0:T(8,128)(2,1)} %own_hbm.1) | copy-start | bytes 589828
  20.2 6.0 %collective-permute-start.4 = (bf16[128,384]{1,0:T(8,128)(2,1)S(1)}, bf16[128,384]{1,0:T(8,128)(2,1)S(1)}, u32[]{:S(2)}, u32[]{:S(2)}) collective-permute-start(bf16[128,384]{1,0:T(8,128)(2,1)S(1)} %dattn.1.d_own_ref), channel_id=1, source_target_pairs={{0,16},{4,20},{8,24},{12,28},{16,0},{20,4},{24,8},{28,12},{1,17},{... | collective-permute-start | bytes 294920 | tf_op jit(solution)/shard_map/ppermute | solution.py:35
  29.8 14.6 %copy-start = (bf16[384,3072]{1,0:T(8,128)(2,1)S(1)}, bf16[384,3072]{1,0:T(8,128)(2,1)}, u32[]{:S(2)}) copy-start(bf16[384,3072]{1,0:T(8,128)(2,1)} %w_ref.1) | copy-start | bytes 7077892
  29.9 10.0 %collective-permute-start.10 = (bf16[384,128]{1,0:T(8,128)(2,1)S(1)}, bf16[384,128]{1,0:T(8,128)(2,1)S(1)}, u32[]{:S(2)}, u32[]{:S(2)}) collective-permute-start(bf16[384,128]{1,0:T(8,128)(2,1)S(1)} %get-tuple-element.47), channel_id=1, source_target_pairs={{0,16},{4,20},{8,24},{12,28},{16,0},{20,4},{24,8},{28,12},{1,17},{... | collective-permute-start | bytes 294920 | tf_op jit(solution)/shard_map/ppermute | solution.py:35
  33.2 5.6 %collective-permute-start.8 = (f32[16,256]{1,0:T(8,128)S(1)}, f32[16,256]{1,0:T(8,128)S(1)}, u32[]{:S(2)}, u32[]{:S(2)}) collective-permute-start(f32[16,256]{1,0:T(8,128)S(1)} %get-tuple-element.39.stats_ref), channel_id=1, source_target_pairs={{0,16},{4,20},{8,24},{12,28},{16,0},{20,4},{24,8},{28,12},{1,17},{... | collective-permute-start | bytes 49160 | tf_op jit(solution)/shard_map/ppermute | solution.py:35
  39.9 7.9 %collective-permute-start.11 = (bf16[320,384]{1,0:T(8,128)(2,1)S(1)}, bf16[320,384]{1,0:T(8,128)(2,1)S(1)}, u32[]{:S(2)}, u32[]{:S(2)}) collective-permute-start(bf16[320,384]{1,0:T(8,128)(2,1)S(1)} %get-tuple-element.50), channel_id=1, source_target_pairs={{0,4},{4,0},{8,12},{12,8},{16,20},{20,16},{24,28},{28,24},{1,5},{5... | collective-permute-start | bytes 737288 | tf_op jit(solution)/shard_map/ppermute | solution.py:35
  41.5 9.7 %collective-permute-start.12 = (bf16[320,384]{1,0:T(8,128)(2,1)S(1)}, bf16[320,384]{1,0:T(8,128)(2,1)S(1)}, u32[]{:S(2)}, u32[]{:S(2)}) collective-permute-start(bf16[320,384]{1,0:T(8,128)(2,1)S(1)} %get-tuple-element.51), channel_id=1, source_target_pairs={{0,8},{4,12},{8,0},{12,4},{16,24},{20,28},{24,16},{28,20},{1,9},{5... | collective-permute-start | bytes 737288 | tf_op jit(solution)/shard_map/ppermute | solution.py:35
  41.8 9.5 %collective-permute-start.9 = (bf16[128,384]{1,0:T(8,128)(2,1)S(1)}, bf16[128,384]{1,0:T(8,128)(2,1)S(1)}, u32[]{:S(2)}, u32[]{:S(2)}) collective-permute-start(bf16[128,384]{1,0:T(8,128)(2,1)S(1)} %get-tuple-element.45), channel_id=1, source_target_pairs={{0,16},{4,20},{8,24},{12,28},{16,0},{20,4},{24,8},{28,12},{1,17},{... | collective-permute-start | bytes 294920 | tf_op jit(solution)/shard_map/ppermute | solution.py:35
  45.1 6.8 %collective-permute-start.15 = (bf16[128,768]{1,0:T(8,128)(2,1)S(1)}, bf16[128,768]{1,0:T(8,128)(2,1)S(1)}, u32[]{:S(2)}, u32[]{:S(2)}) collective-permute-start(bf16[128,768]{1,0:T(8,128)(2,1)S(1)} %get-tuple-element.59), channel_id=1, source_target_pairs={{0,1},{1,0},{2,3},{3,2},{4,5},{5,4},{6,7},{7,6},{8,9},{9,8},{10,11... | collective-permute-start | bytes 589832 | tf_op jit(solution)/shard_map/ppermute | solution.py:35
  45.1 7.8 %collective-permute-start.16 = (bf16[128,768]{1,0:T(8,128)(2,1)S(1)}, bf16[128,768]{1,0:T(8,128)(2,1)S(1)}, u32[]{:S(2)}, u32[]{:S(2)}) collective-permute-start(bf16[128,768]{1,0:T(8,128)(2,1)S(1)} %get-tuple-element.60), channel_id=1, source_target_pairs={{0,2},{1,3},{2,0},{3,1},{4,6},{5,7},{6,4},{7,5},{8,10},{9,11},{10,... | collective-permute-start | bytes 589832 | tf_op jit(solution)/shard_map/ppermute | solution.py:35
  47.8 8.4 %collective-permute-start.17 = (bf16[128,768]{1,0:T(8,128)(2,1)S(1)}, bf16[128,768]{1,0:T(8,128)(2,1)S(1)}, u32[]{:S(2)}, u32[]{:S(2)}) collective-permute-start(bf16[128,768]{1,0:T(8,128)(2,1)S(1)} %get-tuple-element.61), channel_id=1, source_target_pairs={{0,3},{1,2},{2,1},{3,0},{4,7},{5,6},{6,5},{7,4},{8,11},{9,10},{10,... | collective-permute-start | bytes 589832 | tf_op jit(solution)/shard_map/ppermute | solution.py:35
  51.2 5.0 %collective-permute-start.13 = (bf16[160,384]{1,0:T(8,128)(2,1)S(1)}, bf16[160,384]{1,0:T(8,128)(2,1)S(1)}, u32[]{:S(2)}, u32[]{:S(2)}) collective-permute-start(bf16[160,384]{1,0:T(8,128)(2,1)S(1)} %get-tuple-element.54), channel_id=1, source_target_pairs={{0,8},{4,12},{8,0},{12,4},{16,24},{20,28},{24,16},{28,20},{1,9},{5... | collective-permute-start | bytes 368648 | tf_op jit(solution)/shard_map/ppermute | solution.py:35
  51.3 4.9 %collective-permute-start.14 = (bf16[160,384]{1,0:T(8,128)(2,1)S(1)}, bf16[160,384]{1,0:T(8,128)(2,1)S(1)}, u32[]{:S(2)}, u32[]{:S(2)}) collective-permute-start(bf16[160,384]{1,0:T(8,128)(2,1)S(1)} %get-tuple-element.55), channel_id=1, source_target_pairs={{0,4},{4,0},{8,12},{12,8},{16,20},{20,16},{24,28},{28,24},{1,5},{5... | collective-permute-start | bytes 368648 | tf_op jit(solution)/shard_map/ppermute | solution.py:35

commit v7 on v6

--- a/solution.py
+++ b/solution.py
@@ -83,6 +83,18 @@
     )(*arrays)
 
 
+def pass_keys_kernel(kv1, kv2, key_ref, value_ref):
+    keys = key_ref.shape[0]
+    key_ref[...] = kv2[:keys]
+    value_ref[...] = kv1[keys:]
+
+
+def square_blocks(kv0, kv1, kv2, key3, value3):
+    keys = key3.shape[0]
+    pairs = [(ref.at[:keys], ref.at[keys:]) for ref in (kv0, kv1, kv2)]
+    return pairs + [(key3, value3)]
+
+
 def limits_kernel(levels_ref, counts_ref, limits_ref):
     me = lax.axis_index("ctx")
     row = lax.broadcasted_iota(jnp.int32, limits_ref.shape, 0)
@@ -99,16 +111,26 @@
 def dattn_kernel(own_hbm, w_hbm, core_ref, near_ref, far_ref, out_ref, own_ref, w_ref, sems):
     me = lax.axis_index("head")
     size = core_ref.shape[1]
-    copies = [pltpu.make_async_copy(own_hbm, own_ref, sems.at[4])]
+    pieces = w_ref.shape[1] // HDIM
+    own_copy = pltpu.make_async_copy(own_hbm, own_ref, sems.at[4, 0])
+    own_copy.start()
+    copies = []
     for step in range(4):
         columns = pl.ds(pl.multiple_of((me ^ step) * size, HDIM), size)
-        copies.append(pltpu.make_async_copy(w_hbm.at[:, columns], w_ref.at[step], sems.at[step]))
+        for i in range(pieces):
+            part = pl.ds(i * HDIM, HDIM)
+            copies.append(
+                pltpu.make_async_copy(
+                    w_hbm.at[part, columns], w_ref.at[step, part], sems.at[step, i]
+                )
+            )
     for copy in copies:
         copy.start()
-    copies[0].wait()
+    own_copy.wait()
     total = None
     for step, ref in enumerate((own_ref, core_ref, near_ref, far_ref)):
-        copies[1 + step].wait()
+        for copy in copies[step * pieces : (step + 1) * pieces]:
+            copy.wait()
         part = contract(ref[...], w_ref[step], 1, 1)
         total = part if total is None else total + part
     out_ref[...] = total.astype(BF16)
@@ -127,7 +149,7 @@
         scratch_shapes=[
             pltpu.VMEM((rows, share), BF16),
             pltpu.VMEM((4, width, share), BF16),
-            pltpu.SemaphoreType.DMA((5,)),
+            pltpu.SemaphoreType.DMA((5, width // HDIM)),
         ],
         compiler_params=pltpu.CompilerParams(vmem_limit_bytes=52 * 2**20),
         cost_estimate=cost_of(1.5),
@@ -141,19 +163,19 @@
 
 
 def forward_kernel(
-    limits_ref, q_own_ref, q_pair_ref, d_own_ref, d_pair_ref, kv0, kv1, kv2, kv3,
+    limits_ref, q_own_ref, q_pair_ref, d_own_ref, d_pair_ref, kv0, kv1, kv2, key3, value3,
     stats_ref, probs_ref, dprobs_ref,
 ):
     rows = q_own_ref.shape[0]
-    keys = kv0.shape[0] // 2
-    blocks = (kv0, kv1, kv2, kv3)
+    keys = key3.shape[0]
+    blocks = square_blocks(kv0, kv1, kv2, key3, value3)
     stats_ref[...] = jnp.zeros_like(stats_ref)
     for head in range(q_own_ref.shape[1] // HDIM):
         query = both_rows(q_own_ref, q_pair_ref, head)
         dattn = both_rows(d_own_ref, d_pair_ref, head)
         scores = []
-        for step, ref in enumerate(blocks):
-            block = contract(head_slice(ref[:keys], head), query, 1, 1) * SCALE
+        for step, (key_ref, _) in enumerate(blocks):
+            block = contract(head_slice(key_ref[...], head), query, 1, 1) * SCALE
             slot = lax.broadcasted_iota(jnp.int32, block.shape, 0)
             valid = slot < rows + limits_ref[step : step + 1]
             scores.append(jnp.where(valid, block, NEG_FILL))
@@ -164,9 +186,9 @@
         total = sum(jnp.sum(block, axis=0, keepdims=True) for block in weights)
         inverse = 1.0 / total
         delta = None
-        for step, ref in enumerate(blocks):
+        for step, (_, value_ref) in enumerate(blocks):
             probs = weights[step] * inverse
-            dprobs = contract(head_slice(ref[keys:], head), dattn, 1, 1)
+            dprobs = contract(head_slice(value_ref[...], head), dattn, 1, 1)
             part = jnp.sum(probs * dprobs, axis=0, keepdims=True)
             delta = part if delta is None else delta + part
             begin = (head * SQUARE + step) * keys
@@ -176,14 +198,15 @@
         stats_ref[8 + head : 9 + head] = delta
 
 
-def attn_kernel(kv0, kv1, kv2, kv3, probs_ref, own_ref, pair_ref):
+def attn_kernel(kv0, kv1, kv2, key3, value3, probs_ref, own_ref, pair_ref):
     rows = own_ref.shape[1]
-    keys = kv0.shape[0] // 2
+    keys = key3.shape[0]
+    blocks = square_blocks(kv0, kv1, kv2, key3, value3)
     for head in range(own_ref.shape[0] // HDIM):
         attn = None
-        for step, ref in enumerate((kv0, kv1, kv2, kv3)):
+        for step, (_, value_ref) in enumerate(blocks):
             begin = (head * SQUARE + step) * keys
-            part = contract(head_slice(ref[keys:], head), probs_ref[begin : begin + keys], 0, 0)
+            part = contract(head_slice(value_ref[...], head), probs_ref[begin : begin + keys], 0, 0)
             attn = part if attn is None else attn + part
         features = slice(head * HDIM, (head + 1) * HDIM)
         own_ref[features] = attn[:, :rows]
@@ -215,12 +238,13 @@
 
 
 def backward_kernel(
-    q_own_ref, q_pair_ref, d_own_ref, d_pair_ref, kv0, kv1, kv2, kv3,
+    q_own_ref, q_pair_ref, d_own_ref, d_pair_ref, kv0, kv1, kv2, key3, value3,
     stats_ref, stats_pair_ref, probs_ref, dprobs_ref,
     dq_own_ref, dq_pair_ref, dkv_ref, send_k_ref, send_v_ref, near_k_ref, near_v_ref,
 ):
     rows = q_own_ref.shape[0]
-    keys = kv0.shape[0] // 2
+    keys = key3.shape[0]
+    blocks = square_blocks(kv0, kv1, kv2, key3, value3)
     key_parts = (dkv_ref.at[:keys], send_k_ref.at[:keys], near_k_ref, send_k_ref.at[keys:])
     value_parts = (dkv_ref.at[keys:], near_v_ref, send_v_ref.at[:keys], send_v_ref.at[keys:])
 
@@ -237,7 +261,7 @@
         delta += weight_pair * swapped(stats_pair_ref[8 + head : 9 + head])
         features = slice(head * HDIM, (head + 1) * HDIM)
         dquery = None
-        for step, ref in enumerate((kv0, kv1, kv2, kv3)):
+        for step, (key_ref, _) in enumerate(blocks):
             begin = (head * SQUARE + step) * keys
             probs = (probs_ref[begin : begin + keys].astype(F32) * weight).astype(BF16)
             dprobs = dprobs_ref[begin : begin + keys]
@@ -246,7 +270,7 @@
             grad_key = contract(dscores, query, 1, 0) * SCALE
             key_part[:, features] = grad_key.astype(key_part.dtype)
             value_part[:, features] = contract(probs, dattn, 1, 0).astype(value_part.dtype)
-            part = contract(dscores, head_slice(ref[:keys], head), 0, 0)
+            part = contract(dscores, head_slice(key_ref[...], head), 0, 0)
             dquery = part if dquery is None else dquery + part
         dq_own_ref[:, features] = dquery[:rows] * SCALE
         dq_pair_ref[:, features] = (dquery[rows:] * SCALE).astype(BF16)
@@ -289,14 +313,17 @@
 
     q_pair = swap(sec_q, "ctx", PAIR)
     grad_near = swap(grad_out, "head", 2)
-    grad_near, q_pair = lax.optimization_barrier((grad_near, q_pair))
     grad_core = swap(grad_out, "head", 1)
     grad_far = swap(grad_near, "head", 1)
     kv0 = load_keys(sec_k, hist_k, sec_v, hist_v)
     kv2 = swap(kv0, "ctx", 2)
     kv1 = swap(kv0, "ctx", 1)
-    kvs = [kv0, kv1, kv2, swap(kv2, "ctx", 1)]
     d_own = dattn_call(grad_out, w_out, grad_core, grad_near, grad_far)
+    kv1, kv2, q_pair, d_own = lax.optimization_barrier((kv1, kv2, q_pair, d_own))
+    key3, value3 = local_call(
+        pass_keys_kernel, "pass_keys", 0.1, [shape((keys, width), BF16)] * 2, (kv1, kv2)
+    )
+    kvs = [kv0, kv1, kv2, swap(key3, "ctx", 1), swap(value3, "ctx", 2)]
     d_pair = swap(d_own, "ctx", PAIR)
     limits = local_call(
         limits_kernel,

time: 57.4 us -> 53.4 us (0.930)
  waiting for transfers between devices: 24.3 us -> 17.3 us
  starting transfers between devices: 21.9 us -> 24.6 us
    ppermute x18 -> x19, waiting for transfers between devices: 24.3 us -> 17.3 us  [swap(): return lax.ppermute(block, axis, [(i, i ^ bit) for i in range(count)])]
    ppermute x18 -> x19, starting transfers between devices: 21.9 us -> 24.6 us  [swap(): return lax.ppermute(block, axis, [(i, i ^ bit) for i in range(count)])]
    pallas_call x7 -> x8, Pallas kernels: 4.93 us -> 4.97 us  [local_call(): pl.pallas_call(body, name=name, out_shape=out_shapes, in_specs=[pl.BlockS...]
  transfers between devices with their start and end apart: 18 -> 19, of which waited for: 8 -> 9; matrix products, arithmetic and copies ran while one was open for 0% -> 0% of each run, Pallas kernels for 12% -> 13%
where the time goes in v7:
time: 53.4 us; the launch traced here: 53.2 us
  starting transfers between devices  24.6 us (46%)
  waiting for transfers between devices  17.3 us (32%)
  Pallas kernels  9.39 us (18%)
  local copies, waits for them, and re-layouts  1.03 us (2%)
  between operations  0.79 us (1%)
    ppermute x19, starting transfers between devices, swap(): return lax.ppermute(block, axis, [(i, i ^ bit) for i in range(count)])  24.6 us
    ppermute x19, waiting for transfers between devices, swap(): return lax.ppermute(block, axis, [(i, i ^ bit) for i in range(count)])  17.3 us
    pallas_call x8, Pallas kernels, local_call(): pl.pallas_call(body, name=name, out_shape=out_shapes, in_specs=[pl.BlockS...  4.97 us
    pallas_call x1, Pallas kernels, dattn_call(): pl.pallas_call(dattn_kernel, name='dattn', out_shape=jax.ShapeDtypeStruct...  2.75 us
    pallas_call x1, Pallas kernels, load_keys(): pl.pallas_call(load_kernel, name='load', out_shape=jax.ShapeDtypeStruct((...  1.67 us
  transfers between devices with their start and end apart: 19, of which 9 were waited for; matrix products, arithmetic and copies ran while one was open for 0% of the time, Pallas kernels for 13%

profile of v7, /device:TPU:0, one launch (start us, length us, event | category | flops | bytes accessed | tf_op | source)
XLA Modules:
  0.0 53.2 jit_solution(6543469200368041671)
XLA Ops:
  0.6 0.0 copy-start.2
  0.7 3.0 %collective-permute-start.4 = (bf16[128,768]{1,0:T(8,128)(2,1)}, bf16[128,768]{1,0:T(8,128)(2,1)S(1)}, u32[]{:S(2)}, u32[]{:S(2)}) collective-permute-start(bf16[128,768]{1,0:T(8,128)(2,1)} %own_hbm.1), channel_id=1, source_target_pairs={{0,2},{1,3},{2,0},{3,1},{4,6},{5,7},{6,4},{7,5},{8,10},{9,11},{10,... | collective-permute-start | bytes 589832 | tf_op jit(solution)/shard_map/ppermute | solution.py:35
  3.7 1.7 %load.1.kv0 = bf16[320,384]{1,0:T(8,128)(2,1)} custom-call(bf16[128,384]{1,0:T(8,128)(2,1)} %k_ref.1, bf16[32,384]{1,0:T(8,128)(2,1)} %hk_ref.1, bf16[128,384]{1,0:T(8,128)(2,1)} %v_ref.1, bf16[32,384]{1,0:T(8,128)(2,1)} %hv_ref.1), custom_call_target="tpu_custom_call" | custom-call | bytes 5904000 | tf_op jit(solution)/shard_map/load/pallas_call | solution.py:74
  5.4 1.6 %collective-permute-start.1 = (bf16[320,384]{1,0:T(8,128)(2,1)}, bf16[320,384]{1,0:T(8,128)(2,1)S(1)}, u32[]{:S(2)}, u32[]{:S(2)}) collective-permute-start(bf16[320,384]{1,0:T(8,128)(2,1)} %load.1.kv0), channel_id=1, source_target_pairs={{0,8},{4,12},{8,0},{12,4},{16,24},{20,28},{24,16},{28,20},{1,9},{5... | collective-permute-start | bytes 737288 | tf_op jit(solution)/shard_map/ppermute | solution.py:35
  7.0 1.5 %collective-permute-start = (bf16[320,384]{1,0:T(8,128)(2,1)}, bf16[320,384]{1,0:T(8,128)(2,1)S(1)}, u32[]{:S(2)}, u32[]{:S(2)}) collective-permute-start(bf16[320,384]{1,0:T(8,128)(2,1)} %load.1.kv0), channel_id=1, source_target_pairs={{0,4},{4,0},{8,12},{12,8},{16,20},{20,16},{24,28},{28,24},{1,5},{5... | collective-permute-start | bytes 737288 | tf_op jit(solution)/shard_map/ppermute | solution.py:35
  8.5 0.0 collective-permute-start.3
  8.5 0.3 collective-permute-done.4.near_ref
  8.8 0.2 collective-permute-start.5
  9.0 2.6 %collective-permute-start.2 = (bf16[128,384]{1,0:T(8,128)(2,1)}, bf16[128,384]{1,0:T(8,128)(2,1)S(1)}, u32[]{:S(2)}, u32[]{:S(2)}) collective-permute-start(bf16[128,384]{1,0:T(8,128)(2,1)} %q_own_ref.3), channel_id=1, source_target_pairs={{0,16},{4,20},{8,24},{12,28},{16,0},{20,4},{24,8},{28,12},{1,17},{... | collective-permute-start | bytes 294920 | tf_op jit(solution)/shard_map/ppermute | solution.py:35
  11.6 0.0 collective-permute-done.3.core_ref
  11.6 0.0 collective-permute-done.5.far_ref
  11.6 0.9 %copy-done.3 = bf16[128,768]{1,0:T(8,128)(2,1)S(1)} copy-done((bf16[128,768]{1,0:T(8,128)(2,1)S(1)}, bf16[128,768]{1,0:T(8,128)(2,1)}, u32[]{:S(2)}) %copy-start.3) | copy-done | bytes 196632
  12.6 2.8 %dattn.1.d_own_ref = bf16[128,384]{1,0:T(8,128)(2,1)S(1)} custom-call(bf16[128,768]{1,0:T(8,128)(2,1)S(1)} %copy-done.3, bf16[384,3072]{1,0:T(8,128)(2,1)} %w_ref.1, bf16[128,768]{1,0:T(8,128)(2,1)S(1)} %collective-permute-done.3.core_ref, bf16[128,768]{1,0:T(8,128)(2,1)S(1)} %collective-permute-done.4.near_ref, ...), custom_call_target="tpu_custom_call" | custom-call | bytes 5535000 | tf_op jit(solution)/shard_map/dattn/pallas_call | solution.py:143
  15.3 2.1 %collective-permute-done.2.q_pair_ref = bf16[128,384]{1,0:T(8,128)(2,1)S(1)} collective-permute-done((bf16[128,384]{1,0:T(8,128)(2,1)}, bf16[128,384]{1,0:T(8,128)(2,1)S(1)}, u32[]{:S(2)}, u32[]{:S(2)}) %collective-permute-start.2) | collective-permute-done | bytes 98336 | tf_op jit(solution)/shard_map/ppermute | solution.py:35
  17.4 0.0 collective-permute-done.1.kv2
  17.4 0.0 collective-permute-done.kv1
  17.4 1.6 %collective-permute-start.7 = (bf16[160,384]{1,0:T(8,128)(2,1)S(1)}, bf16[160,384]{1,0:T(8,128)(2,1)S(1)}, u32[]{:S(2)}, u32[]{:S(2)}) collective-permute-start(bf16[160,384]{1,0:T(8,128)(2,1)S(1)} %get-tuple-element.45), channel_id=1, source_target_pairs={{0,4},{4,0},{8,12},{12,8},{16,20},{20,16},{24,28},{28,24},{1,5},{5... | collective-permute-start | bytes 368648 | tf_op jit(solution)/shard_map/ppermute | solution.py:35
  19.1 0.8 %collective-permute-start.8 = (bf16[160,384]{1,0:T(8,128)(2,1)S(1)}, bf16[160,384]{1,0:T(8,128)(2,1)S(1)}, u32[]{:S(2)}, u32[]{:S(2)}) collective-permute-start(bf16[160,384]{1,0:T(8,128)(2,1)S(1)} %get-tuple-element.46), channel_id=1, source_target_pairs={{0,8},{4,12},{8,0},{12,4},{16,24},{20,28},{24,16},{28,20},{1,9},{5... | collective-permute-start | bytes 368648 | tf_op jit(solution)/shard_map/ppermute | solution.py:35
  19.9 3.3 %collective-permute-start.6 = (bf16[128,384]{1,0:T(8,128)(2,1)S(1)}, bf16[128,384]{1,0:T(8,128)(2,1)S(1)}, u32[]{:S(2)}, u32[]{:S(2)}) collective-permute-start(bf16[128,384]{1,0:T(8,128)(2,1)S(1)} %dattn.1.d_own_ref), channel_id=1, source_target_pairs={{0,16},{4,20},{8,24},{12,28},{16,0},{20,4},{24,8},{28,12},{1,17},{... | collective-permute-start | bytes 294920 | tf_op jit(solution)/shard_map/ppermute | solution.py:35
  23.1 0.1 copy.15.levels_ref
  23.2 0.6 %limits.1.limits_ref = s32[8,256]{1,0:T(8,128)S(1)} custom-call(s32[8,2]{1,0:T(8,128)S(1)} %copy.15.levels_ref, s32[8]{0:T(128)S(1)} %copy-done.4), custom_call_target="tpu_custom_call" | custom-call | bytes 2214000 | tf_op jit(solution)/shard_map/limits/pallas_call | solution.py:44
  23.9 2.6 %collective-permute-done.6.d_pair_ref = bf16[128,384]{1,0:T(8,128)(2,1)S(1)} collective-permute-done((bf16[128,384]{1,0:T(8,128)(2,1)S(1)}, bf16[128,384]{1,0:T(8,128)(2,1)S(1)}, u32[]{:S(2)}, u32[]{:S(2)}) %collective-permute-start.6) | collective-permute-done | bytes 98336 | tf_op jit(solution)/shard_map/ppermute | solution.py:35
  26.5 0.0 collective-permute-done.7.key3
  26.5 0.0 collective-permute-done.8.value3
  26.5 1.2 %forward.1 = (f32[16,256]{1,0:T(8,128)S(1)}, bf16[1920,256]{1,0:T(8,128)(2,1)S(1)}, f32[1920,256]{1,0:T(8,128)S(1)}) custom-call(s32[8,256]{1,0:T(8,128)S(1)} %limits.1.limits_ref, bf16[128,384]{1,0:T(8,128)(2,1)S(1)} %copy-done.2, bf16[128,384]{1,0:T(8,128)(2,1)S(1)} %collective-permute-done.2.q_pair_ref, bf16[128,384]{1,0:T(8,128)(2,1)S(1)} %dattn.1.d_own_ref, ...), custom_call_target="tpu_custom_call" | custom-call | bytes 5535000 | tf_op jit(solution)/shard_map/forward/pallas_call | solution.py:44
  27.7 0.4 attn.1
  28.1 0.0 copy-start
  28.2 2.2 %collective-permute-start.11 = (bf16[384,128]{1,0:T(8,128)(2,1)S(1)}, bf16[384,128]{1,0:T(8,128)(2,1)S(1)}, u32[]{:S(2)}, u32[]{:S(2)}) collective-permute-start(bf16[384,128]{1,0:T(8,128)(2,1)S(1)} %get-tuple-element.55), channel_id=1, source_target_pairs={{0,16},{4,20},{8,24},{12,28},{16,0},{20,4},{24,8},{28,12},{1,17},{... | collective-permute-start | bytes 294920 | tf_op jit(solution)/shard_map/ppermute | solution.py:35
  30.4 0.8 %collective-permute-start.9 = (f32[16,256]{1,0:T(8,128)S(1)}, f32[16,256]{1,0:T(8,128)S(1)}, u32[]{:S(2)}, u32[]{:S(2)}) collective-permute-start(f32[16,256]{1,0:T(8,128)S(1)} %get-tuple-element.47.stats_ref), channel_id=1, source_target_pairs={{0,16},{4,20},{8,24},{12,28},{16,0},{20,4},{24,8},{28,12},{1,17},{... | collective-permute-start | bytes 49160 | tf_op jit(solution)/shard_map/ppermute | solution.py:35
  31.2 4.8 %collective-permute-done.9.stats_pair_ref = f32[16,256]{1,0:T(8,128)S(1)} collective-permute-done((f32[16,256]{1,0:T(8,128)S(1)}, f32[16,256]{1,0:T(8,128)S(1)}, u32[]{:S(2)}, u32[]{:S(2)}) %collective-permute-start.9) | collective-permute-done | bytes 16416 | tf_op jit(solution)/shard_map/ppermute | solution.py:35
  35.9 1.1 %backward.1 = (f32[128,384]{1,0:T(8,128)S(1)}, bf16[128,384]{1,0:T(8,128)(2,1)S(1)}, f32[320,384]{1,0:T(8,128)S(1)}, bf16[320,384]{1,0:T(8,128)(2,1)S(1)}, bf16[...) custom-call(bf16[128,384]{1,0:T(8,128)(2,1)S(1)} %copy-done.2, ...), custom_call_target="tpu_custom_call" | custom-call | bytes 4059000 | tf_op jit(solution)/shard_map/backward/pallas_call | solution.py:44
  37.0 0.0 collective-permute-done.11.pair_ref
  37.1 0.6 %collective-permute-start.12 = (bf16[320,384]{1,0:T(8,128)(2,1)S(1)}, bf16[320,384]{1,0:T(8,128)(2,1)S(1)}, u32[]{:S(2)}, u32[]{:S(2)}) collective-permute-start(bf16[320,384]{1,0:T(8,128)(2,1)S(1)} %get-tuple-element.58), channel_id=1, source_target_pairs={{0,4},{4,0},{8,12},{12,8},{16,20},{20,16},{24,28},{28,24},{1,5},{5... | collective-permute-start | bytes 737288 | tf_op jit(solution)/shard_map/ppermute | solution.py:35
  37.6 1.2 %collective-permute-start.13 = (bf16[320,384]{1,0:T(8,128)(2,1)S(1)}, bf16[320,384]{1,0:T(8,128)(2,1)S(1)}, u32[]{:S(2)}, u32[]{:S(2)}) collective-permute-start(bf16[320,384]{1,0:T(8,128)(2,1)S(1)} %get-tuple-element.59), channel_id=1, source_target_pairs={{0,8},{4,12},{8,0},{12,4},{16,24},{20,28},{24,16},{28,20},{1,9},{5... | collective-permute-start | bytes 737288 | tf_op jit(solution)/shard_map/ppermute | solution.py:35
  38.8 1.6 %collective-permute-start.10 = (bf16[128,384]{1,0:T(8,128)(2,1)S(1)}, bf16[128,384]{1,0:T(8,128)(2,1)S(1)}, u32[]{:S(2)}, u32[]{:S(2)}) collective-permute-start(bf16[128,384]{1,0:T(8,128)(2,1)S(1)} %get-tuple-element.53), channel_id=1, source_target_pairs={{0,16},{4,20},{8,24},{12,28},{16,0},{20,4},{24,8},{28,12},{1,17},{... | collective-permute-start | bytes 294920 | tf_op jit(solution)/shard_map/ppermute | solution.py:35
  40.5 0.6 %project.1 = (f32[128,768]{1,0:T(8,128)S(1)}, bf16[128,768]{1,0:T(8,128)(2,1)S(1)}, bf16[128,768]{1,0:T(8,128)(2,1)S(1)}, bf16[128,768]{1,0:T(8,128)(2,1)S(1)}) custom-call(f32[384,128]{1,0:T(8,128)S(1)} %get-tuple-element.64.own_ref, bf16[384,128]{1,0:T(8,128)(2,1)S(1)} %collective-permute-done.11.pair_ref, f32[16,256]{1,0:T(8,128)S(1)} %get-tuple-element.47.stats_ref, ...), custom_call_target="tpu_custom_call" | custom-call | bytes 2214000 | tf_op jit(solution)/shard_map/project/pallas_call | solution.py:44
  41.1 0.1 collective-permute-start.16
  41.2 1.6 %collective-permute-start.17 = (bf16[128,768]{1,0:T(8,128)(2,1)S(1)}, bf16[128,768]{1,0:T(8,128)(2,1)S(1)}, u32[]{:S(2)}, u32[]{:S(2)}) collective-permute-start(bf16[128,768]{1,0:T(8,128)(2,1)S(1)} %get-tuple-element.68), channel_id=1, source_target_pairs={{0,2},{1,3},{2,0},{3,1},{4,6},{5,7},{6,4},{7,5},{8,10},{9,11},{10,... | collective-permute-start | bytes 589832 | tf_op jit(solution)/shard_map/ppermute | solution.py:35
  42.7 0.6 %collective-permute-done.12.got_k_ref = bf16[320,384]{1,0:T(8,128)(2,1)S(1)} collective-permute-done((bf16[320,384]{1,0:T(8,128)(2,1)S(1)}, bf16[320,384]{1,0:T(8,128)(2,1)S(1)}, u32[]{:S(2)}, u32[]{:S(2)}) %collective-permute-start.12) | collective-permute-done | bytes 245792 | tf_op jit(solution)/shard_map/ppermute | solution.py:35
  43.3 0.0 collective-permute-start.18
  43.3 1.4 %collective-permute-done.13.got_v_ref = bf16[320,384]{1,0:T(8,128)(2,1)S(1)} collective-permute-done((bf16[320,384]{1,0:T(8,128)(2,1)S(1)}, bf16[320,384]{1,0:T(8,128)(2,1)S(1)}, u32[]{:S(2)}, u32[]{:S(2)}) %collective-permute-start.13) | collective-permute-done | bytes 245792 | tf_op jit(solution)/shard_map/ppermute | solution.py:35
  44.8 0.4 collective-permute-start.14
  45.2 0.3 collective-permute-done.10.dq_pair_ref
  45.4 1.5 %collective-permute-start.15 = (bf16[160,384]{1,0:T(8,128)(2,1)S(1)}, bf16[160,384]{1,0:T(8,128)(2,1)S(1)}, u32[]{:S(2)}, u32[]{:S(2)}) collective-permute-start(bf16[160,384]{1,0:T(8,128)(2,1)S(1)} %get-tuple-element.63), channel_id=1, source_target_pairs={{0,4},{4,0},{8,12},{12,8},{16,20},{20,16},{24,28},{28,24},{1,5},{5... | collective-permute-start | bytes 368648 | tf_op jit(solution)/shard_map/ppermute | solution.py:35
  46.9 0.0 collective-permute-done.16.core_ref
  46.9 2.0 %collective-permute-done.17.near_ref = bf16[128,768]{1,0:T(8,128)(2,1)S(1)} collective-permute-done((bf16[128,768]{1,0:T(8,128)(2,1)S(1)}, bf16[128,768]{1,0:T(8,128)(2,1)S(1)}, u32[]{:S(2)}, u32[]{:S(2)}) %collective-permute-start.17) | collective-permute-done | bytes 196640 | tf_op jit(solution)/shard_map/ppermute | solution.py:35
  49.0 3.3 %collective-permute-done.18.far_ref = bf16[128,768]{1,0:T(8,128)(2,1)S(1)} collective-permute-done((bf16[128,768]{1,0:T(8,128)(2,1)S(1)}, bf16[128,768]{1,0:T(8,128)(2,1)S(1)}, u32[]{:S(2)}, u32[]{:S(2)}) %collective-permute-start.18) | collective-permute-done | bytes 196640 | tf_op jit(solution)/shard_map/ppermute | solution.py:35
  52.3 0.9 %finish.1 = (bf16[128,384]{1,0:T(8,128)(2,1)}, bf16[128,384]{1,0:T(8,128)(2,1)}, bf16[128,384]{1,0:T(8,128)(2,1)}, bf16[32,384]{1,0:T(8,128)(2,1)}, bf16[32,384]{1,0:T(8,128)(2,1)}, /*index=5*/bf16[128,768]{1,0:T(8,128)(2,1)}) custom-call(f32[128,384]{1,0:T(8,128)S(1)} %get-tuple-element.52.dq_ref, bf16[128,384]{1,0:T(8,128)(2,1)S(1)} %collective-permute-done.10.dq_pair_ref, ...), custom_call_target="tpu_custom_call" | custom-call | bytes 3321000 | tf_op jit(solution)/shard_map/finish/pallas_call | solution.py:44
  (13 shorter events, 0.1 us)
Async XLA Ops:
  0.6 25.9 %copy-start.2 = (bf16[128,384]{1,0:T(8,128)(2,1)S(1)}, bf16[128,384]{1,0:T(8,128)(2,1)}, u32[]{:S(2)}) copy-start(bf16[128,384]{1,0:T(8,128)(2,1)} %q_own_ref.3) | copy-start | bytes 294916
  0.6 22.5 %copy-start.5 = (s32[8,2]{0,1:T(2,128)S(1)}, s32[8,2]{0,1:T(2,128)}, u32[]{:S(2)}) copy-start(s32[8,2]{0,1:T(2,128)} %param.14) | copy-start | bytes 196
  0.7 22.6 %copy-start.4 = (s32[8]{0:T(128)S(1)}, s32[8]{0:T(128)}, u32[]{:S(2)}) copy-start(s32[8]{0:T(128)} %counts_ref.1) | copy-start | bytes 100
  0.7 8.1 %collective-permute-start.4 = (bf16[128,768]{1,0:T(8,128)(2,1)}, bf16[128,768]{1,0:T(8,128)(2,1)S(1)}, u32[]{:S(2)}, u32[]{:S(2)}) collective-permute-start(bf16[128,768]{1,0:T(8,128)(2,1)} %own_hbm.1), channel_id=1, source_target_pairs={{0,2},{1,3},{2,0},{3,1},{4,6},{5,7},{6,4},{7,5},{8,10},{9,11},{10,... | collective-permute-start | bytes 589832 | tf_op jit(solution)/shard_map/ppermute | solution.py:35
  5.3 21.2 %copy-start.1 = (bf16[320,384]{1,0:T(8,128)(2,1)S(1)}, bf16[320,384]{1,0:T(8,128)(2,1)}, u32[]{:S(2)}) copy-start(bf16[320,384]{1,0:T(8,128)(2,1)} %load.1.kv0) | copy-start | bytes 737284
  5.4 12.1 %collective-permute-start.1 = (bf16[320,384]{1,0:T(8,128)(2,1)}, bf16[320,384]{1,0:T(8,128)(2,1)S(1)}, u32[]{:S(2)}, u32[]{:S(2)}) collective-permute-start(bf16[320,384]{1,0:T(8,128)(2,1)} %load.1.kv0), channel_id=1, source_target_pairs={{0,8},{4,12},{8,0},{12,4},{16,24},{20,28},{24,16},{28,20},{1,9},{5... | collective-permute-start | bytes 737288 | tf_op jit(solution)/shard_map/ppermute | solution.py:35
  7.0 10.4 %collective-permute-start = (bf16[320,384]{1,0:T(8,128)(2,1)}, bf16[320,384]{1,0:T(8,128)(2,1)S(1)}, u32[]{:S(2)}, u32[]{:S(2)}) collective-permute-start(bf16[320,384]{1,0:T(8,128)(2,1)} %load.1.kv0), channel_id=1, source_target_pairs={{0,4},{4,0},{8,12},{12,8},{16,20},{20,16},{24,28},{28,24},{1,5},{5... | collective-permute-start | bytes 737288 | tf_op jit(solution)/shard_map/ppermute | solution.py:35
  8.5 3.1 %collective-permute-start.3 = (bf16[128,768]{1,0:T(8,128)(2,1)}, bf16[128,768]{1,0:T(8,128)(2,1)S(1)}, u32[]{:S(2)}, u32[]{:S(2)}) collective-permute-start(bf16[128,768]{1,0:T(8,128)(2,1)} %own_hbm.1), channel_id=1, source_target_pairs={{0,1},{1,0},{2,3},{3,2},{4,5},{5,4},{6,7},{7,6},{8,9},{9,8},{10,11... | collective-permute-start | bytes 589832 | tf_op jit(solution)/shard_map/ppermute | solution.py:35
  8.8 2.8 %collective-permute-start.5 = (bf16[128,768]{1,0:T(8,128)(2,1)S(1)}, bf16[128,768]{1,0:T(8,128)(2,1)S(1)}, u32[]{:S(2)}, u32[]{:S(2)}) collective-permute-start(bf16[128,768]{1,0:T(8,128)(2,1)S(1)} %collective-permute-done.4.near_ref), channel_id=1, source_target_pairs={{0,1},{1,0},{2,3},{3,2},{4,5},{5,4},{6,7},{7,6},{8,9},{9,8},{10,11... | collective-permute-start | bytes 589832 | tf_op jit(solution)/shard_map/ppermute | solution.py:35
  9.0 8.4 %collective-permute-start.2 = (bf16[128,384]{1,0:T(8,128)(2,1)}, bf16[128,384]{1,0:T(8,128)(2,1)S(1)}, u32[]{:S(2)}, u32[]{:S(2)}) collective-permute-start(bf16[128,384]{1,0:T(8,128)(2,1)} %q_own_ref.3), channel_id=1, source_target_pairs={{0,16},{4,20},{8,24},{12,28},{16,0},{20,4},{24,8},{28,12},{1,17},{... | collective-permute-start | bytes 294920 | tf_op jit(solution)/shard_map/ppermute | solution.py:35
  11.6 0.9 %copy-start.3 = (bf16[128,768]{1,0:T(8,128)(2,1)S(1)}, bf16[128,768]{1,0:T(8,128)(2,1)}, u32[]{:S(2)}) copy-start(bf16[128,768]{1,0:T(8,128)(2,1)} %own_hbm.1) | copy-start | bytes 589828
  17.4 9.0 %collective-permute-start.7 = (bf16[160,384]{1,0:T(8,128)(2,1)S(1)}, bf16[160,384]{1,0:T(8,128)(2,1)S(1)}, u32[]{:S(2)}, u32[]{:S(2)}) collective-permute-start(bf16[160,384]{1,0:T(8,128)(2,1)S(1)} %get-tuple-element.45), channel_id=1, source_target_pairs={{0,4},{4,0},{8,12},{12,8},{16,20},{20,16},{24,28},{28,24},{1,5},{5... | collective-permute-start | bytes 368648 | tf_op jit(solution)/shard_map/ppermute | solution.py:35
  19.1 7.4 %collective-permute-start.8 = (bf16[160,384]{1,0:T(8,128)(2,1)S(1)}, bf16[160,384]{1,0:T(8,128)(2,1)S(1)}, u32[]{:S(2)}, u32[]{:S(2)}) collective-permute-start(bf16[160,384]{1,0:T(8,128)(2,1)S(1)} %get-tuple-element.46), channel_id=1, source_target_pairs={{0,8},{4,12},{8,0},{12,4},{16,24},{20,28},{24,16},{28,20},{1,9},{5... | collective-permute-start | bytes 368648 | tf_op jit(solution)/shard_map/ppermute | solution.py:35
  19.9 6.6 %collective-permute-start.6 = (bf16[128,384]{1,0:T(8,128)(2,1)S(1)}, bf16[128,384]{1,0:T(8,128)(2,1)S(1)}, u32[]{:S(2)}, u32[]{:S(2)}) collective-permute-start(bf16[128,384]{1,0:T(8,128)(2,1)S(1)} %dattn.1.d_own_ref), channel_id=1, source_target_pairs={{0,16},{4,20},{8,24},{12,28},{16,0},{20,4},{24,8},{28,12},{1,17},{... | collective-permute-start | bytes 294920 | tf_op jit(solution)/shard_map/ppermute | solution.py:35
  28.1 12.3 %copy-start = (bf16[384,3072]{1,0:T(8,128)(2,1)S(1)}, bf16[384,3072]{1,0:T(8,128)(2,1)}, u32[]{:S(2)}) copy-start(bf16[384,3072]{1,0:T(8,128)(2,1)} %w_ref.1) | copy-start | bytes 7077892
  28.2 8.9 %collective-permute-start.11 = (bf16[384,128]{1,0:T(8,128)(2,1)S(1)}, bf16[384,128]{1,0:T(8,128)(2,1)S(1)}, u32[]{:S(2)}, u32[]{:S(2)}) collective-permute-start(bf16[384,128]{1,0:T(8,128)(2,1)S(1)} %get-tuple-element.55), channel_id=1, source_target_pairs={{0,16},{4,20},{8,24},{12,28},{16,0},{20,4},{24,8},{28,12},{1,17},{... | collective-permute-start | bytes 294920 | tf_op jit(solution)/shard_map/ppermute | solution.py:35
  30.4 5.5 %collective-permute-start.9 = (f32[16,256]{1,0:T(8,128)S(1)}, f32[16,256]{1,0:T(8,128)S(1)}, u32[]{:S(2)}, u32[]{:S(2)}) collective-permute-start(f32[16,256]{1,0:T(8,128)S(1)} %get-tuple-element.47.stats_ref), channel_id=1, source_target_pairs={{0,16},{4,20},{8,24},{12,28},{16,0},{20,4},{24,8},{28,12},{1,17},{... | collective-permute-start | bytes 49160 | tf_op jit(solution)/shard_map/ppermute | solution.py:35
  37.1 6.3 %collective-permute-start.12 = (bf16[320,384]{1,0:T(8,128)(2,1)S(1)}, bf16[320,384]{1,0:T(8,128)(2,1)S(1)}, u32[]{:S(2)}, u32[]{:S(2)}) collective-permute-start(bf16[320,384]{1,0:T(8,128)(2,1)S(1)} %get-tuple-element.58), channel_id=1, source_target_pairs={{0,4},{4,0},{8,12},{12,8},{16,20},{20,16},{24,28},{28,24},{1,5},{5... | collective-permute-start | bytes 737288 | tf_op jit(solution)/shard_map/ppermute | solution.py:35
  37.6 7.1 %collective-permute-start.13 = (bf16[320,384]{1,0:T(8,128)(2,1)S(1)}, bf16[320,384]{1,0:T(8,128)(2,1)S(1)}, u32[]{:S(2)}, u32[]{:S(2)}) collective-permute-start(bf16[320,384]{1,0:T(8,128)(2,1)S(1)} %get-tuple-element.59), channel_id=1, source_target_pairs={{0,8},{4,12},{8,0},{12,4},{16,24},{20,28},{24,16},{28,20},{1,9},{5... | collective-permute-start | bytes 737288 | tf_op jit(solution)/shard_map/ppermute | solution.py:35
  38.8 6.6 %collective-permute-start.10 = (bf16[128,384]{1,0:T(8,128)(2,1)S(1)}, bf16[128,384]{1,0:T(8,128)(2,1)S(1)}, u32[]{:S(2)}, u32[]{:S(2)}) collective-permute-start(bf16[128,384]{1,0:T(8,128)(2,1)S(1)} %get-tuple-element.53), channel_id=1, source_target_pairs={{0,16},{4,20},{8,24},{12,28},{16,0},{20,4},{24,8},{28,12},{1,17},{... | collective-permute-start | bytes 294920 | tf_op jit(solution)/shard_map/ppermute | solution.py:35
  41.1 5.8 %collective-permute-start.16 = (bf16[128,768]{1,0:T(8,128)(2,1)S(1)}, bf16[128,768]{1,0:T(8,128)(2,1)S(1)}, u32[]{:S(2)}, u32[]{:S(2)}) collective-permute-start(bf16[128,768]{1,0:T(8,128)(2,1)S(1)} %get-tuple-element.67), channel_id=1, source_target_pairs={{0,1},{1,0},{2,3},{3,2},{4,5},{5,4},{6,7},{7,6},{8,9},{9,8},{10,11... | collective-permute-start | bytes 589832 | tf_op jit(solution)/shard_map/ppermute | solution.py:35
  41.2 7.8 %collective-permute-start.17 = (bf16[128,768]{1,0:T(8,128)(2,1)S(1)}, bf16[128,768]{1,0:T(8,128)(2,1)S(1)}, u32[]{:S(2)}, u32[]{:S(2)}) collective-permute-start(bf16[128,768]{1,0:T(8,128)(2,1)S(1)} %get-tuple-element.68), channel_id=1, source_target_pairs={{0,2},{1,3},{2,0},{3,1},{4,6},{5,7},{6,4},{7,5},{8,10},{9,11},{10,... | collective-permute-start | bytes 589832 | tf_op jit(solution)/shard_map/ppermute | solution.py:35
  43.3 8.9 %collective-permute-start.18 = (bf16[128,768]{1,0:T(8,128)(2,1)S(1)}, bf16[128,768]{1,0:T(8,128)(2,1)S(1)}, u32[]{:S(2)}, u32[]{:S(2)}) collective-permute-start(bf16[128,768]{1,0:T(8,128)(2,1)S(1)} %get-tuple-element.69), channel_id=1, source_target_pairs={{0,3},{1,2},{2,1},{3,0},{4,7},{5,6},{6,5},{7,4},{8,11},{9,10},{10,... | collective-permute-start | bytes 589832 | tf_op jit(solution)/shard_map/ppermute | solution.py:35
  44.8 7.5 %collective-permute-start.14 = (bf16[160,384]{1,0:T(8,128)(2,1)S(1)}, bf16[160,384]{1,0:T(8,128)(2,1)S(1)}, u32[]{:S(2)}, u32[]{:S(2)}) collective-permute-start(bf16[160,384]{1,0:T(8,128)(2,1)S(1)} %get-tuple-element.62), channel_id=1, source_target_pairs={{0,8},{4,12},{8,0},{12,4},{16,24},{20,28},{24,16},{28,20},{1,9},{5... | collective-permute-start | bytes 368648 | tf_op jit(solution)/shard_map/ppermute | solution.py:35
  45.4 6.9 %collective-permute-start.15 = (bf16[160,384]{1,0:T(8,128)(2,1)S(1)}, bf16[160,384]{1,0:T(8,128)(2,1)S(1)}, u32[]{:S(2)}, u32[]{:S(2)}) collective-permute-start(bf16[160,384]{1,0:T(8,128)(2,1)S(1)} %get-tuple-element.63), channel_id=1, source_target_pairs={{0,4},{4,0},{8,12},{12,8},{16,20},{20,16},{24,28},{28,24},{1,5},{5... | collective-permute-start | bytes 368648 | tf_op jit(solution)/shard_map/ppermute | solution.py:35

commit v8 on v7

--- a/solution.py
+++ b/solution.py
@@ -162,17 +162,15 @@
     )
 
 
-def forward_kernel(
-    limits_ref, q_own_ref, q_pair_ref, d_own_ref, d_pair_ref, kv0, kv1, kv2, key3, value3,
-    stats_ref, probs_ref, dprobs_ref,
+def scores_kernel(
+    limits_ref, q_own_ref, q_pair_ref, kv0, kv1, kv2, key3, value3, lse_ref, probs_ref
 ):
     rows = q_own_ref.shape[0]
     keys = key3.shape[0]
     blocks = square_blocks(kv0, kv1, kv2, key3, value3)
-    stats_ref[...] = jnp.zeros_like(stats_ref)
+    lse_ref[...] = jnp.zeros_like(lse_ref)
     for head in range(q_own_ref.shape[1] // HDIM):
         query = both_rows(q_own_ref, q_pair_ref, head)
-        dattn = both_rows(d_own_ref, d_pair_ref, head)
         scores = []
         for step, (key_ref, _) in enumerate(blocks):
             block = contract(head_slice(key_ref[...], head), query, 1, 1) * SCALE
@@ -185,16 +183,28 @@
         weights = [jnp.exp(block - top) for block in scores]
         total = sum(jnp.sum(block, axis=0, keepdims=True) for block in weights)
         inverse = 1.0 / total
+        for step, block in enumerate(weights):
+            begin = (head * SQUARE + step) * keys
+            probs_ref[begin : begin + keys] = (block * inverse).astype(BF16)
+        lse_ref[head : head + 1] = top + jnp.log(total)
+
+
+def delta_kernel(
+    lse_ref, probs_ref, d_own_ref, d_pair_ref, kv0, kv1, kv2, key3, value3, stats_ref, dprobs_ref
+):
+    keys = key3.shape[0]
+    blocks = square_blocks(kv0, kv1, kv2, key3, value3)
+    stats_ref[...] = jnp.zeros_like(stats_ref)
+    stats_ref[: lse_ref.shape[0]] = lse_ref[...]
+    for head in range(d_own_ref.shape[1] // HDIM):
+        dattn = both_rows(d_own_ref, d_pair_ref, head)
         delta = None
         for step, (_, value_ref) in enumerate(blocks):
-            probs = weights[step] * inverse
+            part = pl.ds((head * SQUARE + step) * keys, keys)
             dprobs = contract(head_slice(value_ref[...], head), dattn, 1, 1)
-            part = jnp.sum(probs * dprobs, axis=0, keepdims=True)
-            delta = part if delta is None else delta + part
-            begin = (head * SQUARE + step) * keys
-            probs_ref[begin : begin + keys] = probs.astype(BF16)
-            dprobs_ref[begin : begin + keys] = dprobs
-        stats_ref[head : head + 1] = top + jnp.log(total)
+            dprobs_ref[part] = dprobs
+            share = jnp.sum(probs_ref[part].astype(F32) * dprobs, axis=0, keepdims=True)
+            delta = share if delta is None else delta + share
         stats_ref[8 + head : 9 + head] = delta
 
 
@@ -283,8 +293,8 @@
 
 
 def finish_kernel(
-    dq_ref, dq_pair_ref, dkv_ref, got_k_ref, got_v_ref, rest_k_ref, rest_v_ref,
-    keep_ref, core_ref, near_ref, far_ref,
+    keep_ref, near_ref, far_ref, dq_ref, dq_pair_ref, core_ref,
+    dkv_ref, got_k_ref, got_v_ref, rest_k_ref, rest_v_ref,
     q_out, k_out, v_out, hk_out, hv_out, out_ref,
 ):
     rows, capacity = k_out.shape[0], hk_out.shape[0]
@@ -333,18 +343,13 @@
         (frame_levels, frame_counts),
         tables=2,
     )[0]
-    stats, probs, dprobs = local_call(
-        forward_kernel,
-        "forward",
-        1.5,
-        [
-            shape((16, 2 * rows), F32),
-            shape((heads * SQUARE * keys, 2 * rows), BF16),
-            shape((heads * SQUARE * keys, 2 * rows), F32),
-        ],
-        (limits, sec_q, q_pair, d_own, d_pair, *kvs),
-    )
-    stats_pair = swap(stats, "ctx", PAIR)
+    lse, probs = local_call(
+        scores_kernel,
+        "scores",
+        0.9,
+        [shape((8, 2 * rows), F32), shape((heads * SQUARE * keys, 2 * rows), BF16)],
+        (limits, sec_q, q_pair, *kvs),
+    )
     attn_own, attn_pair = local_call(
         attn_kernel,
         "attn",
@@ -352,7 +357,15 @@
         [shape((width, rows), F32), shape((width, rows), BF16)],
         (*kvs, probs),
     )
-    attn_own, probs = lax.optimization_barrier((attn_own, probs))
+    lse, attn_own = lax.optimization_barrier((lse, attn_own))
+    stats, dprobs = local_call(
+        delta_kernel,
+        "delta",
+        0.7,
+        [shape((16, 2 * rows), F32), shape((heads * SQUARE * keys, 2 * rows), F32)],
+        (lse, probs, d_own, d_pair, *kvs),
+    )
+    stats_pair = swap(stats, "ctx", PAIR)
     dq_own, dq_pair, dkv_own, send_k, send_v, near_k, near_v = local_call(
         backward_kernel,
         "backward",
@@ -366,7 +379,6 @@
     attn_got, send_k, send_v = lax.optimization_barrier((attn_got, send_k, send_v))
     got_k = swap(send_k, "ctx", 1)
     got_v = swap(send_v, "ctx", 2)
-    dq_got = swap(dq_pair, "ctx", PAIR)
     rest_k, rest_v = local_call(
         pass_on_kernel,
         "pass_on",
@@ -383,7 +395,9 @@
         [shape((rows, share), F32)] + [shape((rows, share), BF16)] * 3,
         (attn_own, attn_got, stats, stats_pair, w_out),
     )
-    out_got = [swap(out_send[step - 1], "head", step) for step in (1, 2, 3)]
+    out_near, out_far = (swap(out_send[step - 1], "head", step) for step in (2, 3))
+    dq_got = swap(dq_pair, "ctx", PAIR)
+    out_core = swap(out_send[0], "head", 1)
     grad_q, grad_k, grad_v, grad_hk, grad_hv, out = local_call(
         finish_kernel,
         "finish",
@@ -391,7 +405,10 @@
         [shape((rows, width), BF16)] * 3
         + [shape((capacity, width), BF16)] * 2
         + [shape((rows, share), BF16)],
-        (dq_own, dq_got, dkv_own, got_k, got_v, rest_k, rest_v, out_keep, *out_got),
+        (
+            out_keep, out_near, out_far, dq_own, dq_got, out_core,
+            dkv_own, got_k, got_v, rest_k, rest_v,
+        ),
     )
     return out, grad_q, grad_k, grad_v, grad_hk, grad_hv
 

time: 53.4 us -> 50.5 us (0.946)
  waiting for transfers between devices: 17.3 us -> 12.9 us
  starting transfers between devices: 24.6 us -> 26 us
    ppermute x19, waiting for transfers between devices: 17.3 us -> 12.9 us  [swap(): return lax.ppermute(block, axis, [(i, i ^ bit) for i in range(count)])]
    ppermute x19, starting transfers between devices: 24.6 us -> 26 us  [swap(): return lax.ppermute(block, axis, [(i, i ^ bit) for i in range(count)])]
    pallas_call x8 -> x9, Pallas kernels: 4.97 us -> 5.2 us  [local_call(): pl.pallas_call(body, name=name, out_shape=out_shapes, in_specs=[pl.BlockS...]
  transfers between devices with their start and end apart: 19 -> 19, of which waited for: 9 -> 10; matrix products, arithmetic and copies ran while one was open for 0% -> 0% of each run, Pallas kernels for 13% -> 17%
where the time goes in v8:
time: 50.5 us; the launch traced here: 50.3 us
  starting transfers between devices  26 us (51%)
  waiting for transfers between devices  12.9 us (26%)
  Pallas kernels  9.61 us (19%)
  local copies, waits for them, and re-layouts  1.03 us (2%)
  between operations  0.78 us (2%)
    ppermute x19, starting transfers between devices, swap(): return lax.ppermute(block, axis, [(i, i ^ bit) for i in range(count)])  26 us
    ppermute x19, waiting for transfers between devices, swap(): return lax.ppermute(block, axis, [(i, i ^ bit) for i in range(count)])  12.9 us
    pallas_call x9, Pallas kernels, local_call(): pl.pallas_call(body, name=name, out_shape=out_shapes, in_specs=[pl.BlockS...  5.2 us
    pallas_call x1, Pallas kernels, dattn_call(): pl.pallas_call(dattn_kernel, name='dattn', out_shape=jax.ShapeDtypeStruct...  2.75 us
    pallas_call x1, Pallas kernels, load_keys(): pl.pallas_call(load_kernel, name='load', out_shape=jax.ShapeDtypeStruct((...  1.66 us
    unnamed x13, local copies, waits for them, and re-layouts  1.03 us
  transfers between devices with their start and end apart: 19, of which 10 were waited for; matrix products, arithmetic and copies ran while one was open for 0% of the time, Pallas kernels for 17%

profile of v8, /device:TPU:0, one launch (start us, length us, event | category | flops | bytes accessed | tf_op | source)
XLA Modules:
  0.0 50.3 jit_solution(1086689494316695389)
XLA Ops:
  0.6 0.0 copy-start.2
  0.7 3.0 %collective-permute-start.4 = (bf16[128,768]{1,0:T(8,128)(2,1)}, bf16[128,768]{1,0:T(8,128)(2,1)S(1)}, u32[]{:S(2)}, u32[]{:S(2)}) collective-permute-start(bf16[128,768]{1,0:T(8,128)(2,1)} %own_hbm.1), channel_id=1, source_target_pairs={{0,2},{1,3},{2,0},{3,1},{4,6},{5,7},{6,4},{7,5},{8,10},{9,11},{10,... | collective-permute-start | bytes 589832 | tf_op jit(solution)/shard_map/ppermute | solution.py:35
  3.7 1.7 %load.1.kv0 = bf16[320,384]{1,0:T(8,128)(2,1)} custom-call(bf16[128,384]{1,0:T(8,128)(2,1)} %k_ref.1, bf16[32,384]{1,0:T(8,128)(2,1)} %hk_ref.1, bf16[128,384]{1,0:T(8,128)(2,1)} %v_ref.1, bf16[32,384]{1,0:T(8,128)(2,1)} %hv_ref.1), custom_call_target="tpu_custom_call" | custom-call | bytes 5904000 | tf_op jit(solution)/shard_map/load/pallas_call | solution.py:74
  5.3 1.6 %collective-permute-start.1 = (bf16[320,384]{1,0:T(8,128)(2,1)}, bf16[320,384]{1,0:T(8,128)(2,1)S(1)}, u32[]{:S(2)}, u32[]{:S(2)}) collective-permute-start(bf16[320,384]{1,0:T(8,128)(2,1)} %load.1.kv0), channel_id=1, source_target_pairs={{0,8},{4,12},{8,0},{12,4},{16,24},{20,28},{24,16},{28,20},{1,9},{5... | collective-permute-start | bytes 737288 | tf_op jit(solution)/shard_map/ppermute | solution.py:35
  7.0 1.5 %collective-permute-start = (bf16[320,384]{1,0:T(8,128)(2,1)}, bf16[320,384]{1,0:T(8,128)(2,1)S(1)}, u32[]{:S(2)}, u32[]{:S(2)}) collective-permute-start(bf16[320,384]{1,0:T(8,128)(2,1)} %load.1.kv0), channel_id=1, source_target_pairs={{0,4},{4,0},{8,12},{12,8},{16,20},{20,16},{24,28},{28,24},{1,5},{5... | collective-permute-start | bytes 737288 | tf_op jit(solution)/shard_map/ppermute | solution.py:35
  8.5 0.0 collective-permute-start.3
  8.5 0.3 collective-permute-done.4.near_ref
  8.8 0.2 collective-permute-start.5
  9.0 2.6 %collective-permute-start.2 = (bf16[128,384]{1,0:T(8,128)(2,1)}, bf16[128,384]{1,0:T(8,128)(2,1)S(1)}, u32[]{:S(2)}, u32[]{:S(2)}) collective-permute-start(bf16[128,384]{1,0:T(8,128)(2,1)} %q_own_ref.3), channel_id=1, source_target_pairs={{0,16},{4,20},{8,24},{12,28},{16,0},{20,4},{24,8},{28,12},{1,17},{... | collective-permute-start | bytes 294920 | tf_op jit(solution)/shard_map/ppermute | solution.py:35
  11.6 0.0 collective-permute-done.3.core_ref
  11.6 0.0 collective-permute-done.5.far_ref
  11.6 0.9 %copy-done.3 = bf16[128,768]{1,0:T(8,128)(2,1)S(1)} copy-done((bf16[128,768]{1,0:T(8,128)(2,1)S(1)}, bf16[128,768]{1,0:T(8,128)(2,1)}, u32[]{:S(2)}) %copy-start.3) | copy-done | bytes 196632
  12.6 2.8 %dattn.1.d_own_ref = bf16[128,384]{1,0:T(8,128)(2,1)S(1)} custom-call(bf16[128,768]{1,0:T(8,128)(2,1)S(1)} %copy-done.3, bf16[384,3072]{1,0:T(8,128)(2,1)} %w_ref.1, bf16[128,768]{1,0:T(8,128)(2,1)S(1)} %collective-permute-done.3.core_ref, bf16[128,768]{1,0:T(8,128)(2,1)S(1)} %collective-permute-done.4.near_ref, ...), custom_call_target="tpu_custom_call" | custom-call | bytes 5535000 | tf_op jit(solution)/shard_map/dattn/pallas_call | solution.py:143
  15.3 2.1 %collective-permute-done.2.q_pair_ref = bf16[128,384]{1,0:T(8,128)(2,1)S(1)} collective-permute-done((bf16[128,384]{1,0:T(8,128)(2,1)}, bf16[128,384]{1,0:T(8,128)(2,1)S(1)}, u32[]{:S(2)}, u32[]{:S(2)}) %collective-permute-start.2) | collective-permute-done | bytes 98336 | tf_op jit(solution)/shard_map/ppermute | solution.py:35
  17.4 0.0 collective-permute-done.1.kv2
  17.4 1.6 %collective-permute-start.6 = (bf16[160,384]{1,0:T(8,128)(2,1)S(1)}, bf16[160,384]{1,0:T(8,128)(2,1)S(1)}, u32[]{:S(2)}, u32[]{:S(2)}) collective-permute-start(bf16[160,384]{1,0:T(8,128)(2,1)S(1)} %get-tuple-element.45), channel_id=1, source_target_pairs={{0,4},{4,0},{8,12},{12,8},{16,20},{20,16},{24,28},{28,24},{1,5},{5... | collective-permute-start | bytes 368648 | tf_op jit(solution)/shard_map/ppermute | solution.py:35
  19.1 0.8 %collective-permute-start.7 = (bf16[160,384]{1,0:T(8,128)(2,1)S(1)}, bf16[160,384]{1,0:T(8,128)(2,1)S(1)}, u32[]{:S(2)}, u32[]{:S(2)}) collective-permute-start(bf16[160,384]{1,0:T(8,128)(2,1)S(1)} %get-tuple-element.46), channel_id=1, source_target_pairs={{0,8},{4,12},{8,0},{12,4},{16,24},{20,28},{24,16},{28,20},{1,9},{5... | collective-permute-start | bytes 368648 | tf_op jit(solution)/shard_map/ppermute | solution.py:35
  19.9 3.3 %collective-permute-start.9 = (bf16[128,384]{1,0:T(8,128)(2,1)S(1)}, bf16[128,384]{1,0:T(8,128)(2,1)S(1)}, u32[]{:S(2)}, u32[]{:S(2)}) collective-permute-start(bf16[128,384]{1,0:T(8,128)(2,1)S(1)} %dattn.1.d_own_ref), channel_id=1, source_target_pairs={{0,16},{4,20},{8,24},{12,28},{16,0},{20,4},{24,8},{28,12},{1,17},{... | collective-permute-start | bytes 294920 | tf_op jit(solution)/shard_map/ppermute | solution.py:35
  23.1 0.1 copy.15.levels_ref
  23.2 0.6 %limits.1.limits_ref = s32[8,256]{1,0:T(8,128)S(1)} custom-call(s32[8,2]{1,0:T(8,128)S(1)} %copy.15.levels_ref, s32[8]{0:T(128)S(1)} %copy-done.4), custom_call_target="tpu_custom_call" | custom-call | bytes 2214000 | tf_op jit(solution)/shard_map/limits/pallas_call | solution.py:44
  23.9 0.0 collective-permute-done.6.key3
  23.9 1.8 %collective-permute-done.7.value3 = bf16[160,384]{1,0:T(8,128)(2,1)S(1)} collective-permute-done((bf16[160,384]{1,0:T(8,128)(2,1)S(1)}, bf16[160,384]{1,0:T(8,128)(2,1)S(1)}, u32[]{:S(2)}, u32[]{:S(2)}) %collective-permute-start.7) | collective-permute-done | bytes 122912 | tf_op jit(solution)/shard_map/ppermute | solution.py:35
  25.6 1.0 %scores.1 = (f32[8,256]{1,0:T(8,128)S(1)}, bf16[1920,256]{1,0:T(8,128)(2,1)S(1)}) custom-call(s32[8,256]{1,0:T(8,128)S(1)} %limits.1.limits_ref, bf16[128,384]{1,0:T(8,128)(2,1)S(1)} %copy-done.2, bf16[128,384]{1,0:T(8,128)(2,1)S(1)} %collective-permute-done.2.q_pair_ref, bf16[320,384]{1,0:T(8,128)(2,1)S(1)} %copy-done.1, ...), custom_call_target="tpu_custom_call" | custom-call | bytes 3321000 | tf_op jit(solution)/shard_map/scores/pallas_call | solution.py:44
  26.7 0.4 attn.1
  27.1 1.7 %collective-permute-start.8 = (bf16[384,128]{1,0:T(8,128)(2,1)S(1)}, bf16[384,128]{1,0:T(8,128)(2,1)S(1)}, u32[]{:S(2)}, u32[]{:S(2)}) collective-permute-start(bf16[384,128]{1,0:T(8,128)(2,1)S(1)} %get-tuple-element.51), channel_id=1, source_target_pairs={{0,16},{4,20},{8,24},{12,28},{16,0},{20,4},{24,8},{28,12},{1,17},{... | collective-permute-start | bytes 294920 | tf_op jit(solution)/shard_map/ppermute | solution.py:35
  28.8 0.4 delta.1
  29.2 0.0 copy-start
  29.3 1.4 %collective-permute-start.10 = (f32[16,256]{1,0:T(8,128)S(1)}, f32[16,256]{1,0:T(8,128)S(1)}, u32[]{:S(2)}, u32[]{:S(2)}) collective-permute-start(f32[16,256]{1,0:T(8,128)S(1)} %get-tuple-element.54.stats_ref), channel_id=1, source_target_pairs={{0,16},{4,20},{8,24},{12,28},{16,0},{20,4},{24,8},{28,12},{1,17},{... | collective-permute-start | bytes 49160 | tf_op jit(solution)/shard_map/ppermute | solution.py:35
  30.6 3.5 %collective-permute-done.10.stats_pair_ref = f32[16,256]{1,0:T(8,128)S(1)} collective-permute-done((f32[16,256]{1,0:T(8,128)S(1)}, f32[16,256]{1,0:T(8,128)S(1)}, u32[]{:S(2)}, u32[]{:S(2)}) %collective-permute-start.10) | collective-permute-done | bytes 16416 | tf_op jit(solution)/shard_map/ppermute | solution.py:35
  34.1 1.1 %backward.1 = (f32[128,384]{1,0:T(8,128)S(1)}, bf16[128,384]{1,0:T(8,128)(2,1)S(1)}, f32[320,384]{1,0:T(8,128)S(1)}, bf16[320,384]{1,0:T(8,128)(2,1)S(1)}, bf16[...) custom-call(bf16[128,384]{1,0:T(8,128)(2,1)S(1)} %copy-done.2, ...), custom_call_target="tpu_custom_call" | custom-call | bytes 4059000 | tf_op jit(solution)/shard_map/backward/pallas_call | solution.py:44
  35.2 0.4 collective-permute-start.15
  35.7 2.3 %collective-permute-start.16 = (bf16[320,384]{1,0:T(8,128)(2,1)S(1)}, bf16[320,384]{1,0:T(8,128)(2,1)S(1)}, u32[]{:S(2)}, u32[]{:S(2)}) collective-permute-start(bf16[320,384]{1,0:T(8,128)(2,1)S(1)} %get-tuple-element.67), channel_id=1, source_target_pairs={{0,8},{4,12},{8,0},{12,4},{16,24},{20,28},{24,16},{28,20},{1,9},{5... | collective-permute-start | bytes 737288 | tf_op jit(solution)/shard_map/ppermute | solution.py:35
  38.0 0.9 %collective-permute-start.13 = (bf16[128,384]{1,0:T(8,128)(2,1)S(1)}, bf16[128,384]{1,0:T(8,128)(2,1)S(1)}, u32[]{:S(2)}, u32[]{:S(2)}) collective-permute-start(bf16[128,384]{1,0:T(8,128)(2,1)S(1)} %get-tuple-element.63), channel_id=1, source_target_pairs={{0,16},{4,20},{8,24},{12,28},{16,0},{20,4},{24,8},{28,12},{1,17},{... | collective-permute-start | bytes 294920 | tf_op jit(solution)/shard_map/ppermute | solution.py:35
  38.9 0.6 %project.1 = (f32[128,768]{1,0:T(8,128)S(1)}, bf16[128,768]{1,0:T(8,128)(2,1)S(1)}, bf16[128,768]{1,0:T(8,128)(2,1)S(1)}, bf16[128,768]{1,0:T(8,128)(2,1)S(1)}) custom-call(f32[384,128]{1,0:T(8,128)S(1)} %get-tuple-element.50.own_ref, bf16[384,128]{1,0:T(8,128)(2,1)S(1)} %collective-permute-done.8.pair_ref, f32[16,256]{1,0:T(8,128)S(1)} %get-tuple-element.54.stats_ref, ...), custom_call_target="tpu_custom_call" | custom-call | bytes 2214000 | tf_op jit(solution)/shard_map/project/pallas_call | solution.py:44
  39.5 1.6 %collective-permute-start.11 = (bf16[128,768]{1,0:T(8,128)(2,1)S(1)}, bf16[128,768]{1,0:T(8,128)(2,1)S(1)}, u32[]{:S(2)}, u32[]{:S(2)}) collective-permute-start(bf16[128,768]{1,0:T(8,128)(2,1)S(1)} %get-tuple-element.60), channel_id=1, source_target_pairs={{0,2},{1,3},{2,0},{3,1},{4,6},{5,7},{6,4},{7,5},{8,10},{9,11},{10,... | collective-permute-start | bytes 589832 | tf_op jit(solution)/shard_map/ppermute | solution.py:35
  41.1 0.0 collective-permute-start.12
  41.1 0.4 collective-permute-done.15.got_k_ref
  41.5 0.2 collective-permute-start.14
  41.7 1.4 %collective-permute-done.16.got_v_ref = bf16[320,384]{1,0:T(8,128)(2,1)S(1)} collective-permute-done((bf16[320,384]{1,0:T(8,128)(2,1)S(1)}, bf16[320,384]{1,0:T(8,128)(2,1)S(1)}, u32[]{:S(2)}, u32[]{:S(2)}) %collective-permute-start.16) | collective-permute-done | bytes 245792 | tf_op jit(solution)/shard_map/ppermute | solution.py:35
  43.2 1.3 %collective-permute-start.17 = (bf16[160,384]{1,0:T(8,128)(2,1)S(1)}, bf16[160,384]{1,0:T(8,128)(2,1)S(1)}, u32[]{:S(2)}, u32[]{:S(2)}) collective-permute-start(bf16[160,384]{1,0:T(8,128)(2,1)S(1)} %get-tuple-element.70), channel_id=1, source_target_pairs={{0,8},{4,12},{8,0},{12,4},{16,24},{20,28},{24,16},{28,20},{1,9},{5... | collective-permute-start | bytes 368648 | tf_op jit(solution)/shard_map/ppermute | solution.py:35
  44.4 0.1 collective-permute-done.13.dq_pair_ref
  44.6 1.5 %collective-permute-start.18 = (bf16[160,384]{1,0:T(8,128)(2,1)S(1)}, bf16[160,384]{1,0:T(8,128)(2,1)S(1)}, u32[]{:S(2)}, u32[]{:S(2)}) collective-permute-start(bf16[160,384]{1,0:T(8,128)(2,1)S(1)} %get-tuple-element.71), channel_id=1, source_target_pairs={{0,4},{4,0},{8,12},{12,8},{16,20},{20,16},{24,28},{28,24},{1,5},{5... | collective-permute-start | bytes 368648 | tf_op jit(solution)/shard_map/ppermute | solution.py:35
  46.1 0.4 collective-permute-done.11.near_ref
  46.5 2.0 %collective-permute-done.12.far_ref = bf16[128,768]{1,0:T(8,128)(2,1)S(1)} collective-permute-done((bf16[128,768]{1,0:T(8,128)(2,1)S(1)}, bf16[128,768]{1,0:T(8,128)(2,1)S(1)}, u32[]{:S(2)}, u32[]{:S(2)}) %collective-permute-start.12) | collective-permute-done | bytes 196640 | tf_op jit(solution)/shard_map/ppermute | solution.py:35
  48.4 0.0 collective-permute-done.14.core_ref
  48.4 0.0 collective-permute-done.17.rest_k_ref
  48.4 1.0 %collective-permute-done.18.rest_v_ref = bf16[160,384]{1,0:T(8,128)(2,1)S(1)} collective-permute-done((bf16[160,384]{1,0:T(8,128)(2,1)S(1)}, bf16[160,384]{1,0:T(8,128)(2,1)S(1)}, u32[]{:S(2)}, u32[]{:S(2)}) %collective-permute-start.18) | collective-permute-done | bytes 122912 | tf_op jit(solution)/shard_map/ppermute | solution.py:35
  49.4 0.9 %finish.1 = (bf16[128,384]{1,0:T(8,128)(2,1)}, bf16[128,384]{1,0:T(8,128)(2,1)}, bf16[128,384]{1,0:T(8,128)(2,1)}, bf16[32,384]{1,0:T(8,128)(2,1)}, bf16[32,384]{1,0:T(8,128)(2,1)}, /*index=5*/bf16[128,768]{1,0:T(8,128)(2,1)}) custom-call(f32[128,768]{1,0:T(8,128)S(1)} %get-tuple-element.59.keep_ref, bf16[128,768]{1,0:T(8,128)(2,1)S(1)} %collective-permute-done.11.near_ref, ...), custom_call_target="tpu_custom_call" | custom-call | bytes 3321000 | tf_op jit(solution)/shard_map/finish/pallas_call | solution.py:44
  (14 shorter events, 0.1 us)
Async XLA Ops:
  0.6 25.0 %copy-start.2 = (bf16[128,384]{1,0:T(8,128)(2,1)S(1)}, bf16[128,384]{1,0:T(8,128)(2,1)}, u32[]{:S(2)}) copy-start(bf16[128,384]{1,0:T(8,128)(2,1)} %q_own_ref.3) | copy-start | bytes 294916
  0.6 22.5 %copy-start.5 = (s32[8,2]{0,1:T(2,128)S(1)}, s32[8,2]{0,1:T(2,128)}, u32[]{:S(2)}) copy-start(s32[8,2]{0,1:T(2,128)} %param.14) | copy-start | bytes 196
  0.7 22.6 %copy-start.4 = (s32[8]{0:T(128)S(1)}, s32[8]{0:T(128)}, u32[]{:S(2)}) copy-start(s32[8]{0:T(128)} %counts_ref.1) | copy-start | bytes 100
  0.7 8.1 %collective-permute-start.4 = (bf16[128,768]{1,0:T(8,128)(2,1)}, bf16[128,768]{1,0:T(8,128)(2,1)S(1)}, u32[]{:S(2)}, u32[]{:S(2)}) collective-permute-start(bf16[128,768]{1,0:T(8,128)(2,1)} %own_hbm.1), channel_id=1, source_target_pairs={{0,2},{1,3},{2,0},{3,1},{4,6},{5,7},{6,4},{7,5},{8,10},{9,11},{10,... | collective-permute-start | bytes 589832 | tf_op jit(solution)/shard_map/ppermute | solution.py:35
  5.3 20.3 %copy-start.1 = (bf16[320,384]{1,0:T(8,128)(2,1)S(1)}, bf16[320,384]{1,0:T(8,128)(2,1)}, u32[]{:S(2)}) copy-start(bf16[320,384]{1,0:T(8,128)(2,1)} %load.1.kv0) | copy-start | bytes 737284
  5.3 12.1 %collective-permute-start.1 = (bf16[320,384]{1,0:T(8,128)(2,1)}, bf16[320,384]{1,0:T(8,128)(2,1)S(1)}, u32[]{:S(2)}, u32[]{:S(2)}) collective-permute-start(bf16[320,384]{1,0:T(8,128)(2,1)} %load.1.kv0), channel_id=1, source_target_pairs={{0,8},{4,12},{8,0},{12,4},{16,24},{20,28},{24,16},{28,20},{1,9},{5... | collective-permute-start | bytes 737288 | tf_op jit(solution)/shard_map/ppermute | solution.py:35
  7.0 10.4 %collective-permute-start = (bf16[320,384]{1,0:T(8,128)(2,1)}, bf16[320,384]{1,0:T(8,128)(2,1)S(1)}, u32[]{:S(2)}, u32[]{:S(2)}) collective-permute-start(bf16[320,384]{1,0:T(8,128)(2,1)} %load.1.kv0), channel_id=1, source_target_pairs={{0,4},{4,0},{8,12},{12,8},{16,20},{20,16},{24,28},{28,24},{1,5},{5... | collective-permute-start | bytes 737288 | tf_op jit(solution)/shard_map/ppermute | solution.py:35
  8.5 3.1 %collective-permute-start.3 = (bf16[128,768]{1,0:T(8,128)(2,1)}, bf16[128,768]{1,0:T(8,128)(2,1)S(1)}, u32[]{:S(2)}, u32[]{:S(2)}) collective-permute-start(bf16[128,768]{1,0:T(8,128)(2,1)} %own_hbm.1), channel_id=1, source_target_pairs={{0,1},{1,0},{2,3},{3,2},{4,5},{5,4},{6,7},{7,6},{8,9},{9,8},{10,11... | collective-permute-start | bytes 589832 | tf_op jit(solution)/shard_map/ppermute | solution.py:35
  8.8 2.8 %collective-permute-start.5 = (bf16[128,768]{1,0:T(8,128)(2,1)S(1)}, bf16[128,768]{1,0:T(8,128)(2,1)S(1)}, u32[]{:S(2)}, u32[]{:S(2)}) collective-permute-start(bf16[128,768]{1,0:T(8,128)(2,1)S(1)} %collective-permute-done.4.near_ref), channel_id=1, source_target_pairs={{0,1},{1,0},{2,3},{3,2},{4,5},{5,4},{6,7},{7,6},{8,9},{9,8},{10,11... | collective-permute-start | bytes 589832 | tf_op jit(solution)/shard_map/ppermute | solution.py:35
  9.0 8.4 %collective-permute-start.2 = (bf16[128,384]{1,0:T(8,128)(2,1)}, bf16[128,384]{1,0:T(8,128)(2,1)S(1)}, u32[]{:S(2)}, u32[]{:S(2)}) collective-permute-start(bf16[128,384]{1,0:T(8,128)(2,1)} %q_own_ref.3), channel_id=1, source_target_pairs={{0,16},{4,20},{8,24},{12,28},{16,0},{20,4},{24,8},{28,12},{1,17},{... | collective-permute-start | bytes 294920 | tf_op jit(solution)/shard_map/ppermute | solution.py:35
  11.6 0.9 %copy-start.3 = (bf16[128,768]{1,0:T(8,128)(2,1)S(1)}, bf16[128,768]{1,0:T(8,128)(2,1)}, u32[]{:S(2)}) copy-start(bf16[128,768]{1,0:T(8,128)(2,1)} %own_hbm.1) | copy-start | bytes 589828
  17.4 6.4 %collective-permute-start.6 = (bf16[160,384]{1,0:T(8,128)(2,1)S(1)}, bf16[160,384]{1,0:T(8,128)(2,1)S(1)}, u32[]{:S(2)}, u32[]{:S(2)}) collective-permute-start(bf16[160,384]{1,0:T(8,128)(2,1)S(1)} %get-tuple-element.45), channel_id=1, source_target_pairs={{0,4},{4,0},{8,12},{12,8},{16,20},{20,16},{24,28},{28,24},{1,5},{5... | collective-permute-start | bytes 368648 | tf_op jit(solution)/shard_map/ppermute | solution.py:35
  19.1 6.6 %collective-permute-start.7 = (bf16[160,384]{1,0:T(8,128)(2,1)S(1)}, bf16[160,384]{1,0:T(8,128)(2,1)S(1)}, u32[]{:S(2)}, u32[]{:S(2)}) collective-permute-start(bf16[160,384]{1,0:T(8,128)(2,1)S(1)} %get-tuple-element.46), channel_id=1, source_target_pairs={{0,8},{4,12},{8,0},{12,4},{16,24},{20,28},{24,16},{28,20},{1,9},{5... | collective-permute-start | bytes 368648 | tf_op jit(solution)/shard_map/ppermute | solution.py:35
  19.9 8.9 %collective-permute-start.9 = (bf16[128,384]{1,0:T(8,128)(2,1)S(1)}, bf16[128,384]{1,0:T(8,128)(2,1)S(1)}, u32[]{:S(2)}, u32[]{:S(2)}) collective-permute-start(bf16[128,384]{1,0:T(8,128)(2,1)S(1)} %dattn.1.d_own_ref), channel_id=1, source_target_pairs={{0,16},{4,20},{8,24},{12,28},{16,0},{20,4},{24,8},{28,12},{1,17},{... | collective-permute-start | bytes 294920 | tf_op jit(solution)/shard_map/ppermute | solution.py:35
  27.1 8.1 %collective-permute-start.8 = (bf16[384,128]{1,0:T(8,128)(2,1)S(1)}, bf16[384,128]{1,0:T(8,128)(2,1)S(1)}, u32[]{:S(2)}, u32[]{:S(2)}) collective-permute-start(bf16[384,128]{1,0:T(8,128)(2,1)S(1)} %get-tuple-element.51), channel_id=1, source_target_pairs={{0,16},{4,20},{8,24},{12,28},{16,0},{20,4},{24,8},{28,12},{1,17},{... | collective-permute-start | bytes 294920 | tf_op jit(solution)/shard_map/ppermute | solution.py:35
  29.2 9.7 %copy-start = (bf16[384,3072]{1,0:T(8,128)(2,1)S(1)}, bf16[384,3072]{1,0:T(8,128)(2,1)}, u32[]{:S(2)}) copy-start(bf16[384,3072]{1,0:T(8,128)(2,1)} %w_ref.1) | copy-start | bytes 7077892
  29.3 4.8 %collective-permute-start.10 = (f32[16,256]{1,0:T(8,128)S(1)}, f32[16,256]{1,0:T(8,128)S(1)}, u32[]{:S(2)}, u32[]{:S(2)}) collective-permute-start(f32[16,256]{1,0:T(8,128)S(1)} %get-tuple-element.54.stats_ref), channel_id=1, source_target_pairs={{0,16},{4,20},{8,24},{12,28},{16,0},{20,4},{24,8},{28,12},{1,17},{... | collective-permute-start | bytes 49160 | tf_op jit(solution)/shard_map/ppermute | solution.py:35
  35.2 6.3 %collective-permute-start.15 = (bf16[320,384]{1,0:T(8,128)(2,1)S(1)}, bf16[320,384]{1,0:T(8,128)(2,1)S(1)}, u32[]{:S(2)}, u32[]{:S(2)}) collective-permute-start(bf16[320,384]{1,0:T(8,128)(2,1)S(1)} %get-tuple-element.66), channel_id=1, source_target_pairs={{0,4},{4,0},{8,12},{12,8},{16,20},{20,16},{24,28},{28,24},{1,5},{5... | collective-permute-start | bytes 737288 | tf_op jit(solution)/shard_map/ppermute | solution.py:35
  35.7 7.4 %collective-permute-start.16 = (bf16[320,384]{1,0:T(8,128)(2,1)S(1)}, bf16[320,384]{1,0:T(8,128)(2,1)S(1)}, u32[]{:S(2)}, u32[]{:S(2)}) collective-permute-start(bf16[320,384]{1,0:T(8,128)(2,1)S(1)} %get-tuple-element.67), channel_id=1, source_target_pairs={{0,8},{4,12},{8,0},{12,4},{16,24},{20,28},{24,16},{28,20},{1,9},{5... | collective-permute-start | bytes 737288 | tf_op jit(solution)/shard_map/ppermute | solution.py:35
  38.0 6.6 %collective-permute-start.13 = (bf16[128,384]{1,0:T(8,128)(2,1)S(1)}, bf16[128,384]{1,0:T(8,128)(2,1)S(1)}, u32[]{:S(2)}, u32[]{:S(2)}) collective-permute-start(bf16[128,384]{1,0:T(8,128)(2,1)S(1)} %get-tuple-element.63), channel_id=1, source_target_pairs={{0,16},{4,20},{8,24},{12,28},{16,0},{20,4},{24,8},{28,12},{1,17},{... | collective-permute-start | bytes 294920 | tf_op jit(solution)/shard_map/ppermute | solution.py:35
  39.5 6.9 %collective-permute-start.11 = (bf16[128,768]{1,0:T(8,128)(2,1)S(1)}, bf16[128,768]{1,0:T(8,128)(2,1)S(1)}, u32[]{:S(2)}, u32[]{:S(2)}) collective-permute-start(bf16[128,768]{1,0:T(8,128)(2,1)S(1)} %get-tuple-element.60), channel_id=1, source_target_pairs={{0,2},{1,3},{2,0},{3,1},{4,6},{5,7},{6,4},{7,5},{8,10},{9,11},{10,... | collective-permute-start | bytes 589832 | tf_op jit(solution)/shard_map/ppermute | solution.py:35
  41.1 7.4 %collective-permute-start.12 = (bf16[128,768]{1,0:T(8,128)(2,1)S(1)}, bf16[128,768]{1,0:T(8,128)(2,1)S(1)}, u32[]{:S(2)}, u32[]{:S(2)}) collective-permute-start(bf16[128,768]{1,0:T(8,128)(2,1)S(1)} %get-tuple-element.61), channel_id=1, source_target_pairs={{0,3},{1,2},{2,1},{3,0},{4,7},{5,6},{6,5},{7,4},{8,11},{9,10},{10,... | collective-permute-start | bytes 589832 | tf_op jit(solution)/shard_map/ppermute | solution.py:35
  41.5 7.0 %collective-permute-start.14 = (bf16[128,768]{1,0:T(8,128)(2,1)S(1)}, bf16[128,768]{1,0:T(8,128)(2,1)S(1)}, u32[]{:S(2)}, u32[]{:S(2)}) collective-permute-start(bf16[128,768]{1,0:T(8,128)(2,1)S(1)} %get-tuple-element.64), channel_id=1, source_target_pairs={{0,1},{1,0},{2,3},{3,2},{4,5},{5,4},{6,7},{7,6},{8,9},{9,8},{10,11... | collective-permute-start | bytes 589832 | tf_op jit(solution)/shard_map/ppermute | solution.py:35
  43.2 5.3 %collective-permute-start.17 = (bf16[160,384]{1,0:T(8,128)(2,1)S(1)}, bf16[160,384]{1,0:T(8,128)(2,1)S(1)}, u32[]{:S(2)}, u32[]{:S(2)}) collective-permute-start(bf16[160,384]{1,0:T(8,128)(2,1)S(1)} %get-tuple-element.70), channel_id=1, source_target_pairs={{0,8},{4,12},{8,0},{12,4},{16,24},{20,28},{24,16},{28,20},{1,9},{5... | collective-permute-start | bytes 368648 | tf_op jit(solution)/shard_map/ppermute | solution.py:35
  44.6 4.9 %collective-permute-start.18 = (bf16[160,384]{1,0:T(8,128)(2,1)S(1)}, bf16[160,384]{1,0:T(8,128)(2,1)S(1)}, u32[]{:S(2)}, u32[]{:S(2)}) collective-permute-start(bf16[160,384]{1,0:T(8,128)(2,1)S(1)} %get-tuple-element.71), channel_id=1, source_target_pairs={{0,4},{4,0},{8,12},{12,8},{16,20},{20,16},{24,28},{28,24},{1,5},{5... | collective-permute-start | bytes 368648 | tf_op jit(solution)/shard_map/ppermute | solution.py:35

commit v9 on v8

--- a/solution.py
+++ b/solution.py
@@ -108,52 +108,15 @@
     limits_ref[...] = limits
 
 
-def dattn_kernel(own_hbm, w_hbm, core_ref, near_ref, far_ref, out_ref, own_ref, w_ref, sems):
+def dattn_kernel(own_ref, core_ref, near_ref, far_ref, w_ref, out_ref):
     me = lax.axis_index("head")
-    size = core_ref.shape[1]
-    pieces = w_ref.shape[1] // HDIM
-    own_copy = pltpu.make_async_copy(own_hbm, own_ref, sems.at[4, 0])
-    own_copy.start()
-    copies = []
-    for step in range(4):
-        columns = pl.ds(pl.multiple_of((me ^ step) * size, HDIM), size)
-        for i in range(pieces):
-            part = pl.ds(i * HDIM, HDIM)
-            copies.append(
-                pltpu.make_async_copy(
-                    w_hbm.at[part, columns], w_ref.at[step, part], sems.at[step, i]
-                )
-            )
-    for copy in copies:
-        copy.start()
-    own_copy.wait()
+    size = own_ref.shape[1]
     total = None
     for step, ref in enumerate((own_ref, core_ref, near_ref, far_ref)):
-        for copy in copies[step * pieces : (step + 1) * pieces]:
-            copy.wait()
-        part = contract(ref[...], w_ref[step], 1, 1)
+        columns = pl.ds(pl.multiple_of((me ^ step) * size, HDIM), size)
+        part = contract(ref[...], w_ref[:, columns], 1, 1)
         total = part if total is None else total + part
     out_ref[...] = total.astype(BF16)
-
-
-def dattn_call(grad_own, w_out, *blocks):
-    rows, share = grad_own.shape
-    width = w_out.shape[0]
-    anywhere, inside = pl.BlockSpec(memory_space=pl.ANY), pl.BlockSpec(memory_space=pltpu.VMEM)
-    return pl.pallas_call(
-        dattn_kernel,
-        name="dattn",
-        out_shape=jax.ShapeDtypeStruct((rows, width), BF16),
-        in_specs=[anywhere, anywhere, inside, inside, inside],
-        out_specs=inside,
-        scratch_shapes=[
-            pltpu.VMEM((rows, share), BF16),
-            pltpu.VMEM((4, width, share), BF16),
-            pltpu.SemaphoreType.DMA((5, width // HDIM)),
-        ],
-        compiler_params=pltpu.CompilerParams(vmem_limit_bytes=52 * 2**20),
-        cost_estimate=cost_of(1.5),
-    )(grad_own, w_out, *blocks)
 
 
 def both_rows(own_ref, pair_ref, head):
@@ -321,19 +284,25 @@
     keys = rows + capacity
     share = grad_out.shape[1]
 
-    q_pair = swap(sec_q, "ctx", PAIR)
     grad_near = swap(grad_out, "head", 2)
     grad_core = swap(grad_out, "head", 1)
     grad_far = swap(grad_near, "head", 1)
     kv0 = load_keys(sec_k, hist_k, sec_v, hist_v)
     kv2 = swap(kv0, "ctx", 2)
     kv1 = swap(kv0, "ctx", 1)
-    d_own = dattn_call(grad_out, w_out, grad_core, grad_near, grad_far)
-    kv1, kv2, q_pair, d_own = lax.optimization_barrier((kv1, kv2, q_pair, d_own))
+    d_own = local_call(
+        dattn_kernel,
+        "dattn",
+        0.8,
+        [shape((rows, width), BF16)],
+        (grad_out, grad_core, grad_near, grad_far, w_out),
+    )[0]
+    kv1, kv2, d_own, sec_q = lax.optimization_barrier((kv1, kv2, d_own, sec_q))
     key3, value3 = local_call(
         pass_keys_kernel, "pass_keys", 0.1, [shape((keys, width), BF16)] * 2, (kv1, kv2)
     )
     kvs = [kv0, kv1, kv2, swap(key3, "ctx", 1), swap(value3, "ctx", 2)]
+    q_pair = swap(sec_q, "ctx", PAIR)
     d_pair = swap(d_own, "ctx", PAIR)
     limits = local_call(
         limits_kernel,

time: 50.5 us -> 53.1 us (1.051)
  waiting for transfers between devices: 12.9 us -> 18 us
  starting transfers between devices: 26 us -> 23.7 us
  Pallas kernels: 9.61 us -> 7.7 us
  local copies, waits for them, and re-layouts: 1.03 us -> 2.69 us
    ppermute x19, waiting for transfers between devices: 12.9 us -> 18 us  [swap(): return lax.ppermute(block, axis, [(i, i ^ bit) for i in range(count)])]
    pallas_call x1 -> x0, Pallas kernels: 2.75 us -> none  [dattn_call(): pl.pallas_call(dattn_kernel, name='dattn', out_shape=jax.ShapeDtypeStruct...]
    ppermute x19, starting transfers between devices: 26 us -> 23.7 us  [swap(): return lax.ppermute(block, axis, [(i, i ^ bit) for i in range(count)])]
    unnamed x13 -> x15, local copies, waits for them, and re-layouts: 1.03 us -> 2.69 us
    pallas_call x9 -> x10, Pallas kernels: 5.2 us -> 6.02 us  [local_call(): pl.pallas_call(body, name=name, out_shape=out_shapes, in_specs=[pl.BlockS...]
  transfers between devices with their start and end apart: 19 -> 19, of which waited for: 10 -> 12; matrix products, arithmetic and copies ran while one was open for 0% -> 0% of each run, Pallas kernels for 17% -> 13%
where the time goes in v9:
time: 53.1 us; the launch traced here: 52.9 us
  starting transfers between devices  23.7 us (45%)
  waiting for transfers between devices  18 us (34%)
  Pallas kernels  7.7 us (15%)
  local copies, waits for them, and re-layouts  2.69 us (5%)
  between operations  0.78 us (1%)
    ppermute x19, starting transfers between devices, swap(): return lax.ppermute(block, axis, [(i, i ^ bit) for i in range(count)])  23.7 us
    ppermute x19, waiting for transfers between devices, swap(): return lax.ppermute(block, axis, [(i, i ^ bit) for i in range(count)])  18 us
    pallas_call x10, Pallas kernels, local_call(): pl.pallas_call(body, name=name, out_shape=out_shapes, in_specs=[pl.BlockS...  6.02 us
    unnamed x15, local copies, waits for them, and re-layouts  2.69 us
    pallas_call x1, Pallas kernels, load_keys(): pl.pallas_call(load_kernel, name='load', out_shape=jax.ShapeDtypeStruct((...  1.67 us
  transfers between devices with their start and end apart: 19, of which 12 were waited for; matrix products, arithmetic and copies ran while one was open for 0% of the time, Pallas kernels for 13%

profile of v9, /device:TPU:0, one launch (start us, length us, event | category | flops | bytes accessed | tf_op | source)
XLA Modules:
  0.0 52.9 jit_solution(17473456832714813988)
XLA Ops:
  0.7 3.0 %collective-permute-start.3 = (bf16[128,768]{1,0:T(8,128)(2,1)}, bf16[128,768]{1,0:T(8,128)(2,1)S(1)}, u32[]{:S(2)}, u32[]{:S(2)}) collective-permute-start(bf16[128,768]{1,0:T(8,128)(2,1)} %own_ref.1), channel_id=1, source_target_pairs={{0,2},{1,3},{2,0},{3,1},{4,6},{5,7},{6,4},{7,5},{8,10},{9,11},{10,... | collective-permute-start | bytes 589832 | tf_op jit(solution)/shard_map/ppermute | solution.py:35
  3.7 1.7 %load.1.kv0 = bf16[320,384]{1,0:T(8,128)(2,1)} custom-call(bf16[128,384]{1,0:T(8,128)(2,1)} %k_ref.1, bf16[32,384]{1,0:T(8,128)(2,1)} %hk_ref.1, bf16[128,384]{1,0:T(8,128)(2,1)} %v_ref.1, bf16[32,384]{1,0:T(8,128)(2,1)} %hv_ref.1), custom_call_target="tpu_custom_call" | custom-call | bytes 5904000 | tf_op jit(solution)/shard_map/load/pallas_call | solution.py:74
  5.4 1.6 %collective-permute-start.1 = (bf16[320,384]{1,0:T(8,128)(2,1)}, bf16[320,384]{1,0:T(8,128)(2,1)S(1)}, u32[]{:S(2)}, u32[]{:S(2)}) collective-permute-start(bf16[320,384]{1,0:T(8,128)(2,1)} %load.1.kv0), channel_id=1, source_target_pairs={{0,8},{4,12},{8,0},{12,4},{16,24},{20,28},{24,16},{28,20},{1,9},{5... | collective-permute-start | bytes 737288 | tf_op jit(solution)/shard_map/ppermute | solution.py:35
  7.0 1.5 %collective-permute-start = (bf16[320,384]{1,0:T(8,128)(2,1)}, bf16[320,384]{1,0:T(8,128)(2,1)S(1)}, u32[]{:S(2)}, u32[]{:S(2)}) collective-permute-start(bf16[320,384]{1,0:T(8,128)(2,1)} %load.1.kv0), channel_id=1, source_target_pairs={{0,4},{4,0},{8,12},{12,8},{16,20},{20,16},{24,28},{28,24},{1,5},{5... | collective-permute-start | bytes 737288 | tf_op jit(solution)/shard_map/ppermute | solution.py:35
  8.5 0.0 collective-permute-start.2
  8.5 0.3 collective-permute-done.3.near_ref
  8.8 0.2 collective-permute-start.4
  9.0 1.1 %collective-permute-done.2.core_ref = bf16[128,768]{1,0:T(8,128)(2,1)S(1)} collective-permute-done((bf16[128,768]{1,0:T(8,128)(2,1)}, bf16[128,768]{1,0:T(8,128)(2,1)S(1)}, u32[]{:S(2)}, u32[]{:S(2)}) %collective-permute-start.2) | collective-permute-done | bytes 196640 | tf_op jit(solution)/shard_map/ppermute | solution.py:35
  10.2 0.1 collective-permute-done.4.far_ref
  10.2 1.7 %copy-done = bf16[384,3072]{1,0:T(8,128)(2,1)S(1)} copy-done((bf16[384,3072]{1,0:T(8,128)(2,1)S(1)}, bf16[384,3072]{1,0:T(8,128)(2,1)}, u32[]{:S(2)}) %copy-start) | copy-done | bytes 2359320
  11.9 0.9 %copy-done.4 = bf16[128,768]{1,0:T(8,128)(2,1)S(1)} copy-done((bf16[128,768]{1,0:T(8,128)(2,1)S(1)}, bf16[128,768]{1,0:T(8,128)(2,1)}, u32[]{:S(2)}) %copy-start.4) | copy-done | bytes 196632
  12.8 0.8 %dattn.1.d_own_ref = bf16[128,384]{1,0:T(8,128)(2,1)S(1)} custom-call(bf16[128,768]{1,0:T(8,128)(2,1)S(1)} %copy-done.4, bf16[128,768]{1,0:T(8,128)(2,1)S(1)} %collective-permute-done.2.core_ref, bf16[128,768]{1,0:T(8,128)(2,1)S(1)} %collective-permute-done.3.near_ref, bf16[128,768]{1,0:T(8,128)(2,1)S(1)} %collective-permute-done.4.far_ref, ...), custom_call_target="tpu_custom_call" | custom-call | bytes 2952000 | tf_op jit(solution)/shard_map/dattn/pallas_call | solution.py:44
  13.7 0.7 %collective-permute-done.kv1 = bf16[320,384]{1,0:T(8,128)(2,1)S(1)} collective-permute-done((bf16[320,384]{1,0:T(8,128)(2,1)}, bf16[320,384]{1,0:T(8,128)(2,1)S(1)}, u32[]{:S(2)}, u32[]{:S(2)}) %collective-permute-start) | collective-permute-done | bytes 245792 | tf_op jit(solution)/shard_map/ppermute | solution.py:35
  14.4 1.6 %collective-permute-start.6 = (bf16[160,384]{1,0:T(8,128)(2,1)S(1)}, bf16[160,384]{1,0:T(8,128)(2,1)S(1)}, u32[]{:S(2)}, u32[]{:S(2)}) collective-permute-start(bf16[160,384]{1,0:T(8,128)(2,1)S(1)} %get-tuple-element.45), channel_id=1, source_target_pairs={{0,4},{4,0},{8,12},{12,8},{16,20},{20,16},{24,28},{28,24},{1,5},{5... | collective-permute-start | bytes 368648 | tf_op jit(solution)/shard_map/ppermute | solution.py:35
  15.9 1.2 %collective-permute-start.7 = (bf16[160,384]{1,0:T(8,128)(2,1)S(1)}, bf16[160,384]{1,0:T(8,128)(2,1)S(1)}, u32[]{:S(2)}, u32[]{:S(2)}) collective-permute-start(bf16[160,384]{1,0:T(8,128)(2,1)S(1)} %get-tuple-element.46), channel_id=1, source_target_pairs={{0,8},{4,12},{8,0},{12,4},{16,24},{20,28},{24,16},{28,20},{1,9},{5... | collective-permute-start | bytes 368648 | tf_op jit(solution)/shard_map/ppermute | solution.py:35
  17.1 2.6 %collective-permute-start.5 = (bf16[128,384]{1,0:T(8,128)(2,1)S(1)}, bf16[128,384]{1,0:T(8,128)(2,1)S(1)}, u32[]{:S(2)}, u32[]{:S(2)}) collective-permute-start(bf16[128,384]{1,0:T(8,128)(2,1)S(1)} %copy-done.3), channel_id=1, source_target_pairs={{0,16},{4,20},{8,24},{12,28},{16,0},{20,4},{24,8},{28,12},{1,17},{... | collective-permute-start | bytes 294920 | tf_op jit(solution)/shard_map/ppermute | solution.py:35
  19.7 0.3 collective-permute-start.9
  20.0 0.1 copy.15.levels_ref
  20.1 0.6 %limits.1.limits_ref = s32[8,256]{1,0:T(8,128)S(1)} custom-call(s32[8,2]{1,0:T(8,128)S(1)} %copy.15.levels_ref, s32[8]{0:T(128)S(1)} %copy-done.5), custom_call_target="tpu_custom_call" | custom-call | bytes 2214000 | tf_op jit(solution)/shard_map/limits/pallas_call | solution.py:44
  20.8 6.5 %collective-permute-done.5.q_pair_ref = bf16[128,384]{1,0:T(8,128)(2,1)S(1)} collective-permute-done((bf16[128,384]{1,0:T(8,128)(2,1)S(1)}, bf16[128,384]{1,0:T(8,128)(2,1)S(1)}, u32[]{:S(2)}, u32[]{:S(2)}) %collective-permute-start.5) | collective-permute-done | bytes 98336 | tf_op jit(solution)/shard_map/ppermute | solution.py:35
  27.2 0.0 collective-permute-done.7.value3
  27.2 1.0 %scores.1 = (f32[8,256]{1,0:T(8,128)S(1)}, bf16[1920,256]{1,0:T(8,128)(2,1)S(1)}) custom-call(s32[8,256]{1,0:T(8,128)S(1)} %limits.1.limits_ref, bf16[128,384]{1,0:T(8,128)(2,1)S(1)} %copy-done.3, bf16[128,384]{1,0:T(8,128)(2,1)S(1)} %collective-permute-done.5.q_pair_ref, bf16[320,384]{1,0:T(8,128)(2,1)S(1)} %copy-done.2, ...), custom_call_target="tpu_custom_call" | custom-call | bytes 3321000 | tf_op jit(solution)/shard_map/scores/pallas_call | solution.py:44
  28.3 0.4 attn.1
  28.7 0.1 collective-permute-start.8
  28.8 1.6 %collective-permute-done.9.d_pair_ref = bf16[128,384]{1,0:T(8,128)(2,1)S(1)} collective-permute-done((bf16[128,384]{1,0:T(8,128)(2,1)S(1)}, bf16[128,384]{1,0:T(8,128)(2,1)S(1)}, u32[]{:S(2)}, u32[]{:S(2)}) %collective-permute-start.9) | collective-permute-done | bytes 98336 | tf_op jit(solution)/shard_map/ppermute | solution.py:35
  30.4 0.4 delta.1
  30.8 0.0 copy-start.1
  30.8 1.4 %collective-permute-start.10 = (f32[16,256]{1,0:T(8,128)S(1)}, f32[16,256]{1,0:T(8,128)S(1)}, u32[]{:S(2)}, u32[]{:S(2)}) collective-permute-start(f32[16,256]{1,0:T(8,128)S(1)} %get-tuple-element.54.stats_ref), channel_id=1, source_target_pairs={{0,16},{4,20},{8,24},{12,28},{16,0},{20,4},{24,8},{28,12},{1,17},{... | collective-permute-start | bytes 49160 | tf_op jit(solution)/shard_map/ppermute | solution.py:35
  32.2 3.7 %collective-permute-done.10.stats_pair_ref = f32[16,256]{1,0:T(8,128)S(1)} collective-permute-done((f32[16,256]{1,0:T(8,128)S(1)}, f32[16,256]{1,0:T(8,128)S(1)}, u32[]{:S(2)}, u32[]{:S(2)}) %collective-permute-start.10) | collective-permute-done | bytes 16416 | tf_op jit(solution)/shard_map/ppermute | solution.py:35
  35.8 1.1 %backward.1 = (f32[128,384]{1,0:T(8,128)S(1)}, bf16[128,384]{1,0:T(8,128)(2,1)S(1)}, f32[320,384]{1,0:T(8,128)S(1)}, bf16[320,384]{1,0:T(8,128)(2,1)S(1)}, bf16[...) custom-call(bf16[128,384]{1,0:T(8,128)(2,1)S(1)} %copy-done.3, ...), custom_call_target="tpu_custom_call" | custom-call | bytes 4059000 | tf_op jit(solution)/shard_map/backward/pallas_call | solution.py:44
  37.0 0.0 collective-permute-done.8.pair_ref
  37.0 0.6 %collective-permute-start.15 = (bf16[320,384]{1,0:T(8,128)(2,1)S(1)}, bf16[320,384]{1,0:T(8,128)(2,1)S(1)}, u32[]{:S(2)}, u32[]{:S(2)}) collective-permute-start(bf16[320,384]{1,0:T(8,128)(2,1)S(1)} %get-tuple-element.66), channel_id=1, source_target_pairs={{0,4},{4,0},{8,12},{12,8},{16,20},{20,16},{24,28},{28,24},{1,5},{5... | collective-permute-start | bytes 737288 | tf_op jit(solution)/shard_map/ppermute | solution.py:35
  37.5 3.1 %collective-permute-start.16 = (bf16[320,384]{1,0:T(8,128)(2,1)S(1)}, bf16[320,384]{1,0:T(8,128)(2,1)S(1)}, u32[]{:S(2)}, u32[]{:S(2)}) collective-permute-start(bf16[320,384]{1,0:T(8,128)(2,1)S(1)} %get-tuple-element.67), channel_id=1, source_target_pairs={{0,8},{4,12},{8,0},{12,4},{16,24},{20,28},{24,16},{28,20},{1,9},{5... | collective-permute-start | bytes 737288 | tf_op jit(solution)/shard_map/ppermute | solution.py:35
  40.7 0.5 %collective-permute-start.13 = (bf16[128,384]{1,0:T(8,128)(2,1)S(1)}, bf16[128,384]{1,0:T(8,128)(2,1)S(1)}, u32[]{:S(2)}, u32[]{:S(2)}) collective-permute-start(bf16[128,384]{1,0:T(8,128)(2,1)S(1)} %get-tuple-element.63), channel_id=1, source_target_pairs={{0,16},{4,20},{8,24},{12,28},{16,0},{20,4},{24,8},{28,12},{1,17},{... | collective-permute-start | bytes 294920 | tf_op jit(solution)/shard_map/ppermute | solution.py:35
  41.2 0.6 %project.1 = (f32[128,768]{1,0:T(8,128)S(1)}, bf16[128,768]{1,0:T(8,128)(2,1)S(1)}, bf16[128,768]{1,0:T(8,128)(2,1)S(1)}, bf16[128,768]{1,0:T(8,128)(2,1)S(1)}) custom-call(f32[384,128]{1,0:T(8,128)S(1)} %get-tuple-element.50.own_ref, bf16[384,128]{1,0:T(8,128)(2,1)S(1)} %collective-permute-done.8.pair_ref, f32[16,256]{1,0:T(8,128)S(1)} %get-tuple-element.54.stats_ref, ...), custom_call_target="tpu_custom_call" | custom-call | bytes 2214000 | tf_op jit(solution)/shard_map/project/pallas_call | solution.py:44
  41.8 1.3 %collective-permute-start.11 = (bf16[128,768]{1,0:T(8,128)(2,1)S(1)}, bf16[128,768]{1,0:T(8,128)(2,1)S(1)}, u32[]{:S(2)}, u32[]{:S(2)}) collective-permute-start(bf16[128,768]{1,0:T(8,128)(2,1)S(1)} %get-tuple-element.60), channel_id=1, source_target_pairs={{0,2},{1,3},{2,0},{3,1},{4,6},{5,7},{6,4},{7,5},{8,10},{9,11},{10,... | collective-permute-start | bytes 589832 | tf_op jit(solution)/shard_map/ppermute | solution.py:35
  43.2 0.0 collective-permute-start.12
  43.2 0.1 collective-permute-done.15.got_k_ref
  43.2 0.8 %collective-permute-start.14 = (bf16[128,768]{1,0:T(8,128)(2,1)S(1)}, bf16[128,768]{1,0:T(8,128)(2,1)S(1)}, u32[]{:S(2)}, u32[]{:S(2)}) collective-permute-start(bf16[128,768]{1,0:T(8,128)(2,1)S(1)} %get-tuple-element.64), channel_id=1, source_target_pairs={{0,1},{1,0},{2,3},{3,2},{4,5},{5,4},{6,7},{7,6},{8,9},{9,8},{10,11... | collective-permute-start | bytes 589832 | tf_op jit(solution)/shard_map/ppermute | solution.py:35
  44.0 0.8 %collective-permute-done.16.got_v_ref = bf16[320,384]{1,0:T(8,128)(2,1)S(1)} collective-permute-done((bf16[320,384]{1,0:T(8,128)(2,1)S(1)}, bf16[320,384]{1,0:T(8,128)(2,1)S(1)}, u32[]{:S(2)}, u32[]{:S(2)}) %collective-permute-start.16) | collective-permute-done | bytes 245792 | tf_op jit(solution)/shard_map/ppermute | solution.py:35
  44.9 2.1 %collective-permute-start.17 = (bf16[160,384]{1,0:T(8,128)(2,1)S(1)}, bf16[160,384]{1,0:T(8,128)(2,1)S(1)}, u32[]{:S(2)}, u32[]{:S(2)}) collective-permute-start(bf16[160,384]{1,0:T(8,128)(2,1)S(1)} %get-tuple-element.70), channel_id=1, source_target_pairs={{0,8},{4,12},{8,0},{12,4},{16,24},{20,28},{24,16},{28,20},{1,9},{5... | collective-permute-start | bytes 368648 | tf_op jit(solution)/shard_map/ppermute | solution.py:35
  47.0 1.8 %collective-permute-start.18 = (bf16[160,384]{1,0:T(8,128)(2,1)S(1)}, bf16[160,384]{1,0:T(8,128)(2,1)S(1)}, u32[]{:S(2)}, u32[]{:S(2)}) collective-permute-start(bf16[160,384]{1,0:T(8,128)(2,1)S(1)} %get-tuple-element.71), channel_id=1, source_target_pairs={{0,4},{4,0},{8,12},{12,8},{16,20},{20,16},{24,28},{28,24},{1,5},{5... | collective-permute-start | bytes 368648 | tf_op jit(solution)/shard_map/ppermute | solution.py:35
  48.7 0.3 collective-permute-done.11.near_ref
  49.0 1.5 %collective-permute-done.12.far_ref = bf16[128,768]{1,0:T(8,128)(2,1)S(1)} collective-permute-done((bf16[128,768]{1,0:T(8,128)(2,1)S(1)}, bf16[128,768]{1,0:T(8,128)(2,1)S(1)}, u32[]{:S(2)}, u32[]{:S(2)}) %collective-permute-start.12) | collective-permute-done | bytes 196640 | tf_op jit(solution)/shard_map/ppermute | solution.py:35
  50.6 0.0 collective-permute-done.14.core_ref
  50.6 0.0 collective-permute-done.17.rest_k_ref
  50.6 1.4 %collective-permute-done.18.rest_v_ref = bf16[160,384]{1,0:T(8,128)(2,1)S(1)} collective-permute-done((bf16[160,384]{1,0:T(8,128)(2,1)S(1)}, bf16[160,384]{1,0:T(8,128)(2,1)S(1)}, u32[]{:S(2)}, u32[]{:S(2)}) %collective-permute-start.18) | collective-permute-done | bytes 122912 | tf_op jit(solution)/shard_map/ppermute | solution.py:35
  52.0 0.9 %finish.1 = (bf16[128,384]{1,0:T(8,128)(2,1)}, bf16[128,384]{1,0:T(8,128)(2,1)}, bf16[128,384]{1,0:T(8,128)(2,1)}, bf16[32,384]{1,0:T(8,128)(2,1)}, bf16[32,384]{1,0:T(8,128)(2,1)}, /*index=5*/bf16[128,768]{1,0:T(8,128)(2,1)}) custom-call(f32[128,768]{1,0:T(8,128)S(1)} %get-tuple-element.59.keep_ref, bf16[128,768]{1,0:T(8,128)(2,1)S(1)} %collective-permute-done.11.near_ref, ...), custom_call_target="tpu_custom_call" | custom-call | bytes 3321000 | tf_op jit(solution)/shard_map/finish/pallas_call | solution.py:44
  (16 shorter events, 0.1 us)
Async XLA Ops:
  0.6 16.5 %copy-start.3 = (bf16[128,384]{1,0:T(8,128)(2,1)S(1)}, bf16[128,384]{1,0:T(8,128)(2,1)}, u32[]{:S(2)}) copy-start(bf16[128,384]{1,0:T(8,128)(2,1)} %q_own_ref.1) | copy-start | bytes 294916
  0.6 19.4 %copy-start.6 = (s32[8,2]{0,1:T(2,128)S(1)}, s32[8,2]{0,1:T(2,128)}, u32[]{:S(2)}) copy-start(s32[8,2]{0,1:T(2,128)} %param.14) | copy-start | bytes 196
  0.7 19.5 %copy-start.5 = (s32[8]{0:T(128)S(1)}, s32[8]{0:T(128)}, u32[]{:S(2)}) copy-start(s32[8]{0:T(128)} %counts_ref.1) | copy-start | bytes 100
  0.7 8.1 %collective-permute-start.3 = (bf16[128,768]{1,0:T(8,128)(2,1)}, bf16[128,768]{1,0:T(8,128)(2,1)S(1)}, u32[]{:S(2)}, u32[]{:S(2)}) collective-permute-start(bf16[128,768]{1,0:T(8,128)(2,1)} %own_ref.1), channel_id=1, source_target_pairs={{0,2},{1,3},{2,0},{3,1},{4,6},{5,7},{6,4},{7,5},{8,10},{9,11},{10,... | collective-permute-start | bytes 589832 | tf_op jit(solution)/shard_map/ppermute | solution.py:35
  5.4 8.3 %collective-permute-start.1 = (bf16[320,384]{1,0:T(8,128)(2,1)}, bf16[320,384]{1,0:T(8,128)(2,1)S(1)}, u32[]{:S(2)}, u32[]{:S(2)}) collective-permute-start(bf16[320,384]{1,0:T(8,128)(2,1)} %load.1.kv0), channel_id=1, source_target_pairs={{0,8},{4,12},{8,0},{12,4},{16,24},{20,28},{24,16},{28,20},{1,9},{5... | collective-permute-start | bytes 737288 | tf_op jit(solution)/shard_map/ppermute | solution.py:35
  7.0 7.3 %collective-permute-start = (bf16[320,384]{1,0:T(8,128)(2,1)}, bf16[320,384]{1,0:T(8,128)(2,1)S(1)}, u32[]{:S(2)}, u32[]{:S(2)}) collective-permute-start(bf16[320,384]{1,0:T(8,128)(2,1)} %load.1.kv0), channel_id=1, source_target_pairs={{0,4},{4,0},{8,12},{12,8},{16,20},{20,16},{24,28},{28,24},{1,5},{5... | collective-permute-start | bytes 737288 | tf_op jit(solution)/shard_map/ppermute | solution.py:35
  8.5 1.7 %collective-permute-start.2 = (bf16[128,768]{1,0:T(8,128)(2,1)}, bf16[128,768]{1,0:T(8,128)(2,1)S(1)}, u32[]{:S(2)}, u32[]{:S(2)}) collective-permute-start(bf16[128,768]{1,0:T(8,128)(2,1)} %own_ref.1), channel_id=1, source_target_pairs={{0,1},{1,0},{2,3},{3,2},{4,5},{5,4},{6,7},{7,6},{8,9},{9,8},{10,11... | collective-permute-start | bytes 589832 | tf_op jit(solution)/shard_map/ppermute | solution.py:35
  8.8 1.5 %collective-permute-start.4 = (bf16[128,768]{1,0:T(8,128)(2,1)S(1)}, bf16[128,768]{1,0:T(8,128)(2,1)S(1)}, u32[]{:S(2)}, u32[]{:S(2)}) collective-permute-start(bf16[128,768]{1,0:T(8,128)(2,1)S(1)} %collective-permute-done.3.near_ref), channel_id=1, source_target_pairs={{0,1},{1,0},{2,3},{3,2},{4,5},{5,4},{6,7},{7,6},{8,9},{9,8},{10,11... | collective-permute-start | bytes 589832 | tf_op jit(solution)/shard_map/ppermute | solution.py:35
  10.2 1.7 %copy-start = (bf16[384,3072]{1,0:T(8,128)(2,1)S(1)}, bf16[384,3072]{1,0:T(8,128)(2,1)}, u32[]{:S(2)}) copy-start(bf16[384,3072]{1,0:T(8,128)(2,1)} %w_ref.3) | copy-start | bytes 7077892
  11.9 0.9 %copy-start.4 = (bf16[128,768]{1,0:T(8,128)(2,1)S(1)}, bf16[128,768]{1,0:T(8,128)(2,1)}, u32[]{:S(2)}) copy-start(bf16[128,768]{1,0:T(8,128)(2,1)} %own_ref.1) | copy-start | bytes 589828
  12.8 14.4 %copy-start.2 = (bf16[320,384]{1,0:T(8,128)(2,1)S(1)}, bf16[320,384]{1,0:T(8,128)(2,1)}, u32[]{:S(2)}) copy-start(bf16[320,384]{1,0:T(8,128)(2,1)} %load.1.kv0) | copy-start | bytes 737284
  14.4 12.9 %collective-permute-start.6 = (bf16[160,384]{1,0:T(8,128)(2,1)S(1)}, bf16[160,384]{1,0:T(8,128)(2,1)S(1)}, u32[]{:S(2)}, u32[]{:S(2)}) collective-permute-start(bf16[160,384]{1,0:T(8,128)(2,1)S(1)} %get-tuple-element.45), channel_id=1, source_target_pairs={{0,4},{4,0},{8,12},{12,8},{16,20},{20,16},{24,28},{28,24},{1,5},{5... | collective-permute-start | bytes 368648 | tf_op jit(solution)/shard_map/ppermute | solution.py:35
  15.9 11.3 %collective-permute-start.7 = (bf16[160,384]{1,0:T(8,128)(2,1)S(1)}, bf16[160,384]{1,0:T(8,128)(2,1)S(1)}, u32[]{:S(2)}, u32[]{:S(2)}) collective-permute-start(bf16[160,384]{1,0:T(8,128)(2,1)S(1)} %get-tuple-element.46), channel_id=1, source_target_pairs={{0,8},{4,12},{8,0},{12,4},{16,24},{20,28},{24,16},{28,20},{1,9},{5... | collective-permute-start | bytes 368648 | tf_op jit(solution)/shard_map/ppermute | solution.py:35
  17.1 10.1 %collective-permute-start.5 = (bf16[128,384]{1,0:T(8,128)(2,1)S(1)}, bf16[128,384]{1,0:T(8,128)(2,1)S(1)}, u32[]{:S(2)}, u32[]{:S(2)}) collective-permute-start(bf16[128,384]{1,0:T(8,128)(2,1)S(1)} %copy-done.3), channel_id=1, source_target_pairs={{0,16},{4,20},{8,24},{12,28},{16,0},{20,4},{24,8},{28,12},{1,17},{... | collective-permute-start | bytes 294920 | tf_op jit(solution)/shard_map/ppermute | solution.py:35
  19.7 10.7 %collective-permute-start.9 = (bf16[128,384]{1,0:T(8,128)(2,1)S(1)}, bf16[128,384]{1,0:T(8,128)(2,1)S(1)}, u32[]{:S(2)}, u32[]{:S(2)}) collective-permute-start(bf16[128,384]{1,0:T(8,128)(2,1)S(1)} %dattn.1.d_own_ref), channel_id=1, source_target_pairs={{0,16},{4,20},{8,24},{12,28},{16,0},{20,4},{24,8},{28,12},{1,17},{... | collective-permute-start | bytes 294920 | tf_op jit(solution)/shard_map/ppermute | solution.py:35
  28.7 8.3 %collective-permute-start.8 = (bf16[384,128]{1,0:T(8,128)(2,1)S(1)}, bf16[384,128]{1,0:T(8,128)(2,1)S(1)}, u32[]{:S(2)}, u32[]{:S(2)}) collective-permute-start(bf16[384,128]{1,0:T(8,128)(2,1)S(1)} %get-tuple-element.51), channel_id=1, source_target_pairs={{0,16},{4,20},{8,24},{12,28},{16,0},{20,4},{24,8},{28,12},{1,17},{... | collective-permute-start | bytes 294920 | tf_op jit(solution)/shard_map/ppermute | solution.py:35
  30.8 10.4 %copy-start.1 = (bf16[384,3072]{1,0:T(8,128)(2,1)S(1)}, bf16[384,3072]{1,0:T(8,128)(2,1)}, u32[]{:S(2)}) copy-start(bf16[384,3072]{1,0:T(8,128)(2,1)} %w_ref.3) | copy-start | bytes 7077892
  30.8 5.0 %collective-permute-start.10 = (f32[16,256]{1,0:T(8,128)S(1)}, f32[16,256]{1,0:T(8,128)S(1)}, u32[]{:S(2)}, u32[]{:S(2)}) collective-permute-start(f32[16,256]{1,0:T(8,128)S(1)} %get-tuple-element.54.stats_ref), channel_id=1, source_target_pairs={{0,16},{4,20},{8,24},{12,28},{16,0},{20,4},{24,8},{28,12},{1,17},{... | collective-permute-start | bytes 49160 | tf_op jit(solution)/shard_map/ppermute | solution.py:35
  37.0 6.3 %collective-permute-start.15 = (bf16[320,384]{1,0:T(8,128)(2,1)S(1)}, bf16[320,384]{1,0:T(8,128)(2,1)S(1)}, u32[]{:S(2)}, u32[]{:S(2)}) collective-permute-start(bf16[320,384]{1,0:T(8,128)(2,1)S(1)} %get-tuple-element.66), channel_id=1, source_target_pairs={{0,4},{4,0},{8,12},{12,8},{16,20},{20,16},{24,28},{28,24},{1,5},{5... | collective-permute-start | bytes 737288 | tf_op jit(solution)/shard_map/ppermute | solution.py:35
  37.5 7.3 %collective-permute-start.16 = (bf16[320,384]{1,0:T(8,128)(2,1)S(1)}, bf16[320,384]{1,0:T(8,128)(2,1)S(1)}, u32[]{:S(2)}, u32[]{:S(2)}) collective-permute-start(bf16[320,384]{1,0:T(8,128)(2,1)S(1)} %get-tuple-element.67), channel_id=1, source_target_pairs={{0,8},{4,12},{8,0},{12,4},{16,24},{20,28},{24,16},{28,20},{1,9},{5... | collective-permute-start | bytes 737288 | tf_op jit(solution)/shard_map/ppermute | solution.py:35
  40.7 6.3 %collective-permute-start.13 = (bf16[128,384]{1,0:T(8,128)(2,1)S(1)}, bf16[128,384]{1,0:T(8,128)(2,1)S(1)}, u32[]{:S(2)}, u32[]{:S(2)}) collective-permute-start(bf16[128,384]{1,0:T(8,128)(2,1)S(1)} %get-tuple-element.63), channel_id=1, source_target_pairs={{0,16},{4,20},{8,24},{12,28},{16,0},{20,4},{24,8},{28,12},{1,17},{... | collective-permute-start | bytes 294920 | tf_op jit(solution)/shard_map/ppermute | solution.py:35
  41.8 7.2 %collective-permute-start.11 = (bf16[128,768]{1,0:T(8,128)(2,1)S(1)}, bf16[128,768]{1,0:T(8,128)(2,1)S(1)}, u32[]{:S(2)}, u32[]{:S(2)}) collective-permute-start(bf16[128,768]{1,0:T(8,128)(2,1)S(1)} %get-tuple-element.60), channel_id=1, source_target_pairs={{0,2},{1,3},{2,0},{3,1},{4,6},{5,7},{6,4},{7,5},{8,10},{9,11},{10,... | collective-permute-start | bytes 589832 | tf_op jit(solution)/shard_map/ppermute | solution.py:35
  43.2 7.4 %collective-permute-start.12 = (bf16[128,768]{1,0:T(8,128)(2,1)S(1)}, bf16[128,768]{1,0:T(8,128)(2,1)S(1)}, u32[]{:S(2)}, u32[]{:S(2)}) collective-permute-start(bf16[128,768]{1,0:T(8,128)(2,1)S(1)} %get-tuple-element.61), channel_id=1, source_target_pairs={{0,3},{1,2},{2,1},{3,0},{4,7},{5,6},{6,5},{7,4},{8,11},{9,10},{10,... | collective-permute-start | bytes 589832 | tf_op jit(solution)/shard_map/ppermute | solution.py:35
  43.2 7.3 %collective-permute-start.14 = (bf16[128,768]{1,0:T(8,128)(2,1)S(1)}, bf16[128,768]{1,0:T(8,128)(2,1)S(1)}, u32[]{:S(2)}, u32[]{:S(2)}) collective-permute-start(bf16[128,768]{1,0:T(8,128)(2,1)S(1)} %get-tuple-element.64), channel_id=1, source_target_pairs={{0,1},{1,0},{2,3},{3,2},{4,5},{5,4},{6,7},{7,6},{8,9},{9,8},{10,11... | collective-permute-start | bytes 589832 | tf_op jit(solution)/shard_map/ppermute | solution.py:35
  44.9 5.7 %collective-permute-start.17 = (bf16[160,384]{1,0:T(8,128)(2,1)S(1)}, bf16[160,384]{1,0:T(8,128)(2,1)S(1)}, u32[]{:S(2)}, u32[]{:S(2)}) collective-permute-start(bf16[160,384]{1,0:T(8,128)(2,1)S(1)} %get-tuple-element.70), channel_id=1, source_target_pairs={{0,8},{4,12},{8,0},{12,4},{16,24},{20,28},{24,16},{28,20},{1,9},{5... | collective-permute-start | bytes 368648 | tf_op jit(solution)/shard_map/ppermute | solution.py:35
  47.0 5.0 %collective-permute-start.18 = (bf16[160,384]{1,0:T(8,128)(2,1)S(1)}, bf16[160,384]{1,0:T(8,128)(2,1)S(1)}, u32[]{:S(2)}, u32[]{:S(2)}) collective-permute-start(bf16[160,384]{1,0:T(8,128)(2,1)S(1)} %get-tuple-element.71), channel_id=1, source_target_pairs={{0,4},{4,0},{8,12},{12,8},{16,20},{20,16},{24,28},{28,24},{1,5},{5... | collective-permute-start | bytes 368648 | tf_op jit(solution)/shard_map/ppermute | solution.py:35

commit v10 on v9

--- a/solution.py
+++ b/solution.py
@@ -83,10 +83,12 @@
     )(*arrays)
 
 
-def pass_keys_kernel(kv1, kv2, key_ref, value_ref):
-    keys = key_ref.shape[0]
-    key_ref[...] = kv2[:keys]
-    value_ref[...] = kv1[keys:]
+def pass_keys_kernel(kv2, key_ref):
+    key_ref[...] = kv2[: key_ref.shape[0]]
+
+
+def pass_values_kernel(kv2, value_ref):
+    value_ref[...] = kv2[value_ref.shape[0] :]
 
 
 def square_blocks(kv0, kv1, kv2, key3, value3):
@@ -126,16 +128,16 @@
 
 
 def scores_kernel(
-    limits_ref, q_own_ref, q_pair_ref, kv0, kv1, kv2, key3, value3, lse_ref, probs_ref
+    limits_ref, q_own_ref, q_pair_ref, kv0, kv1, kv2, key3, lse_ref, probs_ref
 ):
     rows = q_own_ref.shape[0]
     keys = key3.shape[0]
-    blocks = square_blocks(kv0, kv1, kv2, key3, value3)
+    blocks = [ref.at[:keys] for ref in (kv0, kv1, kv2)] + [key3]
     lse_ref[...] = jnp.zeros_like(lse_ref)
     for head in range(q_own_ref.shape[1] // HDIM):
         query = both_rows(q_own_ref, q_pair_ref, head)
         scores = []
-        for step, (key_ref, _) in enumerate(blocks):
+        for step, key_ref in enumerate(blocks):
             block = contract(head_slice(key_ref[...], head), query, 1, 1) * SCALE
             slot = lax.broadcasted_iota(jnp.int32, block.shape, 0)
             valid = slot < rows + limits_ref[step : step + 1]
@@ -284,6 +286,7 @@
     keys = rows + capacity
     share = grad_out.shape[1]
 
+    q_pair = swap(sec_q, "ctx", PAIR)
     grad_near = swap(grad_out, "head", 2)
     grad_core = swap(grad_out, "head", 1)
     grad_far = swap(grad_near, "head", 1)
@@ -297,12 +300,13 @@
         [shape((rows, width), BF16)],
         (grad_out, grad_core, grad_near, grad_far, w_out),
     )[0]
-    kv1, kv2, d_own, sec_q = lax.optimization_barrier((kv1, kv2, d_own, sec_q))
-    key3, value3 = local_call(
-        pass_keys_kernel, "pass_keys", 0.1, [shape((keys, width), BF16)] * 2, (kv1, kv2)
-    )
-    kvs = [kv0, kv1, kv2, swap(key3, "ctx", 1), swap(value3, "ctx", 2)]
-    q_pair = swap(sec_q, "ctx", PAIR)
+    kv2, d_own = lax.optimization_barrier((kv2, d_own))
+    key3 = local_call(pass_keys_kernel, "pass_keys", 0.1, [shape((keys, width), BF16)], (kv2,))[0]
+    kv2_kept, q_pair, _ = lax.optimization_barrier((kv2, q_pair, key3))
+    value3 = local_call(
+        pass_values_kernel, "pass_values", 1.0, [shape((keys, width), BF16)], (kv2_kept,)
+    )[0]
+    kvs = [kv0, kv1, kv2, swap(key3, "ctx", 1), swap(value3, "ctx", 1)]
     d_pair = swap(d_own, "ctx", PAIR)
     limits = local_call(
         limits_kernel,
@@ -317,7 +321,7 @@
         "scores",
         0.9,
         [shape((8, 2 * rows), F32), shape((heads * SQUARE * keys, 2 * rows), BF16)],
-        (limits, sec_q, q_pair, *kvs),
+        (limits, sec_q, q_pair, *kvs[:4]),
     )
     attn_own, attn_pair = local_call(
         attn_kernel,

time: 53.1 us -> 49.7 us (0.936)
  starting transfers between devices: 23.7 us -> 20.6 us
    ppermute x19, starting transfers between devices: 23.7 us -> 20.6 us  [swap(): return lax.ppermute(block, axis, [(i, i ^ bit) for i in range(count)])]
    pallas_call x10 -> x11, Pallas kernels: 6.02 us -> 6.03 us  [local_call(): pl.pallas_call(body, name=name, out_shape=out_shapes, in_specs=[pl.BlockS...]
  transfers between devices with their start and end apart: 19 -> 19, of which waited for: 12 -> 11; matrix products, arithmetic and copies ran while one was open for 0% -> 0% of each run, Pallas kernels for 13% -> 14%
where the time goes in v10:
time: 49.7 us; the launch traced here: 49.5 us
  starting transfers between devices  20.6 us (41%)
  waiting for transfers between devices  17.7 us (36%)
  Pallas kernels  7.69 us (15%)
  local copies, waits for them, and re-layouts  2.7 us (5%)
  between operations  0.8 us (2%)
    ppermute x19, starting transfers between devices, swap(): return lax.ppermute(block, axis, [(i, i ^ bit) for i in range(count)])  20.6 us
    ppermute x19, waiting for transfers between devices, swap(): return lax.ppermute(block, axis, [(i, i ^ bit) for i in range(count)])  17.7 us
    pallas_call x11, Pallas kernels, local_call(): pl.pallas_call(body, name=name, out_shape=out_shapes, in_specs=[pl.BlockS...  6.03 us
    unnamed x15, local copies, waits for them, and re-layouts  2.7 us
    pallas_call x1, Pallas kernels, load_keys(): pl.pallas_call(load_kernel, name='load', out_shape=jax.ShapeDtypeStruct((...  1.66 us
  transfers between devices with their start and end apart: 19, of which 11 were waited for; matrix products, arithmetic and copies ran while one was open for 0% of the time, Pallas kernels for 14%

profile of v10, /device:TPU:0, one launch (start us, length us, event | category | flops | bytes accessed | tf_op | source)
XLA Modules:
  0.0 49.5 jit_solution(497448299346978238)
XLA Ops:
  0.6 0.0 copy-start.3
  0.7 3.0 %collective-permute-start.2 = (bf16[128,768]{1,0:T(8,128)(2,1)}, bf16[128,768]{1,0:T(8,128)(2,1)S(1)}, u32[]{:S(2)}, u32[]{:S(2)}) collective-permute-start(bf16[128,768]{1,0:T(8,128)(2,1)} %own_ref.1), channel_id=1, source_target_pairs={{0,2},{1,3},{2,0},{3,1},{4,6},{5,7},{6,4},{7,5},{8,10},{9,11},{10,... | collective-permute-start | bytes 589832 | tf_op jit(solution)/shard_map/ppermute | solution.py:35
  3.7 1.7 %load.1.kv0 = bf16[320,384]{1,0:T(8,128)(2,1)} custom-call(bf16[128,384]{1,0:T(8,128)(2,1)} %k_ref.1, bf16[32,384]{1,0:T(8,128)(2,1)} %hk_ref.1, bf16[128,384]{1,0:T(8,128)(2,1)} %v_ref.1, bf16[32,384]{1,0:T(8,128)(2,1)} %hv_ref.1), custom_call_target="tpu_custom_call" | custom-call | bytes 5904000 | tf_op jit(solution)/shard_map/load/pallas_call | solution.py:74
  5.3 1.6 %collective-permute-start = (bf16[320,384]{1,0:T(8,128)(2,1)}, bf16[320,384]{1,0:T(8,128)(2,1)S(1)}, u32[]{:S(2)}, u32[]{:S(2)}) collective-permute-start(bf16[320,384]{1,0:T(8,128)(2,1)} %load.1.kv0), channel_id=1, source_target_pairs={{0,8},{4,12},{8,0},{12,4},{16,24},{20,28},{24,16},{28,20},{1,9},{5... | collective-permute-start | bytes 737288 | tf_op jit(solution)/shard_map/ppermute | solution.py:35
  7.0 0.0 collective-permute-start.1
  7.0 1.8 %collective-permute-done.2.near_ref = bf16[128,768]{1,0:T(8,128)(2,1)S(1)} collective-permute-done((bf16[128,768]{1,0:T(8,128)(2,1)}, bf16[128,768]{1,0:T(8,128)(2,1)S(1)}, u32[]{:S(2)}, u32[]{:S(2)}) %collective-permute-start.2) | collective-permute-done | bytes 196640 | tf_op jit(solution)/shard_map/ppermute | solution.py:35
  8.8 0.0 collective-permute-start.3
  8.8 1.8 %collective-permute-start.5 = (bf16[320,384]{1,0:T(8,128)(2,1)}, bf16[320,384]{1,0:T(8,128)(2,1)S(1)}, u32[]{:S(2)}, u32[]{:S(2)}) collective-permute-start(bf16[320,384]{1,0:T(8,128)(2,1)} %load.1.kv0), channel_id=1, source_target_pairs={{0,4},{4,0},{8,12},{12,8},{16,20},{20,16},{24,28},{28,24},{1,5},{5... | collective-permute-start | bytes 737288 | tf_op jit(solution)/shard_map/ppermute | solution.py:35
  10.6 2.6 %collective-permute-start.4 = (bf16[128,384]{1,0:T(8,128)(2,1)}, bf16[128,384]{1,0:T(8,128)(2,1)S(1)}, u32[]{:S(2)}, u32[]{:S(2)}) collective-permute-start(bf16[128,384]{1,0:T(8,128)(2,1)} %q_own_ref.3), channel_id=1, source_target_pairs={{0,16},{4,20},{8,24},{12,28},{16,0},{20,4},{24,8},{28,12},{1,17},{... | collective-permute-start | bytes 294920 | tf_op jit(solution)/shard_map/ppermute | solution.py:35
  13.1 0.0 collective-permute-done.1.core_ref
  13.1 0.0 collective-permute-done.3.far_ref
  13.2 1.7 %copy-done = bf16[384,3072]{1,0:T(8,128)(2,1)S(1)} copy-done((bf16[384,3072]{1,0:T(8,128)(2,1)S(1)}, bf16[384,3072]{1,0:T(8,128)(2,1)}, u32[]{:S(2)}) %copy-start) | copy-done | bytes 2359320
  14.8 0.9 %copy-done.4 = bf16[128,768]{1,0:T(8,128)(2,1)S(1)} copy-done((bf16[128,768]{1,0:T(8,128)(2,1)S(1)}, bf16[128,768]{1,0:T(8,128)(2,1)}, u32[]{:S(2)}) %copy-start.4) | copy-done | bytes 196632
  15.7 0.8 %dattn.1.d_own_ref = bf16[128,384]{1,0:T(8,128)(2,1)S(1)} custom-call(bf16[128,768]{1,0:T(8,128)(2,1)S(1)} %copy-done.4, bf16[128,768]{1,0:T(8,128)(2,1)S(1)} %collective-permute-done.1.core_ref, bf16[128,768]{1,0:T(8,128)(2,1)S(1)} %collective-permute-done.2.near_ref, bf16[128,768]{1,0:T(8,128)(2,1)S(1)} %collective-permute-done.3.far_ref, ...), custom_call_target="tpu_custom_call" | custom-call | bytes 2952000 | tf_op jit(solution)/shard_map/dattn/pallas_call | solution.py:44
  16.6 0.0 collective-permute-done.kv2
  16.6 0.6 %collective-permute-start.6 = (bf16[160,384]{1,0:T(8,128)(2,1)S(1)}, bf16[160,384]{1,0:T(8,128)(2,1)S(1)}, u32[]{:S(2)}, u32[]{:S(2)}) collective-permute-start(bf16[160,384]{1,0:T(8,128)(2,1)S(1)} %pass_keys.1), channel_id=1, source_target_pairs={{0,4},{4,0},{8,12},{12,8},{16,20},{20,16},{24,28},{28,24},{1,5},{5... | collective-permute-start | bytes 368648 | tf_op jit(solution)/shard_map/ppermute | solution.py:35
  17.2 1.5 %collective-permute-done.4.q_pair_ref = bf16[128,384]{1,0:T(8,128)(2,1)S(1)} collective-permute-done((bf16[128,384]{1,0:T(8,128)(2,1)}, bf16[128,384]{1,0:T(8,128)(2,1)S(1)}, u32[]{:S(2)}, u32[]{:S(2)}) %collective-permute-start.4) | collective-permute-done | bytes 98336 | tf_op jit(solution)/shard_map/ppermute | solution.py:35
  18.7 0.5 %collective-permute-start.7 = (bf16[160,384]{1,0:T(8,128)(2,1)S(1)}, bf16[160,384]{1,0:T(8,128)(2,1)S(1)}, u32[]{:S(2)}, u32[]{:S(2)}) collective-permute-start(bf16[160,384]{1,0:T(8,128)(2,1)S(1)} %pass_values.1), channel_id=1, source_target_pairs={{0,4},{4,0},{8,12},{12,8},{16,20},{20,16},{24,28},{28,24},{1,5},{5... | collective-permute-start | bytes 368648 | tf_op jit(solution)/shard_map/ppermute | solution.py:35
  19.2 0.6 %collective-permute-start.9 = (bf16[128,384]{1,0:T(8,128)(2,1)S(1)}, bf16[128,384]{1,0:T(8,128)(2,1)S(1)}, u32[]{:S(2)}, u32[]{:S(2)}) collective-permute-start(bf16[128,384]{1,0:T(8,128)(2,1)S(1)} %dattn.1.d_own_ref), channel_id=1, source_target_pairs={{0,16},{4,20},{8,24},{12,28},{16,0},{20,4},{24,8},{28,12},{1,17},{... | collective-permute-start | bytes 294920 | tf_op jit(solution)/shard_map/ppermute | solution.py:35
  19.9 0.1 copy.15.levels_ref
  20.0 0.6 %limits.1.limits_ref = s32[8,256]{1,0:T(8,128)S(1)} custom-call(s32[8,2]{1,0:T(8,128)S(1)} %copy.15.levels_ref, s32[8]{0:T(128)S(1)} %copy-done.5), custom_call_target="tpu_custom_call" | custom-call | bytes 2214000 | tf_op jit(solution)/shard_map/limits/pallas_call | solution.py:44
  20.6 0.0 collective-permute-done.5.kv1
  20.6 2.3 %collective-permute-done.6.key3 = bf16[160,384]{1,0:T(8,128)(2,1)S(1)} collective-permute-done((bf16[160,384]{1,0:T(8,128)(2,1)S(1)}, bf16[160,384]{1,0:T(8,128)(2,1)S(1)}, u32[]{:S(2)}, u32[]{:S(2)}) %collective-permute-start.6) | collective-permute-done | bytes 122912 | tf_op jit(solution)/shard_map/ppermute | solution.py:35
  22.9 1.0 %scores.1 = (f32[8,256]{1,0:T(8,128)S(1)}, bf16[1920,256]{1,0:T(8,128)(2,1)S(1)}) custom-call(s32[8,256]{1,0:T(8,128)S(1)} %limits.1.limits_ref, bf16[128,384]{1,0:T(8,128)(2,1)S(1)} %copy-done.3, bf16[128,384]{1,0:T(8,128)(2,1)S(1)} %collective-permute-done.4.q_pair_ref, bf16[320,384]{1,0:T(8,128)(2,1)S(1)} %copy-done.2, ...), custom_call_target="tpu_custom_call" | custom-call | bytes 3321000 | tf_op jit(solution)/shard_map/scores/pallas_call | solution.py:44
  23.9 0.6 %collective-permute-done.7.value3 = bf16[160,384]{1,0:T(8,128)(2,1)S(1)} collective-permute-done((bf16[160,384]{1,0:T(8,128)(2,1)S(1)}, bf16[160,384]{1,0:T(8,128)(2,1)S(1)}, u32[]{:S(2)}, u32[]{:S(2)}) %collective-permute-start.7) | collective-permute-done | bytes 122912 | tf_op jit(solution)/shard_map/ppermute | solution.py:35
  24.5 0.4 attn.1
  24.9 1.0 %collective-permute-start.8 = (bf16[384,128]{1,0:T(8,128)(2,1)S(1)}, bf16[384,128]{1,0:T(8,128)(2,1)S(1)}, u32[]{:S(2)}, u32[]{:S(2)}) collective-permute-start(bf16[384,128]{1,0:T(8,128)(2,1)S(1)} %get-tuple-element.47), channel_id=1, source_target_pairs={{0,16},{4,20},{8,24},{12,28},{16,0},{20,4},{24,8},{28,12},{1,17},{... | collective-permute-start | bytes 294920 | tf_op jit(solution)/shard_map/ppermute | solution.py:35
  26.0 0.6 %collective-permute-done.9.d_pair_ref = bf16[128,384]{1,0:T(8,128)(2,1)S(1)} collective-permute-done((bf16[128,384]{1,0:T(8,128)(2,1)S(1)}, bf16[128,384]{1,0:T(8,128)(2,1)S(1)}, u32[]{:S(2)}, u32[]{:S(2)}) %collective-permute-start.9) | collective-permute-done | bytes 98336 | tf_op jit(solution)/shard_map/ppermute | solution.py:35
  26.5 0.4 delta.1
  27.0 0.0 copy-start.1
  27.0 1.4 %collective-permute-start.10 = (f32[16,256]{1,0:T(8,128)S(1)}, f32[16,256]{1,0:T(8,128)S(1)}, u32[]{:S(2)}, u32[]{:S(2)}) collective-permute-start(f32[16,256]{1,0:T(8,128)S(1)} %get-tuple-element.50.stats_ref), channel_id=1, source_target_pairs={{0,16},{4,20},{8,24},{12,28},{16,0},{20,4},{24,8},{28,12},{1,17},{... | collective-permute-start | bytes 49160 | tf_op jit(solution)/shard_map/ppermute | solution.py:35
  28.4 3.9 %collective-permute-done.10.stats_pair_ref = f32[16,256]{1,0:T(8,128)S(1)} collective-permute-done((f32[16,256]{1,0:T(8,128)S(1)}, f32[16,256]{1,0:T(8,128)S(1)}, u32[]{:S(2)}, u32[]{:S(2)}) %collective-permute-start.10) | collective-permute-done | bytes 16416 | tf_op jit(solution)/shard_map/ppermute | solution.py:35
  32.3 1.1 %backward.1 = (f32[128,384]{1,0:T(8,128)S(1)}, bf16[128,384]{1,0:T(8,128)(2,1)S(1)}, f32[320,384]{1,0:T(8,128)S(1)}, bf16[320,384]{1,0:T(8,128)(2,1)S(1)}, bf16[...) custom-call(bf16[128,384]{1,0:T(8,128)(2,1)S(1)} %copy-done.3, ...), custom_call_target="tpu_custom_call" | custom-call | bytes 4059000 | tf_op jit(solution)/shard_map/backward/pallas_call | solution.py:44
  33.4 1.0 %collective-permute-start.15 = (bf16[320,384]{1,0:T(8,128)(2,1)S(1)}, bf16[320,384]{1,0:T(8,128)(2,1)S(1)}, u32[]{:S(2)}, u32[]{:S(2)}) collective-permute-start(bf16[320,384]{1,0:T(8,128)(2,1)S(1)} %get-tuple-element.62), channel_id=1, source_target_pairs={{0,4},{4,0},{8,12},{12,8},{16,20},{20,16},{24,28},{28,24},{1,5},{5... | collective-permute-start | bytes 737288 | tf_op jit(solution)/shard_map/ppermute | solution.py:35
  34.4 1.0 %collective-permute-start.16 = (bf16[320,384]{1,0:T(8,128)(2,1)S(1)}, bf16[320,384]{1,0:T(8,128)(2,1)S(1)}, u32[]{:S(2)}, u32[]{:S(2)}) collective-permute-start(bf16[320,384]{1,0:T(8,128)(2,1)S(1)} %get-tuple-element.63), channel_id=1, source_target_pairs={{0,8},{4,12},{8,0},{12,4},{16,24},{20,28},{24,16},{28,20},{1,9},{5... | collective-permute-start | bytes 737288 | tf_op jit(solution)/shard_map/ppermute | solution.py:35
  35.5 2.4 %collective-permute-start.13 = (bf16[128,384]{1,0:T(8,128)(2,1)S(1)}, bf16[128,384]{1,0:T(8,128)(2,1)S(1)}, u32[]{:S(2)}, u32[]{:S(2)}) collective-permute-start(bf16[128,384]{1,0:T(8,128)(2,1)S(1)} %get-tuple-element.59), channel_id=1, source_target_pairs={{0,16},{4,20},{8,24},{12,28},{16,0},{20,4},{24,8},{28,12},{1,17},{... | collective-permute-start | bytes 294920 | tf_op jit(solution)/shard_map/ppermute | solution.py:35
  37.9 0.6 %project.1 = (f32[128,768]{1,0:T(8,128)S(1)}, bf16[128,768]{1,0:T(8,128)(2,1)S(1)}, bf16[128,768]{1,0:T(8,128)(2,1)S(1)}, bf16[128,768]{1,0:T(8,128)(2,1)S(1)}) custom-call(f32[384,128]{1,0:T(8,128)S(1)} %get-tuple-element.46.own_ref, bf16[384,128]{1,0:T(8,128)(2,1)S(1)} %collective-permute-done.8.pair_ref, f32[16,256]{1,0:T(8,128)S(1)} %get-tuple-element.50.stats_ref, ...), custom_call_target="tpu_custom_call" | custom-call | bytes 2214000 | tf_op jit(solution)/shard_map/project/pallas_call | solution.py:44
  38.5 1.6 %collective-permute-start.11 = (bf16[128,768]{1,0:T(8,128)(2,1)S(1)}, bf16[128,768]{1,0:T(8,128)(2,1)S(1)}, u32[]{:S(2)}, u32[]{:S(2)}) collective-permute-start(bf16[128,768]{1,0:T(8,128)(2,1)S(1)} %get-tuple-element.56), channel_id=1, source_target_pairs={{0,2},{1,3},{2,0},{3,1},{4,6},{5,7},{6,4},{7,5},{8,10},{9,11},{10,... | collective-permute-start | bytes 589832 | tf_op jit(solution)/shard_map/ppermute | solution.py:35
  40.1 0.6 %collective-permute-start.14 = (bf16[128,768]{1,0:T(8,128)(2,1)S(1)}, bf16[128,768]{1,0:T(8,128)(2,1)S(1)}, u32[]{:S(2)}, u32[]{:S(2)}) collective-permute-start(bf16[128,768]{1,0:T(8,128)(2,1)S(1)} %get-tuple-element.60), channel_id=1, source_target_pairs={{0,1},{1,0},{2,3},{3,2},{4,5},{5,4},{6,7},{7,6},{8,9},{9,8},{10,11... | collective-permute-start | bytes 589832 | tf_op jit(solution)/shard_map/ppermute | solution.py:35
  40.7 2.8 %collective-permute-done.16.got_v_ref = bf16[320,384]{1,0:T(8,128)(2,1)S(1)} collective-permute-done((bf16[320,384]{1,0:T(8,128)(2,1)S(1)}, bf16[320,384]{1,0:T(8,128)(2,1)S(1)}, u32[]{:S(2)}, u32[]{:S(2)}) %collective-permute-start.16) | collective-permute-done | bytes 245792 | tf_op jit(solution)/shard_map/ppermute | solution.py:35
  43.6 0.1 collective-permute-start.17
  43.7 0.7 %collective-permute-start.18 = (bf16[160,384]{1,0:T(8,128)(2,1)S(1)}, bf16[160,384]{1,0:T(8,128)(2,1)S(1)}, u32[]{:S(2)}, u32[]{:S(2)}) collective-permute-start(bf16[160,384]{1,0:T(8,128)(2,1)S(1)} %get-tuple-element.67), channel_id=1, source_target_pairs={{0,4},{4,0},{8,12},{12,8},{16,20},{20,16},{24,28},{28,24},{1,5},{5... | collective-permute-start | bytes 368648 | tf_op jit(solution)/shard_map/ppermute | solution.py:35
  44.3 1.1 %collective-permute-done.11.near_ref = bf16[128,768]{1,0:T(8,128)(2,1)S(1)} collective-permute-done((bf16[128,768]{1,0:T(8,128)(2,1)S(1)}, bf16[128,768]{1,0:T(8,128)(2,1)S(1)}, u32[]{:S(2)}, u32[]{:S(2)}) %collective-permute-start.11) | collective-permute-done | bytes 196640 | tf_op jit(solution)/shard_map/ppermute | solution.py:35
  45.5 2.0 %collective-permute-done.12.far_ref = bf16[128,768]{1,0:T(8,128)(2,1)S(1)} collective-permute-done((bf16[128,768]{1,0:T(8,128)(2,1)S(1)}, bf16[128,768]{1,0:T(8,128)(2,1)S(1)}, u32[]{:S(2)}, u32[]{:S(2)}) %collective-permute-start.12) | collective-permute-done | bytes 196640 | tf_op jit(solution)/shard_map/ppermute | solution.py:35
  47.5 0.0 collective-permute-done.14.core_ref
  47.5 1.0 %collective-permute-done.17.rest_k_ref = bf16[160,384]{1,0:T(8,128)(2,1)S(1)} collective-permute-done((bf16[160,384]{1,0:T(8,128)(2,1)S(1)}, bf16[160,384]{1,0:T(8,128)(2,1)S(1)}, u32[]{:S(2)}, u32[]{:S(2)}) %collective-permute-start.17) | collective-permute-done | bytes 122912 | tf_op jit(solution)/shard_map/ppermute | solution.py:35
  48.5 0.1 collective-permute-done.18.rest_v_ref
  48.6 0.9 %finish.1 = (bf16[128,384]{1,0:T(8,128)(2,1)}, bf16[128,384]{1,0:T(8,128)(2,1)}, bf16[128,384]{1,0:T(8,128)(2,1)}, bf16[32,384]{1,0:T(8,128)(2,1)}, bf16[32,384]{1,0:T(8,128)(2,1)}, /*index=5*/bf16[128,768]{1,0:T(8,128)(2,1)}) custom-call(f32[128,768]{1,0:T(8,128)S(1)} %get-tuple-element.55.keep_ref, bf16[128,768]{1,0:T(8,128)(2,1)S(1)} %collective-permute-done.11.near_ref, ...), custom_call_target="tpu_custom_call" | custom-call | bytes 3321000 | tf_op jit(solution)/shard_map/finish/pallas_call | solution.py:44
  (17 shorter events, 0.1 us)
Async XLA Ops:
  0.6 22.2 %copy-start.3 = (bf16[128,384]{1,0:T(8,128)(2,1)S(1)}, bf16[128,384]{1,0:T(8,128)(2,1)}, u32[]{:S(2)}) copy-start(bf16[128,384]{1,0:T(8,128)(2,1)} %q_own_ref.3) | copy-start | bytes 294916
  0.6 19.2 %copy-start.6 = (s32[8,2]{0,1:T(2,128)S(1)}, s32[8,2]{0,1:T(2,128)}, u32[]{:S(2)}) copy-start(s32[8,2]{0,1:T(2,128)} %param.14) | copy-start | bytes 196
  0.7 19.3 %copy-start.5 = (s32[8]{0:T(128)S(1)}, s32[8]{0:T(128)}, u32[]{:S(2)}) copy-start(s32[8]{0:T(128)} %counts_ref.1) | copy-start | bytes 100
  0.7 8.1 %collective-permute-start.2 = (bf16[128,768]{1,0:T(8,128)(2,1)}, bf16[128,768]{1,0:T(8,128)(2,1)S(1)}, u32[]{:S(2)}, u32[]{:S(2)}) collective-permute-start(bf16[128,768]{1,0:T(8,128)(2,1)} %own_ref.1), channel_id=1, source_target_pairs={{0,2},{1,3},{2,0},{3,1},{4,6},{5,7},{6,4},{7,5},{8,10},{9,11},{10,... | collective-permute-start | bytes 589832 | tf_op jit(solution)/shard_map/ppermute | solution.py:35
  5.3 11.2 %collective-permute-start = (bf16[320,384]{1,0:T(8,128)(2,1)}, bf16[320,384]{1,0:T(8,128)(2,1)S(1)}, u32[]{:S(2)}, u32[]{:S(2)}) collective-permute-start(bf16[320,384]{1,0:T(8,128)(2,1)} %load.1.kv0), channel_id=1, source_target_pairs={{0,8},{4,12},{8,0},{12,4},{16,24},{20,28},{24,16},{28,20},{1,9},{5... | collective-permute-start | bytes 737288 | tf_op jit(solution)/shard_map/ppermute | solution.py:35
  7.0 6.2 %collective-permute-start.1 = (bf16[128,768]{1,0:T(8,128)(2,1)}, bf16[128,768]{1,0:T(8,128)(2,1)S(1)}, u32[]{:S(2)}, u32[]{:S(2)}) collective-permute-start(bf16[128,768]{1,0:T(8,128)(2,1)} %own_ref.1), channel_id=1, source_target_pairs={{0,1},{1,0},{2,3},{3,2},{4,5},{5,4},{6,7},{7,6},{8,9},{9,8},{10,11... | collective-permute-start | bytes 589832 | tf_op jit(solution)/shard_map/ppermute | solution.py:35
  8.8 4.4 %collective-permute-start.3 = (bf16[128,768]{1,0:T(8,128)(2,1)S(1)}, bf16[128,768]{1,0:T(8,128)(2,1)S(1)}, u32[]{:S(2)}, u32[]{:S(2)}) collective-permute-start(bf16[128,768]{1,0:T(8,128)(2,1)S(1)} %collective-permute-done.2.near_ref), channel_id=1, source_target_pairs={{0,1},{1,0},{2,3},{3,2},{4,5},{5,4},{6,7},{7,6},{8,9},{9,8},{10,11... | collective-permute-start | bytes 589832 | tf_op jit(solution)/shard_map/ppermute | solution.py:35
  8.8 11.8 %collective-permute-start.5 = (bf16[320,384]{1,0:T(8,128)(2,1)}, bf16[320,384]{1,0:T(8,128)(2,1)S(1)}, u32[]{:S(2)}, u32[]{:S(2)}) collective-permute-start(bf16[320,384]{1,0:T(8,128)(2,1)} %load.1.kv0), channel_id=1, source_target_pairs={{0,4},{4,0},{8,12},{12,8},{16,20},{20,16},{24,28},{28,24},{1,5},{5... | collective-permute-start | bytes 737288 | tf_op jit(solution)/shard_map/ppermute | solution.py:35
  10.6 8.1 %collective-permute-start.4 = (bf16[128,384]{1,0:T(8,128)(2,1)}, bf16[128,384]{1,0:T(8,128)(2,1)S(1)}, u32[]{:S(2)}, u32[]{:S(2)}) collective-permute-start(bf16[128,384]{1,0:T(8,128)(2,1)} %q_own_ref.3), channel_id=1, source_target_pairs={{0,16},{4,20},{8,24},{12,28},{16,0},{20,4},{24,8},{28,12},{1,17},{... | collective-permute-start | bytes 294920 | tf_op jit(solution)/shard_map/ppermute | solution.py:35
  13.2 1.7 %copy-start = (bf16[384,3072]{1,0:T(8,128)(2,1)S(1)}, bf16[384,3072]{1,0:T(8,128)(2,1)}, u32[]{:S(2)}) copy-start(bf16[384,3072]{1,0:T(8,128)(2,1)} %w_ref.3) | copy-start | bytes 7077892
  14.8 0.9 %copy-start.4 = (bf16[128,768]{1,0:T(8,128)(2,1)S(1)}, bf16[128,768]{1,0:T(8,128)(2,1)}, u32[]{:S(2)}) copy-start(bf16[128,768]{1,0:T(8,128)(2,1)} %own_ref.1) | copy-start | bytes 589828
  15.7 7.1 %copy-start.2 = (bf16[320,384]{1,0:T(8,128)(2,1)S(1)}, bf16[320,384]{1,0:T(8,128)(2,1)}, u32[]{:S(2)}) copy-start(bf16[320,384]{1,0:T(8,128)(2,1)} %load.1.kv0) | copy-start | bytes 737284
  16.6 6.3 %collective-permute-start.6 = (bf16[160,384]{1,0:T(8,128)(2,1)S(1)}, bf16[160,384]{1,0:T(8,128)(2,1)S(1)}, u32[]{:S(2)}, u32[]{:S(2)}) collective-permute-start(bf16[160,384]{1,0:T(8,128)(2,1)S(1)} %pass_keys.1), channel_id=1, source_target_pairs={{0,4},{4,0},{8,12},{12,8},{16,20},{20,16},{24,28},{28,24},{1,5},{5... | collective-permute-start | bytes 368648 | tf_op jit(solution)/shard_map/ppermute | solution.py:35
  18.7 5.8 %collective-permute-start.7 = (bf16[160,384]{1,0:T(8,128)(2,1)S(1)}, bf16[160,384]{1,0:T(8,128)(2,1)S(1)}, u32[]{:S(2)}, u32[]{:S(2)}) collective-permute-start(bf16[160,384]{1,0:T(8,128)(2,1)S(1)} %pass_values.1), channel_id=1, source_target_pairs={{0,4},{4,0},{8,12},{12,8},{16,20},{20,16},{24,28},{28,24},{1,5},{5... | collective-permute-start | bytes 368648 | tf_op jit(solution)/shard_map/ppermute | solution.py:35
  19.2 7.3 %collective-permute-start.9 = (bf16[128,384]{1,0:T(8,128)(2,1)S(1)}, bf16[128,384]{1,0:T(8,128)(2,1)S(1)}, u32[]{:S(2)}, u32[]{:S(2)}) collective-permute-start(bf16[128,384]{1,0:T(8,128)(2,1)S(1)} %dattn.1.d_own_ref), channel_id=1, source_target_pairs={{0,16},{4,20},{8,24},{12,28},{16,0},{20,4},{24,8},{28,12},{1,17},{... | collective-permute-start | bytes 294920 | tf_op jit(solution)/shard_map/ppermute | solution.py:35
  24.9 8.5 %collective-permute-start.8 = (bf16[384,128]{1,0:T(8,128)(2,1)S(1)}, bf16[384,128]{1,0:T(8,128)(2,1)S(1)}, u32[]{:S(2)}, u32[]{:S(2)}) collective-permute-start(bf16[384,128]{1,0:T(8,128)(2,1)S(1)} %get-tuple-element.47), channel_id=1, source_target_pairs={{0,16},{4,20},{8,24},{12,28},{16,0},{20,4},{24,8},{28,12},{1,17},{... | collective-permute-start | bytes 294920 | tf_op jit(solution)/shard_map/ppermute | solution.py:35
  27.0 10.9 %copy-start.1 = (bf16[384,3072]{1,0:T(8,128)(2,1)S(1)}, bf16[384,3072]{1,0:T(8,128)(2,1)}, u32[]{:S(2)}) copy-start(bf16[384,3072]{1,0:T(8,128)(2,1)} %w_ref.3) | copy-start | bytes 7077892
  27.0 5.3 %collective-permute-start.10 = (f32[16,256]{1,0:T(8,128)S(1)}, f32[16,256]{1,0:T(8,128)S(1)}, u32[]{:S(2)}, u32[]{:S(2)}) collective-permute-start(f32[16,256]{1,0:T(8,128)S(1)} %get-tuple-element.50.stats_ref), channel_id=1, source_target_pairs={{0,16},{4,20},{8,24},{12,28},{16,0},{20,4},{24,8},{28,12},{1,17},{... | collective-permute-start | bytes 49160 | tf_op jit(solution)/shard_map/ppermute | solution.py:35
  33.4 6.7 %collective-permute-start.15 = (bf16[320,384]{1,0:T(8,128)(2,1)S(1)}, bf16[320,384]{1,0:T(8,128)(2,1)S(1)}, u32[]{:S(2)}, u32[]{:S(2)}) collective-permute-start(bf16[320,384]{1,0:T(8,128)(2,1)S(1)} %get-tuple-element.62), channel_id=1, source_target_pairs={{0,4},{4,0},{8,12},{12,8},{16,20},{20,16},{24,28},{28,24},{1,5},{5... | collective-permute-start | bytes 737288 | tf_op jit(solution)/shard_map/ppermute | solution.py:35
  34.4 9.1 %collective-permute-start.16 = (bf16[320,384]{1,0:T(8,128)(2,1)S(1)}, bf16[320,384]{1,0:T(8,128)(2,1)S(1)}, u32[]{:S(2)}, u32[]{:S(2)}) collective-permute-start(bf16[320,384]{1,0:T(8,128)(2,1)S(1)} %get-tuple-element.63), channel_id=1, source_target_pairs={{0,8},{4,12},{8,0},{12,4},{16,24},{20,28},{24,16},{28,20},{1,9},{5... | collective-permute-start | bytes 737288 | tf_op jit(solution)/shard_map/ppermute | solution.py:35
  35.5 8.2 %collective-permute-start.13 = (bf16[128,384]{1,0:T(8,128)(2,1)S(1)}, bf16[128,384]{1,0:T(8,128)(2,1)S(1)}, u32[]{:S(2)}, u32[]{:S(2)}) collective-permute-start(bf16[128,384]{1,0:T(8,128)(2,1)S(1)} %get-tuple-element.59), channel_id=1, source_target_pairs={{0,16},{4,20},{8,24},{12,28},{16,0},{20,4},{24,8},{28,12},{1,17},{... | collective-permute-start | bytes 294920 | tf_op jit(solution)/shard_map/ppermute | solution.py:35
  38.5 6.9 %collective-permute-start.11 = (bf16[128,768]{1,0:T(8,128)(2,1)S(1)}, bf16[128,768]{1,0:T(8,128)(2,1)S(1)}, u32[]{:S(2)}, u32[]{:S(2)}) collective-permute-start(bf16[128,768]{1,0:T(8,128)(2,1)S(1)} %get-tuple-element.56), channel_id=1, source_target_pairs={{0,2},{1,3},{2,0},{3,1},{4,6},{5,7},{6,4},{7,5},{8,10},{9,11},{10,... | collective-permute-start | bytes 589832 | tf_op jit(solution)/shard_map/ppermute | solution.py:35
  40.1 7.4 %collective-permute-start.12 = (bf16[128,768]{1,0:T(8,128)(2,1)S(1)}, bf16[128,768]{1,0:T(8,128)(2,1)S(1)}, u32[]{:S(2)}, u32[]{:S(2)}) collective-permute-start(bf16[128,768]{1,0:T(8,128)(2,1)S(1)} %get-tuple-element.57), channel_id=1, source_target_pairs={{0,3},{1,2},{2,1},{3,0},{4,7},{5,6},{6,5},{7,4},{8,11},{9,10},{10,... | collective-permute-start | bytes 589832 | tf_op jit(solution)/shard_map/ppermute | solution.py:35
  40.1 7.4 %collective-permute-start.14 = (bf16[128,768]{1,0:T(8,128)(2,1)S(1)}, bf16[128,768]{1,0:T(8,128)(2,1)S(1)}, u32[]{:S(2)}, u32[]{:S(2)}) collective-permute-start(bf16[128,768]{1,0:T(8,128)(2,1)S(1)} %get-tuple-element.60), channel_id=1, source_target_pairs={{0,1},{1,0},{2,3},{3,2},{4,5},{5,4},{6,7},{7,6},{8,9},{9,8},{10,11... | collective-permute-start | bytes 589832 | tf_op jit(solution)/shard_map/ppermute | solution.py:35
  43.6 4.9 %collective-permute-start.17 = (bf16[160,384]{1,0:T(8,128)(2,1)S(1)}, bf16[160,384]{1,0:T(8,128)(2,1)S(1)}, u32[]{:S(2)}, u32[]{:S(2)}) collective-permute-start(bf16[160,384]{1,0:T(8,128)(2,1)S(1)} %get-tuple-element.66), channel_id=1, source_target_pairs={{0,8},{4,12},{8,0},{12,4},{16,24},{20,28},{24,16},{28,20},{1,9},{5... | collective-permute-start | bytes 368648 | tf_op jit(solution)/shard_map/ppermute | solution.py:35
  43.7 4.9 %collective-permute-start.18 = (bf16[160,384]{1,0:T(8,128)(2,1)S(1)}, bf16[160,384]{1,0:T(8,128)(2,1)S(1)}, u32[]{:S(2)}, u32[]{:S(2)}) collective-permute-start(bf16[160,384]{1,0:T(8,128)(2,1)S(1)} %get-tuple-element.67), channel_id=1, source_target_pairs={{0,4},{4,0},{8,12},{12,8},{16,20},{20,16},{24,28},{28,24},{1,5},{5... | collective-permute-start | bytes 368648 | tf_op jit(solution)/shard_map/ppermute | solution.py:35

commit v11 on v10

--- a/solution.py
+++ b/solution.py
@@ -293,6 +293,12 @@
     kv0 = load_keys(sec_k, hist_k, sec_v, hist_v)
     kv2 = swap(kv0, "ctx", 2)
     kv1 = swap(kv0, "ctx", 1)
+    kv2, q_pair = lax.optimization_barrier((kv2, q_pair))
+    key3 = local_call(pass_keys_kernel, "pass_keys", 0.1, [shape((keys, width), BF16)], (kv2,))[0]
+    value3 = local_call(
+        pass_values_kernel, "pass_values", 0.1, [shape((keys, width), BF16)], (kv2,)
+    )[0]
+    kvs = [kv0, kv1, kv2, swap(key3, "ctx", 1), swap(value3, "ctx", 1)]
     d_own = local_call(
         dattn_kernel,
         "dattn",
@@ -300,13 +306,6 @@
         [shape((rows, width), BF16)],
         (grad_out, grad_core, grad_near, grad_far, w_out),
     )[0]
-    kv2, d_own = lax.optimization_barrier((kv2, d_own))
-    key3 = local_call(pass_keys_kernel, "pass_keys", 0.1, [shape((keys, width), BF16)], (kv2,))[0]
-    kv2_kept, q_pair, _ = lax.optimization_barrier((kv2, q_pair, key3))
-    value3 = local_call(
-        pass_values_kernel, "pass_values", 1.0, [shape((keys, width), BF16)], (kv2_kept,)
-    )[0]
-    kvs = [kv0, kv1, kv2, swap(key3, "ctx", 1), swap(value3, "ctx", 1)]
     d_pair = swap(d_own, "ctx", PAIR)
     limits = local_call(
         limits_kernel,

time: 49.7 us -> 53.3 us (1.072)
  the two profiles are of different devices: /device:TPU:0 before, /device:TPU:1 now
where the time goes in v11:
time: 53.3 us; the launch traced here: 53.1 us
  starting transfers between devices  29.3 us (55%)
  waiting for transfers between devices  12.5 us (23%)
  Pallas kernels  7.71 us (14%)
  local copies, waits for them, and re-layouts  2.69 us (5%)
  between operations  0.85 us (2%)
    ppermute x19, starting transfers between devices, swap(): return lax.ppermute(block, axis, [(i, i ^ bit) for i in range(count)])  29.3 us
    ppermute x19, waiting for transfers between devices, swap(): return lax.ppermute(block, axis, [(i, i ^ bit) for i in range(count)])  12.5 us
    pallas_call x11, Pallas kernels, local_call(): pl.pallas_call(body, name=name, out_shape=out_shapes, in_specs=[pl.BlockS...  6.05 us
    unnamed x15, local copies, waits for them, and re-layouts  2.69 us
    pallas_call x1, Pallas kernels, load_keys(): pl.pallas_call(load_kernel, name='load', out_shape=jax.ShapeDtypeStruct((...  1.66 us
  transfers between devices with their start and end apart: 19, of which 3 were waited for; matrix products, arithmetic and copies ran while one was open for 0% of the time, Pallas kernels for 13%

profile of v11, /device:TPU:1, one launch (start us, length us, event | category | flops | bytes accessed | tf_op | source)
XLA Modules:
  0.0 53.1 jit_solution(2148803522573451183)
XLA Ops:
  0.6 0.0 copy-start.3
  0.7 2.1 %collective-permute-start.7 = (bf16[128,768]{1,0:T(8,128)(2,1)}, bf16[128,768]{1,0:T(8,128)(2,1)S(1)}, u32[]{:S(2)}, u32[]{:S(2)}) collective-permute-start(bf16[128,768]{1,0:T(8,128)(2,1)} %own_ref.1), channel_id=1, source_target_pairs={{0,2},{1,3},{2,0},{3,1},{4,6},{5,7},{6,4},{7,5},{8,10},{9,11},{10,... | collective-permute-start | bytes 589832 | tf_op jit(solution)/shard_map/ppermute | solution.py:35
  2.8 1.7 %load.1.kv0 = bf16[320,384]{1,0:T(8,128)(2,1)} custom-call(bf16[128,384]{1,0:T(8,128)(2,1)} %k_ref.1, bf16[32,384]{1,0:T(8,128)(2,1)} %hk_ref.1, bf16[128,384]{1,0:T(8,128)(2,1)} %v_ref.1, bf16[32,384]{1,0:T(8,128)(2,1)} %hv_ref.1), custom_call_target="tpu_custom_call" | custom-call | bytes 5904000 | tf_op jit(solution)/shard_map/load/pallas_call | solution.py:74
  4.5 1.4 %collective-permute-start = (bf16[320,384]{1,0:T(8,128)(2,1)}, bf16[320,384]{1,0:T(8,128)(2,1)S(1)}, u32[]{:S(2)}, u32[]{:S(2)}) collective-permute-start(bf16[320,384]{1,0:T(8,128)(2,1)} %load.1.kv0), channel_id=1, source_target_pairs={{0,8},{4,12},{8,0},{12,4},{16,24},{20,28},{24,16},{28,20},{1,9},{5... | collective-permute-start | bytes 737288 | tf_op jit(solution)/shard_map/ppermute | solution.py:35
  5.8 1.2 %collective-permute-start.2 = (bf16[320,384]{1,0:T(8,128)(2,1)}, bf16[320,384]{1,0:T(8,128)(2,1)S(1)}, u32[]{:S(2)}, u32[]{:S(2)}) collective-permute-start(bf16[320,384]{1,0:T(8,128)(2,1)} %load.1.kv0), channel_id=1, source_target_pairs={{0,4},{4,0},{8,12},{12,8},{16,20},{20,16},{24,28},{28,24},{1,5},{5... | collective-permute-start | bytes 737288 | tf_op jit(solution)/shard_map/ppermute | solution.py:35
  7.1 2.3 %collective-permute-start.1 = (bf16[128,384]{1,0:T(8,128)(2,1)}, bf16[128,384]{1,0:T(8,128)(2,1)S(1)}, u32[]{:S(2)}, u32[]{:S(2)}) collective-permute-start(bf16[128,384]{1,0:T(8,128)(2,1)} %q_own_ref.3), channel_id=1, source_target_pairs={{0,16},{4,20},{8,24},{12,28},{16,0},{20,4},{24,8},{28,12},{1,17},{... | collective-permute-start | bytes 294920 | tf_op jit(solution)/shard_map/ppermute | solution.py:35
  9.4 1.8 %collective-permute-start.6 = (bf16[128,768]{1,0:T(8,128)(2,1)}, bf16[128,768]{1,0:T(8,128)(2,1)S(1)}, u32[]{:S(2)}, u32[]{:S(2)}) collective-permute-start(bf16[128,768]{1,0:T(8,128)(2,1)} %own_ref.1), channel_id=1, source_target_pairs={{0,1},{1,0},{2,3},{3,2},{4,5},{5,4},{6,7},{7,6},{8,9},{9,8},{10,11... | collective-permute-start | bytes 589832 | tf_op jit(solution)/shard_map/ppermute | solution.py:35
  11.2 0.0 collective-permute-done.7.near_ref
  11.2 0.0 collective-permute-start.8
  11.2 1.4 %collective-permute-done.1.q_pair_ref = bf16[128,384]{1,0:T(8,128)(2,1)S(1)} collective-permute-done((bf16[128,384]{1,0:T(8,128)(2,1)}, bf16[128,384]{1,0:T(8,128)(2,1)S(1)}, u32[]{:S(2)}, u32[]{:S(2)}) %collective-permute-start.1) | collective-permute-done | bytes 98336 | tf_op jit(solution)/shard_map/ppermute | solution.py:35
  12.5 0.0 collective-permute-done.kv2
  12.6 2.1 %collective-permute-start.3 = (bf16[160,384]{1,0:T(8,128)(2,1)S(1)}, bf16[160,384]{1,0:T(8,128)(2,1)S(1)}, u32[]{:S(2)}, u32[]{:S(2)}) collective-permute-start(bf16[160,384]{1,0:T(8,128)(2,1)S(1)} %pass_keys.1), channel_id=1, source_target_pairs={{0,4},{4,0},{8,12},{12,8},{16,20},{20,16},{24,28},{28,24},{1,5},{5... | collective-permute-start | bytes 368648 | tf_op jit(solution)/shard_map/ppermute | solution.py:35
  14.7 0.1 collective-permute-start.4
  14.8 0.0 collective-permute-done.6.core_ref
  14.8 0.0 collective-permute-done.8.far_ref
  14.8 0.0 copy-start
  14.8 1.7 %copy-done = bf16[384,3072]{1,0:T(8,128)(2,1)S(1)} copy-done((bf16[384,3072]{1,0:T(8,128)(2,1)S(1)}, bf16[384,3072]{1,0:T(8,128)(2,1)}, u32[]{:S(2)}) %copy-start) | copy-done | bytes 2359320
  16.4 0.9 %copy-done.4 = bf16[128,768]{1,0:T(8,128)(2,1)S(1)} copy-done((bf16[128,768]{1,0:T(8,128)(2,1)S(1)}, bf16[128,768]{1,0:T(8,128)(2,1)}, u32[]{:S(2)}) %copy-start.4) | copy-done | bytes 196632
  17.4 0.8 %dattn.1.d_own_ref = bf16[128,384]{1,0:T(8,128)(2,1)S(1)} custom-call(bf16[128,768]{1,0:T(8,128)(2,1)S(1)} %copy-done.4, bf16[128,768]{1,0:T(8,128)(2,1)S(1)} %collective-permute-done.6.core_ref, bf16[128,768]{1,0:T(8,128)(2,1)S(1)} %collective-permute-done.7.near_ref, bf16[128,768]{1,0:T(8,128)(2,1)S(1)} %collective-permute-done.8.far_ref, ...), custom_call_target="tpu_custom_call" | custom-call | bytes 2952000 | tf_op jit(solution)/shard_map/dattn/pallas_call | solution.py:44
  18.2 2.2 %collective-permute-start.9 = (bf16[128,384]{1,0:T(8,128)(2,1)S(1)}, bf16[128,384]{1,0:T(8,128)(2,1)S(1)}, u32[]{:S(2)}, u32[]{:S(2)}) collective-permute-start(bf16[128,384]{1,0:T(8,128)(2,1)S(1)} %dattn.1.d_own_ref), channel_id=1, source_target_pairs={{0,16},{4,20},{8,24},{12,28},{16,0},{20,4},{24,8},{28,12},{1,17},{... | collective-permute-start | bytes 294920 | tf_op jit(solution)/shard_map/ppermute | solution.py:35
  20.4 0.1 copy.15.levels_ref
  20.5 0.6 %limits.1.limits_ref = s32[8,256]{1,0:T(8,128)S(1)} custom-call(s32[8,2]{1,0:T(8,128)S(1)} %copy.15.levels_ref, s32[8]{0:T(128)S(1)} %copy-done.5), custom_call_target="tpu_custom_call" | custom-call | bytes 2214000 | tf_op jit(solution)/shard_map/limits/pallas_call | solution.py:44
  21.1 0.0 collective-permute-done.3.key3
  21.1 1.0 %scores.1 = (f32[8,256]{1,0:T(8,128)S(1)}, bf16[1920,256]{1,0:T(8,128)(2,1)S(1)}) custom-call(s32[8,256]{1,0:T(8,128)S(1)} %limits.1.limits_ref, bf16[128,384]{1,0:T(8,128)(2,1)S(1)} %copy-done.3, bf16[128,384]{1,0:T(8,128)(2,1)S(1)} %collective-permute-done.1.q_pair_ref, bf16[320,384]{1,0:T(8,128)(2,1)S(1)} %copy-done.2, ...), custom_call_target="tpu_custom_call" | custom-call | bytes 3321000 | tf_op jit(solution)/shard_map/scores/pallas_call | solution.py:44
  22.2 0.4 attn.1
  22.6 0.3 collective-permute-start.5
  22.9 0.0 collective-permute-done.9.d_pair_ref
  22.9 0.4 delta.1
  23.4 0.0 copy-start.1
  23.4 2.2 %collective-permute-start.10 = (f32[16,256]{1,0:T(8,128)S(1)}, f32[16,256]{1,0:T(8,128)S(1)}, u32[]{:S(2)}, u32[]{:S(2)}) collective-permute-start(f32[16,256]{1,0:T(8,128)S(1)} %get-tuple-element.46.stats_ref), channel_id=1, source_target_pairs={{0,16},{4,20},{8,24},{12,28},{16,0},{20,4},{24,8},{28,12},{1,17},{... | collective-permute-start | bytes 49160 | tf_op jit(solution)/shard_map/ppermute | solution.py:35
  25.6 3.9 %collective-permute-done.10.stats_pair_ref = f32[16,256]{1,0:T(8,128)S(1)} collective-permute-done((f32[16,256]{1,0:T(8,128)S(1)}, f32[16,256]{1,0:T(8,128)S(1)}, u32[]{:S(2)}, u32[]{:S(2)}) %collective-permute-start.10) | collective-permute-done | bytes 16416 | tf_op jit(solution)/shard_map/ppermute | solution.py:35
  29.5 1.1 %backward.1 = (f32[128,384]{1,0:T(8,128)S(1)}, bf16[128,384]{1,0:T(8,128)(2,1)S(1)}, f32[320,384]{1,0:T(8,128)S(1)}, bf16[320,384]{1,0:T(8,128)(2,1)S(1)}, bf16[...) custom-call(bf16[128,384]{1,0:T(8,128)(2,1)S(1)} %copy-done.3, ...), custom_call_target="tpu_custom_call" | custom-call | bytes 4059000 | tf_op jit(solution)/shard_map/backward/pallas_call | solution.py:44
  30.6 0.0 collective-permute-done.5.pair_ref
  30.6 1.3 %collective-permute-start.15 = (bf16[320,384]{1,0:T(8,128)(2,1)S(1)}, bf16[320,384]{1,0:T(8,128)(2,1)S(1)}, u32[]{:S(2)}, u32[]{:S(2)}) collective-permute-start(bf16[320,384]{1,0:T(8,128)(2,1)S(1)} %get-tuple-element.58), channel_id=1, source_target_pairs={{0,4},{4,0},{8,12},{12,8},{16,20},{20,16},{24,28},{28,24},{1,5},{5... | collective-permute-start | bytes 737288 | tf_op jit(solution)/shard_map/ppermute | solution.py:35
  31.9 1.1 %collective-permute-start.16 = (bf16[320,384]{1,0:T(8,128)(2,1)S(1)}, bf16[320,384]{1,0:T(8,128)(2,1)S(1)}, u32[]{:S(2)}, u32[]{:S(2)}) collective-permute-start(bf16[320,384]{1,0:T(8,128)(2,1)S(1)} %get-tuple-element.59), channel_id=1, source_target_pairs={{0,8},{4,12},{8,0},{12,4},{16,24},{20,28},{24,16},{28,20},{1,9},{5... | collective-permute-start | bytes 737288 | tf_op jit(solution)/shard_map/ppermute | solution.py:35
  33.1 3.1 %collective-permute-start.13 = (bf16[128,384]{1,0:T(8,128)(2,1)S(1)}, bf16[128,384]{1,0:T(8,128)(2,1)S(1)}, u32[]{:S(2)}, u32[]{:S(2)}) collective-permute-start(bf16[128,384]{1,0:T(8,128)(2,1)S(1)} %get-tuple-element.55), channel_id=1, source_target_pairs={{0,16},{4,20},{8,24},{12,28},{16,0},{20,4},{24,8},{28,12},{1,17},{... | collective-permute-start | bytes 294920 | tf_op jit(solution)/shard_map/ppermute | solution.py:35
  36.2 0.6 %project.1 = (f32[128,768]{1,0:T(8,128)S(1)}, bf16[128,768]{1,0:T(8,128)(2,1)S(1)}, bf16[128,768]{1,0:T(8,128)(2,1)S(1)}, bf16[128,768]{1,0:T(8,128)(2,1)S(1)}) custom-call(f32[384,128]{1,0:T(8,128)S(1)} %get-tuple-element.43.own_ref, bf16[384,128]{1,0:T(8,128)(2,1)S(1)} %collective-permute-done.5.pair_ref, f32[16,256]{1,0:T(8,128)S(1)} %get-tuple-element.46.stats_ref, ...), custom_call_target="tpu_custom_call" | custom-call | bytes 2214000 | tf_op jit(solution)/shard_map/project/pallas_call | solution.py:44
  36.8 0.3 collective-permute-start.11
  37.1 7.5 %collective-permute-start.12 = (bf16[128,768]{1,0:T(8,128)(2,1)S(1)}, bf16[128,768]{1,0:T(8,128)(2,1)S(1)}, u32[]{:S(2)}, u32[]{:S(2)}) collective-permute-start(bf16[128,768]{1,0:T(8,128)(2,1)S(1)} %get-tuple-element.53), channel_id=1, source_target_pairs={{0,3},{1,2},{2,1},{3,0},{4,7},{5,6},{6,5},{7,4},{8,11},{9,10},{10,... | collective-permute-start | bytes 589832 | tf_op jit(solution)/shard_map/ppermute | solution.py:35
  44.6 0.0 collective-permute-done.16.got_v_ref
  44.7 0.1 collective-permute-start.17
  44.7 0.0 collective-permute-done.13.dq_pair_ref
  44.8 0.3 collective-permute-start.18
  45.0 0.0 collective-permute-done.11.near_ref
  45.0 7.1 %collective-permute-done.12.far_ref = bf16[128,768]{1,0:T(8,128)(2,1)S(1)} collective-permute-done((bf16[128,768]{1,0:T(8,128)(2,1)S(1)}, bf16[128,768]{1,0:T(8,128)(2,1)S(1)}, u32[]{:S(2)}, u32[]{:S(2)}) %collective-permute-start.12) | collective-permute-done | bytes 196640 | tf_op jit(solution)/shard_map/ppermute | solution.py:35
  52.1 0.0 collective-permute-done.14.core_ref
  52.1 0.0 collective-permute-done.17.rest_k_ref
  52.1 0.9 %finish.1 = (bf16[128,384]{1,0:T(8,128)(2,1)}, bf16[128,384]{1,0:T(8,128)(2,1)}, bf16[128,384]{1,0:T(8,128)(2,1)}, bf16[32,384]{1,0:T(8,128)(2,1)}, bf16[32,384]{1,0:T(8,128)(2,1)}, /*index=5*/bf16[128,768]{1,0:T(8,128)(2,1)}) custom-call(f32[128,768]{1,0:T(8,128)S(1)} %get-tuple-element.51.keep_ref, bf16[128,768]{1,0:T(8,128)(2,1)S(1)} %collective-permute-done.11.near_ref, ...), custom_call_target="tpu_custom_call" | custom-call | bytes 3321000 | tf_op jit(solution)/shard_map/finish/pallas_call | solution.py:44
  (17 shorter events, 0.1 us)
Async XLA Ops:
  0.6 20.5 %copy-start.3 = (bf16[128,384]{1,0:T(8,128)(2,1)S(1)}, bf16[128,384]{1,0:T(8,128)(2,1)}, u32[]{:S(2)}) copy-start(bf16[128,384]{1,0:T(8,128)(2,1)} %q_own_ref.3) | copy-start | bytes 294916
  0.6 19.7 %copy-start.6 = (s32[8,2]{0,1:T(2,128)S(1)}, s32[8,2]{0,1:T(2,128)}, u32[]{:S(2)}) copy-start(s32[8,2]{0,1:T(2,128)} %param.14) | copy-start | bytes 196
  0.7 19.8 %copy-start.5 = (s32[8]{0:T(128)S(1)}, s32[8]{0:T(128)}, u32[]{:S(2)}) copy-start(s32[8]{0:T(128)} %counts_ref.1) | copy-start | bytes 100
  0.7 10.5 %collective-permute-start.7 = (bf16[128,768]{1,0:T(8,128)(2,1)}, bf16[128,768]{1,0:T(8,128)(2,1)S(1)}, u32[]{:S(2)}, u32[]{:S(2)}) collective-permute-start(bf16[128,768]{1,0:T(8,128)(2,1)} %own_ref.1), channel_id=1, source_target_pairs={{0,2},{1,3},{2,0},{3,1},{4,6},{5,7},{6,4},{7,5},{8,10},{9,11},{10,... | collective-permute-start | bytes 589832 | tf_op jit(solution)/shard_map/ppermute | solution.py:35
  4.4 16.7 %copy-start.2 = (bf16[320,384]{1,0:T(8,128)(2,1)S(1)}, bf16[320,384]{1,0:T(8,128)(2,1)}, u32[]{:S(2)}) copy-start(bf16[320,384]{1,0:T(8,128)(2,1)} %load.1.kv0) | copy-start | bytes 737284
  4.5 8.1 %collective-permute-start = (bf16[320,384]{1,0:T(8,128)(2,1)}, bf16[320,384]{1,0:T(8,128)(2,1)S(1)}, u32[]{:S(2)}, u32[]{:S(2)}) collective-permute-start(bf16[320,384]{1,0:T(8,128)(2,1)} %load.1.kv0), channel_id=1, source_target_pairs={{0,8},{4,12},{8,0},{12,4},{16,24},{20,28},{24,16},{28,20},{1,9},{5... | collective-permute-start | bytes 737288 | tf_op jit(solution)/shard_map/ppermute | solution.py:35
  5.8 15.3 %collective-permute-start.2 = (bf16[320,384]{1,0:T(8,128)(2,1)}, bf16[320,384]{1,0:T(8,128)(2,1)S(1)}, u32[]{:S(2)}, u32[]{:S(2)}) collective-permute-start(bf16[320,384]{1,0:T(8,128)(2,1)} %load.1.kv0), channel_id=1, source_target_pairs={{0,4},{4,0},{8,12},{12,8},{16,20},{20,16},{24,28},{28,24},{1,5},{5... | collective-permute-start | bytes 737288 | tf_op jit(solution)/shard_map/ppermute | solution.py:35
  7.1 5.5 %collective-permute-start.1 = (bf16[128,384]{1,0:T(8,128)(2,1)}, bf16[128,384]{1,0:T(8,128)(2,1)S(1)}, u32[]{:S(2)}, u32[]{:S(2)}) collective-permute-start(bf16[128,384]{1,0:T(8,128)(2,1)} %q_own_ref.3), channel_id=1, source_target_pairs={{0,16},{4,20},{8,24},{12,28},{16,0},{20,4},{24,8},{28,12},{1,17},{... | collective-permute-start | bytes 294920 | tf_op jit(solution)/shard_map/ppermute | solution.py:35
  9.4 5.4 %collective-permute-start.6 = (bf16[128,768]{1,0:T(8,128)(2,1)}, bf16[128,768]{1,0:T(8,128)(2,1)S(1)}, u32[]{:S(2)}, u32[]{:S(2)}) collective-permute-start(bf16[128,768]{1,0:T(8,128)(2,1)} %own_ref.1), channel_id=1, source_target_pairs={{0,1},{1,0},{2,3},{3,2},{4,5},{5,4},{6,7},{7,6},{8,9},{9,8},{10,11... | collective-permute-start | bytes 589832 | tf_op jit(solution)/shard_map/ppermute | solution.py:35
  11.2 3.6 %collective-permute-start.8 = (bf16[128,768]{1,0:T(8,128)(2,1)S(1)}, bf16[128,768]{1,0:T(8,128)(2,1)S(1)}, u32[]{:S(2)}, u32[]{:S(2)}) collective-permute-start(bf16[128,768]{1,0:T(8,128)(2,1)S(1)} %collective-permute-done.7.near_ref), channel_id=1, source_target_pairs={{0,1},{1,0},{2,3},{3,2},{4,5},{5,4},{6,7},{7,6},{8,9},{9,8},{10,11... | collective-permute-start | bytes 589832 | tf_op jit(solution)/shard_map/ppermute | solution.py:35
  12.6 8.6 %collective-permute-start.3 = (bf16[160,384]{1,0:T(8,128)(2,1)S(1)}, bf16[160,384]{1,0:T(8,128)(2,1)S(1)}, u32[]{:S(2)}, u32[]{:S(2)}) collective-permute-start(bf16[160,384]{1,0:T(8,128)(2,1)S(1)} %pass_keys.1), channel_id=1, source_target_pairs={{0,4},{4,0},{8,12},{12,8},{16,20},{20,16},{24,28},{28,24},{1,5},{5... | collective-permute-start | bytes 368648 | tf_op jit(solution)/shard_map/ppermute | solution.py:35
  14.7 7.5 %collective-permute-start.4 = (bf16[160,384]{1,0:T(8,128)(2,1)S(1)}, bf16[160,384]{1,0:T(8,128)(2,1)S(1)}, u32[]{:S(2)}, u32[]{:S(2)}) collective-permute-start(bf16[160,384]{1,0:T(8,128)(2,1)S(1)} %pass_values.1), channel_id=1, source_target_pairs={{0,4},{4,0},{8,12},{12,8},{16,20},{20,16},{24,28},{28,24},{1,5},{5... | collective-permute-start | bytes 368648 | tf_op jit(solution)/shard_map/ppermute | solution.py:35
  14.8 1.7 %copy-start = (bf16[384,3072]{1,0:T(8,128)(2,1)S(1)}, bf16[384,3072]{1,0:T(8,128)(2,1)}, u32[]{:S(2)}) copy-start(bf16[384,3072]{1,0:T(8,128)(2,1)} %w_ref.3) | copy-start | bytes 7077892
  16.4 0.9 %copy-start.4 = (bf16[128,768]{1,0:T(8,128)(2,1)S(1)}, bf16[128,768]{1,0:T(8,128)(2,1)}, u32[]{:S(2)}) copy-start(bf16[128,768]{1,0:T(8,128)(2,1)} %own_ref.1) | copy-start | bytes 589828
  18.2 4.7 %collective-permute-start.9 = (bf16[128,384]{1,0:T(8,128)(2,1)S(1)}, bf16[128,384]{1,0:T(8,128)(2,1)S(1)}, u32[]{:S(2)}, u32[]{:S(2)}) collective-permute-start(bf16[128,384]{1,0:T(8,128)(2,1)S(1)} %dattn.1.d_own_ref), channel_id=1, source_target_pairs={{0,16},{4,20},{8,24},{12,28},{16,0},{20,4},{24,8},{28,12},{1,17},{... | collective-permute-start | bytes 294920 | tf_op jit(solution)/shard_map/ppermute | solution.py:35
  22.6 8.0 %collective-permute-start.5 = (bf16[384,128]{1,0:T(8,128)(2,1)S(1)}, bf16[384,128]{1,0:T(8,128)(2,1)S(1)}, u32[]{:S(2)}, u32[]{:S(2)}) collective-permute-start(bf16[384,128]{1,0:T(8,128)(2,1)S(1)} %get-tuple-element.44), channel_id=1, source_target_pairs={{0,16},{4,20},{8,24},{12,28},{16,0},{20,4},{24,8},{28,12},{1,17},{... | collective-permute-start | bytes 294920 | tf_op jit(solution)/shard_map/ppermute | solution.py:35
  23.4 12.8 %copy-start.1 = (bf16[384,3072]{1,0:T(8,128)(2,1)S(1)}, bf16[384,3072]{1,0:T(8,128)(2,1)}, u32[]{:S(2)}) copy-start(bf16[384,3072]{1,0:T(8,128)(2,1)} %w_ref.3) | copy-start | bytes 7077892
  23.4 6.1 %collective-permute-start.10 = (f32[16,256]{1,0:T(8,128)S(1)}, f32[16,256]{1,0:T(8,128)S(1)}, u32[]{:S(2)}, u32[]{:S(2)}) collective-permute-start(f32[16,256]{1,0:T(8,128)S(1)} %get-tuple-element.46.stats_ref), channel_id=1, source_target_pairs={{0,16},{4,20},{8,24},{12,28},{16,0},{20,4},{24,8},{28,12},{1,17},{... | collective-permute-start | bytes 49160 | tf_op jit(solution)/shard_map/ppermute | solution.py:35
  30.6 14.0 %collective-permute-start.15 = (bf16[320,384]{1,0:T(8,128)(2,1)S(1)}, bf16[320,384]{1,0:T(8,128)(2,1)S(1)}, u32[]{:S(2)}, u32[]{:S(2)}) collective-permute-start(bf16[320,384]{1,0:T(8,128)(2,1)S(1)} %get-tuple-element.58), channel_id=1, source_target_pairs={{0,4},{4,0},{8,12},{12,8},{16,20},{20,16},{24,28},{28,24},{1,5},{5... | collective-permute-start | bytes 737288 | tf_op jit(solution)/shard_map/ppermute | solution.py:35
  31.9 12.7 %collective-permute-start.16 = (bf16[320,384]{1,0:T(8,128)(2,1)S(1)}, bf16[320,384]{1,0:T(8,128)(2,1)S(1)}, u32[]{:S(2)}, u32[]{:S(2)}) collective-permute-start(bf16[320,384]{1,0:T(8,128)(2,1)S(1)} %get-tuple-element.59), channel_id=1, source_target_pairs={{0,8},{4,12},{8,0},{12,4},{16,24},{20,28},{24,16},{28,20},{1,9},{5... | collective-permute-start | bytes 737288 | tf_op jit(solution)/shard_map/ppermute | solution.py:35
  33.1 11.7 %collective-permute-start.13 = (bf16[128,384]{1,0:T(8,128)(2,1)S(1)}, bf16[128,384]{1,0:T(8,128)(2,1)S(1)}, u32[]{:S(2)}, u32[]{:S(2)}) collective-permute-start(bf16[128,384]{1,0:T(8,128)(2,1)S(1)} %get-tuple-element.55), channel_id=1, source_target_pairs={{0,16},{4,20},{8,24},{12,28},{16,0},{20,4},{24,8},{28,12},{1,17},{... | collective-permute-start | bytes 294920 | tf_op jit(solution)/shard_map/ppermute | solution.py:35
  36.8 8.2 %collective-permute-start.11 = (bf16[128,768]{1,0:T(8,128)(2,1)S(1)}, bf16[128,768]{1,0:T(8,128)(2,1)S(1)}, u32[]{:S(2)}, u32[]{:S(2)}) collective-permute-start(bf16[128,768]{1,0:T(8,128)(2,1)S(1)} %get-tuple-element.52), channel_id=1, source_target_pairs={{0,2},{1,3},{2,0},{3,1},{4,6},{5,7},{6,4},{7,5},{8,10},{9,11},{10,... | collective-permute-start | bytes 589832 | tf_op jit(solution)/shard_map/ppermute | solution.py:35
  37.1 15.0 %collective-permute-start.12 = (bf16[128,768]{1,0:T(8,128)(2,1)S(1)}, bf16[128,768]{1,0:T(8,128)(2,1)S(1)}, u32[]{:S(2)}, u32[]{:S(2)}) collective-permute-start(bf16[128,768]{1,0:T(8,128)(2,1)S(1)} %get-tuple-element.53), channel_id=1, source_target_pairs={{0,3},{1,2},{2,1},{3,0},{4,7},{5,6},{6,5},{7,4},{8,11},{9,10},{10,... | collective-permute-start | bytes 589832 | tf_op jit(solution)/shard_map/ppermute | solution.py:35
  44.6 7.5 %collective-permute-start.14 = (bf16[128,768]{1,0:T(8,128)(2,1)S(1)}, bf16[128,768]{1,0:T(8,128)(2,1)S(1)}, u32[]{:S(2)}, u32[]{:S(2)}) collective-permute-start(bf16[128,768]{1,0:T(8,128)(2,1)S(1)} %get-tuple-element.56), channel_id=1, source_target_pairs={{0,1},{1,0},{2,3},{3,2},{4,5},{5,4},{6,7},{7,6},{8,9},{9,8},{10,11... | collective-permute-start | bytes 589832 | tf_op jit(solution)/shard_map/ppermute | solution.py:35
  44.7 7.5 %collective-permute-start.17 = (bf16[160,384]{1,0:T(8,128)(2,1)S(1)}, bf16[160,384]{1,0:T(8,128)(2,1)S(1)}, u32[]{:S(2)}, u32[]{:S(2)}) collective-permute-start(bf16[160,384]{1,0:T(8,128)(2,1)S(1)} %get-tuple-element.62), channel_id=1, source_target_pairs={{0,8},{4,12},{8,0},{12,4},{16,24},{20,28},{24,16},{28,20},{1,9},{5... | collective-permute-start | bytes 368648 | tf_op jit(solution)/shard_map/ppermute | solution.py:35
  44.8 7.4 %collective-permute-start.18 = (bf16[160,384]{1,0:T(8,128)(2,1)S(1)}, bf16[160,384]{1,0:T(8,128)(2,1)S(1)}, u32[]{:S(2)}, u32[]{:S(2)}) collective-permute-start(bf16[160,384]{1,0:T(8,128)(2,1)S(1)} %get-tuple-element.63), channel_id=1, source_target_pairs={{0,4},{4,0},{8,12},{12,8},{16,20},{20,16},{24,28},{28,24},{1,5},{5... | collective-permute-start | bytes 368648 | tf_op jit(solution)/shard_map/ppermute | solution.py:35

commit v12 on v10

--- a/solution.py
+++ b/solution.py
@@ -95,6 +95,30 @@
     keys = key3.shape[0]
     pairs = [(ref.at[:keys], ref.at[keys:]) for ref in (kv0, kv1, kv2)]
     return pairs + [(key3, value3)]
+
+
+def load_weight_kernel(w_ref, w_out, sems):
+    copies = []
+    for i in range(sems.shape[0]):
+        part = pl.ds(i * HDIM, HDIM)
+        copies.append(pltpu.make_async_copy(w_ref.at[part], w_out.at[part], sems.at[i]))
+    for copy in copies:
+        copy.start()
+    for copy in copies:
+        copy.wait()
+
+
+def load_weight(w_out):
+    return pl.pallas_call(
+        load_weight_kernel,
+        name="load_w",
+        out_shape=jax.ShapeDtypeStruct(w_out.shape, BF16),
+        in_specs=[pl.BlockSpec(memory_space=pl.ANY)],
+        out_specs=pl.BlockSpec(memory_space=pltpu.VMEM),
+        scratch_shapes=[pltpu.SemaphoreType.DMA((w_out.shape[0] // HDIM,))],
+        compiler_params=pltpu.CompilerParams(vmem_limit_bytes=50 * 2**20 + 2**19),
+        cost_estimate=cost_of(1.6),
+    )(w_out)
 
 
 def limits_kernel(levels_ref, counts_ref, limits_ref):
@@ -289,6 +313,8 @@
     q_pair = swap(sec_q, "ctx", PAIR)
     grad_near = swap(grad_out, "head", 2)
     grad_core = swap(grad_out, "head", 1)
+    weight = load_weight(w_out)
+    grad_near, weight = lax.optimization_barrier((grad_near, weight))
     grad_far = swap(grad_near, "head", 1)
     kv0 = load_keys(sec_k, hist_k, sec_v, hist_v)
     kv2 = swap(kv0, "ctx", 2)
@@ -298,9 +324,9 @@
         "dattn",
         0.8,
         [shape((rows, width), BF16)],
-        (grad_out, grad_core, grad_near, grad_far, w_out),
+        (grad_out, grad_core, grad_near, grad_far, weight),
     )[0]
-    kv2, d_own = lax.optimization_barrier((kv2, d_own))
+    kv1, kv2, d_own = lax.optimization_barrier((kv1, kv2, d_own))
     key3 = local_call(pass_keys_kernel, "pass_keys", 0.1, [shape((keys, width), BF16)], (kv2,))[0]
     kv2_kept, q_pair, _ = lax.optimization_barrier((kv2, q_pair, key3))
     value3 = local_call(
@@ -366,7 +392,7 @@
         "project",
         0.6,
         [shape((rows, share), F32)] + [shape((rows, share), BF16)] * 3,
-        (attn_own, attn_got, stats, stats_pair, w_out),
+        (attn_own, attn_got, stats, stats_pair, weight),
     )
     out_near, out_far = (swap(out_send[step - 1], "head", step) for step in (2, 3))
     dq_got = swap(dq_pair, "ctx", PAIR)

time: 49.7 us -> 49.1 us (0.988)
  waiting for transfers between devices: 17.7 us -> 14.6 us
  Pallas kernels: 7.69 us -> 10.6 us
  local copies, waits for them, and re-layouts: 2.7 us -> 1.9 us
    ppermute x19, waiting for transfers between devices: 17.7 us -> 14.6 us  [swap(): return lax.ppermute(block, axis, [(i, i ^ bit) for i in range(count)])]
    pallas_call x0 -> x1, Pallas kernels: none -> 1.63 us  [load_weight(): pl.pallas_call(load_weight_kernel, name='load_w', out_shape=jax.ShapeDtyp...]
    pallas_call x11, Pallas kernels: 6.03 us -> 7.35 us  [local_call(): pl.pallas_call(body, name=name, out_shape=out_shapes, in_specs=[pl.BlockS...]
    unnamed x15 -> x21, local copies, waits for them, and re-layouts: 2.7 us -> 1.9 us
  transfers between devices with their start and end apart: 19 -> 19, of which waited for: 11 -> 10; matrix products, arithmetic and copies ran while one was open for 0% -> 0% of each run, Pallas kernels for 14% -> 20%
where the time goes in v12:
time: 49.1 us; the launch traced here: 48.8 us
  starting transfers between devices  20.9 us (43%)
  waiting for transfers between devices  14.6 us (30%)
  Pallas kernels  10.6 us (22%)
  local copies, waits for them, and re-layouts  1.9 us (4%)
  between operations  0.83 us (2%)
    ppermute x19, starting transfers between devices, swap(): return lax.ppermute(block, axis, [(i, i ^ bit) for i in range(count)])  20.9 us
    ppermute x19, waiting for transfers between devices, swap(): return lax.ppermute(block, axis, [(i, i ^ bit) for i in range(count)])  14.6 us
    pallas_call x11, Pallas kernels, local_call(): pl.pallas_call(body, name=name, out_shape=out_shapes, in_specs=[pl.BlockS...  7.35 us
    unnamed x21, local copies, waits for them, and re-layouts  1.9 us
    pallas_call x1, Pallas kernels, load_keys(): pl.pallas_call(load_kernel, name='load', out_shape=jax.ShapeDtypeStruct((...  1.66 us
    pallas_call x1, Pallas kernels, load_weight(): pl.pallas_call(load_weight_kernel, name='load_w', out_shape=jax.ShapeDtyp...  1.63 us
  transfers between devices with their start and end apart: 19, of which 10 were waited for; matrix products, arithmetic and copies ran while one was open for 0% of the time, Pallas kernels for 20%

profile of v12, /device:TPU:0, one launch (start us, length us, event | category | flops | bytes accessed | tf_op | source)
XLA Modules:
  0.0 48.8 jit_solution(2439346850265226808)
XLA Ops:
  0.6 3.0 %collective-permute-start.3 = (bf16[128,768]{1,0:T(8,128)(2,1)}, bf16[128,768]{1,0:T(8,128)(2,1)S(1)}, u32[]{:S(2)}, u32[]{:S(2)}) collective-permute-start(bf16[128,768]{1,0:T(8,128)(2,1)} %own_ref.1), channel_id=1, source_target_pairs={{0,2},{1,3},{2,0},{3,1},{4,6},{5,7},{6,4},{7,5},{8,10},{9,11},{10,... | collective-permute-start | bytes 589832 | tf_op jit(solution)/shard_map/ppermute | solution.py:35
  3.6 1.7 %load.1.kv0 = bf16[320,384]{1,0:T(8,128)(2,1)} custom-call(bf16[128,384]{1,0:T(8,128)(2,1)} %k_ref.1, bf16[32,384]{1,0:T(8,128)(2,1)} %hk_ref.1, bf16[128,384]{1,0:T(8,128)(2,1)} %v_ref.1, bf16[32,384]{1,0:T(8,128)(2,1)} %hv_ref.1), custom_call_target="tpu_custom_call" | custom-call | bytes 5904000 | tf_op jit(solution)/shard_map/load/pallas_call | solution.py:74
  5.3 0.0 copy-start.1
  5.3 0.0 copy-start.7
  5.3 1.6 %collective-permute-start.1 = (bf16[320,384]{1,0:T(8,128)(2,1)}, bf16[320,384]{1,0:T(8,128)(2,1)S(1)}, u32[]{:S(2)}, u32[]{:S(2)}) collective-permute-start(bf16[320,384]{1,0:T(8,128)(2,1)} %load.1.kv0), channel_id=1, source_target_pairs={{0,8},{4,12},{8,0},{12,4},{16,24},{20,28},{24,16},{28,20},{1,9},{5... | collective-permute-start | bytes 737288 | tf_op jit(solution)/shard_map/ppermute | solution.py:35
  7.0 1.5 %collective-permute-start = (bf16[320,384]{1,0:T(8,128)(2,1)}, bf16[320,384]{1,0:T(8,128)(2,1)S(1)}, u32[]{:S(2)}, u32[]{:S(2)}) collective-permute-start(bf16[320,384]{1,0:T(8,128)(2,1)} %load.1.kv0), channel_id=1, source_target_pairs={{0,4},{4,0},{8,12},{12,8},{16,20},{20,16},{24,28},{28,24},{1,5},{5... | collective-permute-start | bytes 737288 | tf_op jit(solution)/shard_map/ppermute | solution.py:35
  8.5 1.6 %load_w.1.w_ref = bf16[384,3072]{1,0:T(8,128)(2,1)S(1)} custom-call(bf16[384,3072]{1,0:T(8,128)(2,1)} %w_ref.1), custom_call_target="tpu_custom_call" | custom-call | bytes 5904000 | tf_op jit(solution)/shard_map/load_w/pallas_call | solution.py:112
  10.1 0.0 copy-start.9
  10.1 0.0 copy-start.8
  10.2 0.6 %collective-permute-start.4 = (bf16[128,768]{1,0:T(8,128)(2,1)S(1)}, bf16[128,768]{1,0:T(8,128)(2,1)S(1)}, u32[]{:S(2)}, u32[]{:S(2)}) collective-permute-start(bf16[128,768]{1,0:T(8,128)(2,1)S(1)} %collective-permute-done.3.near_ref), channel_id=1, source_target_pairs={{0,1},{1,0},{2,3},{3,2},{4,5},{5,4},{6,7},{7,6},{8,9},{9,8},{10,11... | collective-permute-start | bytes 589832 | tf_op jit(solution)/shard_map/ppermute | solution.py:35
  10.8 2.6 %collective-permute-start.5 = (bf16[128,384]{1,0:T(8,128)(2,1)S(1)}, bf16[128,384]{1,0:T(8,128)(2,1)S(1)}, u32[]{:S(2)}, u32[]{:S(2)}) collective-permute-start(bf16[128,384]{1,0:T(8,128)(2,1)S(1)} %copy-done.1), channel_id=1, source_target_pairs={{0,16},{4,20},{8,24},{12,28},{16,0},{20,4},{24,8},{28,12},{1,17},{... | collective-permute-start | bytes 294920 | tf_op jit(solution)/shard_map/ppermute | solution.py:35
  13.4 0.8 %dattn.1.d_own_ref = bf16[128,384]{1,0:T(8,128)(2,1)S(1)} custom-call(bf16[128,768]{1,0:T(8,128)(2,1)S(1)} %copy-done.7, bf16[128,768]{1,0:T(8,128)(2,1)S(1)} %collective-permute-done.2.core_ref, bf16[128,768]{1,0:T(8,128)(2,1)S(1)} %collective-permute-done.3.near_ref, bf16[128,768]{1,0:T(8,128)(2,1)S(1)} %collective-permute-done.4.far_ref, ...), custom_call_target="tpu_custom_call" | custom-call | bytes 2952000 | tf_op jit(solution)/shard_map/dattn/pallas_call | solution.py:44
  14.2 0.1 collective-permute-done.kv1
  14.3 0.7 %pass_keys.1 = bf16[160,384]{1,0:T(8,128)(2,1)} custom-call(bf16[320,384]{1,0:T(8,128)(2,1)S(1)} %collective-permute-done.1.kv2), custom_call_target="tpu_custom_call" | custom-call | bytes 369000 | tf_op jit(solution)/shard_map/pass_keys/pallas_call | solution.py:44
  15.0 1.5 %collective-permute-start.6 = (bf16[160,384]{1,0:T(8,128)(2,1)}, bf16[160,384]{1,0:T(8,128)(2,1)S(1)}, u32[]{:S(2)}, u32[]{:S(2)}) collective-permute-start(bf16[160,384]{1,0:T(8,128)(2,1)} %pass_keys.1), channel_id=1, source_target_pairs={{0,4},{4,0},{8,12},{12,8},{16,20},{20,16},{24,28},{28,24},{1,5},{5... | collective-permute-start | bytes 368648 | tf_op jit(solution)/shard_map/ppermute | solution.py:35
  16.5 2.0 %collective-permute-done.5.q_pair_ref = bf16[128,384]{1,0:T(8,128)(2,1)S(1)} collective-permute-done((bf16[128,384]{1,0:T(8,128)(2,1)S(1)}, bf16[128,384]{1,0:T(8,128)(2,1)S(1)}, u32[]{:S(2)}, u32[]{:S(2)}) %collective-permute-start.5) | collective-permute-done | bytes 98336 | tf_op jit(solution)/shard_map/ppermute | solution.py:35
  18.5 0.7 %pass_values.1 = bf16[160,384]{1,0:T(8,128)(2,1)} custom-call(bf16[320,384]{1,0:T(8,128)(2,1)S(1)} %collective-permute-done.1.kv2), custom_call_target="tpu_custom_call" | custom-call | bytes 3690000 | tf_op jit(solution)/shard_map/pass_values/pallas_call | solution.py:44
  19.2 0.5 %collective-permute-start.7 = (bf16[160,384]{1,0:T(8,128)(2,1)}, bf16[160,384]{1,0:T(8,128)(2,1)S(1)}, u32[]{:S(2)}, u32[]{:S(2)}) collective-permute-start(bf16[160,384]{1,0:T(8,128)(2,1)} %pass_values.1), channel_id=1, source_target_pairs={{0,4},{4,0},{8,12},{12,8},{16,20},{20,16},{24,28},{28,24},{1,5},{5... | collective-permute-start | bytes 368648 | tf_op jit(solution)/shard_map/ppermute | solution.py:35
  19.7 0.6 %collective-permute-start.9 = (bf16[128,384]{1,0:T(8,128)(2,1)S(1)}, bf16[128,384]{1,0:T(8,128)(2,1)S(1)}, u32[]{:S(2)}, u32[]{:S(2)}) collective-permute-start(bf16[128,384]{1,0:T(8,128)(2,1)S(1)} %dattn.1.d_own_ref), channel_id=1, source_target_pairs={{0,16},{4,20},{8,24},{12,28},{16,0},{20,4},{24,8},{28,12},{1,17},{... | collective-permute-start | bytes 294920 | tf_op jit(solution)/shard_map/ppermute | solution.py:35
  20.3 0.1 copy.15.levels_ref
  20.4 0.6 %limits.1.limits_ref = s32[8,256]{1,0:T(8,128)S(1)} custom-call(s32[8,2]{1,0:T(8,128)S(1)} %copy.15.levels_ref, s32[8]{0:T(128)S(1)} %copy-done.8), custom_call_target="tpu_custom_call" | custom-call | bytes 2214000 | tf_op jit(solution)/shard_map/limits/pallas_call | solution.py:44
  21.1 0.0 copy-start.2
  21.1 0.9 %copy-done.2 = bf16[128,384]{1,0:T(8,128)(2,1)S(1)} copy-done((bf16[128,384]{1,0:T(8,128)(2,1)S(1)}, bf16[128,384]{1,0:T(8,128)(2,1)}, u32[]{:S(2)}) %copy-start.2) | copy-done | bytes 98328
  22.0 0.9 %copy-done.5 = bf16[128,384]{1,0:T(8,128)(2,1)S(1)} copy-done((bf16[128,384]{1,0:T(8,128)(2,1)S(1)}, bf16[128,384]{1,0:T(8,128)(2,1)}, u32[]{:S(2)}) %copy-start.5) | copy-done | bytes 98328
  22.9 1.0 %scores.1 = (f32[8,256]{1,0:T(8,128)S(1)}, bf16[1920,256]{1,0:T(8,128)(2,1)S(1)}) custom-call(s32[8,256]{1,0:T(8,128)S(1)} %limits.1.limits_ref, bf16[128,384]{1,0:T(8,128)(2,1)S(1)} %copy-done.2, bf16[128,384]{1,0:T(8,128)(2,1)S(1)} %copy-done.5, bf16[320,384]{1,0:T(8,128)(2,1)S(1)} %copy-done, bf16[320,384]{1,0:T(8,128)(2,1)S(1)} %collective-permute-done.kv1, ...), custom_call_target="tpu_custom_call" | custom-call | bytes 3321000 | tf_op jit(solution)/shard_map/scores/pallas_call | solution.py:44
  23.9 0.5 collective-permute-done.7.value3
  24.3 0.4 attn.1
  24.8 2.1 %collective-permute-start.8 = (bf16[384,128]{1,0:T(8,128)(2,1)S(1)}, bf16[384,128]{1,0:T(8,128)(2,1)S(1)}, u32[]{:S(2)}, u32[]{:S(2)}) collective-permute-start(bf16[384,128]{1,0:T(8,128)(2,1)S(1)} %get-tuple-element.53), channel_id=1, source_target_pairs={{0,16},{4,20},{8,24},{12,28},{16,0},{20,4},{24,8},{28,12},{1,17},{... | collective-permute-start | bytes 294920 | tf_op jit(solution)/shard_map/ppermute | solution.py:35
  26.9 0.0 collective-permute-done.9.d_pair_ref
  26.9 0.4 delta.1
  27.3 0.9 %collective-permute-start.10 = (f32[16,256]{1,0:T(8,128)S(1)}, f32[16,256]{1,0:T(8,128)S(1)}, u32[]{:S(2)}, u32[]{:S(2)}) collective-permute-start(f32[16,256]{1,0:T(8,128)S(1)} %get-tuple-element.56.stats_ref), channel_id=1, source_target_pairs={{0,16},{4,20},{8,24},{12,28},{16,0},{20,4},{24,8},{28,12},{1,17},{... | collective-permute-start | bytes 49160 | tf_op jit(solution)/shard_map/ppermute | solution.py:35
  28.3 4.9 %collective-permute-done.10.stats_pair_ref = f32[16,256]{1,0:T(8,128)S(1)} collective-permute-done((f32[16,256]{1,0:T(8,128)S(1)}, f32[16,256]{1,0:T(8,128)S(1)}, u32[]{:S(2)}, u32[]{:S(2)}) %collective-permute-start.10) | collective-permute-done | bytes 16416 | tf_op jit(solution)/shard_map/ppermute | solution.py:35
  33.2 1.1 %backward.1 = (f32[128,384]{1,0:T(8,128)S(1)}, bf16[128,384]{1,0:T(8,128)(2,1)S(1)}, f32[320,384]{1,0:T(8,128)S(1)}, bf16[320,384]{1,0:T(8,128)(2,1)S(1)}, bf16[...) custom-call(bf16[128,384]{1,0:T(8,128)(2,1)S(1)} %copy-done.3, ...), custom_call_target="tpu_custom_call" | custom-call | bytes 4059000 | tf_op jit(solution)/shard_map/backward/pallas_call | solution.py:44
  34.3 0.9 %collective-permute-start.15 = (bf16[320,384]{1,0:T(8,128)(2,1)S(1)}, bf16[320,384]{1,0:T(8,128)(2,1)S(1)}, u32[]{:S(2)}, u32[]{:S(2)}) collective-permute-start(bf16[320,384]{1,0:T(8,128)(2,1)S(1)} %get-tuple-element.68), channel_id=1, source_target_pairs={{0,4},{4,0},{8,12},{12,8},{16,20},{20,16},{24,28},{28,24},{1,5},{5... | collective-permute-start | bytes 737288 | tf_op jit(solution)/shard_map/ppermute | solution.py:35
  35.2 0.5 %collective-permute-start.16 = (bf16[320,384]{1,0:T(8,128)(2,1)S(1)}, bf16[320,384]{1,0:T(8,128)(2,1)S(1)}, u32[]{:S(2)}, u32[]{:S(2)}) collective-permute-start(bf16[320,384]{1,0:T(8,128)(2,1)S(1)} %get-tuple-element.69), channel_id=1, source_target_pairs={{0,8},{4,12},{8,0},{12,4},{16,24},{20,28},{24,16},{28,20},{1,9},{5... | collective-permute-start | bytes 737288 | tf_op jit(solution)/shard_map/ppermute | solution.py:35
  35.7 2.2 %collective-permute-start.13 = (bf16[128,384]{1,0:T(8,128)(2,1)S(1)}, bf16[128,384]{1,0:T(8,128)(2,1)S(1)}, u32[]{:S(2)}, u32[]{:S(2)}) collective-permute-start(bf16[128,384]{1,0:T(8,128)(2,1)S(1)} %get-tuple-element.65), channel_id=1, source_target_pairs={{0,16},{4,20},{8,24},{12,28},{16,0},{20,4},{24,8},{28,12},{1,17},{... | collective-permute-start | bytes 294920 | tf_op jit(solution)/shard_map/ppermute | solution.py:35
  37.9 0.6 %project.1 = (f32[128,768]{1,0:T(8,128)S(1)}, bf16[128,768]{1,0:T(8,128)(2,1)S(1)}, bf16[128,768]{1,0:T(8,128)(2,1)S(1)}, bf16[128,768]{1,0:T(8,128)(2,1)S(1)}) custom-call(f32[384,128]{1,0:T(8,128)S(1)} %get-tuple-element.52.own_ref, bf16[384,128]{1,0:T(8,128)(2,1)S(1)} %collective-permute-done.8.pair_ref, f32[16,256]{1,0:T(8,128)S(1)} %get-tuple-element.56.stats_ref, ...), custom_call_target="tpu_custom_call" | custom-call | bytes 2214000 | tf_op jit(solution)/shard_map/project/pallas_call | solution.py:44
  38.5 1.1 %collective-permute-start.11 = (bf16[128,768]{1,0:T(8,128)(2,1)S(1)}, bf16[128,768]{1,0:T(8,128)(2,1)S(1)}, u32[]{:S(2)}, u32[]{:S(2)}) collective-permute-start(bf16[128,768]{1,0:T(8,128)(2,1)S(1)} %get-tuple-element.62), channel_id=1, source_target_pairs={{0,2},{1,3},{2,0},{3,1},{4,6},{5,7},{6,4},{7,5},{8,10},{9,11},{10,... | collective-permute-start | bytes 589832 | tf_op jit(solution)/shard_map/ppermute | solution.py:35
  39.6 0.9 %collective-permute-done.15.got_k_ref = bf16[320,384]{1,0:T(8,128)(2,1)S(1)} collective-permute-done((bf16[320,384]{1,0:T(8,128)(2,1)S(1)}, bf16[320,384]{1,0:T(8,128)(2,1)S(1)}, u32[]{:S(2)}, u32[]{:S(2)}) %collective-permute-start.15) | collective-permute-done | bytes 245792 | tf_op jit(solution)/shard_map/ppermute | solution.py:35
  40.5 0.2 collective-permute-start.14
  40.7 2.1 %collective-permute-done.16.got_v_ref = bf16[320,384]{1,0:T(8,128)(2,1)S(1)} collective-permute-done((bf16[320,384]{1,0:T(8,128)(2,1)S(1)}, bf16[320,384]{1,0:T(8,128)(2,1)S(1)}, u32[]{:S(2)}, u32[]{:S(2)}) %collective-permute-start.16) | collective-permute-done | bytes 245792 | tf_op jit(solution)/shard_map/ppermute | solution.py:35
  42.9 0.1 collective-permute-start.17
  43.0 1.0 %collective-permute-start.18 = (bf16[160,384]{1,0:T(8,128)(2,1)S(1)}, bf16[160,384]{1,0:T(8,128)(2,1)S(1)}, u32[]{:S(2)}, u32[]{:S(2)}) collective-permute-start(bf16[160,384]{1,0:T(8,128)(2,1)S(1)} %get-tuple-element.73), channel_id=1, source_target_pairs={{0,4},{4,0},{8,12},{12,8},{16,20},{20,16},{24,28},{28,24},{1,5},{5... | collective-permute-start | bytes 368648 | tf_op jit(solution)/shard_map/ppermute | solution.py:35
  43.9 2.0 %collective-permute-done.11.near_ref = bf16[128,768]{1,0:T(8,128)(2,1)S(1)} collective-permute-done((bf16[128,768]{1,0:T(8,128)(2,1)S(1)}, bf16[128,768]{1,0:T(8,128)(2,1)S(1)}, u32[]{:S(2)}, u32[]{:S(2)}) %collective-permute-start.11) | collective-permute-done | bytes 196640 | tf_op jit(solution)/shard_map/ppermute | solution.py:35
  46.0 1.1 %collective-permute-done.12.far_ref = bf16[128,768]{1,0:T(8,128)(2,1)S(1)} collective-permute-done((bf16[128,768]{1,0:T(8,128)(2,1)S(1)}, bf16[128,768]{1,0:T(8,128)(2,1)S(1)}, u32[]{:S(2)}, u32[]{:S(2)}) %collective-permute-start.12) | collective-permute-done | bytes 196640 | tf_op jit(solution)/shard_map/ppermute | solution.py:35
  47.0 0.8 %collective-permute-done.17.rest_k_ref = bf16[160,384]{1,0:T(8,128)(2,1)S(1)} collective-permute-done((bf16[160,384]{1,0:T(8,128)(2,1)S(1)}, bf16[160,384]{1,0:T(8,128)(2,1)S(1)}, u32[]{:S(2)}, u32[]{:S(2)}) %collective-permute-start.17) | collective-permute-done | bytes 122912 | tf_op jit(solution)/shard_map/ppermute | solution.py:35
  47.8 0.1 collective-permute-done.18.rest_v_ref
  47.9 0.9 %finish.1 = (bf16[128,384]{1,0:T(8,128)(2,1)}, bf16[128,384]{1,0:T(8,128)(2,1)}, bf16[128,384]{1,0:T(8,128)(2,1)}, bf16[32,384]{1,0:T(8,128)(2,1)}, bf16[32,384]{1,0:T(8,128)(2,1)}, /*index=5*/bf16[128,768]{1,0:T(8,128)(2,1)}) custom-call(f32[128,768]{1,0:T(8,128)S(1)} %get-tuple-element.61.keep_ref, bf16[128,768]{1,0:T(8,128)(2,1)S(1)} %collective-permute-done.11.near_ref, ...), custom_call_target="tpu_custom_call" | custom-call | bytes 3321000 | tf_op jit(solution)/shard_map/finish/pallas_call | solution.py:44
  (24 shorter events, 0.1 us)
Async XLA Ops:
  0.6 9.5 %collective-permute-start.3 = (bf16[128,768]{1,0:T(8,128)(2,1)}, bf16[128,768]{1,0:T(8,128)(2,1)S(1)}, u32[]{:S(2)}, u32[]{:S(2)}) collective-permute-start(bf16[128,768]{1,0:T(8,128)(2,1)} %own_ref.1), channel_id=1, source_target_pairs={{0,2},{1,3},{2,0},{3,1},{4,6},{5,7},{6,4},{7,5},{8,10},{9,11},{10,... | collective-permute-start | bytes 589832 | tf_op jit(solution)/shard_map/ppermute | solution.py:35
  5.3 5.4 %copy-start.1 = (bf16[128,384]{1,0:T(8,128)(2,1)S(1)}, bf16[128,384]{1,0:T(8,128)(2,1)}, u32[]{:S(2)}) copy-start(bf16[128,384]{1,0:T(8,128)(2,1)} %q_own_ref.3) | copy-start | bytes 294916
  5.3 8.0 %copy-start.7 = (bf16[128,768]{1,0:T(8,128)(2,1)S(1)}, bf16[128,768]{1,0:T(8,128)(2,1)}, u32[]{:S(2)}) copy-start(bf16[128,768]{1,0:T(8,128)(2,1)} %own_ref.1) | copy-start | bytes 589828
  5.3 8.9 %collective-permute-start.1 = (bf16[320,384]{1,0:T(8,128)(2,1)}, bf16[320,384]{1,0:T(8,128)(2,1)S(1)}, u32[]{:S(2)}, u32[]{:S(2)}) collective-permute-start(bf16[320,384]{1,0:T(8,128)(2,1)} %load.1.kv0), channel_id=1, source_target_pairs={{0,8},{4,12},{8,0},{12,4},{16,24},{20,28},{24,16},{28,20},{1,9},{5... | collective-permute-start | bytes 737288 | tf_op jit(solution)/shard_map/ppermute | solution.py:35
  7.0 7.3 %collective-permute-start = (bf16[320,384]{1,0:T(8,128)(2,1)}, bf16[320,384]{1,0:T(8,128)(2,1)S(1)}, u32[]{:S(2)}, u32[]{:S(2)}) collective-permute-start(bf16[320,384]{1,0:T(8,128)(2,1)} %load.1.kv0), channel_id=1, source_target_pairs={{0,4},{4,0},{8,12},{12,8},{16,20},{20,16},{24,28},{28,24},{1,5},{5... | collective-permute-start | bytes 737288 | tf_op jit(solution)/shard_map/ppermute | solution.py:35
  8.5 4.9 %collective-permute-start.2 = (bf16[128,768]{1,0:T(8,128)(2,1)}, bf16[128,768]{1,0:T(8,128)(2,1)S(1)}, u32[]{:S(2)}, u32[]{:S(2)}) collective-permute-start(bf16[128,768]{1,0:T(8,128)(2,1)} %own_ref.1), channel_id=1, source_target_pairs={{0,1},{1,0},{2,3},{3,2},{4,5},{5,4},{6,7},{7,6},{8,9},{9,8},{10,11... | collective-permute-start | bytes 589832 | tf_op jit(solution)/shard_map/ppermute | solution.py:35
  10.1 10.2 %copy-start.9 = (s32[8,2]{0,1:T(2,128)S(1)}, s32[8,2]{0,1:T(2,128)}, u32[]{:S(2)}) copy-start(s32[8,2]{0,1:T(2,128)} %param.14) | copy-start | bytes 196
  10.1 10.3 %copy-start.8 = (s32[8]{0:T(128)S(1)}, s32[8]{0:T(128)}, u32[]{:S(2)}) copy-start(s32[8]{0:T(128)} %counts_ref.1) | copy-start | bytes 100
  10.2 10.9 %copy-start = (bf16[320,384]{1,0:T(8,128)(2,1)S(1)}, bf16[320,384]{1,0:T(8,128)(2,1)}, u32[]{:S(2)}) copy-start(bf16[320,384]{1,0:T(8,128)(2,1)} %load.1.kv0) | copy-start | bytes 737284
  10.2 3.2 %collective-permute-start.4 = (bf16[128,768]{1,0:T(8,128)(2,1)S(1)}, bf16[128,768]{1,0:T(8,128)(2,1)S(1)}, u32[]{:S(2)}, u32[]{:S(2)}) collective-permute-start(bf16[128,768]{1,0:T(8,128)(2,1)S(1)} %collective-permute-done.3.near_ref), channel_id=1, source_target_pairs={{0,1},{1,0},{2,3},{3,2},{4,5},{5,4},{6,7},{7,6},{8,9},{9,8},{10,11... | collective-permute-start | bytes 589832 | tf_op jit(solution)/shard_map/ppermute | solution.py:35
  10.8 7.8 %collective-permute-start.5 = (bf16[128,384]{1,0:T(8,128)(2,1)S(1)}, bf16[128,384]{1,0:T(8,128)(2,1)S(1)}, u32[]{:S(2)}, u32[]{:S(2)}) collective-permute-start(bf16[128,384]{1,0:T(8,128)(2,1)S(1)} %copy-done.1), channel_id=1, source_target_pairs={{0,16},{4,20},{8,24},{12,28},{16,0},{20,4},{24,8},{28,12},{1,17},{... | collective-permute-start | bytes 294920 | tf_op jit(solution)/shard_map/ppermute | solution.py:35
  15.0 6.1 %collective-permute-start.6 = (bf16[160,384]{1,0:T(8,128)(2,1)}, bf16[160,384]{1,0:T(8,128)(2,1)S(1)}, u32[]{:S(2)}, u32[]{:S(2)}) collective-permute-start(bf16[160,384]{1,0:T(8,128)(2,1)} %pass_keys.1), channel_id=1, source_target_pairs={{0,4},{4,0},{8,12},{12,8},{16,20},{20,16},{24,28},{28,24},{1,5},{5... | collective-permute-start | bytes 368648 | tf_op jit(solution)/shard_map/ppermute | solution.py:35
  18.5 0.7 %copy-start.4 = (bf16[128,384]{1,0:T(8,128)(2,1)}, bf16[128,384]{1,0:T(8,128)(2,1)S(1)}, u32[]{:S(2)}) copy-start(bf16[128,384]{1,0:T(8,128)(2,1)S(1)} %collective-permute-done.5.q_pair_ref) | copy-start | bytes 294916
  19.2 5.1 %collective-permute-start.7 = (bf16[160,384]{1,0:T(8,128)(2,1)}, bf16[160,384]{1,0:T(8,128)(2,1)S(1)}, u32[]{:S(2)}, u32[]{:S(2)}) collective-permute-start(bf16[160,384]{1,0:T(8,128)(2,1)} %pass_values.1), channel_id=1, source_target_pairs={{0,4},{4,0},{8,12},{12,8},{16,20},{20,16},{24,28},{28,24},{1,5},{5... | collective-permute-start | bytes 368648 | tf_op jit(solution)/shard_map/ppermute | solution.py:35
  19.7 7.2 %collective-permute-start.9 = (bf16[128,384]{1,0:T(8,128)(2,1)S(1)}, bf16[128,384]{1,0:T(8,128)(2,1)S(1)}, u32[]{:S(2)}, u32[]{:S(2)}) collective-permute-start(bf16[128,384]{1,0:T(8,128)(2,1)S(1)} %dattn.1.d_own_ref), channel_id=1, source_target_pairs={{0,16},{4,20},{8,24},{12,28},{16,0},{20,4},{24,8},{28,12},{1,17},{... | collective-permute-start | bytes 294920 | tf_op jit(solution)/shard_map/ppermute | solution.py:35
  21.1 0.9 %copy-start.2 = (bf16[128,384]{1,0:T(8,128)(2,1)S(1)}, bf16[128,384]{1,0:T(8,128)(2,1)}, u32[]{:S(2)}) copy-start(bf16[128,384]{1,0:T(8,128)(2,1)} %q_own_ref.3) | copy-start | bytes 294916
  22.0 0.9 %copy-start.5 = (bf16[128,384]{1,0:T(8,128)(2,1)S(1)}, bf16[128,384]{1,0:T(8,128)(2,1)}, u32[]{:S(2)}) copy-start(bf16[128,384]{1,0:T(8,128)(2,1)} %copy-done.4) | copy-start | bytes 294916
  22.9 10.3 %copy-start.3 = (bf16[128,384]{1,0:T(8,128)(2,1)S(1)}, bf16[128,384]{1,0:T(8,128)(2,1)}, u32[]{:S(2)}) copy-start(bf16[128,384]{1,0:T(8,128)(2,1)} %q_own_ref.3) | copy-start | bytes 294916
  22.9 10.3 %copy-start.6 = (bf16[128,384]{1,0:T(8,128)(2,1)S(1)}, bf16[128,384]{1,0:T(8,128)(2,1)}, u32[]{:S(2)}) copy-start(bf16[128,384]{1,0:T(8,128)(2,1)} %copy-done.4) | copy-start | bytes 294916
  24.8 9.5 %collective-permute-start.8 = (bf16[384,128]{1,0:T(8,128)(2,1)S(1)}, bf16[384,128]{1,0:T(8,128)(2,1)S(1)}, u32[]{:S(2)}, u32[]{:S(2)}) collective-permute-start(bf16[384,128]{1,0:T(8,128)(2,1)S(1)} %get-tuple-element.53), channel_id=1, source_target_pairs={{0,16},{4,20},{8,24},{12,28},{16,0},{20,4},{24,8},{28,12},{1,17},{... | collective-permute-start | bytes 294920 | tf_op jit(solution)/shard_map/ppermute | solution.py:35
  27.3 5.8 %collective-permute-start.10 = (f32[16,256]{1,0:T(8,128)S(1)}, f32[16,256]{1,0:T(8,128)S(1)}, u32[]{:S(2)}, u32[]{:S(2)}) collective-permute-start(f32[16,256]{1,0:T(8,128)S(1)} %get-tuple-element.56.stats_ref), channel_id=1, source_target_pairs={{0,16},{4,20},{8,24},{12,28},{16,0},{20,4},{24,8},{28,12},{1,17},{... | collective-permute-start | bytes 49160 | tf_op jit(solution)/shard_map/ppermute | solution.py:35
  34.3 6.3 %collective-permute-start.15 = (bf16[320,384]{1,0:T(8,128)(2,1)S(1)}, bf16[320,384]{1,0:T(8,128)(2,1)S(1)}, u32[]{:S(2)}, u32[]{:S(2)}) collective-permute-start(bf16[320,384]{1,0:T(8,128)(2,1)S(1)} %get-tuple-element.68), channel_id=1, source_target_pairs={{0,4},{4,0},{8,12},{12,8},{16,20},{20,16},{24,28},{28,24},{1,5},{5... | collective-permute-start | bytes 737288 | tf_op jit(solution)/shard_map/ppermute | solution.py:35
  35.2 7.7 %collective-permute-start.16 = (bf16[320,384]{1,0:T(8,128)(2,1)S(1)}, bf16[320,384]{1,0:T(8,128)(2,1)S(1)}, u32[]{:S(2)}, u32[]{:S(2)}) collective-permute-start(bf16[320,384]{1,0:T(8,128)(2,1)S(1)} %get-tuple-element.69), channel_id=1, source_target_pairs={{0,8},{4,12},{8,0},{12,4},{16,24},{20,28},{24,16},{28,20},{1,9},{5... | collective-permute-start | bytes 737288 | tf_op jit(solution)/shard_map/ppermute | solution.py:35
  35.7 7.3 %collective-permute-start.13 = (bf16[128,384]{1,0:T(8,128)(2,1)S(1)}, bf16[128,384]{1,0:T(8,128)(2,1)S(1)}, u32[]{:S(2)}, u32[]{:S(2)}) collective-permute-start(bf16[128,384]{1,0:T(8,128)(2,1)S(1)} %get-tuple-element.65), channel_id=1, source_target_pairs={{0,16},{4,20},{8,24},{12,28},{16,0},{20,4},{24,8},{28,12},{1,17},{... | collective-permute-start | bytes 294920 | tf_op jit(solution)/shard_map/ppermute | solution.py:35
  38.5 7.5 %collective-permute-start.11 = (bf16[128,768]{1,0:T(8,128)(2,1)S(1)}, bf16[128,768]{1,0:T(8,128)(2,1)S(1)}, u32[]{:S(2)}, u32[]{:S(2)}) collective-permute-start(bf16[128,768]{1,0:T(8,128)(2,1)S(1)} %get-tuple-element.62), channel_id=1, source_target_pairs={{0,2},{1,3},{2,0},{3,1},{4,6},{5,7},{6,4},{7,5},{8,10},{9,11},{10,... | collective-permute-start | bytes 589832 | tf_op jit(solution)/shard_map/ppermute | solution.py:35
  39.6 7.4 %collective-permute-start.12 = (bf16[128,768]{1,0:T(8,128)(2,1)S(1)}, bf16[128,768]{1,0:T(8,128)(2,1)S(1)}, u32[]{:S(2)}, u32[]{:S(2)}) collective-permute-start(bf16[128,768]{1,0:T(8,128)(2,1)S(1)} %get-tuple-element.63), channel_id=1, source_target_pairs={{0,3},{1,2},{2,1},{3,0},{4,7},{5,6},{6,5},{7,4},{8,11},{9,10},{10,... | collective-permute-start | bytes 589832 | tf_op jit(solution)/shard_map/ppermute | solution.py:35
  40.5 6.5 %collective-permute-start.14 = (bf16[128,768]{1,0:T(8,128)(2,1)S(1)}, bf16[128,768]{1,0:T(8,128)(2,1)S(1)}, u32[]{:S(2)}, u32[]{:S(2)}) collective-permute-start(bf16[128,768]{1,0:T(8,128)(2,1)S(1)} %get-tuple-element.66), channel_id=1, source_target_pairs={{0,1},{1,0},{2,3},{3,2},{4,5},{5,4},{6,7},{7,6},{8,9},{9,8},{10,11... | collective-permute-start | bytes 589832 | tf_op jit(solution)/shard_map/ppermute | solution.py:35
  42.9 4.9 %collective-permute-start.17 = (bf16[160,384]{1,0:T(8,128)(2,1)S(1)}, bf16[160,384]{1,0:T(8,128)(2,1)S(1)}, u32[]{:S(2)}, u32[]{:S(2)}) collective-permute-start(bf16[160,384]{1,0:T(8,128)(2,1)S(1)} %get-tuple-element.72), channel_id=1, source_target_pairs={{0,8},{4,12},{8,0},{12,4},{16,24},{20,28},{24,16},{28,20},{1,9},{5... | collective-permute-start | bytes 368648 | tf_op jit(solution)/shard_map/ppermute | solution.py:35
  43.0 4.9 %collective-permute-start.18 = (bf16[160,384]{1,0:T(8,128)(2,1)S(1)}, bf16[160,384]{1,0:T(8,128)(2,1)S(1)}, u32[]{:S(2)}, u32[]{:S(2)}) collective-permute-start(bf16[160,384]{1,0:T(8,128)(2,1)S(1)} %get-tuple-element.73), channel_id=1, source_target_pairs={{0,4},{4,0},{8,12},{12,8},{16,20},{20,16},{24,28},{28,24},{1,5},{5... | collective-permute-start | bytes 368648 | tf_op jit(solution)/shard_map/ppermute | solution.py:35

commit v13 on v12

--- a/solution.py
+++ b/solution.py
@@ -47,7 +47,7 @@
         out_shape=out_shapes,
         in_specs=[pl.BlockSpec(memory_space=space) for space in spaces],
         out_specs=[pl.BlockSpec(memory_space=pltpu.VMEM)] * len(out_shapes),
-        compiler_params=pltpu.CompilerParams(vmem_limit_bytes=40 * 2**20),
+        compiler_params=pltpu.CompilerParams(vmem_limit_bytes=20 * 2**20),
         cost_estimate=cost_of(micros),
     )(*args)
 
@@ -328,12 +328,6 @@
     )[0]
     kv1, kv2, d_own = lax.optimization_barrier((kv1, kv2, d_own))
     key3 = local_call(pass_keys_kernel, "pass_keys", 0.1, [shape((keys, width), BF16)], (kv2,))[0]
-    kv2_kept, q_pair, _ = lax.optimization_barrier((kv2, q_pair, key3))
-    value3 = local_call(
-        pass_values_kernel, "pass_values", 1.0, [shape((keys, width), BF16)], (kv2_kept,)
-    )[0]
-    kvs = [kv0, kv1, kv2, swap(key3, "ctx", 1), swap(value3, "ctx", 1)]
-    d_pair = swap(d_own, "ctx", PAIR)
     limits = local_call(
         limits_kernel,
         "limits",
@@ -342,6 +336,12 @@
         (frame_levels, frame_counts),
         tables=2,
     )[0]
+    kv2_kept, q_pair, limits, _ = lax.optimization_barrier((kv2, q_pair, limits, key3))
+    value3 = local_call(
+        pass_values_kernel, "pass_values", 1.0, [shape((keys, width), BF16)], (kv2_kept,)
+    )[0]
+    kvs = [kv0, kv1, kv2, swap(key3, "ctx", 1), swap(value3, "ctx", 1)]
+    d_pair = swap(d_own, "ctx", PAIR)
     lse, probs = local_call(
         scores_kernel,
         "scores",

time: 49.1 us -> 49 us (level)
  waiting for transfers between devices: 14.6 us -> 17.6 us
  local copies, waits for them, and re-layouts: 1.9 us -> 0.11 us
  starting transfers between devices: 20.9 us -> 19.8 us
    ppermute x19, waiting for transfers between devices: 14.6 us -> 17.6 us  [swap(): return lax.ppermute(block, axis, [(i, i ^ bit) for i in range(count)])]
    unnamed x21 -> x11, local copies, waits for them, and re-layouts: 1.9 us -> 0.11 us
    ppermute x19, starting transfers between devices: 20.9 us -> 19.8 us  [swap(): return lax.ppermute(block, axis, [(i, i ^ bit) for i in range(count)])]
  transfers between devices with their start and end apart: 19 -> 19, of which waited for: 10 -> 11; matrix products, arithmetic and copies ran while one was open for 0% -> 0% of each run, Pallas kernels for 20% -> 20%
where the time goes in v13:
time: 49 us; the launch traced here: 48.8 us
  starting transfers between devices  19.8 us (40%)
  waiting for transfers between devices  17.6 us (36%)
  Pallas kernels  10.5 us (21%)
  between operations  0.84 us (2%)
    ppermute x19, starting transfers between devices, swap(): return lax.ppermute(block, axis, [(i, i ^ bit) for i in range(count)])  19.8 us
    ppermute x19, waiting for transfers between devices, swap(): return lax.ppermute(block, axis, [(i, i ^ bit) for i in range(count)])  17.6 us
    pallas_call x11, Pallas kernels, local_call(): pl.pallas_call(body, name=name, out_shape=out_shapes, in_specs=[pl.BlockS...  7.15 us
    pallas_call x1, Pallas kernels, load_keys(): pl.pallas_call(load_kernel, name='load', out_shape=jax.ShapeDtypeStruct((...  1.67 us
    pallas_call x1, Pallas kernels, load_weight(): pl.pallas_call(load_weight_kernel, name='load_w', out_shape=jax.ShapeDtyp...  1.63 us
  transfers between devices with their start and end apart: 19, of which 11 were waited for; matrix products, arithmetic and copies ran while one was open for 0% of the time, Pallas kernels for 20%

profile of v13, /device:TPU:0, one launch (start us, length us, event | category | flops | bytes accessed | tf_op | source)
XLA Modules:
  0.0 48.8 jit_solution(6311705265152199649)
XLA Ops:
  0.6 3.0 %collective-permute-start.3 = (bf16[128,768]{1,0:T(8,128)(2,1)}, bf16[128,768]{1,0:T(8,128)(2,1)}, u32[]{:S(2)}, u32[]{:S(2)}) collective-permute-start(bf16[128,768]{1,0:T(8,128)(2,1)} %own_ref.1), channel_id=1, source_target_pairs={{0,2},{1,3},{2,0},{3,1},{4,6},{5,7},{6,4},{7,5},{8,10},{9,11},{10,... | collective-permute-start | bytes 589832 | tf_op jit(solution)/shard_map/ppermute | solution.py:35
  3.6 1.7 %load.1.kv0 = bf16[320,384]{1,0:T(8,128)(2,1)} custom-call(bf16[128,384]{1,0:T(8,128)(2,1)} %k_ref.1, bf16[32,384]{1,0:T(8,128)(2,1)} %hk_ref.1, bf16[128,384]{1,0:T(8,128)(2,1)} %v_ref.1, bf16[32,384]{1,0:T(8,128)(2,1)} %hv_ref.1), custom_call_target="tpu_custom_call" | custom-call | bytes 5904000 | tf_op jit(solution)/shard_map/load/pallas_call | solution.py:74
  5.3 0.0 copy-start.1
  5.3 0.0 copy-start.4
  5.3 0.0 copy-start.3
  5.3 0.0 copy-start.2
  5.4 1.6 %collective-permute-start.1 = (bf16[320,384]{1,0:T(8,128)(2,1)}, bf16[320,384]{1,0:T(8,128)(2,1)S(1)}, u32[]{:S(2)}, u32[]{:S(2)}) collective-permute-start(bf16[320,384]{1,0:T(8,128)(2,1)} %load.1.kv0), channel_id=1, source_target_pairs={{0,8},{4,12},{8,0},{12,4},{16,24},{20,28},{24,16},{28,20},{1,9},{5... | collective-permute-start | bytes 737288 | tf_op jit(solution)/shard_map/ppermute | solution.py:35
  7.0 1.5 %collective-permute-start = (bf16[320,384]{1,0:T(8,128)(2,1)}, bf16[320,384]{1,0:T(8,128)(2,1)S(1)}, u32[]{:S(2)}, u32[]{:S(2)}) collective-permute-start(bf16[320,384]{1,0:T(8,128)(2,1)} %load.1.kv0), channel_id=1, source_target_pairs={{0,4},{4,0},{8,12},{12,8},{16,20},{20,16},{24,28},{28,24},{1,5},{5... | collective-permute-start | bytes 737288 | tf_op jit(solution)/shard_map/ppermute | solution.py:35
  8.5 0.0 collective-permute-start.2
  8.5 1.6 %load_w.1.w_ref = bf16[384,3072]{1,0:T(8,128)(2,1)S(1)} custom-call(bf16[384,3072]{1,0:T(8,128)(2,1)} %w_ref.1), custom_call_target="tpu_custom_call" | custom-call | bytes 5904000 | tf_op jit(solution)/shard_map/load_w/pallas_call | solution.py:112
  10.2 0.6 %collective-permute-start.4 = (bf16[128,768]{1,0:T(8,128)(2,1)}, bf16[128,768]{1,0:T(8,128)(2,1)}, u32[]{:S(2)}, u32[]{:S(2)}) collective-permute-start(bf16[128,768]{1,0:T(8,128)(2,1)} %collective-permute-done.3.near_ref), channel_id=1, source_target_pairs={{0,1},{1,0},{2,3},{3,2},{4,5},{5,4},{6,7},{7,6},{8,9},{9,8},{10,11... | collective-permute-start | bytes 589832 | tf_op jit(solution)/shard_map/ppermute | solution.py:35
  10.8 2.6 %collective-permute-start.5 = (bf16[128,384]{1,0:T(8,128)(2,1)S(1)}, bf16[128,384]{1,0:T(8,128)(2,1)S(1)}, u32[]{:S(2)}, u32[]{:S(2)}) collective-permute-start(bf16[128,384]{1,0:T(8,128)(2,1)S(1)} %copy-done.1), channel_id=1, source_target_pairs={{0,16},{4,20},{8,24},{12,28},{16,0},{20,4},{24,8},{28,12},{1,17},{... | collective-permute-start | bytes 294920 | tf_op jit(solution)/shard_map/ppermute | solution.py:35
  13.4 0.1 copy.15.levels_ref
  13.4 0.6 %limits.1.limits_ref = s32[8,256]{1,0:T(8,128)S(1)} custom-call(s32[8,2]{1,0:T(8,128)S(1)} %copy.15.levels_ref, s32[8]{0:T(128)S(1)} %copy-done.3), custom_call_target="tpu_custom_call" | custom-call | bytes 2214000 | tf_op jit(solution)/shard_map/limits/pallas_call | solution.py:44
  14.1 0.0 collective-permute-done.2.core_ref
  14.1 1.9 %dattn.1.d_own_ref = bf16[128,384]{1,0:T(8,128)(2,1)S(1)} custom-call(bf16[128,768]{1,0:T(8,128)(2,1)S(1)} %copy-done.2, bf16[128,768]{1,0:T(8,128)(2,1)} %collective-permute-done.2.core_ref, bf16[128,768]{1,0:T(8,128)(2,1)} %collective-permute-done.3.near_ref, bf16[128,768]{1,0:T(8,128)(2,1)} %collective-permute-done.4.far_ref, ...), custom_call_target="tpu_custom_call" | custom-call | bytes 2952000 | tf_op jit(solution)/shard_map/dattn/pallas_call | solution.py:44
  16.1 0.0 collective-permute-done.1.kv2
  16.1 0.6 %collective-permute-start.6 = (bf16[160,384]{1,0:T(8,128)(2,1)S(1)}, bf16[160,384]{1,0:T(8,128)(2,1)S(1)}, u32[]{:S(2)}, u32[]{:S(2)}) collective-permute-start(bf16[160,384]{1,0:T(8,128)(2,1)S(1)} %pass_keys.1), channel_id=1, source_target_pairs={{0,4},{4,0},{8,12},{12,8},{16,20},{20,16},{24,28},{28,24},{1,5},{5... | collective-permute-start | bytes 368648 | tf_op jit(solution)/shard_map/ppermute | solution.py:35
  16.7 1.9 %collective-permute-done.5.q_pair_ref = bf16[128,384]{1,0:T(8,128)(2,1)S(1)} collective-permute-done((bf16[128,384]{1,0:T(8,128)(2,1)S(1)}, bf16[128,384]{1,0:T(8,128)(2,1)S(1)}, u32[]{:S(2)}, u32[]{:S(2)}) %collective-permute-start.5) | collective-permute-done | bytes 98336 | tf_op jit(solution)/shard_map/ppermute | solution.py:35
  18.5 0.6 %collective-permute-start.7 = (bf16[160,384]{1,0:T(8,128)(2,1)S(1)}, bf16[160,384]{1,0:T(8,128)(2,1)S(1)}, u32[]{:S(2)}, u32[]{:S(2)}) collective-permute-start(bf16[160,384]{1,0:T(8,128)(2,1)S(1)} %pass_values.1), channel_id=1, source_target_pairs={{0,4},{4,0},{8,12},{12,8},{16,20},{20,16},{24,28},{28,24},{1,5},{5... | collective-permute-start | bytes 368648 | tf_op jit(solution)/shard_map/ppermute | solution.py:35
  19.1 0.6 %collective-permute-start.9 = (bf16[128,384]{1,0:T(8,128)(2,1)S(1)}, bf16[128,384]{1,0:T(8,128)(2,1)S(1)}, u32[]{:S(2)}, u32[]{:S(2)}) collective-permute-start(bf16[128,384]{1,0:T(8,128)(2,1)S(1)} %dattn.1.d_own_ref), channel_id=1, source_target_pairs={{0,16},{4,20},{8,24},{12,28},{16,0},{20,4},{24,8},{28,12},{1,17},{... | collective-permute-start | bytes 294920 | tf_op jit(solution)/shard_map/ppermute | solution.py:35
  19.7 1.8 %collective-permute-done.6.key3 = bf16[160,384]{1,0:T(8,128)(2,1)S(1)} collective-permute-done((bf16[160,384]{1,0:T(8,128)(2,1)S(1)}, bf16[160,384]{1,0:T(8,128)(2,1)S(1)}, u32[]{:S(2)}, u32[]{:S(2)}) %collective-permute-start.6) | collective-permute-done | bytes 122912 | tf_op jit(solution)/shard_map/ppermute | solution.py:35
  21.5 1.0 %scores.1 = (f32[8,256]{1,0:T(8,128)S(1)}, bf16[1920,256]{1,0:T(8,128)(2,1)S(1)}) custom-call(s32[8,256]{1,0:T(8,128)S(1)} %limits.1.limits_ref, bf16[128,384]{1,0:T(8,128)(2,1)S(1)} %copy-done.1, bf16[128,384]{1,0:T(8,128)(2,1)S(1)} %collective-permute-done.5.q_pair_ref, bf16[320,384]{1,0:T(8,128)(2,1)S(1)} %copy-done, ...), custom_call_target="tpu_custom_call" | custom-call | bytes 3321000 | tf_op jit(solution)/shard_map/scores/pallas_call | solution.py:44
  22.5 1.3 %collective-permute-done.7.value3 = bf16[160,384]{1,0:T(8,128)(2,1)S(1)} collective-permute-done((bf16[160,384]{1,0:T(8,128)(2,1)S(1)}, bf16[160,384]{1,0:T(8,128)(2,1)S(1)}, u32[]{:S(2)}, u32[]{:S(2)}) %collective-permute-start.7) | collective-permute-done | bytes 122912 | tf_op jit(solution)/shard_map/ppermute | solution.py:35
  23.8 0.4 attn.1
  24.3 1.3 %collective-permute-start.8 = (bf16[384,128]{1,0:T(8,128)(2,1)S(1)}, bf16[384,128]{1,0:T(8,128)(2,1)S(1)}, u32[]{:S(2)}, u32[]{:S(2)}) collective-permute-start(bf16[384,128]{1,0:T(8,128)(2,1)S(1)} %get-tuple-element.55), channel_id=1, source_target_pairs={{0,16},{4,20},{8,24},{12,28},{16,0},{20,4},{24,8},{28,12},{1,17},{... | collective-permute-start | bytes 294920 | tf_op jit(solution)/shard_map/ppermute | solution.py:35
  25.5 0.6 %collective-permute-done.9.d_pair_ref = bf16[128,384]{1,0:T(8,128)(2,1)S(1)} collective-permute-done((bf16[128,384]{1,0:T(8,128)(2,1)S(1)}, bf16[128,384]{1,0:T(8,128)(2,1)S(1)}, u32[]{:S(2)}, u32[]{:S(2)}) %collective-permute-start.9) | collective-permute-done | bytes 98336 | tf_op jit(solution)/shard_map/ppermute | solution.py:35
  26.2 0.4 delta.1
  26.6 1.2 %collective-permute-start.10 = (f32[16,256]{1,0:T(8,128)S(1)}, f32[16,256]{1,0:T(8,128)S(1)}, u32[]{:S(2)}, u32[]{:S(2)}) collective-permute-start(f32[16,256]{1,0:T(8,128)S(1)} %get-tuple-element.58.stats_ref), channel_id=1, source_target_pairs={{0,16},{4,20},{8,24},{12,28},{16,0},{20,4},{24,8},{28,12},{1,17},{... | collective-permute-start | bytes 49160 | tf_op jit(solution)/shard_map/ppermute | solution.py:35
  27.8 4.1 %collective-permute-done.10.stats_pair_ref = f32[16,256]{1,0:T(8,128)S(1)} collective-permute-done((f32[16,256]{1,0:T(8,128)S(1)}, f32[16,256]{1,0:T(8,128)S(1)}, u32[]{:S(2)}, u32[]{:S(2)}) %collective-permute-start.10) | collective-permute-done | bytes 16416 | tf_op jit(solution)/shard_map/ppermute | solution.py:35
  31.8 1.1 %backward.1 = (f32[128,384]{1,0:T(8,128)S(1)}, bf16[128,384]{1,0:T(8,128)(2,1)S(1)}, f32[320,384]{1,0:T(8,128)S(1)}, bf16[320,384]{1,0:T(8,128)(2,1)S(1)}, bf16[...) custom-call(bf16[128,384]{1,0:T(8,128)(2,1)S(1)} %copy-done.1, ...), custom_call_target="tpu_custom_call" | custom-call | bytes 4059000 | tf_op jit(solution)/shard_map/backward/pallas_call | solution.py:44
  32.9 0.0 collective-permute-done.8.pair_ref
  32.9 1.1 %collective-permute-start.15 = (bf16[320,384]{1,0:T(8,128)(2,1)S(1)}, bf16[320,384]{1,0:T(8,128)(2,1)S(1)}, u32[]{:S(2)}, u32[]{:S(2)}) collective-permute-start(bf16[320,384]{1,0:T(8,128)(2,1)S(1)} %get-tuple-element.70), channel_id=1, source_target_pairs={{0,4},{4,0},{8,12},{12,8},{16,20},{20,16},{24,28},{28,24},{1,5},{5... | collective-permute-start | bytes 737288 | tf_op jit(solution)/shard_map/ppermute | solution.py:35
  34.0 1.0 %collective-permute-start.16 = (bf16[320,384]{1,0:T(8,128)(2,1)S(1)}, bf16[320,384]{1,0:T(8,128)(2,1)S(1)}, u32[]{:S(2)}, u32[]{:S(2)}) collective-permute-start(bf16[320,384]{1,0:T(8,128)(2,1)S(1)} %get-tuple-element.71), channel_id=1, source_target_pairs={{0,8},{4,12},{8,0},{12,4},{16,24},{20,28},{24,16},{28,20},{1,9},{5... | collective-permute-start | bytes 737288 | tf_op jit(solution)/shard_map/ppermute | solution.py:35
  35.1 2.1 %collective-permute-start.13 = (bf16[128,384]{1,0:T(8,128)(2,1)S(1)}, bf16[128,384]{1,0:T(8,128)(2,1)S(1)}, u32[]{:S(2)}, u32[]{:S(2)}) collective-permute-start(bf16[128,384]{1,0:T(8,128)(2,1)S(1)} %get-tuple-element.67), channel_id=1, source_target_pairs={{0,16},{4,20},{8,24},{12,28},{16,0},{20,4},{24,8},{28,12},{1,17},{... | collective-permute-start | bytes 294920 | tf_op jit(solution)/shard_map/ppermute | solution.py:35
  37.1 0.6 %project.1 = (f32[128,768]{1,0:T(8,128)S(1)}, bf16[128,768]{1,0:T(8,128)(2,1)S(1)}, bf16[128,768]{1,0:T(8,128)(2,1)S(1)}, bf16[128,768]{1,0:T(8,128)(2,1)S(1)}) custom-call(f32[384,128]{1,0:T(8,128)S(1)} %get-tuple-element.54.own_ref, bf16[384,128]{1,0:T(8,128)(2,1)S(1)} %collective-permute-done.8.pair_ref, f32[16,256]{1,0:T(8,128)S(1)} %get-tuple-element.58.stats_ref, ...), custom_call_target="tpu_custom_call" | custom-call | bytes 2214000 | tf_op jit(solution)/shard_map/project/pallas_call | solution.py:44
  37.7 1.0 %collective-permute-start.11 = (bf16[128,768]{1,0:T(8,128)(2,1)S(1)}, bf16[128,768]{1,0:T(8,128)(2,1)S(1)}, u32[]{:S(2)}, u32[]{:S(2)}) collective-permute-start(bf16[128,768]{1,0:T(8,128)(2,1)S(1)} %get-tuple-element.64), channel_id=1, source_target_pairs={{0,2},{1,3},{2,0},{3,1},{4,6},{5,7},{6,4},{7,5},{8,10},{9,11},{10,... | collective-permute-start | bytes 589832 | tf_op jit(solution)/shard_map/ppermute | solution.py:35
  38.7 0.0 collective-permute-start.12
  38.7 1.2 %collective-permute-done.15.got_k_ref = bf16[320,384]{1,0:T(8,128)(2,1)S(1)} collective-permute-done((bf16[320,384]{1,0:T(8,128)(2,1)S(1)}, bf16[320,384]{1,0:T(8,128)(2,1)S(1)}, u32[]{:S(2)}, u32[]{:S(2)}) %collective-permute-start.15) | collective-permute-done | bytes 245792 | tf_op jit(solution)/shard_map/ppermute | solution.py:35
  39.9 0.0 collective-permute-start.14
  40.0 2.9 %collective-permute-done.16.got_v_ref = bf16[320,384]{1,0:T(8,128)(2,1)S(1)} collective-permute-done((bf16[320,384]{1,0:T(8,128)(2,1)S(1)}, bf16[320,384]{1,0:T(8,128)(2,1)S(1)}, u32[]{:S(2)}, u32[]{:S(2)}) %collective-permute-start.16) | collective-permute-done | bytes 245792 | tf_op jit(solution)/shard_map/ppermute | solution.py:35
  42.9 0.1 collective-permute-start.17
  43.0 1.0 %collective-permute-start.18 = (bf16[160,384]{1,0:T(8,128)(2,1)S(1)}, bf16[160,384]{1,0:T(8,128)(2,1)S(1)}, u32[]{:S(2)}, u32[]{:S(2)}) collective-permute-start(bf16[160,384]{1,0:T(8,128)(2,1)S(1)} %get-tuple-element.75), channel_id=1, source_target_pairs={{0,4},{4,0},{8,12},{12,8},{16,20},{20,16},{24,28},{28,24},{1,5},{5... | collective-permute-start | bytes 368648 | tf_op jit(solution)/shard_map/ppermute | solution.py:35
  44.0 1.4 %collective-permute-done.11.near_ref = bf16[128,768]{1,0:T(8,128)(2,1)S(1)} collective-permute-done((bf16[128,768]{1,0:T(8,128)(2,1)S(1)}, bf16[128,768]{1,0:T(8,128)(2,1)S(1)}, u32[]{:S(2)}, u32[]{:S(2)}) %collective-permute-start.11) | collective-permute-done | bytes 196640 | tf_op jit(solution)/shard_map/ppermute | solution.py:35
  45.3 0.8 %collective-permute-done.12.far_ref = bf16[128,768]{1,0:T(8,128)(2,1)S(1)} collective-permute-done((bf16[128,768]{1,0:T(8,128)(2,1)S(1)}, bf16[128,768]{1,0:T(8,128)(2,1)S(1)}, u32[]{:S(2)}, u32[]{:S(2)}) %collective-permute-start.12) | collective-permute-done | bytes 196640 | tf_op jit(solution)/shard_map/ppermute | solution.py:35
  46.1 1.7 %collective-permute-done.17.rest_k_ref = bf16[160,384]{1,0:T(8,128)(2,1)S(1)} collective-permute-done((bf16[160,384]{1,0:T(8,128)(2,1)S(1)}, bf16[160,384]{1,0:T(8,128)(2,1)S(1)}, u32[]{:S(2)}, u32[]{:S(2)}) %collective-permute-start.17) | collective-permute-done | bytes 122912 | tf_op jit(solution)/shard_map/ppermute | solution.py:35
  47.8 0.1 collective-permute-done.18.rest_v_ref
  47.9 0.9 %finish.1 = (bf16[128,384]{1,0:T(8,128)(2,1)}, bf16[128,384]{1,0:T(8,128)(2,1)}, bf16[128,384]{1,0:T(8,128)(2,1)}, bf16[32,384]{1,0:T(8,128)(2,1)}, bf16[32,384]{1,0:T(8,128)(2,1)}, /*index=5*/bf16[128,768]{1,0:T(8,128)(2,1)}) custom-call(f32[128,768]{1,0:T(8,128)S(1)} %get-tuple-element.63.keep_ref, bf16[128,768]{1,0:T(8,128)(2,1)S(1)} %collective-permute-done.11.near_ref, ...), custom_call_target="tpu_custom_call" | custom-call | bytes 3321000 | tf_op jit(solution)/shard_map/finish/pallas_call | solution.py:44
  (14 shorter events, 0.1 us)
Async XLA Ops:
  0.6 9.5 %collective-permute-start.3 = (bf16[128,768]{1,0:T(8,128)(2,1)}, bf16[128,768]{1,0:T(8,128)(2,1)}, u32[]{:S(2)}, u32[]{:S(2)}) collective-permute-start(bf16[128,768]{1,0:T(8,128)(2,1)} %own_ref.1), channel_id=1, source_target_pairs={{0,2},{1,3},{2,0},{3,1},{4,6},{5,7},{6,4},{7,5},{8,10},{9,11},{10,... | collective-permute-start | bytes 589832 | tf_op jit(solution)/shard_map/ppermute | solution.py:35
  5.3 5.4 %copy-start.1 = (bf16[128,384]{1,0:T(8,128)(2,1)S(1)}, bf16[128,384]{1,0:T(8,128)(2,1)}, u32[]{:S(2)}) copy-start(bf16[128,384]{1,0:T(8,128)(2,1)} %q_own_ref.3) | copy-start | bytes 294916
  5.3 8.0 %copy-start.4 = (s32[8,2]{0,1:T(2,128)S(1)}, s32[8,2]{0,1:T(2,128)}, u32[]{:S(2)}) copy-start(s32[8,2]{0,1:T(2,128)} %param.14) | copy-start | bytes 196
  5.3 8.1 %copy-start.3 = (s32[8]{0:T(128)S(1)}, s32[8]{0:T(128)}, u32[]{:S(2)}) copy-start(s32[8]{0:T(128)} %counts_ref.1) | copy-start | bytes 100
  5.3 8.7 %copy-start.2 = (bf16[128,768]{1,0:T(8,128)(2,1)S(1)}, bf16[128,768]{1,0:T(8,128)(2,1)}, u32[]{:S(2)}) copy-start(bf16[128,768]{1,0:T(8,128)(2,1)} %own_ref.1) | copy-start | bytes 589828
  5.4 10.7 %collective-permute-start.1 = (bf16[320,384]{1,0:T(8,128)(2,1)}, bf16[320,384]{1,0:T(8,128)(2,1)S(1)}, u32[]{:S(2)}, u32[]{:S(2)}) collective-permute-start(bf16[320,384]{1,0:T(8,128)(2,1)} %load.1.kv0), channel_id=1, source_target_pairs={{0,8},{4,12},{8,0},{12,4},{16,24},{20,28},{24,16},{28,20},{1,9},{5... | collective-permute-start | bytes 737288 | tf_op jit(solution)/shard_map/ppermute | solution.py:35
  7.0 9.1 %collective-permute-start = (bf16[320,384]{1,0:T(8,128)(2,1)}, bf16[320,384]{1,0:T(8,128)(2,1)S(1)}, u32[]{:S(2)}, u32[]{:S(2)}) collective-permute-start(bf16[320,384]{1,0:T(8,128)(2,1)} %load.1.kv0), channel_id=1, source_target_pairs={{0,4},{4,0},{8,12},{12,8},{16,20},{20,16},{24,28},{28,24},{1,5},{5... | collective-permute-start | bytes 737288 | tf_op jit(solution)/shard_map/ppermute | solution.py:35
  8.5 5.6 %collective-permute-start.2 = (bf16[128,768]{1,0:T(8,128)(2,1)}, bf16[128,768]{1,0:T(8,128)(2,1)}, u32[]{:S(2)}, u32[]{:S(2)}) collective-permute-start(bf16[128,768]{1,0:T(8,128)(2,1)} %own_ref.1), channel_id=1, source_target_pairs={{0,1},{1,0},{2,3},{3,2},{4,5},{5,4},{6,7},{7,6},{8,9},{9,8},{10,11... | collective-permute-start | bytes 589832 | tf_op jit(solution)/shard_map/ppermute | solution.py:35
  10.2 11.3 %copy-start = (bf16[320,384]{1,0:T(8,128)(2,1)S(1)}, bf16[320,384]{1,0:T(8,128)(2,1)}, u32[]{:S(2)}) copy-start(bf16[320,384]{1,0:T(8,128)(2,1)} %load.1.kv0) | copy-start | bytes 737284
  10.2 3.9 %collective-permute-start.4 = (bf16[128,768]{1,0:T(8,128)(2,1)}, bf16[128,768]{1,0:T(8,128)(2,1)}, u32[]{:S(2)}, u32[]{:S(2)}) collective-permute-start(bf16[128,768]{1,0:T(8,128)(2,1)} %collective-permute-done.3.near_ref), channel_id=1, source_target_pairs={{0,1},{1,0},{2,3},{3,2},{4,5},{5,4},{6,7},{7,6},{8,9},{9,8},{10,11... | collective-permute-start | bytes 589832 | tf_op jit(solution)/shard_map/ppermute | solution.py:35
  10.8 7.8 %collective-permute-start.5 = (bf16[128,384]{1,0:T(8,128)(2,1)S(1)}, bf16[128,384]{1,0:T(8,128)(2,1)S(1)}, u32[]{:S(2)}, u32[]{:S(2)}) collective-permute-start(bf16[128,384]{1,0:T(8,128)(2,1)S(1)} %copy-done.1), channel_id=1, source_target_pairs={{0,16},{4,20},{8,24},{12,28},{16,0},{20,4},{24,8},{28,12},{1,17},{... | collective-permute-start | bytes 294920 | tf_op jit(solution)/shard_map/ppermute | solution.py:35
  16.1 5.4 %collective-permute-start.6 = (bf16[160,384]{1,0:T(8,128)(2,1)S(1)}, bf16[160,384]{1,0:T(8,128)(2,1)S(1)}, u32[]{:S(2)}, u32[]{:S(2)}) collective-permute-start(bf16[160,384]{1,0:T(8,128)(2,1)S(1)} %pass_keys.1), channel_id=1, source_target_pairs={{0,4},{4,0},{8,12},{12,8},{16,20},{20,16},{24,28},{28,24},{1,5},{5... | collective-permute-start | bytes 368648 | tf_op jit(solution)/shard_map/ppermute | solution.py:35
  18.5 5.3 %collective-permute-start.7 = (bf16[160,384]{1,0:T(8,128)(2,1)S(1)}, bf16[160,384]{1,0:T(8,128)(2,1)S(1)}, u32[]{:S(2)}, u32[]{:S(2)}) collective-permute-start(bf16[160,384]{1,0:T(8,128)(2,1)S(1)} %pass_values.1), channel_id=1, source_target_pairs={{0,4},{4,0},{8,12},{12,8},{16,20},{20,16},{24,28},{28,24},{1,5},{5... | collective-permute-start | bytes 368648 | tf_op jit(solution)/shard_map/ppermute | solution.py:35
  19.1 7.0 %collective-permute-start.9 = (bf16[128,384]{1,0:T(8,128)(2,1)S(1)}, bf16[128,384]{1,0:T(8,128)(2,1)S(1)}, u32[]{:S(2)}, u32[]{:S(2)}) collective-permute-start(bf16[128,384]{1,0:T(8,128)(2,1)S(1)} %dattn.1.d_own_ref), channel_id=1, source_target_pairs={{0,16},{4,20},{8,24},{12,28},{16,0},{20,4},{24,8},{28,12},{1,17},{... | collective-permute-start | bytes 294920 | tf_op jit(solution)/shard_map/ppermute | solution.py:35
  24.3 8.7 %collective-permute-start.8 = (bf16[384,128]{1,0:T(8,128)(2,1)S(1)}, bf16[384,128]{1,0:T(8,128)(2,1)S(1)}, u32[]{:S(2)}, u32[]{:S(2)}) collective-permute-start(bf16[384,128]{1,0:T(8,128)(2,1)S(1)} %get-tuple-element.55), channel_id=1, source_target_pairs={{0,16},{4,20},{8,24},{12,28},{16,0},{20,4},{24,8},{28,12},{1,17},{... | collective-permute-start | bytes 294920 | tf_op jit(solution)/shard_map/ppermute | solution.py:35
  26.6 5.2 %collective-permute-start.10 = (f32[16,256]{1,0:T(8,128)S(1)}, f32[16,256]{1,0:T(8,128)S(1)}, u32[]{:S(2)}, u32[]{:S(2)}) collective-permute-start(f32[16,256]{1,0:T(8,128)S(1)} %get-tuple-element.58.stats_ref), channel_id=1, source_target_pairs={{0,16},{4,20},{8,24},{12,28},{16,0},{20,4},{24,8},{28,12},{1,17},{... | collective-permute-start | bytes 49160 | tf_op jit(solution)/shard_map/ppermute | solution.py:35
  32.9 7.0 %collective-permute-start.15 = (bf16[320,384]{1,0:T(8,128)(2,1)S(1)}, bf16[320,384]{1,0:T(8,128)(2,1)S(1)}, u32[]{:S(2)}, u32[]{:S(2)}) collective-permute-start(bf16[320,384]{1,0:T(8,128)(2,1)S(1)} %get-tuple-element.70), channel_id=1, source_target_pairs={{0,4},{4,0},{8,12},{12,8},{16,20},{20,16},{24,28},{28,24},{1,5},{5... | collective-permute-start | bytes 737288 | tf_op jit(solution)/shard_map/ppermute | solution.py:35
  34.0 8.8 %collective-permute-start.16 = (bf16[320,384]{1,0:T(8,128)(2,1)S(1)}, bf16[320,384]{1,0:T(8,128)(2,1)S(1)}, u32[]{:S(2)}, u32[]{:S(2)}) collective-permute-start(bf16[320,384]{1,0:T(8,128)(2,1)S(1)} %get-tuple-element.71), channel_id=1, source_target_pairs={{0,8},{4,12},{8,0},{12,4},{16,24},{20,28},{24,16},{28,20},{1,9},{5... | collective-permute-start | bytes 737288 | tf_op jit(solution)/shard_map/ppermute | solution.py:35
  35.1 7.9 %collective-permute-start.13 = (bf16[128,384]{1,0:T(8,128)(2,1)S(1)}, bf16[128,384]{1,0:T(8,128)(2,1)S(1)}, u32[]{:S(2)}, u32[]{:S(2)}) collective-permute-start(bf16[128,384]{1,0:T(8,128)(2,1)S(1)} %get-tuple-element.67), channel_id=1, source_target_pairs={{0,16},{4,20},{8,24},{12,28},{16,0},{20,4},{24,8},{28,12},{1,17},{... | collective-permute-start | bytes 294920 | tf_op jit(solution)/shard_map/ppermute | solution.py:35
  37.7 7.6 %collective-permute-start.11 = (bf16[128,768]{1,0:T(8,128)(2,1)S(1)}, bf16[128,768]{1,0:T(8,128)(2,1)S(1)}, u32[]{:S(2)}, u32[]{:S(2)}) collective-permute-start(bf16[128,768]{1,0:T(8,128)(2,1)S(1)} %get-tuple-element.64), channel_id=1, source_target_pairs={{0,2},{1,3},{2,0},{3,1},{4,6},{5,7},{6,4},{7,5},{8,10},{9,11},{10,... | collective-permute-start | bytes 589832 | tf_op jit(solution)/shard_map/ppermute | solution.py:35
  38.7 7.4 %collective-permute-start.12 = (bf16[128,768]{1,0:T(8,128)(2,1)S(1)}, bf16[128,768]{1,0:T(8,128)(2,1)S(1)}, u32[]{:S(2)}, u32[]{:S(2)}) collective-permute-start(bf16[128,768]{1,0:T(8,128)(2,1)S(1)} %get-tuple-element.65), channel_id=1, source_target_pairs={{0,3},{1,2},{2,1},{3,0},{4,7},{5,6},{6,5},{7,4},{8,11},{9,10},{10,... | collective-permute-start | bytes 589832 | tf_op jit(solution)/shard_map/ppermute | solution.py:35
  39.9 6.2 %collective-permute-start.14 = (bf16[128,768]{1,0:T(8,128)(2,1)S(1)}, bf16[128,768]{1,0:T(8,128)(2,1)S(1)}, u32[]{:S(2)}, u32[]{:S(2)}) collective-permute-start(bf16[128,768]{1,0:T(8,128)(2,1)S(1)} %get-tuple-element.68), channel_id=1, source_target_pairs={{0,1},{1,0},{2,3},{3,2},{4,5},{5,4},{6,7},{7,6},{8,9},{9,8},{10,11... | collective-permute-start | bytes 589832 | tf_op jit(solution)/shard_map/ppermute | solution.py:35
  42.9 4.9 %collective-permute-start.17 = (bf16[160,384]{1,0:T(8,128)(2,1)S(1)}, bf16[160,384]{1,0:T(8,128)(2,1)S(1)}, u32[]{:S(2)}, u32[]{:S(2)}) collective-permute-start(bf16[160,384]{1,0:T(8,128)(2,1)S(1)} %get-tuple-element.74), channel_id=1, source_target_pairs={{0,8},{4,12},{8,0},{12,4},{16,24},{20,28},{24,16},{28,20},{1,9},{5... | collective-permute-start | bytes 368648 | tf_op jit(solution)/shard_map/ppermute | solution.py:35
  43.0 4.9 %collective-permute-start.18 = (bf16[160,384]{1,0:T(8,128)(2,1)S(1)}, bf16[160,384]{1,0:T(8,128)(2,1)S(1)}, u32[]{:S(2)}, u32[]{:S(2)}) collective-permute-start(bf16[160,384]{1,0:T(8,128)(2,1)S(1)} %get-tuple-element.75), channel_id=1, source_target_pairs={{0,4},{4,0},{8,12},{12,8},{16,20},{20,16},{24,28},{28,24},{1,5},{5... | collective-permute-start | bytes 368648 | tf_op jit(solution)/shard_map/ppermute | solution.py:35

commit v14 on v13

--- a/solution.py
+++ b/solution.py
@@ -39,7 +39,7 @@
     return pl.CostEstimate(flops=0, bytes_accessed=int(micros * HBM_BYTES), transcendentals=0)
 
 
-def local_call(body, name, micros, out_shapes, args, tables=0):
+def local_call(body, name, micros, out_shapes, args, tables=0, vmem=20):
     spaces = [pltpu.SMEM] * tables + [pltpu.VMEM] * (len(args) - tables)
     return pl.pallas_call(
         body,
@@ -47,7 +47,7 @@
         out_shape=out_shapes,
         in_specs=[pl.BlockSpec(memory_space=space) for space in spaces],
         out_specs=[pl.BlockSpec(memory_space=pltpu.VMEM)] * len(out_shapes),
-        compiler_params=pltpu.CompilerParams(vmem_limit_bytes=20 * 2**20),
+        compiler_params=pltpu.CompilerParams(vmem_limit_bytes=vmem * 2**20),
         cost_estimate=cost_of(micros),
     )(*args)
 
@@ -83,18 +83,19 @@
     )(*arrays)
 
 
-def pass_keys_kernel(kv2, key_ref):
-    key_ref[...] = kv2[: key_ref.shape[0]]
-
-
-def pass_values_kernel(kv2, value_ref):
-    value_ref[...] = kv2[value_ref.shape[0] :]
-
-
-def square_blocks(kv0, kv1, kv2, key3, value3):
-    keys = key3.shape[0]
-    pairs = [(ref.at[:keys], ref.at[keys:]) for ref in (kv0, kv1, kv2)]
-    return pairs + [(key3, value3)]
+def split_heads_kernel(kv_ref, *out_refs):
+    for head, ref in enumerate(out_refs):
+        ref[...] = head_slice(kv_ref[...], head)
+
+
+def square_keys(head, near, far):
+    keys = near[0].shape[0] // 2
+    return [head_slice(ref[:keys], head) for ref in near] + [far[head][:keys]]
+
+
+def square_values(head, near, far):
+    keys = near[0].shape[0] // 2
+    return [head_slice(ref[keys:], head) for ref in near] + [far[head][keys:]]
 
 
 def load_weight_kernel(w_ref, w_out, sems):
@@ -152,17 +153,17 @@
 
 
 def scores_kernel(
-    limits_ref, q_own_ref, q_pair_ref, kv0, kv1, kv2, key3, lse_ref, probs_ref
+    limits_ref, q_own_ref, q_pair_ref, kv0, kv1, kv2, *refs
 ):
     rows = q_own_ref.shape[0]
-    keys = key3.shape[0]
-    blocks = [ref.at[:keys] for ref in (kv0, kv1, kv2)] + [key3]
+    *far, lse_ref, probs_ref = refs
+    keys = kv0.shape[0] // 2
     lse_ref[...] = jnp.zeros_like(lse_ref)
     for head in range(q_own_ref.shape[1] // HDIM):
         query = both_rows(q_own_ref, q_pair_ref, head)
         scores = []
-        for step, key_ref in enumerate(blocks):
-            block = contract(head_slice(key_ref[...], head), query, 1, 1) * SCALE
+        for step, key in enumerate(square_keys(head, (kv0, kv1, kv2), far)):
+            block = contract(key, query, 1, 1) * SCALE
             slot = lax.broadcasted_iota(jnp.int32, block.shape, 0)
             valid = slot < rows + limits_ref[step : step + 1]
             scores.append(jnp.where(valid, block, NEG_FILL))
@@ -178,34 +179,32 @@
         lse_ref[head : head + 1] = top + jnp.log(total)
 
 
-def delta_kernel(
-    lse_ref, probs_ref, d_own_ref, d_pair_ref, kv0, kv1, kv2, key3, value3, stats_ref, dprobs_ref
-):
-    keys = key3.shape[0]
-    blocks = square_blocks(kv0, kv1, kv2, key3, value3)
+def delta_kernel(lse_ref, probs_ref, d_own_ref, d_pair_ref, kv0, kv1, kv2, *refs):
+    *far, stats_ref, dprobs_ref = refs
+    keys = kv0.shape[0] // 2
     stats_ref[...] = jnp.zeros_like(stats_ref)
     stats_ref[: lse_ref.shape[0]] = lse_ref[...]
     for head in range(d_own_ref.shape[1] // HDIM):
         dattn = both_rows(d_own_ref, d_pair_ref, head)
         delta = None
-        for step, (_, value_ref) in enumerate(blocks):
+        for step, value in enumerate(square_values(head, (kv0, kv1, kv2), far)):
             part = pl.ds((head * SQUARE + step) * keys, keys)
-            dprobs = contract(head_slice(value_ref[...], head), dattn, 1, 1)
+            dprobs = contract(value, dattn, 1, 1)
             dprobs_ref[part] = dprobs
             share = jnp.sum(probs_ref[part].astype(F32) * dprobs, axis=0, keepdims=True)
             delta = share if delta is None else delta + share
         stats_ref[8 + head : 9 + head] = delta
 
 
-def attn_kernel(kv0, kv1, kv2, key3, value3, probs_ref, own_ref, pair_ref):
+def attn_kernel(probs_ref, kv0, kv1, kv2, *refs):
+    *far, own_ref, pair_ref = refs
     rows = own_ref.shape[1]
-    keys = key3.shape[0]
-    blocks = square_blocks(kv0, kv1, kv2, key3, value3)
+    keys = kv0.shape[0] // 2
     for head in range(own_ref.shape[0] // HDIM):
         attn = None
-        for step, (_, value_ref) in enumerate(blocks):
+        for step, value in enumerate(square_values(head, (kv0, kv1, kv2), far)):
             begin = (head * SQUARE + step) * keys
-            part = contract(head_slice(value_ref[...], head), probs_ref[begin : begin + keys], 0, 0)
+            part = contract(value, probs_ref[begin : begin + keys], 0, 0)
             attn = part if attn is None else attn + part
         features = slice(head * HDIM, (head + 1) * HDIM)
         own_ref[features] = attn[:, :rows]
@@ -237,13 +236,12 @@
 
 
 def backward_kernel(
-    q_own_ref, q_pair_ref, d_own_ref, d_pair_ref, kv0, kv1, kv2, key3, value3,
-    stats_ref, stats_pair_ref, probs_ref, dprobs_ref,
-    dq_own_ref, dq_pair_ref, dkv_ref, send_k_ref, send_v_ref, near_k_ref, near_v_ref,
+    q_own_ref, q_pair_ref, d_own_ref, d_pair_ref, stats_ref, stats_pair_ref, probs_ref, dprobs_ref,
+    kv0, kv1, kv2, *refs,
 ):
     rows = q_own_ref.shape[0]
-    keys = key3.shape[0]
-    blocks = square_blocks(kv0, kv1, kv2, key3, value3)
+    *far, dq_own_ref, dq_pair_ref, dkv_ref, send_k_ref, send_v_ref, near_k_ref, near_v_ref = refs
+    keys = kv0.shape[0] // 2
     key_parts = (dkv_ref.at[:keys], send_k_ref.at[:keys], near_k_ref, send_k_ref.at[keys:])
     value_parts = (dkv_ref.at[keys:], near_v_ref, send_v_ref.at[:keys], send_v_ref.at[keys:])
 
@@ -260,7 +258,7 @@
         delta += weight_pair * swapped(stats_pair_ref[8 + head : 9 + head])
         features = slice(head * HDIM, (head + 1) * HDIM)
         dquery = None
-        for step, (key_ref, _) in enumerate(blocks):
+        for step, key in enumerate(square_keys(head, (kv0, kv1, kv2), far)):
             begin = (head * SQUARE + step) * keys
             probs = (probs_ref[begin : begin + keys].astype(F32) * weight).astype(BF16)
             dprobs = dprobs_ref[begin : begin + keys]
@@ -269,7 +267,7 @@
             grad_key = contract(dscores, query, 1, 0) * SCALE
             key_part[:, features] = grad_key.astype(key_part.dtype)
             value_part[:, features] = contract(probs, dattn, 1, 0).astype(value_part.dtype)
-            part = contract(dscores, head_slice(key_ref[...], head), 0, 0)
+            part = contract(dscores, key, 0, 0)
             dquery = part if dquery is None else dquery + part
         dq_own_ref[:, features] = dquery[:rows] * SCALE
         dq_pair_ref[:, features] = (dquery[rows:] * SCALE).astype(BF16)
@@ -325,9 +323,8 @@
         0.8,
         [shape((rows, width), BF16)],
         (grad_out, grad_core, grad_near, grad_far, weight),
+        vmem=40,
     )[0]
-    kv1, kv2, d_own = lax.optimization_barrier((kv1, kv2, d_own))
-    key3 = local_call(pass_keys_kernel, "pass_keys", 0.1, [shape((keys, width), BF16)], (kv2,))[0]
     limits = local_call(
         limits_kernel,
         "limits",
@@ -336,25 +333,25 @@
         (frame_levels, frame_counts),
         tables=2,
     )[0]
-    kv2_kept, q_pair, limits, _ = lax.optimization_barrier((kv2, q_pair, limits, key3))
-    value3 = local_call(
-        pass_values_kernel, "pass_values", 1.0, [shape((keys, width), BF16)], (kv2_kept,)
-    )[0]
-    kvs = [kv0, kv1, kv2, swap(key3, "ctx", 1), swap(value3, "ctx", 1)]
+    kv1, kv2, d_own, limits = lax.optimization_barrier((kv1, kv2, d_own, limits))
+    pieces = local_call(
+        split_heads_kernel, "split_heads", 0.1, [shape((2 * keys, HDIM), BF16)] * heads, (kv2,)
+    )
+    kvs = (kv0, kv1, kv2, *(swap(piece, "ctx", 1) for piece in pieces))
     d_pair = swap(d_own, "ctx", PAIR)
     lse, probs = local_call(
         scores_kernel,
         "scores",
         0.9,
         [shape((8, 2 * rows), F32), shape((heads * SQUARE * keys, 2 * rows), BF16)],
-        (limits, sec_q, q_pair, *kvs[:4]),
+        (limits, sec_q, q_pair, *kvs),
     )
     attn_own, attn_pair = local_call(
         attn_kernel,
         "attn",
         0.5,
         [shape((width, rows), F32), shape((width, rows), BF16)],
-        (*kvs, probs),
+        (probs, *kvs),
     )
     lse, attn_own = lax.optimization_barrier((lse, attn_own))
     stats, dprobs = local_call(
@@ -372,7 +369,7 @@
         [shape((rows, width), F32), shape((rows, width), BF16), shape((2 * keys, width), F32)]
         + [shape((2 * keys, width), BF16)] * 2
         + [shape((keys, width), F32)] * 2,
-        (sec_q, q_pair, d_own, d_pair, *kvs, stats, stats_pair, probs, dprobs),
+        (sec_q, q_pair, d_own, d_pair, stats, stats_pair, probs, dprobs, *kvs),
     )
     attn_got = swap(attn_pair, "ctx", PAIR)
     attn_got, send_k, send_v = lax.optimization_barrier((attn_got, send_k, send_v))

time: 49 us -> 50.3 us (1.027)
  starting transfers between devices: 19.8 us -> 22 us
  waiting for transfers between devices: 17.6 us -> 16.6 us
    ppermute x19 -> x20, starting transfers between devices: 19.8 us -> 22 us  [swap(): return lax.ppermute(block, axis, [(i, i ^ bit) for i in range(count)])]
    ppermute x19 -> x20, waiting for transfers between devices: 17.6 us -> 16.6 us  [swap(): return lax.ppermute(block, axis, [(i, i ^ bit) for i in range(count)])]
    pallas_call x11 -> x10, Pallas kernels: 7.15 us -> 7.18 us  [local_call(): pl.pallas_call(body, name=name, out_shape=out_shapes, in_specs=[pl.BlockS...]
  transfers between devices with their start and end apart: 19 -> 20, of which waited for: 11 -> 9; matrix products, arithmetic and copies ran while one was open for 0% -> 0% of each run, Pallas kernels for 20% -> 19%
where the time goes in v14:
time: 50.3 us; the launch traced here: 50.1 us
  starting transfers between devices  22 us (44%)
  waiting for transfers between devices  16.6 us (33%)
  Pallas kernels  10.5 us (21%)
  between operations  0.84 us (2%)
    ppermute x20, starting transfers between devices, swap(): return lax.ppermute(block, axis, [(i, i ^ bit) for i in range(count)])  22 us
    ppermute x20, waiting for transfers between devices, swap(): return lax.ppermute(block, axis, [(i, i ^ bit) for i in range(count)])  16.6 us
    pallas_call x10, Pallas kernels, local_call(): pl.pallas_call(body, name=name, out_shape=out_shapes, in_specs=[pl.BlockS...  7.18 us
    pallas_call x1, Pallas kernels, load_keys(): pl.pallas_call(load_kernel, name='load', out_shape=jax.ShapeDtypeStruct((...  1.66 us
    pallas_call x1, Pallas kernels, load_weight(): pl.pallas_call(load_weight_kernel, name='load_w', out_shape=jax.ShapeDtyp...  1.63 us
  transfers between devices with their start and end apart: 20, of which 9 were waited for; matrix products, arithmetic and copies ran while one was open for 0% of the time, Pallas kernels for 19%

profile of v14, /device:TPU:0, one launch (start us, length us, event | category | flops | bytes accessed | tf_op | source)
XLA Modules:
  0.0 50.1 jit_solution(10133410559283636009)
XLA Ops:
  0.6 3.0 %collective-permute-start.3 = (bf16[128,768]{1,0:T(8,128)(2,1)}, bf16[128,768]{1,0:T(8,128)(2,1)}, u32[]{:S(2)}, u32[]{:S(2)}) collective-permute-start(bf16[128,768]{1,0:T(8,128)(2,1)} %own_ref.1), channel_id=1, source_target_pairs={{0,2},{1,3},{2,0},{3,1},{4,6},{5,7},{6,4},{7,5},{8,10},{9,11},{10,... | collective-permute-start | bytes 589832 | tf_op jit(solution)/shard_map/ppermute | solution.py:35
  3.6 1.7 %load.1.kv0 = bf16[320,384]{1,0:T(8,128)(2,1)} custom-call(bf16[128,384]{1,0:T(8,128)(2,1)} %k_ref.1, bf16[32,384]{1,0:T(8,128)(2,1)} %hk_ref.1, bf16[128,384]{1,0:T(8,128)(2,1)} %v_ref.1, bf16[32,384]{1,0:T(8,128)(2,1)} %hv_ref.1), custom_call_target="tpu_custom_call" | custom-call | bytes 5904000 | tf_op jit(solution)/shard_map/load/pallas_call | solution.py:74
  5.3 0.0 copy-start.1
  5.3 0.0 copy-start.4
  5.3 0.0 copy-start.3
  5.3 0.0 copy-start.2
  5.4 1.6 %collective-permute-start.1 = (bf16[320,384]{1,0:T(8,128)(2,1)}, bf16[320,384]{1,0:T(8,128)(2,1)S(1)}, u32[]{:S(2)}, u32[]{:S(2)}) collective-permute-start(bf16[320,384]{1,0:T(8,128)(2,1)} %load.1.kv0), channel_id=1, source_target_pairs={{0,8},{4,12},{8,0},{12,4},{16,24},{20,28},{24,16},{28,20},{1,9},{5... | collective-permute-start | bytes 737288 | tf_op jit(solution)/shard_map/ppermute | solution.py:35
  7.0 1.5 %collective-permute-start = (bf16[320,384]{1,0:T(8,128)(2,1)}, bf16[320,384]{1,0:T(8,128)(2,1)S(1)}, u32[]{:S(2)}, u32[]{:S(2)}) collective-permute-start(bf16[320,384]{1,0:T(8,128)(2,1)} %load.1.kv0), channel_id=1, source_target_pairs={{0,4},{4,0},{8,12},{12,8},{16,20},{20,16},{24,28},{28,24},{1,5},{5... | collective-permute-start | bytes 737288 | tf_op jit(solution)/shard_map/ppermute | solution.py:35
  8.5 1.6 %load_w.1.w_ref = bf16[384,3072]{1,0:T(8,128)(2,1)S(1)} custom-call(bf16[384,3072]{1,0:T(8,128)(2,1)} %w_ref.1), custom_call_target="tpu_custom_call" | custom-call | bytes 5904000 | tf_op jit(solution)/shard_map/load_w/pallas_call | solution.py:113
  10.2 0.0 collective-permute-done.3.near_ref
  10.2 0.6 %collective-permute-start.4 = (bf16[128,768]{1,0:T(8,128)(2,1)}, bf16[128,768]{1,0:T(8,128)(2,1)}, u32[]{:S(2)}, u32[]{:S(2)}) collective-permute-start(bf16[128,768]{1,0:T(8,128)(2,1)} %collective-permute-done.3.near_ref), channel_id=1, source_target_pairs={{0,1},{1,0},{2,3},{3,2},{4,5},{5,4},{6,7},{7,6},{8,9},{9,8},{10,11... | collective-permute-start | bytes 589832 | tf_op jit(solution)/shard_map/ppermute | solution.py:35
  10.8 2.6 %collective-permute-start.5 = (bf16[128,384]{1,0:T(8,128)(2,1)S(1)}, bf16[128,384]{1,0:T(8,128)(2,1)S(1)}, u32[]{:S(2)}, u32[]{:S(2)}) collective-permute-start(bf16[128,384]{1,0:T(8,128)(2,1)S(1)} %copy-done.1), channel_id=1, source_target_pairs={{0,16},{4,20},{8,24},{12,28},{16,0},{20,4},{24,8},{28,12},{1,17},{... | collective-permute-start | bytes 294920 | tf_op jit(solution)/shard_map/ppermute | solution.py:35
  13.3 0.1 copy.15.levels_ref
  13.4 0.6 %limits.1.limits_ref = s32[8,256]{1,0:T(8,128)S(1)} custom-call(s32[8,2]{1,0:T(8,128)S(1)} %copy.15.levels_ref, s32[8]{0:T(128)S(1)} %copy-done.3), custom_call_target="tpu_custom_call" | custom-call | bytes 2214000 | tf_op jit(solution)/shard_map/limits/pallas_call | solution.py:44
  14.1 0.0 collective-permute-done.4.far_ref
  14.1 1.9 %dattn.1.d_own_ref = bf16[128,384]{1,0:T(8,128)(2,1)S(1)} custom-call(bf16[128,768]{1,0:T(8,128)(2,1)S(1)} %copy-done.2, bf16[128,768]{1,0:T(8,128)(2,1)} %collective-permute-done.2.core_ref, bf16[128,768]{1,0:T(8,128)(2,1)} %collective-permute-done.3.near_ref, bf16[128,768]{1,0:T(8,128)(2,1)} %collective-permute-done.4.far_ref, ...), custom_call_target="tpu_custom_call" | custom-call | bytes 2952000 | tf_op jit(solution)/shard_map/dattn/pallas_call | solution.py:44
  16.1 0.0 collective-permute-done.kv1
  16.1 0.6 %collective-permute-start.6 = (bf16[320,128]{1,0:T(8,128)(2,1)S(1)}, bf16[320,128]{1,0:T(8,128)(2,1)S(1)}, u32[]{:S(2)}, u32[]{:S(2)}) collective-permute-start(bf16[320,128]{1,0:T(8,128)(2,1)S(1)} %get-tuple-element.50), channel_id=1, source_target_pairs={{0,4},{4,0},{8,12},{12,8},{16,20},{20,16},{24,28},{28,24},{1,5},{5... | collective-permute-start | bytes 245768 | tf_op jit(solution)/shard_map/ppermute | solution.py:35
  16.7 1.5 %collective-permute-start.7 = (bf16[320,128]{1,0:T(8,128)(2,1)S(1)}, bf16[320,128]{1,0:T(8,128)(2,1)S(1)}, u32[]{:S(2)}, u32[]{:S(2)}) collective-permute-start(bf16[320,128]{1,0:T(8,128)(2,1)S(1)} %get-tuple-element.51), channel_id=1, source_target_pairs={{0,4},{4,0},{8,12},{12,8},{16,20},{20,16},{24,28},{28,24},{1,5},{5... | collective-permute-start | bytes 245768 | tf_op jit(solution)/shard_map/ppermute | solution.py:35
  18.2 0.5 %collective-permute-start.8 = (bf16[320,128]{1,0:T(8,128)(2,1)S(1)}, bf16[320,128]{1,0:T(8,128)(2,1)S(1)}, u32[]{:S(2)}, u32[]{:S(2)}) collective-permute-start(bf16[320,128]{1,0:T(8,128)(2,1)S(1)} %get-tuple-element.52), channel_id=1, source_target_pairs={{0,4},{4,0},{8,12},{12,8},{16,20},{20,16},{24,28},{28,24},{1,5},{5... | collective-permute-start | bytes 245768 | tf_op jit(solution)/shard_map/ppermute | solution.py:35
  18.7 1.9 %collective-permute-start.10 = (bf16[128,384]{1,0:T(8,128)(2,1)S(1)}, bf16[128,384]{1,0:T(8,128)(2,1)S(1)}, u32[]{:S(2)}, u32[]{:S(2)}) collective-permute-start(bf16[128,384]{1,0:T(8,128)(2,1)S(1)} %dattn.1.d_own_ref), channel_id=1, source_target_pairs={{0,16},{4,20},{8,24},{12,28},{16,0},{20,4},{24,8},{28,12},{1,17},{... | collective-permute-start | bytes 294920 | tf_op jit(solution)/shard_map/ppermute | solution.py:35
  20.6 0.0 collective-permute-done.5.q_pair_ref
  20.6 0.9 %collective-permute-done.6.refs_0_ = bf16[320,128]{1,0:T(8,128)(2,1)S(1)} collective-permute-done((bf16[320,128]{1,0:T(8,128)(2,1)S(1)}, bf16[320,128]{1,0:T(8,128)(2,1)S(1)}, u32[]{:S(2)}, u32[]{:S(2)}) %collective-permute-start.6) | collective-permute-done | bytes 81952 | tf_op jit(solution)/shard_map/ppermute | solution.py:35
  21.5 1.5 %collective-permute-done.7.refs_1_ = bf16[320,128]{1,0:T(8,128)(2,1)S(1)} collective-permute-done((bf16[320,128]{1,0:T(8,128)(2,1)S(1)}, bf16[320,128]{1,0:T(8,128)(2,1)S(1)}, u32[]{:S(2)}, u32[]{:S(2)}) %collective-permute-start.7) | collective-permute-done | bytes 81952 | tf_op jit(solution)/shard_map/ppermute | solution.py:35
  23.0 0.9 %collective-permute-done.8.refs_2_ = bf16[320,128]{1,0:T(8,128)(2,1)S(1)} collective-permute-done((bf16[320,128]{1,0:T(8,128)(2,1)S(1)}, bf16[320,128]{1,0:T(8,128)(2,1)S(1)}, u32[]{:S(2)}, u32[]{:S(2)}) %collective-permute-start.8) | collective-permute-done | bytes 81952 | tf_op jit(solution)/shard_map/ppermute | solution.py:35
  23.9 1.0 %scores.1 = (f32[8,256]{1,0:T(8,128)S(1)}, bf16[1920,256]{1,0:T(8,128)(2,1)S(1)}) custom-call(s32[8,256]{1,0:T(8,128)S(1)} %limits.1.limits_ref, bf16[128,384]{1,0:T(8,128)(2,1)S(1)} %copy-done.1, bf16[128,384]{1,0:T(8,128)(2,1)S(1)} %collective-permute-done.5.q_pair_ref, bf16[320,384]{1,0:T(8,128)(2,1)S(1)} %copy-done, ...), custom_call_target="tpu_custom_call" | custom-call | bytes 3321000 | tf_op jit(solution)/shard_map/scores/pallas_call | solution.py:44
  24.9 0.4 attn.1
  25.3 1.3 %collective-permute-start.9 = (bf16[384,128]{1,0:T(8,128)(2,1)S(1)}, bf16[384,128]{1,0:T(8,128)(2,1)S(1)}, u32[]{:S(2)}, u32[]{:S(2)}) collective-permute-start(bf16[384,128]{1,0:T(8,128)(2,1)S(1)} %get-tuple-element.57), channel_id=1, source_target_pairs={{0,16},{4,20},{8,24},{12,28},{16,0},{20,4},{24,8},{28,12},{1,17},{... | collective-permute-start | bytes 294920 | tf_op jit(solution)/shard_map/ppermute | solution.py:35
  26.6 0.0 collective-permute-done.10.d_pair_ref
  26.6 0.4 delta.1
  27.0 1.8 %collective-permute-start.11 = (f32[16,256]{1,0:T(8,128)S(1)}, f32[16,256]{1,0:T(8,128)S(1)}, u32[]{:S(2)}, u32[]{:S(2)}) collective-permute-start(f32[16,256]{1,0:T(8,128)S(1)} %get-tuple-element.60.stats_ref), channel_id=1, source_target_pairs={{0,16},{4,20},{8,24},{12,28},{16,0},{20,4},{24,8},{28,12},{1,17},{... | collective-permute-start | bytes 49160 | tf_op jit(solution)/shard_map/ppermute | solution.py:35
  28.8 3.9 %collective-permute-done.11.stats_pair_ref = f32[16,256]{1,0:T(8,128)S(1)} collective-permute-done((f32[16,256]{1,0:T(8,128)S(1)}, f32[16,256]{1,0:T(8,128)S(1)}, u32[]{:S(2)}, u32[]{:S(2)}) %collective-permute-start.11) | collective-permute-done | bytes 16416 | tf_op jit(solution)/shard_map/ppermute | solution.py:35
  32.7 1.1 %backward.1 = (f32[128,384]{1,0:T(8,128)S(1)}, bf16[128,384]{1,0:T(8,128)(2,1)S(1)}, f32[320,384]{1,0:T(8,128)S(1)}, bf16[320,384]{1,0:T(8,128)(2,1)S(1)}, bf16[...) custom-call(bf16[128,384]{1,0:T(8,128)(2,1)S(1)} %copy-done.1, ...), custom_call_target="tpu_custom_call" | custom-call | bytes 4059000 | tf_op jit(solution)/shard_map/backward/pallas_call | solution.py:44
  33.8 0.0 collective-permute-done.9.pair_ref
  33.8 1.2 %collective-permute-start.16 = (bf16[320,384]{1,0:T(8,128)(2,1)S(1)}, bf16[320,384]{1,0:T(8,128)(2,1)S(1)}, u32[]{:S(2)}, u32[]{:S(2)}) collective-permute-start(bf16[320,384]{1,0:T(8,128)(2,1)S(1)} %get-tuple-element.72), channel_id=1, source_target_pairs={{0,4},{4,0},{8,12},{12,8},{16,20},{20,16},{24,28},{28,24},{1,5},{5... | collective-permute-start | bytes 737288 | tf_op jit(solution)/shard_map/ppermute | solution.py:35
  35.1 1.5 %collective-permute-start.14 = (bf16[128,384]{1,0:T(8,128)(2,1)S(1)}, bf16[128,384]{1,0:T(8,128)(2,1)S(1)}, u32[]{:S(2)}, u32[]{:S(2)}) collective-permute-start(bf16[128,384]{1,0:T(8,128)(2,1)S(1)} %get-tuple-element.69), channel_id=1, source_target_pairs={{0,16},{4,20},{8,24},{12,28},{16,0},{20,4},{24,8},{28,12},{1,17},{... | collective-permute-start | bytes 294920 | tf_op jit(solution)/shard_map/ppermute | solution.py:35
  36.5 0.6 %project.1 = (f32[128,768]{1,0:T(8,128)S(1)}, bf16[128,768]{1,0:T(8,128)(2,1)S(1)}, bf16[128,768]{1,0:T(8,128)(2,1)S(1)}, bf16[128,768]{1,0:T(8,128)(2,1)S(1)}) custom-call(f32[384,128]{1,0:T(8,128)S(1)} %get-tuple-element.56.own_ref, bf16[384,128]{1,0:T(8,128)(2,1)S(1)} %collective-permute-done.9.pair_ref, f32[16,256]{1,0:T(8,128)S(1)} %get-tuple-element.60.stats_ref, ...), custom_call_target="tpu_custom_call" | custom-call | bytes 2214000 | tf_op jit(solution)/shard_map/project/pallas_call | solution.py:44
  37.2 1.6 %collective-permute-start.12 = (bf16[128,768]{1,0:T(8,128)(2,1)S(1)}, bf16[128,768]{1,0:T(8,128)(2,1)S(1)}, u32[]{:S(2)}, u32[]{:S(2)}) collective-permute-start(bf16[128,768]{1,0:T(8,128)(2,1)S(1)} %get-tuple-element.66), channel_id=1, source_target_pairs={{0,2},{1,3},{2,0},{3,1},{4,6},{5,7},{6,4},{7,5},{8,10},{9,11},{10,... | collective-permute-start | bytes 589832 | tf_op jit(solution)/shard_map/ppermute | solution.py:35
  38.8 0.0 collective-permute-start.13
  38.8 2.2 %collective-permute-done.16.got_k_ref = bf16[320,384]{1,0:T(8,128)(2,1)S(1)} collective-permute-done((bf16[320,384]{1,0:T(8,128)(2,1)S(1)}, bf16[320,384]{1,0:T(8,128)(2,1)S(1)}, u32[]{:S(2)}, u32[]{:S(2)}) %collective-permute-start.16) | collective-permute-done | bytes 245792 | tf_op jit(solution)/shard_map/ppermute | solution.py:35
  41.0 0.0 collective-permute-start.15
  41.0 3.1 %collective-permute-done.17.got_v_ref = bf16[320,384]{1,0:T(8,128)(2,1)S(1)} collective-permute-done((bf16[320,384]{1,0:T(8,128)(2,1)S(1)}, bf16[320,384]{1,0:T(8,128)(2,1)S(1)}, u32[]{:S(2)}, u32[]{:S(2)}) %collective-permute-start.17) | collective-permute-done | bytes 245792 | tf_op jit(solution)/shard_map/ppermute | solution.py:35
  44.1 0.1 collective-permute-start.18
  44.2 0.8 %collective-permute-start.19 = (bf16[160,384]{1,0:T(8,128)(2,1)S(1)}, bf16[160,384]{1,0:T(8,128)(2,1)S(1)}, u32[]{:S(2)}, u32[]{:S(2)}) collective-permute-start(bf16[160,384]{1,0:T(8,128)(2,1)S(1)} %get-tuple-element.77), channel_id=1, source_target_pairs={{0,4},{4,0},{8,12},{12,8},{16,20},{20,16},{24,28},{28,24},{1,5},{5... | collective-permute-start | bytes 368648 | tf_op jit(solution)/shard_map/ppermute | solution.py:35
  45.1 1.0 %collective-permute-done.13.far_ref = bf16[128,768]{1,0:T(8,128)(2,1)S(1)} collective-permute-done((bf16[128,768]{1,0:T(8,128)(2,1)S(1)}, bf16[128,768]{1,0:T(8,128)(2,1)S(1)}, u32[]{:S(2)}, u32[]{:S(2)}) %collective-permute-start.13) | collective-permute-done | bytes 196640 | tf_op jit(solution)/shard_map/ppermute | solution.py:35
  46.1 3.0 %collective-permute-done.18.rest_k_ref = bf16[160,384]{1,0:T(8,128)(2,1)S(1)} collective-permute-done((bf16[160,384]{1,0:T(8,128)(2,1)S(1)}, bf16[160,384]{1,0:T(8,128)(2,1)S(1)}, u32[]{:S(2)}, u32[]{:S(2)}) %collective-permute-start.18) | collective-permute-done | bytes 122912 | tf_op jit(solution)/shard_map/ppermute | solution.py:35
  49.1 0.1 collective-permute-done.19.rest_v_ref
  49.2 0.9 %finish.1 = (bf16[128,384]{1,0:T(8,128)(2,1)}, bf16[128,384]{1,0:T(8,128)(2,1)}, bf16[128,384]{1,0:T(8,128)(2,1)}, bf16[32,384]{1,0:T(8,128)(2,1)}, bf16[32,384]{1,0:T(8,128)(2,1)}, /*index=5*/bf16[128,768]{1,0:T(8,128)(2,1)}) custom-call(f32[128,768]{1,0:T(8,128)S(1)} %get-tuple-element.65.keep_ref, bf16[128,768]{1,0:T(8,128)(2,1)S(1)} %collective-permute-done.12.near_ref, ...), custom_call_target="tpu_custom_call" | custom-call | bytes 3321000 | tf_op jit(solution)/shard_map/finish/pallas_call | solution.py:44
  (15 shorter events, 0.1 us)
Async XLA Ops:
  0.6 9.5 %collective-permute-start.3 = (bf16[128,768]{1,0:T(8,128)(2,1)}, bf16[128,768]{1,0:T(8,128)(2,1)}, u32[]{:S(2)}, u32[]{:S(2)}) collective-permute-start(bf16[128,768]{1,0:T(8,128)(2,1)} %own_ref.1), channel_id=1, source_target_pairs={{0,2},{1,3},{2,0},{3,1},{4,6},{5,7},{6,4},{7,5},{8,10},{9,11},{10,... | collective-permute-start | bytes 589832 | tf_op jit(solution)/shard_map/ppermute | solution.py:35
  5.3 5.4 %copy-start.1 = (bf16[128,384]{1,0:T(8,128)(2,1)S(1)}, bf16[128,384]{1,0:T(8,128)(2,1)}, u32[]{:S(2)}) copy-start(bf16[128,384]{1,0:T(8,128)(2,1)} %q_own_ref.3) | copy-start | bytes 294916
  5.3 8.0 %copy-start.4 = (s32[8,2]{0,1:T(2,128)S(1)}, s32[8,2]{0,1:T(2,128)}, u32[]{:S(2)}) copy-start(s32[8,2]{0,1:T(2,128)} %param.14) | copy-start | bytes 196
  5.3 8.1 %copy-start.3 = (s32[8]{0:T(128)S(1)}, s32[8]{0:T(128)}, u32[]{:S(2)}) copy-start(s32[8]{0:T(128)} %counts_ref.1) | copy-start | bytes 100
  5.3 8.7 %copy-start.2 = (bf16[128,768]{1,0:T(8,128)(2,1)S(1)}, bf16[128,768]{1,0:T(8,128)(2,1)}, u32[]{:S(2)}) copy-start(bf16[128,768]{1,0:T(8,128)(2,1)} %own_ref.1) | copy-start | bytes 589828
  5.4 10.7 %collective-permute-start.1 = (bf16[320,384]{1,0:T(8,128)(2,1)}, bf16[320,384]{1,0:T(8,128)(2,1)S(1)}, u32[]{:S(2)}, u32[]{:S(2)}) collective-permute-start(bf16[320,384]{1,0:T(8,128)(2,1)} %load.1.kv0), channel_id=1, source_target_pairs={{0,8},{4,12},{8,0},{12,4},{16,24},{20,28},{24,16},{28,20},{1,9},{5... | collective-permute-start | bytes 737288 | tf_op jit(solution)/shard_map/ppermute | solution.py:35
  7.0 9.1 %collective-permute-start = (bf16[320,384]{1,0:T(8,128)(2,1)}, bf16[320,384]{1,0:T(8,128)(2,1)S(1)}, u32[]{:S(2)}, u32[]{:S(2)}) collective-permute-start(bf16[320,384]{1,0:T(8,128)(2,1)} %load.1.kv0), channel_id=1, source_target_pairs={{0,4},{4,0},{8,12},{12,8},{16,20},{20,16},{24,28},{28,24},{1,5},{5... | collective-permute-start | bytes 737288 | tf_op jit(solution)/shard_map/ppermute | solution.py:35
  8.5 5.6 %collective-permute-start.2 = (bf16[128,768]{1,0:T(8,128)(2,1)}, bf16[128,768]{1,0:T(8,128)(2,1)}, u32[]{:S(2)}, u32[]{:S(2)}) collective-permute-start(bf16[128,768]{1,0:T(8,128)(2,1)} %own_ref.1), channel_id=1, source_target_pairs={{0,1},{1,0},{2,3},{3,2},{4,5},{5,4},{6,7},{7,6},{8,9},{9,8},{10,11... | collective-permute-start | bytes 589832 | tf_op jit(solution)/shard_map/ppermute | solution.py:35
  10.2 13.7 %copy-start = (bf16[320,384]{1,0:T(8,128)(2,1)S(1)}, bf16[320,384]{1,0:T(8,128)(2,1)}, u32[]{:S(2)}) copy-start(bf16[320,384]{1,0:T(8,128)(2,1)} %load.1.kv0) | copy-start | bytes 737284
  10.2 3.9 %collective-permute-start.4 = (bf16[128,768]{1,0:T(8,128)(2,1)}, bf16[128,768]{1,0:T(8,128)(2,1)}, u32[]{:S(2)}, u32[]{:S(2)}) collective-permute-start(bf16[128,768]{1,0:T(8,128)(2,1)} %collective-permute-done.3.near_ref), channel_id=1, source_target_pairs={{0,1},{1,0},{2,3},{3,2},{4,5},{5,4},{6,7},{7,6},{8,9},{9,8},{10,11... | collective-permute-start | bytes 589832 | tf_op jit(solution)/shard_map/ppermute | solution.py:35
  10.8 9.8 %collective-permute-start.5 = (bf16[128,384]{1,0:T(8,128)(2,1)S(1)}, bf16[128,384]{1,0:T(8,128)(2,1)S(1)}, u32[]{:S(2)}, u32[]{:S(2)}) collective-permute-start(bf16[128,384]{1,0:T(8,128)(2,1)S(1)} %copy-done.1), channel_id=1, source_target_pairs={{0,16},{4,20},{8,24},{12,28},{16,0},{20,4},{24,8},{28,12},{1,17},{... | collective-permute-start | bytes 294920 | tf_op jit(solution)/shard_map/ppermute | solution.py:35
  16.1 5.4 %collective-permute-start.6 = (bf16[320,128]{1,0:T(8,128)(2,1)S(1)}, bf16[320,128]{1,0:T(8,128)(2,1)S(1)}, u32[]{:S(2)}, u32[]{:S(2)}) collective-permute-start(bf16[320,128]{1,0:T(8,128)(2,1)S(1)} %get-tuple-element.50), channel_id=1, source_target_pairs={{0,4},{4,0},{8,12},{12,8},{16,20},{20,16},{24,28},{28,24},{1,5},{5... | collective-permute-start | bytes 245768 | tf_op jit(solution)/shard_map/ppermute | solution.py:35
  16.7 6.3 %collective-permute-start.7 = (bf16[320,128]{1,0:T(8,128)(2,1)S(1)}, bf16[320,128]{1,0:T(8,128)(2,1)S(1)}, u32[]{:S(2)}, u32[]{:S(2)}) collective-permute-start(bf16[320,128]{1,0:T(8,128)(2,1)S(1)} %get-tuple-element.51), channel_id=1, source_target_pairs={{0,4},{4,0},{8,12},{12,8},{16,20},{20,16},{24,28},{28,24},{1,5},{5... | collective-permute-start | bytes 245768 | tf_op jit(solution)/shard_map/ppermute | solution.py:35
  18.2 5.6 %collective-permute-start.8 = (bf16[320,128]{1,0:T(8,128)(2,1)S(1)}, bf16[320,128]{1,0:T(8,128)(2,1)S(1)}, u32[]{:S(2)}, u32[]{:S(2)}) collective-permute-start(bf16[320,128]{1,0:T(8,128)(2,1)S(1)} %get-tuple-element.52), channel_id=1, source_target_pairs={{0,4},{4,0},{8,12},{12,8},{16,20},{20,16},{24,28},{28,24},{1,5},{5... | collective-permute-start | bytes 245768 | tf_op jit(solution)/shard_map/ppermute | solution.py:35
  18.7 7.9 %collective-permute-start.10 = (bf16[128,384]{1,0:T(8,128)(2,1)S(1)}, bf16[128,384]{1,0:T(8,128)(2,1)S(1)}, u32[]{:S(2)}, u32[]{:S(2)}) collective-permute-start(bf16[128,384]{1,0:T(8,128)(2,1)S(1)} %dattn.1.d_own_ref), channel_id=1, source_target_pairs={{0,16},{4,20},{8,24},{12,28},{16,0},{20,4},{24,8},{28,12},{1,17},{... | collective-permute-start | bytes 294920 | tf_op jit(solution)/shard_map/ppermute | solution.py:35
  25.3 8.5 %collective-permute-start.9 = (bf16[384,128]{1,0:T(8,128)(2,1)S(1)}, bf16[384,128]{1,0:T(8,128)(2,1)S(1)}, u32[]{:S(2)}, u32[]{:S(2)}) collective-permute-start(bf16[384,128]{1,0:T(8,128)(2,1)S(1)} %get-tuple-element.57), channel_id=1, source_target_pairs={{0,16},{4,20},{8,24},{12,28},{16,0},{20,4},{24,8},{28,12},{1,17},{... | collective-permute-start | bytes 294920 | tf_op jit(solution)/shard_map/ppermute | solution.py:35
  27.0 5.7 %collective-permute-start.11 = (f32[16,256]{1,0:T(8,128)S(1)}, f32[16,256]{1,0:T(8,128)S(1)}, u32[]{:S(2)}, u32[]{:S(2)}) collective-permute-start(f32[16,256]{1,0:T(8,128)S(1)} %get-tuple-element.60.stats_ref), channel_id=1, source_target_pairs={{0,16},{4,20},{8,24},{12,28},{16,0},{20,4},{24,8},{28,12},{1,17},{... | collective-permute-start | bytes 49160 | tf_op jit(solution)/shard_map/ppermute | solution.py:35
  33.8 7.2 %collective-permute-start.16 = (bf16[320,384]{1,0:T(8,128)(2,1)S(1)}, bf16[320,384]{1,0:T(8,128)(2,1)S(1)}, u32[]{:S(2)}, u32[]{:S(2)}) collective-permute-start(bf16[320,384]{1,0:T(8,128)(2,1)S(1)} %get-tuple-element.72), channel_id=1, source_target_pairs={{0,4},{4,0},{8,12},{12,8},{16,20},{20,16},{24,28},{28,24},{1,5},{5... | collective-permute-start | bytes 737288 | tf_op jit(solution)/shard_map/ppermute | solution.py:35
  35.1 9.0 %collective-permute-start.17 = (bf16[320,384]{1,0:T(8,128)(2,1)S(1)}, bf16[320,384]{1,0:T(8,128)(2,1)S(1)}, u32[]{:S(2)}, u32[]{:S(2)}) collective-permute-start(bf16[320,384]{1,0:T(8,128)(2,1)S(1)} %get-tuple-element.73), channel_id=1, source_target_pairs={{0,8},{4,12},{8,0},{12,4},{16,24},{20,28},{24,16},{28,20},{1,9},{5... | collective-permute-start | bytes 737288 | tf_op jit(solution)/shard_map/ppermute | solution.py:35
  35.1 9.1 %collective-permute-start.14 = (bf16[128,384]{1,0:T(8,128)(2,1)S(1)}, bf16[128,384]{1,0:T(8,128)(2,1)S(1)}, u32[]{:S(2)}, u32[]{:S(2)}) collective-permute-start(bf16[128,384]{1,0:T(8,128)(2,1)S(1)} %get-tuple-element.69), channel_id=1, source_target_pairs={{0,16},{4,20},{8,24},{12,28},{16,0},{20,4},{24,8},{28,12},{1,17},{... | collective-permute-start | bytes 294920 | tf_op jit(solution)/shard_map/ppermute | solution.py:35
  37.2 7.9 %collective-permute-start.12 = (bf16[128,768]{1,0:T(8,128)(2,1)S(1)}, bf16[128,768]{1,0:T(8,128)(2,1)S(1)}, u32[]{:S(2)}, u32[]{:S(2)}) collective-permute-start(bf16[128,768]{1,0:T(8,128)(2,1)S(1)} %get-tuple-element.66), channel_id=1, source_target_pairs={{0,2},{1,3},{2,0},{3,1},{4,6},{5,7},{6,4},{7,5},{8,10},{9,11},{10,... | collective-permute-start | bytes 589832 | tf_op jit(solution)/shard_map/ppermute | solution.py:35
  38.8 7.3 %collective-permute-start.13 = (bf16[128,768]{1,0:T(8,128)(2,1)S(1)}, bf16[128,768]{1,0:T(8,128)(2,1)S(1)}, u32[]{:S(2)}, u32[]{:S(2)}) collective-permute-start(bf16[128,768]{1,0:T(8,128)(2,1)S(1)} %get-tuple-element.67), channel_id=1, source_target_pairs={{0,3},{1,2},{2,1},{3,0},{4,7},{5,6},{6,5},{7,4},{8,11},{9,10},{10,... | collective-permute-start | bytes 589832 | tf_op jit(solution)/shard_map/ppermute | solution.py:35
  41.0 5.1 %collective-permute-start.15 = (bf16[128,768]{1,0:T(8,128)(2,1)S(1)}, bf16[128,768]{1,0:T(8,128)(2,1)S(1)}, u32[]{:S(2)}, u32[]{:S(2)}) collective-permute-start(bf16[128,768]{1,0:T(8,128)(2,1)S(1)} %get-tuple-element.70), channel_id=1, source_target_pairs={{0,1},{1,0},{2,3},{3,2},{4,5},{5,4},{6,7},{7,6},{8,9},{9,8},{10,11... | collective-permute-start | bytes 589832 | tf_op jit(solution)/shard_map/ppermute | solution.py:35
  44.1 4.9 %collective-permute-start.18 = (bf16[160,384]{1,0:T(8,128)(2,1)S(1)}, bf16[160,384]{1,0:T(8,128)(2,1)S(1)}, u32[]{:S(2)}, u32[]{:S(2)}) collective-permute-start(bf16[160,384]{1,0:T(8,128)(2,1)S(1)} %get-tuple-element.76), channel_id=1, source_target_pairs={{0,8},{4,12},{8,0},{12,4},{16,24},{20,28},{24,16},{28,20},{1,9},{5... | collective-permute-start | bytes 368648 | tf_op jit(solution)/shard_map/ppermute | solution.py:35
  44.2 4.9 %collective-permute-start.19 = (bf16[160,384]{1,0:T(8,128)(2,1)S(1)}, bf16[160,384]{1,0:T(8,128)(2,1)S(1)}, u32[]{:S(2)}, u32[]{:S(2)}) collective-permute-start(bf16[160,384]{1,0:T(8,128)(2,1)S(1)} %get-tuple-element.77), channel_id=1, source_target_pairs={{0,4},{4,0},{8,12},{12,8},{16,20},{20,16},{24,28},{28,24},{1,5},{5... | collective-permute-start | bytes 368648 | tf_op jit(solution)/shard_map/ppermute | solution.py:35

commit v15 on v14

--- a/solution.py
+++ b/solution.py
@@ -218,7 +218,10 @@
     return weight * inverse, weight_pair * inverse
 
 
-def project_kernel(own_ref, pair_ref, stats_ref, stats_pair_ref, w_ref, keep_ref, *send_refs):
+def project_kernel(
+    own_ref, pair_ref, stats_ref, stats_pair_ref, w_ref,
+    keep_ref, next_ref, core_ref, far_left_ref, far_right_ref,
+):
     rows = own_ref.shape[1]
     parts = []
     for head in range(own_ref.shape[0] // HDIM):
@@ -230,9 +233,24 @@
     attn = jnp.concatenate(parts, axis=0).astype(BF16)
     me = lax.axis_index("head")
     size = keep_ref.shape[1]
-    for step, ref in enumerate((keep_ref, *send_refs)):
+    half = size // 2
+
+    def columns_of(step):
         columns = pl.ds(pl.multiple_of((me ^ step) * size, HDIM), size)
-        ref[...] = contract(attn, w_ref[:, columns], 0, 0).astype(ref.dtype)
+        return contract(attn, w_ref[:, columns], 0, 0)
+
+    far = columns_of(3).astype(BF16)
+    far_left_ref[...] = far[:, :half]
+    far_right_ref[...] = far[:, half:]
+    next_ref[...] = columns_of(2)
+    core_ref[...] = columns_of(1).astype(BF16)
+    keep_ref[...] = columns_of(0)
+
+
+def add_near_kernel(next_ref, left_ref, right_ref, out_ref):
+    half = left_ref.shape[1]
+    out_ref[:, :half] = (next_ref[:, :half] + left_ref[...].astype(F32)).astype(BF16)
+    out_ref[:, half:] = (next_ref[:, half:] + right_ref[...].astype(F32)).astype(BF16)
 
 
 def backward_kernel(
@@ -242,6 +260,7 @@
     rows = q_own_ref.shape[0]
     *far, dq_own_ref, dq_pair_ref, dkv_ref, send_k_ref, send_v_ref, near_k_ref, near_v_ref = refs
     keys = kv0.shape[0] // 2
+    dq_pair_ref[rows:] = jnp.zeros((dq_pair_ref.shape[0] - rows, dq_pair_ref.shape[1]), BF16)
     key_parts = (dkv_ref.at[:keys], send_k_ref.at[:keys], near_k_ref, send_k_ref.at[keys:])
     value_parts = (dkv_ref.at[keys:], near_v_ref, send_v_ref.at[:keys], send_v_ref.at[keys:])
 
@@ -270,7 +289,7 @@
             part = contract(dscores, key, 0, 0)
             dquery = part if dquery is None else dquery + part
         dq_own_ref[:, features] = dquery[:rows] * SCALE
-        dq_pair_ref[:, features] = (dquery[rows:] * SCALE).astype(BF16)
+        dq_pair_ref[:rows, features] = (dquery[rows:] * SCALE).astype(BF16)
 
 
 def pass_on_kernel(near_k_ref, near_v_ref, got_k_ref, got_v_ref, k_ref, v_ref):
@@ -280,7 +299,7 @@
 
 
 def finish_kernel(
-    keep_ref, near_ref, far_ref, dq_ref, dq_pair_ref, core_ref,
+    keep_ref, core_ref, near_ref, dq_ref, dq_pair_ref,
     dkv_ref, got_k_ref, got_v_ref, rest_k_ref, rest_v_ref,
     q_out, k_out, v_out, hk_out, hv_out, out_ref,
 ):
@@ -292,12 +311,12 @@
             first = first + other.astype(F32)
         return first.astype(BF16)
 
-    q_out[...] = total(dq_ref[...], dq_pair_ref[...])
+    q_out[...] = total(dq_ref[...], dq_pair_ref[:rows])
     k_out[...] = total(dkv_ref[:rows], got_k_ref[:rows], rest_k_ref[:rows])
     hk_out[...] = total(dkv_ref[rows:keys], got_k_ref[rows:keys], rest_k_ref[rows:])
     v_out[...] = total(dkv_ref[keys : keys + rows], got_v_ref[:rows], rest_v_ref[:rows])
     hv_out[...] = total(dkv_ref[keys + rows :], got_v_ref[rows:keys], rest_v_ref[rows:])
-    out_ref[...] = total(keep_ref[...], core_ref[...], near_ref[...], far_ref[...])
+    out_ref[...] = total(keep_ref[...], core_ref[...], near_ref[...])
 
 
 def blocked(sec_q, sec_k, sec_v, hist_k, hist_v, frame_levels, frame_counts, w_out, grad_out):
@@ -317,6 +336,11 @@
     kv0 = load_keys(sec_k, hist_k, sec_v, hist_v)
     kv2 = swap(kv0, "ctx", 2)
     kv1 = swap(kv0, "ctx", 1)
+    kv1, kv2 = lax.optimization_barrier((kv1, kv2))
+    pieces = local_call(
+        split_heads_kernel, "split_heads", 0.1, [shape((2 * keys, HDIM), BF16)] * heads, (kv2,)
+    )
+    kvs = (kv0, kv1, kv2, *(swap(piece, "ctx", 1) for piece in pieces))
     d_own = local_call(
         dattn_kernel,
         "dattn",
@@ -325,6 +349,7 @@
         (grad_out, grad_core, grad_near, grad_far, weight),
         vmem=40,
     )[0]
+    d_pair = swap(d_own, "ctx", PAIR)
     limits = local_call(
         limits_kernel,
         "limits",
@@ -333,12 +358,6 @@
         (frame_levels, frame_counts),
         tables=2,
     )[0]
-    kv1, kv2, d_own, limits = lax.optimization_barrier((kv1, kv2, d_own, limits))
-    pieces = local_call(
-        split_heads_kernel, "split_heads", 0.1, [shape((2 * keys, HDIM), BF16)] * heads, (kv2,)
-    )
-    kvs = (kv0, kv1, kv2, *(swap(piece, "ctx", 1) for piece in pieces))
-    d_pair = swap(d_own, "ctx", PAIR)
     lse, probs = local_call(
         scores_kernel,
         "scores",
@@ -366,7 +385,7 @@
         backward_kernel,
         "backward",
         1.1,
-        [shape((rows, width), F32), shape((rows, width), BF16), shape((2 * keys, width), F32)]
+        [shape((rows, width), F32), shape((keys + 16, width), BF16), shape((2 * keys, width), F32)]
         + [shape((2 * keys, width), BF16)] * 2
         + [shape((keys, width), F32)] * 2,
         (sec_q, q_pair, d_own, d_pair, stats, stats_pair, probs, dprobs, *kvs),
@@ -384,16 +403,30 @@
     )
     rest_k = swap(rest_k, "ctx", 2)
     rest_v = swap(rest_v, "ctx", 1)
-    out_keep, *out_send = local_call(
+    half = share // 2
+    out_keep, out_next, out_core, far_left, far_right = local_call(
         project_kernel,
         "project",
         0.6,
-        [shape((rows, share), F32)] + [shape((rows, share), BF16)] * 3,
+        [shape((rows, share), F32)] * 2
+        + [shape((rows, share), BF16)]
+        + [shape((rows, half), BF16)] * 2,
         (attn_own, attn_got, stats, stats_pair, weight),
     )
-    out_near, out_far = (swap(out_send[step - 1], "head", step) for step in (2, 3))
+    far_left, far_right = (swap(part, "head", 1) for part in (far_left, far_right))
+    out_near = swap(
+        local_call(
+            add_near_kernel,
+            "add_near",
+            0.1,
+            [shape((rows, share), BF16)],
+            (out_next, far_left, far_right),
+        )[0],
+        "head",
+        2,
+    )
     dq_got = swap(dq_pair, "ctx", PAIR)
-    out_core = swap(out_send[0], "head", 1)
+    out_core = swap(out_core, "head", 1)
     grad_q, grad_k, grad_v, grad_hk, grad_hv, out = local_call(
         finish_kernel,
         "finish",
@@ -402,7 +435,7 @@
         + [shape((capacity, width), BF16)] * 2
         + [shape((rows, share), BF16)],
         (
-            out_keep, out_near, out_far, dq_own, dq_got, out_core,
+            out_keep, out_core, out_near, dq_own, dq_got,
             dkv_own, got_k, got_v, rest_k, rest_v,
         ),
     )

time: 50.3 us -> 49.7 us (0.988)
  waiting for transfers between devices: 16.6 us -> 12 us
  starting transfers between devices: 22 us -> 24.6 us
  Pallas kernels: 10.5 us -> 11.9 us
    ppermute x20 -> x21, waiting for transfers between devices: 16.6 us -> 12 us  [swap(): return lax.ppermute(block, axis, [(i, i ^ bit) for i in range(count)])]
    ppermute x20 -> x21, starting transfers between devices: 22 us -> 24.6 us  [swap(): return lax.ppermute(block, axis, [(i, i ^ bit) for i in range(count)])]
    pallas_call x10 -> x11, Pallas kernels: 7.18 us -> 8.63 us  [local_call(): pl.pallas_call(body, name=name, out_shape=out_shapes, in_specs=[pl.BlockS...]
  transfers between devices with their start and end apart: 20 -> 21, of which waited for: 9 -> 8; matrix products, arithmetic and copies ran while one was open for 0% -> 0% of each run, Pallas kernels for 19% -> 22%
where the time goes in v15:
time: 49.7 us; the launch traced here: 49.4 us
  starting transfers between devices  24.6 us (49%)
  waiting for transfers between devices  12 us (24%)
  Pallas kernels  11.9 us (24%)
  between operations  0.82 us (2%)
    ppermute x21, starting transfers between devices, swap(): return lax.ppermute(block, axis, [(i, i ^ bit) for i in range(count)])  24.6 us
    ppermute x21, waiting for transfers between devices, swap(): return lax.ppermute(block, axis, [(i, i ^ bit) for i in range(count)])  12 us
    pallas_call x11, Pallas kernels, local_call(): pl.pallas_call(body, name=name, out_shape=out_shapes, in_specs=[pl.BlockS...  8.63 us
    pallas_call x1, Pallas kernels, load_keys(): pl.pallas_call(load_kernel, name='load', out_shape=jax.ShapeDtypeStruct((...  1.66 us
    pallas_call x1, Pallas kernels, load_weight(): pl.pallas_call(load_weight_kernel, name='load_w', out_shape=jax.ShapeDtyp...  1.63 us
  transfers between devices with their start and end apart: 21, of which 8 were waited for; matrix products, arithmetic and copies ran while one was open for 0% of the time, Pallas kernels for 22%

profile of v15, /device:TPU:0, one launch (start us, length us, event | category | flops | bytes accessed | tf_op | source)
XLA Modules:
  0.0 49.4 jit_solution(3602584950958021741)
XLA Ops:
  0.6 3.0 %collective-permute-start.8 = (bf16[128,768]{1,0:T(8,128)(2,1)}, bf16[128,768]{1,0:T(8,128)(2,1)S(1)}, u32[]{:S(2)}, u32[]{:S(2)}) collective-permute-start(bf16[128,768]{1,0:T(8,128)(2,1)} %own_ref.1), channel_id=1, source_target_pairs={{0,2},{1,3},{2,0},{3,1},{4,6},{5,7},{6,4},{7,5},{8,10},{9,11},{10,... | collective-permute-start | bytes 589832 | tf_op jit(solution)/shard_map/ppermute | solution.py:35
  3.6 1.7 %load.1.kv0 = bf16[320,384]{1,0:T(8,128)(2,1)} custom-call(bf16[128,384]{1,0:T(8,128)(2,1)} %k_ref.1, bf16[32,384]{1,0:T(8,128)(2,1)} %hk_ref.1, bf16[128,384]{1,0:T(8,128)(2,1)} %v_ref.1, bf16[32,384]{1,0:T(8,128)(2,1)} %hv_ref.1), custom_call_target="tpu_custom_call" | custom-call | bytes 5904000 | tf_op jit(solution)/shard_map/load/pallas_call | solution.py:74
  5.3 0.0 copy-start.1
  5.3 1.6 %collective-permute-start.2 = (bf16[320,384]{1,0:T(8,128)(2,1)}, bf16[320,384]{1,0:T(8,128)(2,1)S(1)}, u32[]{:S(2)}, u32[]{:S(2)}) collective-permute-start(bf16[320,384]{1,0:T(8,128)(2,1)} %load.1.kv0), channel_id=1, source_target_pairs={{0,8},{4,12},{8,0},{12,4},{16,24},{20,28},{24,16},{28,20},{1,9},{5... | collective-permute-start | bytes 737288 | tf_op jit(solution)/shard_map/ppermute | solution.py:35
  7.0 1.5 %collective-permute-start.1 = (bf16[320,384]{1,0:T(8,128)(2,1)}, bf16[320,384]{1,0:T(8,128)(2,1)S(1)}, u32[]{:S(2)}, u32[]{:S(2)}) collective-permute-start(bf16[320,384]{1,0:T(8,128)(2,1)} %load.1.kv0), channel_id=1, source_target_pairs={{0,4},{4,0},{8,12},{12,8},{16,20},{20,16},{24,28},{28,24},{1,5},{5... | collective-permute-start | bytes 737288 | tf_op jit(solution)/shard_map/ppermute | solution.py:35
  8.5 0.0 collective-permute-start.7
  8.5 1.6 %load_w.1.w_ref = bf16[384,3072]{1,0:T(8,128)(2,1)S(1)} custom-call(bf16[384,3072]{1,0:T(8,128)(2,1)} %w_ref.1), custom_call_target="tpu_custom_call" | custom-call | bytes 5904000 | tf_op jit(solution)/shard_map/load_w/pallas_call | solution.py:113
  10.1 0.0 copy-start.3
  10.1 0.0 copy-start.2
  10.2 0.0 collective-permute-done.8.near_ref
  10.2 0.6 %collective-permute-start.9 = (bf16[128,768]{1,0:T(8,128)(2,1)S(1)}, bf16[128,768]{1,0:T(8,128)(2,1)S(1)}, u32[]{:S(2)}, u32[]{:S(2)}) collective-permute-start(bf16[128,768]{1,0:T(8,128)(2,1)S(1)} %collective-permute-done.8.near_ref), channel_id=1, source_target_pairs={{0,1},{1,0},{2,3},{3,2},{4,5},{5,4},{6,7},{7,6},{8,9},{9,8},{10,11... | collective-permute-start | bytes 589832 | tf_op jit(solution)/shard_map/ppermute | solution.py:35
  10.7 2.6 %collective-permute-start = (bf16[128,384]{1,0:T(8,128)(2,1)}, bf16[128,384]{1,0:T(8,128)(2,1)}, u32[]{:S(2)}, u32[]{:S(2)}) collective-permute-start(bf16[128,384]{1,0:T(8,128)(2,1)} %q_own_ref.3), channel_id=1, source_target_pairs={{0,16},{4,20},{8,24},{12,28},{16,0},{20,4},{24,8},{28,12},{1,17},{... | collective-permute-start | bytes 294920 | tf_op jit(solution)/shard_map/ppermute | solution.py:35
  13.3 0.0 collective-permute-done.2.kv_ref.kv2
  13.3 1.0 %collective-permute-done.1.kv1 = bf16[320,384]{1,0:T(8,128)(2,1)S(1)} collective-permute-done((bf16[320,384]{1,0:T(8,128)(2,1)}, bf16[320,384]{1,0:T(8,128)(2,1)S(1)}, u32[]{:S(2)}, u32[]{:S(2)}) %collective-permute-start.1) | collective-permute-done | bytes 245792 | tf_op jit(solution)/shard_map/ppermute | solution.py:35
  14.3 0.7 %split_heads.1 = (bf16[320,128]{1,0:T(8,128)(2,1)}, bf16[320,128]{1,0:T(8,128)(2,1)}, bf16[320,128]{1,0:T(8,128)(2,1)}) custom-call(bf16[320,384]{1,0:T(8,128)(2,1)S(1)} %collective-permute-done.2.kv_ref.kv2), custom_call_target="tpu_custom_call" | custom-call | bytes 369000 | tf_op jit(solution)/shard_map/split_heads/pallas_call | solution.py:44
  15.0 1.5 %collective-permute-start.3 = (bf16[320,128]{1,0:T(8,128)(2,1)}, bf16[320,128]{1,0:T(8,128)(2,1)S(1)}, u32[]{:S(2)}, u32[]{:S(2)}) collective-permute-start(bf16[320,128]{1,0:T(8,128)(2,1)} %get-tuple-element.46), channel_id=1, source_target_pairs={{0,4},{4,0},{8,12},{12,8},{16,20},{20,16},{24,28},{28,24},{1,5},{5... | collective-permute-start | bytes 245768 | tf_op jit(solution)/shard_map/ppermute | solution.py:35
  16.6 0.5 %collective-permute-start.4 = (bf16[320,128]{1,0:T(8,128)(2,1)}, bf16[320,128]{1,0:T(8,128)(2,1)S(1)}, u32[]{:S(2)}, u32[]{:S(2)}) collective-permute-start(bf16[320,128]{1,0:T(8,128)(2,1)} %get-tuple-element.47), channel_id=1, source_target_pairs={{0,4},{4,0},{8,12},{12,8},{16,20},{20,16},{24,28},{28,24},{1,5},{5... | collective-permute-start | bytes 245768 | tf_op jit(solution)/shard_map/ppermute | solution.py:35
  17.1 0.0 collective-permute-done.7.core_ref
  17.1 1.5 %collective-permute-start.5 = (bf16[320,128]{1,0:T(8,128)(2,1)}, bf16[320,128]{1,0:T(8,128)(2,1)S(1)}, u32[]{:S(2)}, u32[]{:S(2)}) collective-permute-start(bf16[320,128]{1,0:T(8,128)(2,1)} %get-tuple-element.48), channel_id=1, source_target_pairs={{0,4},{4,0},{8,12},{12,8},{16,20},{20,16},{24,28},{28,24},{1,5},{5... | collective-permute-start | bytes 245768 | tf_op jit(solution)/shard_map/ppermute | solution.py:35
  18.6 0.8 %dattn.1.d_own_ref = bf16[128,384]{1,0:T(8,128)(2,1)S(1)} custom-call(bf16[128,768]{1,0:T(8,128)(2,1)S(1)} %copy-done.1, bf16[128,768]{1,0:T(8,128)(2,1)S(1)} %collective-permute-done.7.core_ref, bf16[128,768]{1,0:T(8,128)(2,1)S(1)} %collective-permute-done.8.near_ref, bf16[128,768]{1,0:T(8,128)(2,1)S(1)} %collective-permute-done.9.far_ref, ...), custom_call_target="tpu_custom_call" | custom-call | bytes 2952000 | tf_op jit(solution)/shard_map/dattn/pallas_call | solution.py:44
  19.4 2.7 %collective-permute-start.10 = (bf16[128,384]{1,0:T(8,128)(2,1)S(1)}, bf16[128,384]{1,0:T(8,128)(2,1)S(1)}, u32[]{:S(2)}, u32[]{:S(2)}) collective-permute-start(bf16[128,384]{1,0:T(8,128)(2,1)S(1)} %dattn.1.d_own_ref), channel_id=1, source_target_pairs={{0,16},{4,20},{8,24},{12,28},{16,0},{20,4},{24,8},{28,12},{1,17},{... | collective-permute-start | bytes 294920 | tf_op jit(solution)/shard_map/ppermute | solution.py:35
  22.1 0.1 copy.15.levels_ref
  22.2 0.6 %limits.1.limits_ref = s32[8,256]{1,0:T(8,128)S(1)} custom-call(s32[8,2]{1,0:T(8,128)S(1)} %copy.15.levels_ref, s32[8]{0:T(128)S(1)} %copy-done.2), custom_call_target="tpu_custom_call" | custom-call | bytes 2214000 | tf_op jit(solution)/shard_map/limits/pallas_call | solution.py:44
  22.9 1.9 %scores.1 = (f32[8,256]{1,0:T(8,128)S(1)}, bf16[1920,256]{1,0:T(8,128)(2,1)S(1)}) custom-call(s32[8,256]{1,0:T(8,128)S(1)} %limits.1.limits_ref, bf16[128,384]{1,0:T(8,128)(2,1)} %q_own_ref.3, bf16[128,384]{1,0:T(8,128)(2,1)} %collective-permute-done.q_pair_ref, bf16[320,384]{1,0:T(8,128)(2,1)S(1)} %copy-done, ...), custom_call_target="tpu_custom_call" | custom-call | bytes 3321000 | tf_op jit(solution)/shard_map/scores/pallas_call | solution.py:44
  24.8 0.4 attn.1
  25.2 1.9 %collective-permute-start.6 = (bf16[384,128]{1,0:T(8,128)(2,1)S(1)}, bf16[384,128]{1,0:T(8,128)(2,1)S(1)}, u32[]{:S(2)}, u32[]{:S(2)}) collective-permute-start(bf16[384,128]{1,0:T(8,128)(2,1)S(1)} %get-tuple-element.53), channel_id=1, source_target_pairs={{0,16},{4,20},{8,24},{12,28},{16,0},{20,4},{24,8},{28,12},{1,17},{... | collective-permute-start | bytes 294920 | tf_op jit(solution)/shard_map/ppermute | solution.py:35
  27.1 0.4 delta.1
  27.5 1.2 %collective-permute-start.11 = (f32[16,256]{1,0:T(8,128)S(1)}, f32[16,256]{1,0:T(8,128)S(1)}, u32[]{:S(2)}, u32[]{:S(2)}) collective-permute-start(f32[16,256]{1,0:T(8,128)S(1)} %get-tuple-element.57.stats_ref), channel_id=1, source_target_pairs={{0,16},{4,20},{8,24},{12,28},{16,0},{20,4},{24,8},{28,12},{1,17},{... | collective-permute-start | bytes 49160 | tf_op jit(solution)/shard_map/ppermute | solution.py:35
  28.7 3.6 %collective-permute-done.11.stats_pair_ref = f32[16,256]{1,0:T(8,128)S(1)} collective-permute-done((f32[16,256]{1,0:T(8,128)S(1)}, f32[16,256]{1,0:T(8,128)S(1)}, u32[]{:S(2)}, u32[]{:S(2)}) %collective-permute-start.11) | collective-permute-done | bytes 16416 | tf_op jit(solution)/shard_map/ppermute | solution.py:35
  32.3 2.1 %backward.1 = (f32[128,384]{1,0:T(8,128)S(1)}, bf16[176,384]{1,0:T(8,128)(2,1)S(1)}, f32[320,384]{1,0:T(8,128)S(1)}, bf16[320,384]{1,0:T(8,128)(2,1)S(1)}, bf16[...) custom-call(bf16[128,384]{1,0:T(8,128)(2,1)} %q_own_ref.3, ...), custom_call_target="tpu_custom_call" | custom-call | bytes 4059000 | tf_op jit(solution)/shard_map/backward/pallas_call | solution.py:44
  34.4 1.2 %collective-permute-start.17 = (bf16[320,384]{1,0:T(8,128)(2,1)S(1)}, bf16[320,384]{1,0:T(8,128)(2,1)S(1)}, u32[]{:S(2)}, u32[]{:S(2)}) collective-permute-start(bf16[320,384]{1,0:T(8,128)(2,1)S(1)} %get-tuple-element.70), channel_id=1, source_target_pairs={{0,4},{4,0},{8,12},{12,8},{16,20},{20,16},{24,28},{28,24},{1,5},{5... | collective-permute-start | bytes 737288 | tf_op jit(solution)/shard_map/ppermute | solution.py:35
  35.6 0.4 collective-permute-start.18
  36.0 0.6 %project.1 = (f32[128,768]{1,0:T(8,128)S(1)}, f32[128,768]{1,0:T(8,128)S(1)}, bf16[128,768]{1,0:T(8,128)(2,1)S(1)}, bf16[128,384]{1,0:T(8,128)(2,1)S(1)}, bf16[128,384]{1,0:T(8,128)(2,1)S(1)}) custom-call(f32[384,128]{1,0:T(8,128)S(1)} %get-tuple-element.52.own_ref, bf16[384,128]{1,0:T(8,128)(2,1)S(1)} %collective-permute-done.6.pair_ref, ...), custom_call_target="tpu_custom_call" | custom-call | bytes 2214000 | tf_op jit(solution)/shard_map/project/pallas_call | solution.py:44
  36.6 0.1 collective-permute-start.13
  36.7 0.5 %collective-permute-start.14 = (bf16[128,384]{1,0:T(8,128)(2,1)S(1)}, bf16[128,384]{1,0:T(8,128)(2,1)S(1)}, u32[]{:S(2)}, u32[]{:S(2)}) collective-permute-start(bf16[128,384]{1,0:T(8,128)(2,1)S(1)} %get-tuple-element.66), channel_id=1, source_target_pairs={{0,1},{1,0},{2,3},{3,2},{4,5},{5,4},{6,7},{7,6},{8,9},{9,8},{10,11... | collective-permute-start | bytes 294920 | tf_op jit(solution)/shard_map/ppermute | solution.py:35
  37.2 0.1 collective-permute-start.12
  37.3 0.7 %collective-permute-done.13.left_ref = bf16[128,384]{1,0:T(8,128)(2,1)S(1)} collective-permute-done((bf16[128,384]{1,0:T(8,128)(2,1)S(1)}, bf16[128,384]{1,0:T(8,128)(2,1)S(1)}, u32[]{:S(2)}, u32[]{:S(2)}) %collective-permute-start.13) | collective-permute-done | bytes 98336 | tf_op jit(solution)/shard_map/ppermute | solution.py:35
  38.0 0.2 collective-permute-done.14.right_ref
  38.2 0.6 %collective-permute-start.15 = (bf16[128,768]{1,0:T(8,128)(2,1)S(1)}, bf16[128,768]{1,0:T(8,128)(2,1)S(1)}, u32[]{:S(2)}, u32[]{:S(2)}) collective-permute-start(bf16[128,768]{1,0:T(8,128)(2,1)S(1)} %add_near.1), channel_id=1, source_target_pairs={{0,2},{1,3},{2,0},{3,1},{4,6},{5,7},{6,4},{7,5},{8,10},{9,11},{10,... | collective-permute-start | bytes 589832 | tf_op jit(solution)/shard_map/ppermute | solution.py:35
  38.8 1.8 %collective-permute-start.16 = (bf16[176,384]{1,0:T(8,128)(2,1)S(1)}, bf16[176,384]{1,0:T(8,128)(2,1)S(1)}, u32[]{:S(2)}, u32[]{:S(2)}) collective-permute-start(bf16[176,384]{1,0:T(8,128)(2,1)S(1)} %get-tuple-element.68), channel_id=1, source_target_pairs={{0,16},{4,20},{8,24},{12,28},{16,0},{20,4},{24,8},{28,12},{1,17},{... | collective-permute-start | bytes 405512 | tf_op jit(solution)/shard_map/ppermute | solution.py:35
  40.6 0.1 collective-permute-done.17.got_k_ref
  40.6 1.2 %collective-permute-done.18.got_v_ref = bf16[320,384]{1,0:T(8,128)(2,1)S(1)} collective-permute-done((bf16[320,384]{1,0:T(8,128)(2,1)S(1)}, bf16[320,384]{1,0:T(8,128)(2,1)S(1)}, u32[]{:S(2)}, u32[]{:S(2)}) %collective-permute-start.18) | collective-permute-done | bytes 245792 | tf_op jit(solution)/shard_map/ppermute | solution.py:35
  41.8 0.1 pass_on.1
  41.9 0.5 collective-permute-start.19
  42.3 0.9 %collective-permute-start.20 = (bf16[160,384]{1,0:T(8,128)(2,1)S(1)}, bf16[160,384]{1,0:T(8,128)(2,1)S(1)}, u32[]{:S(2)}, u32[]{:S(2)}) collective-permute-start(bf16[160,384]{1,0:T(8,128)(2,1)S(1)} %get-tuple-element.75), channel_id=1, source_target_pairs={{0,4},{4,0},{8,12},{12,8},{16,20},{20,16},{24,28},{28,24},{1,5},{5... | collective-permute-start | bytes 368648 | tf_op jit(solution)/shard_map/ppermute | solution.py:35
  43.2 5.1 %collective-permute-done.16.dq_pair_ref = bf16[176,384]{1,0:T(8,128)(2,1)S(1)} collective-permute-done((bf16[176,384]{1,0:T(8,128)(2,1)S(1)}, bf16[176,384]{1,0:T(8,128)(2,1)S(1)}, u32[]{:S(2)}, u32[]{:S(2)}) %collective-permute-start.16) | collective-permute-done | bytes 135200 | tf_op jit(solution)/shard_map/ppermute | solution.py:35
  48.3 0.3 collective-permute-done.19.rest_k_ref
  48.5 0.9 %finish.1 = (bf16[128,384]{1,0:T(8,128)(2,1)}, bf16[128,384]{1,0:T(8,128)(2,1)}, bf16[128,384]{1,0:T(8,128)(2,1)}, bf16[32,384]{1,0:T(8,128)(2,1)}, bf16[32,384]{1,0:T(8,128)(2,1)}, /*index=5*/bf16[128,768]{1,0:T(8,128)(2,1)}) custom-call(f32[128,768]{1,0:T(8,128)S(1)} %get-tuple-element.62.keep_ref, bf16[128,768]{1,0:T(8,128)(2,1)S(1)} %collective-permute-done.12.core_ref, ...), custom_call_target="tpu_custom_call" | custom-call | bytes 3321000 | tf_op jit(solution)/shard_map/finish/pallas_call | solution.py:44
  (16 shorter events, 0.1 us)
Async XLA Ops:
  0.6 9.5 %collective-permute-start.8 = (bf16[128,768]{1,0:T(8,128)(2,1)}, bf16[128,768]{1,0:T(8,128)(2,1)S(1)}, u32[]{:S(2)}, u32[]{:S(2)}) collective-permute-start(bf16[128,768]{1,0:T(8,128)(2,1)} %own_ref.1), channel_id=1, source_target_pairs={{0,2},{1,3},{2,0},{3,1},{4,6},{5,7},{6,4},{7,5},{8,10},{9,11},{10,... | collective-permute-start | bytes 589832 | tf_op jit(solution)/shard_map/ppermute | solution.py:35
  5.3 13.3 %copy-start.1 = (bf16[128,768]{1,0:T(8,128)(2,1)S(1)}, bf16[128,768]{1,0:T(8,128)(2,1)}, u32[]{:S(2)}) copy-start(bf16[128,768]{1,0:T(8,128)(2,1)} %own_ref.1) | copy-start | bytes 589828
  5.3 8.0 %collective-permute-start.2 = (bf16[320,384]{1,0:T(8,128)(2,1)}, bf16[320,384]{1,0:T(8,128)(2,1)S(1)}, u32[]{:S(2)}, u32[]{:S(2)}) collective-permute-start(bf16[320,384]{1,0:T(8,128)(2,1)} %load.1.kv0), channel_id=1, source_target_pairs={{0,8},{4,12},{8,0},{12,4},{16,24},{20,28},{24,16},{28,20},{1,9},{5... | collective-permute-start | bytes 737288 | tf_op jit(solution)/shard_map/ppermute | solution.py:35
  7.0 7.3 %collective-permute-start.1 = (bf16[320,384]{1,0:T(8,128)(2,1)}, bf16[320,384]{1,0:T(8,128)(2,1)S(1)}, u32[]{:S(2)}, u32[]{:S(2)}) collective-permute-start(bf16[320,384]{1,0:T(8,128)(2,1)} %load.1.kv0), channel_id=1, source_target_pairs={{0,4},{4,0},{8,12},{12,8},{16,20},{20,16},{24,28},{28,24},{1,5},{5... | collective-permute-start | bytes 737288 | tf_op jit(solution)/shard_map/ppermute | solution.py:35
  8.5 8.6 %collective-permute-start.7 = (bf16[128,768]{1,0:T(8,128)(2,1)}, bf16[128,768]{1,0:T(8,128)(2,1)S(1)}, u32[]{:S(2)}, u32[]{:S(2)}) collective-permute-start(bf16[128,768]{1,0:T(8,128)(2,1)} %own_ref.1), channel_id=1, source_target_pairs={{0,1},{1,0},{2,3},{3,2},{4,5},{5,4},{6,7},{7,6},{8,9},{9,8},{10,11... | collective-permute-start | bytes 589832 | tf_op jit(solution)/shard_map/ppermute | solution.py:35
  10.1 12.0 %copy-start.3 = (s32[8,2]{0,1:T(2,128)S(1)}, s32[8,2]{0,1:T(2,128)}, u32[]{:S(2)}) copy-start(s32[8,2]{0,1:T(2,128)} %param.14) | copy-start | bytes 196
  10.1 12.0 %copy-start.2 = (s32[8]{0:T(128)S(1)}, s32[8]{0:T(128)}, u32[]{:S(2)}) copy-start(s32[8]{0:T(128)} %counts_ref.1) | copy-start | bytes 100
  10.1 12.7 %copy-start = (bf16[320,384]{1,0:T(8,128)(2,1)S(1)}, bf16[320,384]{1,0:T(8,128)(2,1)}, u32[]{:S(2)}) copy-start(bf16[320,384]{1,0:T(8,128)(2,1)} %load.1.kv0) | copy-start | bytes 737284
  10.2 8.4 %collective-permute-start.9 = (bf16[128,768]{1,0:T(8,128)(2,1)S(1)}, bf16[128,768]{1,0:T(8,128)(2,1)S(1)}, u32[]{:S(2)}, u32[]{:S(2)}) collective-permute-start(bf16[128,768]{1,0:T(8,128)(2,1)S(1)} %collective-permute-done.8.near_ref), channel_id=1, source_target_pairs={{0,1},{1,0},{2,3},{3,2},{4,5},{5,4},{6,7},{7,6},{8,9},{9,8},{10,11... | collective-permute-start | bytes 589832 | tf_op jit(solution)/shard_map/ppermute | solution.py:35
  10.7 12.1 %collective-permute-start = (bf16[128,384]{1,0:T(8,128)(2,1)}, bf16[128,384]{1,0:T(8,128)(2,1)}, u32[]{:S(2)}, u32[]{:S(2)}) collective-permute-start(bf16[128,384]{1,0:T(8,128)(2,1)} %q_own_ref.3), channel_id=1, source_target_pairs={{0,16},{4,20},{8,24},{12,28},{16,0},{20,4},{24,8},{28,12},{1,17},{... | collective-permute-start | bytes 294920 | tf_op jit(solution)/shard_map/ppermute | solution.py:35
  15.0 7.8 %collective-permute-start.3 = (bf16[320,128]{1,0:T(8,128)(2,1)}, bf16[320,128]{1,0:T(8,128)(2,1)S(1)}, u32[]{:S(2)}, u32[]{:S(2)}) collective-permute-start(bf16[320,128]{1,0:T(8,128)(2,1)} %get-tuple-element.46), channel_id=1, source_target_pairs={{0,4},{4,0},{8,12},{12,8},{16,20},{20,16},{24,28},{28,24},{1,5},{5... | collective-permute-start | bytes 245768 | tf_op jit(solution)/shard_map/ppermute | solution.py:35
  16.6 6.3 %collective-permute-start.4 = (bf16[320,128]{1,0:T(8,128)(2,1)}, bf16[320,128]{1,0:T(8,128)(2,1)S(1)}, u32[]{:S(2)}, u32[]{:S(2)}) collective-permute-start(bf16[320,128]{1,0:T(8,128)(2,1)} %get-tuple-element.47), channel_id=1, source_target_pairs={{0,4},{4,0},{8,12},{12,8},{16,20},{20,16},{24,28},{28,24},{1,5},{5... | collective-permute-start | bytes 245768 | tf_op jit(solution)/shard_map/ppermute | solution.py:35
  17.1 5.8 %collective-permute-start.5 = (bf16[320,128]{1,0:T(8,128)(2,1)}, bf16[320,128]{1,0:T(8,128)(2,1)S(1)}, u32[]{:S(2)}, u32[]{:S(2)}) collective-permute-start(bf16[320,128]{1,0:T(8,128)(2,1)} %get-tuple-element.48), channel_id=1, source_target_pairs={{0,4},{4,0},{8,12},{12,8},{16,20},{20,16},{24,28},{28,24},{1,5},{5... | collective-permute-start | bytes 245768 | tf_op jit(solution)/shard_map/ppermute | solution.py:35
  19.4 7.7 %collective-permute-start.10 = (bf16[128,384]{1,0:T(8,128)(2,1)S(1)}, bf16[128,384]{1,0:T(8,128)(2,1)S(1)}, u32[]{:S(2)}, u32[]{:S(2)}) collective-permute-start(bf16[128,384]{1,0:T(8,128)(2,1)S(1)} %dattn.1.d_own_ref), channel_id=1, source_target_pairs={{0,16},{4,20},{8,24},{12,28},{16,0},{20,4},{24,8},{28,12},{1,17},{... | collective-permute-start | bytes 294920 | tf_op jit(solution)/shard_map/ppermute | solution.py:35
  25.2 9.1 %collective-permute-start.6 = (bf16[384,128]{1,0:T(8,128)(2,1)S(1)}, bf16[384,128]{1,0:T(8,128)(2,1)S(1)}, u32[]{:S(2)}, u32[]{:S(2)}) collective-permute-start(bf16[384,128]{1,0:T(8,128)(2,1)S(1)} %get-tuple-element.53), channel_id=1, source_target_pairs={{0,16},{4,20},{8,24},{12,28},{16,0},{20,4},{24,8},{28,12},{1,17},{... | collective-permute-start | bytes 294920 | tf_op jit(solution)/shard_map/ppermute | solution.py:35
  27.5 4.8 %collective-permute-start.11 = (f32[16,256]{1,0:T(8,128)S(1)}, f32[16,256]{1,0:T(8,128)S(1)}, u32[]{:S(2)}, u32[]{:S(2)}) collective-permute-start(f32[16,256]{1,0:T(8,128)S(1)} %get-tuple-element.57.stats_ref), channel_id=1, source_target_pairs={{0,16},{4,20},{8,24},{12,28},{16,0},{20,4},{24,8},{28,12},{1,17},{... | collective-permute-start | bytes 49160 | tf_op jit(solution)/shard_map/ppermute | solution.py:35
  34.4 6.3 %collective-permute-start.17 = (bf16[320,384]{1,0:T(8,128)(2,1)S(1)}, bf16[320,384]{1,0:T(8,128)(2,1)S(1)}, u32[]{:S(2)}, u32[]{:S(2)}) collective-permute-start(bf16[320,384]{1,0:T(8,128)(2,1)S(1)} %get-tuple-element.70), channel_id=1, source_target_pairs={{0,4},{4,0},{8,12},{12,8},{16,20},{20,16},{24,28},{28,24},{1,5},{5... | collective-permute-start | bytes 737288 | tf_op jit(solution)/shard_map/ppermute | solution.py:35
  35.6 6.2 %collective-permute-start.18 = (bf16[320,384]{1,0:T(8,128)(2,1)S(1)}, bf16[320,384]{1,0:T(8,128)(2,1)S(1)}, u32[]{:S(2)}, u32[]{:S(2)}) collective-permute-start(bf16[320,384]{1,0:T(8,128)(2,1)S(1)} %get-tuple-element.71), channel_id=1, source_target_pairs={{0,8},{4,12},{8,0},{12,4},{16,24},{20,28},{24,16},{28,20},{1,9},{5... | collective-permute-start | bytes 737288 | tf_op jit(solution)/shard_map/ppermute | solution.py:35
  36.6 1.4 %collective-permute-start.13 = (bf16[128,384]{1,0:T(8,128)(2,1)S(1)}, bf16[128,384]{1,0:T(8,128)(2,1)S(1)}, u32[]{:S(2)}, u32[]{:S(2)}) collective-permute-start(bf16[128,384]{1,0:T(8,128)(2,1)S(1)} %get-tuple-element.65), channel_id=1, source_target_pairs={{0,1},{1,0},{2,3},{3,2},{4,5},{5,4},{6,7},{7,6},{8,9},{9,8},{10,11... | collective-permute-start | bytes 294920 | tf_op jit(solution)/shard_map/ppermute | solution.py:35
  36.7 1.4 %collective-permute-start.14 = (bf16[128,384]{1,0:T(8,128)(2,1)S(1)}, bf16[128,384]{1,0:T(8,128)(2,1)S(1)}, u32[]{:S(2)}, u32[]{:S(2)}) collective-permute-start(bf16[128,384]{1,0:T(8,128)(2,1)S(1)} %get-tuple-element.66), channel_id=1, source_target_pairs={{0,1},{1,0},{2,3},{3,2},{4,5},{5,4},{6,7},{7,6},{8,9},{9,8},{10,11... | collective-permute-start | bytes 294920 | tf_op jit(solution)/shard_map/ppermute | solution.py:35
  37.2 11.0 %collective-permute-start.12 = (bf16[128,768]{1,0:T(8,128)(2,1)S(1)}, bf16[128,768]{1,0:T(8,128)(2,1)S(1)}, u32[]{:S(2)}, u32[]{:S(2)}) collective-permute-start(bf16[128,768]{1,0:T(8,128)(2,1)S(1)} %get-tuple-element.63), channel_id=1, source_target_pairs={{0,1},{1,0},{2,3},{3,2},{4,5},{5,4},{6,7},{7,6},{8,9},{9,8},{10,11... | collective-permute-start | bytes 589832 | tf_op jit(solution)/shard_map/ppermute | solution.py:35
  38.2 10.1 %collective-permute-start.15 = (bf16[128,768]{1,0:T(8,128)(2,1)S(1)}, bf16[128,768]{1,0:T(8,128)(2,1)S(1)}, u32[]{:S(2)}, u32[]{:S(2)}) collective-permute-start(bf16[128,768]{1,0:T(8,128)(2,1)S(1)} %add_near.1), channel_id=1, source_target_pairs={{0,2},{1,3},{2,0},{3,1},{4,6},{5,7},{6,4},{7,5},{8,10},{9,11},{10,... | collective-permute-start | bytes 589832 | tf_op jit(solution)/shard_map/ppermute | solution.py:35
  38.8 9.5 %collective-permute-start.16 = (bf16[176,384]{1,0:T(8,128)(2,1)S(1)}, bf16[176,384]{1,0:T(8,128)(2,1)S(1)}, u32[]{:S(2)}, u32[]{:S(2)}) collective-permute-start(bf16[176,384]{1,0:T(8,128)(2,1)S(1)} %get-tuple-element.68), channel_id=1, source_target_pairs={{0,16},{4,20},{8,24},{12,28},{16,0},{20,4},{24,8},{28,12},{1,17},{... | collective-permute-start | bytes 405512 | tf_op jit(solution)/shard_map/ppermute | solution.py:35
  41.9 6.6 %collective-permute-start.19 = (bf16[160,384]{1,0:T(8,128)(2,1)S(1)}, bf16[160,384]{1,0:T(8,128)(2,1)S(1)}, u32[]{:S(2)}, u32[]{:S(2)}) collective-permute-start(bf16[160,384]{1,0:T(8,128)(2,1)S(1)} %get-tuple-element.74), channel_id=1, source_target_pairs={{0,8},{4,12},{8,0},{12,4},{16,24},{20,28},{24,16},{28,20},{1,9},{5... | collective-permute-start | bytes 368648 | tf_op jit(solution)/shard_map/ppermute | solution.py:35
  42.3 6.2 %collective-permute-start.20 = (bf16[160,384]{1,0:T(8,128)(2,1)S(1)}, bf16[160,384]{1,0:T(8,128)(2,1)S(1)}, u32[]{:S(2)}, u32[]{:S(2)}) collective-permute-start(bf16[160,384]{1,0:T(8,128)(2,1)S(1)} %get-tuple-element.75), channel_id=1, source_target_pairs={{0,4},{4,0},{8,12},{12,8},{16,20},{20,16},{24,28},{28,24},{1,5},{5... | collective-permute-start | bytes 368648 | tf_op jit(solution)/shard_map/ppermute | solution.py:35

commit v16 on v15

--- a/solution.py
+++ b/solution.py
@@ -39,7 +39,7 @@
     return pl.CostEstimate(flops=0, bytes_accessed=int(micros * HBM_BYTES), transcendentals=0)
 
 
-def local_call(body, name, micros, out_shapes, args, tables=0, vmem=20):
+def local_call(body, name, micros, out_shapes, args, tables=0):
     spaces = [pltpu.SMEM] * tables + [pltpu.VMEM] * (len(args) - tables)
     return pl.pallas_call(
         body,
@@ -47,7 +47,7 @@
         out_shape=out_shapes,
         in_specs=[pl.BlockSpec(memory_space=space) for space in spaces],
         out_specs=[pl.BlockSpec(memory_space=pltpu.VMEM)] * len(out_shapes),
-        compiler_params=pltpu.CompilerParams(vmem_limit_bytes=vmem * 2**20),
+        compiler_params=pltpu.CompilerParams(vmem_limit_bytes=16 * 2**20),
         cost_estimate=cost_of(micros),
     )(*args)
 
@@ -347,7 +347,6 @@
         0.8,
         [shape((rows, width), BF16)],
         (grad_out, grad_core, grad_near, grad_far, weight),
-        vmem=40,
     )[0]
     d_pair = swap(d_own, "ctx", PAIR)
     limits = local_call(
@@ -411,7 +410,7 @@
         [shape((rows, share), F32)] * 2
         + [shape((rows, share), BF16)]
         + [shape((rows, half), BF16)] * 2,
-        (attn_own, attn_got, stats, stats_pair, weight),
+        (attn_own, attn_got, stats, stats_pair, w_out),
     )
     far_left, far_right = (swap(part, "head", 1) for part in (far_left, far_right))
     out_near = swap(

time: 49.7 us -> 47.9 us (0.964)
  Pallas kernels: 11.9 us -> 9.4 us
  waiting for transfers between devices: 12 us -> 14.1 us
  starting transfers between devices: 24.6 us -> 23.3 us
    pallas_call x11, Pallas kernels: 8.63 us -> 6.1 us  [local_call(): pl.pallas_call(body, name=name, out_shape=out_shapes, in_specs=[pl.BlockS...]
    ppermute x21, waiting for transfers between devices: 12 us -> 14.1 us  [swap(): return lax.ppermute(block, axis, [(i, i ^ bit) for i in range(count)])]
    ppermute x21, starting transfers between devices: 24.6 us -> 23.3 us  [swap(): return lax.ppermute(block, axis, [(i, i ^ bit) for i in range(count)])]
  transfers between devices with their start and end apart: 21 -> 21, of which waited for: 8 -> 9; matrix products, arithmetic and copies ran while one was open for 0% -> 0% of each run, Pallas kernels for 22% -> 18%
where the time goes in v16:
time: 47.9 us; the launch traced here: 47.7 us
  starting transfers between devices  23.3 us (49%)
  waiting for transfers between devices  14.1 us (29%)
  Pallas kernels  9.4 us (20%)
  between operations  0.85 us (2%)
    ppermute x21, starting transfers between devices, swap(): return lax.ppermute(block, axis, [(i, i ^ bit) for i in range(count)])  23.3 us
    ppermute x21, waiting for transfers between devices, swap(): return lax.ppermute(block, axis, [(i, i ^ bit) for i in range(count)])  14.1 us
    pallas_call x11, Pallas kernels, local_call(): pl.pallas_call(body, name=name, out_shape=out_shapes, in_specs=[pl.BlockS...  6.1 us
    pallas_call x1, Pallas kernels, load_keys(): pl.pallas_call(load_kernel, name='load', out_shape=jax.ShapeDtypeStruct((...  1.67 us
    pallas_call x1, Pallas kernels, load_weight(): pl.pallas_call(load_weight_kernel, name='load_w', out_shape=jax.ShapeDtyp...  1.63 us
  transfers between devices with their start and end apart: 21, of which 9 were waited for; matrix products, arithmetic and copies ran while one was open for 0% of the time, Pallas kernels for 18%

profile of v16, /device:TPU:0, one launch (start us, length us, event | category | flops | bytes accessed | tf_op | source)
XLA Modules:
  0.0 47.7 jit_solution(11283146901594889027)
XLA Ops:
  0.6 3.0 %collective-permute-start.8 = (bf16[128,768]{1,0:T(8,128)(2,1)}, bf16[128,768]{1,0:T(8,128)(2,1)S(1)}, u32[]{:S(2)}, u32[]{:S(2)}) collective-permute-start(bf16[128,768]{1,0:T(8,128)(2,1)} %own_ref.1), channel_id=1, source_target_pairs={{0,2},{1,3},{2,0},{3,1},{4,6},{5,7},{6,4},{7,5},{8,10},{9,11},{10,... | collective-permute-start | bytes 589832 | tf_op jit(solution)/shard_map/ppermute | solution.py:35
  3.6 1.7 %load.1.kv0 = bf16[320,384]{1,0:T(8,128)(2,1)} custom-call(bf16[128,384]{1,0:T(8,128)(2,1)} %k_ref.1, bf16[32,384]{1,0:T(8,128)(2,1)} %hk_ref.1, bf16[128,384]{1,0:T(8,128)(2,1)} %v_ref.1, bf16[32,384]{1,0:T(8,128)(2,1)} %hv_ref.1), custom_call_target="tpu_custom_call" | custom-call | bytes 5904000 | tf_op jit(solution)/shard_map/load/pallas_call | solution.py:74
  5.3 0.0 copy-start.2
  5.3 0.0 copy-start.3
  5.3 1.6 %collective-permute-start.2 = (bf16[320,384]{1,0:T(8,128)(2,1)}, bf16[320,384]{1,0:T(8,128)(2,1)S(1)}, u32[]{:S(2)}, u32[]{:S(2)}) collective-permute-start(bf16[320,384]{1,0:T(8,128)(2,1)} %load.1.kv0), channel_id=1, source_target_pairs={{0,8},{4,12},{8,0},{12,4},{16,24},{20,28},{24,16},{28,20},{1,9},{5... | collective-permute-start | bytes 737288 | tf_op jit(solution)/shard_map/ppermute | solution.py:35
  7.0 1.5 %collective-permute-start.1 = (bf16[320,384]{1,0:T(8,128)(2,1)}, bf16[320,384]{1,0:T(8,128)(2,1)S(1)}, u32[]{:S(2)}, u32[]{:S(2)}) collective-permute-start(bf16[320,384]{1,0:T(8,128)(2,1)} %load.1.kv0), channel_id=1, source_target_pairs={{0,4},{4,0},{8,12},{12,8},{16,20},{20,16},{24,28},{28,24},{1,5},{5... | collective-permute-start | bytes 737288 | tf_op jit(solution)/shard_map/ppermute | solution.py:35
  8.5 0.0 collective-permute-start.7
  8.5 1.6 %load_w.1.w_ref = bf16[384,3072]{1,0:T(8,128)(2,1)S(1)} custom-call(bf16[384,3072]{1,0:T(8,128)(2,1)} %w_ref.3), custom_call_target="tpu_custom_call" | custom-call | bytes 5904000 | tf_op jit(solution)/shard_map/load_w/pallas_call | solution.py:113
  10.1 0.0 copy-start.5
  10.2 0.0 copy-start.4
  10.2 0.6 %collective-permute-start.9 = (bf16[128,768]{1,0:T(8,128)(2,1)S(1)}, bf16[128,768]{1,0:T(8,128)(2,1)S(1)}, u32[]{:S(2)}, u32[]{:S(2)}) collective-permute-start(bf16[128,768]{1,0:T(8,128)(2,1)S(1)} %collective-permute-done.8.near_ref), channel_id=1, source_target_pairs={{0,1},{1,0},{2,3},{3,2},{4,5},{5,4},{6,7},{7,6},{8,9},{9,8},{10,11... | collective-permute-start | bytes 589832 | tf_op jit(solution)/shard_map/ppermute | solution.py:35
  10.8 2.6 %collective-permute-start = (bf16[128,384]{1,0:T(8,128)(2,1)S(1)}, bf16[128,384]{1,0:T(8,128)(2,1)S(1)}, u32[]{:S(2)}, u32[]{:S(2)}) collective-permute-start(bf16[128,384]{1,0:T(8,128)(2,1)S(1)} %copy-done.2), channel_id=1, source_target_pairs={{0,16},{4,20},{8,24},{12,28},{16,0},{20,4},{24,8},{28,12},{1,17},{... | collective-permute-start | bytes 294920 | tf_op jit(solution)/shard_map/ppermute | solution.py:35
  13.4 1.0 %collective-permute-done.1.kv1 = bf16[320,384]{1,0:T(8,128)(2,1)S(1)} collective-permute-done((bf16[320,384]{1,0:T(8,128)(2,1)}, bf16[320,384]{1,0:T(8,128)(2,1)S(1)}, u32[]{:S(2)}, u32[]{:S(2)}) %collective-permute-start.1) | collective-permute-done | bytes 245792 | tf_op jit(solution)/shard_map/ppermute | solution.py:35
  14.4 1.6 %collective-permute-start.3 = (bf16[320,128]{1,0:T(8,128)(2,1)S(1)}, bf16[320,128]{1,0:T(8,128)(2,1)S(1)}, u32[]{:S(2)}, u32[]{:S(2)}) collective-permute-start(bf16[320,128]{1,0:T(8,128)(2,1)S(1)} %get-tuple-element.46), channel_id=1, source_target_pairs={{0,4},{4,0},{8,12},{12,8},{16,20},{20,16},{24,28},{28,24},{1,5},{5... | collective-permute-start | bytes 245768 | tf_op jit(solution)/shard_map/ppermute | solution.py:35
  16.0 0.5 %collective-permute-start.4 = (bf16[320,128]{1,0:T(8,128)(2,1)S(1)}, bf16[320,128]{1,0:T(8,128)(2,1)S(1)}, u32[]{:S(2)}, u32[]{:S(2)}) collective-permute-start(bf16[320,128]{1,0:T(8,128)(2,1)S(1)} %get-tuple-element.47), channel_id=1, source_target_pairs={{0,4},{4,0},{8,12},{12,8},{16,20},{20,16},{24,28},{28,24},{1,5},{5... | collective-permute-start | bytes 245768 | tf_op jit(solution)/shard_map/ppermute | solution.py:35
  16.5 0.0 collective-permute-done.7.core_ref
  16.5 1.5 %collective-permute-start.5 = (bf16[320,128]{1,0:T(8,128)(2,1)S(1)}, bf16[320,128]{1,0:T(8,128)(2,1)S(1)}, u32[]{:S(2)}, u32[]{:S(2)}) collective-permute-start(bf16[320,128]{1,0:T(8,128)(2,1)S(1)} %get-tuple-element.48), channel_id=1, source_target_pairs={{0,4},{4,0},{8,12},{12,8},{16,20},{20,16},{24,28},{28,24},{1,5},{5... | collective-permute-start | bytes 245768 | tf_op jit(solution)/shard_map/ppermute | solution.py:35
  18.0 0.0 collective-permute-done.9.far_ref
  18.0 0.8 %dattn.1.d_own_ref = bf16[128,384]{1,0:T(8,128)(2,1)S(1)} custom-call(bf16[128,768]{1,0:T(8,128)(2,1)S(1)} %copy-done.3, bf16[128,768]{1,0:T(8,128)(2,1)S(1)} %collective-permute-done.7.core_ref, bf16[128,768]{1,0:T(8,128)(2,1)S(1)} %collective-permute-done.8.near_ref, bf16[128,768]{1,0:T(8,128)(2,1)S(1)} %collective-permute-done.9.far_ref, ...), custom_call_target="tpu_custom_call" | custom-call | bytes 2952000 | tf_op jit(solution)/shard_map/dattn/pallas_call | solution.py:44
  18.8 2.7 %collective-permute-start.10 = (bf16[128,384]{1,0:T(8,128)(2,1)S(1)}, bf16[128,384]{1,0:T(8,128)(2,1)S(1)}, u32[]{:S(2)}, u32[]{:S(2)}) collective-permute-start(bf16[128,384]{1,0:T(8,128)(2,1)S(1)} %dattn.1.d_own_ref), channel_id=1, source_target_pairs={{0,16},{4,20},{8,24},{12,28},{16,0},{20,4},{24,8},{28,12},{1,17},{... | collective-permute-start | bytes 294920 | tf_op jit(solution)/shard_map/ppermute | solution.py:35
  21.5 0.1 copy.15.levels_ref
  21.6 0.6 %limits.1.limits_ref = s32[8,256]{1,0:T(8,128)S(1)} custom-call(s32[8,2]{1,0:T(8,128)S(1)} %copy.15.levels_ref, s32[8]{0:T(128)S(1)} %copy-done.4), custom_call_target="tpu_custom_call" | custom-call | bytes 2214000 | tf_op jit(solution)/shard_map/limits/pallas_call | solution.py:44
  22.2 0.0 collective-permute-done.q_pair_ref
  22.3 1.0 %scores.1 = (f32[8,256]{1,0:T(8,128)S(1)}, bf16[1920,256]{1,0:T(8,128)(2,1)S(1)}) custom-call(s32[8,256]{1,0:T(8,128)S(1)} %limits.1.limits_ref, bf16[128,384]{1,0:T(8,128)(2,1)S(1)} %copy-done.2, bf16[128,384]{1,0:T(8,128)(2,1)S(1)} %collective-permute-done.q_pair_ref, bf16[320,384]{1,0:T(8,128)(2,1)S(1)} %copy-done.1, ...), custom_call_target="tpu_custom_call" | custom-call | bytes 3321000 | tf_op jit(solution)/shard_map/scores/pallas_call | solution.py:44
  23.3 0.4 attn.1
  23.7 1.7 %collective-permute-start.6 = (bf16[384,128]{1,0:T(8,128)(2,1)S(1)}, bf16[384,128]{1,0:T(8,128)(2,1)S(1)}, u32[]{:S(2)}, u32[]{:S(2)}) collective-permute-start(bf16[384,128]{1,0:T(8,128)(2,1)S(1)} %get-tuple-element.53), channel_id=1, source_target_pairs={{0,16},{4,20},{8,24},{12,28},{16,0},{20,4},{24,8},{28,12},{1,17},{... | collective-permute-start | bytes 294920 | tf_op jit(solution)/shard_map/ppermute | solution.py:35
  25.4 2.0 %collective-permute-done.10.d_pair_ref = bf16[128,384]{1,0:T(8,128)(2,1)S(1)} collective-permute-done((bf16[128,384]{1,0:T(8,128)(2,1)S(1)}, bf16[128,384]{1,0:T(8,128)(2,1)S(1)}, u32[]{:S(2)}, u32[]{:S(2)}) %collective-permute-start.10) | collective-permute-done | bytes 98336 | tf_op jit(solution)/shard_map/ppermute | solution.py:35
  27.4 0.4 delta.1
  27.9 0.0 copy-start
  27.9 0.4 collective-permute-start.11
  28.3 4.4 %collective-permute-done.11.stats_pair_ref = f32[16,256]{1,0:T(8,128)S(1)} collective-permute-done((f32[16,256]{1,0:T(8,128)S(1)}, f32[16,256]{1,0:T(8,128)S(1)}, u32[]{:S(2)}, u32[]{:S(2)}) %collective-permute-start.11) | collective-permute-done | bytes 16416 | tf_op jit(solution)/shard_map/ppermute | solution.py:35
  32.7 1.1 %backward.1 = (f32[128,384]{1,0:T(8,128)S(1)}, bf16[176,384]{1,0:T(8,128)(2,1)S(1)}, f32[320,384]{1,0:T(8,128)S(1)}, bf16[320,384]{1,0:T(8,128)(2,1)S(1)}, bf16[...) custom-call(bf16[128,384]{1,0:T(8,128)(2,1)S(1)} %copy-done.2, ...), custom_call_target="tpu_custom_call" | custom-call | bytes 4059000 | tf_op jit(solution)/shard_map/backward/pallas_call | solution.py:44
  33.8 0.5 collective-permute-start.17
  34.3 0.6 %project.1 = (f32[128,768]{1,0:T(8,128)S(1)}, f32[128,768]{1,0:T(8,128)S(1)}, bf16[128,768]{1,0:T(8,128)(2,1)S(1)}, bf16[128,384]{1,0:T(8,128)(2,1)S(1)}, bf16[128,384]{1,0:T(8,128)(2,1)S(1)}) custom-call(f32[384,128]{1,0:T(8,128)S(1)} %get-tuple-element.52.own_ref, bf16[384,128]{1,0:T(8,128)(2,1)S(1)} %collective-permute-done.6.pair_ref, ...), custom_call_target="tpu_custom_call" | custom-call | bytes 2214000 | tf_op jit(solution)/shard_map/project/pallas_call | solution.py:44
  34.9 0.1 collective-permute-start.13
  35.0 0.5 %collective-permute-start.14 = (bf16[128,384]{1,0:T(8,128)(2,1)S(1)}, bf16[128,384]{1,0:T(8,128)(2,1)S(1)}, u32[]{:S(2)}, u32[]{:S(2)}) collective-permute-start(bf16[128,384]{1,0:T(8,128)(2,1)S(1)} %get-tuple-element.66), channel_id=1, source_target_pairs={{0,1},{1,0},{2,3},{3,2},{4,5},{5,4},{6,7},{7,6},{8,9},{9,8},{10,11... | collective-permute-start | bytes 294920 | tf_op jit(solution)/shard_map/ppermute | solution.py:35
  35.5 0.1 collective-permute-start.12
  35.6 0.7 %collective-permute-done.13.left_ref = bf16[128,384]{1,0:T(8,128)(2,1)S(1)} collective-permute-done((bf16[128,384]{1,0:T(8,128)(2,1)S(1)}, bf16[128,384]{1,0:T(8,128)(2,1)S(1)}, u32[]{:S(2)}, u32[]{:S(2)}) %collective-permute-start.13) | collective-permute-done | bytes 98336 | tf_op jit(solution)/shard_map/ppermute | solution.py:35
  36.3 0.2 collective-permute-done.14.right_ref
  36.5 0.1 collective-permute-start.15
  36.6 2.7 %collective-permute-start.16 = (bf16[176,384]{1,0:T(8,128)(2,1)S(1)}, bf16[176,384]{1,0:T(8,128)(2,1)S(1)}, u32[]{:S(2)}, u32[]{:S(2)}) collective-permute-start(bf16[176,384]{1,0:T(8,128)(2,1)S(1)} %get-tuple-element.68), channel_id=1, source_target_pairs={{0,16},{4,20},{8,24},{12,28},{16,0},{20,4},{24,8},{28,12},{1,17},{... | collective-permute-start | bytes 405512 | tf_op jit(solution)/shard_map/ppermute | solution.py:35
  39.3 0.8 %collective-permute-done.17.got_k_ref = bf16[320,384]{1,0:T(8,128)(2,1)S(1)} collective-permute-done((bf16[320,384]{1,0:T(8,128)(2,1)S(1)}, bf16[320,384]{1,0:T(8,128)(2,1)S(1)}, u32[]{:S(2)}, u32[]{:S(2)}) %collective-permute-start.17) | collective-permute-done | bytes 245792 | tf_op jit(solution)/shard_map/ppermute | solution.py:35
  40.1 0.4 collective-permute-done.18.got_v_ref
  40.6 0.1 collective-permute-start.19
  40.6 1.7 %collective-permute-start.20 = (bf16[160,384]{1,0:T(8,128)(2,1)S(1)}, bf16[160,384]{1,0:T(8,128)(2,1)S(1)}, u32[]{:S(2)}, u32[]{:S(2)}) collective-permute-start(bf16[160,384]{1,0:T(8,128)(2,1)S(1)} %get-tuple-element.75), channel_id=1, source_target_pairs={{0,4},{4,0},{8,12},{12,8},{16,20},{20,16},{24,28},{28,24},{1,5},{5... | collective-permute-start | bytes 368648 | tf_op jit(solution)/shard_map/ppermute | solution.py:35
  42.3 4.1 %collective-permute-done.16.dq_pair_ref = bf16[176,384]{1,0:T(8,128)(2,1)S(1)} collective-permute-done((bf16[176,384]{1,0:T(8,128)(2,1)S(1)}, bf16[176,384]{1,0:T(8,128)(2,1)S(1)}, u32[]{:S(2)}, u32[]{:S(2)}) %collective-permute-start.16) | collective-permute-done | bytes 135200 | tf_op jit(solution)/shard_map/ppermute | solution.py:35
  46.4 0.4 collective-permute-done.19.rest_k_ref
  46.8 0.9 %finish.1 = (bf16[128,384]{1,0:T(8,128)(2,1)}, bf16[128,384]{1,0:T(8,128)(2,1)}, bf16[128,384]{1,0:T(8,128)(2,1)}, bf16[32,384]{1,0:T(8,128)(2,1)}, bf16[32,384]{1,0:T(8,128)(2,1)}, /*index=5*/bf16[128,768]{1,0:T(8,128)(2,1)}) custom-call(f32[128,768]{1,0:T(8,128)S(1)} %get-tuple-element.62.keep_ref, bf16[128,768]{1,0:T(8,128)(2,1)S(1)} %collective-permute-done.12.core_ref, ...), custom_call_target="tpu_custom_call" | custom-call | bytes 3321000 | tf_op jit(solution)/shard_map/finish/pallas_call | solution.py:44
  (20 shorter events, 0.2 us)
Async XLA Ops:
  0.6 9.5 %collective-permute-start.8 = (bf16[128,768]{1,0:T(8,128)(2,1)}, bf16[128,768]{1,0:T(8,128)(2,1)S(1)}, u32[]{:S(2)}, u32[]{:S(2)}) collective-permute-start(bf16[128,768]{1,0:T(8,128)(2,1)} %own_ref.1), channel_id=1, source_target_pairs={{0,2},{1,3},{2,0},{3,1},{4,6},{5,7},{6,4},{7,5},{8,10},{9,11},{10,... | collective-permute-start | bytes 589832 | tf_op jit(solution)/shard_map/ppermute | solution.py:35
  5.3 5.4 %copy-start.2 = (bf16[128,384]{1,0:T(8,128)(2,1)S(1)}, bf16[128,384]{1,0:T(8,128)(2,1)}, u32[]{:S(2)}) copy-start(bf16[128,384]{1,0:T(8,128)(2,1)} %q_own_ref.3) | copy-start | bytes 294916
  5.3 12.7 %copy-start.3 = (bf16[128,768]{1,0:T(8,128)(2,1)S(1)}, bf16[128,768]{1,0:T(8,128)(2,1)}, u32[]{:S(2)}) copy-start(bf16[128,768]{1,0:T(8,128)(2,1)} %own_ref.1) | copy-start | bytes 589828
  5.3 8.0 %collective-permute-start.2 = (bf16[320,384]{1,0:T(8,128)(2,1)}, bf16[320,384]{1,0:T(8,128)(2,1)S(1)}, u32[]{:S(2)}, u32[]{:S(2)}) collective-permute-start(bf16[320,384]{1,0:T(8,128)(2,1)} %load.1.kv0), channel_id=1, source_target_pairs={{0,8},{4,12},{8,0},{12,4},{16,24},{20,28},{24,16},{28,20},{1,9},{5... | collective-permute-start | bytes 737288 | tf_op jit(solution)/shard_map/ppermute | solution.py:35
  7.0 7.3 %collective-permute-start.1 = (bf16[320,384]{1,0:T(8,128)(2,1)}, bf16[320,384]{1,0:T(8,128)(2,1)S(1)}, u32[]{:S(2)}, u32[]{:S(2)}) collective-permute-start(bf16[320,384]{1,0:T(8,128)(2,1)} %load.1.kv0), channel_id=1, source_target_pairs={{0,4},{4,0},{8,12},{12,8},{16,20},{20,16},{24,28},{28,24},{1,5},{5... | collective-permute-start | bytes 737288 | tf_op jit(solution)/shard_map/ppermute | solution.py:35
  8.5 8.0 %collective-permute-start.7 = (bf16[128,768]{1,0:T(8,128)(2,1)}, bf16[128,768]{1,0:T(8,128)(2,1)S(1)}, u32[]{:S(2)}, u32[]{:S(2)}) collective-permute-start(bf16[128,768]{1,0:T(8,128)(2,1)} %own_ref.1), channel_id=1, source_target_pairs={{0,1},{1,0},{2,3},{3,2},{4,5},{5,4},{6,7},{7,6},{8,9},{9,8},{10,11... | collective-permute-start | bytes 589832 | tf_op jit(solution)/shard_map/ppermute | solution.py:35
  10.1 11.3 %copy-start.5 = (s32[8,2]{0,1:T(2,128)S(1)}, s32[8,2]{0,1:T(2,128)}, u32[]{:S(2)}) copy-start(s32[8,2]{0,1:T(2,128)} %param.14) | copy-start | bytes 196
  10.2 11.4 %copy-start.4 = (s32[8]{0:T(128)S(1)}, s32[8]{0:T(128)}, u32[]{:S(2)}) copy-start(s32[8]{0:T(128)} %counts_ref.1) | copy-start | bytes 100
  10.2 12.1 %copy-start.1 = (bf16[320,384]{1,0:T(8,128)(2,1)S(1)}, bf16[320,384]{1,0:T(8,128)(2,1)}, u32[]{:S(2)}) copy-start(bf16[320,384]{1,0:T(8,128)(2,1)} %load.1.kv0) | copy-start | bytes 737284
  10.2 7.8 %collective-permute-start.9 = (bf16[128,768]{1,0:T(8,128)(2,1)S(1)}, bf16[128,768]{1,0:T(8,128)(2,1)S(1)}, u32[]{:S(2)}, u32[]{:S(2)}) collective-permute-start(bf16[128,768]{1,0:T(8,128)(2,1)S(1)} %collective-permute-done.8.near_ref), channel_id=1, source_target_pairs={{0,1},{1,0},{2,3},{3,2},{4,5},{5,4},{6,7},{7,6},{8,9},{9,8},{10,11... | collective-permute-start | bytes 589832 | tf_op jit(solution)/shard_map/ppermute | solution.py:35
  10.8 11.4 %collective-permute-start = (bf16[128,384]{1,0:T(8,128)(2,1)S(1)}, bf16[128,384]{1,0:T(8,128)(2,1)S(1)}, u32[]{:S(2)}, u32[]{:S(2)}) collective-permute-start(bf16[128,384]{1,0:T(8,128)(2,1)S(1)} %copy-done.2), channel_id=1, source_target_pairs={{0,16},{4,20},{8,24},{12,28},{16,0},{20,4},{24,8},{28,12},{1,17},{... | collective-permute-start | bytes 294920 | tf_op jit(solution)/shard_map/ppermute | solution.py:35
  14.4 7.9 %collective-permute-start.3 = (bf16[320,128]{1,0:T(8,128)(2,1)S(1)}, bf16[320,128]{1,0:T(8,128)(2,1)S(1)}, u32[]{:S(2)}, u32[]{:S(2)}) collective-permute-start(bf16[320,128]{1,0:T(8,128)(2,1)S(1)} %get-tuple-element.46), channel_id=1, source_target_pairs={{0,4},{4,0},{8,12},{12,8},{16,20},{20,16},{24,28},{28,24},{1,5},{5... | collective-permute-start | bytes 245768 | tf_op jit(solution)/shard_map/ppermute | solution.py:35
  16.0 6.3 %collective-permute-start.4 = (bf16[320,128]{1,0:T(8,128)(2,1)S(1)}, bf16[320,128]{1,0:T(8,128)(2,1)S(1)}, u32[]{:S(2)}, u32[]{:S(2)}) collective-permute-start(bf16[320,128]{1,0:T(8,128)(2,1)S(1)} %get-tuple-element.47), channel_id=1, source_target_pairs={{0,4},{4,0},{8,12},{12,8},{16,20},{20,16},{24,28},{28,24},{1,5},{5... | collective-permute-start | bytes 245768 | tf_op jit(solution)/shard_map/ppermute | solution.py:35
  16.5 5.8 %collective-permute-start.5 = (bf16[320,128]{1,0:T(8,128)(2,1)S(1)}, bf16[320,128]{1,0:T(8,128)(2,1)S(1)}, u32[]{:S(2)}, u32[]{:S(2)}) collective-permute-start(bf16[320,128]{1,0:T(8,128)(2,1)S(1)} %get-tuple-element.48), channel_id=1, source_target_pairs={{0,4},{4,0},{8,12},{12,8},{16,20},{20,16},{24,28},{28,24},{1,5},{5... | collective-permute-start | bytes 245768 | tf_op jit(solution)/shard_map/ppermute | solution.py:35
  18.8 8.6 %collective-permute-start.10 = (bf16[128,384]{1,0:T(8,128)(2,1)S(1)}, bf16[128,384]{1,0:T(8,128)(2,1)S(1)}, u32[]{:S(2)}, u32[]{:S(2)}) collective-permute-start(bf16[128,384]{1,0:T(8,128)(2,1)S(1)} %dattn.1.d_own_ref), channel_id=1, source_target_pairs={{0,16},{4,20},{8,24},{12,28},{16,0},{20,4},{24,8},{28,12},{1,17},{... | collective-permute-start | bytes 294920 | tf_op jit(solution)/shard_map/ppermute | solution.py:35
  23.7 10.1 %collective-permute-start.6 = (bf16[384,128]{1,0:T(8,128)(2,1)S(1)}, bf16[384,128]{1,0:T(8,128)(2,1)S(1)}, u32[]{:S(2)}, u32[]{:S(2)}) collective-permute-start(bf16[384,128]{1,0:T(8,128)(2,1)S(1)} %get-tuple-element.53), channel_id=1, source_target_pairs={{0,16},{4,20},{8,24},{12,28},{16,0},{20,4},{24,8},{28,12},{1,17},{... | collective-permute-start | bytes 294920 | tf_op jit(solution)/shard_map/ppermute | solution.py:35
  27.9 6.5 %copy-start = (bf16[384,3072]{1,0:T(8,128)(2,1)S(1)}, bf16[384,3072]{1,0:T(8,128)(2,1)}, u32[]{:S(2)}) copy-start(bf16[384,3072]{1,0:T(8,128)(2,1)} %w_ref.3) | copy-start | bytes 7077892
  27.9 4.8 %collective-permute-start.11 = (f32[16,256]{1,0:T(8,128)S(1)}, f32[16,256]{1,0:T(8,128)S(1)}, u32[]{:S(2)}, u32[]{:S(2)}) collective-permute-start(f32[16,256]{1,0:T(8,128)S(1)} %get-tuple-element.57.stats_ref), channel_id=1, source_target_pairs={{0,16},{4,20},{8,24},{12,28},{16,0},{20,4},{24,8},{28,12},{1,17},{... | collective-permute-start | bytes 49160 | tf_op jit(solution)/shard_map/ppermute | solution.py:35
  33.8 6.3 %collective-permute-start.17 = (bf16[320,384]{1,0:T(8,128)(2,1)S(1)}, bf16[320,384]{1,0:T(8,128)(2,1)S(1)}, u32[]{:S(2)}, u32[]{:S(2)}) collective-permute-start(bf16[320,384]{1,0:T(8,128)(2,1)S(1)} %get-tuple-element.70), channel_id=1, source_target_pairs={{0,4},{4,0},{8,12},{12,8},{16,20},{20,16},{24,28},{28,24},{1,5},{5... | collective-permute-start | bytes 737288 | tf_op jit(solution)/shard_map/ppermute | solution.py:35
  34.3 6.2 %collective-permute-start.18 = (bf16[320,384]{1,0:T(8,128)(2,1)S(1)}, bf16[320,384]{1,0:T(8,128)(2,1)S(1)}, u32[]{:S(2)}, u32[]{:S(2)}) collective-permute-start(bf16[320,384]{1,0:T(8,128)(2,1)S(1)} %get-tuple-element.71), channel_id=1, source_target_pairs={{0,8},{4,12},{8,0},{12,4},{16,24},{20,28},{24,16},{28,20},{1,9},{5... | collective-permute-start | bytes 737288 | tf_op jit(solution)/shard_map/ppermute | solution.py:35
  34.9 1.4 %collective-permute-start.13 = (bf16[128,384]{1,0:T(8,128)(2,1)S(1)}, bf16[128,384]{1,0:T(8,128)(2,1)S(1)}, u32[]{:S(2)}, u32[]{:S(2)}) collective-permute-start(bf16[128,384]{1,0:T(8,128)(2,1)S(1)} %get-tuple-element.65), channel_id=1, source_target_pairs={{0,1},{1,0},{2,3},{3,2},{4,5},{5,4},{6,7},{7,6},{8,9},{9,8},{10,11... | collective-permute-start | bytes 294920 | tf_op jit(solution)/shard_map/ppermute | solution.py:35
  35.0 1.4 %collective-permute-start.14 = (bf16[128,384]{1,0:T(8,128)(2,1)S(1)}, bf16[128,384]{1,0:T(8,128)(2,1)S(1)}, u32[]{:S(2)}, u32[]{:S(2)}) collective-permute-start(bf16[128,384]{1,0:T(8,128)(2,1)S(1)} %get-tuple-element.66), channel_id=1, source_target_pairs={{0,1},{1,0},{2,3},{3,2},{4,5},{5,4},{6,7},{7,6},{8,9},{9,8},{10,11... | collective-permute-start | bytes 294920 | tf_op jit(solution)/shard_map/ppermute | solution.py:35
  35.5 10.9 %collective-permute-start.12 = (bf16[128,768]{1,0:T(8,128)(2,1)S(1)}, bf16[128,768]{1,0:T(8,128)(2,1)S(1)}, u32[]{:S(2)}, u32[]{:S(2)}) collective-permute-start(bf16[128,768]{1,0:T(8,128)(2,1)S(1)} %get-tuple-element.63), channel_id=1, source_target_pairs={{0,1},{1,0},{2,3},{3,2},{4,5},{5,4},{6,7},{7,6},{8,9},{9,8},{10,11... | collective-permute-start | bytes 589832 | tf_op jit(solution)/shard_map/ppermute | solution.py:35
  36.5 9.9 %collective-permute-start.15 = (bf16[128,768]{1,0:T(8,128)(2,1)S(1)}, bf16[128,768]{1,0:T(8,128)(2,1)S(1)}, u32[]{:S(2)}, u32[]{:S(2)}) collective-permute-start(bf16[128,768]{1,0:T(8,128)(2,1)S(1)} %add_near.1), channel_id=1, source_target_pairs={{0,2},{1,3},{2,0},{3,1},{4,6},{5,7},{6,4},{7,5},{8,10},{9,11},{10,... | collective-permute-start | bytes 589832 | tf_op jit(solution)/shard_map/ppermute | solution.py:35
  36.6 9.8 %collective-permute-start.16 = (bf16[176,384]{1,0:T(8,128)(2,1)S(1)}, bf16[176,384]{1,0:T(8,128)(2,1)S(1)}, u32[]{:S(2)}, u32[]{:S(2)}) collective-permute-start(bf16[176,384]{1,0:T(8,128)(2,1)S(1)} %get-tuple-element.68), channel_id=1, source_target_pairs={{0,16},{4,20},{8,24},{12,28},{16,0},{20,4},{24,8},{28,12},{1,17},{... | collective-permute-start | bytes 405512 | tf_op jit(solution)/shard_map/ppermute | solution.py:35
  40.6 6.3 %collective-permute-start.19 = (bf16[160,384]{1,0:T(8,128)(2,1)S(1)}, bf16[160,384]{1,0:T(8,128)(2,1)S(1)}, u32[]{:S(2)}, u32[]{:S(2)}) collective-permute-start(bf16[160,384]{1,0:T(8,128)(2,1)S(1)} %get-tuple-element.74), channel_id=1, source_target_pairs={{0,8},{4,12},{8,0},{12,4},{16,24},{20,28},{24,16},{28,20},{1,9},{5... | collective-permute-start | bytes 368648 | tf_op jit(solution)/shard_map/ppermute | solution.py:35
  40.6 6.2 %collective-permute-start.20 = (bf16[160,384]{1,0:T(8,128)(2,1)S(1)}, bf16[160,384]{1,0:T(8,128)(2,1)S(1)}, u32[]{:S(2)}, u32[]{:S(2)}) collective-permute-start(bf16[160,384]{1,0:T(8,128)(2,1)S(1)} %get-tuple-element.75), channel_id=1, source_target_pairs={{0,4},{4,0},{8,12},{12,8},{16,20},{20,16},{24,28},{28,24},{1,5},{5... | collective-permute-start | bytes 368648 | tf_op jit(solution)/shard_map/ppermute | solution.py:35

commit v17 on v16

--- a/solution.py
+++ b/solution.py
@@ -336,11 +336,6 @@
     kv0 = load_keys(sec_k, hist_k, sec_v, hist_v)
     kv2 = swap(kv0, "ctx", 2)
     kv1 = swap(kv0, "ctx", 1)
-    kv1, kv2 = lax.optimization_barrier((kv1, kv2))
-    pieces = local_call(
-        split_heads_kernel, "split_heads", 0.1, [shape((2 * keys, HDIM), BF16)] * heads, (kv2,)
-    )
-    kvs = (kv0, kv1, kv2, *(swap(piece, "ctx", 1) for piece in pieces))
     d_own = local_call(
         dattn_kernel,
         "dattn",
@@ -348,6 +343,11 @@
         [shape((rows, width), BF16)],
         (grad_out, grad_core, grad_near, grad_far, weight),
     )[0]
+    kv1, kv2, d_own = lax.optimization_barrier((kv1, kv2, d_own))
+    pieces = local_call(
+        split_heads_kernel, "split_heads", 0.1, [shape((2 * keys, HDIM), BF16)] * heads, (kv2,)
+    )
+    kvs = (kv0, kv1, kv2, *(swap(piece, "ctx", 1) for piece in pieces))
     d_pair = swap(d_own, "ctx", PAIR)
     limits = local_call(
         limits_kernel,

time: 47.9 us -> 47.3 us (0.987)
  waiting for transfers between devices: 14.1 us -> 11.2 us
  starting transfers between devices: 23.3 us -> 25.6 us
    ppermute x21, waiting for transfers between devices: 14.1 us -> 11.2 us  [swap(): return lax.ppermute(block, axis, [(i, i ^ bit) for i in range(count)])]
    ppermute x21, starting transfers between devices: 23.3 us -> 25.6 us  [swap(): return lax.ppermute(block, axis, [(i, i ^ bit) for i in range(count)])]
  transfers between devices with their start and end apart: 21 -> 21, of which waited for: 9 -> 8; matrix products, arithmetic and copies ran while one was open for 0% -> 0% of each run, Pallas kernels for 18% -> 18%
where the time goes in v17:
time: 47.3 us; the launch traced here: 47.1 us
  starting transfers between devices  25.6 us (54%)
  waiting for transfers between devices  11.2 us (24%)
  Pallas kernels  9.4 us (20%)
  between operations  0.84 us (2%)
    ppermute x21, starting transfers between devices, swap(): return lax.ppermute(block, axis, [(i, i ^ bit) for i in range(count)])  25.6 us
    ppermute x21, waiting for transfers between devices, swap(): return lax.ppermute(block, axis, [(i, i ^ bit) for i in range(count)])  11.2 us
    pallas_call x11, Pallas kernels, local_call(): pl.pallas_call(body, name=name, out_shape=out_shapes, in_specs=[pl.BlockS...  6.1 us
    pallas_call x1, Pallas kernels, load_keys(): pl.pallas_call(load_kernel, name='load', out_shape=jax.ShapeDtypeStruct((...  1.67 us
    pallas_call x1, Pallas kernels, load_weight(): pl.pallas_call(load_weight_kernel, name='load_w', out_shape=jax.ShapeDtyp...  1.63 us
  transfers between devices with their start and end apart: 21, of which 8 were waited for; matrix products, arithmetic and copies ran while one was open for 0% of the time, Pallas kernels for 18%

profile of v17, /device:TPU:0, one launch (start us, length us, event | category | flops | bytes accessed | tf_op | source)
XLA Modules:
  0.0 47.1 jit_solution(4717066793282735795)
XLA Ops:
  0.6 3.0 %collective-permute-start.4 = (bf16[128,768]{1,0:T(8,128)(2,1)}, bf16[128,768]{1,0:T(8,128)(2,1)S(1)}, u32[]{:S(2)}, u32[]{:S(2)}) collective-permute-start(bf16[128,768]{1,0:T(8,128)(2,1)} %own_ref.1), channel_id=1, source_target_pairs={{0,2},{1,3},{2,0},{3,1},{4,6},{5,7},{6,4},{7,5},{8,10},{9,11},{10,... | collective-permute-start | bytes 589832 | tf_op jit(solution)/shard_map/ppermute | solution.py:35
  3.6 1.7 %load.1.kv0 = bf16[320,384]{1,0:T(8,128)(2,1)} custom-call(bf16[128,384]{1,0:T(8,128)(2,1)} %k_ref.1, bf16[32,384]{1,0:T(8,128)(2,1)} %hk_ref.1, bf16[128,384]{1,0:T(8,128)(2,1)} %v_ref.1, bf16[32,384]{1,0:T(8,128)(2,1)} %hv_ref.1), custom_call_target="tpu_custom_call" | custom-call | bytes 5904000 | tf_op jit(solution)/shard_map/load/pallas_call | solution.py:74
  5.3 0.0 copy-start.2
  5.3 0.0 copy-start.3
  5.3 1.6 %collective-permute-start.2 = (bf16[320,384]{1,0:T(8,128)(2,1)}, bf16[320,384]{1,0:T(8,128)(2,1)S(1)}, u32[]{:S(2)}, u32[]{:S(2)}) collective-permute-start(bf16[320,384]{1,0:T(8,128)(2,1)} %load.1.kv0), channel_id=1, source_target_pairs={{0,8},{4,12},{8,0},{12,4},{16,24},{20,28},{24,16},{28,20},{1,9},{5... | collective-permute-start | bytes 737288 | tf_op jit(solution)/shard_map/ppermute | solution.py:35
  7.0 1.5 %collective-permute-start.1 = (bf16[320,384]{1,0:T(8,128)(2,1)}, bf16[320,384]{1,0:T(8,128)(2,1)S(1)}, u32[]{:S(2)}, u32[]{:S(2)}) collective-permute-start(bf16[320,384]{1,0:T(8,128)(2,1)} %load.1.kv0), channel_id=1, source_target_pairs={{0,4},{4,0},{8,12},{12,8},{16,20},{20,16},{24,28},{28,24},{1,5},{5... | collective-permute-start | bytes 737288 | tf_op jit(solution)/shard_map/ppermute | solution.py:35
  8.5 0.0 collective-permute-start.3
  8.5 1.6 %load_w.1.w_ref = bf16[384,3072]{1,0:T(8,128)(2,1)S(1)} custom-call(bf16[384,3072]{1,0:T(8,128)(2,1)} %w_ref.3), custom_call_target="tpu_custom_call" | custom-call | bytes 5904000 | tf_op jit(solution)/shard_map/load_w/pallas_call | solution.py:113
  10.1 0.0 copy-start.5
  10.2 0.0 copy-start.4
  10.2 0.0 collective-permute-done.4.near_ref
  10.2 0.6 %collective-permute-start.5 = (bf16[128,768]{1,0:T(8,128)(2,1)S(1)}, bf16[128,768]{1,0:T(8,128)(2,1)S(1)}, u32[]{:S(2)}, u32[]{:S(2)}) collective-permute-start(bf16[128,768]{1,0:T(8,128)(2,1)S(1)} %collective-permute-done.4.near_ref), channel_id=1, source_target_pairs={{0,1},{1,0},{2,3},{3,2},{4,5},{5,4},{6,7},{7,6},{8,9},{9,8},{10,11... | collective-permute-start | bytes 589832 | tf_op jit(solution)/shard_map/ppermute | solution.py:35
  10.8 2.6 %collective-permute-start = (bf16[128,384]{1,0:T(8,128)(2,1)S(1)}, bf16[128,384]{1,0:T(8,128)(2,1)S(1)}, u32[]{:S(2)}, u32[]{:S(2)}) collective-permute-start(bf16[128,384]{1,0:T(8,128)(2,1)S(1)} %copy-done.2), channel_id=1, source_target_pairs={{0,16},{4,20},{8,24},{12,28},{16,0},{20,4},{24,8},{28,12},{1,17},{... | collective-permute-start | bytes 294920 | tf_op jit(solution)/shard_map/ppermute | solution.py:35
  13.4 0.0 collective-permute-done.5.far_ref
  13.4 0.8 %dattn.1.d_own_ref = bf16[128,384]{1,0:T(8,128)(2,1)S(1)} custom-call(bf16[128,768]{1,0:T(8,128)(2,1)S(1)} %copy-done.3, bf16[128,768]{1,0:T(8,128)(2,1)S(1)} %collective-permute-done.3.core_ref, bf16[128,768]{1,0:T(8,128)(2,1)S(1)} %collective-permute-done.4.near_ref, bf16[128,768]{1,0:T(8,128)(2,1)S(1)} %collective-permute-done.5.far_ref, ...), custom_call_target="tpu_custom_call" | custom-call | bytes 2952000 | tf_op jit(solution)/shard_map/dattn/pallas_call | solution.py:44
  14.2 0.1 collective-permute-done.1.kv1
  14.4 1.6 %collective-permute-start.6 = (bf16[320,128]{1,0:T(8,128)(2,1)S(1)}, bf16[320,128]{1,0:T(8,128)(2,1)S(1)}, u32[]{:S(2)}, u32[]{:S(2)}) collective-permute-start(bf16[320,128]{1,0:T(8,128)(2,1)S(1)} %get-tuple-element.49), channel_id=1, source_target_pairs={{0,4},{4,0},{8,12},{12,8},{16,20},{20,16},{24,28},{28,24},{1,5},{5... | collective-permute-start | bytes 245768 | tf_op jit(solution)/shard_map/ppermute | solution.py:35
  16.0 0.5 %collective-permute-start.7 = (bf16[320,128]{1,0:T(8,128)(2,1)S(1)}, bf16[320,128]{1,0:T(8,128)(2,1)S(1)}, u32[]{:S(2)}, u32[]{:S(2)}) collective-permute-start(bf16[320,128]{1,0:T(8,128)(2,1)S(1)} %get-tuple-element.50), channel_id=1, source_target_pairs={{0,4},{4,0},{8,12},{12,8},{16,20},{20,16},{24,28},{28,24},{1,5},{5... | collective-permute-start | bytes 245768 | tf_op jit(solution)/shard_map/ppermute | solution.py:35
  16.5 1.5 %collective-permute-start.8 = (bf16[320,128]{1,0:T(8,128)(2,1)S(1)}, bf16[320,128]{1,0:T(8,128)(2,1)S(1)}, u32[]{:S(2)}, u32[]{:S(2)}) collective-permute-start(bf16[320,128]{1,0:T(8,128)(2,1)S(1)} %get-tuple-element.51), channel_id=1, source_target_pairs={{0,4},{4,0},{8,12},{12,8},{16,20},{20,16},{24,28},{28,24},{1,5},{5... | collective-permute-start | bytes 245768 | tf_op jit(solution)/shard_map/ppermute | solution.py:35
  18.0 2.6 %collective-permute-start.10 = (bf16[128,384]{1,0:T(8,128)(2,1)S(1)}, bf16[128,384]{1,0:T(8,128)(2,1)S(1)}, u32[]{:S(2)}, u32[]{:S(2)}) collective-permute-start(bf16[128,384]{1,0:T(8,128)(2,1)S(1)} %dattn.1.d_own_ref), channel_id=1, source_target_pairs={{0,16},{4,20},{8,24},{12,28},{16,0},{20,4},{24,8},{28,12},{1,17},{... | collective-permute-start | bytes 294920 | tf_op jit(solution)/shard_map/ppermute | solution.py:35
  20.6 0.1 copy.15.levels_ref
  20.7 0.6 %limits.1.limits_ref = s32[8,256]{1,0:T(8,128)S(1)} custom-call(s32[8,2]{1,0:T(8,128)S(1)} %copy.15.levels_ref, s32[8]{0:T(128)S(1)} %copy-done.4), custom_call_target="tpu_custom_call" | custom-call | bytes 2214000 | tf_op jit(solution)/shard_map/limits/pallas_call | solution.py:44
  21.3 0.0 collective-permute-done.6.refs_0_
  21.3 0.7 %collective-permute-done.8.refs_2_ = bf16[320,128]{1,0:T(8,128)(2,1)S(1)} collective-permute-done((bf16[320,128]{1,0:T(8,128)(2,1)S(1)}, bf16[320,128]{1,0:T(8,128)(2,1)S(1)}, u32[]{:S(2)}, u32[]{:S(2)}) %collective-permute-start.8) | collective-permute-done | bytes 81952 | tf_op jit(solution)/shard_map/ppermute | solution.py:35
  22.0 1.0 %scores.1 = (f32[8,256]{1,0:T(8,128)S(1)}, bf16[1920,256]{1,0:T(8,128)(2,1)S(1)}) custom-call(s32[8,256]{1,0:T(8,128)S(1)} %limits.1.limits_ref, bf16[128,384]{1,0:T(8,128)(2,1)S(1)} %copy-done.2, bf16[128,384]{1,0:T(8,128)(2,1)S(1)} %collective-permute-done.q_pair_ref, bf16[320,384]{1,0:T(8,128)(2,1)S(1)} %copy-done.1, ...), custom_call_target="tpu_custom_call" | custom-call | bytes 3321000 | tf_op jit(solution)/shard_map/scores/pallas_call | solution.py:44
  23.0 0.4 attn.1
  23.5 1.9 %collective-permute-start.9 = (bf16[384,128]{1,0:T(8,128)(2,1)S(1)}, bf16[384,128]{1,0:T(8,128)(2,1)S(1)}, u32[]{:S(2)}, u32[]{:S(2)}) collective-permute-start(bf16[384,128]{1,0:T(8,128)(2,1)S(1)} %get-tuple-element.56), channel_id=1, source_target_pairs={{0,16},{4,20},{8,24},{12,28},{16,0},{20,4},{24,8},{28,12},{1,17},{... | collective-permute-start | bytes 294920 | tf_op jit(solution)/shard_map/ppermute | solution.py:35
  25.4 0.4 delta.1
  25.8 0.0 copy-start
  25.8 1.1 %collective-permute-start.11 = (f32[16,256]{1,0:T(8,128)S(1)}, f32[16,256]{1,0:T(8,128)S(1)}, u32[]{:S(2)}, u32[]{:S(2)}) collective-permute-start(f32[16,256]{1,0:T(8,128)S(1)} %get-tuple-element.59.stats_ref), channel_id=1, source_target_pairs={{0,16},{4,20},{8,24},{12,28},{16,0},{20,4},{24,8},{28,12},{1,17},{... | collective-permute-start | bytes 49160 | tf_op jit(solution)/shard_map/ppermute | solution.py:35
  27.0 3.8 %collective-permute-done.11.stats_pair_ref = f32[16,256]{1,0:T(8,128)S(1)} collective-permute-done((f32[16,256]{1,0:T(8,128)S(1)}, f32[16,256]{1,0:T(8,128)S(1)}, u32[]{:S(2)}, u32[]{:S(2)}) %collective-permute-start.11) | collective-permute-done | bytes 16416 | tf_op jit(solution)/shard_map/ppermute | solution.py:35
  30.8 1.1 %backward.1 = (f32[128,384]{1,0:T(8,128)S(1)}, bf16[176,384]{1,0:T(8,128)(2,1)S(1)}, f32[320,384]{1,0:T(8,128)S(1)}, bf16[320,384]{1,0:T(8,128)(2,1)S(1)}, bf16[...) custom-call(bf16[128,384]{1,0:T(8,128)(2,1)S(1)} %copy-done.2, ...), custom_call_target="tpu_custom_call" | custom-call | bytes 4059000 | tf_op jit(solution)/shard_map/backward/pallas_call | solution.py:44
  31.9 1.0 %collective-permute-start.17 = (bf16[320,384]{1,0:T(8,128)(2,1)S(1)}, bf16[320,384]{1,0:T(8,128)(2,1)S(1)}, u32[]{:S(2)}, u32[]{:S(2)}) collective-permute-start(bf16[320,384]{1,0:T(8,128)(2,1)S(1)} %get-tuple-element.72), channel_id=1, source_target_pairs={{0,4},{4,0},{8,12},{12,8},{16,20},{20,16},{24,28},{28,24},{1,5},{5... | collective-permute-start | bytes 737288 | tf_op jit(solution)/shard_map/ppermute | solution.py:35
  33.0 0.4 collective-permute-start.18
  33.4 0.6 %project.1 = (f32[128,768]{1,0:T(8,128)S(1)}, f32[128,768]{1,0:T(8,128)S(1)}, bf16[128,768]{1,0:T(8,128)(2,1)S(1)}, bf16[128,384]{1,0:T(8,128)(2,1)S(1)}, bf16[128,384]{1,0:T(8,128)(2,1)S(1)}) custom-call(f32[384,128]{1,0:T(8,128)S(1)} %get-tuple-element.55.own_ref, bf16[384,128]{1,0:T(8,128)(2,1)S(1)} %collective-permute-done.9.pair_ref, ...), custom_call_target="tpu_custom_call" | custom-call | bytes 2214000 | tf_op jit(solution)/shard_map/project/pallas_call | solution.py:44
  34.0 0.1 collective-permute-start.13
  34.1 0.5 %collective-permute-start.14 = (bf16[128,384]{1,0:T(8,128)(2,1)S(1)}, bf16[128,384]{1,0:T(8,128)(2,1)S(1)}, u32[]{:S(2)}, u32[]{:S(2)}) collective-permute-start(bf16[128,384]{1,0:T(8,128)(2,1)S(1)} %get-tuple-element.68), channel_id=1, source_target_pairs={{0,1},{1,0},{2,3},{3,2},{4,5},{5,4},{6,7},{7,6},{8,9},{9,8},{10,11... | collective-permute-start | bytes 294920 | tf_op jit(solution)/shard_map/ppermute | solution.py:35
  34.6 0.1 collective-permute-start.12
  34.6 0.7 %collective-permute-done.13.left_ref = bf16[128,384]{1,0:T(8,128)(2,1)S(1)} collective-permute-done((bf16[128,384]{1,0:T(8,128)(2,1)S(1)}, bf16[128,384]{1,0:T(8,128)(2,1)S(1)}, u32[]{:S(2)}, u32[]{:S(2)}) %collective-permute-start.13) | collective-permute-done | bytes 98336 | tf_op jit(solution)/shard_map/ppermute | solution.py:35
  35.3 0.2 collective-permute-done.14.right_ref
  35.5 1.3 %collective-permute-start.15 = (bf16[128,768]{1,0:T(8,128)(2,1)S(1)}, bf16[128,768]{1,0:T(8,128)(2,1)S(1)}, u32[]{:S(2)}, u32[]{:S(2)}) collective-permute-start(bf16[128,768]{1,0:T(8,128)(2,1)S(1)} %add_near.1), channel_id=1, source_target_pairs={{0,2},{1,3},{2,0},{3,1},{4,6},{5,7},{6,4},{7,5},{8,10},{9,11},{10,... | collective-permute-start | bytes 589832 | tf_op jit(solution)/shard_map/ppermute | solution.py:35
  36.9 1.8 %collective-permute-start.16 = (bf16[176,384]{1,0:T(8,128)(2,1)S(1)}, bf16[176,384]{1,0:T(8,128)(2,1)S(1)}, u32[]{:S(2)}, u32[]{:S(2)}) collective-permute-start(bf16[176,384]{1,0:T(8,128)(2,1)S(1)} %get-tuple-element.70), channel_id=1, source_target_pairs={{0,16},{4,20},{8,24},{12,28},{16,0},{20,4},{24,8},{28,12},{1,17},{... | collective-permute-start | bytes 405512 | tf_op jit(solution)/shard_map/ppermute | solution.py:35
  38.7 0.1 collective-permute-done.17.got_k_ref
  38.8 0.3 collective-permute-done.18.got_v_ref
  39.2 0.5 collective-permute-start.19
  39.7 1.3 %collective-permute-start.20 = (bf16[160,384]{1,0:T(8,128)(2,1)S(1)}, bf16[160,384]{1,0:T(8,128)(2,1)S(1)}, u32[]{:S(2)}, u32[]{:S(2)}) collective-permute-start(bf16[160,384]{1,0:T(8,128)(2,1)S(1)} %get-tuple-element.77), channel_id=1, source_target_pairs={{0,4},{4,0},{8,12},{12,8},{16,20},{20,16},{24,28},{28,24},{1,5},{5... | collective-permute-start | bytes 368648 | tf_op jit(solution)/shard_map/ppermute | solution.py:35
  41.0 5.2 %collective-permute-done.16.dq_pair_ref = bf16[176,384]{1,0:T(8,128)(2,1)S(1)} collective-permute-done((bf16[176,384]{1,0:T(8,128)(2,1)S(1)}, bf16[176,384]{1,0:T(8,128)(2,1)S(1)}, u32[]{:S(2)}, u32[]{:S(2)}) %collective-permute-start.16) | collective-permute-done | bytes 135200 | tf_op jit(solution)/shard_map/ppermute | solution.py:35
  46.2 0.9 %finish.1 = (bf16[128,384]{1,0:T(8,128)(2,1)}, bf16[128,384]{1,0:T(8,128)(2,1)}, bf16[128,384]{1,0:T(8,128)(2,1)}, bf16[32,384]{1,0:T(8,128)(2,1)}, bf16[32,384]{1,0:T(8,128)(2,1)}, /*index=5*/bf16[128,768]{1,0:T(8,128)(2,1)}) custom-call(f32[128,768]{1,0:T(8,128)S(1)} %get-tuple-element.64.keep_ref, bf16[128,768]{1,0:T(8,128)(2,1)S(1)} %collective-permute-done.12.core_ref, ...), custom_call_target="tpu_custom_call" | custom-call | bytes 3321000 | tf_op jit(solution)/shard_map/finish/pallas_call | solution.py:44
  (20 shorter events, 0.2 us)
Async XLA Ops:
  0.6 9.5 %collective-permute-start.4 = (bf16[128,768]{1,0:T(8,128)(2,1)}, bf16[128,768]{1,0:T(8,128)(2,1)S(1)}, u32[]{:S(2)}, u32[]{:S(2)}) collective-permute-start(bf16[128,768]{1,0:T(8,128)(2,1)} %own_ref.1), channel_id=1, source_target_pairs={{0,2},{1,3},{2,0},{3,1},{4,6},{5,7},{6,4},{7,5},{8,10},{9,11},{10,... | collective-permute-start | bytes 589832 | tf_op jit(solution)/shard_map/ppermute | solution.py:35
  5.3 5.4 %copy-start.2 = (bf16[128,384]{1,0:T(8,128)(2,1)S(1)}, bf16[128,384]{1,0:T(8,128)(2,1)}, u32[]{:S(2)}) copy-start(bf16[128,384]{1,0:T(8,128)(2,1)} %q_own_ref.3) | copy-start | bytes 294916
  5.3 8.0 %copy-start.3 = (bf16[128,768]{1,0:T(8,128)(2,1)S(1)}, bf16[128,768]{1,0:T(8,128)(2,1)}, u32[]{:S(2)}) copy-start(bf16[128,768]{1,0:T(8,128)(2,1)} %own_ref.1) | copy-start | bytes 589828
  5.3 8.9 %collective-permute-start.2 = (bf16[320,384]{1,0:T(8,128)(2,1)}, bf16[320,384]{1,0:T(8,128)(2,1)S(1)}, u32[]{:S(2)}, u32[]{:S(2)}) collective-permute-start(bf16[320,384]{1,0:T(8,128)(2,1)} %load.1.kv0), channel_id=1, source_target_pairs={{0,8},{4,12},{8,0},{12,4},{16,24},{20,28},{24,16},{28,20},{1,9},{5... | collective-permute-start | bytes 737288 | tf_op jit(solution)/shard_map/ppermute | solution.py:35
  7.0 7.3 %collective-permute-start.1 = (bf16[320,384]{1,0:T(8,128)(2,1)}, bf16[320,384]{1,0:T(8,128)(2,1)S(1)}, u32[]{:S(2)}, u32[]{:S(2)}) collective-permute-start(bf16[320,384]{1,0:T(8,128)(2,1)} %load.1.kv0), channel_id=1, source_target_pairs={{0,4},{4,0},{8,12},{12,8},{16,20},{20,16},{24,28},{28,24},{1,5},{5... | collective-permute-start | bytes 737288 | tf_op jit(solution)/shard_map/ppermute | solution.py:35
  8.5 4.9 %collective-permute-start.3 = (bf16[128,768]{1,0:T(8,128)(2,1)}, bf16[128,768]{1,0:T(8,128)(2,1)S(1)}, u32[]{:S(2)}, u32[]{:S(2)}) collective-permute-start(bf16[128,768]{1,0:T(8,128)(2,1)} %own_ref.1), channel_id=1, source_target_pairs={{0,1},{1,0},{2,3},{3,2},{4,5},{5,4},{6,7},{7,6},{8,9},{9,8},{10,11... | collective-permute-start | bytes 589832 | tf_op jit(solution)/shard_map/ppermute | solution.py:35
  10.1 10.4 %copy-start.5 = (s32[8,2]{0,1:T(2,128)S(1)}, s32[8,2]{0,1:T(2,128)}, u32[]{:S(2)}) copy-start(s32[8,2]{0,1:T(2,128)} %param.14) | copy-start | bytes 196
  10.2 10.5 %copy-start.4 = (s32[8]{0:T(128)S(1)}, s32[8]{0:T(128)}, u32[]{:S(2)}) copy-start(s32[8]{0:T(128)} %counts_ref.1) | copy-start | bytes 100
  10.2 11.9 %copy-start.1 = (bf16[320,384]{1,0:T(8,128)(2,1)S(1)}, bf16[320,384]{1,0:T(8,128)(2,1)}, u32[]{:S(2)}) copy-start(bf16[320,384]{1,0:T(8,128)(2,1)} %load.1.kv0) | copy-start | bytes 737284
  10.2 3.2 %collective-permute-start.5 = (bf16[128,768]{1,0:T(8,128)(2,1)S(1)}, bf16[128,768]{1,0:T(8,128)(2,1)S(1)}, u32[]{:S(2)}, u32[]{:S(2)}) collective-permute-start(bf16[128,768]{1,0:T(8,128)(2,1)S(1)} %collective-permute-done.4.near_ref), channel_id=1, source_target_pairs={{0,1},{1,0},{2,3},{3,2},{4,5},{5,4},{6,7},{7,6},{8,9},{9,8},{10,11... | collective-permute-start | bytes 589832 | tf_op jit(solution)/shard_map/ppermute | solution.py:35
  10.8 10.5 %collective-permute-start = (bf16[128,384]{1,0:T(8,128)(2,1)S(1)}, bf16[128,384]{1,0:T(8,128)(2,1)S(1)}, u32[]{:S(2)}, u32[]{:S(2)}) collective-permute-start(bf16[128,384]{1,0:T(8,128)(2,1)S(1)} %copy-done.2), channel_id=1, source_target_pairs={{0,16},{4,20},{8,24},{12,28},{16,0},{20,4},{24,8},{28,12},{1,17},{... | collective-permute-start | bytes 294920 | tf_op jit(solution)/shard_map/ppermute | solution.py:35
  14.4 6.9 %collective-permute-start.6 = (bf16[320,128]{1,0:T(8,128)(2,1)S(1)}, bf16[320,128]{1,0:T(8,128)(2,1)S(1)}, u32[]{:S(2)}, u32[]{:S(2)}) collective-permute-start(bf16[320,128]{1,0:T(8,128)(2,1)S(1)} %get-tuple-element.49), channel_id=1, source_target_pairs={{0,4},{4,0},{8,12},{12,8},{16,20},{20,16},{24,28},{28,24},{1,5},{5... | collective-permute-start | bytes 245768 | tf_op jit(solution)/shard_map/ppermute | solution.py:35
  16.0 5.4 %collective-permute-start.7 = (bf16[320,128]{1,0:T(8,128)(2,1)S(1)}, bf16[320,128]{1,0:T(8,128)(2,1)S(1)}, u32[]{:S(2)}, u32[]{:S(2)}) collective-permute-start(bf16[320,128]{1,0:T(8,128)(2,1)S(1)} %get-tuple-element.50), channel_id=1, source_target_pairs={{0,4},{4,0},{8,12},{12,8},{16,20},{20,16},{24,28},{28,24},{1,5},{5... | collective-permute-start | bytes 245768 | tf_op jit(solution)/shard_map/ppermute | solution.py:35
  16.5 5.6 %collective-permute-start.8 = (bf16[320,128]{1,0:T(8,128)(2,1)S(1)}, bf16[320,128]{1,0:T(8,128)(2,1)S(1)}, u32[]{:S(2)}, u32[]{:S(2)}) collective-permute-start(bf16[320,128]{1,0:T(8,128)(2,1)S(1)} %get-tuple-element.51), channel_id=1, source_target_pairs={{0,4},{4,0},{8,12},{12,8},{16,20},{20,16},{24,28},{28,24},{1,5},{5... | collective-permute-start | bytes 245768 | tf_op jit(solution)/shard_map/ppermute | solution.py:35
  18.0 7.4 %collective-permute-start.10 = (bf16[128,384]{1,0:T(8,128)(2,1)S(1)}, bf16[128,384]{1,0:T(8,128)(2,1)S(1)}, u32[]{:S(2)}, u32[]{:S(2)}) collective-permute-start(bf16[128,384]{1,0:T(8,128)(2,1)S(1)} %dattn.1.d_own_ref), channel_id=1, source_target_pairs={{0,16},{4,20},{8,24},{12,28},{16,0},{20,4},{24,8},{28,12},{1,17},{... | collective-permute-start | bytes 294920 | tf_op jit(solution)/shard_map/ppermute | solution.py:35
  23.5 8.5 %collective-permute-start.9 = (bf16[384,128]{1,0:T(8,128)(2,1)S(1)}, bf16[384,128]{1,0:T(8,128)(2,1)S(1)}, u32[]{:S(2)}, u32[]{:S(2)}) collective-permute-start(bf16[384,128]{1,0:T(8,128)(2,1)S(1)} %get-tuple-element.56), channel_id=1, source_target_pairs={{0,16},{4,20},{8,24},{12,28},{16,0},{20,4},{24,8},{28,12},{1,17},{... | collective-permute-start | bytes 294920 | tf_op jit(solution)/shard_map/ppermute | solution.py:35
  25.8 7.5 %copy-start = (bf16[384,3072]{1,0:T(8,128)(2,1)S(1)}, bf16[384,3072]{1,0:T(8,128)(2,1)}, u32[]{:S(2)}) copy-start(bf16[384,3072]{1,0:T(8,128)(2,1)} %w_ref.3) | copy-start | bytes 7077892
  25.8 4.9 %collective-permute-start.11 = (f32[16,256]{1,0:T(8,128)S(1)}, f32[16,256]{1,0:T(8,128)S(1)}, u32[]{:S(2)}, u32[]{:S(2)}) collective-permute-start(f32[16,256]{1,0:T(8,128)S(1)} %get-tuple-element.59.stats_ref), channel_id=1, source_target_pairs={{0,16},{4,20},{8,24},{12,28},{16,0},{20,4},{24,8},{28,12},{1,17},{... | collective-permute-start | bytes 49160 | tf_op jit(solution)/shard_map/ppermute | solution.py:35
  31.9 6.9 %collective-permute-start.17 = (bf16[320,384]{1,0:T(8,128)(2,1)S(1)}, bf16[320,384]{1,0:T(8,128)(2,1)S(1)}, u32[]{:S(2)}, u32[]{:S(2)}) collective-permute-start(bf16[320,384]{1,0:T(8,128)(2,1)S(1)} %get-tuple-element.72), channel_id=1, source_target_pairs={{0,4},{4,0},{8,12},{12,8},{16,20},{20,16},{24,28},{28,24},{1,5},{5... | collective-permute-start | bytes 737288 | tf_op jit(solution)/shard_map/ppermute | solution.py:35
  33.0 6.2 %collective-permute-start.18 = (bf16[320,384]{1,0:T(8,128)(2,1)S(1)}, bf16[320,384]{1,0:T(8,128)(2,1)S(1)}, u32[]{:S(2)}, u32[]{:S(2)}) collective-permute-start(bf16[320,384]{1,0:T(8,128)(2,1)S(1)} %get-tuple-element.73), channel_id=1, source_target_pairs={{0,8},{4,12},{8,0},{12,4},{16,24},{20,28},{24,16},{28,20},{1,9},{5... | collective-permute-start | bytes 737288 | tf_op jit(solution)/shard_map/ppermute | solution.py:35
  34.0 1.4 %collective-permute-start.13 = (bf16[128,384]{1,0:T(8,128)(2,1)S(1)}, bf16[128,384]{1,0:T(8,128)(2,1)S(1)}, u32[]{:S(2)}, u32[]{:S(2)}) collective-permute-start(bf16[128,384]{1,0:T(8,128)(2,1)S(1)} %get-tuple-element.67), channel_id=1, source_target_pairs={{0,1},{1,0},{2,3},{3,2},{4,5},{5,4},{6,7},{7,6},{8,9},{9,8},{10,11... | collective-permute-start | bytes 294920 | tf_op jit(solution)/shard_map/ppermute | solution.py:35
  34.1 1.4 %collective-permute-start.14 = (bf16[128,384]{1,0:T(8,128)(2,1)S(1)}, bf16[128,384]{1,0:T(8,128)(2,1)S(1)}, u32[]{:S(2)}, u32[]{:S(2)}) collective-permute-start(bf16[128,384]{1,0:T(8,128)(2,1)S(1)} %get-tuple-element.68), channel_id=1, source_target_pairs={{0,1},{1,0},{2,3},{3,2},{4,5},{5,4},{6,7},{7,6},{8,9},{9,8},{10,11... | collective-permute-start | bytes 294920 | tf_op jit(solution)/shard_map/ppermute | solution.py:35
  34.6 11.7 %collective-permute-start.12 = (bf16[128,768]{1,0:T(8,128)(2,1)S(1)}, bf16[128,768]{1,0:T(8,128)(2,1)S(1)}, u32[]{:S(2)}, u32[]{:S(2)}) collective-permute-start(bf16[128,768]{1,0:T(8,128)(2,1)S(1)} %get-tuple-element.65), channel_id=1, source_target_pairs={{0,1},{1,0},{2,3},{3,2},{4,5},{5,4},{6,7},{7,6},{8,9},{9,8},{10,11... | collective-permute-start | bytes 589832 | tf_op jit(solution)/shard_map/ppermute | solution.py:35
  35.5 10.7 %collective-permute-start.15 = (bf16[128,768]{1,0:T(8,128)(2,1)S(1)}, bf16[128,768]{1,0:T(8,128)(2,1)S(1)}, u32[]{:S(2)}, u32[]{:S(2)}) collective-permute-start(bf16[128,768]{1,0:T(8,128)(2,1)S(1)} %add_near.1), channel_id=1, source_target_pairs={{0,2},{1,3},{2,0},{3,1},{4,6},{5,7},{6,4},{7,5},{8,10},{9,11},{10,... | collective-permute-start | bytes 589832 | tf_op jit(solution)/shard_map/ppermute | solution.py:35
  36.9 9.3 %collective-permute-start.16 = (bf16[176,384]{1,0:T(8,128)(2,1)S(1)}, bf16[176,384]{1,0:T(8,128)(2,1)S(1)}, u32[]{:S(2)}, u32[]{:S(2)}) collective-permute-start(bf16[176,384]{1,0:T(8,128)(2,1)S(1)} %get-tuple-element.70), channel_id=1, source_target_pairs={{0,16},{4,20},{8,24},{12,28},{16,0},{20,4},{24,8},{28,12},{1,17},{... | collective-permute-start | bytes 405512 | tf_op jit(solution)/shard_map/ppermute | solution.py:35
  39.2 7.0 %collective-permute-start.19 = (bf16[160,384]{1,0:T(8,128)(2,1)S(1)}, bf16[160,384]{1,0:T(8,128)(2,1)S(1)}, u32[]{:S(2)}, u32[]{:S(2)}) collective-permute-start(bf16[160,384]{1,0:T(8,128)(2,1)S(1)} %get-tuple-element.76), channel_id=1, source_target_pairs={{0,8},{4,12},{8,0},{12,4},{16,24},{20,28},{24,16},{28,20},{1,9},{5... | collective-permute-start | bytes 368648 | tf_op jit(solution)/shard_map/ppermute | solution.py:35
  39.7 6.6 %collective-permute-start.20 = (bf16[160,384]{1,0:T(8,128)(2,1)S(1)}, bf16[160,384]{1,0:T(8,128)(2,1)S(1)}, u32[]{:S(2)}, u32[]{:S(2)}) collective-permute-start(bf16[160,384]{1,0:T(8,128)(2,1)S(1)} %get-tuple-element.77), channel_id=1, source_target_pairs={{0,4},{4,0},{8,12},{12,8},{16,20},{20,16},{24,28},{28,24},{1,5},{5... | collective-permute-start | bytes 368648 | tf_op jit(solution)/shard_map/ppermute | solution.py:35

commit v18 on v17

--- a/solution.py
+++ b/solution.py
@@ -258,11 +258,18 @@
     kv0, kv1, kv2, *refs,
 ):
     rows = q_own_ref.shape[0]
-    *far, dq_own_ref, dq_pair_ref, dkv_ref, send_k_ref, send_v_ref, near_k_ref, near_v_ref = refs
+    *far, dq_own_ref, dq_pair_ref, dkv_ref, send_y_ref, send_z_ref, near_y_ref, near_z_ref = refs
     keys = kv0.shape[0] // 2
-    dq_pair_ref[rows:] = jnp.zeros((dq_pair_ref.shape[0] - rows, dq_pair_ref.shape[1]), BF16)
-    key_parts = (dkv_ref.at[:keys], send_k_ref.at[:keys], near_k_ref, send_k_ref.at[keys:])
-    value_parts = (dkv_ref.at[keys:], near_v_ref, send_v_ref.at[:keys], send_v_ref.at[keys:])
+    wide = near_y_ref.shape[0]
+    key_parts = (
+        dkv_ref.at[:keys], send_y_ref.at[:keys], near_y_ref.at[:keys], send_y_ref.at[wide : wide + keys]
+    )
+    value_parts = (
+        dkv_ref.at[keys : keys + rows], near_z_ref, send_z_ref.at[:rows], send_z_ref.at[rows:]
+    )
+    hist_parts = (
+        dkv_ref.at[keys + rows :], send_y_ref.at[keys:wide], near_y_ref.at[keys:], send_y_ref.at[wide + keys :]
+    )
 
     def swapped(row):
         return jnp.concatenate([row[:, rows:], row[:, :rows]], axis=1)
@@ -282,25 +289,33 @@
             probs = (probs_ref[begin : begin + keys].astype(F32) * weight).astype(BF16)
             dprobs = dprobs_ref[begin : begin + keys]
             dscores = (probs.astype(F32) * (dprobs - delta)).astype(BF16)
-            key_part, value_part = key_parts[step], value_parts[step]
             grad_key = contract(dscores, query, 1, 0) * SCALE
-            key_part[:, features] = grad_key.astype(key_part.dtype)
-            value_part[:, features] = contract(probs, dattn, 1, 0).astype(value_part.dtype)
-            part = contract(dscores, key, 0, 0)
-            dquery = part if dquery is None else dquery + part
+            grad_value = contract(probs, dattn, 1, 0)
+            parts = (grad_key, grad_value[:rows], grad_value[rows:])
+            for part, targets in zip(parts, (key_parts, value_parts, hist_parts)):
+                targets[step][:, features] = part.astype(targets[step].dtype)
+            grad_query = contract(dscores, key, 0, 0)
+            dquery = grad_query if dquery is None else dquery + grad_query
         dq_own_ref[:, features] = dquery[:rows] * SCALE
-        dq_pair_ref[:rows, features] = (dquery[rows:] * SCALE).astype(BF16)
-
-
-def pass_on_kernel(near_k_ref, near_v_ref, got_k_ref, got_v_ref, k_ref, v_ref):
-    keys = near_k_ref.shape[0]
-    k_ref[...] = (near_k_ref[...] + got_k_ref[keys:].astype(F32)).astype(BF16)
-    v_ref[...] = (near_v_ref[...] + got_v_ref[keys:].astype(F32)).astype(BF16)
+        dq_pair_ref[:, features] = (dquery[rows:] * SCALE).astype(BF16)
+
+
+def pass_on_kernel(
+    near_y_ref, near_z_ref, got_y_ref, got_z_ref, keep_ref, core_ref,
+    key_ref, hist_ref, value_ref, sum_ref,
+):
+    rows = key_ref.shape[0]
+    wide = near_y_ref.shape[0]
+    total_y = near_y_ref[...] + got_y_ref[wide:].astype(F32)
+    key_ref[...] = total_y[:rows].astype(BF16)
+    hist_ref[...] = total_y[rows:].astype(BF16)
+    value_ref[...] = (near_z_ref[...] + got_z_ref[rows:].astype(F32)).astype(BF16)
+    sum_ref[...] = keep_ref[...] + core_ref[...].astype(F32)
 
 
 def finish_kernel(
-    keep_ref, core_ref, near_ref, dq_ref, dq_pair_ref,
-    dkv_ref, got_k_ref, got_v_ref, rest_k_ref, rest_v_ref,
+    keep_ref, near_ref, dq_ref, dq_pair_ref,
+    dkv_ref, got_y_ref, got_z_ref, rest_k_ref, rest_h_ref, rest_v_ref,
     q_out, k_out, v_out, hk_out, hv_out, out_ref,
 ):
     rows, capacity = k_out.shape[0], hk_out.shape[0]
@@ -311,12 +326,14 @@
             first = first + other.astype(F32)
         return first.astype(BF16)
 
-    q_out[...] = total(dq_ref[...], dq_pair_ref[:rows])
-    k_out[...] = total(dkv_ref[:rows], got_k_ref[:rows], rest_k_ref[:rows])
-    hk_out[...] = total(dkv_ref[rows:keys], got_k_ref[rows:keys], rest_k_ref[rows:])
-    v_out[...] = total(dkv_ref[keys : keys + rows], got_v_ref[:rows], rest_v_ref[:rows])
-    hv_out[...] = total(dkv_ref[keys + rows :], got_v_ref[rows:keys], rest_v_ref[rows:])
-    out_ref[...] = total(keep_ref[...], core_ref[...], near_ref[...])
+    q_out[...] = total(dq_ref[...], dq_pair_ref[...])
+    k_out[...] = total(dkv_ref[:rows], got_y_ref[:rows], rest_k_ref[...])
+    hk_out[...] = total(dkv_ref[rows:keys], got_y_ref[rows:keys], rest_h_ref[:capacity])
+    v_out[...] = total(dkv_ref[keys : keys + rows], got_z_ref[:rows], rest_v_ref[...])
+    hv_out[...] = total(
+        dkv_ref[keys + rows :], got_y_ref[keys : keys + capacity], rest_h_ref[capacity:]
+    )
+    out_ref[...] = total(keep_ref[...], near_ref[...])
 
 
 def blocked(sec_q, sec_k, sec_v, hist_k, hist_v, frame_levels, frame_counts, w_out, grad_out):
@@ -380,28 +397,20 @@
         (lse, probs, d_own, d_pair, *kvs),
     )
     stats_pair = swap(stats, "ctx", PAIR)
-    dq_own, dq_pair, dkv_own, send_k, send_v, near_k, near_v = local_call(
+    wide = keys + capacity
+    dq_own, dq_pair, dkv_own, send_y, send_z, near_y, near_z = local_call(
         backward_kernel,
         "backward",
         1.1,
-        [shape((rows, width), F32), shape((keys + 16, width), BF16), shape((2 * keys, width), F32)]
-        + [shape((2 * keys, width), BF16)] * 2
-        + [shape((keys, width), F32)] * 2,
+        [shape((rows, width), F32), shape((rows, width), BF16), shape((2 * keys, width), F32)]
+        + [shape((2 * wide, width), BF16), shape((2 * rows, width), BF16)]
+        + [shape((wide, width), F32), shape((rows, width), F32)],
         (sec_q, q_pair, d_own, d_pair, stats, stats_pair, probs, dprobs, *kvs),
     )
     attn_got = swap(attn_pair, "ctx", PAIR)
-    attn_got, send_k, send_v = lax.optimization_barrier((attn_got, send_k, send_v))
-    got_k = swap(send_k, "ctx", 1)
-    got_v = swap(send_v, "ctx", 2)
-    rest_k, rest_v = local_call(
-        pass_on_kernel,
-        "pass_on",
-        0.1,
-        [shape((keys, width), BF16)] * 2,
-        (near_k, near_v, got_k, got_v),
-    )
-    rest_k = swap(rest_k, "ctx", 2)
-    rest_v = swap(rest_v, "ctx", 1)
+    attn_got, send_y, send_z = lax.optimization_barrier((attn_got, send_y, send_z))
+    got_y = swap(send_y, "ctx", 1)
+    got_z = swap(send_z, "ctx", 2)
     half = share // 2
     out_keep, out_next, out_core, far_left, far_right = local_call(
         project_kernel,
@@ -426,6 +435,17 @@
     )
     dq_got = swap(dq_pair, "ctx", PAIR)
     out_core = swap(out_core, "head", 1)
+    rest_k, rest_h, rest_v, out_keep = local_call(
+        pass_on_kernel,
+        "pass_on",
+        0.1,
+        [shape((size, width), BF16) for size in (rows, 2 * capacity, rows)]
+        + [shape((rows, share), F32)],
+        (near_y, near_z, got_y, got_z, out_keep, out_core),
+    )
+    rest_k = swap(rest_k, "ctx", 2)
+    rest_h = swap(rest_h, "ctx", 2)
+    rest_v = swap(rest_v, "ctx", 1)
     grad_q, grad_k, grad_v, grad_hk, grad_hv, out = local_call(
         finish_kernel,
         "finish",
@@ -434,8 +454,8 @@
         + [shape((capacity, width), BF16)] * 2
         + [shape((rows, share), BF16)],
         (
-            out_keep, out_core, out_near, dq_own, dq_got,
-            dkv_own, got_k, got_v, rest_k, rest_v,
+            out_keep, out_near, dq_own, dq_got,
+            dkv_own, got_y, got_z, rest_k, rest_h, rest_v,
         ),
     )
     return out, grad_q, grad_k, grad_v, grad_hk, grad_hv

time: 47.3 us -> 46.9 us (level)
  waiting for transfers between devices: 11.2 us -> 10.1 us
  starting transfers between devices: 25.6 us -> 26.2 us
    ppermute x21 -> x22, waiting for transfers between devices: 11.2 us -> 10.1 us  [swap(): return lax.ppermute(block, axis, [(i, i ^ bit) for i in range(count)])]
    ppermute x21 -> x22, starting transfers between devices: 25.6 us -> 26.2 us  [swap(): return lax.ppermute(block, axis, [(i, i ^ bit) for i in range(count)])]
  transfers between devices with their start and end apart: 21 -> 22, of which waited for: 8 -> 8; matrix products, arithmetic and copies ran while one was open for 0% -> 0% of each run, Pallas kernels for 18% -> 18%
where the time goes in v18:
time: 46.9 us; the launch traced here: 46.7 us
  starting transfers between devices  26.2 us (56%)
  waiting for transfers between devices  10.1 us (22%)
  Pallas kernels  9.38 us (20%)
  between operations  0.84 us (2%)
    ppermute x22, starting transfers between devices, swap(): return lax.ppermute(block, axis, [(i, i ^ bit) for i in range(count)])  26.2 us
    ppermute x22, waiting for transfers between devices, swap(): return lax.ppermute(block, axis, [(i, i ^ bit) for i in range(count)])  10.1 us
    pallas_call x11, Pallas kernels, local_call(): pl.pallas_call(body, name=name, out_shape=out_shapes, in_specs=[pl.BlockS...  6.09 us
    pallas_call x1, Pallas kernels, load_keys(): pl.pallas_call(load_kernel, name='load', out_shape=jax.ShapeDtypeStruct((...  1.66 us
    pallas_call x1, Pallas kernels, load_weight(): pl.pallas_call(load_weight_kernel, name='load_w', out_shape=jax.ShapeDtyp...  1.63 us
  transfers between devices with their start and end apart: 22, of which 8 were waited for; matrix products, arithmetic and copies ran while one was open for 0% of the time, Pallas kernels for 18%

profile of v18, /device:TPU:0, one launch (start us, length us, event | category | flops | bytes accessed | tf_op | source)
XLA Modules:
  0.0 46.7 jit_solution(15870161610045067854)
XLA Ops:
  0.6 3.0 %collective-permute-start.4 = (bf16[128,768]{1,0:T(8,128)(2,1)}, bf16[128,768]{1,0:T(8,128)(2,1)S(1)}, u32[]{:S(2)}, u32[]{:S(2)}) collective-permute-start(bf16[128,768]{1,0:T(8,128)(2,1)} %own_ref.1), channel_id=1, source_target_pairs={{0,2},{1,3},{2,0},{3,1},{4,6},{5,7},{6,4},{7,5},{8,10},{9,11},{10,... | collective-permute-start | bytes 589832 | tf_op jit(solution)/shard_map/ppermute | solution.py:35
  3.6 1.7 %load.1.kv0 = bf16[320,384]{1,0:T(8,128)(2,1)} custom-call(bf16[128,384]{1,0:T(8,128)(2,1)} %k_ref.1, bf16[32,384]{1,0:T(8,128)(2,1)} %hk_ref.1, bf16[128,384]{1,0:T(8,128)(2,1)} %v_ref.1, bf16[32,384]{1,0:T(8,128)(2,1)} %hv_ref.1), custom_call_target="tpu_custom_call" | custom-call | bytes 5904000 | tf_op jit(solution)/shard_map/load/pallas_call | solution.py:74
  5.3 0.0 copy-start.2
  5.3 0.0 copy-start.3
  5.3 1.6 %collective-permute-start.2 = (bf16[320,384]{1,0:T(8,128)(2,1)}, bf16[320,384]{1,0:T(8,128)(2,1)S(1)}, u32[]{:S(2)}, u32[]{:S(2)}) collective-permute-start(bf16[320,384]{1,0:T(8,128)(2,1)} %load.1.kv0), channel_id=1, source_target_pairs={{0,8},{4,12},{8,0},{12,4},{16,24},{20,28},{24,16},{28,20},{1,9},{5... | collective-permute-start | bytes 737288 | tf_op jit(solution)/shard_map/ppermute | solution.py:35
  7.0 1.5 %collective-permute-start.1 = (bf16[320,384]{1,0:T(8,128)(2,1)}, bf16[320,384]{1,0:T(8,128)(2,1)S(1)}, u32[]{:S(2)}, u32[]{:S(2)}) collective-permute-start(bf16[320,384]{1,0:T(8,128)(2,1)} %load.1.kv0), channel_id=1, source_target_pairs={{0,4},{4,0},{8,12},{12,8},{16,20},{20,16},{24,28},{28,24},{1,5},{5... | collective-permute-start | bytes 737288 | tf_op jit(solution)/shard_map/ppermute | solution.py:35
  8.5 1.6 %load_w.1.w_ref = bf16[384,3072]{1,0:T(8,128)(2,1)S(1)} custom-call(bf16[384,3072]{1,0:T(8,128)(2,1)} %w_ref.3), custom_call_target="tpu_custom_call" | custom-call | bytes 5904000 | tf_op jit(solution)/shard_map/load_w/pallas_call | solution.py:113
  10.1 0.0 copy-start.5
  10.1 0.0 copy-start.4
  10.2 0.0 collective-permute-done.4.near_ref
  10.2 0.6 %collective-permute-start.5 = (bf16[128,768]{1,0:T(8,128)(2,1)S(1)}, bf16[128,768]{1,0:T(8,128)(2,1)S(1)}, u32[]{:S(2)}, u32[]{:S(2)}) collective-permute-start(bf16[128,768]{1,0:T(8,128)(2,1)S(1)} %collective-permute-done.4.near_ref), channel_id=1, source_target_pairs={{0,1},{1,0},{2,3},{3,2},{4,5},{5,4},{6,7},{7,6},{8,9},{9,8},{10,11... | collective-permute-start | bytes 589832 | tf_op jit(solution)/shard_map/ppermute | solution.py:35
  10.8 2.6 %collective-permute-start = (bf16[128,384]{1,0:T(8,128)(2,1)S(1)}, bf16[128,384]{1,0:T(8,128)(2,1)S(1)}, u32[]{:S(2)}, u32[]{:S(2)}) collective-permute-start(bf16[128,384]{1,0:T(8,128)(2,1)S(1)} %copy-done.2), channel_id=1, source_target_pairs={{0,16},{4,20},{8,24},{12,28},{16,0},{20,4},{24,8},{28,12},{1,17},{... | collective-permute-start | bytes 294920 | tf_op jit(solution)/shard_map/ppermute | solution.py:35
  13.3 0.0 collective-permute-done.3.core_ref
  13.4 0.8 %dattn.1.d_own_ref = bf16[128,384]{1,0:T(8,128)(2,1)S(1)} custom-call(bf16[128,768]{1,0:T(8,128)(2,1)S(1)} %copy-done.3, bf16[128,768]{1,0:T(8,128)(2,1)S(1)} %collective-permute-done.3.core_ref, bf16[128,768]{1,0:T(8,128)(2,1)S(1)} %collective-permute-done.4.near_ref, bf16[128,768]{1,0:T(8,128)(2,1)S(1)} %collective-permute-done.5.far_ref, ...), custom_call_target="tpu_custom_call" | custom-call | bytes 2952000 | tf_op jit(solution)/shard_map/dattn/pallas_call | solution.py:44
  14.2 0.1 collective-permute-done.1.kv1
  14.4 1.6 %collective-permute-start.7 = (bf16[320,128]{1,0:T(8,128)(2,1)S(1)}, bf16[320,128]{1,0:T(8,128)(2,1)S(1)}, u32[]{:S(2)}, u32[]{:S(2)}) collective-permute-start(bf16[320,128]{1,0:T(8,128)(2,1)S(1)} %get-tuple-element.52), channel_id=1, source_target_pairs={{0,4},{4,0},{8,12},{12,8},{16,20},{20,16},{24,28},{28,24},{1,5},{5... | collective-permute-start | bytes 245768 | tf_op jit(solution)/shard_map/ppermute | solution.py:35
  15.9 0.5 %collective-permute-start.8 = (bf16[320,128]{1,0:T(8,128)(2,1)S(1)}, bf16[320,128]{1,0:T(8,128)(2,1)S(1)}, u32[]{:S(2)}, u32[]{:S(2)}) collective-permute-start(bf16[320,128]{1,0:T(8,128)(2,1)S(1)} %get-tuple-element.53), channel_id=1, source_target_pairs={{0,4},{4,0},{8,12},{12,8},{16,20},{20,16},{24,28},{28,24},{1,5},{5... | collective-permute-start | bytes 245768 | tf_op jit(solution)/shard_map/ppermute | solution.py:35
  16.4 1.5 %collective-permute-start.9 = (bf16[320,128]{1,0:T(8,128)(2,1)S(1)}, bf16[320,128]{1,0:T(8,128)(2,1)S(1)}, u32[]{:S(2)}, u32[]{:S(2)}) collective-permute-start(bf16[320,128]{1,0:T(8,128)(2,1)S(1)} %get-tuple-element.54), channel_id=1, source_target_pairs={{0,4},{4,0},{8,12},{12,8},{16,20},{20,16},{24,28},{28,24},{1,5},{5... | collective-permute-start | bytes 245768 | tf_op jit(solution)/shard_map/ppermute | solution.py:35
  18.0 2.6 %collective-permute-start.6 = (bf16[128,384]{1,0:T(8,128)(2,1)S(1)}, bf16[128,384]{1,0:T(8,128)(2,1)S(1)}, u32[]{:S(2)}, u32[]{:S(2)}) collective-permute-start(bf16[128,384]{1,0:T(8,128)(2,1)S(1)} %dattn.1.d_own_ref), channel_id=1, source_target_pairs={{0,16},{4,20},{8,24},{12,28},{16,0},{20,4},{24,8},{28,12},{1,17},{... | collective-permute-start | bytes 294920 | tf_op jit(solution)/shard_map/ppermute | solution.py:35
  20.6 0.1 copy.15.levels_ref
  20.6 0.6 %limits.1.limits_ref = s32[8,256]{1,0:T(8,128)S(1)} custom-call(s32[8,2]{1,0:T(8,128)S(1)} %copy.15.levels_ref, s32[8]{0:T(128)S(1)} %copy-done.4), custom_call_target="tpu_custom_call" | custom-call | bytes 2214000 | tf_op jit(solution)/shard_map/limits/pallas_call | solution.py:44
  21.3 0.7 %collective-permute-done.9.refs_2_ = bf16[320,128]{1,0:T(8,128)(2,1)S(1)} collective-permute-done((bf16[320,128]{1,0:T(8,128)(2,1)S(1)}, bf16[320,128]{1,0:T(8,128)(2,1)S(1)}, u32[]{:S(2)}, u32[]{:S(2)}) %collective-permute-start.9) | collective-permute-done | bytes 81952 | tf_op jit(solution)/shard_map/ppermute | solution.py:35
  22.0 1.0 %scores.1 = (f32[8,256]{1,0:T(8,128)S(1)}, bf16[1920,256]{1,0:T(8,128)(2,1)S(1)}) custom-call(s32[8,256]{1,0:T(8,128)S(1)} %limits.1.limits_ref, bf16[128,384]{1,0:T(8,128)(2,1)S(1)} %copy-done.2, bf16[128,384]{1,0:T(8,128)(2,1)S(1)} %collective-permute-done.q_pair_ref, bf16[320,384]{1,0:T(8,128)(2,1)S(1)} %copy-done.1, ...), custom_call_target="tpu_custom_call" | custom-call | bytes 3321000 | tf_op jit(solution)/shard_map/scores/pallas_call | solution.py:44
  23.0 0.4 attn.1
  23.5 1.9 %collective-permute-start.11 = (bf16[384,128]{1,0:T(8,128)(2,1)S(1)}, bf16[384,128]{1,0:T(8,128)(2,1)S(1)}, u32[]{:S(2)}, u32[]{:S(2)}) collective-permute-start(bf16[384,128]{1,0:T(8,128)(2,1)S(1)} %get-tuple-element.63), channel_id=1, source_target_pairs={{0,16},{4,20},{8,24},{12,28},{16,0},{20,4},{24,8},{28,12},{1,17},{... | collective-permute-start | bytes 294920 | tf_op jit(solution)/shard_map/ppermute | solution.py:35
  25.4 0.4 delta.1
  25.8 0.0 copy-start
  25.8 1.2 %collective-permute-start.10 = (f32[16,256]{1,0:T(8,128)S(1)}, f32[16,256]{1,0:T(8,128)S(1)}, u32[]{:S(2)}, u32[]{:S(2)}) collective-permute-start(f32[16,256]{1,0:T(8,128)S(1)} %get-tuple-element.59.stats_ref), channel_id=1, source_target_pairs={{0,16},{4,20},{8,24},{12,28},{16,0},{20,4},{24,8},{28,12},{1,17},{... | collective-permute-start | bytes 49160 | tf_op jit(solution)/shard_map/ppermute | solution.py:35
  27.0 3.8 %collective-permute-done.10.stats_pair_ref = f32[16,256]{1,0:T(8,128)S(1)} collective-permute-done((f32[16,256]{1,0:T(8,128)S(1)}, f32[16,256]{1,0:T(8,128)S(1)}, u32[]{:S(2)}, u32[]{:S(2)}) %collective-permute-start.10) | collective-permute-done | bytes 16416 | tf_op jit(solution)/shard_map/ppermute | solution.py:35
  30.8 1.1 %backward.1 = (f32[128,384]{1,0:T(8,128)S(1)}, bf16[128,384]{1,0:T(8,128)(2,1)S(1)}, f32[320,384]{1,0:T(8,128)S(1)}, bf16[384,384]{1,0:T(8,128)(2,1)S(1)}, bf16[...) custom-call(bf16[128,384]{1,0:T(8,128)(2,1)S(1)} %copy-done.2, ...), custom_call_target="tpu_custom_call" | custom-call | bytes 4059000 | tf_op jit(solution)/shard_map/backward/pallas_call | solution.py:44
  31.9 1.0 %collective-permute-start.12 = (bf16[384,384]{1,0:T(8,128)(2,1)S(1)}, bf16[384,384]{1,0:T(8,128)(2,1)S(1)}, u32[]{:S(2)}, u32[]{:S(2)}) collective-permute-start(bf16[384,384]{1,0:T(8,128)(2,1)S(1)} %get-tuple-element.66), channel_id=1, source_target_pairs={{0,4},{4,0},{8,12},{12,8},{16,20},{20,16},{24,28},{28,24},{1,5},{5... | collective-permute-start | bytes 884744 | tf_op jit(solution)/shard_map/ppermute | solution.py:35
  32.9 0.4 collective-permute-start.13
  33.3 0.6 %project.1 = (f32[128,768]{1,0:T(8,128)S(1)}, f32[128,768]{1,0:T(8,128)S(1)}, bf16[128,768]{1,0:T(8,128)(2,1)S(1)}, bf16[128,384]{1,0:T(8,128)(2,1)S(1)}, bf16[128,384]{1,0:T(8,128)(2,1)S(1)}) custom-call(f32[384,128]{1,0:T(8,128)S(1)} %get-tuple-element.68.own_ref, bf16[384,128]{1,0:T(8,128)(2,1)S(1)} %collective-permute-done.11.pair_ref, ...), custom_call_target="tpu_custom_call" | custom-call | bytes 2214000 | tf_op jit(solution)/shard_map/project/pallas_call | solution.py:44
  34.0 0.1 collective-permute-start.14
  34.0 0.5 %collective-permute-start.15 = (bf16[128,384]{1,0:T(8,128)(2,1)S(1)}, bf16[128,384]{1,0:T(8,128)(2,1)S(1)}, u32[]{:S(2)}, u32[]{:S(2)}) collective-permute-start(bf16[128,384]{1,0:T(8,128)(2,1)S(1)} %get-tuple-element.74), channel_id=1, source_target_pairs={{0,1},{1,0},{2,3},{3,2},{4,5},{5,4},{6,7},{7,6},{8,9},{9,8},{10,11... | collective-permute-start | bytes 294920 | tf_op jit(solution)/shard_map/ppermute | solution.py:35
  34.5 0.1 collective-permute-start.16
  34.6 1.0 %collective-permute-done.15.left_ref = bf16[128,384]{1,0:T(8,128)(2,1)S(1)} collective-permute-done((bf16[128,384]{1,0:T(8,128)(2,1)S(1)}, bf16[128,384]{1,0:T(8,128)(2,1)S(1)}, u32[]{:S(2)}, u32[]{:S(2)}) %collective-permute-start.15) | collective-permute-done | bytes 98336 | tf_op jit(solution)/shard_map/ppermute | solution.py:35
  35.6 0.2 collective-permute-done.16.right_ref
  35.9 1.3 %collective-permute-start.17 = (bf16[128,768]{1,0:T(8,128)(2,1)S(1)}, bf16[128,768]{1,0:T(8,128)(2,1)S(1)}, u32[]{:S(2)}, u32[]{:S(2)}) collective-permute-start(bf16[128,768]{1,0:T(8,128)(2,1)S(1)} %add_near.1), channel_id=1, source_target_pairs={{0,2},{1,3},{2,0},{3,1},{4,6},{5,7},{6,4},{7,5},{8,10},{9,11},{10,... | collective-permute-start | bytes 589832 | tf_op jit(solution)/shard_map/ppermute | solution.py:35
  37.2 1.9 %collective-permute-start.18 = (bf16[128,384]{1,0:T(8,128)(2,1)S(1)}, bf16[128,384]{1,0:T(8,128)(2,1)S(1)}, u32[]{:S(2)}, u32[]{:S(2)}) collective-permute-start(bf16[128,384]{1,0:T(8,128)(2,1)S(1)} %get-tuple-element.77), channel_id=1, source_target_pairs={{0,16},{4,20},{8,24},{12,28},{16,0},{20,4},{24,8},{28,12},{1,17},{... | collective-permute-start | bytes 294920 | tf_op jit(solution)/shard_map/ppermute | solution.py:35
  39.0 0.8 %collective-permute-done.12.got_y_ref = bf16[384,384]{1,0:T(8,128)(2,1)S(1)} collective-permute-done((bf16[384,384]{1,0:T(8,128)(2,1)S(1)}, bf16[384,384]{1,0:T(8,128)(2,1)S(1)}, u32[]{:S(2)}, u32[]{:S(2)}) %collective-permute-start.12) | collective-permute-done | bytes 294944 | tf_op jit(solution)/shard_map/ppermute | solution.py:35
  39.8 0.1 pass_on.1
  39.9 0.1 collective-permute-start.19
  40.0 0.4 collective-permute-start.21
  40.3 2.0 %collective-permute-start.20 = (bf16[64,384]{1,0:T(8,128)(2,1)S(1)}, bf16[64,384]{1,0:T(8,128)(2,1)S(1)}, u32[]{:S(2)}, u32[]{:S(2)}) collective-permute-start(bf16[64,384]{1,0:T(8,128)(2,1)S(1)} %get-tuple-element.80), channel_id=1, source_target_pairs={{0,8},{4,12},{8,0},{12,4},{16,24},{20,28},{24,16},{28,20},{1,9},{5... | collective-permute-start | bytes 147464 | tf_op jit(solution)/shard_map/ppermute | solution.py:35
  42.3 2.6 %collective-permute-done.18.dq_pair_ref = bf16[128,384]{1,0:T(8,128)(2,1)S(1)} collective-permute-done((bf16[128,384]{1,0:T(8,128)(2,1)S(1)}, bf16[128,384]{1,0:T(8,128)(2,1)S(1)}, u32[]{:S(2)}, u32[]{:S(2)}) %collective-permute-start.18) | collective-permute-done | bytes 98336 | tf_op jit(solution)/shard_map/ppermute | solution.py:35
  44.9 0.9 %collective-permute-done.20.rest_h_ref = bf16[64,384]{1,0:T(8,128)(2,1)S(1)} collective-permute-done((bf16[64,384]{1,0:T(8,128)(2,1)S(1)}, bf16[64,384]{1,0:T(8,128)(2,1)S(1)}, u32[]{:S(2)}, u32[]{:S(2)}) %collective-permute-start.20) | collective-permute-done | bytes 49184 | tf_op jit(solution)/shard_map/ppermute | solution.py:35
  45.8 0.9 %finish.1 = (bf16[128,384]{1,0:T(8,128)(2,1)}, bf16[128,384]{1,0:T(8,128)(2,1)}, bf16[128,384]{1,0:T(8,128)(2,1)}, bf16[32,384]{1,0:T(8,128)(2,1)}, bf16[32,384]{1,0:T(8,128)(2,1)}, /*index=5*/bf16[128,768]{1,0:T(8,128)(2,1)}) custom-call(f32[128,768]{1,0:T(8,128)S(1)} %get-tuple-element.72.keep_ref, bf16[128,768]{1,0:T(8,128)(2,1)S(1)} %collective-permute-done.17.near_ref, ...), custom_call_target="tpu_custom_call" | custom-call | bytes 3321000 | tf_op jit(solution)/shard_map/finish/pallas_call | solution.py:44
  (22 shorter events, 0.1 us)
Async XLA Ops:
  0.6 9.5 %collective-permute-start.4 = (bf16[128,768]{1,0:T(8,128)(2,1)}, bf16[128,768]{1,0:T(8,128)(2,1)S(1)}, u32[]{:S(2)}, u32[]{:S(2)}) collective-permute-start(bf16[128,768]{1,0:T(8,128)(2,1)} %own_ref.1), channel_id=1, source_target_pairs={{0,2},{1,3},{2,0},{3,1},{4,6},{5,7},{6,4},{7,5},{8,10},{9,11},{10,... | collective-permute-start | bytes 589832 | tf_op jit(solution)/shard_map/ppermute | solution.py:35
  5.3 5.4 %copy-start.2 = (bf16[128,384]{1,0:T(8,128)(2,1)S(1)}, bf16[128,384]{1,0:T(8,128)(2,1)}, u32[]{:S(2)}) copy-start(bf16[128,384]{1,0:T(8,128)(2,1)} %q_own_ref.3) | copy-start | bytes 294916
  5.3 8.0 %copy-start.3 = (bf16[128,768]{1,0:T(8,128)(2,1)S(1)}, bf16[128,768]{1,0:T(8,128)(2,1)}, u32[]{:S(2)}) copy-start(bf16[128,768]{1,0:T(8,128)(2,1)} %own_ref.1) | copy-start | bytes 589828
  5.3 8.9 %collective-permute-start.2 = (bf16[320,384]{1,0:T(8,128)(2,1)}, bf16[320,384]{1,0:T(8,128)(2,1)S(1)}, u32[]{:S(2)}, u32[]{:S(2)}) collective-permute-start(bf16[320,384]{1,0:T(8,128)(2,1)} %load.1.kv0), channel_id=1, source_target_pairs={{0,8},{4,12},{8,0},{12,4},{16,24},{20,28},{24,16},{28,20},{1,9},{5... | collective-permute-start | bytes 737288 | tf_op jit(solution)/shard_map/ppermute | solution.py:35
  7.0 7.3 %collective-permute-start.1 = (bf16[320,384]{1,0:T(8,128)(2,1)}, bf16[320,384]{1,0:T(8,128)(2,1)S(1)}, u32[]{:S(2)}, u32[]{:S(2)}) collective-permute-start(bf16[320,384]{1,0:T(8,128)(2,1)} %load.1.kv0), channel_id=1, source_target_pairs={{0,4},{4,0},{8,12},{12,8},{16,20},{20,16},{24,28},{28,24},{1,5},{5... | collective-permute-start | bytes 737288 | tf_op jit(solution)/shard_map/ppermute | solution.py:35
  8.5 4.9 %collective-permute-start.3 = (bf16[128,768]{1,0:T(8,128)(2,1)}, bf16[128,768]{1,0:T(8,128)(2,1)S(1)}, u32[]{:S(2)}, u32[]{:S(2)}) collective-permute-start(bf16[128,768]{1,0:T(8,128)(2,1)} %own_ref.1), channel_id=1, source_target_pairs={{0,1},{1,0},{2,3},{3,2},{4,5},{5,4},{6,7},{7,6},{8,9},{9,8},{10,11... | collective-permute-start | bytes 589832 | tf_op jit(solution)/shard_map/ppermute | solution.py:35
  10.1 10.4 %copy-start.5 = (s32[8,2]{0,1:T(2,128)S(1)}, s32[8,2]{0,1:T(2,128)}, u32[]{:S(2)}) copy-start(s32[8,2]{0,1:T(2,128)} %param.14) | copy-start | bytes 196
  10.1 10.5 %copy-start.4 = (s32[8]{0:T(128)S(1)}, s32[8]{0:T(128)}, u32[]{:S(2)}) copy-start(s32[8]{0:T(128)} %counts_ref.1) | copy-start | bytes 100
  10.2 11.8 %copy-start.1 = (bf16[320,384]{1,0:T(8,128)(2,1)S(1)}, bf16[320,384]{1,0:T(8,128)(2,1)}, u32[]{:S(2)}) copy-start(bf16[320,384]{1,0:T(8,128)(2,1)} %load.1.kv0) | copy-start | bytes 737284
  10.2 3.2 %collective-permute-start.5 = (bf16[128,768]{1,0:T(8,128)(2,1)S(1)}, bf16[128,768]{1,0:T(8,128)(2,1)S(1)}, u32[]{:S(2)}, u32[]{:S(2)}) collective-permute-start(bf16[128,768]{1,0:T(8,128)(2,1)S(1)} %collective-permute-done.4.near_ref), channel_id=1, source_target_pairs={{0,1},{1,0},{2,3},{3,2},{4,5},{5,4},{6,7},{7,6},{8,9},{9,8},{10,11... | collective-permute-start | bytes 589832 | tf_op jit(solution)/shard_map/ppermute | solution.py:35
  10.8 10.5 %collective-permute-start = (bf16[128,384]{1,0:T(8,128)(2,1)S(1)}, bf16[128,384]{1,0:T(8,128)(2,1)S(1)}, u32[]{:S(2)}, u32[]{:S(2)}) collective-permute-start(bf16[128,384]{1,0:T(8,128)(2,1)S(1)} %copy-done.2), channel_id=1, source_target_pairs={{0,16},{4,20},{8,24},{12,28},{16,0},{20,4},{24,8},{28,12},{1,17},{... | collective-permute-start | bytes 294920 | tf_op jit(solution)/shard_map/ppermute | solution.py:35
  14.4 6.9 %collective-permute-start.7 = (bf16[320,128]{1,0:T(8,128)(2,1)S(1)}, bf16[320,128]{1,0:T(8,128)(2,1)S(1)}, u32[]{:S(2)}, u32[]{:S(2)}) collective-permute-start(bf16[320,128]{1,0:T(8,128)(2,1)S(1)} %get-tuple-element.52), channel_id=1, source_target_pairs={{0,4},{4,0},{8,12},{12,8},{16,20},{20,16},{24,28},{28,24},{1,5},{5... | collective-permute-start | bytes 245768 | tf_op jit(solution)/shard_map/ppermute | solution.py:35
  15.9 5.4 %collective-permute-start.8 = (bf16[320,128]{1,0:T(8,128)(2,1)S(1)}, bf16[320,128]{1,0:T(8,128)(2,1)S(1)}, u32[]{:S(2)}, u32[]{:S(2)}) collective-permute-start(bf16[320,128]{1,0:T(8,128)(2,1)S(1)} %get-tuple-element.53), channel_id=1, source_target_pairs={{0,4},{4,0},{8,12},{12,8},{16,20},{20,16},{24,28},{28,24},{1,5},{5... | collective-permute-start | bytes 245768 | tf_op jit(solution)/shard_map/ppermute | solution.py:35
  16.4 5.6 %collective-permute-start.9 = (bf16[320,128]{1,0:T(8,128)(2,1)S(1)}, bf16[320,128]{1,0:T(8,128)(2,1)S(1)}, u32[]{:S(2)}, u32[]{:S(2)}) collective-permute-start(bf16[320,128]{1,0:T(8,128)(2,1)S(1)} %get-tuple-element.54), channel_id=1, source_target_pairs={{0,4},{4,0},{8,12},{12,8},{16,20},{20,16},{24,28},{28,24},{1,5},{5... | collective-permute-start | bytes 245768 | tf_op jit(solution)/shard_map/ppermute | solution.py:35
  18.0 7.4 %collective-permute-start.6 = (bf16[128,384]{1,0:T(8,128)(2,1)S(1)}, bf16[128,384]{1,0:T(8,128)(2,1)S(1)}, u32[]{:S(2)}, u32[]{:S(2)}) collective-permute-start(bf16[128,384]{1,0:T(8,128)(2,1)S(1)} %dattn.1.d_own_ref), channel_id=1, source_target_pairs={{0,16},{4,20},{8,24},{12,28},{16,0},{20,4},{24,8},{28,12},{1,17},{... | collective-permute-start | bytes 294920 | tf_op jit(solution)/shard_map/ppermute | solution.py:35
  23.5 8.4 %collective-permute-start.11 = (bf16[384,128]{1,0:T(8,128)(2,1)S(1)}, bf16[384,128]{1,0:T(8,128)(2,1)S(1)}, u32[]{:S(2)}, u32[]{:S(2)}) collective-permute-start(bf16[384,128]{1,0:T(8,128)(2,1)S(1)} %get-tuple-element.63), channel_id=1, source_target_pairs={{0,16},{4,20},{8,24},{12,28},{16,0},{20,4},{24,8},{28,12},{1,17},{... | collective-permute-start | bytes 294920 | tf_op jit(solution)/shard_map/ppermute | solution.py:35
  25.8 7.5 %copy-start = (bf16[384,3072]{1,0:T(8,128)(2,1)S(1)}, bf16[384,3072]{1,0:T(8,128)(2,1)}, u32[]{:S(2)}) copy-start(bf16[384,3072]{1,0:T(8,128)(2,1)} %w_ref.3) | copy-start | bytes 7077892
  25.8 4.9 %collective-permute-start.10 = (f32[16,256]{1,0:T(8,128)S(1)}, f32[16,256]{1,0:T(8,128)S(1)}, u32[]{:S(2)}, u32[]{:S(2)}) collective-permute-start(f32[16,256]{1,0:T(8,128)S(1)} %get-tuple-element.59.stats_ref), channel_id=1, source_target_pairs={{0,16},{4,20},{8,24},{12,28},{16,0},{20,4},{24,8},{28,12},{1,17},{... | collective-permute-start | bytes 49160 | tf_op jit(solution)/shard_map/ppermute | solution.py:35
  31.9 7.9 %collective-permute-start.12 = (bf16[384,384]{1,0:T(8,128)(2,1)S(1)}, bf16[384,384]{1,0:T(8,128)(2,1)S(1)}, u32[]{:S(2)}, u32[]{:S(2)}) collective-permute-start(bf16[384,384]{1,0:T(8,128)(2,1)S(1)} %get-tuple-element.66), channel_id=1, source_target_pairs={{0,4},{4,0},{8,12},{12,8},{16,20},{20,16},{24,28},{28,24},{1,5},{5... | collective-permute-start | bytes 884744 | tf_op jit(solution)/shard_map/ppermute | solution.py:35
  32.9 6.1 %collective-permute-start.13 = (bf16[256,384]{1,0:T(8,128)(2,1)S(1)}, bf16[256,384]{1,0:T(8,128)(2,1)S(1)}, u32[]{:S(2)}, u32[]{:S(2)}) collective-permute-start(bf16[256,384]{1,0:T(8,128)(2,1)S(1)} %get-tuple-element.67), channel_id=1, source_target_pairs={{0,8},{4,12},{8,0},{12,4},{16,24},{20,28},{24,16},{28,20},{1,9},{5... | collective-permute-start | bytes 589832 | tf_op jit(solution)/shard_map/ppermute | solution.py:35
  34.0 5.1 %collective-permute-start.14 = (bf16[128,768]{1,0:T(8,128)(2,1)S(1)}, bf16[128,768]{1,0:T(8,128)(2,1)S(1)}, u32[]{:S(2)}, u32[]{:S(2)}) collective-permute-start(bf16[128,768]{1,0:T(8,128)(2,1)S(1)} %get-tuple-element.71), channel_id=1, source_target_pairs={{0,1},{1,0},{2,3},{3,2},{4,5},{5,4},{6,7},{7,6},{8,9},{9,8},{10,11... | collective-permute-start | bytes 589832 | tf_op jit(solution)/shard_map/ppermute | solution.py:35
  34.0 1.6 %collective-permute-start.15 = (bf16[128,384]{1,0:T(8,128)(2,1)S(1)}, bf16[128,384]{1,0:T(8,128)(2,1)S(1)}, u32[]{:S(2)}, u32[]{:S(2)}) collective-permute-start(bf16[128,384]{1,0:T(8,128)(2,1)S(1)} %get-tuple-element.74), channel_id=1, source_target_pairs={{0,1},{1,0},{2,3},{3,2},{4,5},{5,4},{6,7},{7,6},{8,9},{9,8},{10,11... | collective-permute-start | bytes 294920 | tf_op jit(solution)/shard_map/ppermute | solution.py:35
  34.5 1.3 %collective-permute-start.16 = (bf16[128,384]{1,0:T(8,128)(2,1)S(1)}, bf16[128,384]{1,0:T(8,128)(2,1)S(1)}, u32[]{:S(2)}, u32[]{:S(2)}) collective-permute-start(bf16[128,384]{1,0:T(8,128)(2,1)S(1)} %get-tuple-element.75), channel_id=1, source_target_pairs={{0,1},{1,0},{2,3},{3,2},{4,5},{5,4},{6,7},{7,6},{8,9},{9,8},{10,11... | collective-permute-start | bytes 294920 | tf_op jit(solution)/shard_map/ppermute | solution.py:35
  35.9 9.0 %collective-permute-start.17 = (bf16[128,768]{1,0:T(8,128)(2,1)S(1)}, bf16[128,768]{1,0:T(8,128)(2,1)S(1)}, u32[]{:S(2)}, u32[]{:S(2)}) collective-permute-start(bf16[128,768]{1,0:T(8,128)(2,1)S(1)} %add_near.1), channel_id=1, source_target_pairs={{0,2},{1,3},{2,0},{3,1},{4,6},{5,7},{6,4},{7,5},{8,10},{9,11},{10,... | collective-permute-start | bytes 589832 | tf_op jit(solution)/shard_map/ppermute | solution.py:35
  37.2 7.7 %collective-permute-start.18 = (bf16[128,384]{1,0:T(8,128)(2,1)S(1)}, bf16[128,384]{1,0:T(8,128)(2,1)S(1)}, u32[]{:S(2)}, u32[]{:S(2)}) collective-permute-start(bf16[128,384]{1,0:T(8,128)(2,1)S(1)} %get-tuple-element.77), channel_id=1, source_target_pairs={{0,16},{4,20},{8,24},{12,28},{16,0},{20,4},{24,8},{28,12},{1,17},{... | collective-permute-start | bytes 294920 | tf_op jit(solution)/shard_map/ppermute | solution.py:35
  39.9 5.9 %collective-permute-start.19 = (bf16[128,384]{1,0:T(8,128)(2,1)S(1)}, bf16[128,384]{1,0:T(8,128)(2,1)S(1)}, u32[]{:S(2)}, u32[]{:S(2)}) collective-permute-start(bf16[128,384]{1,0:T(8,128)(2,1)S(1)} %get-tuple-element.79), channel_id=1, source_target_pairs={{0,8},{4,12},{8,0},{12,4},{16,24},{20,28},{24,16},{28,20},{1,9},{5... | collective-permute-start | bytes 294920 | tf_op jit(solution)/shard_map/ppermute | solution.py:35
  40.0 5.8 %collective-permute-start.21 = (bf16[128,384]{1,0:T(8,128)(2,1)S(1)}, bf16[128,384]{1,0:T(8,128)(2,1)S(1)}, u32[]{:S(2)}, u32[]{:S(2)}) collective-permute-start(bf16[128,384]{1,0:T(8,128)(2,1)S(1)} %get-tuple-element.81), channel_id=1, source_target_pairs={{0,4},{4,0},{8,12},{12,8},{16,20},{20,16},{24,28},{28,24},{1,5},{5... | collective-permute-start | bytes 294920 | tf_op jit(solution)/shard_map/ppermute | solution.py:35
  40.3 5.5 %collective-permute-start.20 = (bf16[64,384]{1,0:T(8,128)(2,1)S(1)}, bf16[64,384]{1,0:T(8,128)(2,1)S(1)}, u32[]{:S(2)}, u32[]{:S(2)}) collective-permute-start(bf16[64,384]{1,0:T(8,128)(2,1)S(1)} %get-tuple-element.80), channel_id=1, source_target_pairs={{0,8},{4,12},{8,0},{12,4},{16,24},{20,28},{24,16},{28,20},{1,9},{5... | collective-permute-start | bytes 147464 | tf_op jit(solution)/shard_map/ppermute | solution.py:35

commit v19 on v18

--- a/solution.py
+++ b/solution.py
@@ -381,6 +381,15 @@
         [shape((8, 2 * rows), F32), shape((heads * SQUARE * keys, 2 * rows), BF16)],
         (limits, sec_q, q_pair, *kvs),
     )
+    stats, dprobs = local_call(
+        delta_kernel,
+        "delta",
+        0.7,
+        [shape((16, 2 * rows), F32), shape((heads * SQUARE * keys, 2 * rows), F32)],
+        (lse, probs, d_own, d_pair, *kvs),
+    )
+    stats_pair = swap(stats, "ctx", PAIR)
+    probs, stats_pair = lax.optimization_barrier((probs, stats_pair))
     attn_own, attn_pair = local_call(
         attn_kernel,
         "attn",
@@ -388,15 +397,6 @@
         [shape((width, rows), F32), shape((width, rows), BF16)],
         (probs, *kvs),
     )
-    lse, attn_own = lax.optimization_barrier((lse, attn_own))
-    stats, dprobs = local_call(
-        delta_kernel,
-        "delta",
-        0.7,
-        [shape((16, 2 * rows), F32), shape((heads * SQUARE * keys, 2 * rows), F32)],
-        (lse, probs, d_own, d_pair, *kvs),
-    )
-    stats_pair = swap(stats, "ctx", PAIR)
     wide = keys + capacity
     dq_own, dq_pair, dkv_own, send_y, send_z, near_y, near_z = local_call(
         backward_kernel,
@@ -408,7 +408,6 @@
         (sec_q, q_pair, d_own, d_pair, stats, stats_pair, probs, dprobs, *kvs),
     )
     attn_got = swap(attn_pair, "ctx", PAIR)
-    attn_got, send_y, send_z = lax.optimization_barrier((attn_got, send_y, send_z))
     got_y = swap(send_y, "ctx", 1)
     got_z = swap(send_z, "ctx", 2)
     half = share // 2

time: 46.9 us -> 49.9 us (1.064)
  waiting for transfers between devices: 10.1 us -> 16.6 us
  starting transfers between devices: 26.2 us -> 22.8 us
    ppermute x22, waiting for transfers between devices: 10.1 us -> 16.6 us  [swap(): return lax.ppermute(block, axis, [(i, i ^ bit) for i in range(count)])]
    ppermute x22, starting transfers between devices: 26.2 us -> 22.8 us  [swap(): return lax.ppermute(block, axis, [(i, i ^ bit) for i in range(count)])]
  transfers between devices with their start and end apart: 22 -> 22, of which waited for: 8 -> 10; matrix products, arithmetic and copies ran while one was open for 0% -> 0% of each run, Pallas kernels for 18% -> 15%
where the time goes in v19:
time: 49.9 us; the launch traced here: 49.7 us
  starting transfers between devices  22.8 us (46%)
  waiting for transfers between devices  16.6 us (33%)
  Pallas kernels  9.39 us (19%)
  between operations  0.84 us (2%)
    ppermute x22, starting transfers between devices, swap(): return lax.ppermute(block, axis, [(i, i ^ bit) for i in range(count)])  22.8 us
    ppermute x22, waiting for transfers between devices, swap(): return lax.ppermute(block, axis, [(i, i ^ bit) for i in range(count)])  16.6 us
    pallas_call x11, Pallas kernels, local_call(): pl.pallas_call(body, name=name, out_shape=out_shapes, in_specs=[pl.BlockS...  6.09 us
    pallas_call x1, Pallas kernels, load_keys(): pl.pallas_call(load_kernel, name='load', out_shape=jax.ShapeDtypeStruct((...  1.66 us
    pallas_call x1, Pallas kernels, load_weight(): pl.pallas_call(load_weight_kernel, name='load_w', out_shape=jax.ShapeDtyp...  1.63 us
  transfers between devices with their start and end apart: 22, of which 10 were waited for; matrix products, arithmetic and copies ran while one was open for 0% of the time, Pallas kernels for 15%

profile of v19, /device:TPU:0, one launch (start us, length us, event | category | flops | bytes accessed | tf_op | source)
XLA Modules:
  0.0 49.7 jit_solution(7250687489348352548)
XLA Ops:
  0.6 3.0 %collective-permute-start.4 = (bf16[128,768]{1,0:T(8,128)(2,1)}, bf16[128,768]{1,0:T(8,128)(2,1)S(1)}, u32[]{:S(2)}, u32[]{:S(2)}) collective-permute-start(bf16[128,768]{1,0:T(8,128)(2,1)} %own_ref.1), channel_id=1, source_target_pairs={{0,2},{1,3},{2,0},{3,1},{4,6},{5,7},{6,4},{7,5},{8,10},{9,11},{10,... | collective-permute-start | bytes 589832 | tf_op jit(solution)/shard_map/ppermute | solution.py:35
  3.6 1.7 %load.1.kv0 = bf16[320,384]{1,0:T(8,128)(2,1)} custom-call(bf16[128,384]{1,0:T(8,128)(2,1)} %k_ref.1, bf16[32,384]{1,0:T(8,128)(2,1)} %hk_ref.1, bf16[128,384]{1,0:T(8,128)(2,1)} %v_ref.1, bf16[32,384]{1,0:T(8,128)(2,1)} %hv_ref.1), custom_call_target="tpu_custom_call" | custom-call | bytes 5904000 | tf_op jit(solution)/shard_map/load/pallas_call | solution.py:74
  5.3 0.0 copy-start.2
  5.3 0.0 copy-start.3
  5.3 1.6 %collective-permute-start.2 = (bf16[320,384]{1,0:T(8,128)(2,1)}, bf16[320,384]{1,0:T(8,128)(2,1)S(1)}, u32[]{:S(2)}, u32[]{:S(2)}) collective-permute-start(bf16[320,384]{1,0:T(8,128)(2,1)} %load.1.kv0), channel_id=1, source_target_pairs={{0,8},{4,12},{8,0},{12,4},{16,24},{20,28},{24,16},{28,20},{1,9},{5... | collective-permute-start | bytes 737288 | tf_op jit(solution)/shard_map/ppermute | solution.py:35
  7.0 1.5 %collective-permute-start.1 = (bf16[320,384]{1,0:T(8,128)(2,1)}, bf16[320,384]{1,0:T(8,128)(2,1)S(1)}, u32[]{:S(2)}, u32[]{:S(2)}) collective-permute-start(bf16[320,384]{1,0:T(8,128)(2,1)} %load.1.kv0), channel_id=1, source_target_pairs={{0,4},{4,0},{8,12},{12,8},{16,20},{20,16},{24,28},{28,24},{1,5},{5... | collective-permute-start | bytes 737288 | tf_op jit(solution)/shard_map/ppermute | solution.py:35
  8.5 1.6 %load_w.1.w_ref = bf16[384,3072]{1,0:T(8,128)(2,1)S(1)} custom-call(bf16[384,3072]{1,0:T(8,128)(2,1)} %w_ref.3), custom_call_target="tpu_custom_call" | custom-call | bytes 5904000 | tf_op jit(solution)/shard_map/load_w/pallas_call | solution.py:113
  10.1 0.0 copy-start.5
  10.1 0.0 copy-start.4
  10.2 0.6 %collective-permute-start.5 = (bf16[128,768]{1,0:T(8,128)(2,1)S(1)}, bf16[128,768]{1,0:T(8,128)(2,1)S(1)}, u32[]{:S(2)}, u32[]{:S(2)}) collective-permute-start(bf16[128,768]{1,0:T(8,128)(2,1)S(1)} %collective-permute-done.4.near_ref), channel_id=1, source_target_pairs={{0,1},{1,0},{2,3},{3,2},{4,5},{5,4},{6,7},{7,6},{8,9},{9,8},{10,11... | collective-permute-start | bytes 589832 | tf_op jit(solution)/shard_map/ppermute | solution.py:35
  10.8 2.6 %collective-permute-start = (bf16[128,384]{1,0:T(8,128)(2,1)S(1)}, bf16[128,384]{1,0:T(8,128)(2,1)S(1)}, u32[]{:S(2)}, u32[]{:S(2)}) collective-permute-start(bf16[128,384]{1,0:T(8,128)(2,1)S(1)} %copy-done.2), channel_id=1, source_target_pairs={{0,16},{4,20},{8,24},{12,28},{16,0},{20,4},{24,8},{28,12},{1,17},{... | collective-permute-start | bytes 294920 | tf_op jit(solution)/shard_map/ppermute | solution.py:35
  13.4 0.8 %dattn.1.d_own_ref = bf16[128,384]{1,0:T(8,128)(2,1)S(1)} custom-call(bf16[128,768]{1,0:T(8,128)(2,1)S(1)} %copy-done.3, bf16[128,768]{1,0:T(8,128)(2,1)S(1)} %collective-permute-done.3.core_ref, bf16[128,768]{1,0:T(8,128)(2,1)S(1)} %collective-permute-done.4.near_ref, bf16[128,768]{1,0:T(8,128)(2,1)S(1)} %collective-permute-done.5.far_ref, ...), custom_call_target="tpu_custom_call" | custom-call | bytes 2952000 | tf_op jit(solution)/shard_map/dattn/pallas_call | solution.py:44
  14.2 0.1 collective-permute-done.1.kv1
  14.3 2.6 %collective-permute-start.6 = (bf16[128,384]{1,0:T(8,128)(2,1)S(1)}, bf16[128,384]{1,0:T(8,128)(2,1)S(1)}, u32[]{:S(2)}, u32[]{:S(2)}) collective-permute-start(bf16[128,384]{1,0:T(8,128)(2,1)S(1)} %dattn.1.d_own_ref), channel_id=1, source_target_pairs={{0,16},{4,20},{8,24},{12,28},{16,0},{20,4},{24,8},{28,12},{1,17},{... | collective-permute-start | bytes 294920 | tf_op jit(solution)/shard_map/ppermute | solution.py:35
  16.9 1.6 %collective-permute-start.7 = (bf16[320,128]{1,0:T(8,128)(2,1)S(1)}, bf16[320,128]{1,0:T(8,128)(2,1)S(1)}, u32[]{:S(2)}, u32[]{:S(2)}) collective-permute-start(bf16[320,128]{1,0:T(8,128)(2,1)S(1)} %get-tuple-element.49), channel_id=1, source_target_pairs={{0,4},{4,0},{8,12},{12,8},{16,20},{20,16},{24,28},{28,24},{1,5},{5... | collective-permute-start | bytes 245768 | tf_op jit(solution)/shard_map/ppermute | solution.py:35
  18.5 0.5 %collective-permute-start.8 = (bf16[320,128]{1,0:T(8,128)(2,1)S(1)}, bf16[320,128]{1,0:T(8,128)(2,1)S(1)}, u32[]{:S(2)}, u32[]{:S(2)}) collective-permute-start(bf16[320,128]{1,0:T(8,128)(2,1)S(1)} %get-tuple-element.50), channel_id=1, source_target_pairs={{0,4},{4,0},{8,12},{12,8},{16,20},{20,16},{24,28},{28,24},{1,5},{5... | collective-permute-start | bytes 245768 | tf_op jit(solution)/shard_map/ppermute | solution.py:35
  19.0 1.5 %collective-permute-start.9 = (bf16[320,128]{1,0:T(8,128)(2,1)S(1)}, bf16[320,128]{1,0:T(8,128)(2,1)S(1)}, u32[]{:S(2)}, u32[]{:S(2)}) collective-permute-start(bf16[320,128]{1,0:T(8,128)(2,1)S(1)} %get-tuple-element.51), channel_id=1, source_target_pairs={{0,4},{4,0},{8,12},{12,8},{16,20},{20,16},{24,28},{28,24},{1,5},{5... | collective-permute-start | bytes 245768 | tf_op jit(solution)/shard_map/ppermute | solution.py:35
  20.6 0.1 copy.15.levels_ref
  20.6 0.6 %limits.1.limits_ref = s32[8,256]{1,0:T(8,128)S(1)} custom-call(s32[8,2]{1,0:T(8,128)S(1)} %copy.15.levels_ref, s32[8]{0:T(128)S(1)} %copy-done.4), custom_call_target="tpu_custom_call" | custom-call | bytes 2214000 | tf_op jit(solution)/shard_map/limits/pallas_call | solution.py:44
  21.3 0.4 collective-permute-done.7.refs_0_
  21.6 1.3 %collective-permute-done.8.refs_1_ = bf16[320,128]{1,0:T(8,128)(2,1)S(1)} collective-permute-done((bf16[320,128]{1,0:T(8,128)(2,1)S(1)}, bf16[320,128]{1,0:T(8,128)(2,1)S(1)}, u32[]{:S(2)}, u32[]{:S(2)}) %collective-permute-start.8) | collective-permute-done | bytes 81952 | tf_op jit(solution)/shard_map/ppermute | solution.py:35
  23.0 0.9 %collective-permute-done.9.refs_2_ = bf16[320,128]{1,0:T(8,128)(2,1)S(1)} collective-permute-done((bf16[320,128]{1,0:T(8,128)(2,1)S(1)}, bf16[320,128]{1,0:T(8,128)(2,1)S(1)}, u32[]{:S(2)}, u32[]{:S(2)}) %collective-permute-start.9) | collective-permute-done | bytes 81952 | tf_op jit(solution)/shard_map/ppermute | solution.py:35
  23.9 1.0 %scores.1 = (f32[8,256]{1,0:T(8,128)S(1)}, bf16[1920,256]{1,0:T(8,128)(2,1)S(1)}) custom-call(s32[8,256]{1,0:T(8,128)S(1)} %limits.1.limits_ref, bf16[128,384]{1,0:T(8,128)(2,1)S(1)} %copy-done.2, bf16[128,384]{1,0:T(8,128)(2,1)S(1)} %collective-permute-done.q_pair_ref, bf16[320,384]{1,0:T(8,128)(2,1)S(1)} %copy-done.1, ...), custom_call_target="tpu_custom_call" | custom-call | bytes 3321000 | tf_op jit(solution)/shard_map/scores/pallas_call | solution.py:44
  24.9 0.4 delta.1
  25.3 0.9 %collective-permute-start.10 = (f32[16,256]{1,0:T(8,128)S(1)}, f32[16,256]{1,0:T(8,128)S(1)}, u32[]{:S(2)}, u32[]{:S(2)}) collective-permute-start(f32[16,256]{1,0:T(8,128)S(1)} %get-tuple-element.54.stats_ref), channel_id=1, source_target_pairs={{0,16},{4,20},{8,24},{12,28},{16,0},{20,4},{24,8},{28,12},{1,17},{... | collective-permute-start | bytes 49160 | tf_op jit(solution)/shard_map/ppermute | solution.py:35
  26.2 5.0 %collective-permute-done.10.stats_pair_ref = f32[16,256]{1,0:T(8,128)S(1)} collective-permute-done((f32[16,256]{1,0:T(8,128)S(1)}, f32[16,256]{1,0:T(8,128)S(1)}, u32[]{:S(2)}, u32[]{:S(2)}) %collective-permute-start.10) | collective-permute-done | bytes 16416 | tf_op jit(solution)/shard_map/ppermute | solution.py:35
  31.2 0.4 attn.1
  31.6 0.0 copy-start
  31.6 0.1 collective-permute-start.13
  31.7 1.1 %backward.1 = (f32[128,384]{1,0:T(8,128)S(1)}, bf16[128,384]{1,0:T(8,128)(2,1)S(1)}, f32[320,384]{1,0:T(8,128)S(1)}, bf16[384,384]{1,0:T(8,128)(2,1)S(1)}, bf16[...) custom-call(bf16[128,384]{1,0:T(8,128)(2,1)S(1)} %copy-done.2, ...), custom_call_target="tpu_custom_call" | custom-call | bytes 4059000 | tf_op jit(solution)/shard_map/backward/pallas_call | solution.py:44
  32.8 0.6 %collective-permute-start.11 = (bf16[384,384]{1,0:T(8,128)(2,1)S(1)}, bf16[384,384]{1,0:T(8,128)(2,1)S(1)}, u32[]{:S(2)}, u32[]{:S(2)}) collective-permute-start(bf16[384,384]{1,0:T(8,128)(2,1)S(1)} %get-tuple-element.60), channel_id=1, source_target_pairs={{0,4},{4,0},{8,12},{12,8},{16,20},{20,16},{24,28},{28,24},{1,5},{5... | collective-permute-start | bytes 884744 | tf_op jit(solution)/shard_map/ppermute | solution.py:35
  33.4 0.9 %collective-permute-start.12 = (bf16[256,384]{1,0:T(8,128)(2,1)S(1)}, bf16[256,384]{1,0:T(8,128)(2,1)S(1)}, u32[]{:S(2)}, u32[]{:S(2)}) collective-permute-start(bf16[256,384]{1,0:T(8,128)(2,1)S(1)} %get-tuple-element.61), channel_id=1, source_target_pairs={{0,8},{4,12},{8,0},{12,4},{16,24},{20,28},{24,16},{28,20},{1,9},{5... | collective-permute-start | bytes 589832 | tf_op jit(solution)/shard_map/ppermute | solution.py:35
  34.4 3.1 %collective-permute-done.13.pair_ref = bf16[384,128]{1,0:T(8,128)(2,1)S(1)} collective-permute-done((bf16[384,128]{1,0:T(8,128)(2,1)S(1)}, bf16[384,128]{1,0:T(8,128)(2,1)S(1)}, u32[]{:S(2)}, u32[]{:S(2)}) %collective-permute-start.13) | collective-permute-done | bytes 98336 | tf_op jit(solution)/shard_map/ppermute | solution.py:35
  37.5 0.6 %project.1 = (f32[128,768]{1,0:T(8,128)S(1)}, f32[128,768]{1,0:T(8,128)S(1)}, bf16[128,768]{1,0:T(8,128)(2,1)S(1)}, bf16[128,384]{1,0:T(8,128)(2,1)S(1)}, bf16[128,384]{1,0:T(8,128)(2,1)S(1)}) custom-call(f32[384,128]{1,0:T(8,128)S(1)} %get-tuple-element.62.own_ref, bf16[384,128]{1,0:T(8,128)(2,1)S(1)} %collective-permute-done.13.pair_ref, ...), custom_call_target="tpu_custom_call" | custom-call | bytes 2214000 | tf_op jit(solution)/shard_map/project/pallas_call | solution.py:44
  38.1 0.1 collective-permute-start.14
  38.2 0.5 collective-permute-start.15
  38.7 0.1 collective-permute-start.16
  38.8 1.0 %collective-permute-done.15.left_ref = bf16[128,384]{1,0:T(8,128)(2,1)S(1)} collective-permute-done((bf16[128,384]{1,0:T(8,128)(2,1)S(1)}, bf16[128,384]{1,0:T(8,128)(2,1)S(1)}, u32[]{:S(2)}, u32[]{:S(2)}) %collective-permute-start.15) | collective-permute-done | bytes 98336 | tf_op jit(solution)/shard_map/ppermute | solution.py:35
  39.8 0.2 collective-permute-done.16.right_ref
  40.0 0.3 collective-permute-start.17
  40.3 0.6 %collective-permute-start.18 = (bf16[128,384]{1,0:T(8,128)(2,1)S(1)}, bf16[128,384]{1,0:T(8,128)(2,1)S(1)}, u32[]{:S(2)}, u32[]{:S(2)}) collective-permute-start(bf16[128,384]{1,0:T(8,128)(2,1)S(1)} %get-tuple-element.71), channel_id=1, source_target_pairs={{0,16},{4,20},{8,24},{12,28},{16,0},{20,4},{24,8},{28,12},{1,17},{... | collective-permute-start | bytes 294920 | tf_op jit(solution)/shard_map/ppermute | solution.py:35
  40.9 0.1 pass_on.1
  41.0 1.6 %collective-permute-start.19 = (bf16[128,384]{1,0:T(8,128)(2,1)S(1)}, bf16[128,384]{1,0:T(8,128)(2,1)S(1)}, u32[]{:S(2)}, u32[]{:S(2)}) collective-permute-start(bf16[128,384]{1,0:T(8,128)(2,1)S(1)} %get-tuple-element.73), channel_id=1, source_target_pairs={{0,8},{4,12},{8,0},{12,4},{16,24},{20,28},{24,16},{28,20},{1,9},{5... | collective-permute-start | bytes 294920 | tf_op jit(solution)/shard_map/ppermute | solution.py:35
  42.6 1.3 %collective-permute-start.21 = (bf16[128,384]{1,0:T(8,128)(2,1)S(1)}, bf16[128,384]{1,0:T(8,128)(2,1)S(1)}, u32[]{:S(2)}, u32[]{:S(2)}) collective-permute-start(bf16[128,384]{1,0:T(8,128)(2,1)S(1)} %get-tuple-element.75), channel_id=1, source_target_pairs={{0,4},{4,0},{8,12},{12,8},{16,20},{20,16},{24,28},{28,24},{1,5},{5... | collective-permute-start | bytes 294920 | tf_op jit(solution)/shard_map/ppermute | solution.py:35
  43.9 0.4 collective-permute-start.20
  44.3 3.5 %collective-permute-done.18.dq_pair_ref = bf16[128,384]{1,0:T(8,128)(2,1)S(1)} collective-permute-done((bf16[128,384]{1,0:T(8,128)(2,1)S(1)}, bf16[128,384]{1,0:T(8,128)(2,1)S(1)}, u32[]{:S(2)}, u32[]{:S(2)}) %collective-permute-start.18) | collective-permute-done | bytes 98336 | tf_op jit(solution)/shard_map/ppermute | solution.py:35
  47.8 1.0 %collective-permute-done.20.rest_h_ref = bf16[64,384]{1,0:T(8,128)(2,1)S(1)} collective-permute-done((bf16[64,384]{1,0:T(8,128)(2,1)S(1)}, bf16[64,384]{1,0:T(8,128)(2,1)S(1)}, u32[]{:S(2)}, u32[]{:S(2)}) %collective-permute-start.20) | collective-permute-done | bytes 49184 | tf_op jit(solution)/shard_map/ppermute | solution.py:35
  48.8 0.9 %finish.1 = (bf16[128,384]{1,0:T(8,128)(2,1)}, bf16[128,384]{1,0:T(8,128)(2,1)}, bf16[128,384]{1,0:T(8,128)(2,1)}, bf16[32,384]{1,0:T(8,128)(2,1)}, bf16[32,384]{1,0:T(8,128)(2,1)}, /*index=5*/bf16[128,768]{1,0:T(8,128)(2,1)}) custom-call(f32[128,768]{1,0:T(8,128)S(1)} %get-tuple-element.66.keep_ref, bf16[128,768]{1,0:T(8,128)(2,1)S(1)} %collective-permute-done.17.near_ref, ...), custom_call_target="tpu_custom_call" | custom-call | bytes 3321000 | tf_op jit(solution)/shard_map/finish/pallas_call | solution.py:44
  (22 shorter events, 0.1 us)
Async XLA Ops:
  0.6 9.5 %collective-permute-start.4 = (bf16[128,768]{1,0:T(8,128)(2,1)}, bf16[128,768]{1,0:T(8,128)(2,1)S(1)}, u32[]{:S(2)}, u32[]{:S(2)}) collective-permute-start(bf16[128,768]{1,0:T(8,128)(2,1)} %own_ref.1), channel_id=1, source_target_pairs={{0,2},{1,3},{2,0},{3,1},{4,6},{5,7},{6,4},{7,5},{8,10},{9,11},{10,... | collective-permute-start | bytes 589832 | tf_op jit(solution)/shard_map/ppermute | solution.py:35
  5.3 5.4 %copy-start.2 = (bf16[128,384]{1,0:T(8,128)(2,1)S(1)}, bf16[128,384]{1,0:T(8,128)(2,1)}, u32[]{:S(2)}) copy-start(bf16[128,384]{1,0:T(8,128)(2,1)} %q_own_ref.3) | copy-start | bytes 294916
  5.3 8.0 %copy-start.3 = (bf16[128,768]{1,0:T(8,128)(2,1)S(1)}, bf16[128,768]{1,0:T(8,128)(2,1)}, u32[]{:S(2)}) copy-start(bf16[128,768]{1,0:T(8,128)(2,1)} %own_ref.1) | copy-start | bytes 589828
  5.3 8.9 %collective-permute-start.2 = (bf16[320,384]{1,0:T(8,128)(2,1)}, bf16[320,384]{1,0:T(8,128)(2,1)S(1)}, u32[]{:S(2)}, u32[]{:S(2)}) collective-permute-start(bf16[320,384]{1,0:T(8,128)(2,1)} %load.1.kv0), channel_id=1, source_target_pairs={{0,8},{4,12},{8,0},{12,4},{16,24},{20,28},{24,16},{28,20},{1,9},{5... | collective-permute-start | bytes 737288 | tf_op jit(solution)/shard_map/ppermute | solution.py:35
  7.0 7.3 %collective-permute-start.1 = (bf16[320,384]{1,0:T(8,128)(2,1)}, bf16[320,384]{1,0:T(8,128)(2,1)S(1)}, u32[]{:S(2)}, u32[]{:S(2)}) collective-permute-start(bf16[320,384]{1,0:T(8,128)(2,1)} %load.1.kv0), channel_id=1, source_target_pairs={{0,4},{4,0},{8,12},{12,8},{16,20},{20,16},{24,28},{28,24},{1,5},{5... | collective-permute-start | bytes 737288 | tf_op jit(solution)/shard_map/ppermute | solution.py:35
  8.5 4.9 %collective-permute-start.3 = (bf16[128,768]{1,0:T(8,128)(2,1)}, bf16[128,768]{1,0:T(8,128)(2,1)S(1)}, u32[]{:S(2)}, u32[]{:S(2)}) collective-permute-start(bf16[128,768]{1,0:T(8,128)(2,1)} %own_ref.1), channel_id=1, source_target_pairs={{0,1},{1,0},{2,3},{3,2},{4,5},{5,4},{6,7},{7,6},{8,9},{9,8},{10,11... | collective-permute-start | bytes 589832 | tf_op jit(solution)/shard_map/ppermute | solution.py:35
  10.1 10.4 %copy-start.5 = (s32[8,2]{0,1:T(2,128)S(1)}, s32[8,2]{0,1:T(2,128)}, u32[]{:S(2)}) copy-start(s32[8,2]{0,1:T(2,128)} %param.14) | copy-start | bytes 196
  10.1 10.5 %copy-start.4 = (s32[8]{0:T(128)S(1)}, s32[8]{0:T(128)}, u32[]{:S(2)}) copy-start(s32[8]{0:T(128)} %counts_ref.1) | copy-start | bytes 100
  10.2 13.7 %copy-start.1 = (bf16[320,384]{1,0:T(8,128)(2,1)S(1)}, bf16[320,384]{1,0:T(8,128)(2,1)}, u32[]{:S(2)}) copy-start(bf16[320,384]{1,0:T(8,128)(2,1)} %load.1.kv0) | copy-start | bytes 737284
  10.2 3.2 %collective-permute-start.5 = (bf16[128,768]{1,0:T(8,128)(2,1)S(1)}, bf16[128,768]{1,0:T(8,128)(2,1)S(1)}, u32[]{:S(2)}, u32[]{:S(2)}) collective-permute-start(bf16[128,768]{1,0:T(8,128)(2,1)S(1)} %collective-permute-done.4.near_ref), channel_id=1, source_target_pairs={{0,1},{1,0},{2,3},{3,2},{4,5},{5,4},{6,7},{7,6},{8,9},{9,8},{10,11... | collective-permute-start | bytes 589832 | tf_op jit(solution)/shard_map/ppermute | solution.py:35
  10.8 10.5 %collective-permute-start = (bf16[128,384]{1,0:T(8,128)(2,1)S(1)}, bf16[128,384]{1,0:T(8,128)(2,1)S(1)}, u32[]{:S(2)}, u32[]{:S(2)}) collective-permute-start(bf16[128,384]{1,0:T(8,128)(2,1)S(1)} %copy-done.2), channel_id=1, source_target_pairs={{0,16},{4,20},{8,24},{12,28},{16,0},{20,4},{24,8},{28,12},{1,17},{... | collective-permute-start | bytes 294920 | tf_op jit(solution)/shard_map/ppermute | solution.py:35
  14.3 10.6 %collective-permute-start.6 = (bf16[128,384]{1,0:T(8,128)(2,1)S(1)}, bf16[128,384]{1,0:T(8,128)(2,1)S(1)}, u32[]{:S(2)}, u32[]{:S(2)}) collective-permute-start(bf16[128,384]{1,0:T(8,128)(2,1)S(1)} %dattn.1.d_own_ref), channel_id=1, source_target_pairs={{0,16},{4,20},{8,24},{12,28},{16,0},{20,4},{24,8},{28,12},{1,17},{... | collective-permute-start | bytes 294920 | tf_op jit(solution)/shard_map/ppermute | solution.py:35
  16.9 4.7 %collective-permute-start.7 = (bf16[320,128]{1,0:T(8,128)(2,1)S(1)}, bf16[320,128]{1,0:T(8,128)(2,1)S(1)}, u32[]{:S(2)}, u32[]{:S(2)}) collective-permute-start(bf16[320,128]{1,0:T(8,128)(2,1)S(1)} %get-tuple-element.49), channel_id=1, source_target_pairs={{0,4},{4,0},{8,12},{12,8},{16,20},{20,16},{24,28},{28,24},{1,5},{5... | collective-permute-start | bytes 245768 | tf_op jit(solution)/shard_map/ppermute | solution.py:35
  18.5 4.4 %collective-permute-start.8 = (bf16[320,128]{1,0:T(8,128)(2,1)S(1)}, bf16[320,128]{1,0:T(8,128)(2,1)S(1)}, u32[]{:S(2)}, u32[]{:S(2)}) collective-permute-start(bf16[320,128]{1,0:T(8,128)(2,1)S(1)} %get-tuple-element.50), channel_id=1, source_target_pairs={{0,4},{4,0},{8,12},{12,8},{16,20},{20,16},{24,28},{28,24},{1,5},{5... | collective-permute-start | bytes 245768 | tf_op jit(solution)/shard_map/ppermute | solution.py:35
  19.0 4.8 %collective-permute-start.9 = (bf16[320,128]{1,0:T(8,128)(2,1)S(1)}, bf16[320,128]{1,0:T(8,128)(2,1)S(1)}, u32[]{:S(2)}, u32[]{:S(2)}) collective-permute-start(bf16[320,128]{1,0:T(8,128)(2,1)S(1)} %get-tuple-element.51), channel_id=1, source_target_pairs={{0,4},{4,0},{8,12},{12,8},{16,20},{20,16},{24,28},{28,24},{1,5},{5... | collective-permute-start | bytes 245768 | tf_op jit(solution)/shard_map/ppermute | solution.py:35
  25.3 5.9 %collective-permute-start.10 = (f32[16,256]{1,0:T(8,128)S(1)}, f32[16,256]{1,0:T(8,128)S(1)}, u32[]{:S(2)}, u32[]{:S(2)}) collective-permute-start(f32[16,256]{1,0:T(8,128)S(1)} %get-tuple-element.54.stats_ref), channel_id=1, source_target_pairs={{0,16},{4,20},{8,24},{12,28},{16,0},{20,4},{24,8},{28,12},{1,17},{... | collective-permute-start | bytes 49160 | tf_op jit(solution)/shard_map/ppermute | solution.py:35
  31.6 5.9 %copy-start = (bf16[384,3072]{1,0:T(8,128)(2,1)S(1)}, bf16[384,3072]{1,0:T(8,128)(2,1)}, u32[]{:S(2)}) copy-start(bf16[384,3072]{1,0:T(8,128)(2,1)} %w_ref.3) | copy-start | bytes 7077892
  31.6 5.9 %collective-permute-start.13 = (bf16[384,128]{1,0:T(8,128)(2,1)S(1)}, bf16[384,128]{1,0:T(8,128)(2,1)S(1)}, u32[]{:S(2)}, u32[]{:S(2)}) collective-permute-start(bf16[384,128]{1,0:T(8,128)(2,1)S(1)} %get-tuple-element.63), channel_id=1, source_target_pairs={{0,16},{4,20},{8,24},{12,28},{16,0},{20,4},{24,8},{28,12},{1,17},{... | collective-permute-start | bytes 294920 | tf_op jit(solution)/shard_map/ppermute | solution.py:35
  32.8 8.1 %collective-permute-start.11 = (bf16[384,384]{1,0:T(8,128)(2,1)S(1)}, bf16[384,384]{1,0:T(8,128)(2,1)S(1)}, u32[]{:S(2)}, u32[]{:S(2)}) collective-permute-start(bf16[384,384]{1,0:T(8,128)(2,1)S(1)} %get-tuple-element.60), channel_id=1, source_target_pairs={{0,4},{4,0},{8,12},{12,8},{16,20},{20,16},{24,28},{28,24},{1,5},{5... | collective-permute-start | bytes 884744 | tf_op jit(solution)/shard_map/ppermute | solution.py:35
  33.4 7.5 %collective-permute-start.12 = (bf16[256,384]{1,0:T(8,128)(2,1)S(1)}, bf16[256,384]{1,0:T(8,128)(2,1)S(1)}, u32[]{:S(2)}, u32[]{:S(2)}) collective-permute-start(bf16[256,384]{1,0:T(8,128)(2,1)S(1)} %get-tuple-element.61), channel_id=1, source_target_pairs={{0,8},{4,12},{8,0},{12,4},{16,24},{20,28},{24,16},{28,20},{1,9},{5... | collective-permute-start | bytes 589832 | tf_op jit(solution)/shard_map/ppermute | solution.py:35
  38.1 2.8 %collective-permute-start.14 = (bf16[128,768]{1,0:T(8,128)(2,1)S(1)}, bf16[128,768]{1,0:T(8,128)(2,1)S(1)}, u32[]{:S(2)}, u32[]{:S(2)}) collective-permute-start(bf16[128,768]{1,0:T(8,128)(2,1)S(1)} %get-tuple-element.65), channel_id=1, source_target_pairs={{0,1},{1,0},{2,3},{3,2},{4,5},{5,4},{6,7},{7,6},{8,9},{9,8},{10,11... | collective-permute-start | bytes 589832 | tf_op jit(solution)/shard_map/ppermute | solution.py:35
  38.2 1.6 %collective-permute-start.15 = (bf16[128,384]{1,0:T(8,128)(2,1)S(1)}, bf16[128,384]{1,0:T(8,128)(2,1)S(1)}, u32[]{:S(2)}, u32[]{:S(2)}) collective-permute-start(bf16[128,384]{1,0:T(8,128)(2,1)S(1)} %get-tuple-element.68), channel_id=1, source_target_pairs={{0,1},{1,0},{2,3},{3,2},{4,5},{5,4},{6,7},{7,6},{8,9},{9,8},{10,11... | collective-permute-start | bytes 294920 | tf_op jit(solution)/shard_map/ppermute | solution.py:35
  38.7 1.3 %collective-permute-start.16 = (bf16[128,384]{1,0:T(8,128)(2,1)S(1)}, bf16[128,384]{1,0:T(8,128)(2,1)S(1)}, u32[]{:S(2)}, u32[]{:S(2)}) collective-permute-start(bf16[128,384]{1,0:T(8,128)(2,1)S(1)} %get-tuple-element.69), channel_id=1, source_target_pairs={{0,1},{1,0},{2,3},{3,2},{4,5},{5,4},{6,7},{7,6},{8,9},{9,8},{10,11... | collective-permute-start | bytes 294920 | tf_op jit(solution)/shard_map/ppermute | solution.py:35
  40.0 8.8 %collective-permute-start.17 = (bf16[128,768]{1,0:T(8,128)(2,1)S(1)}, bf16[128,768]{1,0:T(8,128)(2,1)S(1)}, u32[]{:S(2)}, u32[]{:S(2)}) collective-permute-start(bf16[128,768]{1,0:T(8,128)(2,1)S(1)} %add_near.1), channel_id=1, source_target_pairs={{0,2},{1,3},{2,0},{3,1},{4,6},{5,7},{6,4},{7,5},{8,10},{9,11},{10,... | collective-permute-start | bytes 589832 | tf_op jit(solution)/shard_map/ppermute | solution.py:35
  40.3 7.5 %collective-permute-start.18 = (bf16[128,384]{1,0:T(8,128)(2,1)S(1)}, bf16[128,384]{1,0:T(8,128)(2,1)S(1)}, u32[]{:S(2)}, u32[]{:S(2)}) collective-permute-start(bf16[128,384]{1,0:T(8,128)(2,1)S(1)} %get-tuple-element.71), channel_id=1, source_target_pairs={{0,16},{4,20},{8,24},{12,28},{16,0},{20,4},{24,8},{28,12},{1,17},{... | collective-permute-start | bytes 294920 | tf_op jit(solution)/shard_map/ppermute | solution.py:35
  41.0 7.8 %collective-permute-start.19 = (bf16[128,384]{1,0:T(8,128)(2,1)S(1)}, bf16[128,384]{1,0:T(8,128)(2,1)S(1)}, u32[]{:S(2)}, u32[]{:S(2)}) collective-permute-start(bf16[128,384]{1,0:T(8,128)(2,1)S(1)} %get-tuple-element.73), channel_id=1, source_target_pairs={{0,8},{4,12},{8,0},{12,4},{16,24},{20,28},{24,16},{28,20},{1,9},{5... | collective-permute-start | bytes 294920 | tf_op jit(solution)/shard_map/ppermute | solution.py:35
  42.6 6.2 %collective-permute-start.21 = (bf16[128,384]{1,0:T(8,128)(2,1)S(1)}, bf16[128,384]{1,0:T(8,128)(2,1)S(1)}, u32[]{:S(2)}, u32[]{:S(2)}) collective-permute-start(bf16[128,384]{1,0:T(8,128)(2,1)S(1)} %get-tuple-element.75), channel_id=1, source_target_pairs={{0,4},{4,0},{8,12},{12,8},{16,20},{20,16},{24,28},{28,24},{1,5},{5... | collective-permute-start | bytes 294920 | tf_op jit(solution)/shard_map/ppermute | solution.py:35
  43.9 4.9 %collective-permute-start.20 = (bf16[64,384]{1,0:T(8,128)(2,1)S(1)}, bf16[64,384]{1,0:T(8,128)(2,1)S(1)}, u32[]{:S(2)}, u32[]{:S(2)}) collective-permute-start(bf16[64,384]{1,0:T(8,128)(2,1)S(1)} %get-tuple-element.74), channel_id=1, source_target_pairs={{0,8},{4,12},{8,0},{12,4},{16,24},{20,28},{24,16},{28,20},{1,9},{5... | collective-permute-start | bytes 147464 | tf_op jit(solution)/shard_map/ppermute | solution.py:35

commit v20 on v18

--- a/solution.py
+++ b/solution.py
@@ -300,17 +300,17 @@
         dq_pair_ref[:, features] = (dquery[rows:] * SCALE).astype(BF16)
 
 
-def pass_on_kernel(
-    near_y_ref, near_z_ref, got_y_ref, got_z_ref, keep_ref, core_ref,
-    key_ref, hist_ref, value_ref, sum_ref,
-):
+def pass_values_kernel(near_ref, got_ref, keep_ref, core_ref, value_ref, sum_ref):
+    rows = value_ref.shape[0]
+    value_ref[...] = (near_ref[...] + got_ref[rows:].astype(F32)).astype(BF16)
+    sum_ref[...] = keep_ref[...] + core_ref[...].astype(F32)
+
+
+def pass_keys_kernel(near_ref, got_ref, key_ref, hist_ref):
     rows = key_ref.shape[0]
-    wide = near_y_ref.shape[0]
-    total_y = near_y_ref[...] + got_y_ref[wide:].astype(F32)
-    key_ref[...] = total_y[:rows].astype(BF16)
-    hist_ref[...] = total_y[rows:].astype(BF16)
-    value_ref[...] = (near_z_ref[...] + got_z_ref[rows:].astype(F32)).astype(BF16)
-    sum_ref[...] = keep_ref[...] + core_ref[...].astype(F32)
+    total = near_ref[...] + got_ref[near_ref.shape[0] :].astype(F32)
+    key_ref[...] = total[:rows].astype(BF16)
+    hist_ref[...] = total[rows:].astype(BF16)
 
 
 def finish_kernel(
@@ -435,13 +435,19 @@
     )
     dq_got = swap(dq_pair, "ctx", PAIR)
     out_core = swap(out_core, "head", 1)
-    rest_k, rest_h, rest_v, out_keep = local_call(
-        pass_on_kernel,
-        "pass_on",
+    rest_v, out_keep = local_call(
+        pass_values_kernel,
+        "pass_values",
         0.1,
-        [shape((size, width), BF16) for size in (rows, 2 * capacity, rows)]
-        + [shape((rows, share), F32)],
-        (near_y, near_z, got_y, got_z, out_keep, out_core),
+        [shape((rows, width), BF16), shape((rows, share), F32)],
+        (near_z, got_z, out_keep, out_core),
+    )
+    rest_k, rest_h = local_call(
+        pass_keys_kernel,
+        "pass_keys",
+        0.1,
+        [shape((rows, width), BF16), shape((2 * capacity, width), BF16)],
+        (near_y, got_y),
     )
     rest_k = swap(rest_k, "ctx", 2)
     rest_h = swap(rest_h, "ctx", 2)

time: 46.9 us -> 47.4 us (1.011)
  starting transfers between devices: 26.2 us -> 26.8 us
    ppermute x22, starting transfers between devices: 26.2 us -> 26.8 us  [swap(): return lax.ppermute(block, axis, [(i, i ^ bit) for i in range(count)])]
    pallas_call x11 -> x12, Pallas kernels: 6.09 us -> 6.09 us  [local_call(): pl.pallas_call(body, name=name, out_shape=out_shapes, in_specs=[pl.BlockS...]
  transfers between devices with their start and end apart: 22 -> 22, of which waited for: 8 -> 7; matrix products, arithmetic and copies ran while one was open for 0% -> 0% of each run, Pallas kernels for 18% -> 18%
where the time goes in v20:
time: 47.4 us; the launch traced here: 47.2 us
  starting transfers between devices  26.8 us (57%)
  waiting for transfers between devices  9.99 us (21%)
  Pallas kernels  9.39 us (20%)
  between operations  0.84 us (2%)
    ppermute x22, starting transfers between devices, swap(): return lax.ppermute(block, axis, [(i, i ^ bit) for i in range(count)])  26.8 us
    ppermute x22, waiting for transfers between devices, swap(): return lax.ppermute(block, axis, [(i, i ^ bit) for i in range(count)])  9.99 us
    pallas_call x12, Pallas kernels, local_call(): pl.pallas_call(body, name=name, out_shape=out_shapes, in_specs=[pl.BlockS...  6.09 us
    pallas_call x1, Pallas kernels, load_keys(): pl.pallas_call(load_kernel, name='load', out_shape=jax.ShapeDtypeStruct((...  1.67 us
    pallas_call x1, Pallas kernels, load_weight(): pl.pallas_call(load_weight_kernel, name='load_w', out_shape=jax.ShapeDtyp...  1.63 us
  transfers between devices with their start and end apart: 22, of which 7 were waited for; matrix products, arithmetic and copies ran while one was open for 0% of the time, Pallas kernels for 18%

profile of v20, /device:TPU:0, one launch (start us, length us, event | category | flops | bytes accessed | tf_op | source)
XLA Modules:
  0.0 47.2 jit_solution(15959745206696621267)
XLA Ops:
  0.6 3.0 %collective-permute-start.4 = (bf16[128,768]{1,0:T(8,128)(2,1)}, bf16[128,768]{1,0:T(8,128)(2,1)S(1)}, u32[]{:S(2)}, u32[]{:S(2)}) collective-permute-start(bf16[128,768]{1,0:T(8,128)(2,1)} %own_ref.1), channel_id=1, source_target_pairs={{0,2},{1,3},{2,0},{3,1},{4,6},{5,7},{6,4},{7,5},{8,10},{9,11},{10,... | collective-permute-start | bytes 589832 | tf_op jit(solution)/shard_map/ppermute | solution.py:35
  3.6 1.7 %load.1.kv0 = bf16[320,384]{1,0:T(8,128)(2,1)} custom-call(bf16[128,384]{1,0:T(8,128)(2,1)} %k_ref.1, bf16[32,384]{1,0:T(8,128)(2,1)} %hk_ref.1, bf16[128,384]{1,0:T(8,128)(2,1)} %v_ref.1, bf16[32,384]{1,0:T(8,128)(2,1)} %hv_ref.1), custom_call_target="tpu_custom_call" | custom-call | bytes 5904000 | tf_op jit(solution)/shard_map/load/pallas_call | solution.py:74
  5.3 0.0 copy-start.2
  5.3 0.0 copy-start.3
  5.3 1.6 %collective-permute-start.2 = (bf16[320,384]{1,0:T(8,128)(2,1)}, bf16[320,384]{1,0:T(8,128)(2,1)S(1)}, u32[]{:S(2)}, u32[]{:S(2)}) collective-permute-start(bf16[320,384]{1,0:T(8,128)(2,1)} %load.1.kv0), channel_id=1, source_target_pairs={{0,8},{4,12},{8,0},{12,4},{16,24},{20,28},{24,16},{28,20},{1,9},{5... | collective-permute-start | bytes 737288 | tf_op jit(solution)/shard_map/ppermute | solution.py:35
  7.0 1.5 %collective-permute-start.1 = (bf16[320,384]{1,0:T(8,128)(2,1)}, bf16[320,384]{1,0:T(8,128)(2,1)S(1)}, u32[]{:S(2)}, u32[]{:S(2)}) collective-permute-start(bf16[320,384]{1,0:T(8,128)(2,1)} %load.1.kv0), channel_id=1, source_target_pairs={{0,4},{4,0},{8,12},{12,8},{16,20},{20,16},{24,28},{28,24},{1,5},{5... | collective-permute-start | bytes 737288 | tf_op jit(solution)/shard_map/ppermute | solution.py:35
  8.5 0.0 collective-permute-start.3
  8.5 1.6 %load_w.1.w_ref = bf16[384,3072]{1,0:T(8,128)(2,1)S(1)} custom-call(bf16[384,3072]{1,0:T(8,128)(2,1)} %w_ref.3), custom_call_target="tpu_custom_call" | custom-call | bytes 5904000 | tf_op jit(solution)/shard_map/load_w/pallas_call | solution.py:113
  10.1 0.0 copy-start.5
  10.2 0.0 copy-start.4
  10.2 0.0 collective-permute-done.4.near_ref
  10.2 0.6 %collective-permute-start.5 = (bf16[128,768]{1,0:T(8,128)(2,1)S(1)}, bf16[128,768]{1,0:T(8,128)(2,1)S(1)}, u32[]{:S(2)}, u32[]{:S(2)}) collective-permute-start(bf16[128,768]{1,0:T(8,128)(2,1)S(1)} %collective-permute-done.4.near_ref), channel_id=1, source_target_pairs={{0,1},{1,0},{2,3},{3,2},{4,5},{5,4},{6,7},{7,6},{8,9},{9,8},{10,11... | collective-permute-start | bytes 589832 | tf_op jit(solution)/shard_map/ppermute | solution.py:35
  10.8 2.6 %collective-permute-start = (bf16[128,384]{1,0:T(8,128)(2,1)S(1)}, bf16[128,384]{1,0:T(8,128)(2,1)S(1)}, u32[]{:S(2)}, u32[]{:S(2)}) collective-permute-start(bf16[128,384]{1,0:T(8,128)(2,1)S(1)} %copy-done.2), channel_id=1, source_target_pairs={{0,16},{4,20},{8,24},{12,28},{16,0},{20,4},{24,8},{28,12},{1,17},{... | collective-permute-start | bytes 294920 | tf_op jit(solution)/shard_map/ppermute | solution.py:35
  13.4 0.0 collective-permute-done.5.far_ref
  13.4 0.8 %dattn.1.d_own_ref = bf16[128,384]{1,0:T(8,128)(2,1)S(1)} custom-call(bf16[128,768]{1,0:T(8,128)(2,1)S(1)} %copy-done.3, bf16[128,768]{1,0:T(8,128)(2,1)S(1)} %collective-permute-done.3.core_ref, bf16[128,768]{1,0:T(8,128)(2,1)S(1)} %collective-permute-done.4.near_ref, bf16[128,768]{1,0:T(8,128)(2,1)S(1)} %collective-permute-done.5.far_ref, ...), custom_call_target="tpu_custom_call" | custom-call | bytes 2952000 | tf_op jit(solution)/shard_map/dattn/pallas_call | solution.py:44
  14.2 0.0 collective-permute-done.2.kv_ref.kv2
  14.2 0.1 collective-permute-done.1.kv1
  14.4 1.6 %collective-permute-start.7 = (bf16[320,128]{1,0:T(8,128)(2,1)S(1)}, bf16[320,128]{1,0:T(8,128)(2,1)S(1)}, u32[]{:S(2)}, u32[]{:S(2)}) collective-permute-start(bf16[320,128]{1,0:T(8,128)(2,1)S(1)} %get-tuple-element.52), channel_id=1, source_target_pairs={{0,4},{4,0},{8,12},{12,8},{16,20},{20,16},{24,28},{28,24},{1,5},{5... | collective-permute-start | bytes 245768 | tf_op jit(solution)/shard_map/ppermute | solution.py:35
  15.9 0.5 %collective-permute-start.8 = (bf16[320,128]{1,0:T(8,128)(2,1)S(1)}, bf16[320,128]{1,0:T(8,128)(2,1)S(1)}, u32[]{:S(2)}, u32[]{:S(2)}) collective-permute-start(bf16[320,128]{1,0:T(8,128)(2,1)S(1)} %get-tuple-element.53), channel_id=1, source_target_pairs={{0,4},{4,0},{8,12},{12,8},{16,20},{20,16},{24,28},{28,24},{1,5},{5... | collective-permute-start | bytes 245768 | tf_op jit(solution)/shard_map/ppermute | solution.py:35
  16.5 1.5 %collective-permute-start.9 = (bf16[320,128]{1,0:T(8,128)(2,1)S(1)}, bf16[320,128]{1,0:T(8,128)(2,1)S(1)}, u32[]{:S(2)}, u32[]{:S(2)}) collective-permute-start(bf16[320,128]{1,0:T(8,128)(2,1)S(1)} %get-tuple-element.54), channel_id=1, source_target_pairs={{0,4},{4,0},{8,12},{12,8},{16,20},{20,16},{24,28},{28,24},{1,5},{5... | collective-permute-start | bytes 245768 | tf_op jit(solution)/shard_map/ppermute | solution.py:35
  18.0 2.6 %collective-permute-start.6 = (bf16[128,384]{1,0:T(8,128)(2,1)S(1)}, bf16[128,384]{1,0:T(8,128)(2,1)S(1)}, u32[]{:S(2)}, u32[]{:S(2)}) collective-permute-start(bf16[128,384]{1,0:T(8,128)(2,1)S(1)} %dattn.1.d_own_ref), channel_id=1, source_target_pairs={{0,16},{4,20},{8,24},{12,28},{16,0},{20,4},{24,8},{28,12},{1,17},{... | collective-permute-start | bytes 294920 | tf_op jit(solution)/shard_map/ppermute | solution.py:35
  20.6 0.1 copy.15.levels_ref
  20.7 0.6 %limits.1.limits_ref = s32[8,256]{1,0:T(8,128)S(1)} custom-call(s32[8,2]{1,0:T(8,128)S(1)} %copy.15.levels_ref, s32[8]{0:T(128)S(1)} %copy-done.4), custom_call_target="tpu_custom_call" | custom-call | bytes 2214000 | tf_op jit(solution)/shard_map/limits/pallas_call | solution.py:44
  21.3 0.7 %collective-permute-done.9.refs_2_ = bf16[320,128]{1,0:T(8,128)(2,1)S(1)} collective-permute-done((bf16[320,128]{1,0:T(8,128)(2,1)S(1)}, bf16[320,128]{1,0:T(8,128)(2,1)S(1)}, u32[]{:S(2)}, u32[]{:S(2)}) %collective-permute-start.9) | collective-permute-done | bytes 81952 | tf_op jit(solution)/shard_map/ppermute | solution.py:35
  22.0 1.0 %scores.1 = (f32[8,256]{1,0:T(8,128)S(1)}, bf16[1920,256]{1,0:T(8,128)(2,1)S(1)}) custom-call(s32[8,256]{1,0:T(8,128)S(1)} %limits.1.limits_ref, bf16[128,384]{1,0:T(8,128)(2,1)S(1)} %copy-done.2, bf16[128,384]{1,0:T(8,128)(2,1)S(1)} %collective-permute-done.q_pair_ref, bf16[320,384]{1,0:T(8,128)(2,1)S(1)} %copy-done.1, ...), custom_call_target="tpu_custom_call" | custom-call | bytes 3321000 | tf_op jit(solution)/shard_map/scores/pallas_call | solution.py:44
  23.0 0.4 attn.1
  23.5 1.9 %collective-permute-start.11 = (bf16[384,128]{1,0:T(8,128)(2,1)S(1)}, bf16[384,128]{1,0:T(8,128)(2,1)S(1)}, u32[]{:S(2)}, u32[]{:S(2)}) collective-permute-start(bf16[384,128]{1,0:T(8,128)(2,1)S(1)} %get-tuple-element.62), channel_id=1, source_target_pairs={{0,16},{4,20},{8,24},{12,28},{16,0},{20,4},{24,8},{28,12},{1,17},{... | collective-permute-start | bytes 294920 | tf_op jit(solution)/shard_map/ppermute | solution.py:35
  25.4 0.4 delta.1
  25.8 0.0 copy-start
  25.8 1.2 %collective-permute-start.10 = (f32[16,256]{1,0:T(8,128)S(1)}, f32[16,256]{1,0:T(8,128)S(1)}, u32[]{:S(2)}, u32[]{:S(2)}) collective-permute-start(f32[16,256]{1,0:T(8,128)S(1)} %get-tuple-element.59.stats_ref), channel_id=1, source_target_pairs={{0,16},{4,20},{8,24},{12,28},{16,0},{20,4},{24,8},{28,12},{1,17},{... | collective-permute-start | bytes 49160 | tf_op jit(solution)/shard_map/ppermute | solution.py:35
  27.0 3.8 %collective-permute-done.10.stats_pair_ref = f32[16,256]{1,0:T(8,128)S(1)} collective-permute-done((f32[16,256]{1,0:T(8,128)S(1)}, f32[16,256]{1,0:T(8,128)S(1)}, u32[]{:S(2)}, u32[]{:S(2)}) %collective-permute-start.10) | collective-permute-done | bytes 16416 | tf_op jit(solution)/shard_map/ppermute | solution.py:35
  30.8 1.1 %backward.1 = (f32[128,384]{1,0:T(8,128)S(1)}, bf16[128,384]{1,0:T(8,128)(2,1)S(1)}, f32[320,384]{1,0:T(8,128)S(1)}, bf16[384,384]{1,0:T(8,128)(2,1)S(1)}, bf16[...) custom-call(bf16[128,384]{1,0:T(8,128)(2,1)S(1)} %copy-done.2, ...), custom_call_target="tpu_custom_call" | custom-call | bytes 4059000 | tf_op jit(solution)/shard_map/backward/pallas_call | solution.py:44
  31.9 1.0 %collective-permute-start.18 = (bf16[384,384]{1,0:T(8,128)(2,1)S(1)}, bf16[384,384]{1,0:T(8,128)(2,1)S(1)}, u32[]{:S(2)}, u32[]{:S(2)}) collective-permute-start(bf16[384,384]{1,0:T(8,128)(2,1)S(1)} %get-tuple-element.77), channel_id=1, source_target_pairs={{0,4},{4,0},{8,12},{12,8},{16,20},{20,16},{24,28},{28,24},{1,5},{5... | collective-permute-start | bytes 884744 | tf_op jit(solution)/shard_map/ppermute | solution.py:35
  32.9 0.4 collective-permute-start.12
  33.3 0.6 %project.1 = (f32[128,768]{1,0:T(8,128)S(1)}, f32[128,768]{1,0:T(8,128)S(1)}, bf16[128,768]{1,0:T(8,128)(2,1)S(1)}, bf16[128,384]{1,0:T(8,128)(2,1)S(1)}, bf16[128,384]{1,0:T(8,128)(2,1)S(1)}) custom-call(f32[384,128]{1,0:T(8,128)S(1)} %get-tuple-element.66.own_ref, bf16[384,128]{1,0:T(8,128)(2,1)S(1)} %collective-permute-done.11.pair_ref, ...), custom_call_target="tpu_custom_call" | custom-call | bytes 2214000 | tf_op jit(solution)/shard_map/project/pallas_call | solution.py:44
  34.0 0.1 collective-permute-start.13
  34.0 0.5 %collective-permute-start.14 = (bf16[128,384]{1,0:T(8,128)(2,1)S(1)}, bf16[128,384]{1,0:T(8,128)(2,1)S(1)}, u32[]{:S(2)}, u32[]{:S(2)}) collective-permute-start(bf16[128,384]{1,0:T(8,128)(2,1)S(1)} %get-tuple-element.72), channel_id=1, source_target_pairs={{0,1},{1,0},{2,3},{3,2},{4,5},{5,4},{6,7},{7,6},{8,9},{9,8},{10,11... | collective-permute-start | bytes 294920 | tf_op jit(solution)/shard_map/ppermute | solution.py:35
  34.5 0.1 collective-permute-start.15
  34.6 1.0 %collective-permute-done.14.left_ref = bf16[128,384]{1,0:T(8,128)(2,1)S(1)} collective-permute-done((bf16[128,384]{1,0:T(8,128)(2,1)S(1)}, bf16[128,384]{1,0:T(8,128)(2,1)S(1)}, u32[]{:S(2)}, u32[]{:S(2)}) %collective-permute-start.14) | collective-permute-done | bytes 98336 | tf_op jit(solution)/shard_map/ppermute | solution.py:35
  35.6 0.2 collective-permute-done.15.right_ref
  35.9 1.3 %collective-permute-start.16 = (bf16[128,768]{1,0:T(8,128)(2,1)S(1)}, bf16[128,768]{1,0:T(8,128)(2,1)S(1)}, u32[]{:S(2)}, u32[]{:S(2)}) collective-permute-start(bf16[128,768]{1,0:T(8,128)(2,1)S(1)} %add_near.1), channel_id=1, source_target_pairs={{0,2},{1,3},{2,0},{3,1},{4,6},{5,7},{6,4},{7,5},{8,10},{9,11},{10,... | collective-permute-start | bytes 589832 | tf_op jit(solution)/shard_map/ppermute | solution.py:35
  37.2 1.9 %collective-permute-start.17 = (bf16[128,384]{1,0:T(8,128)(2,1)S(1)}, bf16[128,384]{1,0:T(8,128)(2,1)S(1)}, u32[]{:S(2)}, u32[]{:S(2)}) collective-permute-start(bf16[128,384]{1,0:T(8,128)(2,1)S(1)} %get-tuple-element.75), channel_id=1, source_target_pairs={{0,16},{4,20},{8,24},{12,28},{16,0},{20,4},{24,8},{28,12},{1,17},{... | collective-permute-start | bytes 294920 | tf_op jit(solution)/shard_map/ppermute | solution.py:35
  39.1 0.9 %collective-permute-start.21 = (bf16[128,384]{1,0:T(8,128)(2,1)S(1)}, bf16[128,384]{1,0:T(8,128)(2,1)S(1)}, u32[]{:S(2)}, u32[]{:S(2)}) collective-permute-start(bf16[128,384]{1,0:T(8,128)(2,1)S(1)} %get-tuple-element.81), channel_id=1, source_target_pairs={{0,4},{4,0},{8,12},{12,8},{16,20},{20,16},{24,28},{28,24},{1,5},{5... | collective-permute-start | bytes 294920 | tf_op jit(solution)/shard_map/ppermute | solution.py:35
  40.1 0.3 collective-permute-start.19
  40.3 1.8 %collective-permute-start.20 = (bf16[64,384]{1,0:T(8,128)(2,1)S(1)}, bf16[64,384]{1,0:T(8,128)(2,1)S(1)}, u32[]{:S(2)}, u32[]{:S(2)}) collective-permute-start(bf16[64,384]{1,0:T(8,128)(2,1)S(1)} %get-tuple-element.80), channel_id=1, source_target_pairs={{0,8},{4,12},{8,0},{12,4},{16,24},{20,28},{24,16},{28,20},{1,9},{5... | collective-permute-start | bytes 147464 | tf_op jit(solution)/shard_map/ppermute | solution.py:35
  42.2 2.7 %collective-permute-done.17.dq_pair_ref = bf16[128,384]{1,0:T(8,128)(2,1)S(1)} collective-permute-done((bf16[128,384]{1,0:T(8,128)(2,1)S(1)}, bf16[128,384]{1,0:T(8,128)(2,1)S(1)}, u32[]{:S(2)}, u32[]{:S(2)}) %collective-permute-start.17) | collective-permute-done | bytes 98336 | tf_op jit(solution)/shard_map/ppermute | solution.py:35
  44.9 1.4 %collective-permute-done.20.rest_h_ref = bf16[64,384]{1,0:T(8,128)(2,1)S(1)} collective-permute-done((bf16[64,384]{1,0:T(8,128)(2,1)S(1)}, bf16[64,384]{1,0:T(8,128)(2,1)S(1)}, u32[]{:S(2)}, u32[]{:S(2)}) %collective-permute-start.20) | collective-permute-done | bytes 49184 | tf_op jit(solution)/shard_map/ppermute | solution.py:35
  46.3 0.9 %finish.1 = (bf16[128,384]{1,0:T(8,128)(2,1)}, bf16[128,384]{1,0:T(8,128)(2,1)}, bf16[128,384]{1,0:T(8,128)(2,1)}, bf16[32,384]{1,0:T(8,128)(2,1)}, bf16[32,384]{1,0:T(8,128)(2,1)}, /*index=5*/bf16[128,768]{1,0:T(8,128)(2,1)}) custom-call(f32[128,768]{1,0:T(8,128)S(1)} %get-tuple-element.70.keep_ref, bf16[128,768]{1,0:T(8,128)(2,1)S(1)} %collective-permute-done.16.near_ref, ...), custom_call_target="tpu_custom_call" | custom-call | bytes 3321000 | tf_op jit(solution)/shard_map/finish/pallas_call | solution.py:44
  (23 shorter events, 0.2 us)
Async XLA Ops:
  0.6 9.5 %collective-permute-start.4 = (bf16[128,768]{1,0:T(8,128)(2,1)}, bf16[128,768]{1,0:T(8,128)(2,1)S(1)}, u32[]{:S(2)}, u32[]{:S(2)}) collective-permute-start(bf16[128,768]{1,0:T(8,128)(2,1)} %own_ref.1), channel_id=1, source_target_pairs={{0,2},{1,3},{2,0},{3,1},{4,6},{5,7},{6,4},{7,5},{8,10},{9,11},{10,... | collective-permute-start | bytes 589832 | tf_op jit(solution)/shard_map/ppermute | solution.py:35
  5.3 5.4 %copy-start.2 = (bf16[128,384]{1,0:T(8,128)(2,1)S(1)}, bf16[128,384]{1,0:T(8,128)(2,1)}, u32[]{:S(2)}) copy-start(bf16[128,384]{1,0:T(8,128)(2,1)} %q_own_ref.3) | copy-start | bytes 294916
  5.3 8.0 %copy-start.3 = (bf16[128,768]{1,0:T(8,128)(2,1)S(1)}, bf16[128,768]{1,0:T(8,128)(2,1)}, u32[]{:S(2)}) copy-start(bf16[128,768]{1,0:T(8,128)(2,1)} %own_ref.1) | copy-start | bytes 589828
  5.3 8.9 %collective-permute-start.2 = (bf16[320,384]{1,0:T(8,128)(2,1)}, bf16[320,384]{1,0:T(8,128)(2,1)S(1)}, u32[]{:S(2)}, u32[]{:S(2)}) collective-permute-start(bf16[320,384]{1,0:T(8,128)(2,1)} %load.1.kv0), channel_id=1, source_target_pairs={{0,8},{4,12},{8,0},{12,4},{16,24},{20,28},{24,16},{28,20},{1,9},{5... | collective-permute-start | bytes 737288 | tf_op jit(solution)/shard_map/ppermute | solution.py:35
  7.0 7.3 %collective-permute-start.1 = (bf16[320,384]{1,0:T(8,128)(2,1)}, bf16[320,384]{1,0:T(8,128)(2,1)S(1)}, u32[]{:S(2)}, u32[]{:S(2)}) collective-permute-start(bf16[320,384]{1,0:T(8,128)(2,1)} %load.1.kv0), channel_id=1, source_target_pairs={{0,4},{4,0},{8,12},{12,8},{16,20},{20,16},{24,28},{28,24},{1,5},{5... | collective-permute-start | bytes 737288 | tf_op jit(solution)/shard_map/ppermute | solution.py:35
  8.5 4.9 %collective-permute-start.3 = (bf16[128,768]{1,0:T(8,128)(2,1)}, bf16[128,768]{1,0:T(8,128)(2,1)S(1)}, u32[]{:S(2)}, u32[]{:S(2)}) collective-permute-start(bf16[128,768]{1,0:T(8,128)(2,1)} %own_ref.1), channel_id=1, source_target_pairs={{0,1},{1,0},{2,3},{3,2},{4,5},{5,4},{6,7},{7,6},{8,9},{9,8},{10,11... | collective-permute-start | bytes 589832 | tf_op jit(solution)/shard_map/ppermute | solution.py:35
  10.1 10.4 %copy-start.5 = (s32[8,2]{0,1:T(2,128)S(1)}, s32[8,2]{0,1:T(2,128)}, u32[]{:S(2)}) copy-start(s32[8,2]{0,1:T(2,128)} %param.14) | copy-start | bytes 196
  10.2 10.5 %copy-start.4 = (s32[8]{0:T(128)S(1)}, s32[8]{0:T(128)}, u32[]{:S(2)}) copy-start(s32[8]{0:T(128)} %counts_ref.1) | copy-start | bytes 100
  10.2 11.8 %copy-start.1 = (bf16[320,384]{1,0:T(8,128)(2,1)S(1)}, bf16[320,384]{1,0:T(8,128)(2,1)}, u32[]{:S(2)}) copy-start(bf16[320,384]{1,0:T(8,128)(2,1)} %load.1.kv0) | copy-start | bytes 737284
  10.2 3.2 %collective-permute-start.5 = (bf16[128,768]{1,0:T(8,128)(2,1)S(1)}, bf16[128,768]{1,0:T(8,128)(2,1)S(1)}, u32[]{:S(2)}, u32[]{:S(2)}) collective-permute-start(bf16[128,768]{1,0:T(8,128)(2,1)S(1)} %collective-permute-done.4.near_ref), channel_id=1, source_target_pairs={{0,1},{1,0},{2,3},{3,2},{4,5},{5,4},{6,7},{7,6},{8,9},{9,8},{10,11... | collective-permute-start | bytes 589832 | tf_op jit(solution)/shard_map/ppermute | solution.py:35
  10.8 10.5 %collective-permute-start = (bf16[128,384]{1,0:T(8,128)(2,1)S(1)}, bf16[128,384]{1,0:T(8,128)(2,1)S(1)}, u32[]{:S(2)}, u32[]{:S(2)}) collective-permute-start(bf16[128,384]{1,0:T(8,128)(2,1)S(1)} %copy-done.2), channel_id=1, source_target_pairs={{0,16},{4,20},{8,24},{12,28},{16,0},{20,4},{24,8},{28,12},{1,17},{... | collective-permute-start | bytes 294920 | tf_op jit(solution)/shard_map/ppermute | solution.py:35
  14.4 6.9 %collective-permute-start.7 = (bf16[320,128]{1,0:T(8,128)(2,1)S(1)}, bf16[320,128]{1,0:T(8,128)(2,1)S(1)}, u32[]{:S(2)}, u32[]{:S(2)}) collective-permute-start(bf16[320,128]{1,0:T(8,128)(2,1)S(1)} %get-tuple-element.52), channel_id=1, source_target_pairs={{0,4},{4,0},{8,12},{12,8},{16,20},{20,16},{24,28},{28,24},{1,5},{5... | collective-permute-start | bytes 245768 | tf_op jit(solution)/shard_map/ppermute | solution.py:35
  15.9 5.4 %collective-permute-start.8 = (bf16[320,128]{1,0:T(8,128)(2,1)S(1)}, bf16[320,128]{1,0:T(8,128)(2,1)S(1)}, u32[]{:S(2)}, u32[]{:S(2)}) collective-permute-start(bf16[320,128]{1,0:T(8,128)(2,1)S(1)} %get-tuple-element.53), channel_id=1, source_target_pairs={{0,4},{4,0},{8,12},{12,8},{16,20},{20,16},{24,28},{28,24},{1,5},{5... | collective-permute-start | bytes 245768 | tf_op jit(solution)/shard_map/ppermute | solution.py:35
  16.5 5.6 %collective-permute-start.9 = (bf16[320,128]{1,0:T(8,128)(2,1)S(1)}, bf16[320,128]{1,0:T(8,128)(2,1)S(1)}, u32[]{:S(2)}, u32[]{:S(2)}) collective-permute-start(bf16[320,128]{1,0:T(8,128)(2,1)S(1)} %get-tuple-element.54), channel_id=1, source_target_pairs={{0,4},{4,0},{8,12},{12,8},{16,20},{20,16},{24,28},{28,24},{1,5},{5... | collective-permute-start | bytes 245768 | tf_op jit(solution)/shard_map/ppermute | solution.py:35
  18.0 7.4 %collective-permute-start.6 = (bf16[128,384]{1,0:T(8,128)(2,1)S(1)}, bf16[128,384]{1,0:T(8,128)(2,1)S(1)}, u32[]{:S(2)}, u32[]{:S(2)}) collective-permute-start(bf16[128,384]{1,0:T(8,128)(2,1)S(1)} %dattn.1.d_own_ref), channel_id=1, source_target_pairs={{0,16},{4,20},{8,24},{12,28},{16,0},{20,4},{24,8},{28,12},{1,17},{... | collective-permute-start | bytes 294920 | tf_op jit(solution)/shard_map/ppermute | solution.py:35
  23.5 8.4 %collective-permute-start.11 = (bf16[384,128]{1,0:T(8,128)(2,1)S(1)}, bf16[384,128]{1,0:T(8,128)(2,1)S(1)}, u32[]{:S(2)}, u32[]{:S(2)}) collective-permute-start(bf16[384,128]{1,0:T(8,128)(2,1)S(1)} %get-tuple-element.62), channel_id=1, source_target_pairs={{0,16},{4,20},{8,24},{12,28},{16,0},{20,4},{24,8},{28,12},{1,17},{... | collective-permute-start | bytes 294920 | tf_op jit(solution)/shard_map/ppermute | solution.py:35
  25.8 7.5 %copy-start = (bf16[384,3072]{1,0:T(8,128)(2,1)S(1)}, bf16[384,3072]{1,0:T(8,128)(2,1)}, u32[]{:S(2)}) copy-start(bf16[384,3072]{1,0:T(8,128)(2,1)} %w_ref.3) | copy-start | bytes 7077892
  25.8 5.0 %collective-permute-start.10 = (f32[16,256]{1,0:T(8,128)S(1)}, f32[16,256]{1,0:T(8,128)S(1)}, u32[]{:S(2)}, u32[]{:S(2)}) collective-permute-start(f32[16,256]{1,0:T(8,128)S(1)} %get-tuple-element.59.stats_ref), channel_id=1, source_target_pairs={{0,16},{4,20},{8,24},{12,28},{16,0},{20,4},{24,8},{28,12},{1,17},{... | collective-permute-start | bytes 49160 | tf_op jit(solution)/shard_map/ppermute | solution.py:35
  31.9 8.1 %collective-permute-start.18 = (bf16[384,384]{1,0:T(8,128)(2,1)S(1)}, bf16[384,384]{1,0:T(8,128)(2,1)S(1)}, u32[]{:S(2)}, u32[]{:S(2)}) collective-permute-start(bf16[384,384]{1,0:T(8,128)(2,1)S(1)} %get-tuple-element.77), channel_id=1, source_target_pairs={{0,4},{4,0},{8,12},{12,8},{16,20},{20,16},{24,28},{28,24},{1,5},{5... | collective-permute-start | bytes 884744 | tf_op jit(solution)/shard_map/ppermute | solution.py:35
  32.9 6.1 %collective-permute-start.12 = (bf16[256,384]{1,0:T(8,128)(2,1)S(1)}, bf16[256,384]{1,0:T(8,128)(2,1)S(1)}, u32[]{:S(2)}, u32[]{:S(2)}) collective-permute-start(bf16[256,384]{1,0:T(8,128)(2,1)S(1)} %get-tuple-element.65), channel_id=1, source_target_pairs={{0,8},{4,12},{8,0},{12,4},{16,24},{20,28},{24,16},{28,20},{1,9},{5... | collective-permute-start | bytes 589832 | tf_op jit(solution)/shard_map/ppermute | solution.py:35
  34.0 5.1 %collective-permute-start.13 = (bf16[128,768]{1,0:T(8,128)(2,1)S(1)}, bf16[128,768]{1,0:T(8,128)(2,1)S(1)}, u32[]{:S(2)}, u32[]{:S(2)}) collective-permute-start(bf16[128,768]{1,0:T(8,128)(2,1)S(1)} %get-tuple-element.69), channel_id=1, source_target_pairs={{0,1},{1,0},{2,3},{3,2},{4,5},{5,4},{6,7},{7,6},{8,9},{9,8},{10,11... | collective-permute-start | bytes 589832 | tf_op jit(solution)/shard_map/ppermute | solution.py:35
  34.0 1.6 %collective-permute-start.14 = (bf16[128,384]{1,0:T(8,128)(2,1)S(1)}, bf16[128,384]{1,0:T(8,128)(2,1)S(1)}, u32[]{:S(2)}, u32[]{:S(2)}) collective-permute-start(bf16[128,384]{1,0:T(8,128)(2,1)S(1)} %get-tuple-element.72), channel_id=1, source_target_pairs={{0,1},{1,0},{2,3},{3,2},{4,5},{5,4},{6,7},{7,6},{8,9},{9,8},{10,11... | collective-permute-start | bytes 294920 | tf_op jit(solution)/shard_map/ppermute | solution.py:35
  34.5 1.3 %collective-permute-start.15 = (bf16[128,384]{1,0:T(8,128)(2,1)S(1)}, bf16[128,384]{1,0:T(8,128)(2,1)S(1)}, u32[]{:S(2)}, u32[]{:S(2)}) collective-permute-start(bf16[128,384]{1,0:T(8,128)(2,1)S(1)} %get-tuple-element.73), channel_id=1, source_target_pairs={{0,1},{1,0},{2,3},{3,2},{4,5},{5,4},{6,7},{7,6},{8,9},{9,8},{10,11... | collective-permute-start | bytes 294920 | tf_op jit(solution)/shard_map/ppermute | solution.py:35
  35.9 9.0 %collective-permute-start.16 = (bf16[128,768]{1,0:T(8,128)(2,1)S(1)}, bf16[128,768]{1,0:T(8,128)(2,1)S(1)}, u32[]{:S(2)}, u32[]{:S(2)}) collective-permute-start(bf16[128,768]{1,0:T(8,128)(2,1)S(1)} %add_near.1), channel_id=1, source_target_pairs={{0,2},{1,3},{2,0},{3,1},{4,6},{5,7},{6,4},{7,5},{8,10},{9,11},{10,... | collective-permute-start | bytes 589832 | tf_op jit(solution)/shard_map/ppermute | solution.py:35
  37.2 7.7 %collective-permute-start.17 = (bf16[128,384]{1,0:T(8,128)(2,1)S(1)}, bf16[128,384]{1,0:T(8,128)(2,1)S(1)}, u32[]{:S(2)}, u32[]{:S(2)}) collective-permute-start(bf16[128,384]{1,0:T(8,128)(2,1)S(1)} %get-tuple-element.75), channel_id=1, source_target_pairs={{0,16},{4,20},{8,24},{12,28},{16,0},{20,4},{24,8},{28,12},{1,17},{... | collective-permute-start | bytes 294920 | tf_op jit(solution)/shard_map/ppermute | solution.py:35
  39.1 5.8 %collective-permute-start.21 = (bf16[128,384]{1,0:T(8,128)(2,1)S(1)}, bf16[128,384]{1,0:T(8,128)(2,1)S(1)}, u32[]{:S(2)}, u32[]{:S(2)}) collective-permute-start(bf16[128,384]{1,0:T(8,128)(2,1)S(1)} %get-tuple-element.81), channel_id=1, source_target_pairs={{0,4},{4,0},{8,12},{12,8},{16,20},{20,16},{24,28},{28,24},{1,5},{5... | collective-permute-start | bytes 294920 | tf_op jit(solution)/shard_map/ppermute | solution.py:35
  40.1 6.2 %collective-permute-start.19 = (bf16[128,384]{1,0:T(8,128)(2,1)S(1)}, bf16[128,384]{1,0:T(8,128)(2,1)S(1)}, u32[]{:S(2)}, u32[]{:S(2)}) collective-permute-start(bf16[128,384]{1,0:T(8,128)(2,1)S(1)} %get-tuple-element.79), channel_id=1, source_target_pairs={{0,8},{4,12},{8,0},{12,4},{16,24},{20,28},{24,16},{28,20},{1,9},{5... | collective-permute-start | bytes 294920 | tf_op jit(solution)/shard_map/ppermute | solution.py:35
  40.3 6.0 %collective-permute-start.20 = (bf16[64,384]{1,0:T(8,128)(2,1)S(1)}, bf16[64,384]{1,0:T(8,128)(2,1)S(1)}, u32[]{:S(2)}, u32[]{:S(2)}) collective-permute-start(bf16[64,384]{1,0:T(8,128)(2,1)S(1)} %get-tuple-element.80), channel_id=1, source_target_pairs={{0,8},{4,12},{8,0},{12,4},{16,24},{20,28},{24,16},{28,20},{1,9},{5... | collective-permute-start | bytes 147464 | tf_op jit(solution)/shard_map/ppermute | solution.py:35

commit v21 on v18

--- a/solution.py
+++ b/solution.py
@@ -360,12 +360,6 @@
         [shape((rows, width), BF16)],
         (grad_out, grad_core, grad_near, grad_far, weight),
     )[0]
-    kv1, kv2, d_own = lax.optimization_barrier((kv1, kv2, d_own))
-    pieces = local_call(
-        split_heads_kernel, "split_heads", 0.1, [shape((2 * keys, HDIM), BF16)] * heads, (kv2,)
-    )
-    kvs = (kv0, kv1, kv2, *(swap(piece, "ctx", 1) for piece in pieces))
-    d_pair = swap(d_own, "ctx", PAIR)
     limits = local_call(
         limits_kernel,
         "limits",
@@ -374,6 +368,12 @@
         (frame_levels, frame_counts),
         tables=2,
     )[0]
+    kv1, kv2, d_own, limits = lax.optimization_barrier((kv1, kv2, d_own, limits))
+    pieces = local_call(
+        split_heads_kernel, "split_heads", 0.1, [shape((2 * keys, HDIM), BF16)] * heads, (kv2,)
+    )
+    kvs = (kv0, kv1, kv2, *(swap(piece, "ctx", 1) for piece in pieces))
+    d_pair = swap(d_own, "ctx", PAIR)
     lse, probs = local_call(
         scores_kernel,
         "scores",

time: 46.9 us -> 48.7 us (1.038)
  waiting for transfers between devices: 10.1 us -> 12 us
  Pallas kernels: 9.38 us -> 10.5 us
  starting transfers between devices: 26.2 us -> 25.1 us
    ppermute x22, waiting for transfers between devices: 10.1 us -> 12 us  [swap(): return lax.ppermute(block, axis, [(i, i ^ bit) for i in range(count)])]
    ppermute x22, starting transfers between devices: 26.2 us -> 25.1 us  [swap(): return lax.ppermute(block, axis, [(i, i ^ bit) for i in range(count)])]
    pallas_call x11, Pallas kernels: 6.09 us -> 7.19 us  [local_call(): pl.pallas_call(body, name=name, out_shape=out_shapes, in_specs=[pl.BlockS...]
  transfers between devices with their start and end apart: 22 -> 22, of which waited for: 8 -> 10; matrix products, arithmetic and copies ran while one was open for 0% -> 0% of each run, Pallas kernels for 18% -> 20%
where the time goes in v21:
time: 48.7 us; the launch traced here: 48.5 us
  starting transfers between devices  25.1 us (52%)
  waiting for transfers between devices  12 us (25%)
  Pallas kernels  10.5 us (22%)
  between operations  0.85 us (2%)
    ppermute x22, starting transfers between devices, swap(): return lax.ppermute(block, axis, [(i, i ^ bit) for i in range(count)])  25.1 us
    ppermute x22, waiting for transfers between devices, swap(): return lax.ppermute(block, axis, [(i, i ^ bit) for i in range(count)])  12 us
    pallas_call x11, Pallas kernels, local_call(): pl.pallas_call(body, name=name, out_shape=out_shapes, in_specs=[pl.BlockS...  7.19 us
    pallas_call x1, Pallas kernels, load_keys(): pl.pallas_call(load_kernel, name='load', out_shape=jax.ShapeDtypeStruct((...  1.66 us
    pallas_call x1, Pallas kernels, load_weight(): pl.pallas_call(load_weight_kernel, name='load_w', out_shape=jax.ShapeDtyp...  1.63 us
  transfers between devices with their start and end apart: 22, of which 10 were waited for; matrix products, arithmetic and copies ran while one was open for 0% of the time, Pallas kernels for 20%

profile of v21, /device:TPU:0, one launch (start us, length us, event | category | flops | bytes accessed | tf_op | source)
XLA Modules:
  0.0 48.5 jit_solution(14904559114801347058)
XLA Ops:
  0.6 3.0 %collective-permute-start.4 = (bf16[128,768]{1,0:T(8,128)(2,1)}, bf16[128,768]{1,0:T(8,128)(2,1)}, u32[]{:S(2)}, u32[]{:S(2)}) collective-permute-start(bf16[128,768]{1,0:T(8,128)(2,1)} %own_ref.1), channel_id=1, source_target_pairs={{0,2},{1,3},{2,0},{3,1},{4,6},{5,7},{6,4},{7,5},{8,10},{9,11},{10,... | collective-permute-start | bytes 589832 | tf_op jit(solution)/shard_map/ppermute | solution.py:35
  3.6 1.7 %load.1.kv0 = bf16[320,384]{1,0:T(8,128)(2,1)} custom-call(bf16[128,384]{1,0:T(8,128)(2,1)} %k_ref.1, bf16[32,384]{1,0:T(8,128)(2,1)} %hk_ref.1, bf16[128,384]{1,0:T(8,128)(2,1)} %v_ref.1, bf16[32,384]{1,0:T(8,128)(2,1)} %hv_ref.1), custom_call_target="tpu_custom_call" | custom-call | bytes 5904000 | tf_op jit(solution)/shard_map/load/pallas_call | solution.py:74
  5.3 0.0 copy-start.2
  5.3 0.0 copy-start.5
  5.3 0.0 copy-start.4
  5.3 0.0 copy-start.3
  5.4 1.6 %collective-permute-start.2 = (bf16[320,384]{1,0:T(8,128)(2,1)}, bf16[320,384]{1,0:T(8,128)(2,1)S(1)}, u32[]{:S(2)}, u32[]{:S(2)}) collective-permute-start(bf16[320,384]{1,0:T(8,128)(2,1)} %load.1.kv0), channel_id=1, source_target_pairs={{0,8},{4,12},{8,0},{12,4},{16,24},{20,28},{24,16},{28,20},{1,9},{5... | collective-permute-start | bytes 737288 | tf_op jit(solution)/shard_map/ppermute | solution.py:35
  7.0 1.5 %collective-permute-start.1 = (bf16[320,384]{1,0:T(8,128)(2,1)}, bf16[320,384]{1,0:T(8,128)(2,1)S(1)}, u32[]{:S(2)}, u32[]{:S(2)}) collective-permute-start(bf16[320,384]{1,0:T(8,128)(2,1)} %load.1.kv0), channel_id=1, source_target_pairs={{0,4},{4,0},{8,12},{12,8},{16,20},{20,16},{24,28},{28,24},{1,5},{5... | collective-permute-start | bytes 737288 | tf_op jit(solution)/shard_map/ppermute | solution.py:35
  8.5 1.6 %load_w.1.w_ref = bf16[384,3072]{1,0:T(8,128)(2,1)S(1)} custom-call(bf16[384,3072]{1,0:T(8,128)(2,1)} %w_ref.3), custom_call_target="tpu_custom_call" | custom-call | bytes 5904000 | tf_op jit(solution)/shard_map/load_w/pallas_call | solution.py:113
  10.2 0.0 collective-permute-done.4.near_ref
  10.2 0.6 %collective-permute-start.5 = (bf16[128,768]{1,0:T(8,128)(2,1)}, bf16[128,768]{1,0:T(8,128)(2,1)}, u32[]{:S(2)}, u32[]{:S(2)}) collective-permute-start(bf16[128,768]{1,0:T(8,128)(2,1)} %collective-permute-done.4.near_ref), channel_id=1, source_target_pairs={{0,1},{1,0},{2,3},{3,2},{4,5},{5,4},{6,7},{7,6},{8,9},{9,8},{10,11... | collective-permute-start | bytes 589832 | tf_op jit(solution)/shard_map/ppermute | solution.py:35
  10.8 2.6 %collective-permute-start = (bf16[128,384]{1,0:T(8,128)(2,1)S(1)}, bf16[128,384]{1,0:T(8,128)(2,1)S(1)}, u32[]{:S(2)}, u32[]{:S(2)}) collective-permute-start(bf16[128,384]{1,0:T(8,128)(2,1)S(1)} %copy-done.2), channel_id=1, source_target_pairs={{0,16},{4,20},{8,24},{12,28},{16,0},{20,4},{24,8},{28,12},{1,17},{... | collective-permute-start | bytes 294920 | tf_op jit(solution)/shard_map/ppermute | solution.py:35
  13.3 0.1 copy.15.levels_ref
  13.4 0.6 %limits.1.limits_ref = s32[8,256]{1,0:T(8,128)S(1)} custom-call(s32[8,2]{1,0:T(8,128)S(1)} %copy.15.levels_ref, s32[8]{0:T(128)S(1)} %copy-done.4), custom_call_target="tpu_custom_call" | custom-call | bytes 2214000 | tf_op jit(solution)/shard_map/limits/pallas_call | solution.py:44
  14.1 1.9 %dattn.1.d_own_ref = bf16[128,384]{1,0:T(8,128)(2,1)S(1)} custom-call(bf16[128,768]{1,0:T(8,128)(2,1)S(1)} %copy-done.3, bf16[128,768]{1,0:T(8,128)(2,1)} %collective-permute-done.3.core_ref, bf16[128,768]{1,0:T(8,128)(2,1)} %collective-permute-done.4.near_ref, bf16[128,768]{1,0:T(8,128)(2,1)} %collective-permute-done.5.far_ref, ...), custom_call_target="tpu_custom_call" | custom-call | bytes 2952000 | tf_op jit(solution)/shard_map/dattn/pallas_call | solution.py:44
  16.1 0.6 %collective-permute-start.7 = (bf16[320,128]{1,0:T(8,128)(2,1)S(1)}, bf16[320,128]{1,0:T(8,128)(2,1)S(1)}, u32[]{:S(2)}, u32[]{:S(2)}) collective-permute-start(bf16[320,128]{1,0:T(8,128)(2,1)S(1)} %get-tuple-element.54), channel_id=1, source_target_pairs={{0,4},{4,0},{8,12},{12,8},{16,20},{20,16},{24,28},{28,24},{1,5},{5... | collective-permute-start | bytes 245768 | tf_op jit(solution)/shard_map/ppermute | solution.py:35
  16.7 1.5 %collective-permute-start.8 = (bf16[320,128]{1,0:T(8,128)(2,1)S(1)}, bf16[320,128]{1,0:T(8,128)(2,1)S(1)}, u32[]{:S(2)}, u32[]{:S(2)}) collective-permute-start(bf16[320,128]{1,0:T(8,128)(2,1)S(1)} %get-tuple-element.55), channel_id=1, source_target_pairs={{0,4},{4,0},{8,12},{12,8},{16,20},{20,16},{24,28},{28,24},{1,5},{5... | collective-permute-start | bytes 245768 | tf_op jit(solution)/shard_map/ppermute | solution.py:35
  18.2 0.5 %collective-permute-start.9 = (bf16[320,128]{1,0:T(8,128)(2,1)S(1)}, bf16[320,128]{1,0:T(8,128)(2,1)S(1)}, u32[]{:S(2)}, u32[]{:S(2)}) collective-permute-start(bf16[320,128]{1,0:T(8,128)(2,1)S(1)} %get-tuple-element.56), channel_id=1, source_target_pairs={{0,4},{4,0},{8,12},{12,8},{16,20},{20,16},{24,28},{28,24},{1,5},{5... | collective-permute-start | bytes 245768 | tf_op jit(solution)/shard_map/ppermute | solution.py:35
  18.7 1.9 %collective-permute-start.6 = (bf16[128,384]{1,0:T(8,128)(2,1)S(1)}, bf16[128,384]{1,0:T(8,128)(2,1)S(1)}, u32[]{:S(2)}, u32[]{:S(2)}) collective-permute-start(bf16[128,384]{1,0:T(8,128)(2,1)S(1)} %dattn.1.d_own_ref), channel_id=1, source_target_pairs={{0,16},{4,20},{8,24},{12,28},{16,0},{20,4},{24,8},{28,12},{1,17},{... | collective-permute-start | bytes 294920 | tf_op jit(solution)/shard_map/ppermute | solution.py:35
  20.6 0.9 %collective-permute-done.7.refs_0_ = bf16[320,128]{1,0:T(8,128)(2,1)S(1)} collective-permute-done((bf16[320,128]{1,0:T(8,128)(2,1)S(1)}, bf16[320,128]{1,0:T(8,128)(2,1)S(1)}, u32[]{:S(2)}, u32[]{:S(2)}) %collective-permute-start.7) | collective-permute-done | bytes 81952 | tf_op jit(solution)/shard_map/ppermute | solution.py:35
  21.5 1.5 %collective-permute-done.8.refs_1_ = bf16[320,128]{1,0:T(8,128)(2,1)S(1)} collective-permute-done((bf16[320,128]{1,0:T(8,128)(2,1)S(1)}, bf16[320,128]{1,0:T(8,128)(2,1)S(1)}, u32[]{:S(2)}, u32[]{:S(2)}) %collective-permute-start.8) | collective-permute-done | bytes 81952 | tf_op jit(solution)/shard_map/ppermute | solution.py:35
  23.0 0.9 %collective-permute-done.9.refs_2_ = bf16[320,128]{1,0:T(8,128)(2,1)S(1)} collective-permute-done((bf16[320,128]{1,0:T(8,128)(2,1)S(1)}, bf16[320,128]{1,0:T(8,128)(2,1)S(1)}, u32[]{:S(2)}, u32[]{:S(2)}) %collective-permute-start.9) | collective-permute-done | bytes 81952 | tf_op jit(solution)/shard_map/ppermute | solution.py:35
  23.9 1.0 %scores.1 = (f32[8,256]{1,0:T(8,128)S(1)}, bf16[1920,256]{1,0:T(8,128)(2,1)S(1)}) custom-call(s32[8,256]{1,0:T(8,128)S(1)} %limits.1.limits_ref, bf16[128,384]{1,0:T(8,128)(2,1)S(1)} %copy-done.2, bf16[128,384]{1,0:T(8,128)(2,1)S(1)} %collective-permute-done.q_pair_ref, bf16[320,384]{1,0:T(8,128)(2,1)S(1)} %copy-done.1, ...), custom_call_target="tpu_custom_call" | custom-call | bytes 3321000 | tf_op jit(solution)/shard_map/scores/pallas_call | solution.py:44
  24.9 0.4 attn.1
  25.3 1.3 %collective-permute-start.11 = (bf16[384,128]{1,0:T(8,128)(2,1)S(1)}, bf16[384,128]{1,0:T(8,128)(2,1)S(1)}, u32[]{:S(2)}, u32[]{:S(2)}) collective-permute-start(bf16[384,128]{1,0:T(8,128)(2,1)S(1)} %get-tuple-element.65), channel_id=1, source_target_pairs={{0,16},{4,20},{8,24},{12,28},{16,0},{20,4},{24,8},{28,12},{1,17},{... | collective-permute-start | bytes 294920 | tf_op jit(solution)/shard_map/ppermute | solution.py:35
  26.6 0.4 delta.1
  27.0 0.0 copy-start
  27.0 1.8 %collective-permute-start.10 = (f32[16,256]{1,0:T(8,128)S(1)}, f32[16,256]{1,0:T(8,128)S(1)}, u32[]{:S(2)}, u32[]{:S(2)}) collective-permute-start(f32[16,256]{1,0:T(8,128)S(1)} %get-tuple-element.61.stats_ref), channel_id=1, source_target_pairs={{0,16},{4,20},{8,24},{12,28},{16,0},{20,4},{24,8},{28,12},{1,17},{... | collective-permute-start | bytes 49160 | tf_op jit(solution)/shard_map/ppermute | solution.py:35
  28.8 3.9 %collective-permute-done.10.stats_pair_ref = f32[16,256]{1,0:T(8,128)S(1)} collective-permute-done((f32[16,256]{1,0:T(8,128)S(1)}, f32[16,256]{1,0:T(8,128)S(1)}, u32[]{:S(2)}, u32[]{:S(2)}) %collective-permute-start.10) | collective-permute-done | bytes 16416 | tf_op jit(solution)/shard_map/ppermute | solution.py:35
  32.7 1.1 %backward.1 = (f32[128,384]{1,0:T(8,128)S(1)}, bf16[128,384]{1,0:T(8,128)(2,1)S(1)}, f32[320,384]{1,0:T(8,128)S(1)}, bf16[384,384]{1,0:T(8,128)(2,1)S(1)}, bf16[...) custom-call(bf16[128,384]{1,0:T(8,128)(2,1)S(1)} %copy-done.2, ...), custom_call_target="tpu_custom_call" | custom-call | bytes 4059000 | tf_op jit(solution)/shard_map/backward/pallas_call | solution.py:44
  33.9 1.2 %collective-permute-start.12 = (bf16[384,384]{1,0:T(8,128)(2,1)S(1)}, bf16[384,384]{1,0:T(8,128)(2,1)S(1)}, u32[]{:S(2)}, u32[]{:S(2)}) collective-permute-start(bf16[384,384]{1,0:T(8,128)(2,1)S(1)} %get-tuple-element.68), channel_id=1, source_target_pairs={{0,4},{4,0},{8,12},{12,8},{16,20},{20,16},{24,28},{28,24},{1,5},{5... | collective-permute-start | bytes 884744 | tf_op jit(solution)/shard_map/ppermute | solution.py:35
  35.1 0.6 %project.1 = (f32[128,768]{1,0:T(8,128)S(1)}, f32[128,768]{1,0:T(8,128)S(1)}, bf16[128,768]{1,0:T(8,128)(2,1)S(1)}, bf16[128,384]{1,0:T(8,128)(2,1)S(1)}, bf16[128,384]{1,0:T(8,128)(2,1)S(1)}) custom-call(f32[384,128]{1,0:T(8,128)S(1)} %get-tuple-element.70.own_ref, bf16[384,128]{1,0:T(8,128)(2,1)S(1)} %collective-permute-done.11.pair_ref, ...), custom_call_target="tpu_custom_call" | custom-call | bytes 2214000 | tf_op jit(solution)/shard_map/project/pallas_call | solution.py:44
  35.7 0.1 collective-permute-start.14
  35.8 0.5 %collective-permute-start.15 = (bf16[128,384]{1,0:T(8,128)(2,1)S(1)}, bf16[128,384]{1,0:T(8,128)(2,1)S(1)}, u32[]{:S(2)}, u32[]{:S(2)}) collective-permute-start(bf16[128,384]{1,0:T(8,128)(2,1)S(1)} %get-tuple-element.76), channel_id=1, source_target_pairs={{0,1},{1,0},{2,3},{3,2},{4,5},{5,4},{6,7},{7,6},{8,9},{9,8},{10,11... | collective-permute-start | bytes 294920 | tf_op jit(solution)/shard_map/ppermute | solution.py:35
  36.3 0.1 collective-permute-start.16
  36.4 1.0 %collective-permute-done.15.left_ref = bf16[128,384]{1,0:T(8,128)(2,1)S(1)} collective-permute-done((bf16[128,384]{1,0:T(8,128)(2,1)S(1)}, bf16[128,384]{1,0:T(8,128)(2,1)S(1)}, u32[]{:S(2)}, u32[]{:S(2)}) %collective-permute-start.15) | collective-permute-done | bytes 98336 | tf_op jit(solution)/shard_map/ppermute | solution.py:35
  37.4 0.2 collective-permute-done.16.right_ref
  37.6 1.2 %collective-permute-start.17 = (bf16[128,768]{1,0:T(8,128)(2,1)S(1)}, bf16[128,768]{1,0:T(8,128)(2,1)S(1)}, u32[]{:S(2)}, u32[]{:S(2)}) collective-permute-start(bf16[128,768]{1,0:T(8,128)(2,1)S(1)} %add_near.1), channel_id=1, source_target_pairs={{0,2},{1,3},{2,0},{3,1},{4,6},{5,7},{6,4},{7,5},{8,10},{9,11},{10,... | collective-permute-start | bytes 589832 | tf_op jit(solution)/shard_map/ppermute | solution.py:35
  38.8 1.9 %collective-permute-start.18 = (bf16[128,384]{1,0:T(8,128)(2,1)S(1)}, bf16[128,384]{1,0:T(8,128)(2,1)S(1)}, u32[]{:S(2)}, u32[]{:S(2)}) collective-permute-start(bf16[128,384]{1,0:T(8,128)(2,1)S(1)} %get-tuple-element.79), channel_id=1, source_target_pairs={{0,16},{4,20},{8,24},{12,28},{16,0},{20,4},{24,8},{28,12},{1,17},{... | collective-permute-start | bytes 294920 | tf_op jit(solution)/shard_map/ppermute | solution.py:35
  40.7 0.2 collective-permute-done.13.got_z_ref
  40.9 1.2 %collective-permute-done.12.got_y_ref = bf16[384,384]{1,0:T(8,128)(2,1)S(1)} collective-permute-done((bf16[384,384]{1,0:T(8,128)(2,1)S(1)}, bf16[384,384]{1,0:T(8,128)(2,1)S(1)}, u32[]{:S(2)}, u32[]{:S(2)}) %collective-permute-start.12) | collective-permute-done | bytes 294944 | tf_op jit(solution)/shard_map/ppermute | solution.py:35
  42.1 0.1 pass_on.1
  42.2 0.1 collective-permute-start.19
  42.2 1.3 %collective-permute-start.21 = (bf16[128,384]{1,0:T(8,128)(2,1)S(1)}, bf16[128,384]{1,0:T(8,128)(2,1)S(1)}, u32[]{:S(2)}, u32[]{:S(2)}) collective-permute-start(bf16[128,384]{1,0:T(8,128)(2,1)S(1)} %get-tuple-element.83), channel_id=1, source_target_pairs={{0,4},{4,0},{8,12},{12,8},{16,20},{20,16},{24,28},{28,24},{1,5},{5... | collective-permute-start | bytes 294920 | tf_op jit(solution)/shard_map/ppermute | solution.py:35
  43.5 1.9 %collective-permute-start.20 = (bf16[64,384]{1,0:T(8,128)(2,1)S(1)}, bf16[64,384]{1,0:T(8,128)(2,1)S(1)}, u32[]{:S(2)}, u32[]{:S(2)}) collective-permute-start(bf16[64,384]{1,0:T(8,128)(2,1)S(1)} %get-tuple-element.82), channel_id=1, source_target_pairs={{0,8},{4,12},{8,0},{12,4},{16,24},{20,28},{24,16},{28,20},{1,9},{5... | collective-permute-start | bytes 147464 | tf_op jit(solution)/shard_map/ppermute | solution.py:35
  45.5 0.5 %collective-permute-done.18.dq_pair_ref = bf16[128,384]{1,0:T(8,128)(2,1)S(1)} collective-permute-done((bf16[128,384]{1,0:T(8,128)(2,1)S(1)}, bf16[128,384]{1,0:T(8,128)(2,1)S(1)}, u32[]{:S(2)}, u32[]{:S(2)}) %collective-permute-start.18) | collective-permute-done | bytes 98336 | tf_op jit(solution)/shard_map/ppermute | solution.py:35
  46.0 1.6 %collective-permute-done.20.rest_h_ref = bf16[64,384]{1,0:T(8,128)(2,1)S(1)} collective-permute-done((bf16[64,384]{1,0:T(8,128)(2,1)S(1)}, bf16[64,384]{1,0:T(8,128)(2,1)S(1)}, u32[]{:S(2)}, u32[]{:S(2)}) %collective-permute-start.20) | collective-permute-done | bytes 49184 | tf_op jit(solution)/shard_map/ppermute | solution.py:35
  47.6 0.9 %finish.1 = (bf16[128,384]{1,0:T(8,128)(2,1)}, bf16[128,384]{1,0:T(8,128)(2,1)}, bf16[128,384]{1,0:T(8,128)(2,1)}, bf16[32,384]{1,0:T(8,128)(2,1)}, bf16[32,384]{1,0:T(8,128)(2,1)}, /*index=5*/bf16[128,768]{1,0:T(8,128)(2,1)}) custom-call(f32[128,768]{1,0:T(8,128)S(1)} %get-tuple-element.74.keep_ref, bf16[128,768]{1,0:T(8,128)(2,1)S(1)} %collective-permute-done.17.near_ref, ...), custom_call_target="tpu_custom_call" | custom-call | bytes 3321000 | tf_op jit(solution)/shard_map/finish/pallas_call | solution.py:44
  (22 shorter events, 0.1 us)
Async XLA Ops:
  0.6 9.5 %collective-permute-start.4 = (bf16[128,768]{1,0:T(8,128)(2,1)}, bf16[128,768]{1,0:T(8,128)(2,1)}, u32[]{:S(2)}, u32[]{:S(2)}) collective-permute-start(bf16[128,768]{1,0:T(8,128)(2,1)} %own_ref.1), channel_id=1, source_target_pairs={{0,2},{1,3},{2,0},{3,1},{4,6},{5,7},{6,4},{7,5},{8,10},{9,11},{10,... | collective-permute-start | bytes 589832 | tf_op jit(solution)/shard_map/ppermute | solution.py:35
  5.3 5.4 %copy-start.2 = (bf16[128,384]{1,0:T(8,128)(2,1)S(1)}, bf16[128,384]{1,0:T(8,128)(2,1)}, u32[]{:S(2)}) copy-start(bf16[128,384]{1,0:T(8,128)(2,1)} %q_own_ref.3) | copy-start | bytes 294916
  5.3 8.0 %copy-start.5 = (s32[8,2]{0,1:T(2,128)S(1)}, s32[8,2]{0,1:T(2,128)}, u32[]{:S(2)}) copy-start(s32[8,2]{0,1:T(2,128)} %param.14) | copy-start | bytes 196
  5.3 8.1 %copy-start.4 = (s32[8]{0:T(128)S(1)}, s32[8]{0:T(128)}, u32[]{:S(2)}) copy-start(s32[8]{0:T(128)} %counts_ref.1) | copy-start | bytes 100
  5.3 8.7 %copy-start.3 = (bf16[128,768]{1,0:T(8,128)(2,1)S(1)}, bf16[128,768]{1,0:T(8,128)(2,1)}, u32[]{:S(2)}) copy-start(bf16[128,768]{1,0:T(8,128)(2,1)} %own_ref.1) | copy-start | bytes 589828
  5.4 10.7 %collective-permute-start.2 = (bf16[320,384]{1,0:T(8,128)(2,1)}, bf16[320,384]{1,0:T(8,128)(2,1)S(1)}, u32[]{:S(2)}, u32[]{:S(2)}) collective-permute-start(bf16[320,384]{1,0:T(8,128)(2,1)} %load.1.kv0), channel_id=1, source_target_pairs={{0,8},{4,12},{8,0},{12,4},{16,24},{20,28},{24,16},{28,20},{1,9},{5... | collective-permute-start | bytes 737288 | tf_op jit(solution)/shard_map/ppermute | solution.py:35
  7.0 9.1 %collective-permute-start.1 = (bf16[320,384]{1,0:T(8,128)(2,1)}, bf16[320,384]{1,0:T(8,128)(2,1)S(1)}, u32[]{:S(2)}, u32[]{:S(2)}) collective-permute-start(bf16[320,384]{1,0:T(8,128)(2,1)} %load.1.kv0), channel_id=1, source_target_pairs={{0,4},{4,0},{8,12},{12,8},{16,20},{20,16},{24,28},{28,24},{1,5},{5... | collective-permute-start | bytes 737288 | tf_op jit(solution)/shard_map/ppermute | solution.py:35
  8.5 5.6 %collective-permute-start.3 = (bf16[128,768]{1,0:T(8,128)(2,1)}, bf16[128,768]{1,0:T(8,128)(2,1)}, u32[]{:S(2)}, u32[]{:S(2)}) collective-permute-start(bf16[128,768]{1,0:T(8,128)(2,1)} %own_ref.1), channel_id=1, source_target_pairs={{0,1},{1,0},{2,3},{3,2},{4,5},{5,4},{6,7},{7,6},{8,9},{9,8},{10,11... | collective-permute-start | bytes 589832 | tf_op jit(solution)/shard_map/ppermute | solution.py:35
  10.2 13.7 %copy-start.1 = (bf16[320,384]{1,0:T(8,128)(2,1)S(1)}, bf16[320,384]{1,0:T(8,128)(2,1)}, u32[]{:S(2)}) copy-start(bf16[320,384]{1,0:T(8,128)(2,1)} %load.1.kv0) | copy-start | bytes 737284
  10.2 3.9 %collective-permute-start.5 = (bf16[128,768]{1,0:T(8,128)(2,1)}, bf16[128,768]{1,0:T(8,128)(2,1)}, u32[]{:S(2)}, u32[]{:S(2)}) collective-permute-start(bf16[128,768]{1,0:T(8,128)(2,1)} %collective-permute-done.4.near_ref), channel_id=1, source_target_pairs={{0,1},{1,0},{2,3},{3,2},{4,5},{5,4},{6,7},{7,6},{8,9},{9,8},{10,11... | collective-permute-start | bytes 589832 | tf_op jit(solution)/shard_map/ppermute | solution.py:35
  10.8 9.8 %collective-permute-start = (bf16[128,384]{1,0:T(8,128)(2,1)S(1)}, bf16[128,384]{1,0:T(8,128)(2,1)S(1)}, u32[]{:S(2)}, u32[]{:S(2)}) collective-permute-start(bf16[128,384]{1,0:T(8,128)(2,1)S(1)} %copy-done.2), channel_id=1, source_target_pairs={{0,16},{4,20},{8,24},{12,28},{16,0},{20,4},{24,8},{28,12},{1,17},{... | collective-permute-start | bytes 294920 | tf_op jit(solution)/shard_map/ppermute | solution.py:35
  16.1 5.4 %collective-permute-start.7 = (bf16[320,128]{1,0:T(8,128)(2,1)S(1)}, bf16[320,128]{1,0:T(8,128)(2,1)S(1)}, u32[]{:S(2)}, u32[]{:S(2)}) collective-permute-start(bf16[320,128]{1,0:T(8,128)(2,1)S(1)} %get-tuple-element.54), channel_id=1, source_target_pairs={{0,4},{4,0},{8,12},{12,8},{16,20},{20,16},{24,28},{28,24},{1,5},{5... | collective-permute-start | bytes 245768 | tf_op jit(solution)/shard_map/ppermute | solution.py:35
  16.7 6.3 %collective-permute-start.8 = (bf16[320,128]{1,0:T(8,128)(2,1)S(1)}, bf16[320,128]{1,0:T(8,128)(2,1)S(1)}, u32[]{:S(2)}, u32[]{:S(2)}) collective-permute-start(bf16[320,128]{1,0:T(8,128)(2,1)S(1)} %get-tuple-element.55), channel_id=1, source_target_pairs={{0,4},{4,0},{8,12},{12,8},{16,20},{20,16},{24,28},{28,24},{1,5},{5... | collective-permute-start | bytes 245768 | tf_op jit(solution)/shard_map/ppermute | solution.py:35
  18.2 5.6 %collective-permute-start.9 = (bf16[320,128]{1,0:T(8,128)(2,1)S(1)}, bf16[320,128]{1,0:T(8,128)(2,1)S(1)}, u32[]{:S(2)}, u32[]{:S(2)}) collective-permute-start(bf16[320,128]{1,0:T(8,128)(2,1)S(1)} %get-tuple-element.56), channel_id=1, source_target_pairs={{0,4},{4,0},{8,12},{12,8},{16,20},{20,16},{24,28},{28,24},{1,5},{5... | collective-permute-start | bytes 245768 | tf_op jit(solution)/shard_map/ppermute | solution.py:35
  18.7 7.9 %collective-permute-start.6 = (bf16[128,384]{1,0:T(8,128)(2,1)S(1)}, bf16[128,384]{1,0:T(8,128)(2,1)S(1)}, u32[]{:S(2)}, u32[]{:S(2)}) collective-permute-start(bf16[128,384]{1,0:T(8,128)(2,1)S(1)} %dattn.1.d_own_ref), channel_id=1, source_target_pairs={{0,16},{4,20},{8,24},{12,28},{16,0},{20,4},{24,8},{28,12},{1,17},{... | collective-permute-start | bytes 294920 | tf_op jit(solution)/shard_map/ppermute | solution.py:35
  25.3 8.5 %collective-permute-start.11 = (bf16[384,128]{1,0:T(8,128)(2,1)S(1)}, bf16[384,128]{1,0:T(8,128)(2,1)S(1)}, u32[]{:S(2)}, u32[]{:S(2)}) collective-permute-start(bf16[384,128]{1,0:T(8,128)(2,1)S(1)} %get-tuple-element.65), channel_id=1, source_target_pairs={{0,16},{4,20},{8,24},{12,28},{16,0},{20,4},{24,8},{28,12},{1,17},{... | collective-permute-start | bytes 294920 | tf_op jit(solution)/shard_map/ppermute | solution.py:35
  27.0 8.1 %copy-start = (bf16[384,3072]{1,0:T(8,128)(2,1)S(1)}, bf16[384,3072]{1,0:T(8,128)(2,1)}, u32[]{:S(2)}) copy-start(bf16[384,3072]{1,0:T(8,128)(2,1)} %w_ref.3) | copy-start | bytes 7077892
  27.0 5.7 %collective-permute-start.10 = (f32[16,256]{1,0:T(8,128)S(1)}, f32[16,256]{1,0:T(8,128)S(1)}, u32[]{:S(2)}, u32[]{:S(2)}) collective-permute-start(f32[16,256]{1,0:T(8,128)S(1)} %get-tuple-element.61.stats_ref), channel_id=1, source_target_pairs={{0,16},{4,20},{8,24},{12,28},{16,0},{20,4},{24,8},{28,12},{1,17},{... | collective-permute-start | bytes 49160 | tf_op jit(solution)/shard_map/ppermute | solution.py:35
  33.9 8.2 %collective-permute-start.12 = (bf16[384,384]{1,0:T(8,128)(2,1)S(1)}, bf16[384,384]{1,0:T(8,128)(2,1)S(1)}, u32[]{:S(2)}, u32[]{:S(2)}) collective-permute-start(bf16[384,384]{1,0:T(8,128)(2,1)S(1)} %get-tuple-element.68), channel_id=1, source_target_pairs={{0,4},{4,0},{8,12},{12,8},{16,20},{20,16},{24,28},{28,24},{1,5},{5... | collective-permute-start | bytes 884744 | tf_op jit(solution)/shard_map/ppermute | solution.py:35
  35.1 5.8 %collective-permute-start.13 = (bf16[256,384]{1,0:T(8,128)(2,1)S(1)}, bf16[256,384]{1,0:T(8,128)(2,1)S(1)}, u32[]{:S(2)}, u32[]{:S(2)}) collective-permute-start(bf16[256,384]{1,0:T(8,128)(2,1)S(1)} %get-tuple-element.69), channel_id=1, source_target_pairs={{0,8},{4,12},{8,0},{12,4},{16,24},{20,28},{24,16},{28,20},{1,9},{5... | collective-permute-start | bytes 589832 | tf_op jit(solution)/shard_map/ppermute | solution.py:35
  35.7 5.2 %collective-permute-start.14 = (bf16[128,768]{1,0:T(8,128)(2,1)S(1)}, bf16[128,768]{1,0:T(8,128)(2,1)S(1)}, u32[]{:S(2)}, u32[]{:S(2)}) collective-permute-start(bf16[128,768]{1,0:T(8,128)(2,1)S(1)} %get-tuple-element.73), channel_id=1, source_target_pairs={{0,1},{1,0},{2,3},{3,2},{4,5},{5,4},{6,7},{7,6},{8,9},{9,8},{10,11... | collective-permute-start | bytes 589832 | tf_op jit(solution)/shard_map/ppermute | solution.py:35
  35.8 1.6 %collective-permute-start.15 = (bf16[128,384]{1,0:T(8,128)(2,1)S(1)}, bf16[128,384]{1,0:T(8,128)(2,1)S(1)}, u32[]{:S(2)}, u32[]{:S(2)}) collective-permute-start(bf16[128,384]{1,0:T(8,128)(2,1)S(1)} %get-tuple-element.76), channel_id=1, source_target_pairs={{0,1},{1,0},{2,3},{3,2},{4,5},{5,4},{6,7},{7,6},{8,9},{9,8},{10,11... | collective-permute-start | bytes 294920 | tf_op jit(solution)/shard_map/ppermute | solution.py:35
  36.3 1.3 %collective-permute-start.16 = (bf16[128,384]{1,0:T(8,128)(2,1)S(1)}, bf16[128,384]{1,0:T(8,128)(2,1)S(1)}, u32[]{:S(2)}, u32[]{:S(2)}) collective-permute-start(bf16[128,384]{1,0:T(8,128)(2,1)S(1)} %get-tuple-element.77), channel_id=1, source_target_pairs={{0,1},{1,0},{2,3},{3,2},{4,5},{5,4},{6,7},{7,6},{8,9},{9,8},{10,11... | collective-permute-start | bytes 294920 | tf_op jit(solution)/shard_map/ppermute | solution.py:35
  37.6 8.4 %collective-permute-start.17 = (bf16[128,768]{1,0:T(8,128)(2,1)S(1)}, bf16[128,768]{1,0:T(8,128)(2,1)S(1)}, u32[]{:S(2)}, u32[]{:S(2)}) collective-permute-start(bf16[128,768]{1,0:T(8,128)(2,1)S(1)} %add_near.1), channel_id=1, source_target_pairs={{0,2},{1,3},{2,0},{3,1},{4,6},{5,7},{6,4},{7,5},{8,10},{9,11},{10,... | collective-permute-start | bytes 589832 | tf_op jit(solution)/shard_map/ppermute | solution.py:35
  38.8 7.2 %collective-permute-start.18 = (bf16[128,384]{1,0:T(8,128)(2,1)S(1)}, bf16[128,384]{1,0:T(8,128)(2,1)S(1)}, u32[]{:S(2)}, u32[]{:S(2)}) collective-permute-start(bf16[128,384]{1,0:T(8,128)(2,1)S(1)} %get-tuple-element.79), channel_id=1, source_target_pairs={{0,16},{4,20},{8,24},{12,28},{16,0},{20,4},{24,8},{28,12},{1,17},{... | collective-permute-start | bytes 294920 | tf_op jit(solution)/shard_map/ppermute | solution.py:35
  42.2 5.5 %collective-permute-start.19 = (bf16[128,384]{1,0:T(8,128)(2,1)S(1)}, bf16[128,384]{1,0:T(8,128)(2,1)S(1)}, u32[]{:S(2)}, u32[]{:S(2)}) collective-permute-start(bf16[128,384]{1,0:T(8,128)(2,1)S(1)} %get-tuple-element.81), channel_id=1, source_target_pairs={{0,8},{4,12},{8,0},{12,4},{16,24},{20,28},{24,16},{28,20},{1,9},{5... | collective-permute-start | bytes 294920 | tf_op jit(solution)/shard_map/ppermute | solution.py:35
  42.2 5.4 %collective-permute-start.21 = (bf16[128,384]{1,0:T(8,128)(2,1)S(1)}, bf16[128,384]{1,0:T(8,128)(2,1)S(1)}, u32[]{:S(2)}, u32[]{:S(2)}) collective-permute-start(bf16[128,384]{1,0:T(8,128)(2,1)S(1)} %get-tuple-element.83), channel_id=1, source_target_pairs={{0,4},{4,0},{8,12},{12,8},{16,20},{20,16},{24,28},{28,24},{1,5},{5... | collective-permute-start | bytes 294920 | tf_op jit(solution)/shard_map/ppermute | solution.py:35
  43.5 4.1 %collective-permute-start.20 = (bf16[64,384]{1,0:T(8,128)(2,1)S(1)}, bf16[64,384]{1,0:T(8,128)(2,1)S(1)}, u32[]{:S(2)}, u32[]{:S(2)}) collective-permute-start(bf16[64,384]{1,0:T(8,128)(2,1)S(1)} %get-tuple-element.82), channel_id=1, source_target_pairs={{0,8},{4,12},{8,0},{12,4},{16,24},{20,28},{24,16},{28,20},{1,9},{5... | collective-permute-start | bytes 147464 | tf_op jit(solution)/shard_map/ppermute | solution.py:35
